TPU v7x, 32 devices: a whole 2x2x4 slice. The times are simulated.
32 devices in a mesh: groups: 2 (over y), space: 8 (over z, x), modes: 2 (over core).
Axes of the slice: x: 2, y: 2, z: 4, core: 2. Of those that a mesh axis runs over, the one named last changes fastest.
Arguments:
- modes: bfloat16 [256, 3, 16, 8, 128], P('modes', None, ('groups', 'space')), parts along dimension 2, may hold values from -6 to 6
- weight_ids: int32 [16, 8, 128], P(('groups', 'space')), parts along dimension 0, may hold values from 0 to 15
- weight_table: float32 [16], replicated, may hold values from 0.2 to 2
- j_block: int32 [2], P('groups'), parts along dimension 0, may hold values from 0 to 63
Outputs:
- galerkin: float32 [512, 4, 256], P(('groups', 'space'), None, 'modes'), parts along dimension 0
There are 2 independent parts, one for each index of `groups`. A program takes and returns all parts, laid end to end along the dimension named above; an argument that names none is the same for every part. Nothing has to cross between parts.
All inputs are finite; a program needn't handle non-finite values.
Results may differ from a plain program's by a relative error of at most 0.005.
Values may be sent and summed in bfloat16 or wider, within the bound.
No kernel may reach another device: no remote copies, remote signals or barrier semaphores. Data moves between devices by JAX's collectives and lax.ppermute only.
A program may use at most 64 MiB of HBM per device.

v0:
```python
import jax
import jax.numpy as jnp
from jax import lax
from jax.sharding import PartitionSpec as P

JB = 4
NW = 16


def broadcast(value, axis, source):
    kept = jnp.where(lax.axis_index(axis) == source, value, 0).astype(value.dtype)
    return lax.psum(kept, axis)


def padded_2(cells, sides, width):
    for axis, dim in sides:
        count = lax.axis_size(axis)
        ends = count - 1
        head = lax.slice_in_dim(cells, 0, width, axis=dim)
        tail = lax.slice_in_dim(cells, cells.shape[dim] - width, cells.shape[dim], axis=dim)
        cells = jnp.concatenate(
            [
                lax.ppermute(tail, axis, [(i, (i + 1) % count) for i in range(ends)]),
                cells,
                lax.ppermute(head, axis, [((i + 1) % count, i) for i in range(ends)]),
            ],
            axis=dim,
        )
    return cells


def derivs(padded):
    core = padded[:, :, 1:-1]
    along_x = 0.5 * (jnp.roll(core, -1, 3) - jnp.roll(core, 1, 3))
    along_y = 0.5 * (padded[:, :, 2:] - padded[:, :, :-2])
    along_z = 0.5 * (jnp.roll(core, -1, 4) - jnp.roll(core, 1, 4))
    return jnp.stack([along_x, along_y, along_z], 2)


def advect_all(phij, grads):
    total = phij[:, 0][:, None, None, :] * grads[None, :, :, 0].astype(jnp.float32)
    total = total + phij[:, 1][:, None, None, :] * grads[None, :, :, 1].astype(jnp.float32)
    total = total + phij[:, 2][:, None, None, :] * grads[None, :, :, 2].astype(jnp.float32)
    return total.astype(jnp.bfloat16)


def on_device(modes, weight_ids, weight_table, j_block):
    own_count = modes.shape[0]
    points = modes.shape[2] * modes.shape[3] * modes.shape[4]
    first = j_block[0] * JB
    owner = first // own_count
    offset = first - owner * own_count
    own_slice = lax.dynamic_slice_in_dim(modes, offset, JB, 0)
    jmodes = broadcast(own_slice, "modes", owner)
    phij = jmodes.astype(jnp.float32).reshape(JB, 3, points)
    weight = jnp.zeros(weight_ids.shape, jnp.float32)
    for entry in range(NW):
        weight = jnp.where(weight_ids == entry, weight_table[entry], weight)
    weighted = (
        (weight[None, None] * modes.astype(jnp.float32))
        .astype(jnp.bfloat16)
        .reshape(own_count, 3, points)
    )
    padded = padded_2(modes, (("space", 2),), 1)
    piece = lax.all_gather(padded, "modes", axis=0, tiled=True)
    grads = (
        derivs(piece.astype(jnp.float32)).astype(jnp.bfloat16).reshape(piece.shape[0], 3, 3, points)
    )
    advect = advect_all(phij, grads)
    block = jnp.einsum("jkcp,icp->kji", advect, weighted, preferred_element_type=jnp.float32)
    return lax.psum_scatter(block, "space", scatter_dimension=0, tiled=True)


def solution(mesh):
    return jax.shard_map(
        on_device,
        mesh=mesh,
        in_specs=(
            P("modes", None, ("groups", "space"), None, None),
            P(("groups", "space"), None, None),
            P(),
            P("groups"),
        ),
        out_specs=P(("groups", "space"), None, "modes"),
        check_vma=False,
    )
```

profile of v0, /device:TPU:0, one launch (start us, length us, event | category | flops | bytes accessed | tf_op | source)
XLA Modules:
  0.0 181.4 jit_solution(11073790696009552011)
XLA Ops:
  6.5 0.0 all-gather.2.cloned.1.call-start
  6.5 1.6 copy.20
  8.1 0.0 copy-start
  8.2 0.0 copy-start.1
  8.2 1.3 collective-permute-start.1
  9.5 5.5 %collective-permute-start = (bf16[128,3,1,8,128]{0,4,3,1,2:T(8,128)(2,1)S(1)}, bf16[128,3,1,8,128]{0,4,3,1,2:T(8,128)(2,1)S(1)}, u32[]{:S(2)}, u32[]{:S(2)}) collective-permute-start(bf16[128,3,1,8,128]{0,4,3,1,2:T(8,128)(2,1)S(1)} %copy.20), channel_id=1, source_target_pairs={{0,2},{2,4},{4,6},{6,8},{8,10},{10,12},{12,14},{1,3},{3,5},{5,7},{... | collective-permute-start | bytes 2359304 | tf_op jit(solution)/shard_map/ppermute | solution.py:23
  15.0 15.6 %collective-permute-done.1 = bf16[128,3,1,8,128]{0,4,3,1,2:T(8,128)(2,1)S(1)} collective-permute-done((bf16[128,3,1,8,128]{0,4,3,1,2:T(8,128)(2,1)S(1)}, bf16[128,3,1,8,128]{0,4,3,1,2:T(8,128)(2,1)S(1)}, u32[]{:S(2)}, u32[]{:S(2)}) %collective-permute-start.1) | collective-permute-done | bytes 786464 | tf_op jit(solution)/shard_map/ppermute | solution.py:25
  30.5 17.0 %collective-permute-done = bf16[128,3,1,8,128]{0,4,3,1,2:T(8,128)(2,1)S(1)} collective-permute-done((bf16[128,3,1,8,128]{0,4,3,1,2:T(8,128)(2,1)S(1)}, bf16[128,3,1,8,128]{0,4,3,1,2:T(8,128)(2,1)S(1)}, u32[]{:S(2)}, u32[]{:S(2)}) %collective-permute-start) | collective-permute-done | bytes 786464 | tf_op jit(solution)/shard_map/ppermute | solution.py:23
  47.5 1.7 pad_maximum_fusion
  49.2 0.0 all-gather.2.cloned.1.call-update
  49.3 0.0 all-reduce.3.cloned.1.call-start
  50.0 0.7 dynamic-slice_select_fusion
  50.8 3.4 %psum.7 = bf16[4,3,1024]{2,0,1:T(4,128)(2,1)S(1)} all-reduce(bf16[4,3,1024]{2,0,1:T(4,128)(2,1)S(1)} %reshape.189), channel_id=1, replica_groups=mesh['groups'=2,'space'=8,'modes'=2] {'modes'}, use_global_device_ids=true, to_apply=%region_0.1 | all-reduce | flops 12288 | bytes 49152 | tf_op jit(solution)/shard_map/psum | solution.py:12
  54.2 0.0 copy-done
  54.2 0.7 fusion.12
  54.9 0.0 copy-done.1
  54.9 10.1 %select_bitcast_fusion = f32[8,128]{1,0:T(8,128)S(1)} fusion(s32[1,8,128]{2,1,0:T(8,128)S(1)} %copy-done.1, f32[]{:T(128)} %bitcast.15, f32[]{:T(128)} %bitcast.14, f32[]{:T(128)} %bitcast.13, f32[]{:T(128)} %bitcast.12, f32[]{:T(128)} %bitcast.11, f32[]{:T(128)} %bitcast.10, f32[]{:T(128)} %bitcast.9, f32[]{:T(128)} %bitcast.8, f32[]{:T(128)} %bitcast.7, ...), kind=kLoop, calls=%fused_computation.18 | loop fusion | flops 32768 | bytes 8256 | tf_op jit(solution)/shard_map/mul | solution.py:60
  65.0 1.2 multiply_convert_fusion
  66.2 0.0 all-gather.2.cloned.1.call-done
  66.2 1.0 fusion.10
  67.2 2.7 %fusion.11 = (f32[256,3,1,8,127]{0,4,3,1,2:T(8,128)S(1)}, f32[256,3,1,8,127]{0,4,3,1,2:T(8,128)S(1)}) fusion(bf16[256,3,3,8,128]{0,4,3,1,2:T(8,128)(2,1)} %all-gather.2.cloned.1.call-done), kind=kLoop, calls=%fused_computation.23 | loop fusion | bytes 12484608 | tf_op jit(solution)/shard_map/jit(_roll_static)/slice | solution.py:36
  69.9 2.0 %fusion.6 = bf16[256,3,1,8,128]{0,4,3,1,2:T(8,128)(2,1)} fusion(f32[256,3,1,8,1]{0,4,3,1,2:T(1,128)S(1)} %get-tuple-element.10, f32[256,3,1,8,127]{0,4,3,1,2:T(8,128)S(1)} %get-tuple-element.12, f32[256,3,1,8,127]{0,4,3,1,2:T(8,128)S(1)} %get-tuple-element.11, f32[256,3,1,8,1]{0,4,3,1,2:T(1,128)S(1)} %get-tuple-element.9), kind=kLoop, calls=%fused_computation.10 | loop fusion | flops 3932160 | bytes 7864320 | tf_op jit(solution)/shard_map/convert.7
  71.9 1.7 copy.27
  73.6 3.6 %convert_element_type.54 = f32[256,3,3,8,128]{0,4,3,1,2:T(8,128)S(1)} convert(bf16[256,3,3,8,128]{0,4,3,1,2:T(8,128)(2,1)} %all-gather.2.cloned.1.call-done) | non-fusion elementwise | flops 2359296 | bytes 14155776 | tf_op jit(solution)/shard_map/convert_element_type | solution.py:67
  77.3 1.8 %fusion.2 = bf16[256,3,1,8,128]{0,4,3,1,2:T(8,128)(2,1)} fusion(f32[256,3,3,8,128]{0,4,3,1,2:T(8,128)S(1)} %convert_element_type.54), kind=kLoop, calls=%fused_computation.4 | loop fusion | flops 2359296 | bytes 7864320 | tf_op jit(solution)/shard_map/convert.8
  79.1 3.1 %copy.26 = f32[256,3,1024]{2,0,1:T(8,128)} copy(bf16[256,3,1024]{0,2,1:T(8,128)(2,1)} %bitcast.47) | data formatting | bytes 4718592 | tf_op jit(solution)/shard_map/convert_element_type | solution.py:42
  82.2 1.1 fusion.8
  83.3 2.5 %fusion.9 = (f32[256,3,1,7,128]{0,4,3,1,2:T(8,128)S(1)}, f32[256,3,1,7,128]{0,4,3,1,2:T(8,128)S(1)}) fusion(bf16[256,3,3,8,128]{0,4,3,1,2:T(8,128)(2,1)} %all-gather.2.cloned.1.call-done), kind=kLoop, calls=%fused_computation.21 | loop fusion | bytes 11010048 | tf_op jit(solution)/shard_map/jit(_roll_static)/slice | solution.py:34
  85.7 1.7 fusion.4
  87.5 3.0 %copy.25 = f32[256,3,1024]{2,0,1:T(8,128)} copy(bf16[256,3,1024]{0,2,1:T(8,128)(2,1)} %bitcast.46) | data formatting | bytes 4718592 | tf_op jit(solution)/shard_map/convert_element_type | solution.py:41
  90.5 0.0 copy-start.2
  90.5 6.8 %fusion.7 = f32[256,4,128]{0,2,1:T(8,128)} fusion(bf16[128,3,1024,1]{0,2,1,3:T(8,128)(2,1)} %bitcast.48, f32[256,3,1024]{2,0,1:T(8,128)S(1)} %copy.27, f32[4,1024]{1,0:T(4,128)S(1)} %get-tuple-element.14, f32[256,3,1024]{2,0,1:T(8,128)} %copy.26, f32[4,1024]{1,0:T(4,128)S(1)} %get-tuple-element.15, f32[256,3,1024]{2,0,1:T(8,128)} %copy.25, ...), kind=kOutput, calls=%fused_computation.13 | convolution fusion | flops 824180736 | bytes 10797056 | tf_op jit(solution)/shard_map/jkcp,icp->kji/dot_general | solution.py:70
  97.3 2.0 %copy.29 = f32[256,4,128]{2,1,0:T(4,128)} copy(f32[256,4,128]{0,2,1:T(8,128)} %fusion.7) | data formatting | bytes 1048576 | tf_op jit(solution)/shard_map/jkcp,icp->kji/transpose | solution.py:70
  99.3 0.0 all-reduce.3.cloned.1.call-update
  99.3 0.0 copy-done.2
  99.4 0.6 dynamic-slice
  100.6 72.5 %all-reduce.3.cloned.1.call-done = f32[256,4,128]{2,1,0:T(4,128)} async-done(((f32[256,4,128]{2,1,0:T(4,128)}), f32[256,4,128]{2,1,0:T(4,128)}) %all-reduce.3.cloned.1.call-update) | async-done | bytes 524304
  173.1 1.5 constant_dynamic-slice_fusion
  (4 shorter events, 0.0 us)
Async XLA Ops:
  6.5 59.7 %all-gather.2.cloned.1.call-start = ((), (), s32[]{:S(2)}) async-start(), calls=%async_computation | async-start | bytes 7077888 | tf_op jit(solution)/shard_map/all_gather | solution.py:65
  8.1 46.1 %copy-start = (f32[16]{0:T(128)S(1)}, f32[16]{0:T(128)}, u32[]{:S(2)}) copy-start(f32[16]{0:T(128)} %param.6) | copy-start | bytes 196
  8.2 46.8 %copy-start.1 = (s32[1,8,128]{2,1,0:T(8,128)S(1)}, s32[1,8,128]{2,1,0:T(8,128)}, u32[]{:S(2)}) copy-start(s32[1,8,128]{2,1,0:T(8,128)} %param.5) | copy-start | bytes 12292
  8.2 22.4 %collective-permute-start.1 = (bf16[128,3,1,8,128]{0,4,3,1,2:T(8,128)(2,1)S(1)}, bf16[128,3,1,8,128]{0,4,3,1,2:T(8,128)(2,1)S(1)}, u32[]{:S(2)}, u32[]{:S(2)}) collective-permute-start(bf16[128,3,1,8,128]{0,4,3,1,2:T(8,128)(2,1)S(1)} %copy.20), channel_id=1, source_target_pairs={{2,0},{4,2},{6,4},{8,6},{10,8},{12,10},{14,12},{3,1},{5,3},{7,5},{... | collective-permute-start | bytes 2359304 | tf_op jit(solution)/shard_map/ppermute | solution.py:25
  9.5 38.1 %collective-permute-start = (bf16[128,3,1,8,128]{0,4,3,1,2:T(8,128)(2,1)S(1)}, bf16[128,3,1,8,128]{0,4,3,1,2:T(8,128)(2,1)S(1)}, u32[]{:S(2)}, u32[]{:S(2)}) collective-permute-start(bf16[128,3,1,8,128]{0,4,3,1,2:T(8,128)(2,1)S(1)} %copy.20), channel_id=1, source_target_pairs={{0,2},{2,4},{4,6},{6,8},{8,10},{10,12},{12,14},{1,3},{3,5},{5,7},{... | collective-permute-start | bytes 2359304 | tf_op jit(solution)/shard_map/ppermute | solution.py:23
  49.3 123.9 %all-reduce.3.cloned.1.call-start = ((), (), s32[]{:S(2)}) async-start(), calls=%async_computation.1 | async-start | bytes 1048576
  90.5 8.8 %copy-start.2 = (u32[32]{0:T(128)S(1)}, u32[32]{0:T(128)}, u32[]{:S(2)}) copy-start(u32[32]{0:T(128)} %constant.65) | copy-start | bytes 388
Sparse Core Ops, SparseCore 0:
  49.4 14.8 all-gather.1
  99.5 73.6 all-reduce.2
where the time goes:
time: 182 us; the launch traced here: 181 us
  waiting for transfers between devices  105 us (58%)
  other arithmetic  22.9 us (13%)
  local copies, waits for them, and re-layouts  21.4 us (12%)
  between operations  14.9 us (8%)
  starting transfers between devices  6.86 us (4%)
  matrix products  6.79 us (4%)
  blocking collectives  3.42 us (2%)
    unnamed x3, waiting for transfers between devices  72.6 us
    ppermute x1, waiting for transfers between devices, padded_2(): lax.ppermute(tail, axis, [(i, (i + 1) % count) for i in range(ends)])  17 us
    ppermute x1, waiting for transfers between devices, padded_2(): lax.ppermute(head, axis, [((i + 1) % count, i) for i in range(ends)])  15.6 us
    mul x1, other arithmetic, on_device(): weight[None, None] * modes.astype(jnp.float32)  10.1 us
    dot_general x1, matrix products, on_device(): jnp.einsum('jkcp,icp->kji', advect, weighted, preferred_element_type=jnp....  6.79 us
    another operation x3, other arithmetic  5.57 us
    ppermute x1, starting transfers between devices, padded_2(): lax.ppermute(tail, axis, [(i, (i + 1) % count) for i in range(ends)])  5.52 us
    unnamed x9, local copies, waits for them, and re-layouts  3.67 us
  transfers between devices with their start and end apart: 4, of which 3 were waited for; matrix products, arithmetic and copies ran while one was open for 7% of the time, Pallas kernels for 0%

commit v1 on v0

v1 whole, which is shorter than its diff:
```python
import functools

import jax
import jax.numpy as jnp
from jax import lax
from jax.experimental import pallas as pl
from jax.experimental.pallas import tpu as pltpu
from jax.sharding import PartitionSpec as P

JB = 4
NW = 16
IDROWS = 16
VMEM_LIMIT = 48 * 1024 * 1024


def prep_kernel(modes_ref, ids_ref, own_ref, core_ref, xs_ref, xc_ref, zs_ref, zc_ref, tr):
    m = lax.axis_index("modes")
    q = lax.rem(lax.axis_index("space"), 2)
    nk, comps, _, nx, nz = modes_ref.shape
    for c in range(comps):
        value = modes_ref[:, c, 0].astype(jnp.float32)
        tr[:, c] = jnp.swapaxes(value, 0, 1).astype(jnp.bfloat16)
    quarter = nx // 4
    for r in range(nx // 2 + 2):
        own_ref[r] = tr[lax.rem(nx // 2 * m + nx - 1 + r, nx)]
        core_ref[r] = tr[lax.rem(nx // 2 * (1 - m) + nx - 1 + r, nx)]
    for ref, at, with_ids in (
        (xs_ref, 2 * m + 1 - q, True),
        (xc_ref, 2 * (1 - m) + 1 - q, False),
        (zs_ref, 2 * m + q, True),
        (zc_ref, 2 * (1 - m) + q, False),
    ):
        for row in range(quarter):
            for c in range(comps):
                ref[pl.ds((row * comps + c) * nk, nk), :] = tr[at * quarter + row, c]
        if with_ids:
            ids = [
                jnp.broadcast_to(ids_ref[0, pl.ds(at * quarter + row, 1), :], (IDROWS // quarter, nz))
                for row in range(quarter)
            ]
            rows = jnp.concatenate(ids, axis=0).astype(jnp.float32).astype(jnp.bfloat16)
            ref[pl.ds(quarter * comps * nk, IDROWS), :] = rows


def picks(jb_ref, m, nk):
    first = jb_ref[0] * JB
    row = lax.broadcasted_iota(jnp.int32, (16, nk), 0)
    col = lax.broadcasted_iota(jnp.int32, (16, nk), 1)
    want = jnp.where(row < JB, first + row, -1)
    own = (want == col + m * nk).astype(jnp.float32).astype(jnp.bfloat16)
    other = (want == col + (1 - m) * nk).astype(jnp.float32).astype(jnp.bfloat16)
    return own, other


def picked(pick, own, other):
    return jnp.dot(pick[0], own, preferred_element_type=jnp.float32) + jnp.dot(
        pick[1], other, preferred_element_type=jnp.float32
    )


def weights_of(ids, table_ref):
    weight = jnp.zeros(ids.shape, jnp.float32)
    for entry in range(NW):
        weight = jnp.where(ids == entry, table_ref[entry], weight)
    return weight


def dot_nt(a, b):
    return lax.dot_general(a, b, (((1,), (1,)), ((), ())), preferred_element_type=jnp.float32)


def local_kernel(own_ref, other_ref, ids_ref, table_ref, jb_ref, acc_ref, adv, wts, wscr):
    m = lax.axis_index("modes")
    rows, comps, nk, nz = own_ref.shape
    rows -= 2
    pick = picks(jb_ref, m, nk)
    wscr[...] = weights_of(ids_ref[0], table_ref)
    for r in range(rows):
        phi = [picked(pick, own_ref[r + 1, d], other_ref[r + 1, d]) for d in range(comps)]
        weight = wscr[pl.ds(rows * m + r, 1), :]
        for c in range(comps):
            at = pl.ds((r * comps + c) * nz, nz)
            for half, ref in enumerate((own_ref, other_ref)):
                block = pl.ds(half * nk, nk)
                here = ref[r + 1, c].astype(jnp.float32)
                gx = 0.5 * (ref[r + 2, c].astype(jnp.float32) - ref[r, c].astype(jnp.float32))
                gz = 0.5 * (pltpu.roll(here, nz - 1, 1) - pltpu.roll(here, 1, 1))
                gx = gx.astype(jnp.bfloat16).astype(jnp.float32)
                gz = gz.astype(jnp.bfloat16).astype(jnp.float32)
                wts[block, at] = (weight * here).astype(jnp.bfloat16)
                for j in range(JB):
                    total = phi[0][j : j + 1] * gx + phi[2][j : j + 1] * gz
                    adv[j, block, at] = total.astype(jnp.bfloat16)
    for j in range(JB):
        acc_ref[j] = dot_nt(adv[j], wts[...])


def cross_kernel(
    chunk, own_ref, other_ref, xs_ref, xc_ref, zs_ref, zc_ref, ids_ref, table_ref, jb_ref, acc_ref,
    keep_ref, send_ref, adv, wts, wscr,
):
    m = lax.axis_index("modes")
    q = lax.rem(lax.axis_index("space"), 2)
    sigma = jnp.where(q == 0, 0.5, -0.5)
    rows, comps, nk, nz = own_ref.shape
    rows -= 2
    quarter = rows // 2
    span = quarter * comps * nz
    pick = picks(jb_ref, m, nk)
    wscr[...] = weights_of(ids_ref[0], table_ref)
    w1 = weights_of(xs_ref[pl.ds(span, IDROWS), :].astype(jnp.float32), table_ref)
    w2 = weights_of(zs_ref[pl.ds(span, IDROWS), :].astype(jnp.float32), table_ref)
    for r in range(quarter):
        row0 = 1 + quarter * q + r
        weight0 = wscr[pl.ds(rows * m + quarter * q + r, 1), :]
        idrow = IDROWS // quarter * r
        weight1, weight2 = w1[idrow : idrow + 1], w2[idrow : idrow + 1]
        along = pl.ds((r * comps + 1) * nk, nk)
        phi0 = sigma * picked(pick, own_ref[row0, 1], other_ref[row0, 1])
        phi1 = picked(pick, xs_ref[along, :], xc_ref[along, :])
        phi2 = -sigma * picked(pick, zs_ref[along, :], zc_ref[along, :])
        for c in range(comps):
            lane = (r * comps + c) * nz
            src = pl.ds((r * comps + c) * nk, nk)
            for half, (p0, p1, p2) in enumerate(
                ((own_ref, xs_ref, zs_ref), (other_ref, xc_ref, zc_ref))
            ):
                block = pl.ds(half * nk, nk)
                f0 = p0[row0, c].astype(jnp.float32)
                f1 = p1[src, :].astype(jnp.float32)
                f2 = p2[src, :].astype(jnp.float32)
                gy = (sigma * (f2 - f0)).astype(jnp.bfloat16).astype(jnp.float32)
                for part, (field, weight) in enumerate(((f0, weight0), (f1, weight1), (f2, weight2))):
                    wts[block, pl.ds(part * span + lane, nz)] = (weight * field).astype(jnp.bfloat16)
                for j in range(JB):
                    for part, (phi, field) in enumerate(((phi0, f1), (phi1, gy), (phi2, f1))):
                        adv[j, block, pl.ds(part * span + lane, nz)] = (
                            phi[j : j + 1] * field
                        ).astype(jnp.bfloat16)
    per_half = nk // chunk
    for j in range(JB):
        total = acc_ref[j] + dot_nt(adv[j], wts[...])
        for half in range(2):
            first = per_half * (m if half == 0 else 1 - m)
            for part in range(per_half):
                piece = total[half * nk + part * chunk : half * nk + (part + 1) * chunk]
                keep_ref[first + part, j] = piece[:, :nk]
                send_ref[first + part, j] = piece[:, nk:]


def on_device(n, modes, weight_ids, weight_table, j_block):
    nk, comps, _, nx, nz = modes.shape
    bf16, f32 = jnp.bfloat16, jnp.float32
    vmem = pl.BlockSpec(memory_space=pltpu.VMEM)
    smem = pl.BlockSpec(memory_space=pltpu.SMEM)
    params = pltpu.CompilerParams(vmem_limit_bytes=VMEM_LIMIT)
    six = nx // 2 + 2
    body = nx // 4 * comps * nk
    own, to_core, xs, xc, zs, zc = pl.pallas_call(
        prep_kernel,
        out_shape=[
            jax.ShapeDtypeStruct((six, comps, nk, nz), bf16),
            jax.ShapeDtypeStruct((six, comps, nk, nz), bf16),
            jax.ShapeDtypeStruct((body + IDROWS, nz), bf16),
            jax.ShapeDtypeStruct((body, nz), bf16),
            jax.ShapeDtypeStruct((body + IDROWS, nz), bf16),
            jax.ShapeDtypeStruct((body, nz), bf16),
        ],
        in_specs=[vmem, vmem],
        out_specs=[vmem] * 6,
        scratch_shapes=[pltpu.VMEM((nx, comps, nk, nz), bf16)],
        compiler_params=params,
        name="prep",
    )(modes, weight_ids)

    both = ("space", "modes")
    x_pairs = [(s, s ^ 1) for s in range(n)]
    z_pairs = [(s, s - 2) for s in range(2, n, 2)] + [(s, s + 2) for s in range(1, n - 2, 2)]
    same = lambda pairs: [(2 * a + m, 2 * b + m) for a, b in pairs for m in range(2)]
    cross = lambda pairs: [(2 * a + m, 2 * b + 1 - m) for a, b in pairs for m in range(2)]
    other = lax.ppermute(to_core, "modes", [(0, 1), (1, 0)])
    xs = lax.ppermute(xs, both, same(x_pairs))
    zs = lax.ppermute(zs, both, same(z_pairs))
    xc = lax.ppermute(xc, both, cross(x_pairs))
    zc = lax.ppermute(zc, both, cross(z_pairs))

    acc = pl.pallas_call(
        local_kernel,
        out_shape=jax.ShapeDtypeStruct((JB, 2 * nk, 2 * nk), f32),
        in_specs=[vmem, vmem, vmem, smem, smem],
        out_specs=vmem,
        scratch_shapes=[
            pltpu.VMEM((JB, 2 * nk, nx // 2 * comps * nz), bf16),
            pltpu.VMEM((2 * nk, nx // 2 * comps * nz), bf16),
            pltpu.VMEM((nx, nz), f32),
        ],
        compiler_params=params,
        cost_estimate=pl.CostEstimate(flops=900_000_000, bytes_accessed=2_400_000, transcendentals=0),
        name="local",
    )(own, other, weight_ids, weight_table, j_block)

    per_target = 2 * nk // n
    chunk = max(16, per_target)
    pieces = 2 * nk // chunk
    keep, send = pl.pallas_call(
        functools.partial(cross_kernel, chunk),
        out_shape=[jax.ShapeDtypeStruct((pieces, JB, chunk, nk), f32)] * 2,
        in_specs=[vmem] * 7 + [smem, smem, vmem],
        out_specs=[vmem] * 2,
        scratch_shapes=[
            pltpu.VMEM((JB, 2 * nk, 3 * nx // 4 * comps * nz), bf16),
            pltpu.VMEM((2 * nk, 3 * nx // 4 * comps * nz), bf16),
            pltpu.VMEM((nx, nz), f32),
        ],
        compiler_params=params,
        cost_estimate=pl.CostEstimate(flops=1_300_000_000, bytes_accessed=4_000_000, transcendentals=0),
        name="cross",
    )(own, other, xs, xc, zs, zc, weight_ids, weight_table, j_block, acc)

    got = lax.ppermute(send, "modes", [(0, 1), (1, 0)])
    share = (keep + got).astype(bf16)
    if chunk != per_target:
        share = share.reshape(pieces, JB, chunk // per_target, per_target, nk)
        share = share.transpose(0, 2, 1, 3, 4).reshape(n, JB, per_target, nk)
    parts = lax.all_to_all(share, "space", 0, 0, tiled=True)
    return jnp.sum(parts.astype(f32), axis=0).transpose(1, 0, 2)


def solution(mesh):
    return jax.shard_map(
        functools.partial(on_device, mesh.shape["space"]),
        mesh=mesh,
        in_specs=(
            P("modes", None, ("groups", "space"), None, None),
            P(("groups", "space"), None, None),
            P(),
            P("groups"),
        ),
        out_specs=P(("groups", "space"), None, "modes"),
        check_vma=False,
    )
```

time: 182 us -> 37.7 us (0.21)
  waiting for transfers between devices: 105 us -> 5.42 us
  other arithmetic: 22.9 us -> 0.14 us
  local copies, waits for them, and re-layouts: 21.4 us -> 3.13 us
  between operations: 14.9 us -> 0.72 us
  blocking collectives: 3.42 us -> 13.9 us
  matrix products: 6.79 us -> 0 us
  Pallas kernels: 0 us -> 5.81 us
    unnamed x3 -> x0, waiting for transfers between devices: 72.6 us -> none
    ppermute x2 -> x6, waiting for transfers between devices: 32.6 us -> 5.42 us  [the longest x1 3.39 us: on_device(): zc = lax.ppermute(zc, both, cross(z_pairs))]
    all_to_all x0 -> x1, blocking collectives: none -> 13.9 us  [on_device(): parts = lax.all_to_all(share, 'space', 0, 0, tiled=True)]
    mul x1 -> x0, other arithmetic: 10.1 us -> none  [on_device(): weight[None, None] * modes.astype(jnp.float32)]
    slice x5 -> x0, local copies, waits for them, and re-layouts: 7.91 us -> none  [the longest x2 3.65 us: derivs(): along_z = 0.5 * (jnp.roll(core, -1, 4) - jnp.roll(core, 1, 4))]
    convert_element_type x3 -> x0, local copies, waits for them, and re-layouts: 7.81 us -> none  [the longest x1 3.07 us: advect_all(): grads[None, :, :, 1].astype(jnp.float32)]
    dot_general x1 -> x0, matrix products: 6.79 us -> none  [on_device(): jnp.einsum('jkcp,icp->kji', advect, weighted, preferred_element_type=jnp....]
    pallas_call x0 -> x3, Pallas kernels: none -> 5.81 us  [the longest x1 2.93 us: on_device(): pl.pallas_call(local_kernel, out_shape=jax.ShapeDtypeStruct((JB, 2 * nk,...]
  transfers between devices with their start and end apart: 4 -> 6, of which waited for: 3 -> 3; matrix products, arithmetic and copies ran while one was open for 7% -> 0% of each run, Pallas kernels for 0% -> 8%
where the time goes in v1:
time: 37.7 us; the launch traced here: 37.4 us
  blocking collectives  13.9 us (37%)
  starting transfers between devices  8.31 us (22%)
  Pallas kernels  5.81 us (15%)
  waiting for transfers between devices  5.42 us (14%)
  local copies, waits for them, and re-layouts  3.13 us (8%)
  between operations  0.72 us (2%)
    all_to_all x1, blocking collectives, on_device(): parts = lax.all_to_all(share, 'space', 0, 0, tiled=True)  13.9 us
    ppermute x1, waiting for transfers between devices, on_device(): zc = lax.ppermute(zc, both, cross(z_pairs))  3.39 us
    pallas_call x1, Pallas kernels, on_device(): pl.pallas_call(local_kernel, out_shape=jax.ShapeDtypeStruct((JB, 2 * nk,...  2.93 us
    ppermute x1, starting transfers between devices, on_device(): xs = lax.ppermute(xs, both, same(x_pairs))  2.56 us
    unnamed x8, local copies, waits for them, and re-layouts  2.45 us
    pallas_call x1, Pallas kernels, on_device(): pl.pallas_call(functools.partial(cross_kernel, chunk), out_shape=[jax.Sha...  2.31 us
    ppermute x1, starting transfers between devices, on_device(): xc = lax.ppermute(xc, both, cross(x_pairs))  2.29 us
    ppermute x1, waiting for transfers between devices, on_device(): got = lax.ppermute(send, 'modes', [(0, 1), (1, 0)])  1.73 us
  transfers between devices with their start and end apart: 6, of which 3 were waited for; matrix products, arithmetic and copies ran while one was open for 0% of the time, Pallas kernels for 8%

profile of v1, /device:TPU:0, one launch (start us, length us, event | category | flops | bytes accessed | tf_op | source)
XLA Modules:
  0.0 37.4 jit_solution(13476307154667765101)
XLA Ops:
  0.0 0.0 copy-start
  0.0 1.1 %copy-done = bf16[128,3,1,8,128]{4,3,2,1,0:T(8,128)(2,1)S(1)} copy-done((bf16[128,3,1,8,128]{4,3,2,1,0:T(8,128)(2,1)S(1)}, bf16[128,3,1,8,128]{4,3,2,1,0:T(8,128)(2,1)}, u32[]{:S(2)}) %copy-start) | copy-done | bytes 786456
  1.1 0.0 copy-start.1
  1.1 0.7 %copy-done.1 = s32[1,8,128]{2,1,0:T(8,128)S(1)} copy-done((s32[1,8,128]{2,1,0:T(8,128)S(1)}, s32[1,8,128]{2,1,0:T(8,128)}, u32[]{:S(2)}) %copy-start.1) | copy-done | bytes 4120
  1.8 0.6 %prep.1 = (bf16[6,3,128,128]{3,2,1,0:T(8,128)(2,1)S(1)}, bf16[6,3,128,128]{3,2,1,0:T(8,128)(2,1)S(1)}, bf16[784,128]{1,0:T(8,128)(2,1)S(1)}, bf16[768,128]{1,0:T...) custom-call(bf16[128,3,1,8,128]{4,3,2,1,0:T(8,128)(2,1)S(1)} %copy-done, ...), custom_call_target="tpu_custom_call" | custom-call | tf_op jit(solution)/shard_map/prep/pallas_call | solution.py:159
  2.4 0.5 %collective-permute-start = (bf16[6,3,128,128]{3,2,1,0:T(8,128)(2,1)S(1)}, bf16[6,3,128,128]{3,2,1,0:T(8,128)(2,1)S(1)}, u32[]{:S(2)}, u32[]{:S(2)}) collective-permute-start(bf16[6,3,128,128]{3,2,1,0:T(8,128)(2,1)S(1)} %get-tuple-element.14), channel_id=1, source_target_pairs={{0,1},{1,0},{2,3},{3,2},{4,5},{5,4},{6,7},{7,6},{8,9},{9,8},{10,11... | collective-permute-start | bytes 1769480 | tf_op jit(solution)/shard_map/ppermute | solution.py:181
  2.9 2.6 %collective-permute-start.1 = (bf16[784,128]{1,0:T(8,128)(2,1)S(1)}, bf16[784,128]{1,0:T(8,128)(2,1)S(1)}, u32[]{:S(2)}, u32[]{:S(2)}) collective-permute-start(bf16[784,128]{1,0:T(8,128)(2,1)S(1)} %get-tuple-element.15), channel_id=1, source_target_pairs={{0,2},{1,3},{2,0},{3,1},{4,6},{5,7},{6,4},{7,5},{8,10},{9,11},{10,... | collective-permute-start | bytes 602120 | tf_op jit(solution)/shard_map/ppermute | solution.py:182
  5.5 0.0 copy-start.2
  5.5 1.4 %collective-permute-start.3 = (bf16[784,128]{1,0:T(8,128)(2,1)S(1)}, bf16[784,128]{1,0:T(8,128)(2,1)S(1)}, u32[]{:S(2)}, u32[]{:S(2)}) collective-permute-start(bf16[784,128]{1,0:T(8,128)(2,1)S(1)} %get-tuple-element.17), channel_id=1, source_target_pairs={{4,0},{5,1},{8,4},{9,5},{12,8},{13,9},{2,6},{3,7},{6,10},{7,11},{1... | collective-permute-start | bytes 602120 | tf_op jit(solution)/shard_map/ppermute | solution.py:183
  6.9 2.3 %collective-permute-start.2 = (bf16[768,128]{1,0:T(8,128)(2,1)S(1)}, bf16[768,128]{1,0:T(8,128)(2,1)S(1)}, u32[]{:S(2)}, u32[]{:S(2)}) collective-permute-start(bf16[768,128]{1,0:T(8,128)(2,1)S(1)} %get-tuple-element.16), channel_id=1, source_target_pairs={{0,3},{1,2},{2,1},{3,0},{4,7},{5,6},{6,5},{7,4},{8,11},{9,10},{10,... | collective-permute-start | bytes 589832 | tf_op jit(solution)/shard_map/ppermute | solution.py:184
  9.2 1.3 %collective-permute-start.4 = (bf16[768,128]{1,0:T(8,128)(2,1)S(1)}, bf16[768,128]{1,0:T(8,128)(2,1)S(1)}, u32[]{:S(2)}, u32[]{:S(2)}) collective-permute-start(bf16[768,128]{1,0:T(8,128)(2,1)S(1)} %get-tuple-element.18), channel_id=1, source_target_pairs={{4,1},{5,0},{8,5},{9,4},{12,9},{13,8},{2,7},{3,6},{6,11},{7,10},{1... | collective-permute-start | bytes 589832 | tf_op jit(solution)/shard_map/ppermute | solution.py:185
  11.1 0.0 copy-start.3
  11.1 0.0 collective-permute-done.other_ref
  11.1 0.0 copy-done.2
  11.2 0.6 %copy-done.3 = f32[16]{0:T(128)S(1)} copy-done((f32[16]{0:T(128)S(1)}, f32[16]{0:T(128)}, u32[]{:S(2)}) %copy-start.3) | copy-done | bytes 88
  11.8 2.9 %local.1.acc_ref = f32[4,256,256]{2,1,0:T(8,128)S(1)} custom-call(bf16[6,3,128,128]{3,2,1,0:T(8,128)(2,1)S(1)} %get-tuple-element.13.own_ref, bf16[6,3,128,128]{3,2,1,0:T(8,128)(2,1)S(1)} %collective-permute-done.other_ref, s32[1,8,128]{2,1,0:T(8,128)S(1)} %copy-done.2, f32[16]{0:T(128)S(1)} %copy-done.3, s32[1]{0:T(128)S(6)} %copy.6.jb_ref), custom_call_target="tpu_custom_call" | custom-call | flops 900000000 | bytes 2400000 | tf_op jit(solution)/shard_map/local/pallas_call | solution.py:187
  14.7 0.3 collective-permute-done.2.xc_ref
  15.0 3.4 %collective-permute-done.4.zc_ref = bf16[768,128]{1,0:T(8,128)(2,1)S(1)} collective-permute-done((bf16[768,128]{1,0:T(8,128)(2,1)S(1)}, bf16[768,128]{1,0:T(8,128)(2,1)S(1)}, u32[]{:S(2)}, u32[]{:S(2)}) %collective-permute-start.4) | collective-permute-done | bytes 196640 | tf_op jit(solution)/shard_map/ppermute | solution.py:185
  18.4 0.0 collective-permute-done.1.xs_ref
  18.4 0.0 collective-permute-done.3.zs_ref
  18.4 2.3 %cross.1 = (f32[8,4,32,128]{3,2,1,0:T(8,128)S(1)}, f32[8,4,32,128]{3,2,1,0:T(8,128)S(1)}) custom-call(bf16[6,3,128,128]{3,2,1,0:T(8,128)(2,1)S(1)} %get-tuple-element.13.own_ref, bf16[6,3,128,128]{3,2,1,0:T(8,128)(2,1)S(1)} %collective-permute-done.other_ref, bf16[784,128]{1,0:T(8,128)(2,1)S(1)} %collective-permute-done.1.xs_ref, ...), custom_call_target="tpu_custom_call" | custom-call | flops 1300000000 | bytes 4000000 | tf_op jit(solution)/shard_map/cross/pallas_call | solution.py:205
  20.7 0.2 collective-permute-start.5
  21.0 1.7 %collective-permute-done.5 = f32[8,4,32,128]{3,2,1,0:T(8,128)S(1)} collective-permute-done((f32[8,4,32,128]{3,2,1,0:T(8,128)S(1)}, f32[8,4,32,128]{3,2,1,0:T(8,128)S(1)}, u32[]{:S(2)}, u32[]{:S(2)}) %collective-permute-start.5) | collective-permute-done | bytes 524320 | tf_op jit(solution)/shard_map/ppermute | solution.py:220
  22.7 0.1 add_convert_fusion
  22.8 13.9 %all_to_all.5 = bf16[8,4,32,128]{3,2,1,0:T(8,128)(2,1)S(1)} all-to-all(bf16[8,4,32,128]{3,2,1,0:T(8,128)(2,1)S(1)} %add_convert_fusion), channel_id=1, replica_groups=mesh['groups'=2,'space'=8,'modes'=2] {'space'}, dimensions={0} | all-to-all | bytes 524288 | tf_op jit(solution)/shard_map/all_to_all | solution.py:225
  36.8 0.7 %copy.5 = f32[32,4,128]{2,1,0:T(4,128)} copy(f32[32,4,128]{2,0,1:T(8,128)S(1)} %bitcast.1) | data formatting | bytes 131072 | tf_op jit(solution)/shard_map/transpose | solution.py:226
  (1 shorter events, 0.0 us)
Async XLA Ops:
  0.0 1.1 %copy-start = (bf16[128,3,1,8,128]{4,3,2,1,0:T(8,128)(2,1)S(1)}, bf16[128,3,1,8,128]{4,3,2,1,0:T(8,128)(2,1)}, u32[]{:S(2)}) copy-start(bf16[128,3,1,8,128]{4,3,2,1,0:T(8,128)(2,1)} %modes_ref.1) | copy-start | bytes 2359300
  1.1 0.7 %copy-start.1 = (s32[1,8,128]{2,1,0:T(8,128)S(1)}, s32[1,8,128]{2,1,0:T(8,128)}, u32[]{:S(2)}) copy-start(s32[1,8,128]{2,1,0:T(8,128)} %ids_ref.5) | copy-start | bytes 12292
  2.4 8.7 %collective-permute-start = (bf16[6,3,128,128]{3,2,1,0:T(8,128)(2,1)S(1)}, bf16[6,3,128,128]{3,2,1,0:T(8,128)(2,1)S(1)}, u32[]{:S(2)}, u32[]{:S(2)}) collective-permute-start(bf16[6,3,128,128]{3,2,1,0:T(8,128)(2,1)S(1)} %get-tuple-element.14), channel_id=1, source_target_pairs={{0,1},{1,0},{2,3},{3,2},{4,5},{5,4},{6,7},{7,6},{8,9},{9,8},{10,11... | collective-permute-start | bytes 1769480 | tf_op jit(solution)/shard_map/ppermute | solution.py:181
  2.9 15.5 %collective-permute-start.1 = (bf16[784,128]{1,0:T(8,128)(2,1)S(1)}, bf16[784,128]{1,0:T(8,128)(2,1)S(1)}, u32[]{:S(2)}, u32[]{:S(2)}) collective-permute-start(bf16[784,128]{1,0:T(8,128)(2,1)S(1)} %get-tuple-element.15), channel_id=1, source_target_pairs={{0,2},{1,3},{2,0},{3,1},{4,6},{5,7},{6,4},{7,5},{8,10},{9,11},{10,... | collective-permute-start | bytes 602120 | tf_op jit(solution)/shard_map/ppermute | solution.py:182
  5.5 5.7 %copy-start.2 = (s32[1,8,128]{2,1,0:T(8,128)S(1)}, s32[1,8,128]{2,1,0:T(8,128)}, u32[]{:S(2)}) copy-start(s32[1,8,128]{2,1,0:T(8,128)} %ids_ref.5) | copy-start | bytes 12292
  5.5 12.9 %collective-permute-start.3 = (bf16[784,128]{1,0:T(8,128)(2,1)S(1)}, bf16[784,128]{1,0:T(8,128)(2,1)S(1)}, u32[]{:S(2)}, u32[]{:S(2)}) collective-permute-start(bf16[784,128]{1,0:T(8,128)(2,1)S(1)} %get-tuple-element.17), channel_id=1, source_target_pairs={{4,0},{5,1},{8,4},{9,5},{12,8},{13,9},{2,6},{3,7},{6,10},{7,11},{1... | collective-permute-start | bytes 602120 | tf_op jit(solution)/shard_map/ppermute | solution.py:183
  6.9 8.1 %collective-permute-start.2 = (bf16[768,128]{1,0:T(8,128)(2,1)S(1)}, bf16[768,128]{1,0:T(8,128)(2,1)S(1)}, u32[]{:S(2)}, u32[]{:S(2)}) collective-permute-start(bf16[768,128]{1,0:T(8,128)(2,1)S(1)} %get-tuple-element.16), channel_id=1, source_target_pairs={{0,3},{1,2},{2,1},{3,0},{4,7},{5,6},{6,5},{7,4},{8,11},{9,10},{10,... | collective-permute-start | bytes 589832 | tf_op jit(solution)/shard_map/ppermute | solution.py:184
  9.2 9.2 %collective-permute-start.4 = (bf16[768,128]{1,0:T(8,128)(2,1)S(1)}, bf16[768,128]{1,0:T(8,128)(2,1)S(1)}, u32[]{:S(2)}, u32[]{:S(2)}) collective-permute-start(bf16[768,128]{1,0:T(8,128)(2,1)S(1)} %get-tuple-element.18), channel_id=1, source_target_pairs={{4,1},{5,0},{8,5},{9,4},{12,9},{13,8},{2,7},{3,6},{6,11},{7,10},{1... | collective-permute-start | bytes 589832 | tf_op jit(solution)/shard_map/ppermute | solution.py:185
  11.1 0.7 %copy-start.3 = (f32[16]{0:T(128)S(1)}, f32[16]{0:T(128)}, u32[]{:S(2)}) copy-start(f32[16]{0:T(128)} %table_ref.3) | copy-start | bytes 196
  20.7 2.0 %collective-permute-start.5 = (f32[8,4,32,128]{3,2,1,0:T(8,128)S(1)}, f32[8,4,32,128]{3,2,1,0:T(8,128)S(1)}, u32[]{:S(2)}, u32[]{:S(2)}) collective-permute-start(f32[8,4,32,128]{3,2,1,0:T(8,128)S(1)} %get-tuple-element.20), channel_id=1, source_target_pairs={{0,1},{1,0},{2,3},{3,2},{4,5},{5,4},{6,7},{7,6},{8,9},{9,8},{10,11... | collective-permute-start | bytes 1572872 | tf_op jit(solution)/shard_map/ppermute | solution.py:220

commit v2 on v1

--- a/solution.py
+++ b/solution.py
@@ -10,16 +10,33 @@
 JB = 4
 NW = 16
 IDROWS = 16
+LOADS = 4
 VMEM_LIMIT = 48 * 1024 * 1024
 
 
-def prep_kernel(modes_ref, ids_ref, own_ref, core_ref, xs_ref, xc_ref, zs_ref, zc_ref, tr):
+def prep_kernel(
+    modes_hbm, ids_hbm, own_ref, core_ref, xs_ref, xc_ref, zs_ref, zc_ref, modes_ref, ids_ref, tr, sems
+):
     m = lax.axis_index("modes")
     q = lax.rem(lax.axis_index("space"), 2)
-    nk, comps, _, nx, nz = modes_ref.shape
-    for c in range(comps):
-        value = modes_ref[:, c, 0].astype(jnp.float32)
-        tr[:, c] = jnp.swapaxes(value, 0, 1).astype(jnp.bfloat16)
+    nk, comps, _, nx, nz = modes_hbm.shape
+    step = nk // LOADS
+    copies = [
+        pltpu.make_async_copy(
+            modes_hbm.at[pl.ds(p * step, step)], modes_ref.at[pl.ds(p * step, step)], sems.at[p]
+        )
+        for p in range(LOADS)
+    ]
+    copies.append(pltpu.make_async_copy(ids_hbm, ids_ref, sems.at[LOADS]))
+    for copy in copies:
+        copy.start()
+    for p in range(LOADS):
+        copies[p].wait()
+        block = pl.ds(p * step, step)
+        for c in range(comps):
+            value = modes_ref[block, c, 0].astype(jnp.float32)
+            tr[:, c, block] = jnp.swapaxes(value, 0, 1).astype(jnp.bfloat16)
+    copies[LOADS].wait()
     quarter = nx // 4
     for r in range(nx // 2 + 2):
         own_ref[r] = tr[lax.rem(nx // 2 * m + nx - 1 + r, nx)]
@@ -96,11 +113,13 @@
 
 
 def cross_kernel(
-    chunk, own_ref, other_ref, xs_ref, xc_ref, zs_ref, zc_ref, ids_ref, table_ref, jb_ref, acc_ref,
+    chunk, planes, own_ref, other_ref, xs_ref, xc_ref, zs_ref, zc_ref, ids_ref, table_ref, jb_ref, acc_ref,
     keep_ref, send_ref, adv, wts, wscr,
 ):
     m = lax.axis_index("modes")
-    q = lax.rem(lax.axis_index("space"), 2)
+    plane = lax.axis_index("space")
+    q = lax.rem(plane, 2)
+    inside = jnp.where(jnp.logical_or(plane == 1, plane == planes - 2), 0.0, 1.0)
     sigma = jnp.where(q == 0, 0.5, -0.5)
     rows, comps, nk, nz = own_ref.shape
     rows -= 2
@@ -128,7 +147,7 @@
                 block = pl.ds(half * nk, nk)
                 f0 = p0[row0, c].astype(jnp.float32)
                 f1 = p1[src, :].astype(jnp.float32)
-                f2 = p2[src, :].astype(jnp.float32)
+                f2 = inside * p2[src, :].astype(jnp.float32)
                 gy = (sigma * (f2 - f0)).astype(jnp.bfloat16).astype(jnp.float32)
                 for part, (field, weight) in enumerate(((f0, weight0), (f1, weight1), (f2, weight2))):
                     wts[block, pl.ds(part * span + lane, nz)] = (weight * field).astype(jnp.bfloat16)
@@ -145,7 +164,24 @@
             for part in range(per_half):
                 piece = total[half * nk + part * chunk : half * nk + (part + 1) * chunk]
                 keep_ref[first + part, j] = piece[:, :nk]
-                send_ref[first + part, j] = piece[:, nk:]
+                send_ref[first + part, j] = piece[:, nk:].astype(jnp.bfloat16)
+
+
+def share_kernel(keep_ref, got_ref, mine_ref, *out_refs):
+    s = lax.axis_index("space")
+    mine_ref[...] = keep_ref[s] + got_ref[s].astype(jnp.float32)
+    for step, ref in enumerate(out_refs, 1):
+        to = jnp.bitwise_xor(s, step)
+        ref[...] = (keep_ref[to] + got_ref[to].astype(jnp.float32)).astype(jnp.bfloat16)
+
+
+def total_kernel(mine_ref, *refs):
+    *parts, out_ref = refs
+    total = mine_ref[...]
+    for ref in parts:
+        total = total + ref[...].astype(jnp.float32)
+    for j in range(JB):
+        out_ref[:, j, :] = total[j]
 
 
 def on_device(n, modes, weight_ids, weight_table, j_block):
@@ -153,6 +189,7 @@
     bf16, f32 = jnp.bfloat16, jnp.float32
     vmem = pl.BlockSpec(memory_space=pltpu.VMEM)
     smem = pl.BlockSpec(memory_space=pltpu.SMEM)
+    hbm = pl.BlockSpec(memory_space=pl.ANY)
     params = pltpu.CompilerParams(vmem_limit_bytes=VMEM_LIMIT)
     six = nx // 2 + 2
     body = nx // 4 * comps * nk
@@ -166,16 +203,21 @@
             jax.ShapeDtypeStruct((body + IDROWS, nz), bf16),
             jax.ShapeDtypeStruct((body, nz), bf16),
         ],
-        in_specs=[vmem, vmem],
+        in_specs=[hbm, hbm],
         out_specs=[vmem] * 6,
-        scratch_shapes=[pltpu.VMEM((nx, comps, nk, nz), bf16)],
+        scratch_shapes=[
+            pltpu.VMEM(modes.shape, bf16),
+            pltpu.VMEM(weight_ids.shape, jnp.int32),
+            pltpu.VMEM((nx, comps, nk, nz), bf16),
+            pltpu.SemaphoreType.DMA((LOADS + 1,)),
+        ],
         compiler_params=params,
         name="prep",
     )(modes, weight_ids)
 
     both = ("space", "modes")
     x_pairs = [(s, s ^ 1) for s in range(n)]
-    z_pairs = [(s, s - 2) for s in range(2, n, 2)] + [(s, s + 2) for s in range(1, n - 2, 2)]
+    z_pairs = [(s, (s + (2 if s % 2 else -2)) % n) for s in range(n)]
     same = lambda pairs: [(2 * a + m, 2 * b + m) for a, b in pairs for m in range(2)]
     cross = lambda pairs: [(2 * a + m, 2 * b + 1 - m) for a, b in pairs for m in range(2)]
     other = lax.ppermute(to_core, "modes", [(0, 1), (1, 0)])
@@ -203,8 +245,11 @@
     chunk = max(16, per_target)
     pieces = 2 * nk // chunk
     keep, send = pl.pallas_call(
-        functools.partial(cross_kernel, chunk),
-        out_shape=[jax.ShapeDtypeStruct((pieces, JB, chunk, nk), f32)] * 2,
+        functools.partial(cross_kernel, chunk, n),
+        out_shape=[
+            jax.ShapeDtypeStruct((pieces, JB, chunk, nk), f32),
+            jax.ShapeDtypeStruct((pieces, JB, chunk, nk), bf16),
+        ],
         in_specs=[vmem] * 7 + [smem, smem, vmem],
         out_specs=[vmem] * 2,
         scratch_shapes=[
@@ -218,6 +263,28 @@
     )(own, other, xs, xc, zs, zc, weight_ids, weight_table, j_block, acc)
 
     got = lax.ppermute(send, "modes", [(0, 1), (1, 0)])
+    if n in (2, 4, 8):
+        piece = (JB, chunk, nk)
+        mine, *shares = pl.pallas_call(
+            share_kernel,
+            out_shape=[jax.ShapeDtypeStruct(piece, f32)] + [jax.ShapeDtypeStruct(piece, bf16)] * (n - 1),
+            in_specs=[vmem] * 2,
+            out_specs=[vmem] * n,
+            compiler_params=params,
+            name="share",
+        )(keep, got)
+        parts = [
+            lax.ppermute(part, "space", [(s, s ^ step) for s in range(n)])
+            for step, part in enumerate(shares, 1)
+        ]
+        return pl.pallas_call(
+            total_kernel,
+            out_shape=jax.ShapeDtypeStruct((chunk, JB, nk), f32),
+            in_specs=[vmem] * n,
+            out_specs=vmem,
+            compiler_params=params,
+            name="total",
+        )(mine, *parts)
     share = (keep + got).astype(bf16)
     if chunk != per_target:
         share = share.reshape(pieces, JB, chunk // per_target, per_target, nk)

time: 37.7 us -> 40.1 us (1.064)
  blocking collectives: 13.9 us -> 0 us
  starting transfers between devices: 8.31 us -> 18.2 us
  waiting for transfers between devices: 5.42 us -> 11 us
  Pallas kernels: 5.81 us -> 7.52 us
  local copies, waits for them, and re-layouts: 3.13 us -> 2.45 us
    all_to_all x1 -> x0, blocking collectives: 13.9 us -> none  [on_device(): parts = lax.all_to_all(share, 'space', 0, 0, tiled=True)]
    ppermute x0 -> x7, starting transfers between devices: none -> 11.2 us  [on_device(): lax.ppermute(part, 'space', [(s, s ^ step) for s in range(n)])]
    ppermute x0 -> x7, waiting for transfers between devices: none -> 5.15 us  [on_device(): lax.ppermute(part, 'space', [(s, s ^ step) for s in range(n)])]
    ppermute x1, waiting for transfers between devices: 0.29 us -> 2.63 us  [on_device(): xc = lax.ppermute(xc, both, cross(x_pairs))]
    ppermute x1, starting transfers between devices: 2.29 us -> 0.01 us  [on_device(): xc = lax.ppermute(xc, both, cross(x_pairs))]
    ppermute x1, starting transfers between devices: 1.41 us -> 3.6 us  [on_device(): zs = lax.ppermute(zs, both, same(z_pairs))]
    ppermute x1, waiting for transfers between devices: 3.39 us -> 1.66 us  [on_device(): zc = lax.ppermute(zc, both, cross(z_pairs))]
    ppermute x1, starting transfers between devices: 1.28 us -> 0.25 us  [on_device(): zc = lax.ppermute(zc, both, cross(z_pairs))]
  transfers between devices with their start and end apart: 6 -> 13, of which waited for: 3 -> 6; matrix products, arithmetic and copies ran while one was open for 0% -> 0% of each run, Pallas kernels for 8% -> 7%
where the time goes in v2:
time: 40.1 us; the launch traced here: 39.9 us
  starting transfers between devices  18.2 us (45%)
  waiting for transfers between devices  11 us (27%)
  Pallas kernels  7.52 us (19%)
  local copies, waits for them, and re-layouts  2.45 us (6%)
  between operations  0.73 us (2%)
    ppermute x7, starting transfers between devices, on_device(): lax.ppermute(part, 'space', [(s, s ^ step) for s in range(n)])  11.2 us
    ppermute x7, waiting for transfers between devices, on_device(): lax.ppermute(part, 'space', [(s, s ^ step) for s in range(n)])  5.15 us
    ppermute x1, starting transfers between devices, on_device(): zs = lax.ppermute(zs, both, same(z_pairs))  3.6 us
    pallas_call x1, Pallas kernels, on_device(): pl.pallas_call(local_kernel, out_shape=jax.ShapeDtypeStruct((JB, 2 * nk,...  2.93 us
    ppermute x1, waiting for transfers between devices, on_device(): xc = lax.ppermute(xc, both, cross(x_pairs))  2.63 us
    ppermute x1, starting transfers between devices, on_device(): xs = lax.ppermute(xs, both, same(x_pairs))  2.56 us
    unnamed x8, local copies, waits for them, and re-layouts  2.45 us
    pallas_call x1, Pallas kernels, on_device(): pl.pallas_call(functools.partial(cross_kernel, chunk, n), out_shape=[jax....  2.34 us
  transfers between devices with their start and end apart: 13, of which 6 were waited for; matrix products, arithmetic and copies ran while one was open for 0% of the time, Pallas kernels for 7%

profile of v2, /device:TPU:0, one launch (start us, length us, event | category | flops | bytes accessed | tf_op | source)
XLA Modules:
  0.0 39.9 jit_solution(8782571356555085251)
XLA Ops:
  0.0 0.0 copy-start
  0.0 1.1 %copy-done = bf16[128,3,1,8,128]{4,3,2,1,0:T(8,128)(2,1)S(1)} copy-done((bf16[128,3,1,8,128]{4,3,2,1,0:T(8,128)(2,1)S(1)}, bf16[128,3,1,8,128]{4,3,2,1,0:T(8,128)(2,1)}, u32[]{:S(2)}) %copy-start) | copy-done | bytes 786456
  1.1 0.0 copy-start.1
  1.1 0.7 %copy-done.1 = s32[1,8,128]{2,1,0:T(8,128)S(1)} copy-done((s32[1,8,128]{2,1,0:T(8,128)S(1)}, s32[1,8,128]{2,1,0:T(8,128)}, u32[]{:S(2)}) %copy-start.1) | copy-done | bytes 4120
  1.8 1.5 %prep.1 = (bf16[6,3,128,128]{3,2,1,0:T(8,128)(2,1)S(1)}, bf16[6,3,128,128]{3,2,1,0:T(8,128)(2,1)S(1)}, bf16[784,128]{1,0:T(8,128)(2,1)S(1)}, bf16[768,128]{1,0:T...) custom-call(bf16[128,3,1,8,128]{4,3,2,1,0:T(8,128)(2,1)S(1)} %copy-done, ...), custom_call_target="tpu_custom_call" | custom-call | tf_op jit(solution)/shard_map/prep/pallas_call | solution.py:196
  3.3 0.5 %collective-permute-start = (bf16[6,3,128,128]{3,2,1,0:T(8,128)(2,1)S(1)}, bf16[6,3,128,128]{3,2,1,0:T(8,128)(2,1)S(1)}, u32[]{:S(2)}, u32[]{:S(2)}) collective-permute-start(bf16[6,3,128,128]{3,2,1,0:T(8,128)(2,1)S(1)} %get-tuple-element.22), channel_id=1, source_target_pairs={{0,1},{1,0},{2,3},{3,2},{4,5},{5,4},{6,7},{7,6},{8,9},{9,8},{10,11... | collective-permute-start | bytes 1769480 | tf_op jit(solution)/shard_map/ppermute | solution.py:223
  3.9 2.6 %collective-permute-start.1 = (bf16[784,128]{1,0:T(8,128)(2,1)S(1)}, bf16[784,128]{1,0:T(8,128)(2,1)S(1)}, u32[]{:S(2)}, u32[]{:S(2)}) collective-permute-start(bf16[784,128]{1,0:T(8,128)(2,1)S(1)} %get-tuple-element.23), channel_id=1, source_target_pairs={{0,2},{1,3},{2,0},{3,1},{4,6},{5,7},{6,4},{7,5},{8,10},{9,11},{10,... | collective-permute-start | bytes 602120 | tf_op jit(solution)/shard_map/ppermute | solution.py:224
  6.4 0.0 copy-start.2
  6.4 3.6 %collective-permute-start.3 = (bf16[784,128]{1,0:T(8,128)(2,1)S(1)}, bf16[784,128]{1,0:T(8,128)(2,1)S(1)}, u32[]{:S(2)}, u32[]{:S(2)}) collective-permute-start(bf16[784,128]{1,0:T(8,128)(2,1)S(1)} %get-tuple-element.25), channel_id=1, source_target_pairs={{0,12},{1,13},{2,6},{3,7},{4,0},{5,1},{6,10},{7,11},{8,4},{9,5},{1... | collective-permute-start | bytes 602120 | tf_op jit(solution)/shard_map/ppermute | solution.py:225
  10.0 0.0 collective-permute-start.2
  10.0 0.3 collective-permute-start.4
  10.9 0.0 copy-start.3
  10.9 0.0 collective-permute-done.other_ref
  11.0 0.0 copy-done.2
  11.0 0.6 %copy-done.3 = f32[16]{0:T(128)S(1)} copy-done((f32[16]{0:T(128)S(1)}, f32[16]{0:T(128)}, u32[]{:S(2)}) %copy-start.3) | copy-done | bytes 88
  11.6 2.9 %local.1.acc_ref = f32[4,256,256]{2,1,0:T(8,128)S(1)} custom-call(bf16[6,3,128,128]{3,2,1,0:T(8,128)(2,1)S(1)} %get-tuple-element.21.own_ref, bf16[6,3,128,128]{3,2,1,0:T(8,128)(2,1)S(1)} %collective-permute-done.other_ref, s32[1,8,128]{2,1,0:T(8,128)S(1)} %copy-done.2, f32[16]{0:T(128)S(1)} %copy-done.3, s32[1]{0:T(128)S(6)} %copy.5.jb_ref), custom_call_target="tpu_custom_call" | custom-call | flops 900000000 | bytes 2400000 | tf_op jit(solution)/shard_map/local/pallas_call | solution.py:229
  14.5 2.6 %collective-permute-done.2.xc_ref = bf16[768,128]{1,0:T(8,128)(2,1)S(1)} collective-permute-done((bf16[768,128]{1,0:T(8,128)(2,1)S(1)}, bf16[768,128]{1,0:T(8,128)(2,1)S(1)}, u32[]{:S(2)}, u32[]{:S(2)}) %collective-permute-start.2) | collective-permute-done | bytes 196640 | tf_op jit(solution)/shard_map/ppermute | solution.py:226
  17.2 1.7 %collective-permute-done.4.zc_ref = bf16[768,128]{1,0:T(8,128)(2,1)S(1)} collective-permute-done((bf16[768,128]{1,0:T(8,128)(2,1)S(1)}, bf16[768,128]{1,0:T(8,128)(2,1)S(1)}, u32[]{:S(2)}, u32[]{:S(2)}) %collective-permute-start.4) | collective-permute-done | bytes 196640 | tf_op jit(solution)/shard_map/ppermute | solution.py:227
  18.8 0.0 collective-permute-done.1.xs_ref
  18.8 0.0 collective-permute-done.3.zs_ref
  18.8 2.3 %cross.1 = (f32[8,4,32,128]{3,2,1,0:T(8,128)S(1)}, bf16[8,4,32,128]{3,2,1,0:T(8,128)(2,1)S(1)}) custom-call(bf16[6,3,128,128]{3,2,1,0:T(8,128)(2,1)S(1)} %get-tuple-element.21.own_ref, bf16[6,3,128,128]{3,2,1,0:T(8,128)(2,1)S(1)} %collective-permute-done.other_ref, bf16[784,128]{1,0:T(8,128)(2,1)S(1)} %collective-permute-done.1.xs_ref, ...), custom_call_target="tpu_custom_call" | custom-call | flops 1300000000 | bytes 4000000 | tf_op jit(solution)/shard_map/cross/pallas_call | solution.py:247
  21.2 0.1 collective-permute-start.5
  21.3 1.5 %collective-permute-done.5.got_ref = bf16[8,4,32,128]{3,2,1,0:T(8,128)(2,1)S(1)} collective-permute-done((bf16[8,4,32,128]{3,2,1,0:T(8,128)(2,1)S(1)}, bf16[8,4,32,128]{3,2,1,0:T(8,128)(2,1)S(1)}, u32[]{:S(2)}, u32[]{:S(2)}) %collective-permute-start.5) | collective-permute-done | bytes 262176 | tf_op jit(solution)/shard_map/ppermute | solution.py:265
  22.8 1.3 %collective-permute-start.6 = (bf16[4,32,128]{2,1,0:T(8,128)(2,1)S(1)}, bf16[4,32,128]{2,1,0:T(8,128)(2,1)S(1)}, u32[]{:S(2)}, u32[]{:S(2)}) collective-permute-start(bf16[4,32,128]{2,1,0:T(8,128)(2,1)S(1)} %get-tuple-element.30), channel_id=1, source_target_pairs={{0,2},{2,0},{4,6},{6,4},{8,10},{10,8},{12,14},{14,12},{1,3},{3,1},... | collective-permute-start | bytes 98312 | tf_op jit(solution)/shard_map/ppermute | solution.py:277
  24.1 0.0 collective-permute-start.7
  24.1 2.3 %collective-permute-start.8 = (bf16[4,32,128]{2,1,0:T(8,128)(2,1)S(1)}, bf16[4,32,128]{2,1,0:T(8,128)(2,1)S(1)}, u32[]{:S(2)}, u32[]{:S(2)}) collective-permute-start(bf16[4,32,128]{2,1,0:T(8,128)(2,1)S(1)} %get-tuple-element.32), channel_id=1, source_target_pairs={{0,6},{2,4},{4,2},{6,0},{8,14},{10,12},{12,10},{14,8},{1,7},{3,5},... | collective-permute-start | bytes 98312 | tf_op jit(solution)/shard_map/ppermute | solution.py:277
  26.4 2.3 %collective-permute-start.9 = (bf16[4,32,128]{2,1,0:T(8,128)(2,1)S(1)}, bf16[4,32,128]{2,1,0:T(8,128)(2,1)S(1)}, u32[]{:S(2)}, u32[]{:S(2)}) collective-permute-start(bf16[4,32,128]{2,1,0:T(8,128)(2,1)S(1)} %get-tuple-element.33), channel_id=1, source_target_pairs={{0,8},{2,10},{4,12},{6,14},{8,0},{10,2},{12,4},{14,6},{1,9},{3,11}... | collective-permute-start | bytes 98312 | tf_op jit(solution)/shard_map/ppermute | solution.py:277
  28.7 1.3 %collective-permute-start.10 = (bf16[4,32,128]{2,1,0:T(8,128)(2,1)S(1)}, bf16[4,32,128]{2,1,0:T(8,128)(2,1)S(1)}, u32[]{:S(2)}, u32[]{:S(2)}) collective-permute-start(bf16[4,32,128]{2,1,0:T(8,128)(2,1)S(1)} %get-tuple-element.34), channel_id=1, source_target_pairs={{0,10},{2,8},{4,14},{6,12},{8,2},{10,0},{12,6},{14,4},{1,11},{3,9}... | collective-permute-start | bytes 98312 | tf_op jit(solution)/shard_map/ppermute | solution.py:277
  29.9 0.0 collective-permute-done.6.refs_0_
  29.9 2.6 %collective-permute-start.11 = (bf16[4,32,128]{2,1,0:T(8,128)(2,1)S(1)}, bf16[4,32,128]{2,1,0:T(8,128)(2,1)S(1)}, u32[]{:S(2)}, u32[]{:S(2)}) collective-permute-start(bf16[4,32,128]{2,1,0:T(8,128)(2,1)S(1)} %get-tuple-element.35), channel_id=1, source_target_pairs={{0,12},{2,14},{4,8},{6,10},{8,4},{10,6},{12,0},{14,2},{1,13},{3,15... | collective-permute-start | bytes 98312 | tf_op jit(solution)/shard_map/ppermute | solution.py:277
  32.6 0.0 collective-permute-done.7.refs_1_
  32.6 1.5 %collective-permute-start.12 = (bf16[4,32,128]{2,1,0:T(8,128)(2,1)S(1)}, bf16[4,32,128]{2,1,0:T(8,128)(2,1)S(1)}, u32[]{:S(2)}, u32[]{:S(2)}) collective-permute-start(bf16[4,32,128]{2,1,0:T(8,128)(2,1)S(1)} %get-tuple-element.36), channel_id=1, source_target_pairs={{0,14},{2,12},{4,10},{6,8},{8,6},{10,4},{12,2},{14,0},{1,15},{3,13... | collective-permute-start | bytes 98312 | tf_op jit(solution)/shard_map/ppermute | solution.py:277
  34.0 0.0 collective-permute-done.8.refs_2_
  34.0 0.0 collective-permute-done.9.refs_3_
  34.0 1.1 %collective-permute-done.10.refs_4_ = bf16[4,32,128]{2,1,0:T(8,128)(2,1)S(1)} collective-permute-done((bf16[4,32,128]{2,1,0:T(8,128)(2,1)S(1)}, bf16[4,32,128]{2,1,0:T(8,128)(2,1)S(1)}, u32[]{:S(2)}, u32[]{:S(2)}) %collective-permute-start.10) | collective-permute-done | bytes 32800 | tf_op jit(solution)/shard_map/ppermute | solution.py:277
  35.1 0.5 %collective-permute-done.11.refs_5_ = bf16[4,32,128]{2,1,0:T(8,128)(2,1)S(1)} collective-permute-done((bf16[4,32,128]{2,1,0:T(8,128)(2,1)S(1)}, bf16[4,32,128]{2,1,0:T(8,128)(2,1)S(1)}, u32[]{:S(2)}, u32[]{:S(2)}) %collective-permute-start.11) | collective-permute-done | bytes 32800 | tf_op jit(solution)/shard_map/ppermute | solution.py:277
  35.6 3.5 %collective-permute-done.12.refs_6_ = bf16[4,32,128]{2,1,0:T(8,128)(2,1)S(1)} collective-permute-done((bf16[4,32,128]{2,1,0:T(8,128)(2,1)S(1)}, bf16[4,32,128]{2,1,0:T(8,128)(2,1)S(1)}, u32[]{:S(2)}, u32[]{:S(2)}) %collective-permute-start.12) | collective-permute-done | bytes 32800 | tf_op jit(solution)/shard_map/ppermute | solution.py:277
  39.2 0.7 %total.1 = f32[32,4,128]{2,1,0:T(4,128)} custom-call(f32[4,32,128]{2,1,0:T(8,128)S(1)} %get-tuple-element.29.mine_ref, bf16[4,32,128]{2,1,0:T(8,128)(2,1)S(1)} %collective-permute-done.6.refs_0_, bf16[4,32,128]{2,1,0:T(8,128)(2,1)S(1)} %collective-permute-done.7.refs_1_, bf16[4,32,128]{2,1,0:T(8,128)(2,1)S(1)} %collective-permute-done.8.refs_2_, ...), custom_call_target="tpu_custom_call" | custom-call | tf_op jit(solution)/shard_map/total/pallas_call | solution.py:280
  (1 shorter events, 0.0 us)
Async XLA Ops:
  0.0 1.1 %copy-start = (bf16[128,3,1,8,128]{4,3,2,1,0:T(8,128)(2,1)S(1)}, bf16[128,3,1,8,128]{4,3,2,1,0:T(8,128)(2,1)}, u32[]{:S(2)}) copy-start(bf16[128,3,1,8,128]{4,3,2,1,0:T(8,128)(2,1)} %modes_hbm.1) | copy-start | bytes 2359300
  1.1 0.7 %copy-start.1 = (s32[1,8,128]{2,1,0:T(8,128)S(1)}, s32[1,8,128]{2,1,0:T(8,128)}, u32[]{:S(2)}) copy-start(s32[1,8,128]{2,1,0:T(8,128)} %ids_ref.3) | copy-start | bytes 12292
  3.3 7.6 %collective-permute-start = (bf16[6,3,128,128]{3,2,1,0:T(8,128)(2,1)S(1)}, bf16[6,3,128,128]{3,2,1,0:T(8,128)(2,1)S(1)}, u32[]{:S(2)}, u32[]{:S(2)}) collective-permute-start(bf16[6,3,128,128]{3,2,1,0:T(8,128)(2,1)S(1)} %get-tuple-element.22), channel_id=1, source_target_pairs={{0,1},{1,0},{2,3},{3,2},{4,5},{5,4},{6,7},{7,6},{8,9},{9,8},{10,11... | collective-permute-start | bytes 1769480 | tf_op jit(solution)/shard_map/ppermute | solution.py:223
  3.9 15.0 %collective-permute-start.1 = (bf16[784,128]{1,0:T(8,128)(2,1)S(1)}, bf16[784,128]{1,0:T(8,128)(2,1)S(1)}, u32[]{:S(2)}, u32[]{:S(2)}) collective-permute-start(bf16[784,128]{1,0:T(8,128)(2,1)S(1)} %get-tuple-element.23), channel_id=1, source_target_pairs={{0,2},{1,3},{2,0},{3,1},{4,6},{5,7},{6,4},{7,5},{8,10},{9,11},{10,... | collective-permute-start | bytes 602120 | tf_op jit(solution)/shard_map/ppermute | solution.py:224
  6.4 4.5 %copy-start.2 = (s32[1,8,128]{2,1,0:T(8,128)S(1)}, s32[1,8,128]{2,1,0:T(8,128)}, u32[]{:S(2)}) copy-start(s32[1,8,128]{2,1,0:T(8,128)} %ids_ref.3) | copy-start | bytes 12292
  6.4 12.4 %collective-permute-start.3 = (bf16[784,128]{1,0:T(8,128)(2,1)S(1)}, bf16[784,128]{1,0:T(8,128)(2,1)S(1)}, u32[]{:S(2)}, u32[]{:S(2)}) collective-permute-start(bf16[784,128]{1,0:T(8,128)(2,1)S(1)} %get-tuple-element.25), channel_id=1, source_target_pairs={{0,12},{1,13},{2,6},{3,7},{4,0},{5,1},{6,10},{7,11},{8,4},{9,5},{1... | collective-permute-start | bytes 602120 | tf_op jit(solution)/shard_map/ppermute | solution.py:225
  10.0 7.1 %collective-permute-start.2 = (bf16[768,128]{1,0:T(8,128)(2,1)S(1)}, bf16[768,128]{1,0:T(8,128)(2,1)S(1)}, u32[]{:S(2)}, u32[]{:S(2)}) collective-permute-start(bf16[768,128]{1,0:T(8,128)(2,1)S(1)} %get-tuple-element.24), channel_id=1, source_target_pairs={{0,3},{1,2},{2,1},{3,0},{4,7},{5,6},{6,5},{7,4},{8,11},{9,10},{10,... | collective-permute-start | bytes 589832 | tf_op jit(solution)/shard_map/ppermute | solution.py:226
  10.0 8.8 %collective-permute-start.4 = (bf16[768,128]{1,0:T(8,128)(2,1)S(1)}, bf16[768,128]{1,0:T(8,128)(2,1)S(1)}, u32[]{:S(2)}, u32[]{:S(2)}) collective-permute-start(bf16[768,128]{1,0:T(8,128)(2,1)S(1)} %get-tuple-element.26), channel_id=1, source_target_pairs={{0,13},{1,12},{2,7},{3,6},{4,1},{5,0},{6,11},{7,10},{8,5},{9,4},{1... | collective-permute-start | bytes 589832 | tf_op jit(solution)/shard_map/ppermute | solution.py:227
  10.9 0.7 %copy-start.3 = (f32[16]{0:T(128)S(1)}, f32[16]{0:T(128)}, u32[]{:S(2)}) copy-start(f32[16]{0:T(128)} %table_ref.3) | copy-start | bytes 196
  21.2 1.6 %collective-permute-start.5 = (bf16[8,4,32,128]{3,2,1,0:T(8,128)(2,1)S(1)}, bf16[8,4,32,128]{3,2,1,0:T(8,128)(2,1)S(1)}, u32[]{:S(2)}, u32[]{:S(2)}) collective-permute-start(bf16[8,4,32,128]{3,2,1,0:T(8,128)(2,1)S(1)} %get-tuple-element.28), channel_id=1, source_target_pairs={{0,1},{1,0},{2,3},{3,2},{4,5},{5,4},{6,7},{7,6},{8,9},{9,8},{10,11... | collective-permute-start | bytes 786440 | tf_op jit(solution)/shard_map/ppermute | solution.py:265
  22.8 7.1 %collective-permute-start.6 = (bf16[4,32,128]{2,1,0:T(8,128)(2,1)S(1)}, bf16[4,32,128]{2,1,0:T(8,128)(2,1)S(1)}, u32[]{:S(2)}, u32[]{:S(2)}) collective-permute-start(bf16[4,32,128]{2,1,0:T(8,128)(2,1)S(1)} %get-tuple-element.30), channel_id=1, source_target_pairs={{0,2},{2,0},{4,6},{6,4},{8,10},{10,8},{12,14},{14,12},{1,3},{3,1},... | collective-permute-start | bytes 98312 | tf_op jit(solution)/shard_map/ppermute | solution.py:277
  24.1 8.5 %collective-permute-start.7 = (bf16[4,32,128]{2,1,0:T(8,128)(2,1)S(1)}, bf16[4,32,128]{2,1,0:T(8,128)(2,1)S(1)}, u32[]{:S(2)}, u32[]{:S(2)}) collective-permute-start(bf16[4,32,128]{2,1,0:T(8,128)(2,1)S(1)} %get-tuple-element.31), channel_id=1, source_target_pairs={{0,4},{2,6},{4,0},{6,2},{8,12},{10,14},{12,8},{14,10},{1,5},{3,7},... | collective-permute-start | bytes 98312 | tf_op jit(solution)/shard_map/ppermute | solution.py:277
  24.1 10.0 %collective-permute-start.8 = (bf16[4,32,128]{2,1,0:T(8,128)(2,1)S(1)}, bf16[4,32,128]{2,1,0:T(8,128)(2,1)S(1)}, u32[]{:S(2)}, u32[]{:S(2)}) collective-permute-start(bf16[4,32,128]{2,1,0:T(8,128)(2,1)S(1)} %get-tuple-element.32), channel_id=1, source_target_pairs={{0,6},{2,4},{4,2},{6,0},{8,14},{10,12},{12,10},{14,8},{1,7},{3,5},... | collective-permute-start | bytes 98312 | tf_op jit(solution)/shard_map/ppermute | solution.py:277
  26.4 7.7 %collective-permute-start.9 = (bf16[4,32,128]{2,1,0:T(8,128)(2,1)S(1)}, bf16[4,32,128]{2,1,0:T(8,128)(2,1)S(1)}, u32[]{:S(2)}, u32[]{:S(2)}) collective-permute-start(bf16[4,32,128]{2,1,0:T(8,128)(2,1)S(1)} %get-tuple-element.33), channel_id=1, source_target_pairs={{0,8},{2,10},{4,12},{6,14},{8,0},{10,2},{12,4},{14,6},{1,9},{3,11}... | collective-permute-start | bytes 98312 | tf_op jit(solution)/shard_map/ppermute | solution.py:277
  28.7 6.5 %collective-permute-start.10 = (bf16[4,32,128]{2,1,0:T(8,128)(2,1)S(1)}, bf16[4,32,128]{2,1,0:T(8,128)(2,1)S(1)}, u32[]{:S(2)}, u32[]{:S(2)}) collective-permute-start(bf16[4,32,128]{2,1,0:T(8,128)(2,1)S(1)} %get-tuple-element.34), channel_id=1, source_target_pairs={{0,10},{2,8},{4,14},{6,12},{8,2},{10,0},{12,6},{14,4},{1,11},{3,9}... | collective-permute-start | bytes 98312 | tf_op jit(solution)/shard_map/ppermute | solution.py:277
  29.9 5.7 %collective-permute-start.11 = (bf16[4,32,128]{2,1,0:T(8,128)(2,1)S(1)}, bf16[4,32,128]{2,1,0:T(8,128)(2,1)S(1)}, u32[]{:S(2)}, u32[]{:S(2)}) collective-permute-start(bf16[4,32,128]{2,1,0:T(8,128)(2,1)S(1)} %get-tuple-element.35), channel_id=1, source_target_pairs={{0,12},{2,14},{4,8},{6,10},{8,4},{10,6},{12,0},{14,2},{1,13},{3,15... | collective-permute-start | bytes 98312 | tf_op jit(solution)/shard_map/ppermute | solution.py:277
  32.6 6.6 %collective-permute-start.12 = (bf16[4,32,128]{2,1,0:T(8,128)(2,1)S(1)}, bf16[4,32,128]{2,1,0:T(8,128)(2,1)S(1)}, u32[]{:S(2)}, u32[]{:S(2)}) collective-permute-start(bf16[4,32,128]{2,1,0:T(8,128)(2,1)S(1)} %get-tuple-element.36), channel_id=1, source_target_pairs={{0,14},{2,12},{4,10},{6,8},{8,6},{10,4},{12,2},{14,0},{1,15},{3,13... | collective-permute-start | bytes 98312 | tf_op jit(solution)/shard_map/ppermute | solution.py:277

commit v3 on v2

--- a/solution.py
+++ b/solution.py
@@ -11,6 +11,7 @@
 NW = 16
 IDROWS = 16
 LOADS = 4
+NEAR = 4
 VMEM_LIMIT = 48 * 1024 * 1024
 
 
@@ -120,6 +121,7 @@
     plane = lax.axis_index("space")
     q = lax.rem(plane, 2)
     inside = jnp.where(jnp.logical_or(plane == 1, plane == planes - 2), 0.0, 1.0)
+    inside = inside.astype(jnp.bfloat16)
     sigma = jnp.where(q == 0, 0.5, -0.5)
     rows, comps, nk, nz = own_ref.shape
     rows -= 2
@@ -135,9 +137,9 @@
         idrow = IDROWS // quarter * r
         weight1, weight2 = w1[idrow : idrow + 1], w2[idrow : idrow + 1]
         along = pl.ds((r * comps + 1) * nk, nk)
-        phi0 = sigma * picked(pick, own_ref[row0, 1], other_ref[row0, 1])
-        phi1 = picked(pick, xs_ref[along, :], xc_ref[along, :])
-        phi2 = -sigma * picked(pick, zs_ref[along, :], zc_ref[along, :])
+        phi0 = (sigma * picked(pick, own_ref[row0, 1], other_ref[row0, 1])).astype(jnp.bfloat16)
+        phi1 = (sigma * picked(pick, xs_ref[along, :], xc_ref[along, :])).astype(jnp.bfloat16)
+        phi2 = (-sigma * picked(pick, zs_ref[along, :], zc_ref[along, :])).astype(jnp.bfloat16)
         for c in range(comps):
             lane = (r * comps + c) * nz
             src = pl.ds((r * comps + c) * nk, nk)
@@ -145,17 +147,17 @@
                 ((own_ref, xs_ref, zs_ref), (other_ref, xc_ref, zc_ref))
             ):
                 block = pl.ds(half * nk, nk)
-                f0 = p0[row0, c].astype(jnp.float32)
-                f1 = p1[src, :].astype(jnp.float32)
-                f2 = inside * p2[src, :].astype(jnp.float32)
-                gy = (sigma * (f2 - f0)).astype(jnp.bfloat16).astype(jnp.float32)
+                f0 = p0[row0, c]
+                f1 = p1[src, :]
+                f2 = inside * p2[src, :]
+                gy = f2 - f0
                 for part, (field, weight) in enumerate(((f0, weight0), (f1, weight1), (f2, weight2))):
-                    wts[block, pl.ds(part * span + lane, nz)] = (weight * field).astype(jnp.bfloat16)
+                    wts[block, pl.ds(part * span + lane, nz)] = (
+                        weight * field.astype(jnp.float32)
+                    ).astype(jnp.bfloat16)
                 for j in range(JB):
                     for part, (phi, field) in enumerate(((phi0, f1), (phi1, gy), (phi2, f1))):
-                        adv[j, block, pl.ds(part * span + lane, nz)] = (
-                            phi[j : j + 1] * field
-                        ).astype(jnp.bfloat16)
+                        adv[j, block, pl.ds(part * span + lane, nz)] = phi[j : j + 1] * field
     per_half = nk // chunk
     for j in range(JB):
         total = acc_ref[j] + dot_nt(adv[j], wts[...])
@@ -167,19 +169,27 @@
                 send_ref[first + part, j] = piece[:, nk:].astype(jnp.bfloat16)
 
 
-def share_kernel(keep_ref, got_ref, mine_ref, *out_refs):
+def near_kernel(keep_ref, got_ref, mine_ref, *out_refs):
     s = lax.axis_index("space")
-    mine_ref[...] = keep_ref[s] + got_ref[s].astype(jnp.float32)
-    for step, ref in enumerate(out_refs, 1):
-        to = jnp.bitwise_xor(s, step)
-        ref[...] = (keep_ref[to] + got_ref[to].astype(jnp.float32)).astype(jnp.bfloat16)
-
-
-def total_kernel(mine_ref, *refs):
-    *parts, out_ref = refs
-    total = mine_ref[...]
-    for ref in parts:
-        total = total + ref[...].astype(jnp.float32)
+    low = lax.rem(s, NEAR)
+    for step, ref in enumerate((mine_ref,) + out_refs):
+        for level in range(mine_ref.shape[0]):
+            to = NEAR * level + jnp.bitwise_xor(low, step)
+            ref[level] = (keep_ref[to] + got_ref[to].astype(jnp.float32)).astype(ref.dtype)
+
+
+def far_kernel(mine_ref, *refs):
+    *parts, keep_ref, send_ref = refs
+    level = lax.div(lax.axis_index("space"), NEAR)
+    for ref, at in ((keep_ref, level), (send_ref, 1 - level)):
+        total = mine_ref[at]
+        for part in parts:
+            total = total + part[at].astype(jnp.float32)
+        ref[...] = total.astype(ref.dtype)
+
+
+def total_kernel(keep_ref, got_ref, out_ref):
+    total = keep_ref[...] + got_ref[...].astype(jnp.float32)
     for j in range(JB):
         out_ref[:, j, :] = total[j]
 
@@ -189,7 +199,7 @@
     bf16, f32 = jnp.bfloat16, jnp.float32
     vmem = pl.BlockSpec(memory_space=pltpu.VMEM)
     smem = pl.BlockSpec(memory_space=pltpu.SMEM)
-    hbm = pl.BlockSpec(memory_space=pl.ANY)
+    hbm = pl.BlockSpec(memory_space=pltpu.HBM)
     params = pltpu.CompilerParams(vmem_limit_bytes=VMEM_LIMIT)
     six = nx // 2 + 2
     body = nx // 4 * comps * nk
@@ -220,11 +230,11 @@
     z_pairs = [(s, (s + (2 if s % 2 else -2)) % n) for s in range(n)]
     same = lambda pairs: [(2 * a + m, 2 * b + m) for a, b in pairs for m in range(2)]
     cross = lambda pairs: [(2 * a + m, 2 * b + 1 - m) for a, b in pairs for m in range(2)]
+    xs = lax.ppermute(xs, both, same(x_pairs))
+    xc = lax.ppermute(xc, both, cross(x_pairs))
+    zs = lax.ppermute(zs, both, same(z_pairs))
+    zc = lax.ppermute(zc, both, cross(z_pairs))
     other = lax.ppermute(to_core, "modes", [(0, 1), (1, 0)])
-    xs = lax.ppermute(xs, both, same(x_pairs))
-    zs = lax.ppermute(zs, both, same(z_pairs))
-    xc = lax.ppermute(xc, both, cross(x_pairs))
-    zc = lax.ppermute(zc, both, cross(z_pairs))
 
     acc = pl.pallas_call(
         local_kernel,
@@ -263,28 +273,38 @@
     )(own, other, xs, xc, zs, zc, weight_ids, weight_table, j_block, acc)
 
     got = lax.ppermute(send, "modes", [(0, 1), (1, 0)])
-    if n in (2, 4, 8):
+    if n == 2 * NEAR:
         piece = (JB, chunk, nk)
         mine, *shares = pl.pallas_call(
-            share_kernel,
-            out_shape=[jax.ShapeDtypeStruct(piece, f32)] + [jax.ShapeDtypeStruct(piece, bf16)] * (n - 1),
+            near_kernel,
+            out_shape=[jax.ShapeDtypeStruct((2, *piece), f32)]
+            + [jax.ShapeDtypeStruct((2, *piece), bf16)] * (NEAR - 1),
             in_specs=[vmem] * 2,
-            out_specs=[vmem] * n,
+            out_specs=[vmem] * NEAR,
             compiler_params=params,
-            name="share",
+            name="near",
         )(keep, got)
         parts = [
             lax.ppermute(part, "space", [(s, s ^ step) for s in range(n)])
             for step, part in enumerate(shares, 1)
         ]
+        keep, send = pl.pallas_call(
+            far_kernel,
+            out_shape=[jax.ShapeDtypeStruct(piece, f32), jax.ShapeDtypeStruct(piece, bf16)],
+            in_specs=[vmem] * NEAR,
+            out_specs=[vmem] * 2,
+            compiler_params=params,
+            name="far",
+        )(mine, *parts)
+        got = lax.ppermute(send, "space", [(s, s ^ NEAR) for s in range(n)])
         return pl.pallas_call(
             total_kernel,
             out_shape=jax.ShapeDtypeStruct((chunk, JB, nk), f32),
-            in_specs=[vmem] * n,
+            in_specs=[vmem] * 2,
             out_specs=vmem,
             compiler_params=params,
             name="total",
-        )(mine, *parts)
+        )(keep, got)
     share = (keep + got).astype(bf16)
     if chunk != per_target:
         share = share.reshape(pieces, JB, chunk // per_target, per_target, nk)

time: 40.1 us -> 35.4 us (0.88)
  starting transfers between devices: 18.2 us -> 13.3 us
    ppermute x7 -> x3, starting transfers between devices: 11.2 us -> 3.55 us  [on_device(): lax.ppermute(part, 'space', [(s, s ^ step) for s in range(n)])]
    ppermute x0 -> x1, starting transfers between devices: none -> 2.74 us  [on_device(): got = lax.ppermute(send, 'space', [(s, s ^ NEAR) for s in range(n)])]
    ppermute x0 -> x1, waiting for transfers between devices: none -> 2.13 us  [on_device(): got = lax.ppermute(send, 'space', [(s, s ^ NEAR) for s in range(n)])]
    ppermute x7 -> x3, waiting for transfers between devices: 5.15 us -> 3.38 us  [on_device(): lax.ppermute(part, 'space', [(s, s ^ step) for s in range(n)])]
  transfers between devices with their start and end apart: 13 -> 10, of which waited for: 6 -> 7; matrix products, arithmetic and copies ran while one was open for 0% -> 0% of each run, Pallas kernels for 7% -> 8%
where the time goes in v3:
time: 35.4 us; the launch traced here: 35.2 us
  starting transfers between devices  13.3 us (38%)
  waiting for transfers between devices  11.3 us (32%)
  Pallas kernels  7.42 us (21%)
  local copies, waits for them, and re-layouts  2.45 us (7%)
  between operations  0.73 us (2%)
    ppermute x1, starting transfers between devices, on_device(): zs = lax.ppermute(zs, both, same(z_pairs))  3.6 us
    ppermute x3, starting transfers between devices, on_device(): lax.ppermute(part, 'space', [(s, s ^ step) for s in range(n)])  3.55 us
    ppermute x3, waiting for transfers between devices, on_device(): lax.ppermute(part, 'space', [(s, s ^ step) for s in range(n)])  3.38 us
    pallas_call x1, Pallas kernels, on_device(): pl.pallas_call(local_kernel, out_shape=jax.ShapeDtypeStruct((JB, 2 * nk,...  2.93 us
    ppermute x1, starting transfers between devices, on_device(): got = lax.ppermute(send, 'space', [(s, s ^ NEAR) for s in range(n)])  2.74 us
    ppermute x1, waiting for transfers between devices, on_device(): xc = lax.ppermute(xc, both, cross(x_pairs))  2.63 us
    ppermute x1, starting transfers between devices, on_device(): xs = lax.ppermute(xs, both, same(x_pairs))  2.56 us
    unnamed x8, local copies, waits for them, and re-layouts  2.45 us
  transfers between devices with their start and end apart: 10, of which 7 were waited for; matrix products, arithmetic and copies ran while one was open for 0% of the time, Pallas kernels for 8%

profile of v3, /device:TPU:0, one launch (start us, length us, event | category | flops | bytes accessed | tf_op | source)
XLA Modules:
  0.0 35.2 jit_solution(14073538062735048449)
XLA Ops:
  0.0 0.0 copy-start
  0.0 1.1 %copy-done = bf16[128,3,1,8,128]{4,3,2,1,0:T(8,128)(2,1)S(1)} copy-done((bf16[128,3,1,8,128]{4,3,2,1,0:T(8,128)(2,1)S(1)}, bf16[128,3,1,8,128]{4,3,2,1,0:T(8,128)(2,1)}, u32[]{:S(2)}) %copy-start) | copy-done | bytes 786456
  1.1 0.0 copy-start.1
  1.1 0.7 %copy-done.1 = s32[1,8,128]{2,1,0:T(8,128)S(1)} copy-done((s32[1,8,128]{2,1,0:T(8,128)S(1)}, s32[1,8,128]{2,1,0:T(8,128)}, u32[]{:S(2)}) %copy-start.1) | copy-done | bytes 4120
  1.8 1.5 %prep.1 = (bf16[6,3,128,128]{3,2,1,0:T(8,128)(2,1)S(1)}, bf16[6,3,128,128]{3,2,1,0:T(8,128)(2,1)S(1)}, bf16[784,128]{1,0:T(8,128)(2,1)S(1)}, bf16[768,128]{1,0:T...) custom-call(bf16[128,3,1,8,128]{4,3,2,1,0:T(8,128)(2,1)S(1)} %copy-done, ...), custom_call_target="tpu_custom_call" | custom-call | tf_op jit(solution)/shard_map/prep/pallas_call | solution.py:206
  3.3 0.5 %collective-permute-start = (bf16[6,3,128,128]{3,2,1,0:T(8,128)(2,1)S(1)}, bf16[6,3,128,128]{3,2,1,0:T(8,128)(2,1)S(1)}, u32[]{:S(2)}, u32[]{:S(2)}) collective-permute-start(bf16[6,3,128,128]{3,2,1,0:T(8,128)(2,1)S(1)} %get-tuple-element.20), channel_id=1, source_target_pairs={{0,1},{1,0},{2,3},{3,2},{4,5},{5,4},{6,7},{7,6},{8,9},{9,8},{10,11... | collective-permute-start | bytes 1769480 | tf_op jit(solution)/shard_map/ppermute | solution.py:237
  3.9 2.6 %collective-permute-start.1 = (bf16[784,128]{1,0:T(8,128)(2,1)S(1)}, bf16[784,128]{1,0:T(8,128)(2,1)S(1)}, u32[]{:S(2)}, u32[]{:S(2)}) collective-permute-start(bf16[784,128]{1,0:T(8,128)(2,1)S(1)} %get-tuple-element.21), channel_id=1, source_target_pairs={{0,2},{1,3},{2,0},{3,1},{4,6},{5,7},{6,4},{7,5},{8,10},{9,11},{10,... | collective-permute-start | bytes 602120 | tf_op jit(solution)/shard_map/ppermute | solution.py:233
  6.4 0.0 copy-start.2
  6.4 3.6 %collective-permute-start.3 = (bf16[784,128]{1,0:T(8,128)(2,1)S(1)}, bf16[784,128]{1,0:T(8,128)(2,1)S(1)}, u32[]{:S(2)}, u32[]{:S(2)}) collective-permute-start(bf16[784,128]{1,0:T(8,128)(2,1)S(1)} %get-tuple-element.23), channel_id=1, source_target_pairs={{0,12},{1,13},{2,6},{3,7},{4,0},{5,1},{6,10},{7,11},{8,4},{9,5},{1... | collective-permute-start | bytes 602120 | tf_op jit(solution)/shard_map/ppermute | solution.py:235
  10.0 0.0 collective-permute-start.2
  10.0 0.3 collective-permute-start.4
  10.9 0.0 copy-start.3
  10.9 0.0 collective-permute-done.other_ref
  11.0 0.0 copy-done.2
  11.0 0.6 %copy-done.3 = f32[16]{0:T(128)S(1)} copy-done((f32[16]{0:T(128)S(1)}, f32[16]{0:T(128)}, u32[]{:S(2)}) %copy-start.3) | copy-done | bytes 88
  11.6 2.9 %local.1.acc_ref = f32[4,256,256]{2,1,0:T(8,128)S(1)} custom-call(bf16[6,3,128,128]{3,2,1,0:T(8,128)(2,1)S(1)} %get-tuple-element.19.own_ref, bf16[6,3,128,128]{3,2,1,0:T(8,128)(2,1)S(1)} %collective-permute-done.other_ref, s32[1,8,128]{2,1,0:T(8,128)S(1)} %copy-done.2, f32[16]{0:T(128)S(1)} %copy-done.3, s32[1]{0:T(128)S(6)} %copy.5.jb_ref), custom_call_target="tpu_custom_call" | custom-call | flops 900000000 | bytes 2400000 | tf_op jit(solution)/shard_map/local/pallas_call | solution.py:239
  14.5 2.6 %collective-permute-done.2.xc_ref = bf16[768,128]{1,0:T(8,128)(2,1)S(1)} collective-permute-done((bf16[768,128]{1,0:T(8,128)(2,1)S(1)}, bf16[768,128]{1,0:T(8,128)(2,1)S(1)}, u32[]{:S(2)}, u32[]{:S(2)}) %collective-permute-start.2) | collective-permute-done | bytes 196640 | tf_op jit(solution)/shard_map/ppermute | solution.py:234
  17.2 1.7 %collective-permute-done.4.zc_ref = bf16[768,128]{1,0:T(8,128)(2,1)S(1)} collective-permute-done((bf16[768,128]{1,0:T(8,128)(2,1)S(1)}, bf16[768,128]{1,0:T(8,128)(2,1)S(1)}, u32[]{:S(2)}, u32[]{:S(2)}) %collective-permute-start.4) | collective-permute-done | bytes 196640 | tf_op jit(solution)/shard_map/ppermute | solution.py:236
  18.8 0.0 collective-permute-done.1.xs_ref
  18.8 0.0 collective-permute-done.3.zs_ref
  18.8 2.2 %cross.1 = (f32[8,4,32,128]{3,2,1,0:T(8,128)S(1)}, bf16[8,4,32,128]{3,2,1,0:T(8,128)(2,1)S(1)}) custom-call(bf16[6,3,128,128]{3,2,1,0:T(8,128)(2,1)S(1)} %get-tuple-element.19.own_ref, bf16[6,3,128,128]{3,2,1,0:T(8,128)(2,1)S(1)} %collective-permute-done.other_ref, bf16[784,128]{1,0:T(8,128)(2,1)S(1)} %collective-permute-done.1.xs_ref, ...), custom_call_target="tpu_custom_call" | custom-call | flops 1300000000 | bytes 4000000 | tf_op jit(solution)/shard_map/cross/pallas_call | solution.py:257
  21.1 0.1 collective-permute-start.5
  21.1 1.5 %collective-permute-done.5.got_ref = bf16[8,4,32,128]{3,2,1,0:T(8,128)(2,1)S(1)} collective-permute-done((bf16[8,4,32,128]{3,2,1,0:T(8,128)(2,1)S(1)}, bf16[8,4,32,128]{3,2,1,0:T(8,128)(2,1)S(1)}, u32[]{:S(2)}, u32[]{:S(2)}) %collective-permute-start.5) | collective-permute-done | bytes 262176 | tf_op jit(solution)/shard_map/ppermute | solution.py:275
  22.7 1.3 %collective-permute-start.6 = (bf16[2,4,32,128]{3,2,1,0:T(8,128)(2,1)S(1)}, bf16[2,4,32,128]{3,2,1,0:T(8,128)(2,1)S(1)}, u32[]{:S(2)}, u32[]{:S(2)}) collective-permute-start(bf16[2,4,32,128]{3,2,1,0:T(8,128)(2,1)S(1)} %get-tuple-element.28), channel_id=1, source_target_pairs={{0,2},{2,0},{4,6},{6,4},{8,10},{10,8},{12,14},{14,12},{1,3},{3,1},... | collective-permute-start | bytes 196616 | tf_op jit(solution)/shard_map/ppermute | solution.py:288
  24.0 0.0 collective-permute-start.7
  24.0 2.3 %collective-permute-start.8 = (bf16[2,4,32,128]{3,2,1,0:T(8,128)(2,1)S(1)}, bf16[2,4,32,128]{3,2,1,0:T(8,128)(2,1)S(1)}, u32[]{:S(2)}, u32[]{:S(2)}) collective-permute-start(bf16[2,4,32,128]{3,2,1,0:T(8,128)(2,1)S(1)} %get-tuple-element.30), channel_id=1, source_target_pairs={{0,6},{2,4},{4,2},{6,0},{8,14},{10,12},{12,10},{14,8},{1,7},{3,5},... | collective-permute-start | bytes 196616 | tf_op jit(solution)/shard_map/ppermute | solution.py:288
  26.3 0.8 %collective-permute-done.6.refs_0_ = bf16[2,4,32,128]{3,2,1,0:T(8,128)(2,1)S(1)} collective-permute-done((bf16[2,4,32,128]{3,2,1,0:T(8,128)(2,1)S(1)}, bf16[2,4,32,128]{3,2,1,0:T(8,128)(2,1)S(1)}, u32[]{:S(2)}, u32[]{:S(2)}) %collective-permute-start.6) | collective-permute-done | bytes 65568 | tf_op jit(solution)/shard_map/ppermute | solution.py:288
  27.0 1.7 %collective-permute-done.7.refs_1_ = bf16[2,4,32,128]{3,2,1,0:T(8,128)(2,1)S(1)} collective-permute-done((bf16[2,4,32,128]{3,2,1,0:T(8,128)(2,1)S(1)}, bf16[2,4,32,128]{3,2,1,0:T(8,128)(2,1)S(1)}, u32[]{:S(2)}, u32[]{:S(2)}) %collective-permute-start.7) | collective-permute-done | bytes 65568 | tf_op jit(solution)/shard_map/ppermute | solution.py:288
  28.7 0.9 %collective-permute-done.8.refs_2_ = bf16[2,4,32,128]{3,2,1,0:T(8,128)(2,1)S(1)} collective-permute-done((bf16[2,4,32,128]{3,2,1,0:T(8,128)(2,1)S(1)}, bf16[2,4,32,128]{3,2,1,0:T(8,128)(2,1)S(1)}, u32[]{:S(2)}, u32[]{:S(2)}) %collective-permute-start.8) | collective-permute-done | bytes 65568 | tf_op jit(solution)/shard_map/ppermute | solution.py:288
  29.7 2.7 %collective-permute-start.9 = (bf16[4,32,128]{2,1,0:T(8,128)(2,1)S(1)}, bf16[4,32,128]{2,1,0:T(8,128)(2,1)S(1)}, u32[]{:S(2)}, u32[]{:S(2)}) collective-permute-start(bf16[4,32,128]{2,1,0:T(8,128)(2,1)S(1)} %get-tuple-element.32), channel_id=1, source_target_pairs={{0,8},{2,10},{4,12},{6,14},{8,0},{10,2},{12,4},{14,6},{1,9},{3,11}... | collective-permute-start | bytes 98312 | tf_op jit(solution)/shard_map/ppermute | solution.py:299
  32.4 2.1 %collective-permute-done.9.got_ref = bf16[4,32,128]{2,1,0:T(8,128)(2,1)S(1)} collective-permute-done((bf16[4,32,128]{2,1,0:T(8,128)(2,1)S(1)}, bf16[4,32,128]{2,1,0:T(8,128)(2,1)S(1)}, u32[]{:S(2)}, u32[]{:S(2)}) %collective-permute-start.9) | collective-permute-done | bytes 32800 | tf_op jit(solution)/shard_map/ppermute | solution.py:299
  34.6 0.7 %total.1 = f32[32,4,128]{2,1,0:T(4,128)} custom-call(f32[4,32,128]{2,1,0:T(8,128)S(1)} %get-tuple-element.31.keep_ref, bf16[4,32,128]{2,1,0:T(8,128)(2,1)S(1)} %collective-permute-done.9.got_ref), custom_call_target="tpu_custom_call" | custom-call | tf_op jit(solution)/shard_map/total/pallas_call | solution.py:300
  (2 shorter events, 0.1 us)
Async XLA Ops:
  0.0 1.1 %copy-start = (bf16[128,3,1,8,128]{4,3,2,1,0:T(8,128)(2,1)S(1)}, bf16[128,3,1,8,128]{4,3,2,1,0:T(8,128)(2,1)}, u32[]{:S(2)}) copy-start(bf16[128,3,1,8,128]{4,3,2,1,0:T(8,128)(2,1)} %modes_hbm.1) | copy-start | bytes 2359300
  1.1 0.7 %copy-start.1 = (s32[1,8,128]{2,1,0:T(8,128)S(1)}, s32[1,8,128]{2,1,0:T(8,128)}, u32[]{:S(2)}) copy-start(s32[1,8,128]{2,1,0:T(8,128)} %ids_ref.3) | copy-start | bytes 12292
  3.3 7.6 %collective-permute-start = (bf16[6,3,128,128]{3,2,1,0:T(8,128)(2,1)S(1)}, bf16[6,3,128,128]{3,2,1,0:T(8,128)(2,1)S(1)}, u32[]{:S(2)}, u32[]{:S(2)}) collective-permute-start(bf16[6,3,128,128]{3,2,1,0:T(8,128)(2,1)S(1)} %get-tuple-element.20), channel_id=1, source_target_pairs={{0,1},{1,0},{2,3},{3,2},{4,5},{5,4},{6,7},{7,6},{8,9},{9,8},{10,11... | collective-permute-start | bytes 1769480 | tf_op jit(solution)/shard_map/ppermute | solution.py:237
  3.9 15.0 %collective-permute-start.1 = (bf16[784,128]{1,0:T(8,128)(2,1)S(1)}, bf16[784,128]{1,0:T(8,128)(2,1)S(1)}, u32[]{:S(2)}, u32[]{:S(2)}) collective-permute-start(bf16[784,128]{1,0:T(8,128)(2,1)S(1)} %get-tuple-element.21), channel_id=1, source_target_pairs={{0,2},{1,3},{2,0},{3,1},{4,6},{5,7},{6,4},{7,5},{8,10},{9,11},{10,... | collective-permute-start | bytes 602120 | tf_op jit(solution)/shard_map/ppermute | solution.py:233
  6.4 4.5 %copy-start.2 = (s32[1,8,128]{2,1,0:T(8,128)S(1)}, s32[1,8,128]{2,1,0:T(8,128)}, u32[]{:S(2)}) copy-start(s32[1,8,128]{2,1,0:T(8,128)} %ids_ref.3) | copy-start | bytes 12292
  6.4 12.4 %collective-permute-start.3 = (bf16[784,128]{1,0:T(8,128)(2,1)S(1)}, bf16[784,128]{1,0:T(8,128)(2,1)S(1)}, u32[]{:S(2)}, u32[]{:S(2)}) collective-permute-start(bf16[784,128]{1,0:T(8,128)(2,1)S(1)} %get-tuple-element.23), channel_id=1, source_target_pairs={{0,12},{1,13},{2,6},{3,7},{4,0},{5,1},{6,10},{7,11},{8,4},{9,5},{1... | collective-permute-start | bytes 602120 | tf_op jit(solution)/shard_map/ppermute | solution.py:235
  10.0 7.1 %collective-permute-start.2 = (bf16[768,128]{1,0:T(8,128)(2,1)S(1)}, bf16[768,128]{1,0:T(8,128)(2,1)S(1)}, u32[]{:S(2)}, u32[]{:S(2)}) collective-permute-start(bf16[768,128]{1,0:T(8,128)(2,1)S(1)} %get-tuple-element.22), channel_id=1, source_target_pairs={{0,3},{1,2},{2,1},{3,0},{4,7},{5,6},{6,5},{7,4},{8,11},{9,10},{10,... | collective-permute-start | bytes 589832 | tf_op jit(solution)/shard_map/ppermute | solution.py:234
  10.0 8.8 %collective-permute-start.4 = (bf16[768,128]{1,0:T(8,128)(2,1)S(1)}, bf16[768,128]{1,0:T(8,128)(2,1)S(1)}, u32[]{:S(2)}, u32[]{:S(2)}) collective-permute-start(bf16[768,128]{1,0:T(8,128)(2,1)S(1)} %get-tuple-element.24), channel_id=1, source_target_pairs={{0,13},{1,12},{2,7},{3,6},{4,1},{5,0},{6,11},{7,10},{8,5},{9,4},{1... | collective-permute-start | bytes 589832 | tf_op jit(solution)/shard_map/ppermute | solution.py:236
  10.9 0.7 %copy-start.3 = (f32[16]{0:T(128)S(1)}, f32[16]{0:T(128)}, u32[]{:S(2)}) copy-start(f32[16]{0:T(128)} %table_ref.3) | copy-start | bytes 196
  21.1 1.6 %collective-permute-start.5 = (bf16[8,4,32,128]{3,2,1,0:T(8,128)(2,1)S(1)}, bf16[8,4,32,128]{3,2,1,0:T(8,128)(2,1)S(1)}, u32[]{:S(2)}, u32[]{:S(2)}) collective-permute-start(bf16[8,4,32,128]{3,2,1,0:T(8,128)(2,1)S(1)} %get-tuple-element.26), channel_id=1, source_target_pairs={{0,1},{1,0},{2,3},{3,2},{4,5},{5,4},{6,7},{7,6},{8,9},{9,8},{10,11... | collective-permute-start | bytes 786440 | tf_op jit(solution)/shard_map/ppermute | solution.py:275
  22.7 4.3 %collective-permute-start.6 = (bf16[2,4,32,128]{3,2,1,0:T(8,128)(2,1)S(1)}, bf16[2,4,32,128]{3,2,1,0:T(8,128)(2,1)S(1)}, u32[]{:S(2)}, u32[]{:S(2)}) collective-permute-start(bf16[2,4,32,128]{3,2,1,0:T(8,128)(2,1)S(1)} %get-tuple-element.28), channel_id=1, source_target_pairs={{0,2},{2,0},{4,6},{6,4},{8,10},{10,8},{12,14},{14,12},{1,3},{3,1},... | collective-permute-start | bytes 196616 | tf_op jit(solution)/shard_map/ppermute | solution.py:288
  24.0 4.8 %collective-permute-start.7 = (bf16[2,4,32,128]{3,2,1,0:T(8,128)(2,1)S(1)}, bf16[2,4,32,128]{3,2,1,0:T(8,128)(2,1)S(1)}, u32[]{:S(2)}, u32[]{:S(2)}) collective-permute-start(bf16[2,4,32,128]{3,2,1,0:T(8,128)(2,1)S(1)} %get-tuple-element.29), channel_id=1, source_target_pairs={{0,4},{2,6},{4,0},{6,2},{8,12},{10,14},{12,8},{14,10},{1,5},{3,7},... | collective-permute-start | bytes 196616 | tf_op jit(solution)/shard_map/ppermute | solution.py:288
  24.0 5.7 %collective-permute-start.8 = (bf16[2,4,32,128]{3,2,1,0:T(8,128)(2,1)S(1)}, bf16[2,4,32,128]{3,2,1,0:T(8,128)(2,1)S(1)}, u32[]{:S(2)}, u32[]{:S(2)}) collective-permute-start(bf16[2,4,32,128]{3,2,1,0:T(8,128)(2,1)S(1)} %get-tuple-element.30), channel_id=1, source_target_pairs={{0,6},{2,4},{4,2},{6,0},{8,14},{10,12},{12,10},{14,8},{1,7},{3,5},... | collective-permute-start | bytes 196616 | tf_op jit(solution)/shard_map/ppermute | solution.py:288
  29.7 4.9 %collective-permute-start.9 = (bf16[4,32,128]{2,1,0:T(8,128)(2,1)S(1)}, bf16[4,32,128]{2,1,0:T(8,128)(2,1)S(1)}, u32[]{:S(2)}, u32[]{:S(2)}) collective-permute-start(bf16[4,32,128]{2,1,0:T(8,128)(2,1)S(1)} %get-tuple-element.32), channel_id=1, source_target_pairs={{0,8},{2,10},{4,12},{6,14},{8,0},{10,2},{12,4},{14,6},{1,9},{3,11}... | collective-permute-start | bytes 98312 | tf_op jit(solution)/shard_map/ppermute | solution.py:299

commit v4 on v3

--- a/solution.py
+++ b/solution.py
@@ -10,14 +10,14 @@
 JB = 4
 NW = 16
 IDROWS = 16
+PADROWS = 16
 LOADS = 4
 NEAR = 4
 VMEM_LIMIT = 48 * 1024 * 1024
-
-
-def prep_kernel(
-    modes_hbm, ids_hbm, own_ref, core_ref, xs_ref, xc_ref, zs_ref, zc_ref, modes_ref, ids_ref, tr, sems
-):
+PREP_LIMIT = 53_100 * 1024
+
+
+def prep_kernel(modes_hbm, own_ref, core_ref, zs_ref, xs_ref, zc_ref, xc_ref, modes_ref, tr, sems):
     m = lax.axis_index("modes")
     q = lax.rem(lax.axis_index("space"), 2)
     nk, comps, _, nx, nz = modes_hbm.shape
@@ -28,7 +28,6 @@
         )
         for p in range(LOADS)
     ]
-    copies.append(pltpu.make_async_copy(ids_hbm, ids_ref, sems.at[LOADS]))
     for copy in copies:
         copy.start()
     for p in range(LOADS):
@@ -37,27 +36,38 @@
         for c in range(comps):
             value = modes_ref[block, c, 0].astype(jnp.float32)
             tr[:, c, block] = jnp.swapaxes(value, 0, 1).astype(jnp.bfloat16)
-    copies[LOADS].wait()
     quarter = nx // 4
     for r in range(nx // 2 + 2):
         own_ref[r] = tr[lax.rem(nx // 2 * m + nx - 1 + r, nx)]
         core_ref[r] = tr[lax.rem(nx // 2 * (1 - m) + nx - 1 + r, nx)]
-    for ref, at, with_ids in (
-        (xs_ref, 2 * m + 1 - q, True),
-        (xc_ref, 2 * (1 - m) + 1 - q, False),
-        (zs_ref, 2 * m + q, True),
-        (zc_ref, 2 * (1 - m) + q, False),
+    for ref, at in (
+        (xs_ref, 2 * m + 1 - q),
+        (xc_ref, 2 * (1 - m) + 1 - q),
+        (zs_ref, 2 * m + q),
+        (zc_ref, 2 * (1 - m) + q),
     ):
         for row in range(quarter):
             for c in range(comps):
                 ref[pl.ds((row * comps + c) * nk, nk), :] = tr[at * quarter + row, c]
-        if with_ids:
-            ids = [
-                jnp.broadcast_to(ids_ref[0, pl.ds(at * quarter + row, 1), :], (IDROWS // quarter, nz))
-                for row in range(quarter)
-            ]
-            rows = jnp.concatenate(ids, axis=0).astype(jnp.float32).astype(jnp.bfloat16)
-            ref[pl.ds(quarter * comps * nk, IDROWS), :] = rows
+    for ref in (zs_ref, xs_ref):
+        pad = ref.shape[0] - quarter * comps * nk
+        ref[pl.ds(quarter * comps * nk, pad), :] = jnp.zeros((pad, nz), jnp.bfloat16)
+
+
+def ids_kernel(ids_ref, zc_ref, xc_ref, _, zc_out, xc_out):
+    m = lax.axis_index("modes")
+    q = lax.rem(lax.axis_index("space"), 2)
+    body, nz = xc_ref.shape
+    quarter = ids_ref.shape[1] // 4
+    for ref, out, at in ((zc_ref, zc_out, 2 * (1 - m) + q), (xc_ref, xc_out, 2 * (1 - m) + 1 - q)):
+        out[pl.ds(0, body), :] = ref[...]
+        ids = [
+            jnp.broadcast_to(ids_ref[0, pl.ds(at * quarter + row, 1), :], (IDROWS // quarter, nz))
+            for row in range(quarter)
+        ]
+        out[pl.ds(body, IDROWS), :] = (
+            jnp.concatenate(ids, axis=0).astype(jnp.float32).astype(jnp.bfloat16)
+        )
 
 
 def picks(jb_ref, m, nk):
@@ -114,7 +124,7 @@
 
 
 def cross_kernel(
-    chunk, planes, own_ref, other_ref, xs_ref, xc_ref, zs_ref, zc_ref, ids_ref, table_ref, jb_ref, acc_ref,
+    chunk, planes, own_ref, other_ref, zs_ref, xs_ref, zc_ref, xc_ref, ids_ref, table_ref, jb_ref, acc_ref,
     keep_ref, send_ref, adv, wts, wscr,
 ):
     m = lax.axis_index("modes")
@@ -129,8 +139,8 @@
     span = quarter * comps * nz
     pick = picks(jb_ref, m, nk)
     wscr[...] = weights_of(ids_ref[0], table_ref)
-    w1 = weights_of(xs_ref[pl.ds(span, IDROWS), :].astype(jnp.float32), table_ref)
-    w2 = weights_of(zs_ref[pl.ds(span, IDROWS), :].astype(jnp.float32), table_ref)
+    w1 = weights_of(xc_ref[pl.ds(span, IDROWS), :].astype(jnp.float32), table_ref)
+    w2 = weights_of(zc_ref[pl.ds(span, IDROWS), :].astype(jnp.float32), table_ref)
     for r in range(quarter):
         row0 = 1 + quarter * q + r
         weight0 = wscr[pl.ds(rows * m + quarter * q + r, 1), :]
@@ -199,42 +209,43 @@
     bf16, f32 = jnp.bfloat16, jnp.float32
     vmem = pl.BlockSpec(memory_space=pltpu.VMEM)
     smem = pl.BlockSpec(memory_space=pltpu.SMEM)
-    hbm = pl.BlockSpec(memory_space=pltpu.HBM)
     params = pltpu.CompilerParams(vmem_limit_bytes=VMEM_LIMIT)
     six = nx // 2 + 2
     body = nx // 4 * comps * nk
-    own, to_core, xs, xc, zs, zc = pl.pallas_call(
+    own, to_core, zs, xs, zc, xc = pl.pallas_call(
         prep_kernel,
-        out_shape=[
-            jax.ShapeDtypeStruct((six, comps, nk, nz), bf16),
-            jax.ShapeDtypeStruct((six, comps, nk, nz), bf16),
-            jax.ShapeDtypeStruct((body + IDROWS, nz), bf16),
-            jax.ShapeDtypeStruct((body, nz), bf16),
-            jax.ShapeDtypeStruct((body + IDROWS, nz), bf16),
-            jax.ShapeDtypeStruct((body, nz), bf16),
-        ],
-        in_specs=[hbm, hbm],
+        out_shape=[jax.ShapeDtypeStruct((six, comps, nk, nz), bf16)] * 2
+        + [jax.ShapeDtypeStruct((body + PADROWS, nz), bf16)] * 2
+        + [jax.ShapeDtypeStruct((body, nz), bf16)] * 2,
+        in_specs=[pl.BlockSpec(memory_space=pltpu.HBM)],
         out_specs=[vmem] * 6,
         scratch_shapes=[
             pltpu.VMEM(modes.shape, bf16),
-            pltpu.VMEM(weight_ids.shape, jnp.int32),
             pltpu.VMEM((nx, comps, nk, nz), bf16),
-            pltpu.SemaphoreType.DMA((LOADS + 1,)),
+            pltpu.SemaphoreType.DMA((LOADS,)),
         ],
-        compiler_params=params,
+        compiler_params=pltpu.CompilerParams(vmem_limit_bytes=PREP_LIMIT),
         name="prep",
-    )(modes, weight_ids)
+    )(modes)
 
     both = ("space", "modes")
     x_pairs = [(s, s ^ 1) for s in range(n)]
     z_pairs = [(s, (s + (2 if s % 2 else -2)) % n) for s in range(n)]
     same = lambda pairs: [(2 * a + m, 2 * b + m) for a, b in pairs for m in range(2)]
     cross = lambda pairs: [(2 * a + m, 2 * b + 1 - m) for a, b in pairs for m in range(2)]
+    other = lax.ppermute(to_core, "modes", [(0, 1), (1, 0)])
+    zs = lax.ppermute(zs, both, same(z_pairs))
     xs = lax.ppermute(xs, both, same(x_pairs))
+    zc, xc = pl.pallas_call(
+        ids_kernel,
+        out_shape=[jax.ShapeDtypeStruct((body + IDROWS, nz), bf16)] * 2,
+        in_specs=[vmem] * 3 + [pl.BlockSpec(memory_space=pl.ANY)],
+        out_specs=[vmem] * 2,
+        compiler_params=params,
+        name="ids",
+    )(weight_ids, zc, xc, other)
+    zc = lax.ppermute(zc, both, cross(z_pairs))
     xc = lax.ppermute(xc, both, cross(x_pairs))
-    zs = lax.ppermute(zs, both, same(z_pairs))
-    zc = lax.ppermute(zc, both, cross(z_pairs))
-    other = lax.ppermute(to_core, "modes", [(0, 1), (1, 0)])
 
     acc = pl.pallas_call(
         local_kernel,
@@ -270,7 +281,7 @@
         compiler_params=params,
         cost_estimate=pl.CostEstimate(flops=1_300_000_000, bytes_accessed=4_000_000, transcendentals=0),
         name="cross",
-    )(own, other, xs, xc, zs, zc, weight_ids, weight_table, j_block, acc)
+    )(own, other, zs, xs, zc, xc, weight_ids, weight_table, j_block, acc)
 
     got = lax.ppermute(send, "modes", [(0, 1), (1, 0)])
     if n == 2 * NEAR:
@@ -285,8 +296,8 @@
             name="near",
         )(keep, got)
         parts = [
-            lax.ppermute(part, "space", [(s, s ^ step) for s in range(n)])
-            for step, part in enumerate(shares, 1)
+            lax.ppermute(shares[step - 1], "space", [(s, s ^ step) for s in range(n)])
+            for step in (3, 1, 2)
         ]
         keep, send = pl.pallas_call(
             far_kernel,

time: 35.4 us -> 33.2 us (0.938)
  local copies, waits for them, and re-layouts: 2.45 us -> 0.66 us
  waiting for transfers between devices: 11.3 us -> 10.5 us
  starting transfers between devices: 13.3 us -> 13.7 us
    ppermute x1, starting transfers between devices: 2.56 us -> 0.01 us  [on_device(): xs = lax.ppermute(xs, both, same(x_pairs))]
    unnamed x8 -> x4, local copies, waits for them, and re-layouts: 2.45 us -> 0.66 us
    ppermute x1, waiting for transfers between devices: 0.01 us -> 1.8 us  [on_device(): xs = lax.ppermute(xs, both, same(x_pairs))]
    ppermute x1, starting transfers between devices: 0.25 us -> 1.72 us  [on_device(): zc = lax.ppermute(zc, both, cross(z_pairs))]
    ppermute x1, waiting for transfers between devices: 2.63 us -> 1.42 us  [on_device(): xc = lax.ppermute(xc, both, cross(x_pairs))]
    ppermute x1, starting transfers between devices: 3.6 us -> 4.66 us  [on_device(): zs = lax.ppermute(zs, both, same(z_pairs))]
    ppermute x3, waiting for transfers between devices: 3.38 us -> 2.47 us  [on_device(): lax.ppermute(shares[step - 1], 'space', [(s, s ^ step) for s in range(n)])]
    ppermute x1, starting transfers between devices: 0.07 us -> 0.66 us  [on_device(): got = lax.ppermute(send, 'modes', [(0, 1), (1, 0)])]
  transfers between devices with their start and end apart: 10 -> 10, of which waited for: 7 -> 7; matrix products, arithmetic and copies ran while one was open for 0% -> 0% of each run, Pallas kernels for 8% -> 9%
where the time goes in v4:
time: 33.2 us; the launch traced here: 33 us
  starting transfers between devices  13.7 us (41%)
  waiting for transfers between devices  10.5 us (32%)
  Pallas kernels  7.42 us (22%)
  between operations  0.73 us (2%)
  local copies, waits for them, and re-layouts  0.66 us (2%)
    ppermute x1, starting transfers between devices, on_device(): zs = lax.ppermute(zs, both, same(z_pairs))  4.66 us
    ppermute x3, starting transfers between devices, on_device(): lax.ppermute(shares[step - 1], 'space', [(s, s ^ step) for s in range(n)])  3.57 us
    pallas_call x1, Pallas kernels, on_device(): pl.pallas_call(local_kernel, out_shape=jax.ShapeDtypeStruct((JB, 2 * nk,...  2.93 us
    ppermute x1, starting transfers between devices, on_device(): got = lax.ppermute(send, 'space', [(s, s ^ NEAR) for s in range(n)])  2.56 us
    ppermute x3, waiting for transfers between devices, on_device(): lax.ppermute(shares[step - 1], 'space', [(s, s ^ step) for s in range(n)])  2.47 us
    ppermute x1, waiting for transfers between devices, on_device(): got = lax.ppermute(send, 'space', [(s, s ^ NEAR) for s in range(n)])  2.32 us
    pallas_call x1, Pallas kernels, on_device(): pl.pallas_call(functools.partial(cross_kernel, chunk, n), out_shape=[jax....  2.22 us
    ppermute x1, waiting for transfers between devices, on_device(): xs = lax.ppermute(xs, both, same(x_pairs))  1.8 us
  transfers between devices with their start and end apart: 10, of which 7 were waited for; matrix products, arithmetic and copies ran while one was open for 0% of the time, Pallas kernels for 9%

profile of v4, /device:TPU:0, one launch (start us, length us, event | category | flops | bytes accessed | tf_op | source)
XLA Modules:
  0.0 33.0 jit_solution(3417021046553946885)
XLA Ops:
  0.0 1.5 %prep.1 = (bf16[6,3,128,128]{3,2,1,0:T(8,128)(2,1)S(1)}, bf16[6,3,128,128]{3,2,1,0:T(8,128)(2,1)S(1)}, bf16[784,128]{1,0:T(8,128)(2,1)S(1)}, bf16[784,128]{1,0:T...) custom-call(bf16[128,3,1,8,128]{4,3,2,1,0:T(8,128)(2,1)} %modes_hbm.1), custom_call_target="tpu_custom_call" | custom-call | tf_op jit(solution)/shard_map/prep/pallas_call | solution.py:215
  1.5 0.0 copy-start
  1.5 0.5 %collective-permute-start = (bf16[6,3,128,128]{3,2,1,0:T(8,128)(2,1)S(1)}, bf16[6,3,128,128]{3,2,1,0:T(8,128)(2,1)S(1)}, u32[]{:S(2)}, u32[]{:S(2)}) collective-permute-start(bf16[6,3,128,128]{3,2,1,0:T(8,128)(2,1)S(1)} %get-tuple-element.22), channel_id=1, source_target_pairs={{0,1},{1,0},{2,3},{3,2},{4,5},{5,4},{6,7},{7,6},{8,9},{9,8},{10,11... | collective-permute-start | bytes 1769480 | tf_op jit(solution)/shard_map/ppermute | solution.py:236
  2.0 4.7 %collective-permute-start.1 = (bf16[784,128]{1,0:T(8,128)(2,1)S(1)}, bf16[784,128]{1,0:T(8,128)(2,1)S(1)}, u32[]{:S(2)}, u32[]{:S(2)}) collective-permute-start(bf16[784,128]{1,0:T(8,128)(2,1)S(1)} %get-tuple-element.23), channel_id=1, source_target_pairs={{0,12},{1,13},{2,6},{3,7},{4,0},{5,1},{6,10},{7,11},{8,4},{9,5},{1... | collective-permute-start | bytes 602120 | tf_op jit(solution)/shard_map/ppermute | solution.py:237
  6.7 0.0 collective-permute-start.2
  6.7 0.0 collective-permute-done._.other_ref
  6.7 0.0 copy-done
  6.7 1.7 %collective-permute-start.3 = (bf16[784,128]{1,0:T(8,128)(2,1)S(1)}, bf16[784,128]{1,0:T(8,128)(2,1)S(1)}, u32[]{:S(2)}, u32[]{:S(2)}) collective-permute-start(bf16[784,128]{1,0:T(8,128)(2,1)S(1)} %get-tuple-element.27), channel_id=1, source_target_pairs={{0,13},{1,12},{2,7},{3,6},{4,1},{5,0},{6,11},{7,10},{8,5},{9,4},{1... | collective-permute-start | bytes 602120 | tf_op jit(solution)/shard_map/ppermute | solution.py:247
  8.4 0.0 collective-permute-start.4
  9.1 0.0 copy-start.1
  9.1 0.6 %copy-done.1 = f32[16]{0:T(128)S(1)} copy-done((f32[16]{0:T(128)S(1)}, f32[16]{0:T(128)}, u32[]{:S(2)}) %copy-start.1) | copy-done | bytes 88
  9.7 2.9 %local.1.acc_ref = f32[4,256,256]{2,1,0:T(8,128)S(1)} custom-call(bf16[6,3,128,128]{3,2,1,0:T(8,128)(2,1)S(1)} %get-tuple-element.21.own_ref, bf16[6,3,128,128]{3,2,1,0:T(8,128)(2,1)S(1)} %collective-permute-done._.other_ref, s32[1,8,128]{2,1,0:T(8,128)S(1)} %copy-done, f32[16]{0:T(128)S(1)} %copy-done.1, s32[1]{0:T(128)S(6)} %copy.5.jb_ref), custom_call_target="tpu_custom_call" | custom-call | flops 900000000 | bytes 2400000 | tf_op jit(solution)/shard_map/local/pallas_call | solution.py:250
  12.7 0.0 collective-permute-done.1.zs_ref
  12.7 1.8 %collective-permute-done.2.xs_ref = bf16[784,128]{1,0:T(8,128)(2,1)S(1)} collective-permute-done((bf16[784,128]{1,0:T(8,128)(2,1)S(1)}, bf16[784,128]{1,0:T(8,128)(2,1)S(1)}, u32[]{:S(2)}, u32[]{:S(2)}) %collective-permute-start.2) | collective-permute-done | bytes 200736 | tf_op jit(solution)/shard_map/ppermute | solution.py:238
  14.5 1.3 %collective-permute-done.3.zc_ref = bf16[784,128]{1,0:T(8,128)(2,1)S(1)} collective-permute-done((bf16[784,128]{1,0:T(8,128)(2,1)S(1)}, bf16[784,128]{1,0:T(8,128)(2,1)S(1)}, u32[]{:S(2)}, u32[]{:S(2)}) %collective-permute-start.3) | collective-permute-done | bytes 200736 | tf_op jit(solution)/shard_map/ppermute | solution.py:247
  15.8 1.4 %collective-permute-done.4.xc_ref = bf16[784,128]{1,0:T(8,128)(2,1)S(1)} collective-permute-done((bf16[784,128]{1,0:T(8,128)(2,1)S(1)}, bf16[784,128]{1,0:T(8,128)(2,1)S(1)}, u32[]{:S(2)}, u32[]{:S(2)}) %collective-permute-start.4) | collective-permute-done | bytes 200736 | tf_op jit(solution)/shard_map/ppermute | solution.py:248
  17.2 2.2 %cross.1 = (f32[8,4,32,128]{3,2,1,0:T(8,128)S(1)}, bf16[8,4,32,128]{3,2,1,0:T(8,128)(2,1)S(1)}) custom-call(bf16[6,3,128,128]{3,2,1,0:T(8,128)(2,1)S(1)} %get-tuple-element.21.own_ref, bf16[6,3,128,128]{3,2,1,0:T(8,128)(2,1)S(1)} %collective-permute-done._.other_ref, bf16[784,128]{1,0:T(8,128)(2,1)S(1)} %collective-permute-done.1.zs_ref, ...), custom_call_target="tpu_custom_call" | custom-call | flops 1300000000 | bytes 4000000 | tf_op jit(solution)/shard_map/cross/pallas_call | solution.py:268
  19.5 0.7 %collective-permute-start.5 = (bf16[8,4,32,128]{3,2,1,0:T(8,128)(2,1)S(1)}, bf16[8,4,32,128]{3,2,1,0:T(8,128)(2,1)S(1)}, u32[]{:S(2)}, u32[]{:S(2)}) collective-permute-start(bf16[8,4,32,128]{3,2,1,0:T(8,128)(2,1)S(1)} %get-tuple-element.30), channel_id=1, source_target_pairs={{0,1},{1,0},{2,3},{3,2},{4,5},{5,4},{6,7},{7,6},{8,9},{9,8},{10,11... | collective-permute-start | bytes 786440 | tf_op jit(solution)/shard_map/ppermute | solution.py:286
  20.1 1.2 %collective-permute-done.5.got_ref = bf16[8,4,32,128]{3,2,1,0:T(8,128)(2,1)S(1)} collective-permute-done((bf16[8,4,32,128]{3,2,1,0:T(8,128)(2,1)S(1)}, bf16[8,4,32,128]{3,2,1,0:T(8,128)(2,1)S(1)}, u32[]{:S(2)}, u32[]{:S(2)}) %collective-permute-start.5) | collective-permute-done | bytes 262176 | tf_op jit(solution)/shard_map/ppermute | solution.py:286
  21.3 0.1 near.1
  21.4 0.6 %collective-permute-start.6 = (bf16[2,4,32,128]{3,2,1,0:T(8,128)(2,1)S(1)}, bf16[2,4,32,128]{3,2,1,0:T(8,128)(2,1)S(1)}, u32[]{:S(2)}, u32[]{:S(2)}) collective-permute-start(bf16[2,4,32,128]{3,2,1,0:T(8,128)(2,1)S(1)} %get-tuple-element.32), channel_id=1, source_target_pairs={{0,6},{2,4},{4,2},{6,0},{8,14},{10,12},{12,10},{14,8},{1,7},{3,5},... | collective-permute-start | bytes 196616 | tf_op jit(solution)/shard_map/ppermute | solution.py:299
  21.9 0.4 %collective-permute-start.7 = (bf16[2,4,32,128]{3,2,1,0:T(8,128)(2,1)S(1)}, bf16[2,4,32,128]{3,2,1,0:T(8,128)(2,1)S(1)}, u32[]{:S(2)}, u32[]{:S(2)}) collective-permute-start(bf16[2,4,32,128]{3,2,1,0:T(8,128)(2,1)S(1)} %get-tuple-element.33), channel_id=1, source_target_pairs={{0,2},{2,0},{4,6},{6,4},{8,10},{10,8},{12,14},{14,12},{1,3},{3,1},... | collective-permute-start | bytes 196616 | tf_op jit(solution)/shard_map/ppermute | solution.py:299
  22.3 2.6 %collective-permute-start.8 = (bf16[2,4,32,128]{3,2,1,0:T(8,128)(2,1)S(1)}, bf16[2,4,32,128]{3,2,1,0:T(8,128)(2,1)S(1)}, u32[]{:S(2)}, u32[]{:S(2)}) collective-permute-start(bf16[2,4,32,128]{3,2,1,0:T(8,128)(2,1)S(1)} %get-tuple-element.34), channel_id=1, source_target_pairs={{0,4},{2,6},{4,0},{6,2},{8,12},{10,14},{12,8},{14,10},{1,5},{3,7},... | collective-permute-start | bytes 196616 | tf_op jit(solution)/shard_map/ppermute | solution.py:299
  24.9 2.3 %collective-permute-done.6.refs_0_ = bf16[2,4,32,128]{3,2,1,0:T(8,128)(2,1)S(1)} collective-permute-done((bf16[2,4,32,128]{3,2,1,0:T(8,128)(2,1)S(1)}, bf16[2,4,32,128]{3,2,1,0:T(8,128)(2,1)S(1)}, u32[]{:S(2)}, u32[]{:S(2)}) %collective-permute-start.6) | collective-permute-done | bytes 65568 | tf_op jit(solution)/shard_map/ppermute | solution.py:299
  27.3 0.1 collective-permute-done.7.refs_1_
  27.4 0.0 collective-permute-done.8.refs_2_
  27.4 2.6 %collective-permute-start.9 = (bf16[4,32,128]{2,1,0:T(8,128)(2,1)S(1)}, bf16[4,32,128]{2,1,0:T(8,128)(2,1)S(1)}, u32[]{:S(2)}, u32[]{:S(2)}) collective-permute-start(bf16[4,32,128]{2,1,0:T(8,128)(2,1)S(1)} %get-tuple-element.36), channel_id=1, source_target_pairs={{0,8},{2,10},{4,12},{6,14},{8,0},{10,2},{12,4},{14,6},{1,9},{3,11}... | collective-permute-start | bytes 98312 | tf_op jit(solution)/shard_map/ppermute | solution.py:310
  30.0 2.3 %collective-permute-done.9.got_ref = bf16[4,32,128]{2,1,0:T(8,128)(2,1)S(1)} collective-permute-done((bf16[4,32,128]{2,1,0:T(8,128)(2,1)S(1)}, bf16[4,32,128]{2,1,0:T(8,128)(2,1)S(1)}, u32[]{:S(2)}, u32[]{:S(2)}) %collective-permute-start.9) | collective-permute-done | bytes 32800 | tf_op jit(solution)/shard_map/ppermute | solution.py:310
  32.3 0.7 %total.1 = f32[32,4,128]{2,1,0:T(4,128)} custom-call(f32[4,32,128]{2,1,0:T(8,128)S(1)} %get-tuple-element.35.keep_ref, bf16[4,32,128]{2,1,0:T(8,128)(2,1)S(1)} %collective-permute-done.9.got_ref), custom_call_target="tpu_custom_call" | custom-call | tf_op jit(solution)/shard_map/total/pallas_call | solution.py:311
  (2 shorter events, 0.1 us)
Async XLA Ops:
  1.5 5.2 %copy-start = (s32[1,8,128]{2,1,0:T(8,128)S(1)}, s32[1,8,128]{2,1,0:T(8,128)}, u32[]{:S(2)}) copy-start(s32[1,8,128]{2,1,0:T(8,128)} %ids_ref.5) | copy-start | bytes 12292
  1.5 5.2 %collective-permute-start = (bf16[6,3,128,128]{3,2,1,0:T(8,128)(2,1)S(1)}, bf16[6,3,128,128]{3,2,1,0:T(8,128)(2,1)S(1)}, u32[]{:S(2)}, u32[]{:S(2)}) collective-permute-start(bf16[6,3,128,128]{3,2,1,0:T(8,128)(2,1)S(1)} %get-tuple-element.22), channel_id=1, source_target_pairs={{0,1},{1,0},{2,3},{3,2},{4,5},{5,4},{6,7},{7,6},{8,9},{9,8},{10,11... | collective-permute-start | bytes 1769480 | tf_op jit(solution)/shard_map/ppermute | solution.py:236
  2.0 10.7 %collective-permute-start.1 = (bf16[784,128]{1,0:T(8,128)(2,1)S(1)}, bf16[784,128]{1,0:T(8,128)(2,1)S(1)}, u32[]{:S(2)}, u32[]{:S(2)}) collective-permute-start(bf16[784,128]{1,0:T(8,128)(2,1)S(1)} %get-tuple-element.23), channel_id=1, source_target_pairs={{0,12},{1,13},{2,6},{3,7},{4,0},{5,1},{6,10},{7,11},{8,4},{9,5},{1... | collective-permute-start | bytes 602120 | tf_op jit(solution)/shard_map/ppermute | solution.py:237
  6.7 7.8 %collective-permute-start.2 = (bf16[784,128]{1,0:T(8,128)(2,1)S(1)}, bf16[784,128]{1,0:T(8,128)(2,1)S(1)}, u32[]{:S(2)}, u32[]{:S(2)}) collective-permute-start(bf16[784,128]{1,0:T(8,128)(2,1)S(1)} %get-tuple-element.24), channel_id=1, source_target_pairs={{0,2},{1,3},{2,0},{3,1},{4,6},{5,7},{6,4},{7,5},{8,10},{9,11},{10,... | collective-permute-start | bytes 602120 | tf_op jit(solution)/shard_map/ppermute | solution.py:238
  6.7 9.1 %collective-permute-start.3 = (bf16[784,128]{1,0:T(8,128)(2,1)S(1)}, bf16[784,128]{1,0:T(8,128)(2,1)S(1)}, u32[]{:S(2)}, u32[]{:S(2)}) collective-permute-start(bf16[784,128]{1,0:T(8,128)(2,1)S(1)} %get-tuple-element.27), channel_id=1, source_target_pairs={{0,13},{1,12},{2,7},{3,6},{4,1},{5,0},{6,11},{7,10},{8,5},{9,4},{1... | collective-permute-start | bytes 602120 | tf_op jit(solution)/shard_map/ppermute | solution.py:247
  8.4 8.8 %collective-permute-start.4 = (bf16[784,128]{1,0:T(8,128)(2,1)S(1)}, bf16[784,128]{1,0:T(8,128)(2,1)S(1)}, u32[]{:S(2)}, u32[]{:S(2)}) collective-permute-start(bf16[784,128]{1,0:T(8,128)(2,1)S(1)} %get-tuple-element.28), channel_id=1, source_target_pairs={{0,3},{1,2},{2,1},{3,0},{4,7},{5,6},{6,5},{7,4},{8,11},{9,10},{10,... | collective-permute-start | bytes 602120 | tf_op jit(solution)/shard_map/ppermute | solution.py:248
  9.1 0.7 %copy-start.1 = (f32[16]{0:T(128)S(1)}, f32[16]{0:T(128)}, u32[]{:S(2)}) copy-start(f32[16]{0:T(128)} %table_ref.3) | copy-start | bytes 196
  19.5 1.8 %collective-permute-start.5 = (bf16[8,4,32,128]{3,2,1,0:T(8,128)(2,1)S(1)}, bf16[8,4,32,128]{3,2,1,0:T(8,128)(2,1)S(1)}, u32[]{:S(2)}, u32[]{:S(2)}) collective-permute-start(bf16[8,4,32,128]{3,2,1,0:T(8,128)(2,1)S(1)} %get-tuple-element.30), channel_id=1, source_target_pairs={{0,1},{1,0},{2,3},{3,2},{4,5},{5,4},{6,7},{7,6},{8,9},{9,8},{10,11... | collective-permute-start | bytes 786440 | tf_op jit(solution)/shard_map/ppermute | solution.py:286
  21.4 5.9 %collective-permute-start.6 = (bf16[2,4,32,128]{3,2,1,0:T(8,128)(2,1)S(1)}, bf16[2,4,32,128]{3,2,1,0:T(8,128)(2,1)S(1)}, u32[]{:S(2)}, u32[]{:S(2)}) collective-permute-start(bf16[2,4,32,128]{3,2,1,0:T(8,128)(2,1)S(1)} %get-tuple-element.32), channel_id=1, source_target_pairs={{0,6},{2,4},{4,2},{6,0},{8,14},{10,12},{12,10},{14,8},{1,7},{3,5},... | collective-permute-start | bytes 196616 | tf_op jit(solution)/shard_map/ppermute | solution.py:299
  21.9 5.5 %collective-permute-start.7 = (bf16[2,4,32,128]{3,2,1,0:T(8,128)(2,1)S(1)}, bf16[2,4,32,128]{3,2,1,0:T(8,128)(2,1)S(1)}, u32[]{:S(2)}, u32[]{:S(2)}) collective-permute-start(bf16[2,4,32,128]{3,2,1,0:T(8,128)(2,1)S(1)} %get-tuple-element.33), channel_id=1, source_target_pairs={{0,2},{2,0},{4,6},{6,4},{8,10},{10,8},{12,14},{14,12},{1,3},{3,1},... | collective-permute-start | bytes 196616 | tf_op jit(solution)/shard_map/ppermute | solution.py:299
  22.3 5.1 %collective-permute-start.8 = (bf16[2,4,32,128]{3,2,1,0:T(8,128)(2,1)S(1)}, bf16[2,4,32,128]{3,2,1,0:T(8,128)(2,1)S(1)}, u32[]{:S(2)}, u32[]{:S(2)}) collective-permute-start(bf16[2,4,32,128]{3,2,1,0:T(8,128)(2,1)S(1)} %get-tuple-element.34), channel_id=1, source_target_pairs={{0,4},{2,6},{4,0},{6,2},{8,12},{10,14},{12,8},{14,10},{1,5},{3,7},... | collective-permute-start | bytes 196616 | tf_op jit(solution)/shard_map/ppermute | solution.py:299
  27.4 4.9 %collective-permute-start.9 = (bf16[4,32,128]{2,1,0:T(8,128)(2,1)S(1)}, bf16[4,32,128]{2,1,0:T(8,128)(2,1)S(1)}, u32[]{:S(2)}, u32[]{:S(2)}) collective-permute-start(bf16[4,32,128]{2,1,0:T(8,128)(2,1)S(1)} %get-tuple-element.36), channel_id=1, source_target_pairs={{0,8},{2,10},{4,12},{6,14},{8,0},{10,2},{12,4},{14,6},{1,9},{3,11}... | collective-permute-start | bytes 98312 | tf_op jit(solution)/shard_map/ppermute | solution.py:310

commit v5 on v4

--- a/solution.py
+++ b/solution.py
@@ -12,7 +12,7 @@
 IDROWS = 16
 PADROWS = 16
 LOADS = 4
-NEAR = 4
+ORDER = ((0, 1, 2), (1, 2, 0))
 VMEM_LIMIT = 48 * 1024 * 1024
 PREP_LIMIT = 53_100 * 1024
 
@@ -118,9 +118,8 @@
                 wts[block, at] = (weight * here).astype(jnp.bfloat16)
                 for j in range(JB):
                     total = phi[0][j : j + 1] * gx + phi[2][j : j + 1] * gz
-                    adv[j, block, at] = total.astype(jnp.bfloat16)
-    for j in range(JB):
-        acc_ref[j] = dot_nt(adv[j], wts[...])
+                    adv[pl.ds((2 * j + half) * nk, nk), at] = total.astype(jnp.bfloat16)
+    acc_ref[...] = dot_nt(adv[...], wts[...])
 
 
 def cross_kernel(
@@ -167,35 +166,41 @@
                     ).astype(jnp.bfloat16)
                 for j in range(JB):
                     for part, (phi, field) in enumerate(((phi0, f1), (phi1, gy), (phi2, f1))):
-                        adv[j, block, pl.ds(part * span + lane, nz)] = phi[j : j + 1] * field
+                        adv[pl.ds((2 * j + half) * nk, nk), pl.ds(part * span + lane, nz)] = (
+                            phi[j : j + 1] * field
+                        )
     per_half = nk // chunk
+    total = acc_ref[...] + dot_nt(adv[...], wts[...])
     for j in range(JB):
-        total = acc_ref[j] + dot_nt(adv[j], wts[...])
         for half in range(2):
             first = per_half * (m if half == 0 else 1 - m)
             for part in range(per_half):
-                piece = total[half * nk + part * chunk : half * nk + (part + 1) * chunk]
+                at = (2 * j + half) * nk + part * chunk
+                piece = total[at : at + chunk]
                 keep_ref[first + part, j] = piece[:, :nk]
                 send_ref[first + part, j] = piece[:, nk:].astype(jnp.bfloat16)
 
 
-def near_kernel(keep_ref, got_ref, mine_ref, *out_refs):
+def first_kernel(keep_ref, got_ref, keep_out, send_out):
+    m = lax.axis_index("modes")
     s = lax.axis_index("space")
-    low = lax.rem(s, NEAR)
-    for step, ref in enumerate((mine_ref,) + out_refs):
-        for level in range(mine_ref.shape[0]):
-            to = NEAR * level + jnp.bitwise_xor(low, step)
-            ref[level] = (keep_ref[to] + got_ref[to].astype(jnp.float32)).astype(ref.dtype)
-
-
-def far_kernel(mine_ref, *refs):
-    *parts, keep_ref, send_ref = refs
-    level = lax.div(lax.axis_index("space"), NEAR)
-    for ref, at in ((keep_ref, level), (send_ref, 1 - level)):
-        total = mine_ref[at]
-        for part in parts:
-            total = total + part[at].astype(jnp.float32)
-        ref[...] = total.astype(ref.dtype)
+    at = [jnp.where(m == 0, *stage) for stage in zip(*ORDER)]
+    own = lax.rem(lax.shift_right_logical(s, at[0]), 2)
+    for second in range(2):
+        for third in range(2):
+            rest = lax.shift_left(second, at[1]) + lax.shift_left(third, at[2])
+            for ref, bit in ((keep_out, own), (send_out, 1 - own)):
+                to = lax.shift_left(bit, at[0]) + rest
+                total = keep_ref[to] + got_ref[to].astype(jnp.float32)
+                ref[second, third] = total.astype(ref.dtype)
+
+
+def stage_kernel(stage, keep_ref, got_ref, keep_out, send_out):
+    m = lax.axis_index("modes")
+    bit = jnp.where(m == 0, ORDER[0][stage], ORDER[1][stage])
+    own = lax.rem(lax.shift_right_logical(lax.axis_index("space"), bit), 2)
+    for ref, at in ((keep_out, own), (send_out, 1 - own)):
+        ref[...] = (keep_ref[at] + got_ref[at].astype(jnp.float32)).astype(ref.dtype)
 
 
 def total_kernel(keep_ref, got_ref, out_ref):
@@ -249,11 +254,11 @@
 
     acc = pl.pallas_call(
         local_kernel,
-        out_shape=jax.ShapeDtypeStruct((JB, 2 * nk, 2 * nk), f32),
+        out_shape=jax.ShapeDtypeStruct((JB * 2 * nk, 2 * nk), f32),
         in_specs=[vmem, vmem, vmem, smem, smem],
         out_specs=vmem,
         scratch_shapes=[
-            pltpu.VMEM((JB, 2 * nk, nx // 2 * comps * nz), bf16),
+            pltpu.VMEM((JB * 2 * nk, nx // 2 * comps * nz), bf16),
             pltpu.VMEM((2 * nk, nx // 2 * comps * nz), bf16),
             pltpu.VMEM((nx, nz), f32),
         ],
@@ -274,7 +279,7 @@
         in_specs=[vmem] * 7 + [smem, smem, vmem],
         out_specs=[vmem] * 2,
         scratch_shapes=[
-            pltpu.VMEM((JB, 2 * nk, 3 * nx // 4 * comps * nz), bf16),
+            pltpu.VMEM((JB * 2 * nk, 3 * nx // 4 * comps * nz), bf16),
             pltpu.VMEM((2 * nk, 3 * nx // 4 * comps * nz), bf16),
             pltpu.VMEM((nx, nz), f32),
         ],
@@ -284,30 +289,25 @@
     )(own, other, zs, xs, zc, xc, weight_ids, weight_table, j_block, acc)
 
     got = lax.ppermute(send, "modes", [(0, 1), (1, 0)])
-    if n == 2 * NEAR:
-        piece = (JB, chunk, nk)
-        mine, *shares = pl.pallas_call(
-            near_kernel,
-            out_shape=[jax.ShapeDtypeStruct((2, *piece), f32)]
-            + [jax.ShapeDtypeStruct((2, *piece), bf16)] * (NEAR - 1),
-            in_specs=[vmem] * 2,
-            out_specs=[vmem] * NEAR,
-            compiler_params=params,
-            name="near",
-        )(keep, got)
-        parts = [
-            lax.ppermute(shares[step - 1], "space", [(s, s ^ step) for s in range(n)])
-            for step in (3, 1, 2)
-        ]
-        keep, send = pl.pallas_call(
-            far_kernel,
-            out_shape=[jax.ShapeDtypeStruct(piece, f32), jax.ShapeDtypeStruct(piece, bf16)],
-            in_specs=[vmem] * NEAR,
-            out_specs=[vmem] * 2,
-            compiler_params=params,
-            name="far",
-        )(mine, *parts)
-        got = lax.ppermute(send, "space", [(s, s ^ NEAR) for s in range(n)])
+    if n == 8:
+        left = (2, 2, JB, chunk, nk)
+        for stage in range(3):
+            if stage == 0:
+                body_of, dims = first_kernel, left
+            else:
+                body_of, dims = functools.partial(stage_kernel, stage), left[stage:]
+            keep, send = pl.pallas_call(
+                body_of,
+                out_shape=[jax.ShapeDtypeStruct(dims, f32), jax.ShapeDtypeStruct(dims, bf16)],
+                in_specs=[vmem] * 2,
+                out_specs=[vmem] * 2,
+                compiler_params=params,
+                name=f"stage{stage}",
+            )(keep, got)
+            pairs = [
+                (2 * s + m, 2 * (s ^ (1 << ORDER[m][stage])) + m) for s in range(n) for m in range(2)
+            ]
+            got = lax.ppermute(send, both, pairs)
         return pl.pallas_call(
             total_kernel,
             out_shape=jax.ShapeDtypeStruct((chunk, JB, nk), f32),

time: 33.2 us -> 37 us (1.11)
  waiting for transfers between devices: 10.5 us -> 19.1 us
  starting transfers between devices: 13.7 us -> 8.68 us
    ppermute x4 -> x3, waiting for transfers between devices: 4.79 us -> 13.4 us  [on_device(): got = lax.ppermute(send, both, pairs)]
    ppermute x4 -> x3, starting transfers between devices: 6.13 us -> 1.11 us  [on_device(): got = lax.ppermute(send, both, pairs)]
    pallas_call x3 -> x4, Pallas kernels: 3.03 us -> 3.12 us  [the longest x1 3.01 us: on_device(): pl.pallas_call(local_kernel, out_shape=jax.ShapeDtypeStruct((JB * 2 * nk,...]
  transfers between devices with their start and end apart: 10 -> 9, of which waited for: 7 -> 7; matrix products, arithmetic and copies ran while one was open for 0% -> 0% of each run, Pallas kernels for 9% -> 8%
where the time goes in v5:
time: 37 us; the launch traced here: 36.8 us
  waiting for transfers between devices  19.1 us (52%)
  starting transfers between devices  8.68 us (23%)
  Pallas kernels  7.68 us (21%)
  between operations  0.73 us (2%)
  local copies, waits for them, and re-layouts  0.66 us (2%)
    ppermute x3, waiting for transfers between devices, on_device(): got = lax.ppermute(send, both, pairs)  13.4 us
    ppermute x1, starting transfers between devices, on_device(): zs = lax.ppermute(zs, both, same(z_pairs))  4.66 us
    pallas_call x1, Pallas kernels, on_device(): pl.pallas_call(local_kernel, out_shape=jax.ShapeDtypeStruct((JB * 2 * nk,...  3.01 us
    pallas_call x1, Pallas kernels, on_device(): pl.pallas_call(functools.partial(cross_kernel, chunk, n), out_shape=[jax....  2.4 us
    ppermute x1, waiting for transfers between devices, on_device(): xs = lax.ppermute(xs, both, same(x_pairs))  1.72 us
    ppermute x1, starting transfers between devices, on_device(): zc = lax.ppermute(zc, both, cross(z_pairs))  1.72 us
    pallas_call x1, Pallas kernels, on_device(): pl.pallas_call(prep_kernel, out_shape=[jax.ShapeDtypeStruct((six, comps,...  1.46 us
    ppermute x1, waiting for transfers between devices, on_device(): xc = lax.ppermute(xc, both, cross(x_pairs))  1.42 us
  transfers between devices with their start and end apart: 9, of which 7 were waited for; matrix products, arithmetic and copies ran while one was open for 0% of the time, Pallas kernels for 8%

profile of v5, /device:TPU:0, one launch (start us, length us, event | category | flops | bytes accessed | tf_op | source)
XLA Modules:
  0.0 36.8 jit_solution(10835523701274009797)
XLA Ops:
  0.0 1.5 %prep.1 = (bf16[6,3,128,128]{3,2,1,0:T(8,128)(2,1)S(1)}, bf16[6,3,128,128]{3,2,1,0:T(8,128)(2,1)S(1)}, bf16[784,128]{1,0:T(8,128)(2,1)S(1)}, bf16[784,128]{1,0:T...) custom-call(bf16[128,3,1,8,128]{4,3,2,1,0:T(8,128)(2,1)} %modes_hbm.1), custom_call_target="tpu_custom_call" | custom-call | tf_op jit(solution)/shard_map/prep/pallas_call | solution.py:220
  1.5 0.0 copy-start
  1.5 0.5 %collective-permute-start = (bf16[6,3,128,128]{3,2,1,0:T(8,128)(2,1)S(1)}, bf16[6,3,128,128]{3,2,1,0:T(8,128)(2,1)S(1)}, u32[]{:S(2)}, u32[]{:S(2)}) collective-permute-start(bf16[6,3,128,128]{3,2,1,0:T(8,128)(2,1)S(1)} %get-tuple-element.22), channel_id=1, source_target_pairs={{0,1},{1,0},{2,3},{3,2},{4,5},{5,4},{6,7},{7,6},{8,9},{9,8},{10,11... | collective-permute-start | bytes 1769480 | tf_op jit(solution)/shard_map/ppermute | solution.py:241
  2.0 4.7 %collective-permute-start.1 = (bf16[784,128]{1,0:T(8,128)(2,1)S(1)}, bf16[784,128]{1,0:T(8,128)(2,1)S(1)}, u32[]{:S(2)}, u32[]{:S(2)}) collective-permute-start(bf16[784,128]{1,0:T(8,128)(2,1)S(1)} %get-tuple-element.23), channel_id=1, source_target_pairs={{0,12},{1,13},{2,6},{3,7},{4,0},{5,1},{6,10},{7,11},{8,4},{9,5},{1... | collective-permute-start | bytes 602120 | tf_op jit(solution)/shard_map/ppermute | solution.py:242
  6.7 0.0 collective-permute-start.2
  6.7 0.0 collective-permute-done._.other_ref
  6.7 0.0 copy-done
  6.7 1.7 %collective-permute-start.3 = (bf16[784,128]{1,0:T(8,128)(2,1)S(1)}, bf16[784,128]{1,0:T(8,128)(2,1)S(1)}, u32[]{:S(2)}, u32[]{:S(2)}) collective-permute-start(bf16[784,128]{1,0:T(8,128)(2,1)S(1)} %get-tuple-element.27), channel_id=1, source_target_pairs={{0,13},{1,12},{2,7},{3,6},{4,1},{5,0},{6,11},{7,10},{8,5},{9,4},{1... | collective-permute-start | bytes 602120 | tf_op jit(solution)/shard_map/ppermute | solution.py:252
  8.4 0.0 collective-permute-start.4
  9.1 0.0 copy-start.1
  9.1 0.6 %copy-done.1 = f32[16]{0:T(128)S(1)} copy-done((f32[16]{0:T(128)S(1)}, f32[16]{0:T(128)}, u32[]{:S(2)}) %copy-start.1) | copy-done | bytes 88
  9.7 3.0 %local.1.acc_ref = f32[1024,256]{1,0:T(8,128)S(1)} custom-call(bf16[6,3,128,128]{3,2,1,0:T(8,128)(2,1)S(1)} %get-tuple-element.21.own_ref, bf16[6,3,128,128]{3,2,1,0:T(8,128)(2,1)S(1)} %collective-permute-done._.other_ref, s32[1,8,128]{2,1,0:T(8,128)S(1)} %copy-done, f32[16]{0:T(128)S(1)} %copy-done.1, s32[1]{0:T(128)S(6)} %copy.5.jb_ref), custom_call_target="tpu_custom_call" | custom-call | flops 900000000 | bytes 2400000 | tf_op jit(solution)/shard_map/local/pallas_call | solution.py:255
  12.8 0.0 collective-permute-done.1.zs_ref
  12.8 1.7 %collective-permute-done.2.xs_ref = bf16[784,128]{1,0:T(8,128)(2,1)S(1)} collective-permute-done((bf16[784,128]{1,0:T(8,128)(2,1)S(1)}, bf16[784,128]{1,0:T(8,128)(2,1)S(1)}, u32[]{:S(2)}, u32[]{:S(2)}) %collective-permute-start.2) | collective-permute-done | bytes 200736 | tf_op jit(solution)/shard_map/ppermute | solution.py:243
  14.5 1.3 %collective-permute-done.3.zc_ref = bf16[784,128]{1,0:T(8,128)(2,1)S(1)} collective-permute-done((bf16[784,128]{1,0:T(8,128)(2,1)S(1)}, bf16[784,128]{1,0:T(8,128)(2,1)S(1)}, u32[]{:S(2)}, u32[]{:S(2)}) %collective-permute-start.3) | collective-permute-done | bytes 200736 | tf_op jit(solution)/shard_map/ppermute | solution.py:252
  15.8 1.4 %collective-permute-done.4.xc_ref = bf16[784,128]{1,0:T(8,128)(2,1)S(1)} collective-permute-done((bf16[784,128]{1,0:T(8,128)(2,1)S(1)}, bf16[784,128]{1,0:T(8,128)(2,1)S(1)}, u32[]{:S(2)}, u32[]{:S(2)}) %collective-permute-start.4) | collective-permute-done | bytes 200736 | tf_op jit(solution)/shard_map/ppermute | solution.py:253
  17.2 2.4 %cross.1 = (f32[8,4,32,128]{3,2,1,0:T(8,128)S(1)}, bf16[8,4,32,128]{3,2,1,0:T(8,128)(2,1)S(1)}) custom-call(bf16[6,3,128,128]{3,2,1,0:T(8,128)(2,1)S(1)} %get-tuple-element.21.own_ref, bf16[6,3,128,128]{3,2,1,0:T(8,128)(2,1)S(1)} %collective-permute-done._.other_ref, bf16[784,128]{1,0:T(8,128)(2,1)S(1)} %collective-permute-done.1.zs_ref, ...), custom_call_target="tpu_custom_call" | custom-call | flops 1300000000 | bytes 4000000 | tf_op jit(solution)/shard_map/cross/pallas_call | solution.py:273
  19.6 0.7 %collective-permute-start.5 = (bf16[8,4,32,128]{3,2,1,0:T(8,128)(2,1)S(1)}, bf16[8,4,32,128]{3,2,1,0:T(8,128)(2,1)S(1)}, u32[]{:S(2)}, u32[]{:S(2)}) collective-permute-start(bf16[8,4,32,128]{3,2,1,0:T(8,128)(2,1)S(1)} %get-tuple-element.30), channel_id=1, source_target_pairs={{0,1},{1,0},{2,3},{3,2},{4,5},{5,4},{6,7},{7,6},{8,9},{9,8},{10,11... | collective-permute-start | bytes 786440 | tf_op jit(solution)/shard_map/ppermute | solution.py:291
  20.3 1.2 %collective-permute-done.5.got_ref = bf16[8,4,32,128]{3,2,1,0:T(8,128)(2,1)S(1)} collective-permute-done((bf16[8,4,32,128]{3,2,1,0:T(8,128)(2,1)S(1)}, bf16[8,4,32,128]{3,2,1,0:T(8,128)(2,1)S(1)}, u32[]{:S(2)}, u32[]{:S(2)}) %collective-permute-start.5) | collective-permute-done | bytes 262176 | tf_op jit(solution)/shard_map/ppermute | solution.py:291
  21.5 0.1 stage0.1
  21.5 0.5 %collective-permute-start.6 = (bf16[2,2,4,32,128]{4,3,2,1,0:T(8,128)(2,1)S(1)}, bf16[2,2,4,32,128]{4,3,2,1,0:T(8,128)(2,1)S(1)}, u32[]{:S(2)}, u32[]{:S(2)}) collective-permute-start(bf16[2,2,4,32,128]{4,3,2,1,0:T(8,128)(2,1)S(1)} %get-tuple-element.32), channel_id=1, source_target_pairs={{0,2},{1,5},{2,0},{3,7},{4,6},{5,1},{6,4},{7,3},{8,10},{9,13},{10,... | collective-permute-start | bytes 393224 | tf_op jit(solution)/shard_map/ppermute | solution.py:310
  22.1 4.5 %collective-permute-done.6.got_ref = bf16[2,2,4,32,128]{4,3,2,1,0:T(8,128)(2,1)S(1)} collective-permute-done((bf16[2,2,4,32,128]{4,3,2,1,0:T(8,128)(2,1)S(1)}, bf16[2,2,4,32,128]{4,3,2,1,0:T(8,128)(2,1)S(1)}, u32[]{:S(2)}, u32[]{:S(2)}) %collective-permute-start.6) | collective-permute-done | bytes 131104 | tf_op jit(solution)/shard_map/ppermute | solution.py:310
  26.6 0.1 collective-permute-start.7
  26.7 4.5 %collective-permute-done.7.got_ref = bf16[2,4,32,128]{3,2,1,0:T(8,128)(2,1)S(1)} collective-permute-done((bf16[2,4,32,128]{3,2,1,0:T(8,128)(2,1)S(1)}, bf16[2,4,32,128]{3,2,1,0:T(8,128)(2,1)S(1)}, u32[]{:S(2)}, u32[]{:S(2)}) %collective-permute-start.7) | collective-permute-done | bytes 65568 | tf_op jit(solution)/shard_map/ppermute | solution.py:310
  31.2 0.5 %collective-permute-start.8 = (bf16[4,32,128]{2,1,0:T(8,128)(2,1)S(1)}, bf16[4,32,128]{2,1,0:T(8,128)(2,1)S(1)}, u32[]{:S(2)}, u32[]{:S(2)}) collective-permute-start(bf16[4,32,128]{2,1,0:T(8,128)(2,1)S(1)} %get-tuple-element.36), channel_id=1, source_target_pairs={{0,8},{1,3},{2,10},{3,1},{4,12},{5,7},{6,14},{7,5},{8,0},{9,11},{1... | collective-permute-start | bytes 98312 | tf_op jit(solution)/shard_map/ppermute | solution.py:310
  31.8 4.4 %collective-permute-done.8.got_ref = bf16[4,32,128]{2,1,0:T(8,128)(2,1)S(1)} collective-permute-done((bf16[4,32,128]{2,1,0:T(8,128)(2,1)S(1)}, bf16[4,32,128]{2,1,0:T(8,128)(2,1)S(1)}, u32[]{:S(2)}, u32[]{:S(2)}) %collective-permute-start.8) | collective-permute-done | bytes 32800 | tf_op jit(solution)/shard_map/ppermute | solution.py:310
  36.1 0.7 %total.1 = f32[32,4,128]{2,1,0:T(4,128)} custom-call(f32[4,32,128]{2,1,0:T(8,128)S(1)} %get-tuple-element.35.keep_ref, bf16[4,32,128]{2,1,0:T(8,128)(2,1)S(1)} %collective-permute-done.8.got_ref), custom_call_target="tpu_custom_call" | custom-call | tf_op jit(solution)/shard_map/total/pallas_call | solution.py:311
  (3 shorter events, 0.1 us)
Async XLA Ops:
  1.5 5.2 %copy-start = (s32[1,8,128]{2,1,0:T(8,128)S(1)}, s32[1,8,128]{2,1,0:T(8,128)}, u32[]{:S(2)}) copy-start(s32[1,8,128]{2,1,0:T(8,128)} %ids_ref.5) | copy-start | bytes 12292
  1.5 5.2 %collective-permute-start = (bf16[6,3,128,128]{3,2,1,0:T(8,128)(2,1)S(1)}, bf16[6,3,128,128]{3,2,1,0:T(8,128)(2,1)S(1)}, u32[]{:S(2)}, u32[]{:S(2)}) collective-permute-start(bf16[6,3,128,128]{3,2,1,0:T(8,128)(2,1)S(1)} %get-tuple-element.22), channel_id=1, source_target_pairs={{0,1},{1,0},{2,3},{3,2},{4,5},{5,4},{6,7},{7,6},{8,9},{9,8},{10,11... | collective-permute-start | bytes 1769480 | tf_op jit(solution)/shard_map/ppermute | solution.py:241
  2.0 10.8 %collective-permute-start.1 = (bf16[784,128]{1,0:T(8,128)(2,1)S(1)}, bf16[784,128]{1,0:T(8,128)(2,1)S(1)}, u32[]{:S(2)}, u32[]{:S(2)}) collective-permute-start(bf16[784,128]{1,0:T(8,128)(2,1)S(1)} %get-tuple-element.23), channel_id=1, source_target_pairs={{0,12},{1,13},{2,6},{3,7},{4,0},{5,1},{6,10},{7,11},{8,4},{9,5},{1... | collective-permute-start | bytes 602120 | tf_op jit(solution)/shard_map/ppermute | solution.py:242
  6.7 7.8 %collective-permute-start.2 = (bf16[784,128]{1,0:T(8,128)(2,1)S(1)}, bf16[784,128]{1,0:T(8,128)(2,1)S(1)}, u32[]{:S(2)}, u32[]{:S(2)}) collective-permute-start(bf16[784,128]{1,0:T(8,128)(2,1)S(1)} %get-tuple-element.24), channel_id=1, source_target_pairs={{0,2},{1,3},{2,0},{3,1},{4,6},{5,7},{6,4},{7,5},{8,10},{9,11},{10,... | collective-permute-start | bytes 602120 | tf_op jit(solution)/shard_map/ppermute | solution.py:243
  6.7 9.1 %collective-permute-start.3 = (bf16[784,128]{1,0:T(8,128)(2,1)S(1)}, bf16[784,128]{1,0:T(8,128)(2,1)S(1)}, u32[]{:S(2)}, u32[]{:S(2)}) collective-permute-start(bf16[784,128]{1,0:T(8,128)(2,1)S(1)} %get-tuple-element.27), channel_id=1, source_target_pairs={{0,13},{1,12},{2,7},{3,6},{4,1},{5,0},{6,11},{7,10},{8,5},{9,4},{1... | collective-permute-start | bytes 602120 | tf_op jit(solution)/shard_map/ppermute | solution.py:252
  8.4 8.8 %collective-permute-start.4 = (bf16[784,128]{1,0:T(8,128)(2,1)S(1)}, bf16[784,128]{1,0:T(8,128)(2,1)S(1)}, u32[]{:S(2)}, u32[]{:S(2)}) collective-permute-start(bf16[784,128]{1,0:T(8,128)(2,1)S(1)} %get-tuple-element.28), channel_id=1, source_target_pairs={{0,3},{1,2},{2,1},{3,0},{4,7},{5,6},{6,5},{7,4},{8,11},{9,10},{10,... | collective-permute-start | bytes 602120 | tf_op jit(solution)/shard_map/ppermute | solution.py:253
  9.1 0.7 %copy-start.1 = (f32[16]{0:T(128)S(1)}, f32[16]{0:T(128)}, u32[]{:S(2)}) copy-start(f32[16]{0:T(128)} %table_ref.3) | copy-start | bytes 196
  19.6 1.8 %collective-permute-start.5 = (bf16[8,4,32,128]{3,2,1,0:T(8,128)(2,1)S(1)}, bf16[8,4,32,128]{3,2,1,0:T(8,128)(2,1)S(1)}, u32[]{:S(2)}, u32[]{:S(2)}) collective-permute-start(bf16[8,4,32,128]{3,2,1,0:T(8,128)(2,1)S(1)} %get-tuple-element.30), channel_id=1, source_target_pairs={{0,1},{1,0},{2,3},{3,2},{4,5},{5,4},{6,7},{7,6},{8,9},{9,8},{10,11... | collective-permute-start | bytes 786440 | tf_op jit(solution)/shard_map/ppermute | solution.py:291
  21.5 5.0 %collective-permute-start.6 = (bf16[2,2,4,32,128]{4,3,2,1,0:T(8,128)(2,1)S(1)}, bf16[2,2,4,32,128]{4,3,2,1,0:T(8,128)(2,1)S(1)}, u32[]{:S(2)}, u32[]{:S(2)}) collective-permute-start(bf16[2,2,4,32,128]{4,3,2,1,0:T(8,128)(2,1)S(1)} %get-tuple-element.32), channel_id=1, source_target_pairs={{0,2},{1,5},{2,0},{3,7},{4,6},{5,1},{6,4},{7,3},{8,10},{9,13},{10,... | collective-permute-start | bytes 393224 | tf_op jit(solution)/shard_map/ppermute | solution.py:310
  26.6 4.6 %collective-permute-start.7 = (bf16[2,4,32,128]{3,2,1,0:T(8,128)(2,1)S(1)}, bf16[2,4,32,128]{3,2,1,0:T(8,128)(2,1)S(1)}, u32[]{:S(2)}, u32[]{:S(2)}) collective-permute-start(bf16[2,4,32,128]{3,2,1,0:T(8,128)(2,1)S(1)} %get-tuple-element.34), channel_id=1, source_target_pairs={{0,4},{1,9},{2,6},{3,11},{4,0},{5,13},{6,2},{7,15},{8,12},{9,1},{1... | collective-permute-start | bytes 196616 | tf_op jit(solution)/shard_map/ppermute | solution.py:310
  31.2 4.9 %collective-permute-start.8 = (bf16[4,32,128]{2,1,0:T(8,128)(2,1)S(1)}, bf16[4,32,128]{2,1,0:T(8,128)(2,1)S(1)}, u32[]{:S(2)}, u32[]{:S(2)}) collective-permute-start(bf16[4,32,128]{2,1,0:T(8,128)(2,1)S(1)} %get-tuple-element.36), channel_id=1, source_target_pairs={{0,8},{1,3},{2,10},{3,1},{4,12},{5,7},{6,14},{7,5},{8,0},{9,11},{1... | collective-permute-start | bytes 98312 | tf_op jit(solution)/shard_map/ppermute | solution.py:310

commit v6 on v4

--- a/solution.py
+++ b/solution.py
@@ -118,74 +118,102 @@
                 wts[block, at] = (weight * here).astype(jnp.bfloat16)
                 for j in range(JB):
                     total = phi[0][j : j + 1] * gx + phi[2][j : j + 1] * gz
-                    adv[j, block, at] = total.astype(jnp.bfloat16)
-    for j in range(JB):
-        acc_ref[j] = dot_nt(adv[j], wts[...])
-
-
-def cross_kernel(
-    chunk, planes, own_ref, other_ref, zs_ref, xs_ref, zc_ref, xc_ref, ids_ref, table_ref, jb_ref, acc_ref,
-    keep_ref, send_ref, adv, wts, wscr,
+                    adv[pl.ds((2 * j + half) * nk, nk), at] = total.astype(jnp.bfloat16)
+    acc_ref[...] = dot_nt(adv[...], wts[...])
+
+
+def sign_of_plane():
+    return jnp.where(lax.rem(lax.axis_index("space"), 2) == 0, 0.5, -0.5)
+
+
+def early_kernel(
+    own_ref, other_ref, _, xs_ref, xc_ref, ids_ref, table_ref, jb_ref, acc_ref, out_ref, w1_ref, adv, wts, wscr
 ):
+    m = lax.axis_index("modes")
+    q = lax.rem(lax.axis_index("space"), 2)
+    rows, comps, nk, nz = own_ref.shape
+    rows -= 2
+    quarter = rows // 2
+    pick = picks(jb_ref, m, nk)
+    wscr[...] = weights_of(ids_ref[0], table_ref)
+    w1 = weights_of(xc_ref[pl.ds(quarter * comps * nk, IDROWS), :].astype(jnp.float32), table_ref)
+    for r in range(quarter):
+        row0 = 1 + quarter * q + r
+        weight0 = wscr[pl.ds(rows * m + quarter * q + r, 1), :]
+        weight1 = w1[IDROWS // quarter * r : IDROWS // quarter * r + 1]
+        phi0 = sign_of_plane() * picked(pick, own_ref[row0, 1], other_ref[row0, 1])
+        phi0 = phi0.astype(jnp.bfloat16)
+        for c in range(comps):
+            at = pl.ds((r * comps + c) * nz, nz)
+            src = pl.ds((r * comps + c) * nk, nk)
+            for half, (p0, p1) in enumerate(((own_ref, xs_ref), (other_ref, xc_ref))):
+                block = pl.ds(half * nk, nk)
+                f0, f1 = p0[row0, c], p1[src, :]
+                wts[block, at] = (weight0 * f0.astype(jnp.float32)).astype(jnp.bfloat16)
+                w1_ref[block, at] = (weight1 * f1.astype(jnp.float32)).astype(jnp.bfloat16)
+                for j in range(JB):
+                    adv[pl.ds((2 * j + half) * nk, nk), at] = phi0[j : j + 1] * f1
+    out_ref[...] = acc_ref[...] + dot_nt(adv[...], wts[...])
+
+
+def cross_kernel(classes_of, chunk, planes, has_w2, own_ref, other_ref, *refs):
+    zs_ref, xs_ref, zc_ref, xc_ref, w1_ref, table_ref, jb_ref, acc_ref, *refs = refs
+    if has_w2:
+        w2_ref, keep_ref, send_ref, adv = refs
+    else:
+        keep_ref, send_ref, w2_ref, adv = refs
     m = lax.axis_index("modes")
     plane = lax.axis_index("space")
     q = lax.rem(plane, 2)
     inside = jnp.where(jnp.logical_or(plane == 1, plane == planes - 2), 0.0, 1.0)
     inside = inside.astype(jnp.bfloat16)
-    sigma = jnp.where(q == 0, 0.5, -0.5)
     rows, comps, nk, nz = own_ref.shape
-    rows -= 2
-    quarter = rows // 2
+    quarter = (rows - 2) // 2
     span = quarter * comps * nz
     pick = picks(jb_ref, m, nk)
-    wscr[...] = weights_of(ids_ref[0], table_ref)
-    w1 = weights_of(xc_ref[pl.ds(span, IDROWS), :].astype(jnp.float32), table_ref)
-    w2 = weights_of(zc_ref[pl.ds(span, IDROWS), :].astype(jnp.float32), table_ref)
+    classes = [pl.multiple_of(chunk * cls, chunk) for cls in classes_of(plane)]
+    w2 = weights_of(zc_ref[pl.ds(quarter * comps * nk, IDROWS), :].astype(jnp.float32), table_ref)
     for r in range(quarter):
         row0 = 1 + quarter * q + r
-        weight0 = wscr[pl.ds(rows * m + quarter * q + r, 1), :]
-        idrow = IDROWS // quarter * r
-        weight1, weight2 = w1[idrow : idrow + 1], w2[idrow : idrow + 1]
         along = pl.ds((r * comps + 1) * nk, nk)
-        phi0 = (sigma * picked(pick, own_ref[row0, 1], other_ref[row0, 1])).astype(jnp.bfloat16)
-        phi1 = (sigma * picked(pick, xs_ref[along, :], xc_ref[along, :])).astype(jnp.bfloat16)
-        phi2 = (-sigma * picked(pick, zs_ref[along, :], zc_ref[along, :])).astype(jnp.bfloat16)
+        phi1 = sign_of_plane() * picked(pick, xs_ref[along, :], xc_ref[along, :])
+        phi2 = -sign_of_plane() * picked(pick, zs_ref[along, :], zc_ref[along, :])
+        phi1, phi2 = phi1.astype(jnp.bfloat16), phi2.astype(jnp.bfloat16)
+        weight2 = w2[IDROWS // quarter * r : IDROWS // quarter * r + 1]
         for c in range(comps):
             lane = (r * comps + c) * nz
-            src = pl.ds((r * comps + c) * nk, nk)
+            src = (r * comps + c) * nk
             for half, (p0, p1, p2) in enumerate(
                 ((own_ref, xs_ref, zs_ref), (other_ref, xc_ref, zc_ref))
             ):
-                block = pl.ds(half * nk, nk)
-                f0 = p0[row0, c]
-                f1 = p1[src, :]
-                f2 = inside * p2[src, :]
-                gy = f2 - f0
-                for part, (field, weight) in enumerate(((f0, weight0), (f1, weight1), (f2, weight2))):
-                    wts[block, pl.ds(part * span + lane, nz)] = (
-                        weight * field.astype(jnp.float32)
+                if not has_w2:
+                    f2 = inside * p2[pl.ds(src, nk), :]
+                    w2_ref[pl.ds(half * nk, nk), pl.ds(lane, nz)] = (
+                        weight2 * f2.astype(jnp.float32)
                     ).astype(jnp.bfloat16)
-                for j in range(JB):
-                    for part, (phi, field) in enumerate(((phi0, f1), (phi1, gy), (phi2, f1))):
-                        adv[j, block, pl.ds(part * span + lane, nz)] = phi[j : j + 1] * field
-    per_half = nk // chunk
-    for j in range(JB):
-        total = acc_ref[j] + dot_nt(adv[j], wts[...])
+                for at, cls in enumerate(classes):
+                    f0 = p0[row0, c, pl.ds(cls, chunk), :]
+                    f1 = p1[pl.ds(src + cls, chunk), :]
+                    gy = inside * p2[pl.ds(src + cls, chunk), :] - f0
+                    for j in range(JB):
+                        block = pl.ds(((2 * at + half) * JB + j) * chunk, chunk)
+                        adv[block, pl.ds(lane, nz)] = phi1[j : j + 1] * gy
+                        adv[block, pl.ds(span + lane, nz)] = phi2[j : j + 1] * f1
+    total = dot_nt(adv[:, pl.ds(0, span)], w1_ref[...])
+    total = total + dot_nt(adv[:, pl.ds(span, span)], w2_ref[...])
+    for at, cls in enumerate(classes):
         for half in range(2):
-            first = per_half * (m if half == 0 else 1 - m)
-            for part in range(per_half):
-                piece = total[half * nk + part * chunk : half * nk + (part + 1) * chunk]
-                keep_ref[first + part, j] = piece[:, :nk]
-                send_ref[first + part, j] = piece[:, nk:].astype(jnp.bfloat16)
-
-
-def near_kernel(keep_ref, got_ref, mine_ref, *out_refs):
-    s = lax.axis_index("space")
-    low = lax.rem(s, NEAR)
-    for step, ref in enumerate((mine_ref,) + out_refs):
-        for level in range(mine_ref.shape[0]):
-            to = NEAR * level + jnp.bitwise_xor(low, step)
-            ref[level] = (keep_ref[to] + got_ref[to].astype(jnp.float32)).astype(ref.dtype)
+            level = m if half == 0 else 1 - m
+            for j in range(JB):
+                first = ((2 * at + half) * JB + j) * chunk
+                piece = total[first : first + chunk] + acc_ref[pl.ds((2 * j + half) * nk + cls, chunk), :]
+                keep_ref[at, level, j] = piece[:, :nk]
+                send_ref[at, level, j] = piece[:, nk:].astype(jnp.bfloat16)
+
+
+def near_kernel(keep_ref, got_ref, *out_refs):
+    for at, ref in enumerate(out_refs):
+        ref[...] = (keep_ref[at] + got_ref[at].astype(jnp.float32)).astype(ref.dtype)
 
 
 def far_kernel(mine_ref, *refs):
@@ -244,60 +272,92 @@
         compiler_params=params,
         name="ids",
     )(weight_ids, zc, xc, other)
+    xc = lax.ppermute(xc, both, cross(x_pairs))
     zc = lax.ppermute(zc, both, cross(z_pairs))
-    xc = lax.ppermute(xc, both, cross(x_pairs))
-
+
+    def estimate(depth, size):
+        return pl.CostEstimate(
+            flops=2 * JB * (2 * nk) ** 2 * depth, bytes_accessed=size, transcendentals=0
+        )
+
+    depth = nx // 4 * comps * nz
     acc = pl.pallas_call(
         local_kernel,
-        out_shape=jax.ShapeDtypeStruct((JB, 2 * nk, 2 * nk), f32),
+        out_shape=jax.ShapeDtypeStruct((JB * 2 * nk, 2 * nk), f32),
         in_specs=[vmem, vmem, vmem, smem, smem],
         out_specs=vmem,
         scratch_shapes=[
-            pltpu.VMEM((JB, 2 * nk, nx // 2 * comps * nz), bf16),
-            pltpu.VMEM((2 * nk, nx // 2 * comps * nz), bf16),
+            pltpu.VMEM((JB * 2 * nk, 2 * depth), bf16),
+            pltpu.VMEM((2 * nk, 2 * depth), bf16),
             pltpu.VMEM((nx, nz), f32),
         ],
         compiler_params=params,
-        cost_estimate=pl.CostEstimate(flops=900_000_000, bytes_accessed=2_400_000, transcendentals=0),
+        cost_estimate=estimate(2 * depth, 2_400_000),
         name="local",
     )(own, other, weight_ids, weight_table, j_block)
-
-    per_target = 2 * nk // n
-    chunk = max(16, per_target)
-    pieces = 2 * nk // chunk
-    keep, send = pl.pallas_call(
-        functools.partial(cross_kernel, chunk, n),
+    acc, w1 = pl.pallas_call(
+        early_kernel,
         out_shape=[
-            jax.ShapeDtypeStruct((pieces, JB, chunk, nk), f32),
-            jax.ShapeDtypeStruct((pieces, JB, chunk, nk), bf16),
+            jax.ShapeDtypeStruct((JB * 2 * nk, 2 * nk), f32),
+            jax.ShapeDtypeStruct((2 * nk, depth), bf16),
         ],
-        in_specs=[vmem] * 7 + [smem, smem, vmem],
+        in_specs=[vmem, vmem, pl.BlockSpec(memory_space=pl.ANY)] + [vmem] * 3 + [smem, smem, vmem],
         out_specs=[vmem] * 2,
         scratch_shapes=[
-            pltpu.VMEM((JB, 2 * nk, 3 * nx // 4 * comps * nz), bf16),
-            pltpu.VMEM((2 * nk, 3 * nx // 4 * comps * nz), bf16),
+            pltpu.VMEM((JB * 2 * nk, depth), bf16),
+            pltpu.VMEM((2 * nk, depth), bf16),
             pltpu.VMEM((nx, nz), f32),
         ],
         compiler_params=params,
-        cost_estimate=pl.CostEstimate(flops=1_300_000_000, bytes_accessed=4_000_000, transcendentals=0),
-        name="cross",
-    )(own, other, zs, xs, zc, xc, weight_ids, weight_table, j_block, acc)
-
-    got = lax.ppermute(send, "modes", [(0, 1), (1, 0)])
+        cost_estimate=estimate(depth, 2_400_000),
+        name="early",
+    )(own, other, zs, xs, xc, weight_ids, weight_table, j_block, acc)
+
+    per_target = 2 * nk // n
+    chunk = max(16, per_target)
+
+    def crossed(count, classes_of, w2):
+        piece = (count, 2, JB, chunk, nk)
+        out_shape = [jax.ShapeDtypeStruct(piece, f32), jax.ShapeDtypeStruct(piece, bf16)]
+        if not w2:
+            out_shape.append(jax.ShapeDtypeStruct((2 * nk, depth), bf16))
+        return pl.pallas_call(
+            functools.partial(cross_kernel, classes_of, chunk, n, bool(w2)),
+            out_shape=out_shape,
+            in_specs=[vmem] * 7 + [smem, smem] + [vmem] * (1 + len(w2)),
+            out_specs=[vmem] * len(out_shape),
+            scratch_shapes=[pltpu.VMEM((count * 2 * JB * chunk, 2 * depth), bf16)],
+            compiler_params=params,
+            cost_estimate=estimate(depth, 4_000_000),
+            name="cross",
+        )(own, other, zs, xs, zc, xc, w1, weight_table, j_block, acc, *w2)
+
+    swap = [(0, 1), (1, 0)]
     if n == 2 * NEAR:
+        def partners(*steps):
+            return lambda s: [jnp.bitwise_xor(lax.rem(s, NEAR), step) for step in steps]
+
+        keep_a, send_a, w2 = crossed(2, partners(3, 1), ())
+        got_a = lax.ppermute(send_a, "modes", swap)
+        keep_b, send_b = crossed(2, partners(0, 2), (w2,))
+        got_b = lax.ppermute(send_b, "modes", swap)
         piece = (JB, chunk, nk)
-        mine, *shares = pl.pallas_call(
-            near_kernel,
-            out_shape=[jax.ShapeDtypeStruct((2, *piece), f32)]
-            + [jax.ShapeDtypeStruct((2, *piece), bf16)] * (NEAR - 1),
-            in_specs=[vmem] * 2,
-            out_specs=[vmem] * NEAR,
-            compiler_params=params,
-            name="near",
-        )(keep, got)
+
+        def summed(kinds, keep, got):
+            return pl.pallas_call(
+                near_kernel,
+                out_shape=[jax.ShapeDtypeStruct((2, *piece), kind) for kind in kinds],
+                in_specs=[vmem] * 2,
+                out_specs=[vmem] * 2,
+                compiler_params=params,
+                name="near",
+            )(keep, got)
+
+        part_3, part_1 = summed((bf16, bf16), keep_a, got_a)
+        mine, part_2 = summed((f32, bf16), keep_b, got_b)
         parts = [
-            lax.ppermute(shares[step - 1], "space", [(s, s ^ step) for s in range(n)])
-            for step in (3, 1, 2)
+            lax.ppermute(part, "space", [(s, s ^ step) for s in range(n)])
+            for part, step in ((part_3, 3), (part_1, 1), (part_2, 2))
         ]
         keep, send = pl.pallas_call(
             far_kernel,
@@ -316,10 +376,12 @@
             compiler_params=params,
             name="total",
         )(keep, got)
-    share = (keep + got).astype(bf16)
-    if chunk != per_target:
-        share = share.reshape(pieces, JB, chunk // per_target, per_target, nk)
-        share = share.transpose(0, 2, 1, 3, 4).reshape(n, JB, per_target, nk)
+
+    count = nk // chunk
+    keep, send, _ = crossed(count, lambda s: list(range(count)), ())
+    share = (keep + lax.ppermute(send, "modes", swap)).astype(bf16)
+    share = share.reshape(count, 2, JB, chunk // per_target, per_target, nk)
+    share = share.transpose(1, 0, 3, 2, 4, 5).reshape(n, JB, per_target, nk)
     parts = lax.all_to_all(share, "space", 0, 0, tiled=True)
     return jnp.sum(parts.astype(f32), axis=0).transpose(1, 0, 2)
 

time: 33.2 us -> 33.9 us (1.021)
  Pallas kernels: 7.42 us -> 9.2 us
  waiting for transfers between devices: 10.5 us -> 9.23 us
    pallas_call x3 -> x6, Pallas kernels: 5.22 us -> 7 us  [the longest x1 3.01 us: on_device(): pl.pallas_call(local_kernel, out_shape=jax.ShapeDtypeStruct((JB * 2 * nk,...]
    ppermute x1, starting transfers between devices: 0.01 us -> 1.57 us  [on_device(): xc = lax.ppermute(xc, both, cross(x_pairs))]
    ppermute x1, waiting for transfers between devices: 1.8 us -> 0.24 us  [on_device(): xs = lax.ppermute(xs, both, same(x_pairs))]
    ppermute x1, waiting for transfers between devices: 1.42 us -> 2.75 us  [on_device(): xc = lax.ppermute(xc, both, cross(x_pairs))]
    ppermute x1, waiting for transfers between devices: 1.33 us -> 0.01 us  [on_device(): zc = lax.ppermute(zc, both, cross(z_pairs))]
    ppermute x1, waiting for transfers between devices: 2.32 us -> 3.48 us  [on_device(): got = lax.ppermute(send, 'space', [(s, s ^ NEAR) for s in range(n)])]
    ppermute x1, starting transfers between devices: 2.56 us -> 1.4 us  [on_device(): got = lax.ppermute(send, 'space', [(s, s ^ NEAR) for s in range(n)])]
    ppermute x4 -> x5, waiting for transfers between devices: 3.63 us -> 2.75 us  [the longest x3 2.5 us: on_device(): lax.ppermute(part, 'space', [(s, s ^ step) for s in range(n)])]
  transfers between devices with their start and end apart: 10 -> 11, of which waited for: 7 -> 6; matrix products, arithmetic and copies ran while one was open for 0% -> 0% of each run, Pallas kernels for 9% -> 17%
where the time goes in v6:
time: 33.9 us; the launch traced here: 33.7 us
  starting transfers between devices  13.9 us (41%)
  waiting for transfers between devices  9.23 us (27%)
  Pallas kernels  9.2 us (27%)
  between operations  0.75 us (2%)
  local copies, waits for them, and re-layouts  0.66 us (2%)
    ppermute x1, starting transfers between devices, on_device(): zs = lax.ppermute(zs, both, same(z_pairs))  4.66 us
    ppermute x1, waiting for transfers between devices, on_device(): got = lax.ppermute(send, 'space', [(s, s ^ NEAR) for s in range(n)])  3.48 us
    ppermute x3, starting transfers between devices, on_device(): lax.ppermute(part, 'space', [(s, s ^ step) for s in range(n)])  3.38 us
    pallas_call x1, Pallas kernels, on_device(): pl.pallas_call(local_kernel, out_shape=jax.ShapeDtypeStruct((JB * 2 * nk,...  3.01 us
    ppermute x1, waiting for transfers between devices, on_device(): xc = lax.ppermute(xc, both, cross(x_pairs))  2.75 us
    pallas_call x2, Pallas kernels, crossed(): pl.pallas_call(functools.partial(cross_kernel, classes_of, chunk, n, bool...  2.58 us
    ppermute x3, waiting for transfers between devices, on_device(): lax.ppermute(part, 'space', [(s, s ^ step) for s in range(n)])  2.5 us
    ppermute x1, starting transfers between devices, on_device(): zc = lax.ppermute(zc, both, cross(z_pairs))  1.63 us
  transfers between devices with their start and end apart: 11, of which 6 were waited for; matrix products, arithmetic and copies ran while one was open for 0% of the time, Pallas kernels for 17%

profile of v6, /device:TPU:0, one launch (start us, length us, event | category | flops | bytes accessed | tf_op | source)
XLA Modules:
  0.0 33.7 jit_solution(4999454753635552557)
XLA Ops:
  0.0 1.5 %prep.1 = (bf16[6,3,128,128]{3,2,1,0:T(8,128)(2,1)S(1)}, bf16[6,3,128,128]{3,2,1,0:T(8,128)(2,1)S(1)}, bf16[784,128]{1,0:T(8,128)(2,1)S(1)}, bf16[784,128]{1,0:T...) custom-call(bf16[128,3,1,8,128]{4,3,2,1,0:T(8,128)(2,1)} %modes_hbm.1), custom_call_target="tpu_custom_call" | custom-call | tf_op jit(solution)/shard_map/prep/pallas_call | solution.py:243
  1.5 0.0 copy-start
  1.5 0.5 %collective-permute-start = (bf16[6,3,128,128]{3,2,1,0:T(8,128)(2,1)S(1)}, bf16[6,3,128,128]{3,2,1,0:T(8,128)(2,1)S(1)}, u32[]{:S(2)}, u32[]{:S(2)}) collective-permute-start(bf16[6,3,128,128]{3,2,1,0:T(8,128)(2,1)S(1)} %get-tuple-element.27), channel_id=1, source_target_pairs={{0,1},{1,0},{2,3},{3,2},{4,5},{5,4},{6,7},{7,6},{8,9},{9,8},{10,11... | collective-permute-start | bytes 1769480 | tf_op jit(solution)/shard_map/ppermute | solution.py:264
  2.0 4.7 %collective-permute-start.1 = (bf16[784,128]{1,0:T(8,128)(2,1)S(1)}, bf16[784,128]{1,0:T(8,128)(2,1)S(1)}, u32[]{:S(2)}, u32[]{:S(2)}) collective-permute-start(bf16[784,128]{1,0:T(8,128)(2,1)S(1)} %get-tuple-element.28), channel_id=1, source_target_pairs={{0,12},{1,13},{2,6},{3,7},{4,0},{5,1},{6,10},{7,11},{8,4},{9,5},{1... | collective-permute-start | bytes 602120 | tf_op jit(solution)/shard_map/ppermute | solution.py:265
  6.7 0.0 collective-permute-start.2
  6.7 0.0 collective-permute-done._.other_ref
  6.7 0.0 copy-done
  6.7 1.6 %collective-permute-start.4 = (bf16[784,128]{1,0:T(8,128)(2,1)S(1)}, bf16[784,128]{1,0:T(8,128)(2,1)S(1)}, u32[]{:S(2)}, u32[]{:S(2)}) collective-permute-start(bf16[784,128]{1,0:T(8,128)(2,1)S(1)} %get-tuple-element.33), channel_id=1, source_target_pairs={{0,3},{1,2},{2,1},{3,0},{4,7},{5,6},{6,5},{7,4},{8,11},{9,10},{10,... | collective-permute-start | bytes 602120 | tf_op jit(solution)/shard_map/ppermute | solution.py:275
  8.3 1.6 %collective-permute-start.3 = (bf16[784,128]{1,0:T(8,128)(2,1)S(1)}, bf16[784,128]{1,0:T(8,128)(2,1)S(1)}, u32[]{:S(2)}, u32[]{:S(2)}) collective-permute-start(bf16[784,128]{1,0:T(8,128)(2,1)S(1)} %get-tuple-element.32), channel_id=1, source_target_pairs={{0,13},{1,12},{2,7},{3,6},{4,1},{5,0},{6,11},{7,10},{8,5},{9,4},{1... | collective-permute-start | bytes 602120 | tf_op jit(solution)/shard_map/ppermute | solution.py:276
  10.6 0.0 copy-start.1
  10.6 0.6 %copy-done.1 = f32[16]{0:T(128)S(1)} copy-done((f32[16]{0:T(128)S(1)}, f32[16]{0:T(128)}, u32[]{:S(2)}) %copy-start.1) | copy-done | bytes 88
  11.2 3.0 %local.1.acc_ref = f32[1024,256]{1,0:T(8,128)S(1)} custom-call(bf16[6,3,128,128]{3,2,1,0:T(8,128)(2,1)S(1)} %get-tuple-element.26.own_ref, bf16[6,3,128,128]{3,2,1,0:T(8,128)(2,1)S(1)} %collective-permute-done._.other_ref, s32[1,8,128]{2,1,0:T(8,128)S(1)} %copy-done, f32[16]{0:T(128)S(1)} %copy-done.1, s32[1]{0:T(128)S(6)} %copy.5.jb_ref.refs_6_), custom_call_target="tpu_custom_call" | custom-call | flops 805306368 | bytes 2400000 | tf_op jit(solution)/shard_map/local/pallas_call | solution.py:284
  14.2 0.0 collective-permute-done.1._.refs_0_
  14.2 0.2 collective-permute-done.2.xs_ref.refs_1_
  14.5 2.7 %collective-permute-done.4.xc_ref.refs_3_ = bf16[784,128]{1,0:T(8,128)(2,1)S(1)} collective-permute-done((bf16[784,128]{1,0:T(8,128)(2,1)S(1)}, bf16[784,128]{1,0:T(8,128)(2,1)S(1)}, u32[]{:S(2)}, u32[]{:S(2)}) %collective-permute-start.4) | collective-permute-done | bytes 200736 | tf_op jit(solution)/shard_map/ppermute | solution.py:275
  17.2 1.3 %early.1 = (f32[1024,256]{1,0:T(8,128)S(1)}, bf16[256,768]{1,0:T(8,128)(2,1)S(1)}) custom-call(bf16[6,3,128,128]{3,2,1,0:T(8,128)(2,1)S(1)} %get-tuple-element.26.own_ref, bf16[6,3,128,128]{3,2,1,0:T(8,128)(2,1)S(1)} %collective-permute-done._.other_ref, bf16[784,128]{1,0:T(8,128)(2,1)S(1)} %collective-permute-done.1._.refs_0_, ...), custom_call_target="tpu_custom_call" | custom-call | flops 402653184 | bytes 2400000 | tf_op jit(solution)/shard_map/early/pallas_call | solution.py:298
  18.6 0.0 collective-permute-done.3.refs_2_
  18.6 1.3 %cross.2 = (f32[2,2,4,32,128]{4,3,2,1,0:T(8,128)S(1)}, bf16[2,2,4,32,128]{4,3,2,1,0:T(8,128)(2,1)S(1)}, bf16[256,768]{1,0:T(8,128)(2,1)S(1)}) custom-call(bf16[6,3,128,128]{3,2,1,0:T(8,128)(2,1)S(1)} %get-tuple-element.26.own_ref, bf16[6,3,128,128]{3,2,1,0:T(8,128)(2,1)S(1)} %collective-permute-done._.other_ref, ...), custom_call_target="tpu_custom_call" | custom-call | flops 402653184 | bytes 4000000 | tf_op jit(solution)/shard_map/cross/pallas_call | solution.py:324
  19.9 0.7 %collective-permute-start.6 = (bf16[2,2,4,32,128]{4,3,2,1,0:T(8,128)(2,1)S(1)}, bf16[2,2,4,32,128]{4,3,2,1,0:T(8,128)(2,1)S(1)}, u32[]{:S(2)}, u32[]{:S(2)}) collective-permute-start(bf16[2,2,4,32,128]{4,3,2,1,0:T(8,128)(2,1)S(1)} %get-tuple-element.41), channel_id=1, source_target_pairs={{0,1},{1,0},{2,3},{3,2},{4,5},{5,4},{6,7},{7,6},{8,9},{9,8},{10,11... | collective-permute-start | bytes 393224 | tf_op jit(solution)/shard_map/ppermute | solution.py:341
  20.6 1.3 %cross.3 = (f32[2,2,4,32,128]{4,3,2,1,0:T(8,128)S(1)}, bf16[2,2,4,32,128]{4,3,2,1,0:T(8,128)(2,1)S(1)}) custom-call(bf16[6,3,128,128]{3,2,1,0:T(8,128)(2,1)S(1)} %get-tuple-element.26.own_ref, bf16[6,3,128,128]{3,2,1,0:T(8,128)(2,1)S(1)} %collective-permute-done._.other_ref, bf16[784,128]{1,0:T(8,128)(2,1)S(1)} %collective-permute-done.1._.refs_0_, ...), custom_call_target="tpu_custom_call" | custom-call | flops 402653184 | bytes 4000000 | tf_op jit(solution)/shard_map/cross/pallas_call | solution.py:324
  21.9 0.1 collective-permute-start.5
  22.0 0.0 collective-permute-done.6.got_ref
  22.0 0.6 %collective-permute-start.7 = (bf16[2,4,32,128]{3,2,1,0:T(8,128)(2,1)S(1)}, bf16[2,4,32,128]{3,2,1,0:T(8,128)(2,1)S(1)}, u32[]{:S(2)}, u32[]{:S(2)}) collective-permute-start(bf16[2,4,32,128]{3,2,1,0:T(8,128)(2,1)S(1)} %get-tuple-element.42), channel_id=1, source_target_pairs={{0,6},{2,4},{4,2},{6,0},{8,14},{10,12},{12,10},{14,8},{1,7},{3,5},... | collective-permute-start | bytes 196616 | tf_op jit(solution)/shard_map/ppermute | solution.py:359
  22.5 0.5 %collective-permute-start.8 = (bf16[2,4,32,128]{3,2,1,0:T(8,128)(2,1)S(1)}, bf16[2,4,32,128]{3,2,1,0:T(8,128)(2,1)S(1)}, u32[]{:S(2)}, u32[]{:S(2)}) collective-permute-start(bf16[2,4,32,128]{3,2,1,0:T(8,128)(2,1)S(1)} %get-tuple-element.43), channel_id=1, source_target_pairs={{0,2},{2,0},{4,6},{6,4},{8,10},{10,8},{12,14},{14,12},{1,3},{3,1},... | collective-permute-start | bytes 196616 | tf_op jit(solution)/shard_map/ppermute | solution.py:359
  23.0 0.2 collective-permute-done.5.got_ref
  23.3 2.3 %collective-permute-start.9 = (bf16[2,4,32,128]{3,2,1,0:T(8,128)(2,1)S(1)}, bf16[2,4,32,128]{3,2,1,0:T(8,128)(2,1)S(1)}, u32[]{:S(2)}, u32[]{:S(2)}) collective-permute-start(bf16[2,4,32,128]{3,2,1,0:T(8,128)(2,1)S(1)} %get-tuple-element.44), channel_id=1, source_target_pairs={{0,4},{2,6},{4,0},{6,2},{8,12},{10,14},{12,8},{14,10},{1,5},{3,7},... | collective-permute-start | bytes 196616 | tf_op jit(solution)/shard_map/ppermute | solution.py:359
  25.7 2.2 %collective-permute-done.7.refs_0_ = bf16[2,4,32,128]{3,2,1,0:T(8,128)(2,1)S(1)} collective-permute-done((bf16[2,4,32,128]{3,2,1,0:T(8,128)(2,1)S(1)}, bf16[2,4,32,128]{3,2,1,0:T(8,128)(2,1)S(1)}, u32[]{:S(2)}, u32[]{:S(2)}) %collective-permute-start.7) | collective-permute-done | bytes 65568 | tf_op jit(solution)/shard_map/ppermute | solution.py:359
  27.9 0.3 collective-permute-done.8.refs_1_
  28.2 0.0 collective-permute-done.9.refs_2_
  28.2 1.4 %collective-permute-start.10 = (bf16[4,32,128]{2,1,0:T(8,128)(2,1)S(1)}, bf16[4,32,128]{2,1,0:T(8,128)(2,1)S(1)}, u32[]{:S(2)}, u32[]{:S(2)}) collective-permute-start(bf16[4,32,128]{2,1,0:T(8,128)(2,1)S(1)} %get-tuple-element.46), channel_id=1, source_target_pairs={{0,8},{2,10},{4,12},{6,14},{8,0},{10,2},{12,4},{14,6},{1,9},{3,11}... | collective-permute-start | bytes 98312 | tf_op jit(solution)/shard_map/ppermute | solution.py:370
  29.6 3.5 %collective-permute-done.10.got_ref = bf16[4,32,128]{2,1,0:T(8,128)(2,1)S(1)} collective-permute-done((bf16[4,32,128]{2,1,0:T(8,128)(2,1)S(1)}, bf16[4,32,128]{2,1,0:T(8,128)(2,1)S(1)}, u32[]{:S(2)}, u32[]{:S(2)}) %collective-permute-start.10) | collective-permute-done | bytes 32800 | tf_op jit(solution)/shard_map/ppermute | solution.py:370
  33.1 0.7 %total.1 = f32[32,4,128]{2,1,0:T(4,128)} custom-call(f32[4,32,128]{2,1,0:T(8,128)S(1)} %get-tuple-element.45.keep_ref, bf16[4,32,128]{2,1,0:T(8,128)(2,1)S(1)} %collective-permute-done.10.got_ref), custom_call_target="tpu_custom_call" | custom-call | tf_op jit(solution)/shard_map/total/pallas_call | solution.py:371
  (4 shorter events, 0.1 us)
Async XLA Ops:
  1.5 5.2 %copy-start = (s32[1,8,128]{2,1,0:T(8,128)S(1)}, s32[1,8,128]{2,1,0:T(8,128)}, u32[]{:S(2)}) copy-start(s32[1,8,128]{2,1,0:T(8,128)} %ids_ref.5) | copy-start | bytes 12292
  1.5 5.2 %collective-permute-start = (bf16[6,3,128,128]{3,2,1,0:T(8,128)(2,1)S(1)}, bf16[6,3,128,128]{3,2,1,0:T(8,128)(2,1)S(1)}, u32[]{:S(2)}, u32[]{:S(2)}) collective-permute-start(bf16[6,3,128,128]{3,2,1,0:T(8,128)(2,1)S(1)} %get-tuple-element.27), channel_id=1, source_target_pairs={{0,1},{1,0},{2,3},{3,2},{4,5},{5,4},{6,7},{7,6},{8,9},{9,8},{10,11... | collective-permute-start | bytes 1769480 | tf_op jit(solution)/shard_map/ppermute | solution.py:264
  2.0 12.2 %collective-permute-start.1 = (bf16[784,128]{1,0:T(8,128)(2,1)S(1)}, bf16[784,128]{1,0:T(8,128)(2,1)S(1)}, u32[]{:S(2)}, u32[]{:S(2)}) collective-permute-start(bf16[784,128]{1,0:T(8,128)(2,1)S(1)} %get-tuple-element.28), channel_id=1, source_target_pairs={{0,12},{1,13},{2,6},{3,7},{4,0},{5,1},{6,10},{7,11},{8,4},{9,5},{1... | collective-permute-start | bytes 602120 | tf_op jit(solution)/shard_map/ppermute | solution.py:265
  6.7 7.8 %collective-permute-start.2 = (bf16[784,128]{1,0:T(8,128)(2,1)S(1)}, bf16[784,128]{1,0:T(8,128)(2,1)S(1)}, u32[]{:S(2)}, u32[]{:S(2)}) collective-permute-start(bf16[784,128]{1,0:T(8,128)(2,1)S(1)} %get-tuple-element.29), channel_id=1, source_target_pairs={{0,2},{1,3},{2,0},{3,1},{4,6},{5,7},{6,4},{7,5},{8,10},{9,11},{10,... | collective-permute-start | bytes 602120 | tf_op jit(solution)/shard_map/ppermute | solution.py:266
  6.7 10.5 %collective-permute-start.4 = (bf16[784,128]{1,0:T(8,128)(2,1)S(1)}, bf16[784,128]{1,0:T(8,128)(2,1)S(1)}, u32[]{:S(2)}, u32[]{:S(2)}) collective-permute-start(bf16[784,128]{1,0:T(8,128)(2,1)S(1)} %get-tuple-element.33), channel_id=1, source_target_pairs={{0,3},{1,2},{2,1},{3,0},{4,7},{5,6},{6,5},{7,4},{8,11},{9,10},{10,... | collective-permute-start | bytes 602120 | tf_op jit(solution)/shard_map/ppermute | solution.py:275
  8.3 10.3 %collective-permute-start.3 = (bf16[784,128]{1,0:T(8,128)(2,1)S(1)}, bf16[784,128]{1,0:T(8,128)(2,1)S(1)}, u32[]{:S(2)}, u32[]{:S(2)}) collective-permute-start(bf16[784,128]{1,0:T(8,128)(2,1)S(1)} %get-tuple-element.32), channel_id=1, source_target_pairs={{0,13},{1,12},{2,7},{3,6},{4,1},{5,0},{6,11},{7,10},{8,5},{9,4},{1... | collective-permute-start | bytes 602120 | tf_op jit(solution)/shard_map/ppermute | solution.py:276
  10.6 0.7 %copy-start.1 = (f32[16]{0:T(128)S(1)}, f32[16]{0:T(128)}, u32[]{:S(2)}) copy-start(f32[16]{0:T(128)} %refs_5_.3) | copy-start | bytes 196
  19.9 2.0 %collective-permute-start.6 = (bf16[2,2,4,32,128]{4,3,2,1,0:T(8,128)(2,1)S(1)}, bf16[2,2,4,32,128]{4,3,2,1,0:T(8,128)(2,1)S(1)}, u32[]{:S(2)}, u32[]{:S(2)}) collective-permute-start(bf16[2,2,4,32,128]{4,3,2,1,0:T(8,128)(2,1)S(1)} %get-tuple-element.41), channel_id=1, source_target_pairs={{0,1},{1,0},{2,3},{3,2},{4,5},{5,4},{6,7},{7,6},{8,9},{9,8},{10,11... | collective-permute-start | bytes 393224 | tf_op jit(solution)/shard_map/ppermute | solution.py:341
  21.9 1.4 %collective-permute-start.5 = (bf16[2,2,4,32,128]{4,3,2,1,0:T(8,128)(2,1)S(1)}, bf16[2,2,4,32,128]{4,3,2,1,0:T(8,128)(2,1)S(1)}, u32[]{:S(2)}, u32[]{:S(2)}) collective-permute-start(bf16[2,2,4,32,128]{4,3,2,1,0:T(8,128)(2,1)S(1)} %get-tuple-element.38), channel_id=1, source_target_pairs={{0,1},{1,0},{2,3},{3,2},{4,5},{5,4},{6,7},{7,6},{8,9},{9,8},{10,11... | collective-permute-start | bytes 393224 | tf_op jit(solution)/shard_map/ppermute | solution.py:343
  22.0 5.9 %collective-permute-start.7 = (bf16[2,4,32,128]{3,2,1,0:T(8,128)(2,1)S(1)}, bf16[2,4,32,128]{3,2,1,0:T(8,128)(2,1)S(1)}, u32[]{:S(2)}, u32[]{:S(2)}) collective-permute-start(bf16[2,4,32,128]{3,2,1,0:T(8,128)(2,1)S(1)} %get-tuple-element.42), channel_id=1, source_target_pairs={{0,6},{2,4},{4,2},{6,0},{8,14},{10,12},{12,10},{14,8},{1,7},{3,5},... | collective-permute-start | bytes 196616 | tf_op jit(solution)/shard_map/ppermute | solution.py:359
  22.5 5.6 %collective-permute-start.8 = (bf16[2,4,32,128]{3,2,1,0:T(8,128)(2,1)S(1)}, bf16[2,4,32,128]{3,2,1,0:T(8,128)(2,1)S(1)}, u32[]{:S(2)}, u32[]{:S(2)}) collective-permute-start(bf16[2,4,32,128]{3,2,1,0:T(8,128)(2,1)S(1)} %get-tuple-element.43), channel_id=1, source_target_pairs={{0,2},{2,0},{4,6},{6,4},{8,10},{10,8},{12,14},{14,12},{1,3},{3,1},... | collective-permute-start | bytes 196616 | tf_op jit(solution)/shard_map/ppermute | solution.py:359
  23.3 4.8 %collective-permute-start.9 = (bf16[2,4,32,128]{3,2,1,0:T(8,128)(2,1)S(1)}, bf16[2,4,32,128]{3,2,1,0:T(8,128)(2,1)S(1)}, u32[]{:S(2)}, u32[]{:S(2)}) collective-permute-start(bf16[2,4,32,128]{3,2,1,0:T(8,128)(2,1)S(1)} %get-tuple-element.44), channel_id=1, source_target_pairs={{0,4},{2,6},{4,0},{6,2},{8,12},{10,14},{12,8},{14,10},{1,5},{3,7},... | collective-permute-start | bytes 196616 | tf_op jit(solution)/shard_map/ppermute | solution.py:359
  28.2 4.9 %collective-permute-start.10 = (bf16[4,32,128]{2,1,0:T(8,128)(2,1)S(1)}, bf16[4,32,128]{2,1,0:T(8,128)(2,1)S(1)}, u32[]{:S(2)}, u32[]{:S(2)}) collective-permute-start(bf16[4,32,128]{2,1,0:T(8,128)(2,1)S(1)} %get-tuple-element.46), channel_id=1, source_target_pairs={{0,8},{2,10},{4,12},{6,14},{8,0},{10,2},{12,4},{14,6},{1,9},{3,11}... | collective-permute-start | bytes 98312 | tf_op jit(solution)/shard_map/ppermute | solution.py:370

commit v7 on v6

--- a/solution.py
+++ b/solution.py
@@ -72,18 +72,30 @@
 
 def picks(jb_ref, m, nk):
     first = jb_ref[0] * JB
-    row = lax.broadcasted_iota(jnp.int32, (16, nk), 0)
-    col = lax.broadcasted_iota(jnp.int32, (16, nk), 1)
-    want = jnp.where(row < JB, first + row, -1)
-    own = (want == col + m * nk).astype(jnp.float32).astype(jnp.bfloat16)
-    other = (want == col + (1 - m) * nk).astype(jnp.float32).astype(jnp.bfloat16)
-    return own, other
+    owner = (first >= nk).astype(jnp.int32)
+    row = first - owner * nk
+    within = lax.rem(row, 16)
+    return owner == m, pl.multiple_of(row - within, 16), within
 
 
 def picked(pick, own, other):
-    return jnp.dot(pick[0], own, preferred_element_type=jnp.float32) + jnp.dot(
-        pick[1], other, preferred_element_type=jnp.float32
+    mine, block, within = pick
+    rows = jnp.where(
+        mine, own[pl.ds(block, 16), :].astype(jnp.float32), other[pl.ds(block, 16), :].astype(jnp.float32)
     )
+    result = rows[0:JB]
+    for start in range(JB, 16, JB):
+        result = jnp.where(within == start, rows[start : start + JB], result)
+    return result
+
+
+def spread(row):
+    return jnp.broadcast_to(row, (16, row.shape[1])).astype(jnp.bfloat16)[None]
+
+
+def scaled(tile, field):
+    rows, lanes = field.shape
+    return (tile * field.reshape(rows // 16, 16, lanes)).reshape(rows, lanes)
 
 
 def weights_of(ids, table_ref):
@@ -104,7 +116,7 @@
     pick = picks(jb_ref, m, nk)
     wscr[...] = weights_of(ids_ref[0], table_ref)
     for r in range(rows):
-        phi = [picked(pick, own_ref[r + 1, d], other_ref[r + 1, d]) for d in range(comps)]
+        phi = [picked(pick, own_ref.at[r + 1, d], other_ref.at[r + 1, d]) for d in range(comps)]
         weight = wscr[pl.ds(rows * m + r, 1), :]
         for c in range(comps):
             at = pl.ds((r * comps + c) * nz, nz)
@@ -141,8 +153,8 @@
         row0 = 1 + quarter * q + r
         weight0 = wscr[pl.ds(rows * m + quarter * q + r, 1), :]
         weight1 = w1[IDROWS // quarter * r : IDROWS // quarter * r + 1]
-        phi0 = sign_of_plane() * picked(pick, own_ref[row0, 1], other_ref[row0, 1])
-        phi0 = phi0.astype(jnp.bfloat16)
+        phi0 = sign_of_plane() * picked(pick, own_ref.at[row0, 1], other_ref.at[row0, 1])
+        phi0 = [spread(phi0[j : j + 1]) for j in range(JB)]
         for c in range(comps):
             at = pl.ds((r * comps + c) * nz, nz)
             src = pl.ds((r * comps + c) * nk, nk)
@@ -152,7 +164,7 @@
                 wts[block, at] = (weight0 * f0.astype(jnp.float32)).astype(jnp.bfloat16)
                 w1_ref[block, at] = (weight1 * f1.astype(jnp.float32)).astype(jnp.bfloat16)
                 for j in range(JB):
-                    adv[pl.ds((2 * j + half) * nk, nk), at] = phi0[j : j + 1] * f1
+                    adv[pl.ds((2 * j + half) * nk, nk), at] = scaled(phi0[j], f1)
     out_ref[...] = acc_ref[...] + dot_nt(adv[...], wts[...])
 
 
@@ -176,9 +188,10 @@
     for r in range(quarter):
         row0 = 1 + quarter * q + r
         along = pl.ds((r * comps + 1) * nk, nk)
-        phi1 = sign_of_plane() * picked(pick, xs_ref[along, :], xc_ref[along, :])
-        phi2 = -sign_of_plane() * picked(pick, zs_ref[along, :], zc_ref[along, :])
-        phi1, phi2 = phi1.astype(jnp.bfloat16), phi2.astype(jnp.bfloat16)
+        phi1 = sign_of_plane() * picked(pick, xs_ref.at[along], xc_ref.at[along])
+        phi2 = -sign_of_plane() * picked(pick, zs_ref.at[along], zc_ref.at[along])
+        phi1 = [spread(phi1[j : j + 1]) for j in range(JB)]
+        phi2 = [spread(phi2[j : j + 1]) for j in range(JB)]
         weight2 = w2[IDROWS // quarter * r : IDROWS // quarter * r + 1]
         for c in range(comps):
             lane = (r * comps + c) * nz
@@ -197,8 +210,8 @@
                     gy = inside * p2[pl.ds(src + cls, chunk), :] - f0
                     for j in range(JB):
                         block = pl.ds(((2 * at + half) * JB + j) * chunk, chunk)
-                        adv[block, pl.ds(lane, nz)] = phi1[j : j + 1] * gy
-                        adv[block, pl.ds(span + lane, nz)] = phi2[j : j + 1] * f1
+                        adv[block, pl.ds(lane, nz)] = scaled(phi1[j], gy)
+                        adv[block, pl.ds(span + lane, nz)] = scaled(phi2[j], f1)
     total = dot_nt(adv[:, pl.ds(0, span)], w1_ref[...])
     total = total + dot_nt(adv[:, pl.ds(span, span)], w2_ref[...])
     for at, cls in enumerate(classes):

time: 33.9 us -> 33.7 us (level)
  Pallas kernels: 9.2 us -> 8.72 us
  transfers between devices with their start and end apart: 11 -> 11, of which waited for: 6 -> 6; matrix products, arithmetic and copies ran while one was open for 0% -> 0% of each run, Pallas kernels for 17% -> 16%
where the time goes in v7:
time: 33.7 us; the launch traced here: 33.5 us
  starting transfers between devices  13.9 us (41%)
  waiting for transfers between devices  9.5 us (28%)
  Pallas kernels  8.72 us (26%)
  between operations  0.75 us (2%)
  local copies, waits for them, and re-layouts  0.66 us (2%)
    ppermute x1, starting transfers between devices, on_device(): zs = lax.ppermute(zs, both, same(z_pairs))  4.66 us
    ppermute x1, waiting for transfers between devices, on_device(): got = lax.ppermute(send, 'space', [(s, s ^ NEAR) for s in range(n)])  3.48 us
    ppermute x3, starting transfers between devices, on_device(): lax.ppermute(part, 'space', [(s, s ^ step) for s in range(n)])  3.38 us
    ppermute x1, waiting for transfers between devices, on_device(): xc = lax.ppermute(xc, both, cross(x_pairs))  2.75 us
    pallas_call x1, Pallas kernels, on_device(): pl.pallas_call(local_kernel, out_shape=jax.ShapeDtypeStruct((JB * 2 * nk,...  2.73 us
    ppermute x3, waiting for transfers between devices, on_device(): lax.ppermute(part, 'space', [(s, s ^ step) for s in range(n)])  2.5 us
    pallas_call x2, Pallas kernels, crossed(): pl.pallas_call(functools.partial(cross_kernel, classes_of, chunk, n, bool...  2.41 us
    ppermute x1, starting transfers between devices, on_device(): zc = lax.ppermute(zc, both, cross(z_pairs))  1.63 us
  transfers between devices with their start and end apart: 11, of which 6 were waited for; matrix products, arithmetic and copies ran while one was open for 0% of the time, Pallas kernels for 16%

profile of v7, /device:TPU:0, one launch (start us, length us, event | category | flops | bytes accessed | tf_op | source)
XLA Modules:
  0.0 33.5 jit_solution(16018773238756576523)
XLA Ops:
  0.0 1.5 %prep.1 = (bf16[6,3,128,128]{3,2,1,0:T(8,128)(2,1)S(1)}, bf16[6,3,128,128]{3,2,1,0:T(8,128)(2,1)S(1)}, bf16[784,128]{1,0:T(8,128)(2,1)S(1)}, bf16[784,128]{1,0:T...) custom-call(bf16[128,3,1,8,128]{4,3,2,1,0:T(8,128)(2,1)} %modes_hbm.1), custom_call_target="tpu_custom_call" | custom-call | tf_op jit(solution)/shard_map/prep/pallas_call | solution.py:256
  1.5 0.0 copy-start
  1.5 0.5 %collective-permute-start = (bf16[6,3,128,128]{3,2,1,0:T(8,128)(2,1)S(1)}, bf16[6,3,128,128]{3,2,1,0:T(8,128)(2,1)S(1)}, u32[]{:S(2)}, u32[]{:S(2)}) collective-permute-start(bf16[6,3,128,128]{3,2,1,0:T(8,128)(2,1)S(1)} %get-tuple-element.27), channel_id=1, source_target_pairs={{0,1},{1,0},{2,3},{3,2},{4,5},{5,4},{6,7},{7,6},{8,9},{9,8},{10,11... | collective-permute-start | bytes 1769480 | tf_op jit(solution)/shard_map/ppermute | solution.py:277
  2.0 4.7 %collective-permute-start.1 = (bf16[784,128]{1,0:T(8,128)(2,1)S(1)}, bf16[784,128]{1,0:T(8,128)(2,1)S(1)}, u32[]{:S(2)}, u32[]{:S(2)}) collective-permute-start(bf16[784,128]{1,0:T(8,128)(2,1)S(1)} %get-tuple-element.28), channel_id=1, source_target_pairs={{0,12},{1,13},{2,6},{3,7},{4,0},{5,1},{6,10},{7,11},{8,4},{9,5},{1... | collective-permute-start | bytes 602120 | tf_op jit(solution)/shard_map/ppermute | solution.py:278
  6.7 0.0 collective-permute-start.2
  6.7 0.0 collective-permute-done._.other_ref
  6.7 0.0 copy-done
  6.7 1.6 %collective-permute-start.4 = (bf16[784,128]{1,0:T(8,128)(2,1)S(1)}, bf16[784,128]{1,0:T(8,128)(2,1)S(1)}, u32[]{:S(2)}, u32[]{:S(2)}) collective-permute-start(bf16[784,128]{1,0:T(8,128)(2,1)S(1)} %get-tuple-element.33), channel_id=1, source_target_pairs={{0,3},{1,2},{2,1},{3,0},{4,7},{5,6},{6,5},{7,4},{8,11},{9,10},{10,... | collective-permute-start | bytes 602120 | tf_op jit(solution)/shard_map/ppermute | solution.py:288
  8.3 1.6 %collective-permute-start.3 = (bf16[784,128]{1,0:T(8,128)(2,1)S(1)}, bf16[784,128]{1,0:T(8,128)(2,1)S(1)}, u32[]{:S(2)}, u32[]{:S(2)}) collective-permute-start(bf16[784,128]{1,0:T(8,128)(2,1)S(1)} %get-tuple-element.32), channel_id=1, source_target_pairs={{0,13},{1,12},{2,7},{3,6},{4,1},{5,0},{6,11},{7,10},{8,5},{9,4},{1... | collective-permute-start | bytes 602120 | tf_op jit(solution)/shard_map/ppermute | solution.py:289
  10.6 0.0 copy-start.1
  10.6 0.6 %copy-done.1 = f32[16]{0:T(128)S(1)} copy-done((f32[16]{0:T(128)S(1)}, f32[16]{0:T(128)}, u32[]{:S(2)}) %copy-start.1) | copy-done | bytes 88
  11.2 2.7 %local.1.acc_ref = f32[1024,256]{1,0:T(8,128)S(1)} custom-call(bf16[6,3,128,128]{3,2,1,0:T(8,128)(2,1)S(1)} %get-tuple-element.26.own_ref, bf16[6,3,128,128]{3,2,1,0:T(8,128)(2,1)S(1)} %collective-permute-done._.other_ref, s32[1,8,128]{2,1,0:T(8,128)S(1)} %copy-done, f32[16]{0:T(128)S(1)} %copy-done.1, s32[1]{0:T(128)S(6)} %copy.5.jb_ref.refs_6_), custom_call_target="tpu_custom_call" | custom-call | flops 805306368 | bytes 2400000 | tf_op jit(solution)/shard_map/local/pallas_call | solution.py:297
  14.0 0.0 collective-permute-done.1._.refs_0_
  14.0 0.5 %collective-permute-done.2.xs_ref.refs_1_ = bf16[784,128]{1,0:T(8,128)(2,1)S(1)} collective-permute-done((bf16[784,128]{1,0:T(8,128)(2,1)S(1)}, bf16[784,128]{1,0:T(8,128)(2,1)S(1)}, u32[]{:S(2)}, u32[]{:S(2)}) %collective-permute-start.2) | collective-permute-done | bytes 200736 | tf_op jit(solution)/shard_map/ppermute | solution.py:279
  14.5 2.7 %collective-permute-done.4.xc_ref.refs_3_ = bf16[784,128]{1,0:T(8,128)(2,1)S(1)} collective-permute-done((bf16[784,128]{1,0:T(8,128)(2,1)S(1)}, bf16[784,128]{1,0:T(8,128)(2,1)S(1)}, u32[]{:S(2)}, u32[]{:S(2)}) %collective-permute-start.4) | collective-permute-done | bytes 200736 | tf_op jit(solution)/shard_map/ppermute | solution.py:288
  17.2 1.3 %early.1 = (f32[1024,256]{1,0:T(8,128)S(1)}, bf16[256,768]{1,0:T(8,128)(2,1)S(1)}) custom-call(bf16[6,3,128,128]{3,2,1,0:T(8,128)(2,1)S(1)} %get-tuple-element.26.own_ref, bf16[6,3,128,128]{3,2,1,0:T(8,128)(2,1)S(1)} %collective-permute-done._.other_ref, bf16[784,128]{1,0:T(8,128)(2,1)S(1)} %collective-permute-done.1._.refs_0_, ...), custom_call_target="tpu_custom_call" | custom-call | flops 402653184 | bytes 2400000 | tf_op jit(solution)/shard_map/early/pallas_call | solution.py:311
  18.6 0.0 collective-permute-done.3.refs_2_
  18.6 1.2 %cross.2 = (f32[2,2,4,32,128]{4,3,2,1,0:T(8,128)S(1)}, bf16[2,2,4,32,128]{4,3,2,1,0:T(8,128)(2,1)S(1)}, bf16[256,768]{1,0:T(8,128)(2,1)S(1)}) custom-call(bf16[6,3,128,128]{3,2,1,0:T(8,128)(2,1)S(1)} %get-tuple-element.26.own_ref, bf16[6,3,128,128]{3,2,1,0:T(8,128)(2,1)S(1)} %collective-permute-done._.other_ref, ...), custom_call_target="tpu_custom_call" | custom-call | flops 402653184 | bytes 4000000 | tf_op jit(solution)/shard_map/cross/pallas_call | solution.py:337
  19.8 0.7 %collective-permute-start.6 = (bf16[2,2,4,32,128]{4,3,2,1,0:T(8,128)(2,1)S(1)}, bf16[2,2,4,32,128]{4,3,2,1,0:T(8,128)(2,1)S(1)}, u32[]{:S(2)}, u32[]{:S(2)}) collective-permute-start(bf16[2,2,4,32,128]{4,3,2,1,0:T(8,128)(2,1)S(1)} %get-tuple-element.41), channel_id=1, source_target_pairs={{0,1},{1,0},{2,3},{3,2},{4,5},{5,4},{6,7},{7,6},{8,9},{9,8},{10,11... | collective-permute-start | bytes 393224 | tf_op jit(solution)/shard_map/ppermute | solution.py:354
  20.5 1.2 %cross.3 = (f32[2,2,4,32,128]{4,3,2,1,0:T(8,128)S(1)}, bf16[2,2,4,32,128]{4,3,2,1,0:T(8,128)(2,1)S(1)}) custom-call(bf16[6,3,128,128]{3,2,1,0:T(8,128)(2,1)S(1)} %get-tuple-element.26.own_ref, bf16[6,3,128,128]{3,2,1,0:T(8,128)(2,1)S(1)} %collective-permute-done._.other_ref, bf16[784,128]{1,0:T(8,128)(2,1)S(1)} %collective-permute-done.1._.refs_0_, ...), custom_call_target="tpu_custom_call" | custom-call | flops 402653184 | bytes 4000000 | tf_op jit(solution)/shard_map/cross/pallas_call | solution.py:337
  21.7 0.1 collective-permute-start.5
  21.8 0.0 collective-permute-done.6.got_ref
  21.8 0.5 %collective-permute-start.7 = (bf16[2,4,32,128]{3,2,1,0:T(8,128)(2,1)S(1)}, bf16[2,4,32,128]{3,2,1,0:T(8,128)(2,1)S(1)}, u32[]{:S(2)}, u32[]{:S(2)}) collective-permute-start(bf16[2,4,32,128]{3,2,1,0:T(8,128)(2,1)S(1)} %get-tuple-element.42), channel_id=1, source_target_pairs={{0,6},{2,4},{4,2},{6,0},{8,14},{10,12},{12,10},{14,8},{1,7},{3,5},... | collective-permute-start | bytes 196616 | tf_op jit(solution)/shard_map/ppermute | solution.py:372
  22.3 0.5 %collective-permute-start.8 = (bf16[2,4,32,128]{3,2,1,0:T(8,128)(2,1)S(1)}, bf16[2,4,32,128]{3,2,1,0:T(8,128)(2,1)S(1)}, u32[]{:S(2)}, u32[]{:S(2)}) collective-permute-start(bf16[2,4,32,128]{3,2,1,0:T(8,128)(2,1)S(1)} %get-tuple-element.43), channel_id=1, source_target_pairs={{0,2},{2,0},{4,6},{6,4},{8,10},{10,8},{12,14},{14,12},{1,3},{3,1},... | collective-permute-start | bytes 196616 | tf_op jit(solution)/shard_map/ppermute | solution.py:372
  22.8 0.2 collective-permute-done.5.got_ref
  23.1 2.3 %collective-permute-start.9 = (bf16[2,4,32,128]{3,2,1,0:T(8,128)(2,1)S(1)}, bf16[2,4,32,128]{3,2,1,0:T(8,128)(2,1)S(1)}, u32[]{:S(2)}, u32[]{:S(2)}) collective-permute-start(bf16[2,4,32,128]{3,2,1,0:T(8,128)(2,1)S(1)} %get-tuple-element.44), channel_id=1, source_target_pairs={{0,4},{2,6},{4,0},{6,2},{8,12},{10,14},{12,8},{14,10},{1,5},{3,7},... | collective-permute-start | bytes 196616 | tf_op jit(solution)/shard_map/ppermute | solution.py:372
  25.5 2.2 %collective-permute-done.7.refs_0_ = bf16[2,4,32,128]{3,2,1,0:T(8,128)(2,1)S(1)} collective-permute-done((bf16[2,4,32,128]{3,2,1,0:T(8,128)(2,1)S(1)}, bf16[2,4,32,128]{3,2,1,0:T(8,128)(2,1)S(1)}, u32[]{:S(2)}, u32[]{:S(2)}) %collective-permute-start.7) | collective-permute-done | bytes 65568 | tf_op jit(solution)/shard_map/ppermute | solution.py:372
  27.6 0.3 collective-permute-done.8.refs_1_
  28.0 0.0 collective-permute-done.9.refs_2_
  28.0 1.4 %collective-permute-start.10 = (bf16[4,32,128]{2,1,0:T(8,128)(2,1)S(1)}, bf16[4,32,128]{2,1,0:T(8,128)(2,1)S(1)}, u32[]{:S(2)}, u32[]{:S(2)}) collective-permute-start(bf16[4,32,128]{2,1,0:T(8,128)(2,1)S(1)} %get-tuple-element.46), channel_id=1, source_target_pairs={{0,8},{2,10},{4,12},{6,14},{8,0},{10,2},{12,4},{14,6},{1,9},{3,11}... | collective-permute-start | bytes 98312 | tf_op jit(solution)/shard_map/ppermute | solution.py:383
  29.4 3.5 %collective-permute-done.10.got_ref = bf16[4,32,128]{2,1,0:T(8,128)(2,1)S(1)} collective-permute-done((bf16[4,32,128]{2,1,0:T(8,128)(2,1)S(1)}, bf16[4,32,128]{2,1,0:T(8,128)(2,1)S(1)}, u32[]{:S(2)}, u32[]{:S(2)}) %collective-permute-start.10) | collective-permute-done | bytes 32800 | tf_op jit(solution)/shard_map/ppermute | solution.py:383
  32.9 0.7 %total.1 = f32[32,4,128]{2,1,0:T(4,128)} custom-call(f32[4,32,128]{2,1,0:T(8,128)S(1)} %get-tuple-element.45.keep_ref, bf16[4,32,128]{2,1,0:T(8,128)(2,1)S(1)} %collective-permute-done.10.got_ref), custom_call_target="tpu_custom_call" | custom-call | tf_op jit(solution)/shard_map/total/pallas_call | solution.py:384
  (4 shorter events, 0.1 us)
Async XLA Ops:
  1.5 5.2 %copy-start = (s32[1,8,128]{2,1,0:T(8,128)S(1)}, s32[1,8,128]{2,1,0:T(8,128)}, u32[]{:S(2)}) copy-start(s32[1,8,128]{2,1,0:T(8,128)} %ids_ref.5) | copy-start | bytes 12292
  1.5 5.2 %collective-permute-start = (bf16[6,3,128,128]{3,2,1,0:T(8,128)(2,1)S(1)}, bf16[6,3,128,128]{3,2,1,0:T(8,128)(2,1)S(1)}, u32[]{:S(2)}, u32[]{:S(2)}) collective-permute-start(bf16[6,3,128,128]{3,2,1,0:T(8,128)(2,1)S(1)} %get-tuple-element.27), channel_id=1, source_target_pairs={{0,1},{1,0},{2,3},{3,2},{4,5},{5,4},{6,7},{7,6},{8,9},{9,8},{10,11... | collective-permute-start | bytes 1769480 | tf_op jit(solution)/shard_map/ppermute | solution.py:277
  2.0 12.0 %collective-permute-start.1 = (bf16[784,128]{1,0:T(8,128)(2,1)S(1)}, bf16[784,128]{1,0:T(8,128)(2,1)S(1)}, u32[]{:S(2)}, u32[]{:S(2)}) collective-permute-start(bf16[784,128]{1,0:T(8,128)(2,1)S(1)} %get-tuple-element.28), channel_id=1, source_target_pairs={{0,12},{1,13},{2,6},{3,7},{4,0},{5,1},{6,10},{7,11},{8,4},{9,5},{1... | collective-permute-start | bytes 602120 | tf_op jit(solution)/shard_map/ppermute | solution.py:278
  6.7 7.8 %collective-permute-start.2 = (bf16[784,128]{1,0:T(8,128)(2,1)S(1)}, bf16[784,128]{1,0:T(8,128)(2,1)S(1)}, u32[]{:S(2)}, u32[]{:S(2)}) collective-permute-start(bf16[784,128]{1,0:T(8,128)(2,1)S(1)} %get-tuple-element.29), channel_id=1, source_target_pairs={{0,2},{1,3},{2,0},{3,1},{4,6},{5,7},{6,4},{7,5},{8,10},{9,11},{10,... | collective-permute-start | bytes 602120 | tf_op jit(solution)/shard_map/ppermute | solution.py:279
  6.7 10.5 %collective-permute-start.4 = (bf16[784,128]{1,0:T(8,128)(2,1)S(1)}, bf16[784,128]{1,0:T(8,128)(2,1)S(1)}, u32[]{:S(2)}, u32[]{:S(2)}) collective-permute-start(bf16[784,128]{1,0:T(8,128)(2,1)S(1)} %get-tuple-element.33), channel_id=1, source_target_pairs={{0,3},{1,2},{2,1},{3,0},{4,7},{5,6},{6,5},{7,4},{8,11},{9,10},{10,... | collective-permute-start | bytes 602120 | tf_op jit(solution)/shard_map/ppermute | solution.py:288
  8.3 10.3 %collective-permute-start.3 = (bf16[784,128]{1,0:T(8,128)(2,1)S(1)}, bf16[784,128]{1,0:T(8,128)(2,1)S(1)}, u32[]{:S(2)}, u32[]{:S(2)}) collective-permute-start(bf16[784,128]{1,0:T(8,128)(2,1)S(1)} %get-tuple-element.32), channel_id=1, source_target_pairs={{0,13},{1,12},{2,7},{3,6},{4,1},{5,0},{6,11},{7,10},{8,5},{9,4},{1... | collective-permute-start | bytes 602120 | tf_op jit(solution)/shard_map/ppermute | solution.py:289
  10.6 0.7 %copy-start.1 = (f32[16]{0:T(128)S(1)}, f32[16]{0:T(128)}, u32[]{:S(2)}) copy-start(f32[16]{0:T(128)} %refs_5_.3) | copy-start | bytes 196
  19.8 1.9 %collective-permute-start.6 = (bf16[2,2,4,32,128]{4,3,2,1,0:T(8,128)(2,1)S(1)}, bf16[2,2,4,32,128]{4,3,2,1,0:T(8,128)(2,1)S(1)}, u32[]{:S(2)}, u32[]{:S(2)}) collective-permute-start(bf16[2,2,4,32,128]{4,3,2,1,0:T(8,128)(2,1)S(1)} %get-tuple-element.41), channel_id=1, source_target_pairs={{0,1},{1,0},{2,3},{3,2},{4,5},{5,4},{6,7},{7,6},{8,9},{9,8},{10,11... | collective-permute-start | bytes 393224 | tf_op jit(solution)/shard_map/ppermute | solution.py:354
  21.7 1.4 %collective-permute-start.5 = (bf16[2,2,4,32,128]{4,3,2,1,0:T(8,128)(2,1)S(1)}, bf16[2,2,4,32,128]{4,3,2,1,0:T(8,128)(2,1)S(1)}, u32[]{:S(2)}, u32[]{:S(2)}) collective-permute-start(bf16[2,2,4,32,128]{4,3,2,1,0:T(8,128)(2,1)S(1)} %get-tuple-element.38), channel_id=1, source_target_pairs={{0,1},{1,0},{2,3},{3,2},{4,5},{5,4},{6,7},{7,6},{8,9},{9,8},{10,11... | collective-permute-start | bytes 393224 | tf_op jit(solution)/shard_map/ppermute | solution.py:356
  21.8 5.9 %collective-permute-start.7 = (bf16[2,4,32,128]{3,2,1,0:T(8,128)(2,1)S(1)}, bf16[2,4,32,128]{3,2,1,0:T(8,128)(2,1)S(1)}, u32[]{:S(2)}, u32[]{:S(2)}) collective-permute-start(bf16[2,4,32,128]{3,2,1,0:T(8,128)(2,1)S(1)} %get-tuple-element.42), channel_id=1, source_target_pairs={{0,6},{2,4},{4,2},{6,0},{8,14},{10,12},{12,10},{14,8},{1,7},{3,5},... | collective-permute-start | bytes 196616 | tf_op jit(solution)/shard_map/ppermute | solution.py:372
  22.3 5.6 %collective-permute-start.8 = (bf16[2,4,32,128]{3,2,1,0:T(8,128)(2,1)S(1)}, bf16[2,4,32,128]{3,2,1,0:T(8,128)(2,1)S(1)}, u32[]{:S(2)}, u32[]{:S(2)}) collective-permute-start(bf16[2,4,32,128]{3,2,1,0:T(8,128)(2,1)S(1)} %get-tuple-element.43), channel_id=1, source_target_pairs={{0,2},{2,0},{4,6},{6,4},{8,10},{10,8},{12,14},{14,12},{1,3},{3,1},... | collective-permute-start | bytes 196616 | tf_op jit(solution)/shard_map/ppermute | solution.py:372
  23.1 4.8 %collective-permute-start.9 = (bf16[2,4,32,128]{3,2,1,0:T(8,128)(2,1)S(1)}, bf16[2,4,32,128]{3,2,1,0:T(8,128)(2,1)S(1)}, u32[]{:S(2)}, u32[]{:S(2)}) collective-permute-start(bf16[2,4,32,128]{3,2,1,0:T(8,128)(2,1)S(1)} %get-tuple-element.44), channel_id=1, source_target_pairs={{0,4},{2,6},{4,0},{6,2},{8,12},{10,14},{12,8},{14,10},{1,5},{3,7},... | collective-permute-start | bytes 196616 | tf_op jit(solution)/shard_map/ppermute | solution.py:372
  28.0 4.9 %collective-permute-start.10 = (bf16[4,32,128]{2,1,0:T(8,128)(2,1)S(1)}, bf16[4,32,128]{2,1,0:T(8,128)(2,1)S(1)}, u32[]{:S(2)}, u32[]{:S(2)}) collective-permute-start(bf16[4,32,128]{2,1,0:T(8,128)(2,1)S(1)} %get-tuple-element.46), channel_id=1, source_target_pairs={{0,8},{2,10},{4,12},{6,14},{8,0},{10,2},{12,4},{14,6},{1,9},{3,11}... | collective-permute-start | bytes 98312 | tf_op jit(solution)/shard_map/ppermute | solution.py:383

commit v8 on v7

--- a/solution.py
+++ b/solution.py
@@ -54,11 +54,19 @@
         ref[pl.ds(quarter * comps * nk, pad), :] = jnp.zeros((pad, nz), jnp.bfloat16)
 
 
-def ids_kernel(ids_ref, zc_ref, xc_ref, _, zc_out, xc_out):
+def weights_of(ids, table_ref):
+    weight = jnp.zeros(ids.shape, jnp.float32)
+    for entry in range(NW):
+        weight = jnp.where(ids == entry, table_ref[entry], weight)
+    return weight
+
+
+def ids_kernel(ids_ref, table_ref, zc_ref, xc_ref, _, weight_out, zc_out, xc_out):
     m = lax.axis_index("modes")
     q = lax.rem(lax.axis_index("space"), 2)
     body, nz = xc_ref.shape
     quarter = ids_ref.shape[1] // 4
+    weight_out[...] = weights_of(ids_ref[0], table_ref)
     for ref, out, at in ((zc_ref, zc_out, 2 * (1 - m) + q), (xc_ref, xc_out, 2 * (1 - m) + 1 - q)):
         out[pl.ds(0, body), :] = ref[...]
         ids = [
@@ -98,28 +106,20 @@
     return (tile * field.reshape(rows // 16, 16, lanes)).reshape(rows, lanes)
 
 
-def weights_of(ids, table_ref):
-    weight = jnp.zeros(ids.shape, jnp.float32)
-    for entry in range(NW):
-        weight = jnp.where(ids == entry, table_ref[entry], weight)
-    return weight
-
-
 def dot_nt(a, b):
     return lax.dot_general(a, b, (((1,), (1,)), ((), ())), preferred_element_type=jnp.float32)
 
 
-def local_kernel(own_ref, other_ref, ids_ref, table_ref, jb_ref, acc_ref, adv, wts, wscr):
+def local_kernel(own_ref, other_ref, weight_ref, jb_ref, acc_ref, w0_ref, adv, wts):
     m = lax.axis_index("modes")
+    q = lax.rem(lax.axis_index("space"), 2)
     rows, comps, nk, nz = own_ref.shape
     rows -= 2
     pick = picks(jb_ref, m, nk)
-    wscr[...] = weights_of(ids_ref[0], table_ref)
     for r in range(rows):
         phi = [picked(pick, own_ref.at[r + 1, d], other_ref.at[r + 1, d]) for d in range(comps)]
-        weight = wscr[pl.ds(rows * m + r, 1), :]
+        weight = weight_ref[pl.ds(rows * m + r, 1), :]
         for c in range(comps):
-            at = pl.ds((r * comps + c) * nz, nz)
             for half, ref in enumerate((own_ref, other_ref)):
                 block = pl.ds(half * nk, nk)
                 here = ref[r + 1, c].astype(jnp.float32)
@@ -127,98 +127,83 @@
                 gz = 0.5 * (pltpu.roll(here, nz - 1, 1) - pltpu.roll(here, 1, 1))
                 gx = gx.astype(jnp.bfloat16).astype(jnp.float32)
                 gz = gz.astype(jnp.bfloat16).astype(jnp.float32)
-                wts[block, at] = (weight * here).astype(jnp.bfloat16)
+                wts[r, block, pl.ds(c * nz, nz)] = (weight * here).astype(jnp.bfloat16)
                 for j in range(JB):
                     total = phi[0][j : j + 1] * gx + phi[2][j : j + 1] * gz
-                    adv[pl.ds((2 * j + half) * nk, nk), at] = total.astype(jnp.bfloat16)
-    acc_ref[...] = dot_nt(adv[...], wts[...])
-
-
-def sign_of_plane():
-    return jnp.where(lax.rem(lax.axis_index("space"), 2) == 0, 0.5, -0.5)
-
-
-def early_kernel(
-    own_ref, other_ref, _, xs_ref, xc_ref, ids_ref, table_ref, jb_ref, acc_ref, out_ref, w1_ref, adv, wts, wscr
-):
-    m = lax.axis_index("modes")
-    q = lax.rem(lax.axis_index("space"), 2)
-    rows, comps, nk, nz = own_ref.shape
-    rows -= 2
+                    adv[r, pl.ds((2 * j + half) * nk, nk), pl.ds(c * nz, nz)] = total.astype(jnp.bfloat16)
+    total = dot_nt(adv[0], wts[0])
+    for r in range(1, rows):
+        total = total + dot_nt(adv[r], wts[r])
+    acc_ref[...] = total
     quarter = rows // 2
-    pick = picks(jb_ref, m, nk)
-    wscr[...] = weights_of(ids_ref[0], table_ref)
-    w1 = weights_of(xc_ref[pl.ds(quarter * comps * nk, IDROWS), :].astype(jnp.float32), table_ref)
     for r in range(quarter):
-        row0 = 1 + quarter * q + r
-        weight0 = wscr[pl.ds(rows * m + quarter * q + r, 1), :]
-        weight1 = w1[IDROWS // quarter * r : IDROWS // quarter * r + 1]
-        phi0 = sign_of_plane() * picked(pick, own_ref.at[row0, 1], other_ref.at[row0, 1])
-        phi0 = [spread(phi0[j : j + 1]) for j in range(JB)]
-        for c in range(comps):
-            at = pl.ds((r * comps + c) * nz, nz)
-            src = pl.ds((r * comps + c) * nk, nk)
-            for half, (p0, p1) in enumerate(((own_ref, xs_ref), (other_ref, xc_ref))):
-                block = pl.ds(half * nk, nk)
-                f0, f1 = p0[row0, c], p1[src, :]
-                wts[block, at] = (weight0 * f0.astype(jnp.float32)).astype(jnp.bfloat16)
-                w1_ref[block, at] = (weight1 * f1.astype(jnp.float32)).astype(jnp.bfloat16)
-                for j in range(JB):
-                    adv[pl.ds((2 * j + half) * nk, nk), at] = scaled(phi0[j], f1)
-    out_ref[...] = acc_ref[...] + dot_nt(adv[...], wts[...])
-
-
-def cross_kernel(classes_of, chunk, planes, has_w2, own_ref, other_ref, *refs):
-    zs_ref, xs_ref, zc_ref, xc_ref, w1_ref, table_ref, jb_ref, acc_ref, *refs = refs
-    if has_w2:
-        w2_ref, keep_ref, send_ref, adv = refs
+        w0_ref[r] = wts[quarter * q + r]
+
+
+def cross_kernel(classes_of, chunk, planes, has_weighted, own_ref, other_ref, *refs):
+    zs_ref, xs_ref, zc_ref, xc_ref, w0_ref, table_ref, jb_ref, acc_ref, *refs = refs
+    if has_weighted:
+        wts, keep_ref, send_ref, adv = refs
     else:
-        keep_ref, send_ref, w2_ref, adv = refs
+        keep_ref, send_ref, wts, adv = refs
     m = lax.axis_index("modes")
     plane = lax.axis_index("space")
     q = lax.rem(plane, 2)
+    sigma = jnp.where(q == 0, 0.5, -0.5)
     inside = jnp.where(jnp.logical_or(plane == 1, plane == planes - 2), 0.0, 1.0)
-    inside = inside.astype(jnp.bfloat16)
     rows, comps, nk, nz = own_ref.shape
     quarter = (rows - 2) // 2
     span = quarter * comps * nz
     pick = picks(jb_ref, m, nk)
     classes = [pl.multiple_of(chunk * cls, chunk) for cls in classes_of(plane)]
-    w2 = weights_of(zc_ref[pl.ds(quarter * comps * nk, IDROWS), :].astype(jnp.float32), table_ref)
+    if not has_weighted:
+        ids = pl.ds(quarter * comps * nk, IDROWS)
+        w1 = weights_of(xc_ref[ids, :].astype(jnp.float32), table_ref)
+        w2 = inside * weights_of(zc_ref[ids, :].astype(jnp.float32), table_ref)
+        for r in range(quarter):
+            wts[:, pl.ds(r * comps * nz, comps * nz)] = w0_ref[r]
+            row = IDROWS // quarter * r
+            for c in range(comps):
+                lane = (r * comps + c) * nz
+                src = pl.ds((r * comps + c) * nk, nk)
+                for half, (p1, p2) in enumerate(((xs_ref, zs_ref), (xc_ref, zc_ref))):
+                    block = pl.ds(half * nk, nk)
+                    for part, (field, weight) in enumerate(((p1, w1), (p2, w2)), 1):
+                        wts[block, pl.ds(part * span + lane, nz)] = (
+                            weight[row : row + 1] * field[src, :].astype(jnp.float32)
+                        ).astype(jnp.bfloat16)
+    phis = []
     for r in range(quarter):
         row0 = 1 + quarter * q + r
         along = pl.ds((r * comps + 1) * nk, nk)
-        phi1 = sign_of_plane() * picked(pick, xs_ref.at[along], xc_ref.at[along])
-        phi2 = -sign_of_plane() * picked(pick, zs_ref.at[along], zc_ref.at[along])
-        phi1 = [spread(phi1[j : j + 1]) for j in range(JB)]
-        phi2 = [spread(phi2[j : j + 1]) for j in range(JB)]
-        weight2 = w2[IDROWS // quarter * r : IDROWS // quarter * r + 1]
-        for c in range(comps):
-            lane = (r * comps + c) * nz
-            src = (r * comps + c) * nk
-            for half, (p0, p1, p2) in enumerate(
-                ((own_ref, xs_ref, zs_ref), (other_ref, xc_ref, zc_ref))
-            ):
-                if not has_w2:
-                    f2 = inside * p2[pl.ds(src, nk), :]
-                    w2_ref[pl.ds(half * nk, nk), pl.ds(lane, nz)] = (
-                        weight2 * f2.astype(jnp.float32)
-                    ).astype(jnp.bfloat16)
-                for at, cls in enumerate(classes):
+        phi0 = sigma * picked(pick, own_ref.at[row0, 1], other_ref.at[row0, 1])
+        phi1 = sigma * picked(pick, xs_ref.at[along], xc_ref.at[along])
+        phi2 = -sigma * picked(pick, zs_ref.at[along], zc_ref.at[along])
+        phis.append([[spread(phi[j : j + 1]) for j in range(JB)] for phi in (phi0, phi1, phi2)])
+    inside = inside.astype(jnp.bfloat16)
+    for at, cls in enumerate(classes):
+        for r in range(quarter):
+            row0 = 1 + quarter * q + r
+            phi0, phi1, phi2 = phis[r]
+            for c in range(comps):
+                lane = (r * comps + c) * nz
+                src = (r * comps + c) * nk
+                for half, (p0, p1, p2) in enumerate(
+                    ((own_ref, xs_ref, zs_ref), (other_ref, xc_ref, zc_ref))
+                ):
                     f0 = p0[row0, c, pl.ds(cls, chunk), :]
                     f1 = p1[pl.ds(src + cls, chunk), :]
                     gy = inside * p2[pl.ds(src + cls, chunk), :] - f0
                     for j in range(JB):
-                        block = pl.ds(((2 * at + half) * JB + j) * chunk, chunk)
-                        adv[block, pl.ds(lane, nz)] = scaled(phi1[j], gy)
-                        adv[block, pl.ds(span + lane, nz)] = scaled(phi2[j], f1)
-    total = dot_nt(adv[:, pl.ds(0, span)], w1_ref[...])
-    total = total + dot_nt(adv[:, pl.ds(span, span)], w2_ref[...])
-    for at, cls in enumerate(classes):
+                        here = pl.ds((half * JB + j) * chunk, chunk)
+                        adv[at, here, pl.ds(lane, nz)] = scaled(phi0[j], f1)
+                        adv[at, here, pl.ds(span + lane, nz)] = scaled(phi1[j], gy)
+                        adv[at, here, pl.ds(2 * span + lane, nz)] = scaled(phi2[j], f1)
+        total = dot_nt(adv[at], wts[...])
         for half in range(2):
             level = m if half == 0 else 1 - m
             for j in range(JB):
-                first = ((2 * at + half) * JB + j) * chunk
+                first = (half * JB + j) * chunk
                 piece = total[first : first + chunk] + acc_ref[pl.ds((2 * j + half) * nk + cls, chunk), :]
                 keep_ref[at, level, j] = piece[:, :nk]
                 send_ref[at, level, j] = piece[:, nk:].astype(jnp.bfloat16)
@@ -266,6 +251,7 @@
             pltpu.SemaphoreType.DMA((LOADS,)),
         ],
         compiler_params=pltpu.CompilerParams(vmem_limit_bytes=PREP_LIMIT),
+        cost_estimate=pl.CostEstimate(flops=1_500_000_000, bytes_accessed=2_800_000, transcendentals=0),
         name="prep",
     )(modes)
 
@@ -277,14 +263,15 @@
     other = lax.ppermute(to_core, "modes", [(0, 1), (1, 0)])
     zs = lax.ppermute(zs, both, same(z_pairs))
     xs = lax.ppermute(xs, both, same(x_pairs))
-    zc, xc = pl.pallas_call(
+    weight, zc, xc = pl.pallas_call(
         ids_kernel,
-        out_shape=[jax.ShapeDtypeStruct((body + IDROWS, nz), bf16)] * 2,
-        in_specs=[vmem] * 3 + [pl.BlockSpec(memory_space=pl.ANY)],
-        out_specs=[vmem] * 2,
+        out_shape=[jax.ShapeDtypeStruct((nx, nz), f32)]
+        + [jax.ShapeDtypeStruct((body + IDROWS, nz), bf16)] * 2,
+        in_specs=[vmem, smem, vmem, vmem, pl.BlockSpec(memory_space=pl.ANY)],
+        out_specs=[vmem] * 3,
         compiler_params=params,
         name="ids",
-    )(weight_ids, zc, xc, other)
+    )(weight_ids, weight_table, zc, xc, other)
     xc = lax.ppermute(xc, both, cross(x_pairs))
     zc = lax.ppermute(zc, both, cross(z_pairs))
 
@@ -294,56 +281,45 @@
         )
 
     depth = nx // 4 * comps * nz
-    acc = pl.pallas_call(
+    quarter = nx // 4
+    depth = quarter * comps * nz
+    acc, w0 = pl.pallas_call(
         local_kernel,
-        out_shape=jax.ShapeDtypeStruct((JB * 2 * nk, 2 * nk), f32),
-        in_specs=[vmem, vmem, vmem, smem, smem],
-        out_specs=vmem,
+        out_shape=[
+            jax.ShapeDtypeStruct((JB * 2 * nk, 2 * nk), f32),
+            jax.ShapeDtypeStruct((quarter, 2 * nk, comps * nz), bf16),
+        ],
+        in_specs=[vmem, vmem, vmem, smem],
+        out_specs=[vmem] * 2,
         scratch_shapes=[
-            pltpu.VMEM((JB * 2 * nk, 2 * depth), bf16),
-            pltpu.VMEM((2 * nk, 2 * depth), bf16),
-            pltpu.VMEM((nx, nz), f32),
+            pltpu.VMEM((2 * quarter, JB * 2 * nk, comps * nz), bf16),
+            pltpu.VMEM((2 * quarter, 2 * nk, comps * nz), bf16),
         ],
         compiler_params=params,
-        cost_estimate=estimate(2 * depth, 2_400_000),
+        cost_estimate=pl.CostEstimate(flops=900_000_000, bytes_accessed=2_400_000, transcendentals=0),
         name="local",
-    )(own, other, weight_ids, weight_table, j_block)
-    acc, w1 = pl.pallas_call(
-        early_kernel,
-        out_shape=[
-            jax.ShapeDtypeStruct((JB * 2 * nk, 2 * nk), f32),
-            jax.ShapeDtypeStruct((2 * nk, depth), bf16),
-        ],
-        in_specs=[vmem, vmem, pl.BlockSpec(memory_space=pl.ANY)] + [vmem] * 3 + [smem, smem, vmem],
-        out_specs=[vmem] * 2,
-        scratch_shapes=[
-            pltpu.VMEM((JB * 2 * nk, depth), bf16),
-            pltpu.VMEM((2 * nk, depth), bf16),
-            pltpu.VMEM((nx, nz), f32),
-        ],
-        compiler_params=params,
-        cost_estimate=estimate(depth, 2_400_000),
-        name="early",
-    )(own, other, zs, xs, xc, weight_ids, weight_table, j_block, acc)
+    )(own, other, weight, j_block)
 
     per_target = 2 * nk // n
     chunk = max(16, per_target)
 
-    def crossed(count, classes_of, w2):
+    def crossed(count, classes_of, weighted):
         piece = (count, 2, JB, chunk, nk)
         out_shape = [jax.ShapeDtypeStruct(piece, f32), jax.ShapeDtypeStruct(piece, bf16)]
-        if not w2:
-            out_shape.append(jax.ShapeDtypeStruct((2 * nk, depth), bf16))
+        if not weighted:
+            out_shape.append(jax.ShapeDtypeStruct((2 * nk, 3 * depth), bf16))
         return pl.pallas_call(
-            functools.partial(cross_kernel, classes_of, chunk, n, bool(w2)),
+            functools.partial(cross_kernel, classes_of, chunk, n, bool(weighted)),
             out_shape=out_shape,
-            in_specs=[vmem] * 7 + [smem, smem] + [vmem] * (1 + len(w2)),
+            in_specs=[vmem] * 7 + [smem, smem] + [vmem] * (1 + len(weighted)),
             out_specs=[vmem] * len(out_shape),
-            scratch_shapes=[pltpu.VMEM((count * 2 * JB * chunk, 2 * depth), bf16)],
+            scratch_shapes=[pltpu.VMEM((count, 2 * JB * chunk, 3 * depth), bf16)],
             compiler_params=params,
-            cost_estimate=estimate(depth, 4_000_000),
+            cost_estimate=pl.CostEstimate(
+                flops=900_000_000, bytes_accessed=4_000_000, transcendentals=0
+            ),
             name="cross",
-        )(own, other, zs, xs, zc, xc, w1, weight_table, j_block, acc, *w2)
+        )(own, other, zs, xs, zc, xc, w0, weight_table, j_block, acc, *weighted)
 
     swap = [(0, 1), (1, 0)]
     if n == 2 * NEAR:

time: 33.7 us -> 32.8 us (0.973)
  Pallas kernels: 8.72 us -> 8.03 us
  local copies, waits for them, and re-layouts: 0.66 us -> 0.01 us
  waiting for transfers between devices: 9.5 us -> 10.1 us
    ppermute x1, waiting for transfers between devices: 0.52 us -> 2.42 us  [on_device(): xs = lax.ppermute(xs, both, same(x_pairs))]
    ppermute x1, starting transfers between devices: 1.57 us -> 0.01 us  [on_device(): xc = lax.ppermute(xc, both, cross(x_pairs))]
    ppermute x1, waiting for transfers between devices: 2.75 us -> 1.42 us  [on_device(): xc = lax.ppermute(xc, both, cross(x_pairs))]
    ppermute x1, waiting for transfers between devices: 0.01 us -> 1.33 us  [on_device(): zc = lax.ppermute(zc, both, cross(z_pairs))]
    ppermute x1, starting transfers between devices: 1.4 us -> 2.65 us  [on_device(): got = lax.ppermute(send, 'space', [(s, s ^ NEAR) for s in range(n)])]
    ppermute x1, waiting for transfers between devices: 3.48 us -> 2.23 us  [on_device(): got = lax.ppermute(send, 'space', [(s, s ^ NEAR) for s in range(n)])]
    pallas_call x3 -> x2, Pallas kernels: 4.08 us -> 3 us  [the longest x1 2.42 us: on_device(): pl.pallas_call(local_kernel, out_shape=[jax.ShapeDtypeStruct((JB * 2 * nk...]
    unnamed x4, local copies, waits for them, and re-layouts: 0.66 us -> 0.01 us
  transfers between devices with their start and end apart: 11 -> 11, of which waited for: 6 -> 7; matrix products, arithmetic and copies ran while one was open for 0% -> 0% of each run, Pallas kernels for 16% -> 14%
where the time goes in v8:
time: 32.8 us; the launch traced here: 32.6 us
  starting transfers between devices  13.8 us (42%)
  waiting for transfers between devices  10.1 us (31%)
  Pallas kernels  8.03 us (24%)
  between operations  0.73 us (2%)
    ppermute x1, starting transfers between devices, on_device(): zs = lax.ppermute(zs, both, same(z_pairs))  4.66 us
    ppermute x3, starting transfers between devices, on_device(): lax.ppermute(part, 'space', [(s, s ^ step) for s in range(n)])  3.48 us
    pallas_call x2, Pallas kernels, crossed(): pl.pallas_call(functools.partial(cross_kernel, classes_of, chunk, n, bool...  2.79 us
    ppermute x1, starting transfers between devices, on_device(): got = lax.ppermute(send, 'space', [(s, s ^ NEAR) for s in range(n)])  2.65 us
    ppermute x3, waiting for transfers between devices, on_device(): lax.ppermute(part, 'space', [(s, s ^ step) for s in range(n)])  2.51 us
    pallas_call x1, Pallas kernels, on_device(): pl.pallas_call(local_kernel, out_shape=[jax.ShapeDtypeStruct((JB * 2 * nk...  2.42 us
    ppermute x1, waiting for transfers between devices, on_device(): xs = lax.ppermute(xs, both, same(x_pairs))  2.42 us
    ppermute x1, waiting for transfers between devices, on_device(): got = lax.ppermute(send, 'space', [(s, s ^ NEAR) for s in range(n)])  2.23 us
  transfers between devices with their start and end apart: 11, of which 7 were waited for; matrix products, arithmetic and copies ran while one was open for 0% of the time, Pallas kernels for 14%

profile of v8, /device:TPU:0, one launch (start us, length us, event | category | flops | bytes accessed | tf_op | source)
XLA Modules:
  0.0 32.6 jit_solution(15353463342917399099)
XLA Ops:
  0.0 0.0 copy-start.1
  0.0 0.0 copy-start
  0.0 1.5 %prep.1 = (bf16[6,3,128,128]{3,2,1,0:T(8,128)(2,1)S(1)}, bf16[6,3,128,128]{3,2,1,0:T(8,128)(2,1)S(1)}, bf16[784,128]{1,0:T(8,128)(2,1)S(1)}, bf16[784,128]{1,0:T...) custom-call(bf16[128,3,1,8,128]{4,3,2,1,0:T(8,128)(2,1)} %modes_hbm.1), custom_call_target="tpu_custom_call" | custom-call | flops 1500000000 | bytes 2800000 | tf_op jit(solution)/shard_map/prep/pallas_call | solution.py:241
  1.5 0.5 %collective-permute-start = (bf16[6,3,128,128]{3,2,1,0:T(8,128)(2,1)S(1)}, bf16[6,3,128,128]{3,2,1,0:T(8,128)(2,1)S(1)}, u32[]{:S(2)}, u32[]{:S(2)}) collective-permute-start(bf16[6,3,128,128]{3,2,1,0:T(8,128)(2,1)S(1)} %get-tuple-element.28), channel_id=1, source_target_pairs={{0,1},{1,0},{2,3},{3,2},{4,5},{5,4},{6,7},{7,6},{8,9},{9,8},{10,11... | collective-permute-start | bytes 1769480 | tf_op jit(solution)/shard_map/ppermute | solution.py:263
  2.0 4.7 %collective-permute-start.1 = (bf16[784,128]{1,0:T(8,128)(2,1)S(1)}, bf16[784,128]{1,0:T(8,128)(2,1)S(1)}, u32[]{:S(2)}, u32[]{:S(2)}) collective-permute-start(bf16[784,128]{1,0:T(8,128)(2,1)S(1)} %get-tuple-element.29), channel_id=1, source_target_pairs={{0,12},{1,13},{2,6},{3,7},{4,0},{5,1},{6,10},{7,11},{8,4},{9,5},{1... | collective-permute-start | bytes 602120 | tf_op jit(solution)/shard_map/ppermute | solution.py:264
  6.7 0.0 collective-permute-start.2
  6.7 0.0 collective-permute-done._.other_ref
  6.7 0.0 copy-done.1
  6.7 0.0 copy-done
  6.7 0.6 %ids.1 = (f32[8,128]{1,0:T(8,128)S(1)}, bf16[784,128]{1,0:T(8,128)(2,1)S(1)}, bf16[784,128]{1,0:T(8,128)(2,1)S(1)}) custom-call(s32[1,8,128]{2,1,0:T(8,128)S(1)} %copy-done.1, f32[16]{0:T(128)S(1)} %copy-done, bf16[768,128]{1,0:T(8,128)(2,1)S(1)} %get-tuple-element.31.zc_ref, bf16[768,128]{1,0:T(8,128)(2,1)S(1)} %get-tuple-element.32.xc_ref, ...), custom_call_target="tpu_custom_call" | custom-call | tf_op jit(solution)/shard_map/ids/pallas_call | solution.py:266
  7.3 1.7 %collective-permute-start.3 = (bf16[784,128]{1,0:T(8,128)(2,1)S(1)}, bf16[784,128]{1,0:T(8,128)(2,1)S(1)}, u32[]{:S(2)}, u32[]{:S(2)}) collective-permute-start(bf16[784,128]{1,0:T(8,128)(2,1)S(1)} %get-tuple-element.33), channel_id=1, source_target_pairs={{0,13},{1,12},{2,7},{3,6},{4,1},{5,0},{6,11},{7,10},{8,5},{9,4},{1... | collective-permute-start | bytes 602120 | tf_op jit(solution)/shard_map/ppermute | solution.py:276
  9.0 0.0 collective-permute-start.4
  9.6 2.4 %local.1 = (f32[1024,256]{1,0:T(8,128)S(1)}, bf16[2,256,384]{2,1,0:T(8,128)(2,1)S(1)}) custom-call(bf16[6,3,128,128]{3,2,1,0:T(8,128)(2,1)S(1)} %get-tuple-element.27.own_ref, bf16[6,3,128,128]{3,2,1,0:T(8,128)(2,1)S(1)} %collective-permute-done._.other_ref, f32[8,128]{1,0:T(8,128)S(1)} %get-tuple-element.35.weight_ref, s32[1]{0:T(128)S(6)} %copy.5.jb_ref.refs_6_), custom_call_target="tpu_custom_call" | custom-call | flops 900000000 | bytes 2400000 | tf_op jit(solution)/shard_map/local/pallas_call | solution.py:286
  12.1 0.0 collective-permute-done.1.refs_0_
  12.1 2.4 %collective-permute-done.2.refs_1_ = bf16[784,128]{1,0:T(8,128)(2,1)S(1)} collective-permute-done((bf16[784,128]{1,0:T(8,128)(2,1)S(1)}, bf16[784,128]{1,0:T(8,128)(2,1)S(1)}, u32[]{:S(2)}, u32[]{:S(2)}) %collective-permute-start.2) | collective-permute-done | bytes 200736 | tf_op jit(solution)/shard_map/ppermute | solution.py:265
  14.5 1.3 %collective-permute-done.3.refs_2_ = bf16[784,128]{1,0:T(8,128)(2,1)S(1)} collective-permute-done((bf16[784,128]{1,0:T(8,128)(2,1)S(1)}, bf16[784,128]{1,0:T(8,128)(2,1)S(1)}, u32[]{:S(2)}, u32[]{:S(2)}) %collective-permute-start.3) | collective-permute-done | bytes 200736 | tf_op jit(solution)/shard_map/ppermute | solution.py:276
  15.8 1.4 %collective-permute-done.4.refs_3_ = bf16[784,128]{1,0:T(8,128)(2,1)S(1)} collective-permute-done((bf16[784,128]{1,0:T(8,128)(2,1)S(1)}, bf16[784,128]{1,0:T(8,128)(2,1)S(1)}, u32[]{:S(2)}, u32[]{:S(2)}) %collective-permute-start.4) | collective-permute-done | bytes 200736 | tf_op jit(solution)/shard_map/ppermute | solution.py:275
  17.3 1.4 %cross.2 = (f32[2,2,4,32,128]{4,3,2,1,0:T(8,128)S(1)}, bf16[2,2,4,32,128]{4,3,2,1,0:T(8,128)(2,1)S(1)}, bf16[256,2304]{1,0:T(8,128)(2,1)S(1)}) custom-call(bf16[6,3,128,128]{3,2,1,0:T(8,128)(2,1)S(1)} %get-tuple-element.27.own_ref, bf16[6,3,128,128]{3,2,1,0:T(8,128)(2,1)S(1)} %collective-permute-done._.other_ref, ...), custom_call_target="tpu_custom_call" | custom-call | flops 900000000 | bytes 4000000 | tf_op jit(solution)/shard_map/cross/pallas_call | solution.py:311
  18.7 0.7 %collective-permute-start.6 = (bf16[2,2,4,32,128]{4,3,2,1,0:T(8,128)(2,1)S(1)}, bf16[2,2,4,32,128]{4,3,2,1,0:T(8,128)(2,1)S(1)}, u32[]{:S(2)}, u32[]{:S(2)}) collective-permute-start(bf16[2,2,4,32,128]{4,3,2,1,0:T(8,128)(2,1)S(1)} %get-tuple-element.43), channel_id=1, source_target_pairs={{0,1},{1,0},{2,3},{3,2},{4,5},{5,4},{6,7},{7,6},{8,9},{9,8},{10,11... | collective-permute-start | bytes 393224 | tf_op jit(solution)/shard_map/ppermute | solution.py:330
  19.3 1.4 %cross.3 = (f32[2,2,4,32,128]{4,3,2,1,0:T(8,128)S(1)}, bf16[2,2,4,32,128]{4,3,2,1,0:T(8,128)(2,1)S(1)}) custom-call(bf16[6,3,128,128]{3,2,1,0:T(8,128)(2,1)S(1)} %get-tuple-element.27.own_ref, bf16[6,3,128,128]{3,2,1,0:T(8,128)(2,1)S(1)} %collective-permute-done._.other_ref, bf16[784,128]{1,0:T(8,128)(2,1)S(1)} %collective-permute-done.1.refs_0_, ...), custom_call_target="tpu_custom_call" | custom-call | flops 900000000 | bytes 4000000 | tf_op jit(solution)/shard_map/cross/pallas_call | solution.py:311
  20.7 0.1 collective-permute-start.5
  20.8 0.0 collective-permute-done.6.got_ref
  20.9 0.5 %collective-permute-start.7 = (bf16[2,4,32,128]{3,2,1,0:T(8,128)(2,1)S(1)}, bf16[2,4,32,128]{3,2,1,0:T(8,128)(2,1)S(1)}, u32[]{:S(2)}, u32[]{:S(2)}) collective-permute-start(bf16[2,4,32,128]{3,2,1,0:T(8,128)(2,1)S(1)} %get-tuple-element.44), channel_id=1, source_target_pairs={{0,6},{2,4},{4,2},{6,0},{8,14},{10,12},{12,10},{14,8},{1,7},{3,5},... | collective-permute-start | bytes 196616 | tf_op jit(solution)/shard_map/ppermute | solution.py:348
  21.4 0.6 %collective-permute-start.8 = (bf16[2,4,32,128]{3,2,1,0:T(8,128)(2,1)S(1)}, bf16[2,4,32,128]{3,2,1,0:T(8,128)(2,1)S(1)}, u32[]{:S(2)}, u32[]{:S(2)}) collective-permute-start(bf16[2,4,32,128]{3,2,1,0:T(8,128)(2,1)S(1)} %get-tuple-element.45), channel_id=1, source_target_pairs={{0,2},{2,0},{4,6},{6,4},{8,10},{10,8},{12,14},{14,12},{1,3},{3,1},... | collective-permute-start | bytes 196616 | tf_op jit(solution)/shard_map/ppermute | solution.py:348
  22.0 0.1 collective-permute-done.5.got_ref
  22.2 2.3 %collective-permute-start.9 = (bf16[2,4,32,128]{3,2,1,0:T(8,128)(2,1)S(1)}, bf16[2,4,32,128]{3,2,1,0:T(8,128)(2,1)S(1)}, u32[]{:S(2)}, u32[]{:S(2)}) collective-permute-start(bf16[2,4,32,128]{3,2,1,0:T(8,128)(2,1)S(1)} %get-tuple-element.46), channel_id=1, source_target_pairs={{0,4},{2,6},{4,0},{6,2},{8,12},{10,14},{12,8},{14,10},{1,5},{3,7},... | collective-permute-start | bytes 196616 | tf_op jit(solution)/shard_map/ppermute | solution.py:348
  24.5 2.2 %collective-permute-done.7.refs_0_ = bf16[2,4,32,128]{3,2,1,0:T(8,128)(2,1)S(1)} collective-permute-done((bf16[2,4,32,128]{3,2,1,0:T(8,128)(2,1)S(1)}, bf16[2,4,32,128]{3,2,1,0:T(8,128)(2,1)S(1)}, u32[]{:S(2)}, u32[]{:S(2)}) %collective-permute-start.7) | collective-permute-done | bytes 65568 | tf_op jit(solution)/shard_map/ppermute | solution.py:348
  26.7 0.3 collective-permute-done.8.refs_1_
  27.0 0.0 collective-permute-done.9.refs_2_
  27.1 2.7 %collective-permute-start.10 = (bf16[4,32,128]{2,1,0:T(8,128)(2,1)S(1)}, bf16[4,32,128]{2,1,0:T(8,128)(2,1)S(1)}, u32[]{:S(2)}, u32[]{:S(2)}) collective-permute-start(bf16[4,32,128]{2,1,0:T(8,128)(2,1)S(1)} %get-tuple-element.48), channel_id=1, source_target_pairs={{0,8},{2,10},{4,12},{6,14},{8,0},{10,2},{12,4},{14,6},{1,9},{3,11}... | collective-permute-start | bytes 98312 | tf_op jit(solution)/shard_map/ppermute | solution.py:359
  29.7 2.2 %collective-permute-done.10.got_ref = bf16[4,32,128]{2,1,0:T(8,128)(2,1)S(1)} collective-permute-done((bf16[4,32,128]{2,1,0:T(8,128)(2,1)S(1)}, bf16[4,32,128]{2,1,0:T(8,128)(2,1)S(1)}, u32[]{:S(2)}, u32[]{:S(2)}) %collective-permute-start.10) | collective-permute-done | bytes 32800 | tf_op jit(solution)/shard_map/ppermute | solution.py:359
  31.9 0.7 %total.1 = f32[32,4,128]{2,1,0:T(4,128)} custom-call(f32[4,32,128]{2,1,0:T(8,128)S(1)} %get-tuple-element.47.keep_ref, bf16[4,32,128]{2,1,0:T(8,128)(2,1)S(1)} %collective-permute-done.10.got_ref), custom_call_target="tpu_custom_call" | custom-call | tf_op jit(solution)/shard_map/total/pallas_call | solution.py:360
  (3 shorter events, 0.1 us)
Async XLA Ops:
  0.0 6.7 %copy-start.1 = (s32[1,8,128]{2,1,0:T(8,128)S(1)}, s32[1,8,128]{2,1,0:T(8,128)}, u32[]{:S(2)}) copy-start(s32[1,8,128]{2,1,0:T(8,128)} %ids_ref.1) | copy-start | bytes 12292
  0.0 6.7 %copy-start = (f32[16]{0:T(128)S(1)}, f32[16]{0:T(128)}, u32[]{:S(2)}) copy-start(f32[16]{0:T(128)} %refs_5_.3) | copy-start | bytes 196
  1.5 5.2 %collective-permute-start = (bf16[6,3,128,128]{3,2,1,0:T(8,128)(2,1)S(1)}, bf16[6,3,128,128]{3,2,1,0:T(8,128)(2,1)S(1)}, u32[]{:S(2)}, u32[]{:S(2)}) collective-permute-start(bf16[6,3,128,128]{3,2,1,0:T(8,128)(2,1)S(1)} %get-tuple-element.28), channel_id=1, source_target_pairs={{0,1},{1,0},{2,3},{3,2},{4,5},{5,4},{6,7},{7,6},{8,9},{9,8},{10,11... | collective-permute-start | bytes 1769480 | tf_op jit(solution)/shard_map/ppermute | solution.py:263
  2.0 10.1 %collective-permute-start.1 = (bf16[784,128]{1,0:T(8,128)(2,1)S(1)}, bf16[784,128]{1,0:T(8,128)(2,1)S(1)}, u32[]{:S(2)}, u32[]{:S(2)}) collective-permute-start(bf16[784,128]{1,0:T(8,128)(2,1)S(1)} %get-tuple-element.29), channel_id=1, source_target_pairs={{0,12},{1,13},{2,6},{3,7},{4,0},{5,1},{6,10},{7,11},{8,4},{9,5},{1... | collective-permute-start | bytes 602120 | tf_op jit(solution)/shard_map/ppermute | solution.py:264
  6.7 7.8 %collective-permute-start.2 = (bf16[784,128]{1,0:T(8,128)(2,1)S(1)}, bf16[784,128]{1,0:T(8,128)(2,1)S(1)}, u32[]{:S(2)}, u32[]{:S(2)}) collective-permute-start(bf16[784,128]{1,0:T(8,128)(2,1)S(1)} %get-tuple-element.30), channel_id=1, source_target_pairs={{0,2},{1,3},{2,0},{3,1},{4,6},{5,7},{6,4},{7,5},{8,10},{9,11},{10,... | collective-permute-start | bytes 602120 | tf_op jit(solution)/shard_map/ppermute | solution.py:265
  7.3 8.6 %collective-permute-start.3 = (bf16[784,128]{1,0:T(8,128)(2,1)S(1)}, bf16[784,128]{1,0:T(8,128)(2,1)S(1)}, u32[]{:S(2)}, u32[]{:S(2)}) collective-permute-start(bf16[784,128]{1,0:T(8,128)(2,1)S(1)} %get-tuple-element.33), channel_id=1, source_target_pairs={{0,13},{1,12},{2,7},{3,6},{4,1},{5,0},{6,11},{7,10},{8,5},{9,4},{1... | collective-permute-start | bytes 602120 | tf_op jit(solution)/shard_map/ppermute | solution.py:276
  9.0 8.3 %collective-permute-start.4 = (bf16[784,128]{1,0:T(8,128)(2,1)S(1)}, bf16[784,128]{1,0:T(8,128)(2,1)S(1)}, u32[]{:S(2)}, u32[]{:S(2)}) collective-permute-start(bf16[784,128]{1,0:T(8,128)(2,1)S(1)} %get-tuple-element.34), channel_id=1, source_target_pairs={{0,3},{1,2},{2,1},{3,0},{4,7},{5,6},{6,5},{7,4},{8,11},{9,10},{10,... | collective-permute-start | bytes 602120 | tf_op jit(solution)/shard_map/ppermute | solution.py:275
  18.7 2.1 %collective-permute-start.6 = (bf16[2,2,4,32,128]{4,3,2,1,0:T(8,128)(2,1)S(1)}, bf16[2,2,4,32,128]{4,3,2,1,0:T(8,128)(2,1)S(1)}, u32[]{:S(2)}, u32[]{:S(2)}) collective-permute-start(bf16[2,2,4,32,128]{4,3,2,1,0:T(8,128)(2,1)S(1)} %get-tuple-element.43), channel_id=1, source_target_pairs={{0,1},{1,0},{2,3},{3,2},{4,5},{5,4},{6,7},{7,6},{8,9},{9,8},{10,11... | collective-permute-start | bytes 393224 | tf_op jit(solution)/shard_map/ppermute | solution.py:330
  20.7 1.4 %collective-permute-start.5 = (bf16[2,2,4,32,128]{4,3,2,1,0:T(8,128)(2,1)S(1)}, bf16[2,2,4,32,128]{4,3,2,1,0:T(8,128)(2,1)S(1)}, u32[]{:S(2)}, u32[]{:S(2)}) collective-permute-start(bf16[2,2,4,32,128]{4,3,2,1,0:T(8,128)(2,1)S(1)} %get-tuple-element.40), channel_id=1, source_target_pairs={{0,1},{1,0},{2,3},{3,2},{4,5},{5,4},{6,7},{7,6},{8,9},{9,8},{10,11... | collective-permute-start | bytes 393224 | tf_op jit(solution)/shard_map/ppermute | solution.py:332
  20.9 5.9 %collective-permute-start.7 = (bf16[2,4,32,128]{3,2,1,0:T(8,128)(2,1)S(1)}, bf16[2,4,32,128]{3,2,1,0:T(8,128)(2,1)S(1)}, u32[]{:S(2)}, u32[]{:S(2)}) collective-permute-start(bf16[2,4,32,128]{3,2,1,0:T(8,128)(2,1)S(1)} %get-tuple-element.44), channel_id=1, source_target_pairs={{0,6},{2,4},{4,2},{6,0},{8,14},{10,12},{12,10},{14,8},{1,7},{3,5},... | collective-permute-start | bytes 196616 | tf_op jit(solution)/shard_map/ppermute | solution.py:348
  21.4 5.6 %collective-permute-start.8 = (bf16[2,4,32,128]{3,2,1,0:T(8,128)(2,1)S(1)}, bf16[2,4,32,128]{3,2,1,0:T(8,128)(2,1)S(1)}, u32[]{:S(2)}, u32[]{:S(2)}) collective-permute-start(bf16[2,4,32,128]{3,2,1,0:T(8,128)(2,1)S(1)} %get-tuple-element.45), channel_id=1, source_target_pairs={{0,2},{2,0},{4,6},{6,4},{8,10},{10,8},{12,14},{14,12},{1,3},{3,1},... | collective-permute-start | bytes 196616 | tf_op jit(solution)/shard_map/ppermute | solution.py:348
  22.2 4.8 %collective-permute-start.9 = (bf16[2,4,32,128]{3,2,1,0:T(8,128)(2,1)S(1)}, bf16[2,4,32,128]{3,2,1,0:T(8,128)(2,1)S(1)}, u32[]{:S(2)}, u32[]{:S(2)}) collective-permute-start(bf16[2,4,32,128]{3,2,1,0:T(8,128)(2,1)S(1)} %get-tuple-element.46), channel_id=1, source_target_pairs={{0,4},{2,6},{4,0},{6,2},{8,12},{10,14},{12,8},{14,10},{1,5},{3,7},... | collective-permute-start | bytes 196616 | tf_op jit(solution)/shard_map/ppermute | solution.py:348
  27.1 4.9 %collective-permute-start.10 = (bf16[4,32,128]{2,1,0:T(8,128)(2,1)S(1)}, bf16[4,32,128]{2,1,0:T(8,128)(2,1)S(1)}, u32[]{:S(2)}, u32[]{:S(2)}) collective-permute-start(bf16[4,32,128]{2,1,0:T(8,128)(2,1)S(1)} %get-tuple-element.48), channel_id=1, source_target_pairs={{0,8},{2,10},{4,12},{6,14},{8,0},{10,2},{12,4},{14,6},{1,9},{3,11}... | collective-permute-start | bytes 98312 | tf_op jit(solution)/shard_map/ppermute | solution.py:359

commit v9 on v8

--- a/solution.py
+++ b/solution.py
@@ -9,7 +9,6 @@
 
 JB = 4
 NW = 16
-IDROWS = 16
 PADROWS = 16
 LOADS = 4
 NEAR = 4
@@ -54,28 +53,41 @@
         ref[pl.ds(quarter * comps * nk, pad), :] = jnp.zeros((pad, nz), jnp.bfloat16)
 
 
-def weights_of(ids, table_ref):
-    weight = jnp.zeros(ids.shape, jnp.float32)
-    for entry in range(NW):
-        weight = jnp.where(ids == entry, table_ref[entry], weight)
-    return weight
-
-
-def ids_kernel(ids_ref, table_ref, zc_ref, xc_ref, _, weight_out, zc_out, xc_out):
+def weights_kernel(ids_ref, table_ref, zc_ref, xc_ref, _, weight_ref, zc_out, xc_out):
     m = lax.axis_index("modes")
     q = lax.rem(lax.axis_index("space"), 2)
     body, nz = xc_ref.shape
-    quarter = ids_ref.shape[1] // 4
-    weight_out[...] = weights_of(ids_ref[0], table_ref)
+    nx = ids_ref.shape[1]
+    quarter = nx // 4
+    table = table_ref[...]
+    weight = jnp.zeros((nx, nz), jnp.float32)
+    for entry in range(NW):
+        weight = jnp.where(ids_ref[0] == entry, table[:, entry : entry + 1], weight)
+    weight_ref[...] = weight
     for ref, out, at in ((zc_ref, zc_out, 2 * (1 - m) + q), (xc_ref, xc_out, 2 * (1 - m) + 1 - q)):
         out[pl.ds(0, body), :] = ref[...]
-        ids = [
-            jnp.broadcast_to(ids_ref[0, pl.ds(at * quarter + row, 1), :], (IDROWS // quarter, nz))
-            for row in range(quarter)
-        ]
-        out[pl.ds(body, IDROWS), :] = (
-            jnp.concatenate(ids, axis=0).astype(jnp.float32).astype(jnp.bfloat16)
+        rest = jnp.concatenate(
+            [
+                jnp.broadcast_to(weight_ref[pl.ds(at * quarter + row, 1), :], (8, nz))
+                for row in range(quarter)
+            ],
+            axis=0,
         )
+        piece_of = lax.rem(lax.broadcasted_iota(jnp.int32, rest.shape, 0), 8)
+        pieces = jnp.zeros(rest.shape, jnp.float32)
+        for piece in range(3):
+            rounded = rest.astype(jnp.bfloat16).astype(jnp.float32)
+            pieces = jnp.where(piece_of == piece, rounded, pieces)
+            rest = rest - rounded
+        out[pl.ds(body, 8 * quarter), :] = pieces.astype(jnp.bfloat16)
+
+
+def received_weights(ref, first, quarter):
+    pieces = ref[pl.ds(first, 8 * quarter), :].astype(jnp.float32)
+    return [
+        pieces[8 * r : 8 * r + 1] + pieces[8 * r + 1 : 8 * r + 2] + pieces[8 * r + 2 : 8 * r + 3]
+        for r in range(quarter)
+    ]
 
 
 def picks(jb_ref, m, nk):
@@ -141,7 +153,7 @@
 
 
 def cross_kernel(classes_of, chunk, planes, has_weighted, own_ref, other_ref, *refs):
-    zs_ref, xs_ref, zc_ref, xc_ref, w0_ref, table_ref, jb_ref, acc_ref, *refs = refs
+    zs_ref, xs_ref, zc_ref, xc_ref, w0_ref, jb_ref, acc_ref, *refs = refs
     if has_weighted:
         wts, keep_ref, send_ref, adv = refs
     else:
@@ -157,20 +169,18 @@
     pick = picks(jb_ref, m, nk)
     classes = [pl.multiple_of(chunk * cls, chunk) for cls in classes_of(plane)]
     if not has_weighted:
-        ids = pl.ds(quarter * comps * nk, IDROWS)
-        w1 = weights_of(xc_ref[ids, :].astype(jnp.float32), table_ref)
-        w2 = inside * weights_of(zc_ref[ids, :].astype(jnp.float32), table_ref)
+        w1 = received_weights(xc_ref, quarter * comps * nk, quarter)
+        w2 = [inside * weight for weight in received_weights(zc_ref, quarter * comps * nk, quarter)]
         for r in range(quarter):
             wts[:, pl.ds(r * comps * nz, comps * nz)] = w0_ref[r]
-            row = IDROWS // quarter * r
             for c in range(comps):
                 lane = (r * comps + c) * nz
                 src = pl.ds((r * comps + c) * nk, nk)
                 for half, (p1, p2) in enumerate(((xs_ref, zs_ref), (xc_ref, zc_ref))):
                     block = pl.ds(half * nk, nk)
-                    for part, (field, weight) in enumerate(((p1, w1), (p2, w2)), 1):
+                    for part, (field, weight) in enumerate(((p1, w1[r]), (p2, w2[r])), 1):
                         wts[block, pl.ds(part * span + lane, nz)] = (
-                            weight[row : row + 1] * field[src, :].astype(jnp.float32)
+                            weight * field[src, :].astype(jnp.float32)
                         ).astype(jnp.bfloat16)
     phis = []
     for r in range(quarter):
@@ -237,7 +247,8 @@
     smem = pl.BlockSpec(memory_space=pltpu.SMEM)
     params = pltpu.CompilerParams(vmem_limit_bytes=VMEM_LIMIT)
     six = nx // 2 + 2
-    body = nx // 4 * comps * nk
+    quarter = nx // 4
+    body = quarter * comps * nk
     own, to_core, zs, xs, zc, xc = pl.pallas_call(
         prep_kernel,
         out_shape=[jax.ShapeDtypeStruct((six, comps, nk, nz), bf16)] * 2
@@ -264,14 +275,14 @@
     zs = lax.ppermute(zs, both, same(z_pairs))
     xs = lax.ppermute(xs, both, same(x_pairs))
     weight, zc, xc = pl.pallas_call(
-        ids_kernel,
+        weights_kernel,
         out_shape=[jax.ShapeDtypeStruct((nx, nz), f32)]
-        + [jax.ShapeDtypeStruct((body + IDROWS, nz), bf16)] * 2,
-        in_specs=[vmem, smem, vmem, vmem, pl.BlockSpec(memory_space=pl.ANY)],
+        + [jax.ShapeDtypeStruct((body + 8 * quarter, nz), bf16)] * 2,
+        in_specs=[vmem] * 4 + [pl.BlockSpec(memory_space=pl.ANY)],
         out_specs=[vmem] * 3,
         compiler_params=params,
-        name="ids",
-    )(weight_ids, weight_table, zc, xc, other)
+        name="weights",
+    )(weight_ids, weight_table.reshape(1, NW), zc, xc, other)
     xc = lax.ppermute(xc, both, cross(x_pairs))
     zc = lax.ppermute(zc, both, cross(z_pairs))
 
@@ -281,7 +292,6 @@
         )
 
     depth = nx // 4 * comps * nz
-    quarter = nx // 4
     depth = quarter * comps * nz
     acc, w0 = pl.pallas_call(
         local_kernel,
@@ -311,7 +321,7 @@
         return pl.pallas_call(
             functools.partial(cross_kernel, classes_of, chunk, n, bool(weighted)),
             out_shape=out_shape,
-            in_specs=[vmem] * 7 + [smem, smem] + [vmem] * (1 + len(weighted)),
+            in_specs=[vmem] * 7 + [smem] + [vmem] * (1 + len(weighted)),
             out_specs=[vmem] * len(out_shape),
             scratch_shapes=[pltpu.VMEM((count, 2 * JB * chunk, 3 * depth), bf16)],
             compiler_params=params,
@@ -319,7 +329,7 @@
                 flops=900_000_000, bytes_accessed=4_000_000, transcendentals=0
             ),
             name="cross",
-        )(own, other, zs, xs, zc, xc, w0, weight_table, j_block, acc, *weighted)
+        )(own, other, zs, xs, zc, xc, w0, j_block, acc, *weighted)
 
     swap = [(0, 1), (1, 0)]
     if n == 2 * NEAR:

time: 32.8 us -> 31.7 us (0.966)
  Pallas kernels: 8.03 us -> 6.51 us
  waiting for transfers between devices: 10.1 us -> 10.6 us
    pallas_call x2, Pallas kernels: 2.79 us -> 1.74 us  [crossed(): pl.pallas_call(functools.partial(cross_kernel, classes_of, chunk, n, bool...]
    pallas_call x1, Pallas kernels: 0.58 us -> 0.11 us  [on_device(): pl.pallas_call(weights_kernel, out_shape=[jax.ShapeDtypeStruct((nx, nz),...]
    ppermute x1, waiting for transfers between devices: 0.01 us -> 0.38 us  [on_device(): zs = lax.ppermute(zs, both, same(z_pairs))]
  transfers between devices with their start and end apart: 11 -> 11, of which waited for: 7 -> 9; matrix products, arithmetic and copies ran while one was open for 0% -> 0% of each run, Pallas kernels for 14% -> 11%
where the time goes in v9:
time: 31.7 us; the launch traced here: 31.5 us
  starting transfers between devices  13.7 us (43%)
  waiting for transfers between devices  10.6 us (33%)
  Pallas kernels  6.51 us (21%)
  between operations  0.72 us (2%)
    ppermute x1, starting transfers between devices, on_device(): zs = lax.ppermute(zs, both, same(z_pairs))  4.66 us
    ppermute x3, starting transfers between devices, on_device(): lax.ppermute(part, 'space', [(s, s ^ step) for s in range(n)])  3.39 us
    ppermute x1, starting transfers between devices, on_device(): got = lax.ppermute(send, 'space', [(s, s ^ NEAR) for s in range(n)])  2.67 us
    ppermute x1, waiting for transfers between devices, on_device(): xs = lax.ppermute(xs, both, same(x_pairs))  2.52 us
    ppermute x3, waiting for transfers between devices, on_device(): lax.ppermute(part, 'space', [(s, s ^ step) for s in range(n)])  2.45 us
    pallas_call x1, Pallas kernels, on_device(): pl.pallas_call(local_kernel, out_shape=[jax.ShapeDtypeStruct((JB * 2 * nk...  2.42 us
    ppermute x1, waiting for transfers between devices, on_device(): got = lax.ppermute(send, 'space', [(s, s ^ NEAR) for s in range(n)])  2.21 us
    pallas_call x2, Pallas kernels, crossed(): pl.pallas_call(functools.partial(cross_kernel, classes_of, chunk, n, bool...  1.74 us
  transfers between devices with their start and end apart: 11, of which 9 were waited for; matrix products, arithmetic and copies ran while one was open for 0% of the time, Pallas kernels for 11%

profile of v9, /device:TPU:0, one launch (start us, length us, event | category | flops | bytes accessed | tf_op | source)
XLA Modules:
  0.0 31.5 jit_solution(8172511912657347573)
XLA Ops:
  0.0 0.0 copy-start.1
  0.0 0.0 copy-start
  0.0 1.5 %prep.1 = (bf16[6,3,128,128]{3,2,1,0:T(8,128)(2,1)S(1)}, bf16[6,3,128,128]{3,2,1,0:T(8,128)(2,1)S(1)}, bf16[784,128]{1,0:T(8,128)(2,1)S(1)}, bf16[784,128]{1,0:T...) custom-call(bf16[128,3,1,8,128]{4,3,2,1,0:T(8,128)(2,1)} %modes_hbm.1), custom_call_target="tpu_custom_call" | custom-call | flops 1500000000 | bytes 2800000 | tf_op jit(solution)/shard_map/prep/pallas_call | solution.py:252
  1.5 0.5 %collective-permute-start = (bf16[6,3,128,128]{3,2,1,0:T(8,128)(2,1)S(1)}, bf16[6,3,128,128]{3,2,1,0:T(8,128)(2,1)S(1)}, u32[]{:S(2)}, u32[]{:S(2)}) collective-permute-start(bf16[6,3,128,128]{3,2,1,0:T(8,128)(2,1)S(1)} %get-tuple-element.28), channel_id=1, source_target_pairs={{0,1},{1,0},{2,3},{3,2},{4,5},{5,4},{6,7},{7,6},{8,9},{9,8},{10,11... | collective-permute-start | bytes 1769480 | tf_op jit(solution)/shard_map/ppermute | solution.py:274
  2.0 4.7 %collective-permute-start.1 = (bf16[784,128]{1,0:T(8,128)(2,1)S(1)}, bf16[784,128]{1,0:T(8,128)(2,1)S(1)}, u32[]{:S(2)}, u32[]{:S(2)}) collective-permute-start(bf16[784,128]{1,0:T(8,128)(2,1)S(1)} %get-tuple-element.29), channel_id=1, source_target_pairs={{0,12},{1,13},{2,6},{3,7},{4,0},{5,1},{6,10},{7,11},{8,4},{9,5},{1... | collective-permute-start | bytes 602120 | tf_op jit(solution)/shard_map/ppermute | solution.py:275
  6.7 0.0 collective-permute-start.2
  6.7 0.0 collective-permute-done._.other_ref
  6.7 0.0 copy-done.1
  6.7 0.0 copy-done
  6.7 0.1 weights.1
  6.8 1.7 %collective-permute-start.3 = (bf16[784,128]{1,0:T(8,128)(2,1)S(1)}, bf16[784,128]{1,0:T(8,128)(2,1)S(1)}, u32[]{:S(2)}, u32[]{:S(2)}) collective-permute-start(bf16[784,128]{1,0:T(8,128)(2,1)S(1)} %get-tuple-element.33), channel_id=1, source_target_pairs={{0,13},{1,12},{2,7},{3,6},{4,1},{5,0},{6,11},{7,10},{8,5},{9,4},{1... | collective-permute-start | bytes 602120 | tf_op jit(solution)/shard_map/ppermute | solution.py:287
  8.5 0.0 collective-permute-start.4
  9.2 2.4 %local.1 = (f32[1024,256]{1,0:T(8,128)S(1)}, bf16[2,256,384]{2,1,0:T(8,128)(2,1)S(1)}) custom-call(bf16[6,3,128,128]{3,2,1,0:T(8,128)(2,1)S(1)} %get-tuple-element.27.own_ref, bf16[6,3,128,128]{3,2,1,0:T(8,128)(2,1)S(1)} %collective-permute-done._.other_ref, f32[8,128]{1,0:T(8,128)S(1)} %get-tuple-element.35.weight_ref, s32[1]{0:T(128)S(6)} %copy.5.jb_ref.refs_5_), custom_call_target="tpu_custom_call" | custom-call | flops 900000000 | bytes 2400000 | tf_op jit(solution)/shard_map/local/pallas_call | solution.py:296
  11.6 0.4 %collective-permute-done.1.refs_0_ = bf16[784,128]{1,0:T(8,128)(2,1)S(1)} collective-permute-done((bf16[784,128]{1,0:T(8,128)(2,1)S(1)}, bf16[784,128]{1,0:T(8,128)(2,1)S(1)}, u32[]{:S(2)}, u32[]{:S(2)}) %collective-permute-start.1) | collective-permute-done | bytes 200736 | tf_op jit(solution)/shard_map/ppermute | solution.py:275
  12.0 2.5 %collective-permute-done.2.refs_1_ = bf16[784,128]{1,0:T(8,128)(2,1)S(1)} collective-permute-done((bf16[784,128]{1,0:T(8,128)(2,1)S(1)}, bf16[784,128]{1,0:T(8,128)(2,1)S(1)}, u32[]{:S(2)}, u32[]{:S(2)}) %collective-permute-start.2) | collective-permute-done | bytes 200736 | tf_op jit(solution)/shard_map/ppermute | solution.py:276
  14.5 1.3 %collective-permute-done.3.refs_2_ = bf16[784,128]{1,0:T(8,128)(2,1)S(1)} collective-permute-done((bf16[784,128]{1,0:T(8,128)(2,1)S(1)}, bf16[784,128]{1,0:T(8,128)(2,1)S(1)}, u32[]{:S(2)}, u32[]{:S(2)}) %collective-permute-start.3) | collective-permute-done | bytes 200736 | tf_op jit(solution)/shard_map/ppermute | solution.py:287
  15.8 1.4 %collective-permute-done.4.refs_3_ = bf16[784,128]{1,0:T(8,128)(2,1)S(1)} collective-permute-done((bf16[784,128]{1,0:T(8,128)(2,1)S(1)}, bf16[784,128]{1,0:T(8,128)(2,1)S(1)}, u32[]{:S(2)}, u32[]{:S(2)}) %collective-permute-start.4) | collective-permute-done | bytes 200736 | tf_op jit(solution)/shard_map/ppermute | solution.py:286
  17.3 0.9 %cross.2 = (f32[2,2,4,32,128]{4,3,2,1,0:T(8,128)S(1)}, bf16[2,2,4,32,128]{4,3,2,1,0:T(8,128)(2,1)S(1)}, bf16[256,2304]{1,0:T(8,128)(2,1)S(1)}) custom-call(bf16[6,3,128,128]{3,2,1,0:T(8,128)(2,1)S(1)} %get-tuple-element.27.own_ref, bf16[6,3,128,128]{3,2,1,0:T(8,128)(2,1)S(1)} %collective-permute-done._.other_ref, ...), custom_call_target="tpu_custom_call" | custom-call | flops 900000000 | bytes 4000000 | tf_op jit(solution)/shard_map/cross/pallas_call | solution.py:321
  18.2 0.6 %collective-permute-start.6 = (bf16[2,2,4,32,128]{4,3,2,1,0:T(8,128)(2,1)S(1)}, bf16[2,2,4,32,128]{4,3,2,1,0:T(8,128)(2,1)S(1)}, u32[]{:S(2)}, u32[]{:S(2)}) collective-permute-start(bf16[2,2,4,32,128]{4,3,2,1,0:T(8,128)(2,1)S(1)} %get-tuple-element.43), channel_id=1, source_target_pairs={{0,1},{1,0},{2,3},{3,2},{4,5},{5,4},{6,7},{7,6},{8,9},{9,8},{10,11... | collective-permute-start | bytes 393224 | tf_op jit(solution)/shard_map/ppermute | solution.py:340
  18.8 0.8 %cross.3 = (f32[2,2,4,32,128]{4,3,2,1,0:T(8,128)S(1)}, bf16[2,2,4,32,128]{4,3,2,1,0:T(8,128)(2,1)S(1)}) custom-call(bf16[6,3,128,128]{3,2,1,0:T(8,128)(2,1)S(1)} %get-tuple-element.27.own_ref, bf16[6,3,128,128]{3,2,1,0:T(8,128)(2,1)S(1)} %collective-permute-done._.other_ref, bf16[784,128]{1,0:T(8,128)(2,1)S(1)} %collective-permute-done.1.refs_0_, ...), custom_call_target="tpu_custom_call" | custom-call | flops 900000000 | bytes 4000000 | tf_op jit(solution)/shard_map/cross/pallas_call | solution.py:321
  19.7 0.1 collective-permute-start.5
  19.7 0.1 collective-permute-done.6.got_ref
  19.8 0.5 %collective-permute-start.7 = (bf16[2,4,32,128]{3,2,1,0:T(8,128)(2,1)S(1)}, bf16[2,4,32,128]{3,2,1,0:T(8,128)(2,1)S(1)}, u32[]{:S(2)}, u32[]{:S(2)}) collective-permute-start(bf16[2,4,32,128]{3,2,1,0:T(8,128)(2,1)S(1)} %get-tuple-element.44), channel_id=1, source_target_pairs={{0,6},{2,4},{4,2},{6,0},{8,14},{10,12},{12,10},{14,8},{1,7},{3,5},... | collective-permute-start | bytes 196616 | tf_op jit(solution)/shard_map/ppermute | solution.py:358
  20.4 0.5 %collective-permute-start.8 = (bf16[2,4,32,128]{3,2,1,0:T(8,128)(2,1)S(1)}, bf16[2,4,32,128]{3,2,1,0:T(8,128)(2,1)S(1)}, u32[]{:S(2)}, u32[]{:S(2)}) collective-permute-start(bf16[2,4,32,128]{3,2,1,0:T(8,128)(2,1)S(1)} %get-tuple-element.45), channel_id=1, source_target_pairs={{0,2},{2,0},{4,6},{6,4},{8,10},{10,8},{12,14},{14,12},{1,3},{3,1},... | collective-permute-start | bytes 196616 | tf_op jit(solution)/shard_map/ppermute | solution.py:358
  20.8 0.2 collective-permute-done.5.got_ref
  21.1 2.4 %collective-permute-start.9 = (bf16[2,4,32,128]{3,2,1,0:T(8,128)(2,1)S(1)}, bf16[2,4,32,128]{3,2,1,0:T(8,128)(2,1)S(1)}, u32[]{:S(2)}, u32[]{:S(2)}) collective-permute-start(bf16[2,4,32,128]{3,2,1,0:T(8,128)(2,1)S(1)} %get-tuple-element.46), channel_id=1, source_target_pairs={{0,4},{2,6},{4,0},{6,2},{8,12},{10,14},{12,8},{14,10},{1,5},{3,7},... | collective-permute-start | bytes 196616 | tf_op jit(solution)/shard_map/ppermute | solution.py:358
  23.5 2.2 %collective-permute-done.7.refs_0_ = bf16[2,4,32,128]{3,2,1,0:T(8,128)(2,1)S(1)} collective-permute-done((bf16[2,4,32,128]{3,2,1,0:T(8,128)(2,1)S(1)}, bf16[2,4,32,128]{3,2,1,0:T(8,128)(2,1)S(1)}, u32[]{:S(2)}, u32[]{:S(2)}) %collective-permute-start.7) | collective-permute-done | bytes 65568 | tf_op jit(solution)/shard_map/ppermute | solution.py:358
  25.7 0.2 collective-permute-done.8.refs_1_
  25.9 0.0 collective-permute-done.9.refs_2_
  26.0 2.7 %collective-permute-start.10 = (bf16[4,32,128]{2,1,0:T(8,128)(2,1)S(1)}, bf16[4,32,128]{2,1,0:T(8,128)(2,1)S(1)}, u32[]{:S(2)}, u32[]{:S(2)}) collective-permute-start(bf16[4,32,128]{2,1,0:T(8,128)(2,1)S(1)} %get-tuple-element.48), channel_id=1, source_target_pairs={{0,8},{2,10},{4,12},{6,14},{8,0},{10,2},{12,4},{14,6},{1,9},{3,11}... | collective-permute-start | bytes 98312 | tf_op jit(solution)/shard_map/ppermute | solution.py:369
  28.6 2.2 %collective-permute-done.10.got_ref = bf16[4,32,128]{2,1,0:T(8,128)(2,1)S(1)} collective-permute-done((bf16[4,32,128]{2,1,0:T(8,128)(2,1)S(1)}, bf16[4,32,128]{2,1,0:T(8,128)(2,1)S(1)}, u32[]{:S(2)}, u32[]{:S(2)}) %collective-permute-start.10) | collective-permute-done | bytes 32800 | tf_op jit(solution)/shard_map/ppermute | solution.py:369
  30.9 0.7 %total.1 = f32[32,4,128]{2,1,0:T(4,128)} custom-call(f32[4,32,128]{2,1,0:T(8,128)S(1)} %get-tuple-element.47.keep_ref, bf16[4,32,128]{2,1,0:T(8,128)(2,1)S(1)} %collective-permute-done.10.got_ref), custom_call_target="tpu_custom_call" | custom-call | tf_op jit(solution)/shard_map/total/pallas_call | solution.py:370
  (3 shorter events, 0.1 us)
Async XLA Ops:
  0.0 6.7 %copy-start.1 = (f32[16]{0:T(128)S(1)}, f32[16]{0:T(128)}, u32[]{:S(2)}) copy-start(f32[16]{0:T(128)} %param.6) | copy-start | bytes 196
  0.0 6.7 %copy-start = (s32[1,8,128]{2,1,0:T(8,128)S(1)}, s32[1,8,128]{2,1,0:T(8,128)}, u32[]{:S(2)}) copy-start(s32[1,8,128]{2,1,0:T(8,128)} %ids_ref.1) | copy-start | bytes 12292
  1.5 5.2 %collective-permute-start = (bf16[6,3,128,128]{3,2,1,0:T(8,128)(2,1)S(1)}, bf16[6,3,128,128]{3,2,1,0:T(8,128)(2,1)S(1)}, u32[]{:S(2)}, u32[]{:S(2)}) collective-permute-start(bf16[6,3,128,128]{3,2,1,0:T(8,128)(2,1)S(1)} %get-tuple-element.28), channel_id=1, source_target_pairs={{0,1},{1,0},{2,3},{3,2},{4,5},{5,4},{6,7},{7,6},{8,9},{9,8},{10,11... | collective-permute-start | bytes 1769480 | tf_op jit(solution)/shard_map/ppermute | solution.py:274
  2.0 10.0 %collective-permute-start.1 = (bf16[784,128]{1,0:T(8,128)(2,1)S(1)}, bf16[784,128]{1,0:T(8,128)(2,1)S(1)}, u32[]{:S(2)}, u32[]{:S(2)}) collective-permute-start(bf16[784,128]{1,0:T(8,128)(2,1)S(1)} %get-tuple-element.29), channel_id=1, source_target_pairs={{0,12},{1,13},{2,6},{3,7},{4,0},{5,1},{6,10},{7,11},{8,4},{9,5},{1... | collective-permute-start | bytes 602120 | tf_op jit(solution)/shard_map/ppermute | solution.py:275
  6.7 7.8 %collective-permute-start.2 = (bf16[784,128]{1,0:T(8,128)(2,1)S(1)}, bf16[784,128]{1,0:T(8,128)(2,1)S(1)}, u32[]{:S(2)}, u32[]{:S(2)}) collective-permute-start(bf16[784,128]{1,0:T(8,128)(2,1)S(1)} %get-tuple-element.30), channel_id=1, source_target_pairs={{0,2},{1,3},{2,0},{3,1},{4,6},{5,7},{6,4},{7,5},{8,10},{9,11},{10,... | collective-permute-start | bytes 602120 | tf_op jit(solution)/shard_map/ppermute | solution.py:276
  6.8 9.0 %collective-permute-start.3 = (bf16[784,128]{1,0:T(8,128)(2,1)S(1)}, bf16[784,128]{1,0:T(8,128)(2,1)S(1)}, u32[]{:S(2)}, u32[]{:S(2)}) collective-permute-start(bf16[784,128]{1,0:T(8,128)(2,1)S(1)} %get-tuple-element.33), channel_id=1, source_target_pairs={{0,13},{1,12},{2,7},{3,6},{4,1},{5,0},{6,11},{7,10},{8,5},{9,4},{1... | collective-permute-start | bytes 602120 | tf_op jit(solution)/shard_map/ppermute | solution.py:287
  8.5 8.7 %collective-permute-start.4 = (bf16[784,128]{1,0:T(8,128)(2,1)S(1)}, bf16[784,128]{1,0:T(8,128)(2,1)S(1)}, u32[]{:S(2)}, u32[]{:S(2)}) collective-permute-start(bf16[784,128]{1,0:T(8,128)(2,1)S(1)} %get-tuple-element.34), channel_id=1, source_target_pairs={{0,3},{1,2},{2,1},{3,0},{4,7},{5,6},{6,5},{7,4},{8,11},{9,10},{10,... | collective-permute-start | bytes 602120 | tf_op jit(solution)/shard_map/ppermute | solution.py:286
  18.2 1.6 %collective-permute-start.6 = (bf16[2,2,4,32,128]{4,3,2,1,0:T(8,128)(2,1)S(1)}, bf16[2,2,4,32,128]{4,3,2,1,0:T(8,128)(2,1)S(1)}, u32[]{:S(2)}, u32[]{:S(2)}) collective-permute-start(bf16[2,2,4,32,128]{4,3,2,1,0:T(8,128)(2,1)S(1)} %get-tuple-element.43), channel_id=1, source_target_pairs={{0,1},{1,0},{2,3},{3,2},{4,5},{5,4},{6,7},{7,6},{8,9},{9,8},{10,11... | collective-permute-start | bytes 393224 | tf_op jit(solution)/shard_map/ppermute | solution.py:340
  19.7 1.4 %collective-permute-start.5 = (bf16[2,2,4,32,128]{4,3,2,1,0:T(8,128)(2,1)S(1)}, bf16[2,2,4,32,128]{4,3,2,1,0:T(8,128)(2,1)S(1)}, u32[]{:S(2)}, u32[]{:S(2)}) collective-permute-start(bf16[2,2,4,32,128]{4,3,2,1,0:T(8,128)(2,1)S(1)} %get-tuple-element.40), channel_id=1, source_target_pairs={{0,1},{1,0},{2,3},{3,2},{4,5},{5,4},{6,7},{7,6},{8,9},{9,8},{10,11... | collective-permute-start | bytes 393224 | tf_op jit(solution)/shard_map/ppermute | solution.py:342
  19.8 5.9 %collective-permute-start.7 = (bf16[2,4,32,128]{3,2,1,0:T(8,128)(2,1)S(1)}, bf16[2,4,32,128]{3,2,1,0:T(8,128)(2,1)S(1)}, u32[]{:S(2)}, u32[]{:S(2)}) collective-permute-start(bf16[2,4,32,128]{3,2,1,0:T(8,128)(2,1)S(1)} %get-tuple-element.44), channel_id=1, source_target_pairs={{0,6},{2,4},{4,2},{6,0},{8,14},{10,12},{12,10},{14,8},{1,7},{3,5},... | collective-permute-start | bytes 196616 | tf_op jit(solution)/shard_map/ppermute | solution.py:358
  20.4 5.6 %collective-permute-start.8 = (bf16[2,4,32,128]{3,2,1,0:T(8,128)(2,1)S(1)}, bf16[2,4,32,128]{3,2,1,0:T(8,128)(2,1)S(1)}, u32[]{:S(2)}, u32[]{:S(2)}) collective-permute-start(bf16[2,4,32,128]{3,2,1,0:T(8,128)(2,1)S(1)} %get-tuple-element.45), channel_id=1, source_target_pairs={{0,2},{2,0},{4,6},{6,4},{8,10},{10,8},{12,14},{14,12},{1,3},{3,1},... | collective-permute-start | bytes 196616 | tf_op jit(solution)/shard_map/ppermute | solution.py:358
  21.1 4.8 %collective-permute-start.9 = (bf16[2,4,32,128]{3,2,1,0:T(8,128)(2,1)S(1)}, bf16[2,4,32,128]{3,2,1,0:T(8,128)(2,1)S(1)}, u32[]{:S(2)}, u32[]{:S(2)}) collective-permute-start(bf16[2,4,32,128]{3,2,1,0:T(8,128)(2,1)S(1)} %get-tuple-element.46), channel_id=1, source_target_pairs={{0,4},{2,6},{4,0},{6,2},{8,12},{10,14},{12,8},{14,10},{1,5},{3,7},... | collective-permute-start | bytes 196616 | tf_op jit(solution)/shard_map/ppermute | solution.py:358
  26.0 4.9 %collective-permute-start.10 = (bf16[4,32,128]{2,1,0:T(8,128)(2,1)S(1)}, bf16[4,32,128]{2,1,0:T(8,128)(2,1)S(1)}, u32[]{:S(2)}, u32[]{:S(2)}) collective-permute-start(bf16[4,32,128]{2,1,0:T(8,128)(2,1)S(1)} %get-tuple-element.48), channel_id=1, source_target_pairs={{0,8},{2,10},{4,12},{6,14},{8,0},{10,2},{12,4},{14,6},{1,9},{3,11}... | collective-permute-start | bytes 98312 | tf_op jit(solution)/shard_map/ppermute | solution.py:369

commit v10 on v9

--- a/solution.py
+++ b/solution.py
@@ -10,7 +10,7 @@
 JB = 4
 NW = 16
 PADROWS = 16
-LOADS = 4
+LOADS = 8
 NEAR = 4
 VMEM_LIMIT = 48 * 1024 * 1024
 PREP_LIMIT = 53_100 * 1024
@@ -29,31 +29,32 @@
     ]
     for copy in copies:
         copy.start()
+    quarter = nx // 4
     for p in range(LOADS):
         copies[p].wait()
         block = pl.ds(p * step, step)
         for c in range(comps):
             value = modes_ref[block, c, 0].astype(jnp.float32)
             tr[:, c, block] = jnp.swapaxes(value, 0, 1).astype(jnp.bfloat16)
-    quarter = nx // 4
-    for r in range(nx // 2 + 2):
-        own_ref[r] = tr[lax.rem(nx // 2 * m + nx - 1 + r, nx)]
-        core_ref[r] = tr[lax.rem(nx // 2 * (1 - m) + nx - 1 + r, nx)]
-    for ref, at in (
-        (xs_ref, 2 * m + 1 - q),
-        (xc_ref, 2 * (1 - m) + 1 - q),
-        (zs_ref, 2 * m + q),
-        (zc_ref, 2 * (1 - m) + q),
-    ):
-        for row in range(quarter):
-            for c in range(comps):
-                ref[pl.ds((row * comps + c) * nk, nk), :] = tr[at * quarter + row, c]
+        for ref, at in (
+            (zs_ref, 2 * m + q),
+            (xs_ref, 2 * m + 1 - q),
+            (zc_ref, 2 * (1 - m) + q),
+            (xc_ref, 2 * (1 - m) + 1 - q),
+        ):
+            for row in range(quarter):
+                for c in range(comps):
+                    first = (row * comps + c) * nk + p * step
+                    ref[pl.ds(first, step), :] = tr[at * quarter + row, c, block]
+        for r in range(nx // 2 + 2):
+            core_ref[r, :, block] = tr[lax.rem(nx // 2 * (1 - m) + nx - 1 + r, nx), :, block]
+            own_ref[r, :, block] = tr[lax.rem(nx // 2 * m + nx - 1 + r, nx), :, block]
     for ref in (zs_ref, xs_ref):
         pad = ref.shape[0] - quarter * comps * nk
         ref[pl.ds(quarter * comps * nk, pad), :] = jnp.zeros((pad, nz), jnp.bfloat16)
 
 
-def weights_kernel(ids_ref, table_ref, zc_ref, xc_ref, _, weight_ref, zc_out, xc_out):
+def weights_kernel(ids_ref, table_ref, zc_ref, xc_ref, _, weight_ref, xc_out, ze_out, zo_out):
     m = lax.axis_index("modes")
     q = lax.rem(lax.axis_index("space"), 2)
     body, nz = xc_ref.shape
@@ -64,8 +65,10 @@
     for entry in range(NW):
         weight = jnp.where(ids_ref[0] == entry, table[:, entry : entry + 1], weight)
     weight_ref[...] = weight
-    for ref, out, at in ((zc_ref, zc_out, 2 * (1 - m) + q), (xc_ref, xc_out, 2 * (1 - m) + 1 - q)):
-        out[pl.ds(0, body), :] = ref[...]
+    for ref, outs, at in (
+        (xc_ref, (xc_out,), 2 * (1 - m) + 1 - q),
+        (zc_ref, (ze_out, zo_out), 2 * (1 - m) + q),
+    ):
         rest = jnp.concatenate(
             [
                 jnp.broadcast_to(weight_ref[pl.ds(at * quarter + row, 1), :], (8, nz))
@@ -79,11 +82,13 @@
             rounded = rest.astype(jnp.bfloat16).astype(jnp.float32)
             pieces = jnp.where(piece_of == piece, rounded, pieces)
             rest = rest - rounded
-        out[pl.ds(body, 8 * quarter), :] = pieces.astype(jnp.bfloat16)
-
-
-def received_weights(ref, first, quarter):
-    pieces = ref[pl.ds(first, 8 * quarter), :].astype(jnp.float32)
+        for out in outs:
+            out[pl.ds(0, body), :] = ref[...]
+            out[pl.ds(body, 8 * quarter), :] = pieces.astype(jnp.bfloat16)
+
+
+def received_weights(sent, quarter):
+    pieces = sent.astype(jnp.float32)
     return [
         pieces[8 * r : 8 * r + 1] + pieces[8 * r + 1 : 8 * r + 2] + pieces[8 * r + 2 : 8 * r + 3]
         for r in range(quarter)
@@ -100,9 +105,8 @@
 
 def picked(pick, own, other):
     mine, block, within = pick
-    rows = jnp.where(
-        mine, own[pl.ds(block, 16), :].astype(jnp.float32), other[pl.ds(block, 16), :].astype(jnp.float32)
-    )
+    rows = pl.ds(block, 16)
+    rows = jnp.where(mine, own(rows).astype(jnp.float32), other(rows).astype(jnp.float32))
     result = rows[0:JB]
     for start in range(JB, 16, JB):
         result = jnp.where(within == start, rows[start : start + JB], result)
@@ -129,7 +133,7 @@
     rows -= 2
     pick = picks(jb_ref, m, nk)
     for r in range(rows):
-        phi = [picked(pick, own_ref.at[r + 1, d], other_ref.at[r + 1, d]) for d in range(comps)]
+        phi = [picked(pick, lambda at: own_ref[r + 1, d, at, :], lambda at: other_ref[r + 1, d, at, :]) for d in range(comps)]
         weight = weight_ref[pl.ds(rows * m + r, 1), :]
         for c in range(comps):
             for half, ref in enumerate((own_ref, other_ref)):
@@ -153,7 +157,7 @@
 
 
 def cross_kernel(classes_of, chunk, planes, has_weighted, own_ref, other_ref, *refs):
-    zs_ref, xs_ref, zc_ref, xc_ref, w0_ref, jb_ref, acc_ref, *refs = refs
+    xs_ref, zs_ref, xc_ref, ze_ref, zo_ref, w0_ref, jb_ref, acc_ref, *refs = refs
     if has_weighted:
         wts, keep_ref, send_ref, adv = refs
     else:
@@ -163,32 +167,46 @@
     q = lax.rem(plane, 2)
     sigma = jnp.where(q == 0, 0.5, -0.5)
     inside = jnp.where(jnp.logical_or(plane == 1, plane == planes - 2), 0.0, 1.0)
+    by_even = lax.rem(lax.div(plane, 2), 2) == q
+
+    def zc_rows(rows):
+        return jnp.where(by_even, ze_ref[rows, :], zo_ref[rows, :])
+
     rows, comps, nk, nz = own_ref.shape
     quarter = (rows - 2) // 2
     span = quarter * comps * nz
     pick = picks(jb_ref, m, nk)
     classes = [pl.multiple_of(chunk * cls, chunk) for cls in classes_of(plane)]
     if not has_weighted:
-        w1 = received_weights(xc_ref, quarter * comps * nk, quarter)
-        w2 = [inside * weight for weight in received_weights(zc_ref, quarter * comps * nk, quarter)]
+        sent = pl.ds(quarter * comps * nk, 8 * quarter)
+        w1 = received_weights(xc_ref[sent, :], quarter)
+        w2 = [inside * weight for weight in received_weights(zc_rows(sent), quarter)]
         for r in range(quarter):
             wts[:, pl.ds(r * comps * nz, comps * nz)] = w0_ref[r]
             for c in range(comps):
                 lane = (r * comps + c) * nz
                 src = pl.ds((r * comps + c) * nk, nk)
-                for half, (p1, p2) in enumerate(((xs_ref, zs_ref), (xc_ref, zc_ref))):
+                for half, (f1, f2) in enumerate(
+                    ((xs_ref[src, :], zs_ref[src, :]), (xc_ref[src, :], zc_rows(src)))
+                ):
                     block = pl.ds(half * nk, nk)
-                    for part, (field, weight) in enumerate(((p1, w1[r]), (p2, w2[r])), 1):
+                    for part, (field, weight) in enumerate(((f1, w1[r]), (f2, w2[r])), 1):
                         wts[block, pl.ds(part * span + lane, nz)] = (
-                            weight * field[src, :].astype(jnp.float32)
+                            weight * field.astype(jnp.float32)
                         ).astype(jnp.bfloat16)
     phis = []
     for r in range(quarter):
         row0 = 1 + quarter * q + r
-        along = pl.ds((r * comps + 1) * nk, nk)
-        phi0 = sigma * picked(pick, own_ref.at[row0, 1], other_ref.at[row0, 1])
-        phi1 = sigma * picked(pick, xs_ref.at[along], xc_ref.at[along])
-        phi2 = -sigma * picked(pick, zs_ref.at[along], zc_ref.at[along])
+        along = (r * comps + 1) * nk
+
+        def moved(at):
+            return pl.ds(pl.multiple_of(along + at.start, 16), at.size)
+
+        phi0 = sigma * picked(
+            pick, lambda at: own_ref[row0, 1, at, :], lambda at: other_ref[row0, 1, at, :]
+        )
+        phi1 = sigma * picked(pick, lambda at: xs_ref[moved(at), :], lambda at: xc_ref[moved(at), :])
+        phi2 = -sigma * picked(pick, lambda at: zs_ref[moved(at), :], lambda at: zc_rows(moved(at)))
         phis.append([[spread(phi[j : j + 1]) for j in range(JB)] for phi in (phi0, phi1, phi2)])
     inside = inside.astype(jnp.bfloat16)
     for at, cls in enumerate(classes):
@@ -198,12 +216,11 @@
             for c in range(comps):
                 lane = (r * comps + c) * nz
                 src = (r * comps + c) * nk
-                for half, (p0, p1, p2) in enumerate(
-                    ((own_ref, xs_ref, zs_ref), (other_ref, xc_ref, zc_ref))
-                ):
+                rows_at = pl.ds(pl.multiple_of(src + cls, 16), chunk)
+                for half, (p0, p1) in enumerate(((own_ref, xs_ref), (other_ref, xc_ref))):
                     f0 = p0[row0, c, pl.ds(cls, chunk), :]
-                    f1 = p1[pl.ds(src + cls, chunk), :]
-                    gy = inside * p2[pl.ds(src + cls, chunk), :] - f0
+                    f1 = p1[rows_at, :]
+                    gy = inside * (zc_rows(rows_at) if half else zs_ref[rows_at, :]) - f0
                     for j in range(JB):
                         here = pl.ds((half * JB + j) * chunk, chunk)
                         adv[at, here, pl.ds(lane, nz)] = scaled(phi0[j], f1)
@@ -238,6 +255,14 @@
     total = keep_ref[...] + got_ref[...].astype(jnp.float32)
     for j in range(JB):
         out_ref[:, j, :] = total[j]
+
+
+def level_swaps(n, odd):
+    pairs = []
+    for s in range(n):
+        to = s // 2 + (1 if s // 2 % 2 == odd else -1)
+        pairs.append((s, 2 * to + s % 2 if 0 <= to < n // 2 else s))
+    return pairs
 
 
 def on_device(n, modes, weight_ids, weight_table, j_block):
@@ -274,24 +299,25 @@
     other = lax.ppermute(to_core, "modes", [(0, 1), (1, 0)])
     zs = lax.ppermute(zs, both, same(z_pairs))
     xs = lax.ppermute(xs, both, same(x_pairs))
-    weight, zc, xc = pl.pallas_call(
+    weight, xc, *zc = pl.pallas_call(
         weights_kernel,
         out_shape=[jax.ShapeDtypeStruct((nx, nz), f32)]
-        + [jax.ShapeDtypeStruct((body + 8 * quarter, nz), bf16)] * 2,
+        + [jax.ShapeDtypeStruct((body + 8 * quarter, nz), bf16)] * 3,
         in_specs=[vmem] * 4 + [pl.BlockSpec(memory_space=pl.ANY)],
-        out_specs=[vmem] * 3,
+        out_specs=[vmem] * 4,
         compiler_params=params,
         name="weights",
     )(weight_ids, weight_table.reshape(1, NW), zc, xc, other)
     xc = lax.ppermute(xc, both, cross(x_pairs))
-    zc = lax.ppermute(zc, both, cross(z_pairs))
-
-    def estimate(depth, size):
-        return pl.CostEstimate(
-            flops=2 * JB * (2 * nk) ** 2 * depth, bytes_accessed=size, transcendentals=0
+    zc = [
+        lax.ppermute(
+            zc[odd],
+            both,
+            [(2 * a + m, 2 * b + (m if a == b else 1 - m)) for a, b in level_swaps(n, odd) for m in range(2)],
         )
-
-    depth = nx // 4 * comps * nz
+        for odd in range(2)
+    ]
+
     depth = quarter * comps * nz
     acc, w0 = pl.pallas_call(
         local_kernel,
@@ -321,7 +347,7 @@
         return pl.pallas_call(
             functools.partial(cross_kernel, classes_of, chunk, n, bool(weighted)),
             out_shape=out_shape,
-            in_specs=[vmem] * 7 + [smem] + [vmem] * (1 + len(weighted)),
+            in_specs=[vmem] * 8 + [smem] + [vmem] * (1 + len(weighted)),
             out_specs=[vmem] * len(out_shape),
             scratch_shapes=[pltpu.VMEM((count, 2 * JB * chunk, 3 * depth), bf16)],
             compiler_params=params,
@@ -329,7 +355,7 @@
                 flops=900_000_000, bytes_accessed=4_000_000, transcendentals=0
             ),
             name="cross",
-        )(own, other, zs, xs, zc, xc, w0, j_block, acc, *weighted)
+        )(own, other, xs, zs, xc, *zc, w0, j_block, acc, *weighted)
 
     swap = [(0, 1), (1, 0)]
     if n == 2 * NEAR:

time: 31.7 us -> 33.5 us (1.057)
  starting transfers between devices: 13.7 us -> 15.2 us
    ppermute x1, starting transfers between devices: 0.01 us -> 2.55 us  [on_device(): xs = lax.ppermute(xs, both, same(x_pairs))]
    ppermute x1, waiting for transfers between devices: 2.52 us -> 0.01 us  [on_device(): xs = lax.ppermute(xs, both, same(x_pairs))]
    ppermute x3, waiting for transfers between devices: 2.45 us -> 3.63 us  [on_device(): lax.ppermute(part, 'space', [(s, s ^ step) for s in range(n)])]
    ppermute x1, starting transfers between devices: 4.66 us -> 3.6 us  [on_device(): zs = lax.ppermute(zs, both, same(z_pairs))]
    ppermute x3, starting transfers between devices: 3.39 us -> 4.39 us  [on_device(): lax.ppermute(part, 'space', [(s, s ^ step) for s in range(n)])]
    ppermute x1 -> x2, starting transfers between devices: 1.71 us -> 0.74 us  [on_device(): lax.ppermute(zc[odd], both, [(2 * a + m, 2 * b + (m if a == b else 1 - m)...]
    ppermute x1, waiting for transfers between devices: 0.38 us -> 1.31 us  [on_device(): zs = lax.ppermute(zs, both, same(z_pairs))]
    ppermute x1, waiting for transfers between devices: 1.42 us -> 2.06 us  [on_device(): xc = lax.ppermute(xc, both, cross(x_pairs))]
  transfers between devices with their start and end apart: 11 -> 12, of which waited for: 9 -> 7; matrix products, arithmetic and copies ran while one was open for 0% -> 0% of each run, Pallas kernels for 11% -> 10%
where the time goes in v10:
time: 33.5 us; the launch traced here: 33.3 us
  starting transfers between devices  15.2 us (45%)
  waiting for transfers between devices  10.6 us (32%)
  Pallas kernels  6.68 us (20%)
  between operations  0.75 us (2%)
    ppermute x3, starting transfers between devices, on_device(): lax.ppermute(part, 'space', [(s, s ^ step) for s in range(n)])  4.39 us
    ppermute x3, waiting for transfers between devices, on_device(): lax.ppermute(part, 'space', [(s, s ^ step) for s in range(n)])  3.63 us
    ppermute x1, starting transfers between devices, on_device(): zs = lax.ppermute(zs, both, same(z_pairs))  3.6 us
    ppermute x1, starting transfers between devices, on_device(): got = lax.ppermute(send, 'space', [(s, s ^ NEAR) for s in range(n)])  2.7 us
    ppermute x1, starting transfers between devices, on_device(): xs = lax.ppermute(xs, both, same(x_pairs))  2.55 us
    pallas_call x1, Pallas kernels, on_device(): pl.pallas_call(local_kernel, out_shape=[jax.ShapeDtypeStruct((JB * 2 * nk...  2.42 us
    ppermute x1, waiting for transfers between devices, on_device(): got = lax.ppermute(send, 'space', [(s, s ^ NEAR) for s in range(n)])  2.18 us
    ppermute x1, waiting for transfers between devices, on_device(): xc = lax.ppermute(xc, both, cross(x_pairs))  2.06 us
  transfers between devices with their start and end apart: 12, of which 7 were waited for; matrix products, arithmetic and copies ran while one was open for 0% of the time, Pallas kernels for 10%

profile of v10, /device:TPU:0, one launch (start us, length us, event | category | flops | bytes accessed | tf_op | source)
XLA Modules:
  0.0 33.3 jit_solution(17005927938695254616)
XLA Ops:
  0.0 0.0 copy-start.1
  0.0 0.0 copy-start
  0.0 1.6 %prep.1 = (bf16[6,3,128,128]{3,2,1,0:T(8,128)(2,1)S(1)}, bf16[6,3,128,128]{3,2,1,0:T(8,128)(2,1)S(1)}, bf16[784,128]{1,0:T(8,128)(2,1)S(1)}, bf16[784,128]{1,0:T...) custom-call(bf16[128,3,1,8,128]{4,3,2,1,0:T(8,128)(2,1)} %modes_hbm.1), custom_call_target="tpu_custom_call" | custom-call | flops 1500000000 | bytes 2800000 | tf_op jit(solution)/shard_map/prep/pallas_call | solution.py:277
  1.7 0.5 %collective-permute-start = (bf16[6,3,128,128]{3,2,1,0:T(8,128)(2,1)S(1)}, bf16[6,3,128,128]{3,2,1,0:T(8,128)(2,1)S(1)}, u32[]{:S(2)}, u32[]{:S(2)}) collective-permute-start(bf16[6,3,128,128]{3,2,1,0:T(8,128)(2,1)S(1)} %get-tuple-element.29), channel_id=1, source_target_pairs={{0,1},{1,0},{2,3},{3,2},{4,5},{5,4},{6,7},{7,6},{8,9},{9,8},{10,11... | collective-permute-start | bytes 1769480 | tf_op jit(solution)/shard_map/ppermute | solution.py:299
  2.2 2.6 %collective-permute-start.1 = (bf16[784,128]{1,0:T(8,128)(2,1)S(1)}, bf16[784,128]{1,0:T(8,128)(2,1)S(1)}, u32[]{:S(2)}, u32[]{:S(2)}) collective-permute-start(bf16[784,128]{1,0:T(8,128)(2,1)S(1)} %get-tuple-element.30), channel_id=1, source_target_pairs={{0,2},{1,3},{2,0},{3,1},{4,6},{5,7},{6,4},{7,5},{8,10},{9,11},{10,... | collective-permute-start | bytes 602120 | tf_op jit(solution)/shard_map/ppermute | solution.py:301
  4.7 3.6 %collective-permute-start.2 = (bf16[784,128]{1,0:T(8,128)(2,1)S(1)}, bf16[784,128]{1,0:T(8,128)(2,1)S(1)}, u32[]{:S(2)}, u32[]{:S(2)}) collective-permute-start(bf16[784,128]{1,0:T(8,128)(2,1)S(1)} %get-tuple-element.31), channel_id=1, source_target_pairs={{0,12},{1,13},{2,6},{3,7},{4,0},{5,1},{6,10},{7,11},{8,4},{9,5},{1... | collective-permute-start | bytes 602120 | tf_op jit(solution)/shard_map/ppermute | solution.py:300
  8.3 0.0 collective-permute-done._.other_ref
  8.3 0.0 copy-done.1
  8.3 0.0 copy-done
  8.4 0.1 weights.1
  8.5 0.1 collective-permute-start.3
  8.5 0.1 collective-permute-start.4
  8.6 0.7 %collective-permute-start.5 = (bf16[784,128]{1,0:T(8,128)(2,1)S(1)}, bf16[784,128]{1,0:T(8,128)(2,1)S(1)}, u32[]{:S(2)}, u32[]{:S(2)}) collective-permute-start(bf16[784,128]{1,0:T(8,128)(2,1)S(1)} %get-tuple-element.36), channel_id=1, source_target_pairs={{0,0},{1,1},{2,2},{3,3},{4,9},{5,8},{6,11},{7,10},{8,5},{9,4},{10,... | collective-permute-start | bytes 602120 | tf_op jit(solution)/shard_map/ppermute | solution.py:313
  10.0 2.4 %local.1 = (f32[1024,256]{1,0:T(8,128)S(1)}, bf16[2,256,384]{2,1,0:T(8,128)(2,1)S(1)}) custom-call(bf16[6,3,128,128]{3,2,1,0:T(8,128)(2,1)S(1)} %get-tuple-element.28.own_ref, bf16[6,3,128,128]{3,2,1,0:T(8,128)(2,1)S(1)} %collective-permute-done._.other_ref, f32[8,128]{1,0:T(8,128)S(1)} %get-tuple-element.37.weight_ref, s32[1]{0:T(128)S(6)} %copy.5.jb_ref.refs_6_), custom_call_target="tpu_custom_call" | custom-call | flops 900000000 | bytes 2400000 | tf_op jit(solution)/shard_map/local/pallas_call | solution.py:322
  12.4 0.0 collective-permute-done.1.refs_0_
  12.4 1.3 %collective-permute-done.2.refs_1_ = bf16[784,128]{1,0:T(8,128)(2,1)S(1)} collective-permute-done((bf16[784,128]{1,0:T(8,128)(2,1)S(1)}, bf16[784,128]{1,0:T(8,128)(2,1)S(1)}, u32[]{:S(2)}, u32[]{:S(2)}) %collective-permute-start.2) | collective-permute-done | bytes 200736 | tf_op jit(solution)/shard_map/ppermute | solution.py:300
  13.7 2.1 %collective-permute-done.3.refs_2_ = bf16[784,128]{1,0:T(8,128)(2,1)S(1)} collective-permute-done((bf16[784,128]{1,0:T(8,128)(2,1)S(1)}, bf16[784,128]{1,0:T(8,128)(2,1)S(1)}, u32[]{:S(2)}, u32[]{:S(2)}) %collective-permute-start.3) | collective-permute-done | bytes 200736 | tf_op jit(solution)/shard_map/ppermute | solution.py:311
  15.8 1.5 %collective-permute-done.4.refs_3_ = bf16[784,128]{1,0:T(8,128)(2,1)S(1)} collective-permute-done((bf16[784,128]{1,0:T(8,128)(2,1)S(1)}, bf16[784,128]{1,0:T(8,128)(2,1)S(1)}, u32[]{:S(2)}, u32[]{:S(2)}) %collective-permute-start.4) | collective-permute-done | bytes 200736 | tf_op jit(solution)/shard_map/ppermute | solution.py:313
  17.2 0.0 collective-permute-done.5.refs_4_
  17.2 0.9 %cross.2 = (f32[2,2,4,32,128]{4,3,2,1,0:T(8,128)S(1)}, bf16[2,2,4,32,128]{4,3,2,1,0:T(8,128)(2,1)S(1)}, bf16[256,2304]{1,0:T(8,128)(2,1)S(1)}) custom-call(bf16[6,3,128,128]{3,2,1,0:T(8,128)(2,1)S(1)} %get-tuple-element.28.own_ref, bf16[6,3,128,128]{3,2,1,0:T(8,128)(2,1)S(1)} %collective-permute-done._.other_ref, ...), custom_call_target="tpu_custom_call" | custom-call | flops 900000000 | bytes 4000000 | tf_op jit(solution)/shard_map/cross/pallas_call | solution.py:347
  18.1 0.1 collective-permute-start.7
  18.2 0.9 %cross.3 = (f32[2,2,4,32,128]{4,3,2,1,0:T(8,128)S(1)}, bf16[2,2,4,32,128]{4,3,2,1,0:T(8,128)(2,1)S(1)}) custom-call(bf16[6,3,128,128]{3,2,1,0:T(8,128)(2,1)S(1)} %get-tuple-element.28.own_ref, bf16[6,3,128,128]{3,2,1,0:T(8,128)(2,1)S(1)} %collective-permute-done._.other_ref, bf16[784,128]{1,0:T(8,128)(2,1)S(1)} %collective-permute-done.1.refs_0_, ...), custom_call_target="tpu_custom_call" | custom-call | flops 900000000 | bytes 4000000 | tf_op jit(solution)/shard_map/cross/pallas_call | solution.py:347
  19.1 0.6 %collective-permute-start.6 = (bf16[2,2,4,32,128]{4,3,2,1,0:T(8,128)(2,1)S(1)}, bf16[2,2,4,32,128]{4,3,2,1,0:T(8,128)(2,1)S(1)}, u32[]{:S(2)}, u32[]{:S(2)}) collective-permute-start(bf16[2,2,4,32,128]{4,3,2,1,0:T(8,128)(2,1)S(1)} %get-tuple-element.42), channel_id=1, source_target_pairs={{0,1},{1,0},{2,3},{3,2},{4,5},{5,4},{6,7},{7,6},{8,9},{9,8},{10,11... | collective-permute-start | bytes 393224 | tf_op jit(solution)/shard_map/ppermute | solution.py:368
  19.6 0.0 collective-permute-done.7.got_ref
  19.7 3.7 %collective-permute-start.8 = (bf16[2,4,32,128]{3,2,1,0:T(8,128)(2,1)S(1)}, bf16[2,4,32,128]{3,2,1,0:T(8,128)(2,1)S(1)}, u32[]{:S(2)}, u32[]{:S(2)}) collective-permute-start(bf16[2,4,32,128]{3,2,1,0:T(8,128)(2,1)S(1)} %get-tuple-element.46), channel_id=1, source_target_pairs={{0,6},{2,4},{4,2},{6,0},{8,14},{10,12},{12,10},{14,8},{1,7},{3,5},... | collective-permute-start | bytes 196616 | tf_op jit(solution)/shard_map/ppermute | solution.py:384
  23.3 0.0 collective-permute-start.9
  23.3 0.0 collective-permute-done.6.got_ref
  23.4 0.7 %collective-permute-start.10 = (bf16[2,4,32,128]{3,2,1,0:T(8,128)(2,1)S(1)}, bf16[2,4,32,128]{3,2,1,0:T(8,128)(2,1)S(1)}, u32[]{:S(2)}, u32[]{:S(2)}) collective-permute-start(bf16[2,4,32,128]{3,2,1,0:T(8,128)(2,1)S(1)} %get-tuple-element.48), channel_id=1, source_target_pairs={{0,4},{2,6},{4,0},{6,2},{8,12},{10,14},{12,8},{14,10},{1,5},{3,7},... | collective-permute-start | bytes 196616 | tf_op jit(solution)/shard_map/ppermute | solution.py:384
  24.1 1.6 %collective-permute-done.8.refs_0_ = bf16[2,4,32,128]{3,2,1,0:T(8,128)(2,1)S(1)} collective-permute-done((bf16[2,4,32,128]{3,2,1,0:T(8,128)(2,1)S(1)}, bf16[2,4,32,128]{3,2,1,0:T(8,128)(2,1)S(1)}, u32[]{:S(2)}, u32[]{:S(2)}) %collective-permute-start.8) | collective-permute-done | bytes 65568 | tf_op jit(solution)/shard_map/ppermute | solution.py:384
  25.7 1.9 %collective-permute-done.9.refs_1_ = bf16[2,4,32,128]{3,2,1,0:T(8,128)(2,1)S(1)} collective-permute-done((bf16[2,4,32,128]{3,2,1,0:T(8,128)(2,1)S(1)}, bf16[2,4,32,128]{3,2,1,0:T(8,128)(2,1)S(1)}, u32[]{:S(2)}, u32[]{:S(2)}) %collective-permute-start.9) | collective-permute-done | bytes 65568 | tf_op jit(solution)/shard_map/ppermute | solution.py:384
  27.6 0.1 collective-permute-done.10.refs_2_
  27.7 2.7 %collective-permute-start.11 = (bf16[4,32,128]{2,1,0:T(8,128)(2,1)S(1)}, bf16[4,32,128]{2,1,0:T(8,128)(2,1)S(1)}, u32[]{:S(2)}, u32[]{:S(2)}) collective-permute-start(bf16[4,32,128]{2,1,0:T(8,128)(2,1)S(1)} %get-tuple-element.50), channel_id=1, source_target_pairs={{0,8},{2,10},{4,12},{6,14},{8,0},{10,2},{12,4},{14,6},{1,9},{3,11}... | collective-permute-start | bytes 98312 | tf_op jit(solution)/shard_map/ppermute | solution.py:395
  30.4 2.2 %collective-permute-done.11.got_ref = bf16[4,32,128]{2,1,0:T(8,128)(2,1)S(1)} collective-permute-done((bf16[4,32,128]{2,1,0:T(8,128)(2,1)S(1)}, bf16[4,32,128]{2,1,0:T(8,128)(2,1)S(1)}, u32[]{:S(2)}, u32[]{:S(2)}) %collective-permute-start.11) | collective-permute-done | bytes 32800 | tf_op jit(solution)/shard_map/ppermute | solution.py:395
  32.6 0.7 %total.1 = f32[32,4,128]{2,1,0:T(4,128)} custom-call(f32[4,32,128]{2,1,0:T(8,128)S(1)} %get-tuple-element.49.keep_ref, bf16[4,32,128]{2,1,0:T(8,128)(2,1)S(1)} %collective-permute-done.11.got_ref), custom_call_target="tpu_custom_call" | custom-call | tf_op jit(solution)/shard_map/total/pallas_call | solution.py:396
  (3 shorter events, 0.1 us)
Async XLA Ops:
  0.0 8.3 %copy-start.1 = (f32[16]{0:T(128)S(1)}, f32[16]{0:T(128)}, u32[]{:S(2)}) copy-start(f32[16]{0:T(128)} %param.6) | copy-start | bytes 196
  0.0 8.3 %copy-start = (s32[1,8,128]{2,1,0:T(8,128)S(1)}, s32[1,8,128]{2,1,0:T(8,128)}, u32[]{:S(2)}) copy-start(s32[1,8,128]{2,1,0:T(8,128)} %ids_ref.1) | copy-start | bytes 12292
  1.7 6.7 %collective-permute-start = (bf16[6,3,128,128]{3,2,1,0:T(8,128)(2,1)S(1)}, bf16[6,3,128,128]{3,2,1,0:T(8,128)(2,1)S(1)}, u32[]{:S(2)}, u32[]{:S(2)}) collective-permute-start(bf16[6,3,128,128]{3,2,1,0:T(8,128)(2,1)S(1)} %get-tuple-element.29), channel_id=1, source_target_pairs={{0,1},{1,0},{2,3},{3,2},{4,5},{5,4},{6,7},{7,6},{8,9},{9,8},{10,11... | collective-permute-start | bytes 1769480 | tf_op jit(solution)/shard_map/ppermute | solution.py:299
  2.2 10.2 %collective-permute-start.1 = (bf16[784,128]{1,0:T(8,128)(2,1)S(1)}, bf16[784,128]{1,0:T(8,128)(2,1)S(1)}, u32[]{:S(2)}, u32[]{:S(2)}) collective-permute-start(bf16[784,128]{1,0:T(8,128)(2,1)S(1)} %get-tuple-element.30), channel_id=1, source_target_pairs={{0,2},{1,3},{2,0},{3,1},{4,6},{5,7},{6,4},{7,5},{8,10},{9,11},{10,... | collective-permute-start | bytes 602120 | tf_op jit(solution)/shard_map/ppermute | solution.py:301
  4.7 9.0 %collective-permute-start.2 = (bf16[784,128]{1,0:T(8,128)(2,1)S(1)}, bf16[784,128]{1,0:T(8,128)(2,1)S(1)}, u32[]{:S(2)}, u32[]{:S(2)}) collective-permute-start(bf16[784,128]{1,0:T(8,128)(2,1)S(1)} %get-tuple-element.31), channel_id=1, source_target_pairs={{0,12},{1,13},{2,6},{3,7},{4,0},{5,1},{6,10},{7,11},{8,4},{9,5},{1... | collective-permute-start | bytes 602120 | tf_op jit(solution)/shard_map/ppermute | solution.py:300
  8.5 7.3 %collective-permute-start.3 = (bf16[784,128]{1,0:T(8,128)(2,1)S(1)}, bf16[784,128]{1,0:T(8,128)(2,1)S(1)}, u32[]{:S(2)}, u32[]{:S(2)}) collective-permute-start(bf16[784,128]{1,0:T(8,128)(2,1)S(1)} %get-tuple-element.34), channel_id=1, source_target_pairs={{0,3},{1,2},{2,1},{3,0},{4,7},{5,6},{6,5},{7,4},{8,11},{9,10},{10,... | collective-permute-start | bytes 602120 | tf_op jit(solution)/shard_map/ppermute | solution.py:311
  8.5 8.7 %collective-permute-start.4 = (bf16[784,128]{1,0:T(8,128)(2,1)S(1)}, bf16[784,128]{1,0:T(8,128)(2,1)S(1)}, u32[]{:S(2)}, u32[]{:S(2)}) collective-permute-start(bf16[784,128]{1,0:T(8,128)(2,1)S(1)} %get-tuple-element.35), channel_id=1, source_target_pairs={{0,5},{1,4},{2,7},{3,6},{4,1},{5,0},{6,3},{7,2},{8,13},{9,12},{10,... | collective-permute-start | bytes 602120 | tf_op jit(solution)/shard_map/ppermute | solution.py:313
  8.6 8.6 %collective-permute-start.5 = (bf16[784,128]{1,0:T(8,128)(2,1)S(1)}, bf16[784,128]{1,0:T(8,128)(2,1)S(1)}, u32[]{:S(2)}, u32[]{:S(2)}) collective-permute-start(bf16[784,128]{1,0:T(8,128)(2,1)S(1)} %get-tuple-element.36), channel_id=1, source_target_pairs={{0,0},{1,1},{2,2},{3,3},{4,9},{5,8},{6,11},{7,10},{8,5},{9,4},{10,... | collective-permute-start | bytes 602120 | tf_op jit(solution)/shard_map/ppermute | solution.py:313
  18.1 1.5 %collective-permute-start.7 = (bf16[2,2,4,32,128]{4,3,2,1,0:T(8,128)(2,1)S(1)}, bf16[2,2,4,32,128]{4,3,2,1,0:T(8,128)(2,1)S(1)}, u32[]{:S(2)}, u32[]{:S(2)}) collective-permute-start(bf16[2,2,4,32,128]{4,3,2,1,0:T(8,128)(2,1)S(1)} %get-tuple-element.45), channel_id=1, source_target_pairs={{0,1},{1,0},{2,3},{3,2},{4,5},{5,4},{6,7},{7,6},{8,9},{9,8},{10,11... | collective-permute-start | bytes 393224 | tf_op jit(solution)/shard_map/ppermute | solution.py:366
  19.1 4.3 %collective-permute-start.6 = (bf16[2,2,4,32,128]{4,3,2,1,0:T(8,128)(2,1)S(1)}, bf16[2,2,4,32,128]{4,3,2,1,0:T(8,128)(2,1)S(1)}, u32[]{:S(2)}, u32[]{:S(2)}) collective-permute-start(bf16[2,2,4,32,128]{4,3,2,1,0:T(8,128)(2,1)S(1)} %get-tuple-element.42), channel_id=1, source_target_pairs={{0,1},{1,0},{2,3},{3,2},{4,5},{5,4},{6,7},{7,6},{8,9},{9,8},{10,11... | collective-permute-start | bytes 393224 | tf_op jit(solution)/shard_map/ppermute | solution.py:368
  19.7 6.0 %collective-permute-start.8 = (bf16[2,4,32,128]{3,2,1,0:T(8,128)(2,1)S(1)}, bf16[2,4,32,128]{3,2,1,0:T(8,128)(2,1)S(1)}, u32[]{:S(2)}, u32[]{:S(2)}) collective-permute-start(bf16[2,4,32,128]{3,2,1,0:T(8,128)(2,1)S(1)} %get-tuple-element.46), channel_id=1, source_target_pairs={{0,6},{2,4},{4,2},{6,0},{8,14},{10,12},{12,10},{14,8},{1,7},{3,5},... | collective-permute-start | bytes 196616 | tf_op jit(solution)/shard_map/ppermute | solution.py:384
  23.3 4.3 %collective-permute-start.9 = (bf16[2,4,32,128]{3,2,1,0:T(8,128)(2,1)S(1)}, bf16[2,4,32,128]{3,2,1,0:T(8,128)(2,1)S(1)}, u32[]{:S(2)}, u32[]{:S(2)}) collective-permute-start(bf16[2,4,32,128]{3,2,1,0:T(8,128)(2,1)S(1)} %get-tuple-element.47), channel_id=1, source_target_pairs={{0,2},{2,0},{4,6},{6,4},{8,10},{10,8},{12,14},{14,12},{1,3},{3,1},... | collective-permute-start | bytes 196616 | tf_op jit(solution)/shard_map/ppermute | solution.py:384
  23.4 4.3 %collective-permute-start.10 = (bf16[2,4,32,128]{3,2,1,0:T(8,128)(2,1)S(1)}, bf16[2,4,32,128]{3,2,1,0:T(8,128)(2,1)S(1)}, u32[]{:S(2)}, u32[]{:S(2)}) collective-permute-start(bf16[2,4,32,128]{3,2,1,0:T(8,128)(2,1)S(1)} %get-tuple-element.48), channel_id=1, source_target_pairs={{0,4},{2,6},{4,0},{6,2},{8,12},{10,14},{12,8},{14,10},{1,5},{3,7},... | collective-permute-start | bytes 196616 | tf_op jit(solution)/shard_map/ppermute | solution.py:384
  27.7 4.9 %collective-permute-start.11 = (bf16[4,32,128]{2,1,0:T(8,128)(2,1)S(1)}, bf16[4,32,128]{2,1,0:T(8,128)(2,1)S(1)}, u32[]{:S(2)}, u32[]{:S(2)}) collective-permute-start(bf16[4,32,128]{2,1,0:T(8,128)(2,1)S(1)} %get-tuple-element.50), channel_id=1, source_target_pairs={{0,8},{2,10},{4,12},{6,14},{8,0},{10,2},{12,4},{14,6},{1,9},{3,11}... | collective-permute-start | bytes 98312 | tf_op jit(solution)/shard_map/ppermute | solution.py:395

commit v11 on v9

--- a/solution.py
+++ b/solution.py
@@ -11,14 +11,26 @@
 NW = 16
 PADROWS = 16
 LOADS = 4
+X_FIRST = 0b10011111
 NEAR = 4
 VMEM_LIMIT = 48 * 1024 * 1024
 PREP_LIMIT = 53_100 * 1024
 
 
-def prep_kernel(modes_hbm, own_ref, core_ref, zs_ref, xs_ref, zc_ref, xc_ref, modes_ref, tr, sems):
+def x_first(s, planes):
+    if planes != 8:
+        return s >= 0
+    return lax.rem(lax.shift_right_logical(X_FIRST, s), 2) == 1
+
+
+def prep_kernel(
+    planes, modes_hbm, own_ref, core_ref, first_ref, second_ref, xc_ref, zc_ref, modes_ref, tr, sems
+):
     m = lax.axis_index("modes")
-    q = lax.rem(lax.axis_index("space"), 2)
+    s = lax.axis_index("space")
+    q = lax.rem(s, 2)
+    to_x, to_z = 2 * m + 1 - q, 2 * m + q
+    x_now = x_first(s, planes)
     nk, comps, _, nx, nz = modes_hbm.shape
     step = nk // LOADS
     copies = [
@@ -40,20 +52,20 @@
         own_ref[r] = tr[lax.rem(nx // 2 * m + nx - 1 + r, nx)]
         core_ref[r] = tr[lax.rem(nx // 2 * (1 - m) + nx - 1 + r, nx)]
     for ref, at in (
-        (xs_ref, 2 * m + 1 - q),
+        (first_ref, jnp.where(x_now, to_x, to_z)),
+        (second_ref, jnp.where(x_now, to_z, to_x)),
         (xc_ref, 2 * (1 - m) + 1 - q),
-        (zs_ref, 2 * m + q),
         (zc_ref, 2 * (1 - m) + q),
     ):
         for row in range(quarter):
             for c in range(comps):
                 ref[pl.ds((row * comps + c) * nk, nk), :] = tr[at * quarter + row, c]
-    for ref in (zs_ref, xs_ref):
+    for ref in (first_ref, second_ref):
         pad = ref.shape[0] - quarter * comps * nk
         ref[pl.ds(quarter * comps * nk, pad), :] = jnp.zeros((pad, nz), jnp.bfloat16)
 
 
-def weights_kernel(ids_ref, table_ref, zc_ref, xc_ref, _, weight_ref, zc_out, xc_out):
+def weights_kernel(ids_ref, table_ref, xc_ref, zc_ref, _, weight_ref, xc_out, zc_out):
     m = lax.axis_index("modes")
     q = lax.rem(lax.axis_index("space"), 2)
     body, nz = xc_ref.shape
@@ -100,9 +112,8 @@
 
 def picked(pick, own, other):
     mine, block, within = pick
-    rows = jnp.where(
-        mine, own[pl.ds(block, 16), :].astype(jnp.float32), other[pl.ds(block, 16), :].astype(jnp.float32)
-    )
+    rows = pl.ds(block, 16)
+    rows = jnp.where(mine, own(rows).astype(jnp.float32), other(rows).astype(jnp.float32))
     result = rows[0:JB]
     for start in range(JB, 16, JB):
         result = jnp.where(within == start, rows[start : start + JB], result)
@@ -129,7 +140,7 @@
     rows -= 2
     pick = picks(jb_ref, m, nk)
     for r in range(rows):
-        phi = [picked(pick, own_ref.at[r + 1, d], other_ref.at[r + 1, d]) for d in range(comps)]
+        phi = [picked(pick, lambda at: own_ref[r + 1, d, at, :], lambda at: other_ref[r + 1, d, at, :]) for d in range(comps)]
         weight = weight_ref[pl.ds(rows * m + r, 1), :]
         for c in range(comps):
             for half, ref in enumerate((own_ref, other_ref)):
@@ -153,7 +164,7 @@
 
 
 def cross_kernel(classes_of, chunk, planes, has_weighted, own_ref, other_ref, *refs):
-    zs_ref, xs_ref, zc_ref, xc_ref, w0_ref, jb_ref, acc_ref, *refs = refs
+    first_ref, second_ref, xc_ref, zc_ref, w0_ref, jb_ref, acc_ref, *refs = refs
     if has_weighted:
         wts, keep_ref, send_ref, adv = refs
     else:
@@ -163,6 +174,14 @@
     q = lax.rem(plane, 2)
     sigma = jnp.where(q == 0, 0.5, -0.5)
     inside = jnp.where(jnp.logical_or(plane == 1, plane == planes - 2), 0.0, 1.0)
+    x_came = x_first(jnp.bitwise_xor(plane, 1), planes)
+
+    def xs_rows(rows):
+        return jnp.where(x_came, first_ref[rows, :], second_ref[rows, :])
+
+    def zs_rows(rows):
+        return jnp.where(x_came, second_ref[rows, :], first_ref[rows, :])
+
     rows, comps, nk, nz = own_ref.shape
     quarter = (rows - 2) // 2
     span = quarter * comps * nz
@@ -176,19 +195,27 @@
             for c in range(comps):
                 lane = (r * comps + c) * nz
                 src = pl.ds((r * comps + c) * nk, nk)
-                for half, (p1, p2) in enumerate(((xs_ref, zs_ref), (xc_ref, zc_ref))):
+                for half, (f1, f2) in enumerate(
+                    ((xs_rows(src), zs_rows(src)), (xc_ref[src, :], zc_ref[src, :]))
+                ):
                     block = pl.ds(half * nk, nk)
-                    for part, (field, weight) in enumerate(((p1, w1[r]), (p2, w2[r])), 1):
+                    for part, (field, weight) in enumerate(((f1, w1[r]), (f2, w2[r])), 1):
                         wts[block, pl.ds(part * span + lane, nz)] = (
-                            weight * field[src, :].astype(jnp.float32)
+                            weight * field.astype(jnp.float32)
                         ).astype(jnp.bfloat16)
     phis = []
     for r in range(quarter):
         row0 = 1 + quarter * q + r
-        along = pl.ds((r * comps + 1) * nk, nk)
-        phi0 = sigma * picked(pick, own_ref.at[row0, 1], other_ref.at[row0, 1])
-        phi1 = sigma * picked(pick, xs_ref.at[along], xc_ref.at[along])
-        phi2 = -sigma * picked(pick, zs_ref.at[along], zc_ref.at[along])
+        along = (r * comps + 1) * nk
+
+        def moved(at):
+            return pl.ds(pl.multiple_of(along + at.start, 16), at.size)
+
+        phi0 = sigma * picked(
+            pick, lambda at: own_ref[row0, 1, at, :], lambda at: other_ref[row0, 1, at, :]
+        )
+        phi1 = sigma * picked(pick, lambda at: xs_rows(moved(at)), lambda at: xc_ref[moved(at), :])
+        phi2 = -sigma * picked(pick, lambda at: zs_rows(moved(at)), lambda at: zc_ref[moved(at), :])
         phis.append([[spread(phi[j : j + 1]) for j in range(JB)] for phi in (phi0, phi1, phi2)])
     inside = inside.astype(jnp.bfloat16)
     for at, cls in enumerate(classes):
@@ -198,12 +225,15 @@
             for c in range(comps):
                 lane = (r * comps + c) * nz
                 src = (r * comps + c) * nk
-                for half, (p0, p1, p2) in enumerate(
-                    ((own_ref, xs_ref, zs_ref), (other_ref, xc_ref, zc_ref))
+                rows_at = pl.ds(pl.multiple_of(src + cls, 16), chunk)
+                for half, (p0, f1, f2) in enumerate(
+                    (
+                        (own_ref, xs_rows(rows_at), zs_rows(rows_at)),
+                        (other_ref, xc_ref[rows_at, :], zc_ref[rows_at, :]),
+                    )
                 ):
                     f0 = p0[row0, c, pl.ds(cls, chunk), :]
-                    f1 = p1[pl.ds(src + cls, chunk), :]
-                    gy = inside * p2[pl.ds(src + cls, chunk), :] - f0
+                    gy = inside * f2 - f0
                     for j in range(JB):
                         here = pl.ds((half * JB + j) * chunk, chunk)
                         adv[at, here, pl.ds(lane, nz)] = scaled(phi0[j], f1)
@@ -249,8 +279,8 @@
     six = nx // 2 + 2
     quarter = nx // 4
     body = quarter * comps * nk
-    own, to_core, zs, xs, zc, xc = pl.pallas_call(
-        prep_kernel,
+    own, to_core, first, second, xc, zc = pl.pallas_call(
+        functools.partial(prep_kernel, n),
         out_shape=[jax.ShapeDtypeStruct((six, comps, nk, nz), bf16)] * 2
         + [jax.ShapeDtypeStruct((body + PADROWS, nz), bf16)] * 2
         + [jax.ShapeDtypeStruct((body, nz), bf16)] * 2,
@@ -267,14 +297,17 @@
     )(modes)
 
     both = ("space", "modes")
-    x_pairs = [(s, s ^ 1) for s in range(n)]
-    z_pairs = [(s, (s + (2 if s % 2 else -2)) % n) for s in range(n)]
+    x_to = lambda s: s ^ 1
+    z_to = lambda s: s + 2 if s % 2 else s - 2
+    x_now = [n != 8 or X_FIRST >> s & 1 for s in range(n)]
+    firsts = [(s, x_to(s) if x_now[s] else z_to(s)) for s in range(n)]
+    seconds = [(s, z_to(s) % n if x_now[s] else x_to(s)) for s in range(n)]
     same = lambda pairs: [(2 * a + m, 2 * b + m) for a, b in pairs for m in range(2)]
     cross = lambda pairs: [(2 * a + m, 2 * b + 1 - m) for a, b in pairs for m in range(2)]
     other = lax.ppermute(to_core, "modes", [(0, 1), (1, 0)])
-    zs = lax.ppermute(zs, both, same(z_pairs))
-    xs = lax.ppermute(xs, both, same(x_pairs))
-    weight, zc, xc = pl.pallas_call(
+    first = lax.ppermute(first, both, same(firsts))
+    second = lax.ppermute(second, both, same(seconds))
+    weight, xc, zc = pl.pallas_call(
         weights_kernel,
         out_shape=[jax.ShapeDtypeStruct((nx, nz), f32)]
         + [jax.ShapeDtypeStruct((body + 8 * quarter, nz), bf16)] * 2,
@@ -282,16 +315,10 @@
         out_specs=[vmem] * 3,
         compiler_params=params,
         name="weights",
-    )(weight_ids, weight_table.reshape(1, NW), zc, xc, other)
-    xc = lax.ppermute(xc, both, cross(x_pairs))
-    zc = lax.ppermute(zc, both, cross(z_pairs))
-
-    def estimate(depth, size):
-        return pl.CostEstimate(
-            flops=2 * JB * (2 * nk) ** 2 * depth, bytes_accessed=size, transcendentals=0
-        )
-
-    depth = nx // 4 * comps * nz
+    )(weight_ids, weight_table.reshape(1, NW), xc, zc, other)
+    xc = lax.ppermute(xc, both, cross([(s, x_to(s)) for s in range(n)]))
+    zc = lax.ppermute(zc, both, cross([(s, z_to(s)) for s in range(n) if 0 <= z_to(s) < n]))
+
     depth = quarter * comps * nz
     acc, w0 = pl.pallas_call(
         local_kernel,
@@ -329,7 +356,7 @@
                 flops=900_000_000, bytes_accessed=4_000_000, transcendentals=0
             ),
             name="cross",
-        )(own, other, zs, xs, zc, xc, w0, j_block, acc, *weighted)
+        )(own, other, first, second, xc, zc, w0, j_block, acc, *weighted)
 
     swap = [(0, 1), (1, 0)]
     if n == 2 * NEAR:

time: 31.7 us -> 31.6 us (level)
  starting transfers between devices: 13.7 us -> 12.7 us
  waiting for transfers between devices: 10.6 us -> 11.5 us
    ppermute x1, waiting for transfers between devices: 2.21 us -> 3.42 us  [on_device(): got = lax.ppermute(send, 'space', [(s, s ^ NEAR) for s in range(n)])]
    ppermute x1, starting transfers between devices: 2.67 us -> 1.46 us  [on_device(): got = lax.ppermute(send, 'space', [(s, s ^ NEAR) for s in range(n)])]
    ppermute x4, waiting for transfers between devices: 5.66 us -> 4.87 us  [the longest x1 2.83 us: on_device(): xc = lax.ppermute(xc, both, cross([(s, x_to(s)) for s in range(n)]))]
    ppermute x3, waiting for transfers between devices: 2.45 us -> 3.19 us  [on_device(): lax.ppermute(part, 'space', [(s, s ^ step) for s in range(n)])]
    ppermute x1, starting transfers between devices: 0.64 us -> 0.18 us  [on_device(): got_a = lax.ppermute(send_a, 'modes', swap)]
    ppermute x1, starting transfers between devices: 0.08 us -> 0.47 us  [on_device(): got_b = lax.ppermute(send_b, 'modes', swap)]
  transfers between devices with their start and end apart: 11 -> 11, of which waited for: 9 -> 6; matrix products, arithmetic and copies ran while one was open for 0% -> 0% of each run, Pallas kernels for 11% -> 11%
where the time goes in v11:
time: 31.6 us; the launch traced here: 31.5 us
  starting transfers between devices  12.7 us (40%)
  waiting for transfers between devices  11.5 us (36%)
  Pallas kernels  6.51 us (21%)
  between operations  0.74 us (2%)
    ppermute x3, starting transfers between devices, on_device(): lax.ppermute(part, 'space', [(s, s ^ step) for s in range(n)])  3.62 us
    ppermute x1, waiting for transfers between devices, on_device(): got = lax.ppermute(send, 'space', [(s, s ^ NEAR) for s in range(n)])  3.42 us
    ppermute x3, waiting for transfers between devices, on_device(): lax.ppermute(part, 'space', [(s, s ^ step) for s in range(n)])  3.19 us
    ppermute x1, waiting for transfers between devices, on_device(): xc = lax.ppermute(xc, both, cross([(s, x_to(s)) for s in range(n)]))  2.83 us
    ppermute x1, starting transfers between devices, on_device(): second = lax.ppermute(second, both, same(seconds))  2.6 us
    ppermute x1, starting transfers between devices, on_device(): first = lax.ppermute(first, both, same(firsts))  2.54 us
    pallas_call x1, Pallas kernels, on_device(): pl.pallas_call(local_kernel, out_shape=[jax.ShapeDtypeStruct((JB * 2 * nk...  2.41 us
    ppermute x1, waiting for transfers between devices, on_device(): lax.ppermute(zc, both, cross([(s, z_to(s)) for s in range(n) if 0 <= z_to...  2.04 us
  transfers between devices with their start and end apart: 11, of which 6 were waited for; matrix products, arithmetic and copies ran while one was open for 0% of the time, Pallas kernels for 11%

profile of v11, /device:TPU:0, one launch (start us, length us, event | category | flops | bytes accessed | tf_op | source)
XLA Modules:
  0.0 31.5 jit_solution(7486874284286871233)
XLA Ops:
  0.0 0.0 copy-start.1
  0.0 0.0 copy-start
  0.0 1.5 %prep.1 = (bf16[6,3,128,128]{3,2,1,0:T(8,128)(2,1)S(1)}, bf16[6,3,128,128]{3,2,1,0:T(8,128)(2,1)S(1)}, bf16[784,128]{1,0:T(8,128)(2,1)S(1)}, bf16[784,128]{1,0:T...) custom-call(bf16[128,3,1,8,128]{4,3,2,1,0:T(8,128)(2,1)} %modes_hbm.1), custom_call_target="tpu_custom_call" | custom-call | flops 1500000000 | bytes 2800000 | tf_op jit(solution)/shard_map/prep/pallas_call | solution.py:282
  1.5 0.5 %collective-permute-start = (bf16[6,3,128,128]{3,2,1,0:T(8,128)(2,1)S(1)}, bf16[6,3,128,128]{3,2,1,0:T(8,128)(2,1)S(1)}, u32[]{:S(2)}, u32[]{:S(2)}) collective-permute-start(bf16[6,3,128,128]{3,2,1,0:T(8,128)(2,1)S(1)} %get-tuple-element.28), channel_id=1, source_target_pairs={{0,1},{1,0},{2,3},{3,2},{4,5},{5,4},{6,7},{7,6},{8,9},{9,8},{10,11... | collective-permute-start | bytes 1769480 | tf_op jit(solution)/shard_map/ppermute | solution.py:307
  2.0 2.5 %collective-permute-start.1 = (bf16[784,128]{1,0:T(8,128)(2,1)S(1)}, bf16[784,128]{1,0:T(8,128)(2,1)S(1)}, u32[]{:S(2)}, u32[]{:S(2)}) collective-permute-start(bf16[784,128]{1,0:T(8,128)(2,1)S(1)} %get-tuple-element.29), channel_id=1, source_target_pairs={{0,2},{1,3},{2,0},{3,1},{4,6},{5,7},{6,4},{7,5},{8,10},{9,11},{10,... | collective-permute-start | bytes 602120 | tf_op jit(solution)/shard_map/ppermute | solution.py:308
  4.5 2.6 %collective-permute-start.2 = (bf16[784,128]{1,0:T(8,128)(2,1)S(1)}, bf16[784,128]{1,0:T(8,128)(2,1)S(1)}, u32[]{:S(2)}, u32[]{:S(2)}) collective-permute-start(bf16[784,128]{1,0:T(8,128)(2,1)S(1)} %get-tuple-element.30), channel_id=1, source_target_pairs={{0,12},{1,13},{2,6},{3,7},{4,0},{5,1},{6,10},{7,11},{8,4},{9,5},{1... | collective-permute-start | bytes 602120 | tf_op jit(solution)/shard_map/ppermute | solution.py:309
  7.1 0.0 collective-permute-done._.other_ref
  7.1 0.0 copy-done.1
  7.2 0.0 copy-done
  7.2 0.1 weights.1
  7.3 0.1 collective-permute-start.3
  7.3 1.3 %collective-permute-start.4 = (bf16[784,128]{1,0:T(8,128)(2,1)S(1)}, bf16[784,128]{1,0:T(8,128)(2,1)S(1)}, u32[]{:S(2)}, u32[]{:S(2)}) collective-permute-start(bf16[784,128]{1,0:T(8,128)(2,1)S(1)} %get-tuple-element.34), channel_id=1, source_target_pairs={{2,7},{3,6},{4,1},{5,0},{6,11},{7,10},{8,5},{9,4},{10,15},{11,14},... | collective-permute-start | bytes 602120 | tf_op jit(solution)/shard_map/ppermute | solution.py:320
  9.3 2.4 %local.1 = (f32[1024,256]{1,0:T(8,128)S(1)}, bf16[2,256,384]{2,1,0:T(8,128)(2,1)S(1)}) custom-call(bf16[6,3,128,128]{3,2,1,0:T(8,128)(2,1)S(1)} %get-tuple-element.27.own_ref, bf16[6,3,128,128]{3,2,1,0:T(8,128)(2,1)S(1)} %collective-permute-done._.other_ref, f32[8,128]{1,0:T(8,128)S(1)} %get-tuple-element.35.weight_ref, s32[1]{0:T(128)S(6)} %copy.5.jb_ref.refs_5_), custom_call_target="tpu_custom_call" | custom-call | flops 900000000 | bytes 2400000 | tf_op jit(solution)/shard_map/local/pallas_call | solution.py:323
  11.7 0.0 collective-permute-done.1.refs_0_
  11.7 0.0 collective-permute-done.2.refs_1_
  11.7 2.8 %collective-permute-done.3.refs_2_ = bf16[784,128]{1,0:T(8,128)(2,1)S(1)} collective-permute-done((bf16[784,128]{1,0:T(8,128)(2,1)S(1)}, bf16[784,128]{1,0:T(8,128)(2,1)S(1)}, u32[]{:S(2)}, u32[]{:S(2)}) %collective-permute-start.3) | collective-permute-done | bytes 200736 | tf_op jit(solution)/shard_map/ppermute | solution.py:319
  14.6 2.0 %collective-permute-done.4.refs_3_ = bf16[784,128]{1,0:T(8,128)(2,1)S(1)} collective-permute-done((bf16[784,128]{1,0:T(8,128)(2,1)S(1)}, bf16[784,128]{1,0:T(8,128)(2,1)S(1)}, u32[]{:S(2)}, u32[]{:S(2)}) %collective-permute-start.4) | collective-permute-done | bytes 200736 | tf_op jit(solution)/shard_map/ppermute | solution.py:320
  16.6 0.9 %cross.2 = (f32[2,2,4,32,128]{4,3,2,1,0:T(8,128)S(1)}, bf16[2,2,4,32,128]{4,3,2,1,0:T(8,128)(2,1)S(1)}, bf16[256,2304]{1,0:T(8,128)(2,1)S(1)}) custom-call(bf16[6,3,128,128]{3,2,1,0:T(8,128)(2,1)S(1)} %get-tuple-element.27.own_ref, bf16[6,3,128,128]{3,2,1,0:T(8,128)(2,1)S(1)} %collective-permute-done._.other_ref, ...), custom_call_target="tpu_custom_call" | custom-call | flops 900000000 | bytes 4000000 | tf_op jit(solution)/shard_map/cross/pallas_call | solution.py:348
  17.5 0.2 collective-permute-start.6
  17.7 0.8 %cross.3 = (f32[2,2,4,32,128]{4,3,2,1,0:T(8,128)S(1)}, bf16[2,2,4,32,128]{4,3,2,1,0:T(8,128)(2,1)S(1)}) custom-call(bf16[6,3,128,128]{3,2,1,0:T(8,128)(2,1)S(1)} %get-tuple-element.27.own_ref, bf16[6,3,128,128]{3,2,1,0:T(8,128)(2,1)S(1)} %collective-permute-done._.other_ref, bf16[784,128]{1,0:T(8,128)(2,1)S(1)} %collective-permute-done.1.refs_0_, ...), custom_call_target="tpu_custom_call" | custom-call | flops 900000000 | bytes 4000000 | tf_op jit(solution)/shard_map/cross/pallas_call | solution.py:348
  18.5 0.5 %collective-permute-start.5 = (bf16[2,2,4,32,128]{4,3,2,1,0:T(8,128)(2,1)S(1)}, bf16[2,2,4,32,128]{4,3,2,1,0:T(8,128)(2,1)S(1)}, u32[]{:S(2)}, u32[]{:S(2)}) collective-permute-start(bf16[2,2,4,32,128]{4,3,2,1,0:T(8,128)(2,1)S(1)} %get-tuple-element.40), channel_id=1, source_target_pairs={{0,1},{1,0},{2,3},{3,2},{4,5},{5,4},{6,7},{7,6},{8,9},{9,8},{10,11... | collective-permute-start | bytes 393224 | tf_op jit(solution)/shard_map/ppermute | solution.py:369
  19.0 0.0 collective-permute-done.6.got_ref
  19.0 1.5 %collective-permute-start.7 = (bf16[2,4,32,128]{3,2,1,0:T(8,128)(2,1)S(1)}, bf16[2,4,32,128]{3,2,1,0:T(8,128)(2,1)S(1)}, u32[]{:S(2)}, u32[]{:S(2)}) collective-permute-start(bf16[2,4,32,128]{3,2,1,0:T(8,128)(2,1)S(1)} %get-tuple-element.44), channel_id=1, source_target_pairs={{0,6},{2,4},{4,2},{6,0},{8,14},{10,12},{12,10},{14,8},{1,7},{3,5},... | collective-permute-start | bytes 196616 | tf_op jit(solution)/shard_map/ppermute | solution.py:385
  20.6 0.9 %collective-permute-start.8 = (bf16[2,4,32,128]{3,2,1,0:T(8,128)(2,1)S(1)}, bf16[2,4,32,128]{3,2,1,0:T(8,128)(2,1)S(1)}, u32[]{:S(2)}, u32[]{:S(2)}) collective-permute-start(bf16[2,4,32,128]{3,2,1,0:T(8,128)(2,1)S(1)} %get-tuple-element.45), channel_id=1, source_target_pairs={{0,2},{2,0},{4,6},{6,4},{8,10},{10,8},{12,14},{14,12},{1,3},{3,1},... | collective-permute-start | bytes 196616 | tf_op jit(solution)/shard_map/ppermute | solution.py:385
  21.5 0.0 collective-permute-done.5.got_ref
  21.6 1.1 %collective-permute-start.9 = (bf16[2,4,32,128]{3,2,1,0:T(8,128)(2,1)S(1)}, bf16[2,4,32,128]{3,2,1,0:T(8,128)(2,1)S(1)}, u32[]{:S(2)}, u32[]{:S(2)}) collective-permute-start(bf16[2,4,32,128]{3,2,1,0:T(8,128)(2,1)S(1)} %get-tuple-element.46), channel_id=1, source_target_pairs={{0,4},{2,6},{4,0},{6,2},{8,12},{10,14},{12,8},{14,10},{1,5},{3,7},... | collective-permute-start | bytes 196616 | tf_op jit(solution)/shard_map/ppermute | solution.py:385
  22.7 1.6 %collective-permute-done.7.refs_0_ = bf16[2,4,32,128]{3,2,1,0:T(8,128)(2,1)S(1)} collective-permute-done((bf16[2,4,32,128]{3,2,1,0:T(8,128)(2,1)S(1)}, bf16[2,4,32,128]{3,2,1,0:T(8,128)(2,1)S(1)}, u32[]{:S(2)}, u32[]{:S(2)}) %collective-permute-start.7) | collective-permute-done | bytes 65568 | tf_op jit(solution)/shard_map/ppermute | solution.py:385
  24.3 1.2 %collective-permute-done.8.refs_1_ = bf16[2,4,32,128]{3,2,1,0:T(8,128)(2,1)S(1)} collective-permute-done((bf16[2,4,32,128]{3,2,1,0:T(8,128)(2,1)S(1)}, bf16[2,4,32,128]{3,2,1,0:T(8,128)(2,1)S(1)}, u32[]{:S(2)}, u32[]{:S(2)}) %collective-permute-start.8) | collective-permute-done | bytes 65568 | tf_op jit(solution)/shard_map/ppermute | solution.py:385
  25.5 0.4 %collective-permute-done.9.refs_2_ = bf16[2,4,32,128]{3,2,1,0:T(8,128)(2,1)S(1)} collective-permute-done((bf16[2,4,32,128]{3,2,1,0:T(8,128)(2,1)S(1)}, bf16[2,4,32,128]{3,2,1,0:T(8,128)(2,1)S(1)}, u32[]{:S(2)}, u32[]{:S(2)}) %collective-permute-start.9) | collective-permute-done | bytes 65568 | tf_op jit(solution)/shard_map/ppermute | solution.py:385
  25.9 1.5 %collective-permute-start.10 = (bf16[4,32,128]{2,1,0:T(8,128)(2,1)S(1)}, bf16[4,32,128]{2,1,0:T(8,128)(2,1)S(1)}, u32[]{:S(2)}, u32[]{:S(2)}) collective-permute-start(bf16[4,32,128]{2,1,0:T(8,128)(2,1)S(1)} %get-tuple-element.48), channel_id=1, source_target_pairs={{0,8},{2,10},{4,12},{6,14},{8,0},{10,2},{12,4},{14,6},{1,9},{3,11}... | collective-permute-start | bytes 98312 | tf_op jit(solution)/shard_map/ppermute | solution.py:396
  27.4 3.4 %collective-permute-done.10.got_ref = bf16[4,32,128]{2,1,0:T(8,128)(2,1)S(1)} collective-permute-done((bf16[4,32,128]{2,1,0:T(8,128)(2,1)S(1)}, bf16[4,32,128]{2,1,0:T(8,128)(2,1)S(1)}, u32[]{:S(2)}, u32[]{:S(2)}) %collective-permute-start.10) | collective-permute-done | bytes 32800 | tf_op jit(solution)/shard_map/ppermute | solution.py:396
  30.8 0.7 %total.1 = f32[32,4,128]{2,1,0:T(4,128)} custom-call(f32[4,32,128]{2,1,0:T(8,128)S(1)} %get-tuple-element.47.keep_ref, bf16[4,32,128]{2,1,0:T(8,128)(2,1)S(1)} %collective-permute-done.10.got_ref), custom_call_target="tpu_custom_call" | custom-call | tf_op jit(solution)/shard_map/total/pallas_call | solution.py:397
  (3 shorter events, 0.1 us)
Async XLA Ops:
  0.0 7.1 %copy-start.1 = (f32[16]{0:T(128)S(1)}, f32[16]{0:T(128)}, u32[]{:S(2)}) copy-start(f32[16]{0:T(128)} %param.6) | copy-start | bytes 196
  0.0 7.2 %copy-start = (s32[1,8,128]{2,1,0:T(8,128)S(1)}, s32[1,8,128]{2,1,0:T(8,128)}, u32[]{:S(2)}) copy-start(s32[1,8,128]{2,1,0:T(8,128)} %ids_ref.1) | copy-start | bytes 12292
  1.5 5.7 %collective-permute-start = (bf16[6,3,128,128]{3,2,1,0:T(8,128)(2,1)S(1)}, bf16[6,3,128,128]{3,2,1,0:T(8,128)(2,1)S(1)}, u32[]{:S(2)}, u32[]{:S(2)}) collective-permute-start(bf16[6,3,128,128]{3,2,1,0:T(8,128)(2,1)S(1)} %get-tuple-element.28), channel_id=1, source_target_pairs={{0,1},{1,0},{2,3},{3,2},{4,5},{5,4},{6,7},{7,6},{8,9},{9,8},{10,11... | collective-permute-start | bytes 1769480 | tf_op jit(solution)/shard_map/ppermute | solution.py:307
  2.0 9.7 %collective-permute-start.1 = (bf16[784,128]{1,0:T(8,128)(2,1)S(1)}, bf16[784,128]{1,0:T(8,128)(2,1)S(1)}, u32[]{:S(2)}, u32[]{:S(2)}) collective-permute-start(bf16[784,128]{1,0:T(8,128)(2,1)S(1)} %get-tuple-element.29), channel_id=1, source_target_pairs={{0,2},{1,3},{2,0},{3,1},{4,6},{5,7},{6,4},{7,5},{8,10},{9,11},{10,... | collective-permute-start | bytes 602120 | tf_op jit(solution)/shard_map/ppermute | solution.py:308
  4.5 7.2 %collective-permute-start.2 = (bf16[784,128]{1,0:T(8,128)(2,1)S(1)}, bf16[784,128]{1,0:T(8,128)(2,1)S(1)}, u32[]{:S(2)}, u32[]{:S(2)}) collective-permute-start(bf16[784,128]{1,0:T(8,128)(2,1)S(1)} %get-tuple-element.30), channel_id=1, source_target_pairs={{0,12},{1,13},{2,6},{3,7},{4,0},{5,1},{6,10},{7,11},{8,4},{9,5},{1... | collective-permute-start | bytes 602120 | tf_op jit(solution)/shard_map/ppermute | solution.py:309
  7.3 7.3 %collective-permute-start.3 = (bf16[784,128]{1,0:T(8,128)(2,1)S(1)}, bf16[784,128]{1,0:T(8,128)(2,1)S(1)}, u32[]{:S(2)}, u32[]{:S(2)}) collective-permute-start(bf16[784,128]{1,0:T(8,128)(2,1)S(1)} %get-tuple-element.33), channel_id=1, source_target_pairs={{0,3},{1,2},{2,1},{3,0},{4,7},{5,6},{6,5},{7,4},{8,11},{9,10},{10,... | collective-permute-start | bytes 602120 | tf_op jit(solution)/shard_map/ppermute | solution.py:319
  7.3 9.3 %collective-permute-start.4 = (bf16[784,128]{1,0:T(8,128)(2,1)S(1)}, bf16[784,128]{1,0:T(8,128)(2,1)S(1)}, u32[]{:S(2)}, u32[]{:S(2)}) collective-permute-start(bf16[784,128]{1,0:T(8,128)(2,1)S(1)} %get-tuple-element.34), channel_id=1, source_target_pairs={{2,7},{3,6},{4,1},{5,0},{6,11},{7,10},{8,5},{9,4},{10,15},{11,14},... | collective-permute-start | bytes 602120 | tf_op jit(solution)/shard_map/ppermute | solution.py:320
  17.5 1.5 %collective-permute-start.6 = (bf16[2,2,4,32,128]{4,3,2,1,0:T(8,128)(2,1)S(1)}, bf16[2,2,4,32,128]{4,3,2,1,0:T(8,128)(2,1)S(1)}, u32[]{:S(2)}, u32[]{:S(2)}) collective-permute-start(bf16[2,2,4,32,128]{4,3,2,1,0:T(8,128)(2,1)S(1)} %get-tuple-element.43), channel_id=1, source_target_pairs={{0,1},{1,0},{2,3},{3,2},{4,5},{5,4},{6,7},{7,6},{8,9},{9,8},{10,11... | collective-permute-start | bytes 393224 | tf_op jit(solution)/shard_map/ppermute | solution.py:367
  18.5 3.0 %collective-permute-start.5 = (bf16[2,2,4,32,128]{4,3,2,1,0:T(8,128)(2,1)S(1)}, bf16[2,2,4,32,128]{4,3,2,1,0:T(8,128)(2,1)S(1)}, u32[]{:S(2)}, u32[]{:S(2)}) collective-permute-start(bf16[2,2,4,32,128]{4,3,2,1,0:T(8,128)(2,1)S(1)} %get-tuple-element.40), channel_id=1, source_target_pairs={{0,1},{1,0},{2,3},{3,2},{4,5},{5,4},{6,7},{7,6},{8,9},{9,8},{10,11... | collective-permute-start | bytes 393224 | tf_op jit(solution)/shard_map/ppermute | solution.py:369
  19.0 5.3 %collective-permute-start.7 = (bf16[2,4,32,128]{3,2,1,0:T(8,128)(2,1)S(1)}, bf16[2,4,32,128]{3,2,1,0:T(8,128)(2,1)S(1)}, u32[]{:S(2)}, u32[]{:S(2)}) collective-permute-start(bf16[2,4,32,128]{3,2,1,0:T(8,128)(2,1)S(1)} %get-tuple-element.44), channel_id=1, source_target_pairs={{0,6},{2,4},{4,2},{6,0},{8,14},{10,12},{12,10},{14,8},{1,7},{3,5},... | collective-permute-start | bytes 196616 | tf_op jit(solution)/shard_map/ppermute | solution.py:385
  20.6 4.9 %collective-permute-start.8 = (bf16[2,4,32,128]{3,2,1,0:T(8,128)(2,1)S(1)}, bf16[2,4,32,128]{3,2,1,0:T(8,128)(2,1)S(1)}, u32[]{:S(2)}, u32[]{:S(2)}) collective-permute-start(bf16[2,4,32,128]{3,2,1,0:T(8,128)(2,1)S(1)} %get-tuple-element.45), channel_id=1, source_target_pairs={{0,2},{2,0},{4,6},{6,4},{8,10},{10,8},{12,14},{14,12},{1,3},{3,1},... | collective-permute-start | bytes 196616 | tf_op jit(solution)/shard_map/ppermute | solution.py:385
  21.6 4.3 %collective-permute-start.9 = (bf16[2,4,32,128]{3,2,1,0:T(8,128)(2,1)S(1)}, bf16[2,4,32,128]{3,2,1,0:T(8,128)(2,1)S(1)}, u32[]{:S(2)}, u32[]{:S(2)}) collective-permute-start(bf16[2,4,32,128]{3,2,1,0:T(8,128)(2,1)S(1)} %get-tuple-element.46), channel_id=1, source_target_pairs={{0,4},{2,6},{4,0},{6,2},{8,12},{10,14},{12,8},{14,10},{1,5},{3,7},... | collective-permute-start | bytes 196616 | tf_op jit(solution)/shard_map/ppermute | solution.py:385
  25.9 4.9 %collective-permute-start.10 = (bf16[4,32,128]{2,1,0:T(8,128)(2,1)S(1)}, bf16[4,32,128]{2,1,0:T(8,128)(2,1)S(1)}, u32[]{:S(2)}, u32[]{:S(2)}) collective-permute-start(bf16[4,32,128]{2,1,0:T(8,128)(2,1)S(1)} %get-tuple-element.48), channel_id=1, source_target_pairs={{0,8},{2,10},{4,12},{6,14},{8,0},{10,2},{12,4},{14,6},{1,9},{3,11}... | collective-permute-start | bytes 98312 | tf_op jit(solution)/shard_map/ppermute | solution.py:396

commit v12 on v11

--- a/solution.py
+++ b/solution.py
@@ -249,9 +249,12 @@
                 send_ref[at, level, j] = piece[:, nk:].astype(jnp.bfloat16)
 
 
-def near_kernel(keep_ref, got_ref, *out_refs):
+def near_kernel(by_core, keep_ref, got_ref, *out_refs):
+    first_core = lax.axis_index("modes") == 0
+    totals = [keep_ref[at] + got_ref[at].astype(jnp.float32) for at in range(2)]
     for at, ref in enumerate(out_refs):
-        ref[...] = (keep_ref[at] + got_ref[at].astype(jnp.float32)).astype(ref.dtype)
+        total = jnp.where(first_core, totals[at], totals[1 - at]) if by_core else totals[at]
+        ref[...] = total.astype(ref.dtype)
 
 
 def far_kernel(mine_ref, *refs):
@@ -369,9 +372,9 @@
         got_b = lax.ppermute(send_b, "modes", swap)
         piece = (JB, chunk, nk)
 
-        def summed(kinds, keep, got):
+        def summed(by_core, kinds, keep, got):
             return pl.pallas_call(
-                near_kernel,
+                functools.partial(near_kernel, by_core),
                 out_shape=[jax.ShapeDtypeStruct((2, *piece), kind) for kind in kinds],
                 in_specs=[vmem] * 2,
                 out_specs=[vmem] * 2,
@@ -379,11 +382,13 @@
                 name="near",
             )(keep, got)
 
-        part_3, part_1 = summed((bf16, bf16), keep_a, got_a)
-        mine, part_2 = summed((f32, bf16), keep_b, got_b)
+        out_0, out_1 = summed(True, (bf16, bf16), keep_a, got_a)
+        mine, out_2 = summed(False, (f32, bf16), keep_b, got_b)
         parts = [
-            lax.ppermute(part, "space", [(s, s ^ step) for s in range(n)])
-            for part, step in ((part_3, 3), (part_1, 1), (part_2, 2))
+            lax.ppermute(
+                part, both, [(2 * s + m, 2 * (s ^ steps[m]) + m) for s in range(n) for m in range(2)]
+            )
+            for part, steps in ((out_0, (3, 1)), (out_1, (1, 3)), (out_2, (2, 2)))
         ]
         keep, send = pl.pallas_call(
             far_kernel,

time: 31.6 us -> 31.7 us (level)
  no operation moved by 1% of the time
where the time goes in v12:
time: 31.7 us; the launch traced here: 31.5 us
  starting transfers between devices  12.9 us (41%)
  waiting for transfers between devices  11.3 us (36%)
  Pallas kernels  6.53 us (21%)
  between operations  0.74 us (2%)
    ppermute x3, starting transfers between devices, on_device(): lax.ppermute(part, both, [(2 * s + m, 2 * (s ^ steps[m]) + m) for s in ra...  3.62 us
    ppermute x1, waiting for transfers between devices, on_device(): got = lax.ppermute(send, 'space', [(s, s ^ NEAR) for s in range(n)])  3.21 us
    ppermute x3, waiting for transfers between devices, on_device(): lax.ppermute(part, both, [(2 * s + m, 2 * (s ^ steps[m]) + m) for s in ra...  3.19 us
    ppermute x1, waiting for transfers between devices, on_device(): xc = lax.ppermute(xc, both, cross([(s, x_to(s)) for s in range(n)]))  2.83 us
    ppermute x1, starting transfers between devices, on_device(): second = lax.ppermute(second, both, same(seconds))  2.6 us
    ppermute x1, starting transfers between devices, on_device(): first = lax.ppermute(first, both, same(firsts))  2.54 us
    pallas_call x1, Pallas kernels, on_device(): pl.pallas_call(local_kernel, out_shape=[jax.ShapeDtypeStruct((JB * 2 * nk...  2.41 us
    ppermute x1, waiting for transfers between devices, on_device(): lax.ppermute(zc, both, cross([(s, z_to(s)) for s in range(n) if 0 <= z_to...  2.04 us
  transfers between devices with their start and end apart: 11, of which 6 were waited for; matrix products, arithmetic and copies ran while one was open for 0% of the time, Pallas kernels for 11%

profile of v12, /device:TPU:0, one launch (start us, length us, event | category | flops | bytes accessed | tf_op | source)
XLA Modules:
  0.0 31.5 jit_solution(2334469436486173650)
XLA Ops:
  0.0 0.0 copy-start.1
  0.0 0.0 copy-start
  0.0 1.5 %prep.1 = (bf16[6,3,128,128]{3,2,1,0:T(8,128)(2,1)S(1)}, bf16[6,3,128,128]{3,2,1,0:T(8,128)(2,1)S(1)}, bf16[784,128]{1,0:T(8,128)(2,1)S(1)}, bf16[784,128]{1,0:T...) custom-call(bf16[128,3,1,8,128]{4,3,2,1,0:T(8,128)(2,1)} %modes_hbm.1), custom_call_target="tpu_custom_call" | custom-call | flops 1500000000 | bytes 2800000 | tf_op jit(solution)/shard_map/prep/pallas_call | solution.py:285
  1.5 0.5 %collective-permute-start = (bf16[6,3,128,128]{3,2,1,0:T(8,128)(2,1)S(1)}, bf16[6,3,128,128]{3,2,1,0:T(8,128)(2,1)S(1)}, u32[]{:S(2)}, u32[]{:S(2)}) collective-permute-start(bf16[6,3,128,128]{3,2,1,0:T(8,128)(2,1)S(1)} %get-tuple-element.28), channel_id=1, source_target_pairs={{0,1},{1,0},{2,3},{3,2},{4,5},{5,4},{6,7},{7,6},{8,9},{9,8},{10,11... | collective-permute-start | bytes 1769480 | tf_op jit(solution)/shard_map/ppermute | solution.py:310
  2.0 2.5 %collective-permute-start.1 = (bf16[784,128]{1,0:T(8,128)(2,1)S(1)}, bf16[784,128]{1,0:T(8,128)(2,1)S(1)}, u32[]{:S(2)}, u32[]{:S(2)}) collective-permute-start(bf16[784,128]{1,0:T(8,128)(2,1)S(1)} %get-tuple-element.29), channel_id=1, source_target_pairs={{0,2},{1,3},{2,0},{3,1},{4,6},{5,7},{6,4},{7,5},{8,10},{9,11},{10,... | collective-permute-start | bytes 602120 | tf_op jit(solution)/shard_map/ppermute | solution.py:311
  4.5 2.6 %collective-permute-start.2 = (bf16[784,128]{1,0:T(8,128)(2,1)S(1)}, bf16[784,128]{1,0:T(8,128)(2,1)S(1)}, u32[]{:S(2)}, u32[]{:S(2)}) collective-permute-start(bf16[784,128]{1,0:T(8,128)(2,1)S(1)} %get-tuple-element.30), channel_id=1, source_target_pairs={{0,12},{1,13},{2,6},{3,7},{4,0},{5,1},{6,10},{7,11},{8,4},{9,5},{1... | collective-permute-start | bytes 602120 | tf_op jit(solution)/shard_map/ppermute | solution.py:312
  7.1 0.0 collective-permute-done._.other_ref
  7.1 0.0 copy-done.1
  7.2 0.0 copy-done
  7.2 0.1 weights.1
  7.3 0.1 collective-permute-start.3
  7.3 1.3 %collective-permute-start.4 = (bf16[784,128]{1,0:T(8,128)(2,1)S(1)}, bf16[784,128]{1,0:T(8,128)(2,1)S(1)}, u32[]{:S(2)}, u32[]{:S(2)}) collective-permute-start(bf16[784,128]{1,0:T(8,128)(2,1)S(1)} %get-tuple-element.34), channel_id=1, source_target_pairs={{2,7},{3,6},{4,1},{5,0},{6,11},{7,10},{8,5},{9,4},{10,15},{11,14},... | collective-permute-start | bytes 602120 | tf_op jit(solution)/shard_map/ppermute | solution.py:323
  9.3 2.4 %local.1 = (f32[1024,256]{1,0:T(8,128)S(1)}, bf16[2,256,384]{2,1,0:T(8,128)(2,1)S(1)}) custom-call(bf16[6,3,128,128]{3,2,1,0:T(8,128)(2,1)S(1)} %get-tuple-element.27.own_ref, bf16[6,3,128,128]{3,2,1,0:T(8,128)(2,1)S(1)} %collective-permute-done._.other_ref, f32[8,128]{1,0:T(8,128)S(1)} %get-tuple-element.35.weight_ref, s32[1]{0:T(128)S(6)} %copy.5.jb_ref.refs_5_), custom_call_target="tpu_custom_call" | custom-call | flops 900000000 | bytes 2400000 | tf_op jit(solution)/shard_map/local/pallas_call | solution.py:326
  11.7 0.0 collective-permute-done.1.refs_0_
  11.7 0.0 collective-permute-done.2.refs_1_
  11.7 2.8 %collective-permute-done.3.refs_2_ = bf16[784,128]{1,0:T(8,128)(2,1)S(1)} collective-permute-done((bf16[784,128]{1,0:T(8,128)(2,1)S(1)}, bf16[784,128]{1,0:T(8,128)(2,1)S(1)}, u32[]{:S(2)}, u32[]{:S(2)}) %collective-permute-start.3) | collective-permute-done | bytes 200736 | tf_op jit(solution)/shard_map/ppermute | solution.py:322
  14.6 2.0 %collective-permute-done.4.refs_3_ = bf16[784,128]{1,0:T(8,128)(2,1)S(1)} collective-permute-done((bf16[784,128]{1,0:T(8,128)(2,1)S(1)}, bf16[784,128]{1,0:T(8,128)(2,1)S(1)}, u32[]{:S(2)}, u32[]{:S(2)}) %collective-permute-start.4) | collective-permute-done | bytes 200736 | tf_op jit(solution)/shard_map/ppermute | solution.py:323
  16.6 0.9 %cross.2 = (f32[2,2,4,32,128]{4,3,2,1,0:T(8,128)S(1)}, bf16[2,2,4,32,128]{4,3,2,1,0:T(8,128)(2,1)S(1)}, bf16[256,2304]{1,0:T(8,128)(2,1)S(1)}) custom-call(bf16[6,3,128,128]{3,2,1,0:T(8,128)(2,1)S(1)} %get-tuple-element.27.own_ref, bf16[6,3,128,128]{3,2,1,0:T(8,128)(2,1)S(1)} %collective-permute-done._.other_ref, ...), custom_call_target="tpu_custom_call" | custom-call | flops 900000000 | bytes 4000000 | tf_op jit(solution)/shard_map/cross/pallas_call | solution.py:351
  17.5 0.2 collective-permute-start.6
  17.7 0.8 %cross.3 = (f32[2,2,4,32,128]{4,3,2,1,0:T(8,128)S(1)}, bf16[2,2,4,32,128]{4,3,2,1,0:T(8,128)(2,1)S(1)}) custom-call(bf16[6,3,128,128]{3,2,1,0:T(8,128)(2,1)S(1)} %get-tuple-element.27.own_ref, bf16[6,3,128,128]{3,2,1,0:T(8,128)(2,1)S(1)} %collective-permute-done._.other_ref, bf16[784,128]{1,0:T(8,128)(2,1)S(1)} %collective-permute-done.1.refs_0_, ...), custom_call_target="tpu_custom_call" | custom-call | flops 900000000 | bytes 4000000 | tf_op jit(solution)/shard_map/cross/pallas_call | solution.py:351
  18.5 0.5 %collective-permute-start.5 = (bf16[2,2,4,32,128]{4,3,2,1,0:T(8,128)(2,1)S(1)}, bf16[2,2,4,32,128]{4,3,2,1,0:T(8,128)(2,1)S(1)}, u32[]{:S(2)}, u32[]{:S(2)}) collective-permute-start(bf16[2,2,4,32,128]{4,3,2,1,0:T(8,128)(2,1)S(1)} %get-tuple-element.40), channel_id=1, source_target_pairs={{0,1},{1,0},{2,3},{3,2},{4,5},{5,4},{6,7},{7,6},{8,9},{9,8},{10,11... | collective-permute-start | bytes 393224 | tf_op jit(solution)/shard_map/ppermute | solution.py:372
  19.0 0.0 collective-permute-done.6.got_ref
  19.1 1.5 %collective-permute-start.7 = (bf16[2,4,32,128]{3,2,1,0:T(8,128)(2,1)S(1)}, bf16[2,4,32,128]{3,2,1,0:T(8,128)(2,1)S(1)}, u32[]{:S(2)}, u32[]{:S(2)}) collective-permute-start(bf16[2,4,32,128]{3,2,1,0:T(8,128)(2,1)S(1)} %get-tuple-element.44), channel_id=1, source_target_pairs={{0,6},{1,3},{2,4},{3,1},{4,2},{5,7},{6,0},{7,5},{8,14},{9,11},{10,... | collective-permute-start | bytes 196616 | tf_op jit(solution)/shard_map/ppermute | solution.py:388
  20.6 0.9 %collective-permute-start.8 = (bf16[2,4,32,128]{3,2,1,0:T(8,128)(2,1)S(1)}, bf16[2,4,32,128]{3,2,1,0:T(8,128)(2,1)S(1)}, u32[]{:S(2)}, u32[]{:S(2)}) collective-permute-start(bf16[2,4,32,128]{3,2,1,0:T(8,128)(2,1)S(1)} %get-tuple-element.45), channel_id=1, source_target_pairs={{0,2},{1,7},{2,0},{3,5},{4,6},{5,3},{6,4},{7,1},{8,10},{9,15},{10,... | collective-permute-start | bytes 196616 | tf_op jit(solution)/shard_map/ppermute | solution.py:388
  21.5 0.0 collective-permute-done.5.got_ref
  21.6 1.1 %collective-permute-start.9 = (bf16[2,4,32,128]{3,2,1,0:T(8,128)(2,1)S(1)}, bf16[2,4,32,128]{3,2,1,0:T(8,128)(2,1)S(1)}, u32[]{:S(2)}, u32[]{:S(2)}) collective-permute-start(bf16[2,4,32,128]{3,2,1,0:T(8,128)(2,1)S(1)} %get-tuple-element.46), channel_id=1, source_target_pairs={{0,4},{1,5},{2,6},{3,7},{4,0},{5,1},{6,2},{7,3},{8,12},{9,13},{10,... | collective-permute-start | bytes 196616 | tf_op jit(solution)/shard_map/ppermute | solution.py:388
  22.7 1.6 %collective-permute-done.7.refs_0_ = bf16[2,4,32,128]{3,2,1,0:T(8,128)(2,1)S(1)} collective-permute-done((bf16[2,4,32,128]{3,2,1,0:T(8,128)(2,1)S(1)}, bf16[2,4,32,128]{3,2,1,0:T(8,128)(2,1)S(1)}, u32[]{:S(2)}, u32[]{:S(2)}) %collective-permute-start.7) | collective-permute-done | bytes 65568 | tf_op jit(solution)/shard_map/ppermute | solution.py:388
  24.3 0.7 %collective-permute-done.8.refs_1_ = bf16[2,4,32,128]{3,2,1,0:T(8,128)(2,1)S(1)} collective-permute-done((bf16[2,4,32,128]{3,2,1,0:T(8,128)(2,1)S(1)}, bf16[2,4,32,128]{3,2,1,0:T(8,128)(2,1)S(1)}, u32[]{:S(2)}, u32[]{:S(2)}) %collective-permute-start.8) | collective-permute-done | bytes 65568 | tf_op jit(solution)/shard_map/ppermute | solution.py:388
  25.0 0.9 %collective-permute-done.9.refs_2_ = bf16[2,4,32,128]{3,2,1,0:T(8,128)(2,1)S(1)} collective-permute-done((bf16[2,4,32,128]{3,2,1,0:T(8,128)(2,1)S(1)}, bf16[2,4,32,128]{3,2,1,0:T(8,128)(2,1)S(1)}, u32[]{:S(2)}, u32[]{:S(2)}) %collective-permute-start.9) | collective-permute-done | bytes 65568 | tf_op jit(solution)/shard_map/ppermute | solution.py:388
  25.9 1.7 %collective-permute-start.10 = (bf16[4,32,128]{2,1,0:T(8,128)(2,1)S(1)}, bf16[4,32,128]{2,1,0:T(8,128)(2,1)S(1)}, u32[]{:S(2)}, u32[]{:S(2)}) collective-permute-start(bf16[4,32,128]{2,1,0:T(8,128)(2,1)S(1)} %get-tuple-element.48), channel_id=1, source_target_pairs={{0,8},{2,10},{4,12},{6,14},{8,0},{10,2},{12,4},{14,6},{1,9},{3,11}... | collective-permute-start | bytes 98312 | tf_op jit(solution)/shard_map/ppermute | solution.py:401
  27.6 3.2 %collective-permute-done.10.got_ref = bf16[4,32,128]{2,1,0:T(8,128)(2,1)S(1)} collective-permute-done((bf16[4,32,128]{2,1,0:T(8,128)(2,1)S(1)}, bf16[4,32,128]{2,1,0:T(8,128)(2,1)S(1)}, u32[]{:S(2)}, u32[]{:S(2)}) %collective-permute-start.10) | collective-permute-done | bytes 32800 | tf_op jit(solution)/shard_map/ppermute | solution.py:401
  30.8 0.7 %total.1 = f32[32,4,128]{2,1,0:T(4,128)} custom-call(f32[4,32,128]{2,1,0:T(8,128)S(1)} %get-tuple-element.47.keep_ref, bf16[4,32,128]{2,1,0:T(8,128)(2,1)S(1)} %collective-permute-done.10.got_ref), custom_call_target="tpu_custom_call" | custom-call | tf_op jit(solution)/shard_map/total/pallas_call | solution.py:402
  (3 shorter events, 0.1 us)
Async XLA Ops:
  0.0 7.1 %copy-start.1 = (f32[16]{0:T(128)S(1)}, f32[16]{0:T(128)}, u32[]{:S(2)}) copy-start(f32[16]{0:T(128)} %param.6) | copy-start | bytes 196
  0.0 7.2 %copy-start = (s32[1,8,128]{2,1,0:T(8,128)S(1)}, s32[1,8,128]{2,1,0:T(8,128)}, u32[]{:S(2)}) copy-start(s32[1,8,128]{2,1,0:T(8,128)} %ids_ref.1) | copy-start | bytes 12292
  1.5 5.7 %collective-permute-start = (bf16[6,3,128,128]{3,2,1,0:T(8,128)(2,1)S(1)}, bf16[6,3,128,128]{3,2,1,0:T(8,128)(2,1)S(1)}, u32[]{:S(2)}, u32[]{:S(2)}) collective-permute-start(bf16[6,3,128,128]{3,2,1,0:T(8,128)(2,1)S(1)} %get-tuple-element.28), channel_id=1, source_target_pairs={{0,1},{1,0},{2,3},{3,2},{4,5},{5,4},{6,7},{7,6},{8,9},{9,8},{10,11... | collective-permute-start | bytes 1769480 | tf_op jit(solution)/shard_map/ppermute | solution.py:310
  2.0 9.7 %collective-permute-start.1 = (bf16[784,128]{1,0:T(8,128)(2,1)S(1)}, bf16[784,128]{1,0:T(8,128)(2,1)S(1)}, u32[]{:S(2)}, u32[]{:S(2)}) collective-permute-start(bf16[784,128]{1,0:T(8,128)(2,1)S(1)} %get-tuple-element.29), channel_id=1, source_target_pairs={{0,2},{1,3},{2,0},{3,1},{4,6},{5,7},{6,4},{7,5},{8,10},{9,11},{10,... | collective-permute-start | bytes 602120 | tf_op jit(solution)/shard_map/ppermute | solution.py:311
  4.5 7.2 %collective-permute-start.2 = (bf16[784,128]{1,0:T(8,128)(2,1)S(1)}, bf16[784,128]{1,0:T(8,128)(2,1)S(1)}, u32[]{:S(2)}, u32[]{:S(2)}) collective-permute-start(bf16[784,128]{1,0:T(8,128)(2,1)S(1)} %get-tuple-element.30), channel_id=1, source_target_pairs={{0,12},{1,13},{2,6},{3,7},{4,0},{5,1},{6,10},{7,11},{8,4},{9,5},{1... | collective-permute-start | bytes 602120 | tf_op jit(solution)/shard_map/ppermute | solution.py:312
  7.3 7.3 %collective-permute-start.3 = (bf16[784,128]{1,0:T(8,128)(2,1)S(1)}, bf16[784,128]{1,0:T(8,128)(2,1)S(1)}, u32[]{:S(2)}, u32[]{:S(2)}) collective-permute-start(bf16[784,128]{1,0:T(8,128)(2,1)S(1)} %get-tuple-element.33), channel_id=1, source_target_pairs={{0,3},{1,2},{2,1},{3,0},{4,7},{5,6},{6,5},{7,4},{8,11},{9,10},{10,... | collective-permute-start | bytes 602120 | tf_op jit(solution)/shard_map/ppermute | solution.py:322
  7.3 9.3 %collective-permute-start.4 = (bf16[784,128]{1,0:T(8,128)(2,1)S(1)}, bf16[784,128]{1,0:T(8,128)(2,1)S(1)}, u32[]{:S(2)}, u32[]{:S(2)}) collective-permute-start(bf16[784,128]{1,0:T(8,128)(2,1)S(1)} %get-tuple-element.34), channel_id=1, source_target_pairs={{2,7},{3,6},{4,1},{5,0},{6,11},{7,10},{8,5},{9,4},{10,15},{11,14},... | collective-permute-start | bytes 602120 | tf_op jit(solution)/shard_map/ppermute | solution.py:323
  17.5 1.5 %collective-permute-start.6 = (bf16[2,2,4,32,128]{4,3,2,1,0:T(8,128)(2,1)S(1)}, bf16[2,2,4,32,128]{4,3,2,1,0:T(8,128)(2,1)S(1)}, u32[]{:S(2)}, u32[]{:S(2)}) collective-permute-start(bf16[2,2,4,32,128]{4,3,2,1,0:T(8,128)(2,1)S(1)} %get-tuple-element.43), channel_id=1, source_target_pairs={{0,1},{1,0},{2,3},{3,2},{4,5},{5,4},{6,7},{7,6},{8,9},{9,8},{10,11... | collective-permute-start | bytes 393224 | tf_op jit(solution)/shard_map/ppermute | solution.py:370
  18.5 3.0 %collective-permute-start.5 = (bf16[2,2,4,32,128]{4,3,2,1,0:T(8,128)(2,1)S(1)}, bf16[2,2,4,32,128]{4,3,2,1,0:T(8,128)(2,1)S(1)}, u32[]{:S(2)}, u32[]{:S(2)}) collective-permute-start(bf16[2,2,4,32,128]{4,3,2,1,0:T(8,128)(2,1)S(1)} %get-tuple-element.40), channel_id=1, source_target_pairs={{0,1},{1,0},{2,3},{3,2},{4,5},{5,4},{6,7},{7,6},{8,9},{9,8},{10,11... | collective-permute-start | bytes 393224 | tf_op jit(solution)/shard_map/ppermute | solution.py:372
  19.1 5.2 %collective-permute-start.7 = (bf16[2,4,32,128]{3,2,1,0:T(8,128)(2,1)S(1)}, bf16[2,4,32,128]{3,2,1,0:T(8,128)(2,1)S(1)}, u32[]{:S(2)}, u32[]{:S(2)}) collective-permute-start(bf16[2,4,32,128]{3,2,1,0:T(8,128)(2,1)S(1)} %get-tuple-element.44), channel_id=1, source_target_pairs={{0,6},{1,3},{2,4},{3,1},{4,2},{5,7},{6,0},{7,5},{8,14},{9,11},{10,... | collective-permute-start | bytes 196616 | tf_op jit(solution)/shard_map/ppermute | solution.py:388
  20.6 4.4 %collective-permute-start.8 = (bf16[2,4,32,128]{3,2,1,0:T(8,128)(2,1)S(1)}, bf16[2,4,32,128]{3,2,1,0:T(8,128)(2,1)S(1)}, u32[]{:S(2)}, u32[]{:S(2)}) collective-permute-start(bf16[2,4,32,128]{3,2,1,0:T(8,128)(2,1)S(1)} %get-tuple-element.45), channel_id=1, source_target_pairs={{0,2},{1,7},{2,0},{3,5},{4,6},{5,3},{6,4},{7,1},{8,10},{9,15},{10,... | collective-permute-start | bytes 196616 | tf_op jit(solution)/shard_map/ppermute | solution.py:388
  21.6 4.3 %collective-permute-start.9 = (bf16[2,4,32,128]{3,2,1,0:T(8,128)(2,1)S(1)}, bf16[2,4,32,128]{3,2,1,0:T(8,128)(2,1)S(1)}, u32[]{:S(2)}, u32[]{:S(2)}) collective-permute-start(bf16[2,4,32,128]{3,2,1,0:T(8,128)(2,1)S(1)} %get-tuple-element.46), channel_id=1, source_target_pairs={{0,4},{1,5},{2,6},{3,7},{4,0},{5,1},{6,2},{7,3},{8,12},{9,13},{10,... | collective-permute-start | bytes 196616 | tf_op jit(solution)/shard_map/ppermute | solution.py:388
  25.9 4.9 %collective-permute-start.10 = (bf16[4,32,128]{2,1,0:T(8,128)(2,1)S(1)}, bf16[4,32,128]{2,1,0:T(8,128)(2,1)S(1)}, u32[]{:S(2)}, u32[]{:S(2)}) collective-permute-start(bf16[4,32,128]{2,1,0:T(8,128)(2,1)S(1)} %get-tuple-element.48), channel_id=1, source_target_pairs={{0,8},{2,10},{4,12},{6,14},{8,0},{10,2},{12,4},{14,6},{1,9},{3,11}... | collective-permute-start | bytes 98312 | tf_op jit(solution)/shard_map/ppermute | solution.py:401

commit v13 on v9

--- a/solution.py
+++ b/solution.py
@@ -16,7 +16,7 @@
 PREP_LIMIT = 53_100 * 1024
 
 
-def prep_kernel(modes_hbm, own_ref, core_ref, zs_ref, xs_ref, zc_ref, xc_ref, modes_ref, tr, sems):
+def prep_kernel(modes_hbm, own_ref, core_ref, xs_ref, zs_ref, xc_ref, zc_ref, modes_ref, tr, sems):
     m = lax.axis_index("modes")
     q = lax.rem(lax.axis_index("space"), 2)
     nk, comps, _, nx, nz = modes_hbm.shape
@@ -53,7 +53,7 @@
         ref[pl.ds(quarter * comps * nk, pad), :] = jnp.zeros((pad, nz), jnp.bfloat16)
 
 
-def weights_kernel(ids_ref, table_ref, zc_ref, xc_ref, _, weight_ref, zc_out, xc_out):
+def weights_kernel(ids_ref, table_ref, xc_ref, zc_ref, _, weight_ref, xc_out, zc_out):
     m = lax.axis_index("modes")
     q = lax.rem(lax.axis_index("space"), 2)
     body, nz = xc_ref.shape
@@ -62,7 +62,7 @@
     table = table_ref[...]
     weight = jnp.zeros((nx, nz), jnp.float32)
     for entry in range(NW):
-        weight = jnp.where(ids_ref[0] == entry, table[:, entry : entry + 1], weight)
+        weight = jnp.where(ids_ref[0] == entry, table[0:1, entry : entry + 1], weight)
     weight_ref[...] = weight
     for ref, out, at in ((zc_ref, zc_out, 2 * (1 - m) + q), (xc_ref, xc_out, 2 * (1 - m) + 1 - q)):
         out[pl.ds(0, body), :] = ref[...]
@@ -152,8 +152,39 @@
         w0_ref[r] = wts[quarter * q + r]
 
 
+def sign_of_plane():
+    return jnp.where(lax.rem(lax.axis_index("space"), 2) == 0, 0.5, -0.5)
+
+
+def early_kernel(own_ref, other_ref, xs_ref, _, xc_ref, w0_ref, jb_ref, acc_ref, out_ref, w1_ref, adv):
+    m = lax.axis_index("modes")
+    q = lax.rem(lax.axis_index("space"), 2)
+    rows, comps, nk, nz = own_ref.shape
+    quarter = (rows - 2) // 2
+    pick = picks(jb_ref, m, nk)
+    weights = received_weights(xc_ref, quarter * comps * nk, quarter)
+    for r in range(quarter):
+        row0 = 1 + quarter * q + r
+        phi0 = sign_of_plane() * picked(pick, own_ref.at[row0, 1], other_ref.at[row0, 1])
+        phi0 = [spread(phi0[j : j + 1]) for j in range(JB)]
+        for c in range(comps):
+            at = pl.ds((r * comps + c) * nz, nz)
+            src = pl.ds((r * comps + c) * nk, nk)
+            for half, p1 in enumerate((xs_ref, xc_ref)):
+                f1 = p1[src, :]
+                w1_ref[pl.ds(half * nk, nk), at] = (weights[r] * f1.astype(jnp.float32)).astype(
+                    jnp.bfloat16
+                )
+                for j in range(JB):
+                    adv[r, pl.ds((2 * j + half) * nk, nk), pl.ds(c * nz, nz)] = scaled(phi0[j], f1)
+    total = acc_ref[...]
+    for r in range(quarter):
+        total = total + dot_nt(adv[r], w0_ref[r])
+    out_ref[...] = total
+
+
 def cross_kernel(classes_of, chunk, planes, has_weighted, own_ref, other_ref, *refs):
-    zs_ref, xs_ref, zc_ref, xc_ref, w0_ref, jb_ref, acc_ref, *refs = refs
+    xs_ref, zs_ref, xc_ref, zc_ref, w1_ref, jb_ref, acc_ref, *refs = refs
     if has_weighted:
         wts, keep_ref, send_ref, adv = refs
     else:
@@ -161,7 +192,6 @@
     m = lax.axis_index("modes")
     plane = lax.axis_index("space")
     q = lax.rem(plane, 2)
-    sigma = jnp.where(q == 0, 0.5, -0.5)
     inside = jnp.where(jnp.logical_or(plane == 1, plane == planes - 2), 0.0, 1.0)
     rows, comps, nk, nz = own_ref.shape
     quarter = (rows - 2) // 2
@@ -169,32 +199,27 @@
     pick = picks(jb_ref, m, nk)
     classes = [pl.multiple_of(chunk * cls, chunk) for cls in classes_of(plane)]
     if not has_weighted:
-        w1 = received_weights(xc_ref, quarter * comps * nk, quarter)
-        w2 = [inside * weight for weight in received_weights(zc_ref, quarter * comps * nk, quarter)]
+        weights = received_weights(zc_ref, quarter * comps * nk, quarter)
+        wts[:, pl.ds(0, span)] = w1_ref[...]
         for r in range(quarter):
-            wts[:, pl.ds(r * comps * nz, comps * nz)] = w0_ref[r]
+            weight = inside * weights[r]
             for c in range(comps):
-                lane = (r * comps + c) * nz
                 src = pl.ds((r * comps + c) * nk, nk)
-                for half, (p1, p2) in enumerate(((xs_ref, zs_ref), (xc_ref, zc_ref))):
-                    block = pl.ds(half * nk, nk)
-                    for part, (field, weight) in enumerate(((p1, w1[r]), (p2, w2[r])), 1):
-                        wts[block, pl.ds(part * span + lane, nz)] = (
-                            weight * field[src, :].astype(jnp.float32)
-                        ).astype(jnp.bfloat16)
+                for half, p2 in enumerate((zs_ref, zc_ref)):
+                    wts[pl.ds(half * nk, nk), pl.ds(span + (r * comps + c) * nz, nz)] = (
+                        weight * p2[src, :].astype(jnp.float32)
+                    ).astype(jnp.bfloat16)
     phis = []
     for r in range(quarter):
-        row0 = 1 + quarter * q + r
         along = pl.ds((r * comps + 1) * nk, nk)
-        phi0 = sigma * picked(pick, own_ref.at[row0, 1], other_ref.at[row0, 1])
-        phi1 = sigma * picked(pick, xs_ref.at[along], xc_ref.at[along])
-        phi2 = -sigma * picked(pick, zs_ref.at[along], zc_ref.at[along])
-        phis.append([[spread(phi[j : j + 1]) for j in range(JB)] for phi in (phi0, phi1, phi2)])
+        phi1 = sign_of_plane() * picked(pick, xs_ref.at[along], xc_ref.at[along])
+        phi2 = -sign_of_plane() * picked(pick, zs_ref.at[along], zc_ref.at[along])
+        phis.append([[spread(phi[j : j + 1]) for j in range(JB)] for phi in (phi1, phi2)])
     inside = inside.astype(jnp.bfloat16)
     for at, cls in enumerate(classes):
         for r in range(quarter):
             row0 = 1 + quarter * q + r
-            phi0, phi1, phi2 = phis[r]
+            phi1, phi2 = phis[r]
             for c in range(comps):
                 lane = (r * comps + c) * nz
                 src = (r * comps + c) * nk
@@ -206,9 +231,8 @@
                     gy = inside * p2[pl.ds(src + cls, chunk), :] - f0
                     for j in range(JB):
                         here = pl.ds((half * JB + j) * chunk, chunk)
-                        adv[at, here, pl.ds(lane, nz)] = scaled(phi0[j], f1)
-                        adv[at, here, pl.ds(span + lane, nz)] = scaled(phi1[j], gy)
-                        adv[at, here, pl.ds(2 * span + lane, nz)] = scaled(phi2[j], f1)
+                        adv[at, here, pl.ds(lane, nz)] = scaled(phi1[j], gy)
+                        adv[at, here, pl.ds(span + lane, nz)] = scaled(phi2[j], f1)
         total = dot_nt(adv[at], wts[...])
         for half in range(2):
             level = m if half == 0 else 1 - m
@@ -249,7 +273,7 @@
     six = nx // 2 + 2
     quarter = nx // 4
     body = quarter * comps * nk
-    own, to_core, zs, xs, zc, xc = pl.pallas_call(
+    own, to_core, xs, zs, xc, zc = pl.pallas_call(
         prep_kernel,
         out_shape=[jax.ShapeDtypeStruct((six, comps, nk, nz), bf16)] * 2
         + [jax.ShapeDtypeStruct((body + PADROWS, nz), bf16)] * 2
@@ -272,9 +296,9 @@
     same = lambda pairs: [(2 * a + m, 2 * b + m) for a, b in pairs for m in range(2)]
     cross = lambda pairs: [(2 * a + m, 2 * b + 1 - m) for a, b in pairs for m in range(2)]
     other = lax.ppermute(to_core, "modes", [(0, 1), (1, 0)])
+    xs = lax.ppermute(xs, both, same(x_pairs))
     zs = lax.ppermute(zs, both, same(z_pairs))
-    xs = lax.ppermute(xs, both, same(x_pairs))
-    weight, zc, xc = pl.pallas_call(
+    weight, xc, zc = pl.pallas_call(
         weights_kernel,
         out_shape=[jax.ShapeDtypeStruct((nx, nz), f32)]
         + [jax.ShapeDtypeStruct((body + 8 * quarter, nz), bf16)] * 2,
@@ -282,14 +306,9 @@
         out_specs=[vmem] * 3,
         compiler_params=params,
         name="weights",
-    )(weight_ids, weight_table.reshape(1, NW), zc, xc, other)
+    )(weight_ids, jnp.broadcast_to(weight_table[None], (8, NW)), xc, zc, other)
     xc = lax.ppermute(xc, both, cross(x_pairs))
-    zc = lax.ppermute(zc, both, cross(z_pairs))
-
-    def estimate(depth, size):
-        return pl.CostEstimate(
-            flops=2 * JB * (2 * nk) ** 2 * depth, bytes_accessed=size, transcendentals=0
-        )
+    zc = lax.ppermute(zc, both, cross([(s, to) for s, to in z_pairs if abs(s - to) == 2]))
 
     depth = nx // 4 * comps * nz
     depth = quarter * comps * nz
@@ -310,6 +329,20 @@
         name="local",
     )(own, other, weight, j_block)
 
+    acc, w1 = pl.pallas_call(
+        early_kernel,
+        out_shape=[
+            jax.ShapeDtypeStruct((JB * 2 * nk, 2 * nk), f32),
+            jax.ShapeDtypeStruct((2 * nk, depth), bf16),
+        ],
+        in_specs=[vmem] * 3 + [pl.BlockSpec(memory_space=pl.ANY), vmem, vmem, smem, vmem],
+        out_specs=[vmem] * 2,
+        scratch_shapes=[pltpu.VMEM((quarter, JB * 2 * nk, comps * nz), bf16)],
+        compiler_params=params,
+        cost_estimate=pl.CostEstimate(flops=600_000_000, bytes_accessed=2_400_000, transcendentals=0),
+        name="early",
+    )(own, other, xs, zs, xc, w0, j_block, acc)
+
     per_target = 2 * nk // n
     chunk = max(16, per_target)
 
@@ -317,19 +350,19 @@
         piece = (count, 2, JB, chunk, nk)
         out_shape = [jax.ShapeDtypeStruct(piece, f32), jax.ShapeDtypeStruct(piece, bf16)]
         if not weighted:
-            out_shape.append(jax.ShapeDtypeStruct((2 * nk, 3 * depth), bf16))
+            out_shape.append(jax.ShapeDtypeStruct((2 * nk, 2 * depth), bf16))
         return pl.pallas_call(
             functools.partial(cross_kernel, classes_of, chunk, n, bool(weighted)),
             out_shape=out_shape,
             in_specs=[vmem] * 7 + [smem] + [vmem] * (1 + len(weighted)),
             out_specs=[vmem] * len(out_shape),
-            scratch_shapes=[pltpu.VMEM((count, 2 * JB * chunk, 3 * depth), bf16)],
+            scratch_shapes=[pltpu.VMEM((count, 2 * JB * chunk, 2 * depth), bf16)],
             compiler_params=params,
             cost_estimate=pl.CostEstimate(
                 flops=900_000_000, bytes_accessed=4_000_000, transcendentals=0
             ),
             name="cross",
-        )(own, other, zs, xs, zc, xc, w0, j_block, acc, *weighted)
+        )(own, other, xs, zs, xc, zc, w1, j_block, acc, *weighted)
 
     swap = [(0, 1), (1, 0)]
     if n == 2 * NEAR:

time: 31.7 us -> 31.5 us (level)
  waiting for transfers between devices: 10.6 us -> 9.98 us
  Pallas kernels: 6.51 us -> 6.83 us
    ppermute x1, starting transfers between devices: 0.01 us -> 2.56 us  [on_device(): xs = lax.ppermute(xs, both, same(x_pairs))]
    ppermute x1, waiting for transfers between devices: 2.52 us -> 0.01 us  [on_device(): xs = lax.ppermute(xs, both, same(x_pairs))]
    ppermute x1, waiting for transfers between devices: 1.42 us -> 2.8 us  [on_device(): xc = lax.ppermute(xc, both, cross(x_pairs))]
    ppermute x1, waiting for transfers between devices: 2.21 us -> 3.39 us  [on_device(): got = lax.ppermute(send, 'space', [(s, s ^ NEAR) for s in range(n)])]
    ppermute x1, starting transfers between devices: 2.67 us -> 1.48 us  [on_device(): got = lax.ppermute(send, 'space', [(s, s ^ NEAR) for s in range(n)])]
    ppermute x1, starting transfers between devices: 4.66 us -> 3.6 us  [on_device(): zs = lax.ppermute(zs, both, same(z_pairs))]
    pallas_call x0 -> x1, Pallas kernels: none -> 0.75 us  [on_device(): pl.pallas_call(early_kernel, out_shape=[jax.ShapeDtypeStruct((JB * 2 * nk...]
    ppermute x1, starting transfers between devices: 0.64 us -> 0.18 us  [on_device(): got_a = lax.ppermute(send_a, 'modes', swap)]
  transfers between devices with their start and end apart: 11 -> 11, of which waited for: 9 -> 6; matrix products, arithmetic and copies ran while one was open for 0% -> 0% of each run, Pallas kernels for 11% -> 13%
where the time goes in v13:
time: 31.5 us; the launch traced here: 31.4 us
  starting transfers between devices  13.8 us (44%)
  waiting for transfers between devices  9.98 us (32%)
  Pallas kernels  6.83 us (22%)
  between operations  0.75 us (2%)
    ppermute x3, starting transfers between devices, on_device(): lax.ppermute(part, 'space', [(s, s ^ step) for s in range(n)])  3.62 us
    ppermute x1, starting transfers between devices, on_device(): zs = lax.ppermute(zs, both, same(z_pairs))  3.6 us
    ppermute x1, waiting for transfers between devices, on_device(): got = lax.ppermute(send, 'space', [(s, s ^ NEAR) for s in range(n)])  3.39 us
    ppermute x1, waiting for transfers between devices, on_device(): xc = lax.ppermute(xc, both, cross(x_pairs))  2.8 us
    ppermute x1, starting transfers between devices, on_device(): xs = lax.ppermute(xs, both, same(x_pairs))  2.56 us
    ppermute x3, waiting for transfers between devices, on_device(): lax.ppermute(part, 'space', [(s, s ^ step) for s in range(n)])  2.51 us
    pallas_call x1, Pallas kernels, on_device(): pl.pallas_call(local_kernel, out_shape=[jax.ShapeDtypeStruct((JB * 2 * nk...  2.43 us
    ppermute x1, starting transfers between devices, on_device(): got = lax.ppermute(send, 'space', [(s, s ^ NEAR) for s in range(n)])  1.48 us
  transfers between devices with their start and end apart: 11, of which 6 were waited for; matrix products, arithmetic and copies ran while one was open for 0% of the time, Pallas kernels for 13%

profile of v13, /device:TPU:0, one launch (start us, length us, event | category | flops | bytes accessed | tf_op | source)
XLA Modules:
  0.0 31.4 jit_solution(9543301593882558730)
XLA Ops:
  0.0 0.0 copy-start.1
  0.0 1.5 %prep.1 = (bf16[6,3,128,128]{3,2,1,0:T(8,128)(2,1)S(1)}, bf16[6,3,128,128]{3,2,1,0:T(8,128)(2,1)S(1)}, bf16[784,128]{1,0:T(8,128)(2,1)S(1)}, bf16[784,128]{1,0:T...) custom-call(bf16[128,3,1,8,128]{4,3,2,1,0:T(8,128)(2,1)} %modes_hbm.1), custom_call_target="tpu_custom_call" | custom-call | flops 1500000000 | bytes 2800000 | tf_op jit(solution)/shard_map/prep/pallas_call | solution.py:276
  1.5 0.5 %collective-permute-start = (bf16[6,3,128,128]{3,2,1,0:T(8,128)(2,1)S(1)}, bf16[6,3,128,128]{3,2,1,0:T(8,128)(2,1)S(1)}, u32[]{:S(2)}, u32[]{:S(2)}) collective-permute-start(bf16[6,3,128,128]{3,2,1,0:T(8,128)(2,1)S(1)} %get-tuple-element.30), channel_id=1, source_target_pairs={{0,1},{1,0},{2,3},{3,2},{4,5},{5,4},{6,7},{7,6},{8,9},{9,8},{10,11... | collective-permute-start | bytes 1769480 | tf_op jit(solution)/shard_map/ppermute | solution.py:298
  2.0 2.6 %collective-permute-start.1 = (bf16[784,128]{1,0:T(8,128)(2,1)S(1)}, bf16[784,128]{1,0:T(8,128)(2,1)S(1)}, u32[]{:S(2)}, u32[]{:S(2)}) collective-permute-start(bf16[784,128]{1,0:T(8,128)(2,1)S(1)} %get-tuple-element.31), channel_id=1, source_target_pairs={{0,2},{1,3},{2,0},{3,1},{4,6},{5,7},{6,4},{7,5},{8,10},{9,11},{10,... | collective-permute-start | bytes 602120 | tf_op jit(solution)/shard_map/ppermute | solution.py:299
  4.6 0.0 copy-start
  4.6 3.6 %collective-permute-start.2 = (bf16[784,128]{1,0:T(8,128)(2,1)S(1)}, bf16[784,128]{1,0:T(8,128)(2,1)S(1)}, u32[]{:S(2)}, u32[]{:S(2)}) collective-permute-start(bf16[784,128]{1,0:T(8,128)(2,1)S(1)} %get-tuple-element.32), channel_id=1, source_target_pairs={{0,12},{1,13},{2,6},{3,7},{4,0},{5,1},{6,10},{7,11},{8,4},{9,5},{1... | collective-permute-start | bytes 602120 | tf_op jit(solution)/shard_map/ppermute | solution.py:300
  8.2 0.0 collective-permute-done._.other_ref
  8.2 0.0 copy-done.1
  8.2 0.0 copy-done
  8.2 0.1 weights.1
  8.3 0.1 collective-permute-start.3
  8.4 1.3 %collective-permute-start.4 = (bf16[784,128]{1,0:T(8,128)(2,1)S(1)}, bf16[784,128]{1,0:T(8,128)(2,1)S(1)}, u32[]{:S(2)}, u32[]{:S(2)}) collective-permute-start(bf16[784,128]{1,0:T(8,128)(2,1)S(1)} %get-tuple-element.36), channel_id=1, source_target_pairs={{2,7},{3,6},{4,1},{5,0},{6,11},{7,10},{8,5},{9,4},{10,15},{11,14},... | collective-permute-start | bytes 602120 | tf_op jit(solution)/shard_map/ppermute | solution.py:311
  10.3 2.4 %local.1 = (f32[1024,256]{1,0:T(8,128)S(1)}, bf16[2,256,384]{2,1,0:T(8,128)(2,1)S(1)}) custom-call(bf16[6,3,128,128]{3,2,1,0:T(8,128)(2,1)S(1)} %get-tuple-element.29.own_ref, bf16[6,3,128,128]{3,2,1,0:T(8,128)(2,1)S(1)} %collective-permute-done._.other_ref, f32[8,128]{1,0:T(8,128)S(1)} %get-tuple-element.37.weight_ref, s32[1]{0:T(128)S(6)} %copy.5.jb_ref.refs_5_), custom_call_target="tpu_custom_call" | custom-call | flops 900000000 | bytes 2400000 | tf_op jit(solution)/shard_map/local/pallas_call | solution.py:315
  12.8 0.0 collective-permute-done.1.xs_ref.refs_0_
  12.8 0.0 collective-permute-done.2._.refs_1_
  12.8 2.8 %collective-permute-done.3.xc_ref.refs_2_ = bf16[784,128]{1,0:T(8,128)(2,1)S(1)} collective-permute-done((bf16[784,128]{1,0:T(8,128)(2,1)S(1)}, bf16[784,128]{1,0:T(8,128)(2,1)S(1)}, u32[]{:S(2)}, u32[]{:S(2)}) %collective-permute-start.3) | collective-permute-done | bytes 200736 | tf_op jit(solution)/shard_map/ppermute | solution.py:310
  15.6 0.8 %early.1 = (f32[1024,256]{1,0:T(8,128)S(1)}, bf16[256,768]{1,0:T(8,128)(2,1)S(1)}) custom-call(bf16[6,3,128,128]{3,2,1,0:T(8,128)(2,1)S(1)} %get-tuple-element.29.own_ref, bf16[6,3,128,128]{3,2,1,0:T(8,128)(2,1)S(1)} %collective-permute-done._.other_ref, bf16[784,128]{1,0:T(8,128)(2,1)S(1)} %collective-permute-done.1.xs_ref.refs_0_, ...), custom_call_target="tpu_custom_call" | custom-call | flops 600000000 | bytes 2400000 | tf_op jit(solution)/shard_map/early/pallas_call | solution.py:332
  16.4 1.1 %collective-permute-done.4.refs_3_ = bf16[784,128]{1,0:T(8,128)(2,1)S(1)} collective-permute-done((bf16[784,128]{1,0:T(8,128)(2,1)S(1)}, bf16[784,128]{1,0:T(8,128)(2,1)S(1)}, u32[]{:S(2)}, u32[]{:S(2)}) %collective-permute-start.4) | collective-permute-done | bytes 200736 | tf_op jit(solution)/shard_map/ppermute | solution.py:311
  17.5 0.6 %cross.2 = (f32[2,2,4,32,128]{4,3,2,1,0:T(8,128)S(1)}, bf16[2,2,4,32,128]{4,3,2,1,0:T(8,128)(2,1)S(1)}, bf16[256,1536]{1,0:T(8,128)(2,1)S(1)}) custom-call(bf16[6,3,128,128]{3,2,1,0:T(8,128)(2,1)S(1)} %get-tuple-element.29.own_ref, bf16[6,3,128,128]{3,2,1,0:T(8,128)(2,1)S(1)} %collective-permute-done._.other_ref, ...), custom_call_target="tpu_custom_call" | custom-call | flops 900000000 | bytes 4000000 | tf_op jit(solution)/shard_map/cross/pallas_call | solution.py:354
  18.2 0.2 collective-permute-start.6
  18.3 0.6 %cross.3 = (f32[2,2,4,32,128]{4,3,2,1,0:T(8,128)S(1)}, bf16[2,2,4,32,128]{4,3,2,1,0:T(8,128)(2,1)S(1)}) custom-call(bf16[6,3,128,128]{3,2,1,0:T(8,128)(2,1)S(1)} %get-tuple-element.29.own_ref, bf16[6,3,128,128]{3,2,1,0:T(8,128)(2,1)S(1)} %collective-permute-done._.other_ref, bf16[784,128]{1,0:T(8,128)(2,1)S(1)} %collective-permute-done.1.xs_ref.refs_0_, ...), custom_call_target="tpu_custom_call" | custom-call | flops 900000000 | bytes 4000000 | tf_op jit(solution)/shard_map/cross/pallas_call | solution.py:354
  19.0 0.5 %collective-permute-start.5 = (bf16[2,2,4,32,128]{4,3,2,1,0:T(8,128)(2,1)S(1)}, bf16[2,2,4,32,128]{4,3,2,1,0:T(8,128)(2,1)S(1)}, u32[]{:S(2)}, u32[]{:S(2)}) collective-permute-start(bf16[2,2,4,32,128]{4,3,2,1,0:T(8,128)(2,1)S(1)} %get-tuple-element.44), channel_id=1, source_target_pairs={{0,1},{1,0},{2,3},{3,2},{4,5},{5,4},{6,7},{7,6},{8,9},{9,8},{10,11... | collective-permute-start | bytes 393224 | tf_op jit(solution)/shard_map/ppermute | solution.py:375
  19.5 0.1 collective-permute-done.6.got_ref
  19.6 0.9 %collective-permute-start.7 = (bf16[2,4,32,128]{3,2,1,0:T(8,128)(2,1)S(1)}, bf16[2,4,32,128]{3,2,1,0:T(8,128)(2,1)S(1)}, u32[]{:S(2)}, u32[]{:S(2)}) collective-permute-start(bf16[2,4,32,128]{3,2,1,0:T(8,128)(2,1)S(1)} %get-tuple-element.48), channel_id=1, source_target_pairs={{0,6},{2,4},{4,2},{6,0},{8,14},{10,12},{12,10},{14,8},{1,7},{3,5},... | collective-permute-start | bytes 196616 | tf_op jit(solution)/shard_map/ppermute | solution.py:391
  20.5 0.3 collective-permute-start.8
  20.8 0.0 collective-permute-done.5.got_ref
  20.8 2.5 %collective-permute-start.9 = (bf16[2,4,32,128]{3,2,1,0:T(8,128)(2,1)S(1)}, bf16[2,4,32,128]{3,2,1,0:T(8,128)(2,1)S(1)}, u32[]{:S(2)}, u32[]{:S(2)}) collective-permute-start(bf16[2,4,32,128]{3,2,1,0:T(8,128)(2,1)S(1)} %get-tuple-element.50), channel_id=1, source_target_pairs={{0,4},{2,6},{4,0},{6,2},{8,12},{10,14},{12,8},{14,10},{1,5},{3,7},... | collective-permute-start | bytes 196616 | tf_op jit(solution)/shard_map/ppermute | solution.py:391
  23.3 2.2 %collective-permute-done.7.refs_0_ = bf16[2,4,32,128]{3,2,1,0:T(8,128)(2,1)S(1)} collective-permute-done((bf16[2,4,32,128]{3,2,1,0:T(8,128)(2,1)S(1)}, bf16[2,4,32,128]{3,2,1,0:T(8,128)(2,1)S(1)}, u32[]{:S(2)}, u32[]{:S(2)}) %collective-permute-start.7) | collective-permute-done | bytes 65568 | tf_op jit(solution)/shard_map/ppermute | solution.py:391
  25.4 0.3 %collective-permute-done.8.refs_1_ = bf16[2,4,32,128]{3,2,1,0:T(8,128)(2,1)S(1)} collective-permute-done((bf16[2,4,32,128]{3,2,1,0:T(8,128)(2,1)S(1)}, bf16[2,4,32,128]{3,2,1,0:T(8,128)(2,1)S(1)}, u32[]{:S(2)}, u32[]{:S(2)}) %collective-permute-start.8) | collective-permute-done | bytes 65568 | tf_op jit(solution)/shard_map/ppermute | solution.py:391
  25.8 0.0 collective-permute-done.9.refs_2_
  25.8 1.5 %collective-permute-start.10 = (bf16[4,32,128]{2,1,0:T(8,128)(2,1)S(1)}, bf16[4,32,128]{2,1,0:T(8,128)(2,1)S(1)}, u32[]{:S(2)}, u32[]{:S(2)}) collective-permute-start(bf16[4,32,128]{2,1,0:T(8,128)(2,1)S(1)} %get-tuple-element.52), channel_id=1, source_target_pairs={{0,8},{2,10},{4,12},{6,14},{8,0},{10,2},{12,4},{14,6},{1,9},{3,11}... | collective-permute-start | bytes 98312 | tf_op jit(solution)/shard_map/ppermute | solution.py:402
  27.3 3.4 %collective-permute-done.10.got_ref = bf16[4,32,128]{2,1,0:T(8,128)(2,1)S(1)} collective-permute-done((bf16[4,32,128]{2,1,0:T(8,128)(2,1)S(1)}, bf16[4,32,128]{2,1,0:T(8,128)(2,1)S(1)}, u32[]{:S(2)}, u32[]{:S(2)}) %collective-permute-start.10) | collective-permute-done | bytes 32800 | tf_op jit(solution)/shard_map/ppermute | solution.py:402
  30.7 0.7 %total.1 = f32[32,4,128]{2,1,0:T(4,128)} custom-call(f32[4,32,128]{2,1,0:T(8,128)S(1)} %get-tuple-element.51.keep_ref, bf16[4,32,128]{2,1,0:T(8,128)(2,1)S(1)} %collective-permute-done.10.got_ref), custom_call_target="tpu_custom_call" | custom-call | tf_op jit(solution)/shard_map/total/pallas_call | solution.py:403
  (4 shorter events, 0.1 us)
Async XLA Ops:
  0.0 8.2 %copy-start.1 = (f32[16]{0:T(128)S(1)}, f32[16]{0:T(128)}, u32[]{:S(2)}) copy-start(f32[16]{0:T(128)} %param.6) | copy-start | bytes 196
  1.5 6.7 %collective-permute-start = (bf16[6,3,128,128]{3,2,1,0:T(8,128)(2,1)S(1)}, bf16[6,3,128,128]{3,2,1,0:T(8,128)(2,1)S(1)}, u32[]{:S(2)}, u32[]{:S(2)}) collective-permute-start(bf16[6,3,128,128]{3,2,1,0:T(8,128)(2,1)S(1)} %get-tuple-element.30), channel_id=1, source_target_pairs={{0,1},{1,0},{2,3},{3,2},{4,5},{5,4},{6,7},{7,6},{8,9},{9,8},{10,11... | collective-permute-start | bytes 1769480 | tf_op jit(solution)/shard_map/ppermute | solution.py:298
  2.0 10.8 %collective-permute-start.1 = (bf16[784,128]{1,0:T(8,128)(2,1)S(1)}, bf16[784,128]{1,0:T(8,128)(2,1)S(1)}, u32[]{:S(2)}, u32[]{:S(2)}) collective-permute-start(bf16[784,128]{1,0:T(8,128)(2,1)S(1)} %get-tuple-element.31), channel_id=1, source_target_pairs={{0,2},{1,3},{2,0},{3,1},{4,6},{5,7},{6,4},{7,5},{8,10},{9,11},{10,... | collective-permute-start | bytes 602120 | tf_op jit(solution)/shard_map/ppermute | solution.py:299
  4.6 3.6 %copy-start = (s32[1,8,128]{2,1,0:T(8,128)S(1)}, s32[1,8,128]{2,1,0:T(8,128)}, u32[]{:S(2)}) copy-start(s32[1,8,128]{2,1,0:T(8,128)} %ids_ref.1) | copy-start | bytes 12292
  4.6 8.2 %collective-permute-start.2 = (bf16[784,128]{1,0:T(8,128)(2,1)S(1)}, bf16[784,128]{1,0:T(8,128)(2,1)S(1)}, u32[]{:S(2)}, u32[]{:S(2)}) collective-permute-start(bf16[784,128]{1,0:T(8,128)(2,1)S(1)} %get-tuple-element.32), channel_id=1, source_target_pairs={{0,12},{1,13},{2,6},{3,7},{4,0},{5,1},{6,10},{7,11},{8,4},{9,5},{1... | collective-permute-start | bytes 602120 | tf_op jit(solution)/shard_map/ppermute | solution.py:300
  8.3 7.3 %collective-permute-start.3 = (bf16[784,128]{1,0:T(8,128)(2,1)S(1)}, bf16[784,128]{1,0:T(8,128)(2,1)S(1)}, u32[]{:S(2)}, u32[]{:S(2)}) collective-permute-start(bf16[784,128]{1,0:T(8,128)(2,1)S(1)} %get-tuple-element.35), channel_id=1, source_target_pairs={{0,3},{1,2},{2,1},{3,0},{4,7},{5,6},{6,5},{7,4},{8,11},{9,10},{10,... | collective-permute-start | bytes 602120 | tf_op jit(solution)/shard_map/ppermute | solution.py:310
  8.4 9.1 %collective-permute-start.4 = (bf16[784,128]{1,0:T(8,128)(2,1)S(1)}, bf16[784,128]{1,0:T(8,128)(2,1)S(1)}, u32[]{:S(2)}, u32[]{:S(2)}) collective-permute-start(bf16[784,128]{1,0:T(8,128)(2,1)S(1)} %get-tuple-element.36), channel_id=1, source_target_pairs={{2,7},{3,6},{4,1},{5,0},{6,11},{7,10},{8,5},{9,4},{10,15},{11,14},... | collective-permute-start | bytes 602120 | tf_op jit(solution)/shard_map/ppermute | solution.py:311
  18.2 1.4 %collective-permute-start.6 = (bf16[2,2,4,32,128]{4,3,2,1,0:T(8,128)(2,1)S(1)}, bf16[2,2,4,32,128]{4,3,2,1,0:T(8,128)(2,1)S(1)}, u32[]{:S(2)}, u32[]{:S(2)}) collective-permute-start(bf16[2,2,4,32,128]{4,3,2,1,0:T(8,128)(2,1)S(1)} %get-tuple-element.47), channel_id=1, source_target_pairs={{0,1},{1,0},{2,3},{3,2},{4,5},{5,4},{6,7},{7,6},{8,9},{9,8},{10,11... | collective-permute-start | bytes 393224 | tf_op jit(solution)/shard_map/ppermute | solution.py:373
  19.0 1.8 %collective-permute-start.5 = (bf16[2,2,4,32,128]{4,3,2,1,0:T(8,128)(2,1)S(1)}, bf16[2,2,4,32,128]{4,3,2,1,0:T(8,128)(2,1)S(1)}, u32[]{:S(2)}, u32[]{:S(2)}) collective-permute-start(bf16[2,2,4,32,128]{4,3,2,1,0:T(8,128)(2,1)S(1)} %get-tuple-element.44), channel_id=1, source_target_pairs={{0,1},{1,0},{2,3},{3,2},{4,5},{5,4},{6,7},{7,6},{8,9},{9,8},{10,11... | collective-permute-start | bytes 393224 | tf_op jit(solution)/shard_map/ppermute | solution.py:375
  19.6 5.8 %collective-permute-start.7 = (bf16[2,4,32,128]{3,2,1,0:T(8,128)(2,1)S(1)}, bf16[2,4,32,128]{3,2,1,0:T(8,128)(2,1)S(1)}, u32[]{:S(2)}, u32[]{:S(2)}) collective-permute-start(bf16[2,4,32,128]{3,2,1,0:T(8,128)(2,1)S(1)} %get-tuple-element.48), channel_id=1, source_target_pairs={{0,6},{2,4},{4,2},{6,0},{8,14},{10,12},{12,10},{14,8},{1,7},{3,5},... | collective-permute-start | bytes 196616 | tf_op jit(solution)/shard_map/ppermute | solution.py:391
  20.5 5.3 %collective-permute-start.8 = (bf16[2,4,32,128]{3,2,1,0:T(8,128)(2,1)S(1)}, bf16[2,4,32,128]{3,2,1,0:T(8,128)(2,1)S(1)}, u32[]{:S(2)}, u32[]{:S(2)}) collective-permute-start(bf16[2,4,32,128]{3,2,1,0:T(8,128)(2,1)S(1)} %get-tuple-element.49), channel_id=1, source_target_pairs={{0,2},{2,0},{4,6},{6,4},{8,10},{10,8},{12,14},{14,12},{1,3},{3,1},... | collective-permute-start | bytes 196616 | tf_op jit(solution)/shard_map/ppermute | solution.py:391
  20.8 5.0 %collective-permute-start.9 = (bf16[2,4,32,128]{3,2,1,0:T(8,128)(2,1)S(1)}, bf16[2,4,32,128]{3,2,1,0:T(8,128)(2,1)S(1)}, u32[]{:S(2)}, u32[]{:S(2)}) collective-permute-start(bf16[2,4,32,128]{3,2,1,0:T(8,128)(2,1)S(1)} %get-tuple-element.50), channel_id=1, source_target_pairs={{0,4},{2,6},{4,0},{6,2},{8,12},{10,14},{12,8},{14,10},{1,5},{3,7},... | collective-permute-start | bytes 196616 | tf_op jit(solution)/shard_map/ppermute | solution.py:391
  25.8 4.9 %collective-permute-start.10 = (bf16[4,32,128]{2,1,0:T(8,128)(2,1)S(1)}, bf16[4,32,128]{2,1,0:T(8,128)(2,1)S(1)}, u32[]{:S(2)}, u32[]{:S(2)}) collective-permute-start(bf16[4,32,128]{2,1,0:T(8,128)(2,1)S(1)} %get-tuple-element.52), channel_id=1, source_target_pairs={{0,8},{2,10},{4,12},{6,14},{8,0},{10,2},{12,4},{14,6},{1,9},{3,11}... | collective-permute-start | bytes 98312 | tf_op jit(solution)/shard_map/ppermute | solution.py:402

commit v14 on v13

--- a/solution.py
+++ b/solution.py
@@ -369,9 +369,9 @@
         def partners(*steps):
             return lambda s: [jnp.bitwise_xor(lax.rem(s, NEAR), step) for step in steps]
 
-        keep_a, send_a, w2 = crossed(2, partners(3, 1), ())
+        keep_a, send_a, w2 = crossed(2, partners(3, 2), ())
         got_a = lax.ppermute(send_a, "modes", swap)
-        keep_b, send_b = crossed(2, partners(0, 2), (w2,))
+        keep_b, send_b = crossed(2, partners(0, 1), (w2,))
         got_b = lax.ppermute(send_b, "modes", swap)
         piece = (JB, chunk, nk)
 
@@ -385,11 +385,11 @@
                 name="near",
             )(keep, got)
 
-        part_3, part_1 = summed((bf16, bf16), keep_a, got_a)
-        mine, part_2 = summed((f32, bf16), keep_b, got_b)
+        part_3, part_2 = summed((bf16, bf16), keep_a, got_a)
+        mine, part_1 = summed((f32, bf16), keep_b, got_b)
         parts = [
             lax.ppermute(part, "space", [(s, s ^ step) for s in range(n)])
-            for part, step in ((part_3, 3), (part_1, 1), (part_2, 2))
+            for part, step in ((part_3, 3), (part_2, 2), (part_1, 1))
         ]
         keep, send = pl.pallas_call(
             far_kernel,

time: 31.5 us -> 32.2 us (1.022)
  waiting for transfers between devices: 9.98 us -> 11.1 us
  starting transfers between devices: 13.8 us -> 13.4 us
    ppermute x1, waiting for transfers between devices: 3.39 us -> 4.12 us  [on_device(): got = lax.ppermute(send, 'space', [(s, s ^ NEAR) for s in range(n)])]
    ppermute x1, starting transfers between devices: 1.48 us -> 1.11 us  [on_device(): got = lax.ppermute(send, 'space', [(s, s ^ NEAR) for s in range(n)])]
    ppermute x3, waiting for transfers between devices: 2.51 us -> 2.86 us  [on_device(): lax.ppermute(part, 'space', [(s, s ^ step) for s in range(n)])]
where the time goes in v14:
time: 32.2 us; the launch traced here: 32.1 us
  starting transfers between devices  13.4 us (42%)
  waiting for transfers between devices  11.1 us (34%)
  Pallas kernels  6.84 us (21%)
  between operations  0.75 us (2%)
    ppermute x1, waiting for transfers between devices, on_device(): got = lax.ppermute(send, 'space', [(s, s ^ NEAR) for s in range(n)])  4.12 us
    ppermute x3, starting transfers between devices, on_device(): lax.ppermute(part, 'space', [(s, s ^ step) for s in range(n)])  3.62 us
    ppermute x1, starting transfers between devices, on_device(): zs = lax.ppermute(zs, both, same(z_pairs))  3.6 us
    ppermute x3, waiting for transfers between devices, on_device(): lax.ppermute(part, 'space', [(s, s ^ step) for s in range(n)])  2.86 us
    ppermute x1, waiting for transfers between devices, on_device(): xc = lax.ppermute(xc, both, cross(x_pairs))  2.8 us
    ppermute x1, starting transfers between devices, on_device(): xs = lax.ppermute(xs, both, same(x_pairs))  2.56 us
    pallas_call x1, Pallas kernels, on_device(): pl.pallas_call(local_kernel, out_shape=[jax.ShapeDtypeStruct((JB * 2 * nk...  2.43 us
    pallas_call x1, Pallas kernels, on_device(): pl.pallas_call(prep_kernel, out_shape=[jax.ShapeDtypeStruct((six, comps,...  1.47 us
  transfers between devices with their start and end apart: 11, of which 6 were waited for; matrix products, arithmetic and copies ran while one was open for 0% of the time, Pallas kernels for 13%

profile of v14, /device:TPU:0, one launch (start us, length us, event | category | flops | bytes accessed | tf_op | source)
XLA Modules:
  0.0 32.1 jit_solution(6521748486911057263)
XLA Ops:
  0.0 0.0 copy-start.1
  0.0 1.5 %prep.1 = (bf16[6,3,128,128]{3,2,1,0:T(8,128)(2,1)S(1)}, bf16[6,3,128,128]{3,2,1,0:T(8,128)(2,1)S(1)}, bf16[784,128]{1,0:T(8,128)(2,1)S(1)}, bf16[784,128]{1,0:T...) custom-call(bf16[128,3,1,8,128]{4,3,2,1,0:T(8,128)(2,1)} %modes_hbm.1), custom_call_target="tpu_custom_call" | custom-call | flops 1500000000 | bytes 2800000 | tf_op jit(solution)/shard_map/prep/pallas_call | solution.py:276
  1.5 0.5 %collective-permute-start = (bf16[6,3,128,128]{3,2,1,0:T(8,128)(2,1)S(1)}, bf16[6,3,128,128]{3,2,1,0:T(8,128)(2,1)S(1)}, u32[]{:S(2)}, u32[]{:S(2)}) collective-permute-start(bf16[6,3,128,128]{3,2,1,0:T(8,128)(2,1)S(1)} %get-tuple-element.30), channel_id=1, source_target_pairs={{0,1},{1,0},{2,3},{3,2},{4,5},{5,4},{6,7},{7,6},{8,9},{9,8},{10,11... | collective-permute-start | bytes 1769480 | tf_op jit(solution)/shard_map/ppermute | solution.py:298
  2.0 2.6 %collective-permute-start.1 = (bf16[784,128]{1,0:T(8,128)(2,1)S(1)}, bf16[784,128]{1,0:T(8,128)(2,1)S(1)}, u32[]{:S(2)}, u32[]{:S(2)}) collective-permute-start(bf16[784,128]{1,0:T(8,128)(2,1)S(1)} %get-tuple-element.31), channel_id=1, source_target_pairs={{0,2},{1,3},{2,0},{3,1},{4,6},{5,7},{6,4},{7,5},{8,10},{9,11},{10,... | collective-permute-start | bytes 602120 | tf_op jit(solution)/shard_map/ppermute | solution.py:299
  4.6 0.0 copy-start
  4.6 3.6 %collective-permute-start.2 = (bf16[784,128]{1,0:T(8,128)(2,1)S(1)}, bf16[784,128]{1,0:T(8,128)(2,1)S(1)}, u32[]{:S(2)}, u32[]{:S(2)}) collective-permute-start(bf16[784,128]{1,0:T(8,128)(2,1)S(1)} %get-tuple-element.32), channel_id=1, source_target_pairs={{0,12},{1,13},{2,6},{3,7},{4,0},{5,1},{6,10},{7,11},{8,4},{9,5},{1... | collective-permute-start | bytes 602120 | tf_op jit(solution)/shard_map/ppermute | solution.py:300
  8.2 0.0 collective-permute-done._.other_ref
  8.2 0.0 copy-done.1
  8.2 0.0 copy-done
  8.2 0.1 weights.1
  8.3 0.1 collective-permute-start.3
  8.4 1.3 %collective-permute-start.4 = (bf16[784,128]{1,0:T(8,128)(2,1)S(1)}, bf16[784,128]{1,0:T(8,128)(2,1)S(1)}, u32[]{:S(2)}, u32[]{:S(2)}) collective-permute-start(bf16[784,128]{1,0:T(8,128)(2,1)S(1)} %get-tuple-element.36), channel_id=1, source_target_pairs={{2,7},{3,6},{4,1},{5,0},{6,11},{7,10},{8,5},{9,4},{10,15},{11,14},... | collective-permute-start | bytes 602120 | tf_op jit(solution)/shard_map/ppermute | solution.py:311
  10.3 2.4 %local.1 = (f32[1024,256]{1,0:T(8,128)S(1)}, bf16[2,256,384]{2,1,0:T(8,128)(2,1)S(1)}) custom-call(bf16[6,3,128,128]{3,2,1,0:T(8,128)(2,1)S(1)} %get-tuple-element.29.own_ref, bf16[6,3,128,128]{3,2,1,0:T(8,128)(2,1)S(1)} %collective-permute-done._.other_ref, f32[8,128]{1,0:T(8,128)S(1)} %get-tuple-element.37.weight_ref, s32[1]{0:T(128)S(6)} %copy.5.jb_ref.refs_5_), custom_call_target="tpu_custom_call" | custom-call | flops 900000000 | bytes 2400000 | tf_op jit(solution)/shard_map/local/pallas_call | solution.py:315
  12.8 0.0 collective-permute-done.1.xs_ref.refs_0_
  12.8 0.0 collective-permute-done.2._.refs_1_
  12.8 2.8 %collective-permute-done.3.xc_ref.refs_2_ = bf16[784,128]{1,0:T(8,128)(2,1)S(1)} collective-permute-done((bf16[784,128]{1,0:T(8,128)(2,1)S(1)}, bf16[784,128]{1,0:T(8,128)(2,1)S(1)}, u32[]{:S(2)}, u32[]{:S(2)}) %collective-permute-start.3) | collective-permute-done | bytes 200736 | tf_op jit(solution)/shard_map/ppermute | solution.py:310
  15.6 0.8 %early.1 = (f32[1024,256]{1,0:T(8,128)S(1)}, bf16[256,768]{1,0:T(8,128)(2,1)S(1)}) custom-call(bf16[6,3,128,128]{3,2,1,0:T(8,128)(2,1)S(1)} %get-tuple-element.29.own_ref, bf16[6,3,128,128]{3,2,1,0:T(8,128)(2,1)S(1)} %collective-permute-done._.other_ref, bf16[784,128]{1,0:T(8,128)(2,1)S(1)} %collective-permute-done.1.xs_ref.refs_0_, ...), custom_call_target="tpu_custom_call" | custom-call | flops 600000000 | bytes 2400000 | tf_op jit(solution)/shard_map/early/pallas_call | solution.py:332
  16.4 1.1 %collective-permute-done.4.refs_3_ = bf16[784,128]{1,0:T(8,128)(2,1)S(1)} collective-permute-done((bf16[784,128]{1,0:T(8,128)(2,1)S(1)}, bf16[784,128]{1,0:T(8,128)(2,1)S(1)}, u32[]{:S(2)}, u32[]{:S(2)}) %collective-permute-start.4) | collective-permute-done | bytes 200736 | tf_op jit(solution)/shard_map/ppermute | solution.py:311
  17.5 0.6 %cross.2 = (f32[2,2,4,32,128]{4,3,2,1,0:T(8,128)S(1)}, bf16[2,2,4,32,128]{4,3,2,1,0:T(8,128)(2,1)S(1)}, bf16[256,1536]{1,0:T(8,128)(2,1)S(1)}) custom-call(bf16[6,3,128,128]{3,2,1,0:T(8,128)(2,1)S(1)} %get-tuple-element.29.own_ref, bf16[6,3,128,128]{3,2,1,0:T(8,128)(2,1)S(1)} %collective-permute-done._.other_ref, ...), custom_call_target="tpu_custom_call" | custom-call | flops 900000000 | bytes 4000000 | tf_op jit(solution)/shard_map/cross/pallas_call | solution.py:354
  18.2 0.2 collective-permute-start.6
  18.3 0.6 %cross.3 = (f32[2,2,4,32,128]{4,3,2,1,0:T(8,128)S(1)}, bf16[2,2,4,32,128]{4,3,2,1,0:T(8,128)(2,1)S(1)}) custom-call(bf16[6,3,128,128]{3,2,1,0:T(8,128)(2,1)S(1)} %get-tuple-element.29.own_ref, bf16[6,3,128,128]{3,2,1,0:T(8,128)(2,1)S(1)} %collective-permute-done._.other_ref, bf16[784,128]{1,0:T(8,128)(2,1)S(1)} %collective-permute-done.1.xs_ref.refs_0_, ...), custom_call_target="tpu_custom_call" | custom-call | flops 900000000 | bytes 4000000 | tf_op jit(solution)/shard_map/cross/pallas_call | solution.py:354
  19.0 0.5 %collective-permute-start.5 = (bf16[2,2,4,32,128]{4,3,2,1,0:T(8,128)(2,1)S(1)}, bf16[2,2,4,32,128]{4,3,2,1,0:T(8,128)(2,1)S(1)}, u32[]{:S(2)}, u32[]{:S(2)}) collective-permute-start(bf16[2,2,4,32,128]{4,3,2,1,0:T(8,128)(2,1)S(1)} %get-tuple-element.44), channel_id=1, source_target_pairs={{0,1},{1,0},{2,3},{3,2},{4,5},{5,4},{6,7},{7,6},{8,9},{9,8},{10,11... | collective-permute-start | bytes 393224 | tf_op jit(solution)/shard_map/ppermute | solution.py:375
  19.5 0.1 collective-permute-done.6.got_ref
  19.6 0.9 %collective-permute-start.7 = (bf16[2,4,32,128]{3,2,1,0:T(8,128)(2,1)S(1)}, bf16[2,4,32,128]{3,2,1,0:T(8,128)(2,1)S(1)}, u32[]{:S(2)}, u32[]{:S(2)}) collective-permute-start(bf16[2,4,32,128]{3,2,1,0:T(8,128)(2,1)S(1)} %get-tuple-element.48), channel_id=1, source_target_pairs={{0,6},{2,4},{4,2},{6,0},{8,14},{10,12},{12,10},{14,8},{1,7},{3,5},... | collective-permute-start | bytes 196616 | tf_op jit(solution)/shard_map/ppermute | solution.py:391
  20.5 0.0 collective-permute-start.8
  20.5 0.0 collective-permute-done.5.got_ref
  20.5 2.7 %collective-permute-start.9 = (bf16[2,4,32,128]{3,2,1,0:T(8,128)(2,1)S(1)}, bf16[2,4,32,128]{3,2,1,0:T(8,128)(2,1)S(1)}, u32[]{:S(2)}, u32[]{:S(2)}) collective-permute-start(bf16[2,4,32,128]{3,2,1,0:T(8,128)(2,1)S(1)} %get-tuple-element.50), channel_id=1, source_target_pairs={{0,2},{2,0},{4,6},{6,4},{8,10},{10,8},{12,14},{14,12},{1,3},{3,1},... | collective-permute-start | bytes 196616 | tf_op jit(solution)/shard_map/ppermute | solution.py:391
  23.3 2.2 %collective-permute-done.7.refs_0_ = bf16[2,4,32,128]{3,2,1,0:T(8,128)(2,1)S(1)} collective-permute-done((bf16[2,4,32,128]{3,2,1,0:T(8,128)(2,1)S(1)}, bf16[2,4,32,128]{3,2,1,0:T(8,128)(2,1)S(1)}, u32[]{:S(2)}, u32[]{:S(2)}) %collective-permute-start.7) | collective-permute-done | bytes 65568 | tf_op jit(solution)/shard_map/ppermute | solution.py:391
  25.4 0.0 collective-permute-done.8.refs_1_
  25.4 0.7 %collective-permute-done.9.refs_2_ = bf16[2,4,32,128]{3,2,1,0:T(8,128)(2,1)S(1)} collective-permute-done((bf16[2,4,32,128]{3,2,1,0:T(8,128)(2,1)S(1)}, bf16[2,4,32,128]{3,2,1,0:T(8,128)(2,1)S(1)}, u32[]{:S(2)}, u32[]{:S(2)}) %collective-permute-start.9) | collective-permute-done | bytes 65568 | tf_op jit(solution)/shard_map/ppermute | solution.py:391
  26.2 1.1 %collective-permute-start.10 = (bf16[4,32,128]{2,1,0:T(8,128)(2,1)S(1)}, bf16[4,32,128]{2,1,0:T(8,128)(2,1)S(1)}, u32[]{:S(2)}, u32[]{:S(2)}) collective-permute-start(bf16[4,32,128]{2,1,0:T(8,128)(2,1)S(1)} %get-tuple-element.52), channel_id=1, source_target_pairs={{0,8},{2,10},{4,12},{6,14},{8,0},{10,2},{12,4},{14,6},{1,9},{3,11}... | collective-permute-start | bytes 98312 | tf_op jit(solution)/shard_map/ppermute | solution.py:402
  27.3 4.1 %collective-permute-done.10.got_ref = bf16[4,32,128]{2,1,0:T(8,128)(2,1)S(1)} collective-permute-done((bf16[4,32,128]{2,1,0:T(8,128)(2,1)S(1)}, bf16[4,32,128]{2,1,0:T(8,128)(2,1)S(1)}, u32[]{:S(2)}, u32[]{:S(2)}) %collective-permute-start.10) | collective-permute-done | bytes 32800 | tf_op jit(solution)/shard_map/ppermute | solution.py:402
  31.4 0.7 %total.1 = f32[32,4,128]{2,1,0:T(4,128)} custom-call(f32[4,32,128]{2,1,0:T(8,128)S(1)} %get-tuple-element.51.keep_ref, bf16[4,32,128]{2,1,0:T(8,128)(2,1)S(1)} %collective-permute-done.10.got_ref), custom_call_target="tpu_custom_call" | custom-call | tf_op jit(solution)/shard_map/total/pallas_call | solution.py:403
  (4 shorter events, 0.1 us)
Async XLA Ops:
  0.0 8.2 %copy-start.1 = (f32[16]{0:T(128)S(1)}, f32[16]{0:T(128)}, u32[]{:S(2)}) copy-start(f32[16]{0:T(128)} %param.6) | copy-start | bytes 196
  1.5 6.7 %collective-permute-start = (bf16[6,3,128,128]{3,2,1,0:T(8,128)(2,1)S(1)}, bf16[6,3,128,128]{3,2,1,0:T(8,128)(2,1)S(1)}, u32[]{:S(2)}, u32[]{:S(2)}) collective-permute-start(bf16[6,3,128,128]{3,2,1,0:T(8,128)(2,1)S(1)} %get-tuple-element.30), channel_id=1, source_target_pairs={{0,1},{1,0},{2,3},{3,2},{4,5},{5,4},{6,7},{7,6},{8,9},{9,8},{10,11... | collective-permute-start | bytes 1769480 | tf_op jit(solution)/shard_map/ppermute | solution.py:298
  2.0 10.8 %collective-permute-start.1 = (bf16[784,128]{1,0:T(8,128)(2,1)S(1)}, bf16[784,128]{1,0:T(8,128)(2,1)S(1)}, u32[]{:S(2)}, u32[]{:S(2)}) collective-permute-start(bf16[784,128]{1,0:T(8,128)(2,1)S(1)} %get-tuple-element.31), channel_id=1, source_target_pairs={{0,2},{1,3},{2,0},{3,1},{4,6},{5,7},{6,4},{7,5},{8,10},{9,11},{10,... | collective-permute-start | bytes 602120 | tf_op jit(solution)/shard_map/ppermute | solution.py:299
  4.6 3.6 %copy-start = (s32[1,8,128]{2,1,0:T(8,128)S(1)}, s32[1,8,128]{2,1,0:T(8,128)}, u32[]{:S(2)}) copy-start(s32[1,8,128]{2,1,0:T(8,128)} %ids_ref.1) | copy-start | bytes 12292
  4.6 8.2 %collective-permute-start.2 = (bf16[784,128]{1,0:T(8,128)(2,1)S(1)}, bf16[784,128]{1,0:T(8,128)(2,1)S(1)}, u32[]{:S(2)}, u32[]{:S(2)}) collective-permute-start(bf16[784,128]{1,0:T(8,128)(2,1)S(1)} %get-tuple-element.32), channel_id=1, source_target_pairs={{0,12},{1,13},{2,6},{3,7},{4,0},{5,1},{6,10},{7,11},{8,4},{9,5},{1... | collective-permute-start | bytes 602120 | tf_op jit(solution)/shard_map/ppermute | solution.py:300
  8.3 7.3 %collective-permute-start.3 = (bf16[784,128]{1,0:T(8,128)(2,1)S(1)}, bf16[784,128]{1,0:T(8,128)(2,1)S(1)}, u32[]{:S(2)}, u32[]{:S(2)}) collective-permute-start(bf16[784,128]{1,0:T(8,128)(2,1)S(1)} %get-tuple-element.35), channel_id=1, source_target_pairs={{0,3},{1,2},{2,1},{3,0},{4,7},{5,6},{6,5},{7,4},{8,11},{9,10},{10,... | collective-permute-start | bytes 602120 | tf_op jit(solution)/shard_map/ppermute | solution.py:310
  8.4 9.1 %collective-permute-start.4 = (bf16[784,128]{1,0:T(8,128)(2,1)S(1)}, bf16[784,128]{1,0:T(8,128)(2,1)S(1)}, u32[]{:S(2)}, u32[]{:S(2)}) collective-permute-start(bf16[784,128]{1,0:T(8,128)(2,1)S(1)} %get-tuple-element.36), channel_id=1, source_target_pairs={{2,7},{3,6},{4,1},{5,0},{6,11},{7,10},{8,5},{9,4},{10,15},{11,14},... | collective-permute-start | bytes 602120 | tf_op jit(solution)/shard_map/ppermute | solution.py:311
  18.2 1.4 %collective-permute-start.6 = (bf16[2,2,4,32,128]{4,3,2,1,0:T(8,128)(2,1)S(1)}, bf16[2,2,4,32,128]{4,3,2,1,0:T(8,128)(2,1)S(1)}, u32[]{:S(2)}, u32[]{:S(2)}) collective-permute-start(bf16[2,2,4,32,128]{4,3,2,1,0:T(8,128)(2,1)S(1)} %get-tuple-element.47), channel_id=1, source_target_pairs={{0,1},{1,0},{2,3},{3,2},{4,5},{5,4},{6,7},{7,6},{8,9},{9,8},{10,11... | collective-permute-start | bytes 393224 | tf_op jit(solution)/shard_map/ppermute | solution.py:373
  19.0 1.5 %collective-permute-start.5 = (bf16[2,2,4,32,128]{4,3,2,1,0:T(8,128)(2,1)S(1)}, bf16[2,2,4,32,128]{4,3,2,1,0:T(8,128)(2,1)S(1)}, u32[]{:S(2)}, u32[]{:S(2)}) collective-permute-start(bf16[2,2,4,32,128]{4,3,2,1,0:T(8,128)(2,1)S(1)} %get-tuple-element.44), channel_id=1, source_target_pairs={{0,1},{1,0},{2,3},{3,2},{4,5},{5,4},{6,7},{7,6},{8,9},{9,8},{10,11... | collective-permute-start | bytes 393224 | tf_op jit(solution)/shard_map/ppermute | solution.py:375
  19.6 5.8 %collective-permute-start.7 = (bf16[2,4,32,128]{3,2,1,0:T(8,128)(2,1)S(1)}, bf16[2,4,32,128]{3,2,1,0:T(8,128)(2,1)S(1)}, u32[]{:S(2)}, u32[]{:S(2)}) collective-permute-start(bf16[2,4,32,128]{3,2,1,0:T(8,128)(2,1)S(1)} %get-tuple-element.48), channel_id=1, source_target_pairs={{0,6},{2,4},{4,2},{6,0},{8,14},{10,12},{12,10},{14,8},{1,7},{3,5},... | collective-permute-start | bytes 196616 | tf_op jit(solution)/shard_map/ppermute | solution.py:391
  20.5 4.9 %collective-permute-start.8 = (bf16[2,4,32,128]{3,2,1,0:T(8,128)(2,1)S(1)}, bf16[2,4,32,128]{3,2,1,0:T(8,128)(2,1)S(1)}, u32[]{:S(2)}, u32[]{:S(2)}) collective-permute-start(bf16[2,4,32,128]{3,2,1,0:T(8,128)(2,1)S(1)} %get-tuple-element.49), channel_id=1, source_target_pairs={{0,4},{2,6},{4,0},{6,2},{8,12},{10,14},{12,8},{14,10},{1,5},{3,7},... | collective-permute-start | bytes 196616 | tf_op jit(solution)/shard_map/ppermute | solution.py:391
  20.5 5.6 %collective-permute-start.9 = (bf16[2,4,32,128]{3,2,1,0:T(8,128)(2,1)S(1)}, bf16[2,4,32,128]{3,2,1,0:T(8,128)(2,1)S(1)}, u32[]{:S(2)}, u32[]{:S(2)}) collective-permute-start(bf16[2,4,32,128]{3,2,1,0:T(8,128)(2,1)S(1)} %get-tuple-element.50), channel_id=1, source_target_pairs={{0,2},{2,0},{4,6},{6,4},{8,10},{10,8},{12,14},{14,12},{1,3},{3,1},... | collective-permute-start | bytes 196616 | tf_op jit(solution)/shard_map/ppermute | solution.py:391
  26.2 5.2 %collective-permute-start.10 = (bf16[4,32,128]{2,1,0:T(8,128)(2,1)S(1)}, bf16[4,32,128]{2,1,0:T(8,128)(2,1)S(1)}, u32[]{:S(2)}, u32[]{:S(2)}) collective-permute-start(bf16[4,32,128]{2,1,0:T(8,128)(2,1)S(1)} %get-tuple-element.52), channel_id=1, source_target_pairs={{0,8},{2,10},{4,12},{6,14},{8,0},{10,2},{12,4},{14,6},{1,9},{3,11}... | collective-permute-start | bytes 98312 | tf_op jit(solution)/shard_map/ppermute | solution.py:402

commit v15 on v13

--- a/solution.py
+++ b/solution.py
@@ -13,10 +13,17 @@
 LOADS = 4
 NEAR = 4
 VMEM_LIMIT = 48 * 1024 * 1024
-PREP_LIMIT = 53_100 * 1024
-
-
-def prep_kernel(modes_hbm, own_ref, core_ref, xs_ref, zs_ref, xc_ref, zc_ref, modes_ref, tr, sems):
+PREP_LIMIT = 53_600 * 1024
+
+
+def copy_rows(ref, tr, at):
+    nx, comps, nk, _ = tr.shape
+    for row in range(nx // 4):
+        for c in range(comps):
+            ref[pl.ds((row * comps + c) * nk, nk), :] = tr[at * (nx // 4) + row, c]
+
+
+def prep_kernel(modes_hbm, tr, xs_ref, zs_ref, modes_ref, sems):
     m = lax.axis_index("modes")
     q = lax.rem(lax.axis_index("space"), 2)
     nk, comps, _, nx, nz = modes_hbm.shape
@@ -35,37 +42,24 @@
         for c in range(comps):
             value = modes_ref[block, c, 0].astype(jnp.float32)
             tr[:, c, block] = jnp.swapaxes(value, 0, 1).astype(jnp.bfloat16)
-    quarter = nx // 4
-    for r in range(nx // 2 + 2):
-        own_ref[r] = tr[lax.rem(nx // 2 * m + nx - 1 + r, nx)]
-        core_ref[r] = tr[lax.rem(nx // 2 * (1 - m) + nx - 1 + r, nx)]
-    for ref, at in (
-        (xs_ref, 2 * m + 1 - q),
-        (xc_ref, 2 * (1 - m) + 1 - q),
-        (zs_ref, 2 * m + q),
-        (zc_ref, 2 * (1 - m) + q),
-    ):
-        for row in range(quarter):
-            for c in range(comps):
-                ref[pl.ds((row * comps + c) * nk, nk), :] = tr[at * quarter + row, c]
-    for ref in (zs_ref, xs_ref):
-        pad = ref.shape[0] - quarter * comps * nk
-        ref[pl.ds(quarter * comps * nk, pad), :] = jnp.zeros((pad, nz), jnp.bfloat16)
-
-
-def weights_kernel(ids_ref, table_ref, xc_ref, zc_ref, _, weight_ref, xc_out, zc_out):
+    body = nx // 4 * comps * nk
+    for ref, at in ((xs_ref, 2 * m + 1 - q), (zs_ref, 2 * m + q)):
+        copy_rows(ref, tr, at)
+        ref[pl.ds(body, PADROWS), :] = jnp.zeros((PADROWS, nz), jnp.bfloat16)
+
+
+def weights_kernel(ids_ref, table_ref, tr, _, weight_ref, xc_ref, zc_ref):
     m = lax.axis_index("modes")
     q = lax.rem(lax.axis_index("space"), 2)
-    body, nz = xc_ref.shape
-    nx = ids_ref.shape[1]
+    nx, comps, nk, nz = tr.shape
     quarter = nx // 4
     table = table_ref[...]
     weight = jnp.zeros((nx, nz), jnp.float32)
     for entry in range(NW):
         weight = jnp.where(ids_ref[0] == entry, table[0:1, entry : entry + 1], weight)
     weight_ref[...] = weight
-    for ref, out, at in ((zc_ref, zc_out, 2 * (1 - m) + q), (xc_ref, xc_out, 2 * (1 - m) + 1 - q)):
-        out[pl.ds(0, body), :] = ref[...]
+    for ref, at in ((xc_ref, 2 * (1 - m) + 1 - q), (zc_ref, 2 * (1 - m) + q)):
+        copy_rows(ref, tr, at)
         rest = jnp.concatenate(
             [
                 jnp.broadcast_to(weight_ref[pl.ds(at * quarter + row, 1), :], (8, nz))
@@ -79,7 +73,7 @@
             rounded = rest.astype(jnp.bfloat16).astype(jnp.float32)
             pieces = jnp.where(piece_of == piece, rounded, pieces)
             rest = rest - rounded
-        out[pl.ds(body, 8 * quarter), :] = pieces.astype(jnp.bfloat16)
+        ref[pl.ds(quarter * comps * nk, 8 * quarter), :] = pieces.astype(jnp.bfloat16)
 
 
 def received_weights(ref, first, quarter):
@@ -125,17 +119,19 @@
 def local_kernel(own_ref, other_ref, weight_ref, jb_ref, acc_ref, w0_ref, adv, wts):
     m = lax.axis_index("modes")
     q = lax.rem(lax.axis_index("space"), 2)
-    rows, comps, nk, nz = own_ref.shape
-    rows -= 2
+    nx, comps, nk, nz = own_ref.shape
+    rows = nx // 2
     pick = picks(jb_ref, m, nk)
     for r in range(rows):
-        phi = [picked(pick, own_ref.at[r + 1, d], other_ref.at[r + 1, d]) for d in range(comps)]
-        weight = weight_ref[pl.ds(rows * m + r, 1), :]
+        row = rows * m + r
+        below, above = lax.rem(row + nx - 1, nx), lax.rem(row + 1, nx)
+        phi = [picked(pick, own_ref.at[row, d], other_ref.at[row, d]) for d in range(comps)]
+        weight = weight_ref[pl.ds(row, 1), :]
         for c in range(comps):
             for half, ref in enumerate((own_ref, other_ref)):
                 block = pl.ds(half * nk, nk)
-                here = ref[r + 1, c].astype(jnp.float32)
-                gx = 0.5 * (ref[r + 2, c].astype(jnp.float32) - ref[r, c].astype(jnp.float32))
+                here = ref[row, c].astype(jnp.float32)
+                gx = 0.5 * (ref[above, c].astype(jnp.float32) - ref[below, c].astype(jnp.float32))
                 gz = 0.5 * (pltpu.roll(here, nz - 1, 1) - pltpu.roll(here, 1, 1))
                 gx = gx.astype(jnp.bfloat16).astype(jnp.float32)
                 gz = gz.astype(jnp.bfloat16).astype(jnp.float32)
@@ -159,12 +155,12 @@
 def early_kernel(own_ref, other_ref, xs_ref, _, xc_ref, w0_ref, jb_ref, acc_ref, out_ref, w1_ref, adv):
     m = lax.axis_index("modes")
     q = lax.rem(lax.axis_index("space"), 2)
-    rows, comps, nk, nz = own_ref.shape
-    quarter = (rows - 2) // 2
+    nx, comps, nk, nz = own_ref.shape
+    quarter = nx // 4
     pick = picks(jb_ref, m, nk)
     weights = received_weights(xc_ref, quarter * comps * nk, quarter)
     for r in range(quarter):
-        row0 = 1 + quarter * q + r
+        row0 = quarter * (2 * m + q) + r
         phi0 = sign_of_plane() * picked(pick, own_ref.at[row0, 1], other_ref.at[row0, 1])
         phi0 = [spread(phi0[j : j + 1]) for j in range(JB)]
         for c in range(comps):
@@ -193,8 +189,8 @@
     plane = lax.axis_index("space")
     q = lax.rem(plane, 2)
     inside = jnp.where(jnp.logical_or(plane == 1, plane == planes - 2), 0.0, 1.0)
-    rows, comps, nk, nz = own_ref.shape
-    quarter = (rows - 2) // 2
+    nx, comps, nk, nz = own_ref.shape
+    quarter = nx // 4
     span = quarter * comps * nz
     pick = picks(jb_ref, m, nk)
     classes = [pl.multiple_of(chunk * cls, chunk) for cls in classes_of(plane)]
@@ -218,7 +214,7 @@
     inside = inside.astype(jnp.bfloat16)
     for at, cls in enumerate(classes):
         for r in range(quarter):
-            row0 = 1 + quarter * q + r
+            row0 = quarter * (2 * m + q) + r
             phi1, phi2 = phis[r]
             for c in range(comps):
                 lane = (r * comps + c) * nz
@@ -270,21 +266,15 @@
     vmem = pl.BlockSpec(memory_space=pltpu.VMEM)
     smem = pl.BlockSpec(memory_space=pltpu.SMEM)
     params = pltpu.CompilerParams(vmem_limit_bytes=VMEM_LIMIT)
-    six = nx // 2 + 2
     quarter = nx // 4
     body = quarter * comps * nk
-    own, to_core, xs, zs, xc, zc = pl.pallas_call(
+    own, xs, zs = pl.pallas_call(
         prep_kernel,
-        out_shape=[jax.ShapeDtypeStruct((six, comps, nk, nz), bf16)] * 2
-        + [jax.ShapeDtypeStruct((body + PADROWS, nz), bf16)] * 2
-        + [jax.ShapeDtypeStruct((body, nz), bf16)] * 2,
+        out_shape=[jax.ShapeDtypeStruct((nx, comps, nk, nz), bf16)]
+        + [jax.ShapeDtypeStruct((body + PADROWS, nz), bf16)] * 2,
         in_specs=[pl.BlockSpec(memory_space=pltpu.HBM)],
-        out_specs=[vmem] * 6,
-        scratch_shapes=[
-            pltpu.VMEM(modes.shape, bf16),
-            pltpu.VMEM((nx, comps, nk, nz), bf16),
-            pltpu.SemaphoreType.DMA((LOADS,)),
-        ],
+        out_specs=[vmem] * 3,
+        scratch_shapes=[pltpu.VMEM(modes.shape, bf16), pltpu.SemaphoreType.DMA((LOADS,))],
         compiler_params=pltpu.CompilerParams(vmem_limit_bytes=PREP_LIMIT),
         cost_estimate=pl.CostEstimate(flops=1_500_000_000, bytes_accessed=2_800_000, transcendentals=0),
         name="prep",
@@ -295,18 +285,18 @@
     z_pairs = [(s, (s + (2 if s % 2 else -2)) % n) for s in range(n)]
     same = lambda pairs: [(2 * a + m, 2 * b + m) for a, b in pairs for m in range(2)]
     cross = lambda pairs: [(2 * a + m, 2 * b + 1 - m) for a, b in pairs for m in range(2)]
-    other = lax.ppermute(to_core, "modes", [(0, 1), (1, 0)])
+    other = lax.ppermute(own, "modes", [(0, 1), (1, 0)])
     xs = lax.ppermute(xs, both, same(x_pairs))
     zs = lax.ppermute(zs, both, same(z_pairs))
     weight, xc, zc = pl.pallas_call(
         weights_kernel,
         out_shape=[jax.ShapeDtypeStruct((nx, nz), f32)]
         + [jax.ShapeDtypeStruct((body + 8 * quarter, nz), bf16)] * 2,
-        in_specs=[vmem] * 4 + [pl.BlockSpec(memory_space=pl.ANY)],
+        in_specs=[vmem] * 3 + [pl.BlockSpec(memory_space=pl.ANY)],
         out_specs=[vmem] * 3,
         compiler_params=params,
         name="weights",
-    )(weight_ids, jnp.broadcast_to(weight_table[None], (8, NW)), xc, zc, other)
+    )(weight_ids, jnp.broadcast_to(weight_table[None], (8, NW)), own, other)
     xc = lax.ppermute(xc, both, cross(x_pairs))
     zc = lax.ppermute(zc, both, cross([(s, to) for s, to in z_pairs if abs(s - to) == 2]))
 

time: 31.5 us -> 31.4 us (level)
  no operation moved by 1% of the time
where the time goes in v15:
time: 31.4 us; the launch traced here: 31.3 us
  starting transfers between devices  13.8 us (44%)
  waiting for transfers between devices  9.98 us (32%)
  Pallas kernels  6.73 us (21%)
  between operations  0.76 us (2%)
    ppermute x3, starting transfers between devices, on_device(): lax.ppermute(part, 'space', [(s, s ^ step) for s in range(n)])  3.62 us
    ppermute x1, starting transfers between devices, on_device(): zs = lax.ppermute(zs, both, same(z_pairs))  3.6 us
    ppermute x1, waiting for transfers between devices, on_device(): got = lax.ppermute(send, 'space', [(s, s ^ NEAR) for s in range(n)])  3.4 us
    ppermute x1, waiting for transfers between devices, on_device(): xc = lax.ppermute(xc, both, cross(x_pairs))  2.8 us
    ppermute x1, starting transfers between devices, on_device(): xs = lax.ppermute(xs, both, same(x_pairs))  2.56 us
    ppermute x3, waiting for transfers between devices, on_device(): lax.ppermute(part, 'space', [(s, s ^ step) for s in range(n)])  2.51 us
    pallas_call x1, Pallas kernels, on_device(): pl.pallas_call(local_kernel, out_shape=[jax.ShapeDtypeStruct((JB * 2 * nk...  2.44 us
    ppermute x1, starting transfers between devices, on_device(): got = lax.ppermute(send, 'space', [(s, s ^ NEAR) for s in range(n)])  1.48 us
  transfers between devices with their start and end apart: 11, of which 6 were waited for; matrix products, arithmetic and copies ran while one was open for 0% of the time, Pallas kernels for 13%

profile of v15, /device:TPU:0, one launch (start us, length us, event | category | flops | bytes accessed | tf_op | source)
XLA Modules:
  0.0 31.3 jit_solution(1702389180643728392)
XLA Ops:
  0.0 0.0 copy-start.1
  0.0 1.4 %prep.1 = (bf16[8,3,128,128]{3,2,1,0:T(8,128)(2,1)S(1)}, bf16[784,128]{1,0:T(8,128)(2,1)S(1)}, bf16[784,128]{1,0:T(8,128)(2,1)S(1)}) custom-call(bf16[128,3,1,8,128]{4,3,2,1,0:T(8,128)(2,1)} %modes_hbm.1), custom_call_target="tpu_custom_call" | custom-call | flops 1500000000 | bytes 2800000 | tf_op jit(solution)/shard_map/prep/pallas_call | solution.py:271
  1.4 0.0 copy-start
  1.4 0.5 %collective-permute-start = (bf16[8,3,128,128]{3,2,1,0:T(8,128)(2,1)S(1)}, bf16[8,3,128,128]{3,2,1,0:T(8,128)(2,1)S(1)}, u32[]{:S(2)}, u32[]{:S(2)}) collective-permute-start(bf16[8,3,128,128]{3,2,1,0:T(8,128)(2,1)S(1)} %get-tuple-element.26.tr.own_ref), channel_id=1, source_target_pairs={{0,1},{1,0},{2,3},{3,2},{4,5},{5,4},{6,7},{7,6},{8,9},{9,8},{10,11... | collective-permute-start | bytes 2359304 | tf_op jit(solution)/shard_map/ppermute | solution.py:288
  1.9 2.6 %collective-permute-start.1 = (bf16[784,128]{1,0:T(8,128)(2,1)S(1)}, bf16[784,128]{1,0:T(8,128)(2,1)S(1)}, u32[]{:S(2)}, u32[]{:S(2)}) collective-permute-start(bf16[784,128]{1,0:T(8,128)(2,1)S(1)} %get-tuple-element.27), channel_id=1, source_target_pairs={{0,2},{1,3},{2,0},{3,1},{4,6},{5,7},{6,4},{7,5},{8,10},{9,11},{10,... | collective-permute-start | bytes 602120 | tf_op jit(solution)/shard_map/ppermute | solution.py:289
  4.5 3.6 %collective-permute-start.2 = (bf16[784,128]{1,0:T(8,128)(2,1)S(1)}, bf16[784,128]{1,0:T(8,128)(2,1)S(1)}, u32[]{:S(2)}, u32[]{:S(2)}) collective-permute-start(bf16[784,128]{1,0:T(8,128)(2,1)S(1)} %get-tuple-element.28), channel_id=1, source_target_pairs={{0,12},{1,13},{2,6},{3,7},{4,0},{5,1},{6,10},{7,11},{8,4},{9,5},{1... | collective-permute-start | bytes 602120 | tf_op jit(solution)/shard_map/ppermute | solution.py:290
  8.1 0.0 collective-permute-done._.other_ref
  8.1 0.0 copy-done.1
  8.1 0.0 copy-done
  8.1 0.1 weights.1
  8.2 0.1 collective-permute-start.3
  8.3 1.3 %collective-permute-start.4 = (bf16[784,128]{1,0:T(8,128)(2,1)S(1)}, bf16[784,128]{1,0:T(8,128)(2,1)S(1)}, u32[]{:S(2)}, u32[]{:S(2)}) collective-permute-start(bf16[784,128]{1,0:T(8,128)(2,1)S(1)} %get-tuple-element.30), channel_id=1, source_target_pairs={{2,7},{3,6},{4,1},{5,0},{6,11},{7,10},{8,5},{9,4},{10,15},{11,14},... | collective-permute-start | bytes 602120 | tf_op jit(solution)/shard_map/ppermute | solution.py:301
  10.3 2.4 %local.1 = (f32[1024,256]{1,0:T(8,128)S(1)}, bf16[2,256,384]{2,1,0:T(8,128)(2,1)S(1)}) custom-call(bf16[8,3,128,128]{3,2,1,0:T(8,128)(2,1)S(1)} %get-tuple-element.26.tr.own_ref, bf16[8,3,128,128]{3,2,1,0:T(8,128)(2,1)S(1)} %collective-permute-done._.other_ref, f32[8,128]{1,0:T(8,128)S(1)} %get-tuple-element.31.weight_ref, s32[1]{0:T(128)S(6)} %copy.5.jb_ref.refs_5_), custom_call_target="tpu_custom_call" | custom-call | flops 900000000 | bytes 2400000 | tf_op jit(solution)/shard_map/local/pallas_call | solution.py:305
  12.7 0.0 collective-permute-done.1.xs_ref.refs_0_
  12.7 0.0 collective-permute-done.2._.refs_1_
  12.7 2.8 %collective-permute-done.3.xc_ref.refs_2_ = bf16[784,128]{1,0:T(8,128)(2,1)S(1)} collective-permute-done((bf16[784,128]{1,0:T(8,128)(2,1)S(1)}, bf16[784,128]{1,0:T(8,128)(2,1)S(1)}, u32[]{:S(2)}, u32[]{:S(2)}) %collective-permute-start.3) | collective-permute-done | bytes 200736 | tf_op jit(solution)/shard_map/ppermute | solution.py:300
  15.5 0.8 %early.1 = (f32[1024,256]{1,0:T(8,128)S(1)}, bf16[256,768]{1,0:T(8,128)(2,1)S(1)}) custom-call(bf16[8,3,128,128]{3,2,1,0:T(8,128)(2,1)S(1)} %get-tuple-element.26.tr.own_ref, bf16[8,3,128,128]{3,2,1,0:T(8,128)(2,1)S(1)} %collective-permute-done._.other_ref, bf16[784,128]{1,0:T(8,128)(2,1)S(1)} %collective-permute-done.1.xs_ref.refs_0_, ...), custom_call_target="tpu_custom_call" | custom-call | flops 600000000 | bytes 2400000 | tf_op jit(solution)/shard_map/early/pallas_call | solution.py:322
  16.3 1.1 %collective-permute-done.4.refs_3_ = bf16[784,128]{1,0:T(8,128)(2,1)S(1)} collective-permute-done((bf16[784,128]{1,0:T(8,128)(2,1)S(1)}, bf16[784,128]{1,0:T(8,128)(2,1)S(1)}, u32[]{:S(2)}, u32[]{:S(2)}) %collective-permute-start.4) | collective-permute-done | bytes 200736 | tf_op jit(solution)/shard_map/ppermute | solution.py:301
  17.4 0.6 %cross.2 = (f32[2,2,4,32,128]{4,3,2,1,0:T(8,128)S(1)}, bf16[2,2,4,32,128]{4,3,2,1,0:T(8,128)(2,1)S(1)}, bf16[256,1536]{1,0:T(8,128)(2,1)S(1)}) custom-call(bf16[8,3,128,128]{3,2,1,0:T(8,128)(2,1)S(1)} %get-tuple-element.26.tr.own_ref, bf16[8,3,128,128]{3,2,1,0:T(8,128)(2,1)S(1)} %collective-permute-done._.other_ref, ...), custom_call_target="tpu_custom_call" | custom-call | flops 900000000 | bytes 4000000 | tf_op jit(solution)/shard_map/cross/pallas_call | solution.py:344
  18.1 0.2 collective-permute-start.6
  18.3 0.6 %cross.3 = (f32[2,2,4,32,128]{4,3,2,1,0:T(8,128)S(1)}, bf16[2,2,4,32,128]{4,3,2,1,0:T(8,128)(2,1)S(1)}) custom-call(bf16[8,3,128,128]{3,2,1,0:T(8,128)(2,1)S(1)} %get-tuple-element.26.tr.own_ref, bf16[8,3,128,128]{3,2,1,0:T(8,128)(2,1)S(1)} %collective-permute-done._.other_ref, bf16[784,128]{1,0:T(8,128)(2,1)S(1)} %collective-permute-done.1.xs_ref.refs_0_, ...), custom_call_target="tpu_custom_call" | custom-call | flops 900000000 | bytes 4000000 | tf_op jit(solution)/shard_map/cross/pallas_call | solution.py:344
  18.9 0.5 %collective-permute-start.5 = (bf16[2,2,4,32,128]{4,3,2,1,0:T(8,128)(2,1)S(1)}, bf16[2,2,4,32,128]{4,3,2,1,0:T(8,128)(2,1)S(1)}, u32[]{:S(2)}, u32[]{:S(2)}) collective-permute-start(bf16[2,2,4,32,128]{4,3,2,1,0:T(8,128)(2,1)S(1)} %get-tuple-element.38), channel_id=1, source_target_pairs={{0,1},{1,0},{2,3},{3,2},{4,5},{5,4},{6,7},{7,6},{8,9},{9,8},{10,11... | collective-permute-start | bytes 393224 | tf_op jit(solution)/shard_map/ppermute | solution.py:365
  19.4 0.1 collective-permute-done.6.got_ref
  19.5 0.9 %collective-permute-start.7 = (bf16[2,4,32,128]{3,2,1,0:T(8,128)(2,1)S(1)}, bf16[2,4,32,128]{3,2,1,0:T(8,128)(2,1)S(1)}, u32[]{:S(2)}, u32[]{:S(2)}) collective-permute-start(bf16[2,4,32,128]{3,2,1,0:T(8,128)(2,1)S(1)} %get-tuple-element.42), channel_id=1, source_target_pairs={{0,6},{2,4},{4,2},{6,0},{8,14},{10,12},{12,10},{14,8},{1,7},{3,5},... | collective-permute-start | bytes 196616 | tf_op jit(solution)/shard_map/ppermute | solution.py:381
  20.4 0.3 collective-permute-start.8
  20.7 0.0 collective-permute-done.5.got_ref
  20.7 2.5 %collective-permute-start.9 = (bf16[2,4,32,128]{3,2,1,0:T(8,128)(2,1)S(1)}, bf16[2,4,32,128]{3,2,1,0:T(8,128)(2,1)S(1)}, u32[]{:S(2)}, u32[]{:S(2)}) collective-permute-start(bf16[2,4,32,128]{3,2,1,0:T(8,128)(2,1)S(1)} %get-tuple-element.44), channel_id=1, source_target_pairs={{0,4},{2,6},{4,0},{6,2},{8,12},{10,14},{12,8},{14,10},{1,5},{3,7},... | collective-permute-start | bytes 196616 | tf_op jit(solution)/shard_map/ppermute | solution.py:381
  23.2 2.2 %collective-permute-done.7.refs_0_ = bf16[2,4,32,128]{3,2,1,0:T(8,128)(2,1)S(1)} collective-permute-done((bf16[2,4,32,128]{3,2,1,0:T(8,128)(2,1)S(1)}, bf16[2,4,32,128]{3,2,1,0:T(8,128)(2,1)S(1)}, u32[]{:S(2)}, u32[]{:S(2)}) %collective-permute-start.7) | collective-permute-done | bytes 65568 | tf_op jit(solution)/shard_map/ppermute | solution.py:381
  25.4 0.3 %collective-permute-done.8.refs_1_ = bf16[2,4,32,128]{3,2,1,0:T(8,128)(2,1)S(1)} collective-permute-done((bf16[2,4,32,128]{3,2,1,0:T(8,128)(2,1)S(1)}, bf16[2,4,32,128]{3,2,1,0:T(8,128)(2,1)S(1)}, u32[]{:S(2)}, u32[]{:S(2)}) %collective-permute-start.8) | collective-permute-done | bytes 65568 | tf_op jit(solution)/shard_map/ppermute | solution.py:381
  25.7 0.0 collective-permute-done.9.refs_2_
  25.7 1.5 %collective-permute-start.10 = (bf16[4,32,128]{2,1,0:T(8,128)(2,1)S(1)}, bf16[4,32,128]{2,1,0:T(8,128)(2,1)S(1)}, u32[]{:S(2)}, u32[]{:S(2)}) collective-permute-start(bf16[4,32,128]{2,1,0:T(8,128)(2,1)S(1)} %get-tuple-element.46), channel_id=1, source_target_pairs={{0,8},{2,10},{4,12},{6,14},{8,0},{10,2},{12,4},{14,6},{1,9},{3,11}... | collective-permute-start | bytes 98312 | tf_op jit(solution)/shard_map/ppermute | solution.py:392
  27.2 3.4 %collective-permute-done.10.got_ref = bf16[4,32,128]{2,1,0:T(8,128)(2,1)S(1)} collective-permute-done((bf16[4,32,128]{2,1,0:T(8,128)(2,1)S(1)}, bf16[4,32,128]{2,1,0:T(8,128)(2,1)S(1)}, u32[]{:S(2)}, u32[]{:S(2)}) %collective-permute-start.10) | collective-permute-done | bytes 32800 | tf_op jit(solution)/shard_map/ppermute | solution.py:392
  30.6 0.7 %total.1 = f32[32,4,128]{2,1,0:T(4,128)} custom-call(f32[4,32,128]{2,1,0:T(8,128)S(1)} %get-tuple-element.45.keep_ref, bf16[4,32,128]{2,1,0:T(8,128)(2,1)S(1)} %collective-permute-done.10.got_ref), custom_call_target="tpu_custom_call" | custom-call | tf_op jit(solution)/shard_map/total/pallas_call | solution.py:393
  (4 shorter events, 0.1 us)
Async XLA Ops:
  0.0 8.1 %copy-start.1 = (f32[16]{0:T(128)S(1)}, f32[16]{0:T(128)}, u32[]{:S(2)}) copy-start(f32[16]{0:T(128)} %param.6) | copy-start | bytes 196
  1.4 6.7 %copy-start = (s32[1,8,128]{2,1,0:T(8,128)S(1)}, s32[1,8,128]{2,1,0:T(8,128)}, u32[]{:S(2)}) copy-start(s32[1,8,128]{2,1,0:T(8,128)} %ids_ref.1) | copy-start | bytes 12292
  1.4 6.7 %collective-permute-start = (bf16[8,3,128,128]{3,2,1,0:T(8,128)(2,1)S(1)}, bf16[8,3,128,128]{3,2,1,0:T(8,128)(2,1)S(1)}, u32[]{:S(2)}, u32[]{:S(2)}) collective-permute-start(bf16[8,3,128,128]{3,2,1,0:T(8,128)(2,1)S(1)} %get-tuple-element.26.tr.own_ref), channel_id=1, source_target_pairs={{0,1},{1,0},{2,3},{3,2},{4,5},{5,4},{6,7},{7,6},{8,9},{9,8},{10,11... | collective-permute-start | bytes 2359304 | tf_op jit(solution)/shard_map/ppermute | solution.py:288
  1.9 10.8 %collective-permute-start.1 = (bf16[784,128]{1,0:T(8,128)(2,1)S(1)}, bf16[784,128]{1,0:T(8,128)(2,1)S(1)}, u32[]{:S(2)}, u32[]{:S(2)}) collective-permute-start(bf16[784,128]{1,0:T(8,128)(2,1)S(1)} %get-tuple-element.27), channel_id=1, source_target_pairs={{0,2},{1,3},{2,0},{3,1},{4,6},{5,7},{6,4},{7,5},{8,10},{9,11},{10,... | collective-permute-start | bytes 602120 | tf_op jit(solution)/shard_map/ppermute | solution.py:289
  4.5 8.2 %collective-permute-start.2 = (bf16[784,128]{1,0:T(8,128)(2,1)S(1)}, bf16[784,128]{1,0:T(8,128)(2,1)S(1)}, u32[]{:S(2)}, u32[]{:S(2)}) collective-permute-start(bf16[784,128]{1,0:T(8,128)(2,1)S(1)} %get-tuple-element.28), channel_id=1, source_target_pairs={{0,12},{1,13},{2,6},{3,7},{4,0},{5,1},{6,10},{7,11},{8,4},{9,5},{1... | collective-permute-start | bytes 602120 | tf_op jit(solution)/shard_map/ppermute | solution.py:290
  8.2 7.3 %collective-permute-start.3 = (bf16[784,128]{1,0:T(8,128)(2,1)S(1)}, bf16[784,128]{1,0:T(8,128)(2,1)S(1)}, u32[]{:S(2)}, u32[]{:S(2)}) collective-permute-start(bf16[784,128]{1,0:T(8,128)(2,1)S(1)} %get-tuple-element.29), channel_id=1, source_target_pairs={{0,3},{1,2},{2,1},{3,0},{4,7},{5,6},{6,5},{7,4},{8,11},{9,10},{10,... | collective-permute-start | bytes 602120 | tf_op jit(solution)/shard_map/ppermute | solution.py:300
  8.3 9.1 %collective-permute-start.4 = (bf16[784,128]{1,0:T(8,128)(2,1)S(1)}, bf16[784,128]{1,0:T(8,128)(2,1)S(1)}, u32[]{:S(2)}, u32[]{:S(2)}) collective-permute-start(bf16[784,128]{1,0:T(8,128)(2,1)S(1)} %get-tuple-element.30), channel_id=1, source_target_pairs={{2,7},{3,6},{4,1},{5,0},{6,11},{7,10},{8,5},{9,4},{10,15},{11,14},... | collective-permute-start | bytes 602120 | tf_op jit(solution)/shard_map/ppermute | solution.py:301
  18.1 1.4 %collective-permute-start.6 = (bf16[2,2,4,32,128]{4,3,2,1,0:T(8,128)(2,1)S(1)}, bf16[2,2,4,32,128]{4,3,2,1,0:T(8,128)(2,1)S(1)}, u32[]{:S(2)}, u32[]{:S(2)}) collective-permute-start(bf16[2,2,4,32,128]{4,3,2,1,0:T(8,128)(2,1)S(1)} %get-tuple-element.41), channel_id=1, source_target_pairs={{0,1},{1,0},{2,3},{3,2},{4,5},{5,4},{6,7},{7,6},{8,9},{9,8},{10,11... | collective-permute-start | bytes 393224 | tf_op jit(solution)/shard_map/ppermute | solution.py:363
  18.9 1.8 %collective-permute-start.5 = (bf16[2,2,4,32,128]{4,3,2,1,0:T(8,128)(2,1)S(1)}, bf16[2,2,4,32,128]{4,3,2,1,0:T(8,128)(2,1)S(1)}, u32[]{:S(2)}, u32[]{:S(2)}) collective-permute-start(bf16[2,2,4,32,128]{4,3,2,1,0:T(8,128)(2,1)S(1)} %get-tuple-element.38), channel_id=1, source_target_pairs={{0,1},{1,0},{2,3},{3,2},{4,5},{5,4},{6,7},{7,6},{8,9},{9,8},{10,11... | collective-permute-start | bytes 393224 | tf_op jit(solution)/shard_map/ppermute | solution.py:365
  19.5 5.8 %collective-permute-start.7 = (bf16[2,4,32,128]{3,2,1,0:T(8,128)(2,1)S(1)}, bf16[2,4,32,128]{3,2,1,0:T(8,128)(2,1)S(1)}, u32[]{:S(2)}, u32[]{:S(2)}) collective-permute-start(bf16[2,4,32,128]{3,2,1,0:T(8,128)(2,1)S(1)} %get-tuple-element.42), channel_id=1, source_target_pairs={{0,6},{2,4},{4,2},{6,0},{8,14},{10,12},{12,10},{14,8},{1,7},{3,5},... | collective-permute-start | bytes 196616 | tf_op jit(solution)/shard_map/ppermute | solution.py:381
  20.4 5.3 %collective-permute-start.8 = (bf16[2,4,32,128]{3,2,1,0:T(8,128)(2,1)S(1)}, bf16[2,4,32,128]{3,2,1,0:T(8,128)(2,1)S(1)}, u32[]{:S(2)}, u32[]{:S(2)}) collective-permute-start(bf16[2,4,32,128]{3,2,1,0:T(8,128)(2,1)S(1)} %get-tuple-element.43), channel_id=1, source_target_pairs={{0,2},{2,0},{4,6},{6,4},{8,10},{10,8},{12,14},{14,12},{1,3},{3,1},... | collective-permute-start | bytes 196616 | tf_op jit(solution)/shard_map/ppermute | solution.py:381
  20.7 5.0 %collective-permute-start.9 = (bf16[2,4,32,128]{3,2,1,0:T(8,128)(2,1)S(1)}, bf16[2,4,32,128]{3,2,1,0:T(8,128)(2,1)S(1)}, u32[]{:S(2)}, u32[]{:S(2)}) collective-permute-start(bf16[2,4,32,128]{3,2,1,0:T(8,128)(2,1)S(1)} %get-tuple-element.44), channel_id=1, source_target_pairs={{0,4},{2,6},{4,0},{6,2},{8,12},{10,14},{12,8},{14,10},{1,5},{3,7},... | collective-permute-start | bytes 196616 | tf_op jit(solution)/shard_map/ppermute | solution.py:381
  25.7 4.9 %collective-permute-start.10 = (bf16[4,32,128]{2,1,0:T(8,128)(2,1)S(1)}, bf16[4,32,128]{2,1,0:T(8,128)(2,1)S(1)}, u32[]{:S(2)}, u32[]{:S(2)}) collective-permute-start(bf16[4,32,128]{2,1,0:T(8,128)(2,1)S(1)} %get-tuple-element.46), channel_id=1, source_target_pairs={{0,8},{2,10},{4,12},{6,14},{8,0},{10,2},{12,4},{14,6},{1,9},{3,11}... | collective-permute-start | bytes 98312 | tf_op jit(solution)/shard_map/ppermute | solution.py:392

commit v16 on v15

--- a/solution.py
+++ b/solution.py
@@ -359,7 +359,7 @@
         def partners(*steps):
             return lambda s: [jnp.bitwise_xor(lax.rem(s, NEAR), step) for step in steps]
 
-        keep_a, send_a, w2 = crossed(2, partners(3, 1), ())
+        keep_a, send_a, w2 = crossed(2, partners(1, 3), ())
         got_a = lax.ppermute(send_a, "modes", swap)
         keep_b, send_b = crossed(2, partners(0, 2), (w2,))
         got_b = lax.ppermute(send_b, "modes", swap)
@@ -375,11 +375,11 @@
                 name="near",
             )(keep, got)
 
-        part_3, part_1 = summed((bf16, bf16), keep_a, got_a)
+        part_1, part_3 = summed((bf16, bf16), keep_a, got_a)
         mine, part_2 = summed((f32, bf16), keep_b, got_b)
         parts = [
             lax.ppermute(part, "space", [(s, s ^ step) for s in range(n)])
-            for part, step in ((part_3, 3), (part_1, 1), (part_2, 2))
+            for part, step in ((part_1, 1), (part_3, 3), (part_2, 2))
         ]
         keep, send = pl.pallas_call(
             far_kernel,

time: 31.4 us -> 32.1 us (1.022)
  waiting for transfers between devices: 9.98 us -> 11.1 us
  starting transfers between devices: 13.8 us -> 13.3 us
    ppermute x3, waiting for transfers between devices: 2.51 us -> 3.14 us  [on_device(): lax.ppermute(part, 'space', [(s, s ^ step) for s in range(n)])]
    ppermute x1, starting transfers between devices: 1.48 us -> 1 us  [on_device(): got = lax.ppermute(send, 'space', [(s, s ^ NEAR) for s in range(n)])]
    ppermute x1, waiting for transfers between devices: 3.4 us -> 3.88 us  [on_device(): got = lax.ppermute(send, 'space', [(s, s ^ NEAR) for s in range(n)])]
  transfers between devices with their start and end apart: 11 -> 11, of which waited for: 6 -> 7; matrix products, arithmetic and copies ran while one was open for 0% -> 0% of each run, Pallas kernels for 13% -> 13%
where the time goes in v16:
time: 32.1 us; the launch traced here: 31.9 us
  starting transfers between devices  13.3 us (41%)
  waiting for transfers between devices  11.1 us (35%)
  Pallas kernels  6.73 us (21%)
  between operations  0.76 us (2%)
    ppermute x1, waiting for transfers between devices, on_device(): got = lax.ppermute(send, 'space', [(s, s ^ NEAR) for s in range(n)])  3.88 us
    ppermute x3, starting transfers between devices, on_device(): lax.ppermute(part, 'space', [(s, s ^ step) for s in range(n)])  3.61 us
    ppermute x1, starting transfers between devices, on_device(): zs = lax.ppermute(zs, both, same(z_pairs))  3.6 us
    ppermute x3, waiting for transfers between devices, on_device(): lax.ppermute(part, 'space', [(s, s ^ step) for s in range(n)])  3.14 us
    ppermute x1, waiting for transfers between devices, on_device(): xc = lax.ppermute(xc, both, cross(x_pairs))  2.8 us
    ppermute x1, starting transfers between devices, on_device(): xs = lax.ppermute(xs, both, same(x_pairs))  2.56 us
    pallas_call x1, Pallas kernels, on_device(): pl.pallas_call(local_kernel, out_shape=[jax.ShapeDtypeStruct((JB * 2 * nk...  2.44 us
    pallas_call x1, Pallas kernels, on_device(): pl.pallas_call(prep_kernel, out_shape=[jax.ShapeDtypeStruct((nx, comps, n...  1.38 us
  transfers between devices with their start and end apart: 11, of which 7 were waited for; matrix products, arithmetic and copies ran while one was open for 0% of the time, Pallas kernels for 13%

profile of v16, /device:TPU:0, one launch (start us, length us, event | category | flops | bytes accessed | tf_op | source)
XLA Modules:
  0.0 31.9 jit_solution(15845739088419138101)
XLA Ops:
  0.0 0.0 copy-start.1
  0.0 1.4 %prep.1 = (bf16[8,3,128,128]{3,2,1,0:T(8,128)(2,1)S(1)}, bf16[784,128]{1,0:T(8,128)(2,1)S(1)}, bf16[784,128]{1,0:T(8,128)(2,1)S(1)}) custom-call(bf16[128,3,1,8,128]{4,3,2,1,0:T(8,128)(2,1)} %modes_hbm.1), custom_call_target="tpu_custom_call" | custom-call | flops 1500000000 | bytes 2800000 | tf_op jit(solution)/shard_map/prep/pallas_call | solution.py:271
  1.4 0.0 copy-start
  1.4 0.5 %collective-permute-start = (bf16[8,3,128,128]{3,2,1,0:T(8,128)(2,1)S(1)}, bf16[8,3,128,128]{3,2,1,0:T(8,128)(2,1)S(1)}, u32[]{:S(2)}, u32[]{:S(2)}) collective-permute-start(bf16[8,3,128,128]{3,2,1,0:T(8,128)(2,1)S(1)} %get-tuple-element.26.tr.own_ref), channel_id=1, source_target_pairs={{0,1},{1,0},{2,3},{3,2},{4,5},{5,4},{6,7},{7,6},{8,9},{9,8},{10,11... | collective-permute-start | bytes 2359304 | tf_op jit(solution)/shard_map/ppermute | solution.py:288
  1.9 2.6 %collective-permute-start.1 = (bf16[784,128]{1,0:T(8,128)(2,1)S(1)}, bf16[784,128]{1,0:T(8,128)(2,1)S(1)}, u32[]{:S(2)}, u32[]{:S(2)}) collective-permute-start(bf16[784,128]{1,0:T(8,128)(2,1)S(1)} %get-tuple-element.27), channel_id=1, source_target_pairs={{0,2},{1,3},{2,0},{3,1},{4,6},{5,7},{6,4},{7,5},{8,10},{9,11},{10,... | collective-permute-start | bytes 602120 | tf_op jit(solution)/shard_map/ppermute | solution.py:289
  4.5 3.6 %collective-permute-start.2 = (bf16[784,128]{1,0:T(8,128)(2,1)S(1)}, bf16[784,128]{1,0:T(8,128)(2,1)S(1)}, u32[]{:S(2)}, u32[]{:S(2)}) collective-permute-start(bf16[784,128]{1,0:T(8,128)(2,1)S(1)} %get-tuple-element.28), channel_id=1, source_target_pairs={{0,12},{1,13},{2,6},{3,7},{4,0},{5,1},{6,10},{7,11},{8,4},{9,5},{1... | collective-permute-start | bytes 602120 | tf_op jit(solution)/shard_map/ppermute | solution.py:290
  8.1 0.0 collective-permute-done._.other_ref
  8.1 0.0 copy-done.1
  8.1 0.0 copy-done
  8.1 0.1 weights.1
  8.2 0.1 collective-permute-start.3
  8.3 1.3 %collective-permute-start.4 = (bf16[784,128]{1,0:T(8,128)(2,1)S(1)}, bf16[784,128]{1,0:T(8,128)(2,1)S(1)}, u32[]{:S(2)}, u32[]{:S(2)}) collective-permute-start(bf16[784,128]{1,0:T(8,128)(2,1)S(1)} %get-tuple-element.30), channel_id=1, source_target_pairs={{2,7},{3,6},{4,1},{5,0},{6,11},{7,10},{8,5},{9,4},{10,15},{11,14},... | collective-permute-start | bytes 602120 | tf_op jit(solution)/shard_map/ppermute | solution.py:301
  10.3 2.4 %local.1 = (f32[1024,256]{1,0:T(8,128)S(1)}, bf16[2,256,384]{2,1,0:T(8,128)(2,1)S(1)}) custom-call(bf16[8,3,128,128]{3,2,1,0:T(8,128)(2,1)S(1)} %get-tuple-element.26.tr.own_ref, bf16[8,3,128,128]{3,2,1,0:T(8,128)(2,1)S(1)} %collective-permute-done._.other_ref, f32[8,128]{1,0:T(8,128)S(1)} %get-tuple-element.31.weight_ref, s32[1]{0:T(128)S(6)} %copy.5.jb_ref.refs_5_), custom_call_target="tpu_custom_call" | custom-call | flops 900000000 | bytes 2400000 | tf_op jit(solution)/shard_map/local/pallas_call | solution.py:305
  12.7 0.0 collective-permute-done.1.xs_ref.refs_0_
  12.7 0.0 collective-permute-done.2._.refs_1_
  12.7 2.8 %collective-permute-done.3.xc_ref.refs_2_ = bf16[784,128]{1,0:T(8,128)(2,1)S(1)} collective-permute-done((bf16[784,128]{1,0:T(8,128)(2,1)S(1)}, bf16[784,128]{1,0:T(8,128)(2,1)S(1)}, u32[]{:S(2)}, u32[]{:S(2)}) %collective-permute-start.3) | collective-permute-done | bytes 200736 | tf_op jit(solution)/shard_map/ppermute | solution.py:300
  15.5 0.8 %early.1 = (f32[1024,256]{1,0:T(8,128)S(1)}, bf16[256,768]{1,0:T(8,128)(2,1)S(1)}) custom-call(bf16[8,3,128,128]{3,2,1,0:T(8,128)(2,1)S(1)} %get-tuple-element.26.tr.own_ref, bf16[8,3,128,128]{3,2,1,0:T(8,128)(2,1)S(1)} %collective-permute-done._.other_ref, bf16[784,128]{1,0:T(8,128)(2,1)S(1)} %collective-permute-done.1.xs_ref.refs_0_, ...), custom_call_target="tpu_custom_call" | custom-call | flops 600000000 | bytes 2400000 | tf_op jit(solution)/shard_map/early/pallas_call | solution.py:322
  16.3 1.1 %collective-permute-done.4.refs_3_ = bf16[784,128]{1,0:T(8,128)(2,1)S(1)} collective-permute-done((bf16[784,128]{1,0:T(8,128)(2,1)S(1)}, bf16[784,128]{1,0:T(8,128)(2,1)S(1)}, u32[]{:S(2)}, u32[]{:S(2)}) %collective-permute-start.4) | collective-permute-done | bytes 200736 | tf_op jit(solution)/shard_map/ppermute | solution.py:301
  17.4 0.6 %cross.2 = (f32[2,2,4,32,128]{4,3,2,1,0:T(8,128)S(1)}, bf16[2,2,4,32,128]{4,3,2,1,0:T(8,128)(2,1)S(1)}, bf16[256,1536]{1,0:T(8,128)(2,1)S(1)}) custom-call(bf16[8,3,128,128]{3,2,1,0:T(8,128)(2,1)S(1)} %get-tuple-element.26.tr.own_ref, bf16[8,3,128,128]{3,2,1,0:T(8,128)(2,1)S(1)} %collective-permute-done._.other_ref, ...), custom_call_target="tpu_custom_call" | custom-call | flops 900000000 | bytes 4000000 | tf_op jit(solution)/shard_map/cross/pallas_call | solution.py:344
  18.1 0.2 collective-permute-start.6
  18.3 0.6 %cross.3 = (f32[2,2,4,32,128]{4,3,2,1,0:T(8,128)S(1)}, bf16[2,2,4,32,128]{4,3,2,1,0:T(8,128)(2,1)S(1)}) custom-call(bf16[8,3,128,128]{3,2,1,0:T(8,128)(2,1)S(1)} %get-tuple-element.26.tr.own_ref, bf16[8,3,128,128]{3,2,1,0:T(8,128)(2,1)S(1)} %collective-permute-done._.other_ref, bf16[784,128]{1,0:T(8,128)(2,1)S(1)} %collective-permute-done.1.xs_ref.refs_0_, ...), custom_call_target="tpu_custom_call" | custom-call | flops 900000000 | bytes 4000000 | tf_op jit(solution)/shard_map/cross/pallas_call | solution.py:344
  18.9 0.5 %collective-permute-start.5 = (bf16[2,2,4,32,128]{4,3,2,1,0:T(8,128)(2,1)S(1)}, bf16[2,2,4,32,128]{4,3,2,1,0:T(8,128)(2,1)S(1)}, u32[]{:S(2)}, u32[]{:S(2)}) collective-permute-start(bf16[2,2,4,32,128]{4,3,2,1,0:T(8,128)(2,1)S(1)} %get-tuple-element.38), channel_id=1, source_target_pairs={{0,1},{1,0},{2,3},{3,2},{4,5},{5,4},{6,7},{7,6},{8,9},{9,8},{10,11... | collective-permute-start | bytes 393224 | tf_op jit(solution)/shard_map/ppermute | solution.py:365
  19.4 0.1 collective-permute-done.6.got_ref
  19.5 0.1 collective-permute-start.7
  19.6 1.1 %collective-permute-start.8 = (bf16[2,4,32,128]{3,2,1,0:T(8,128)(2,1)S(1)}, bf16[2,4,32,128]{3,2,1,0:T(8,128)(2,1)S(1)}, u32[]{:S(2)}, u32[]{:S(2)}) collective-permute-start(bf16[2,4,32,128]{3,2,1,0:T(8,128)(2,1)S(1)} %get-tuple-element.43), channel_id=1, source_target_pairs={{0,6},{2,4},{4,2},{6,0},{8,14},{10,12},{12,10},{14,8},{1,7},{3,5},... | collective-permute-start | bytes 196616 | tf_op jit(solution)/shard_map/ppermute | solution.py:381
  20.7 0.0 collective-permute-done.5.got_ref
  20.7 2.5 %collective-permute-start.9 = (bf16[2,4,32,128]{3,2,1,0:T(8,128)(2,1)S(1)}, bf16[2,4,32,128]{3,2,1,0:T(8,128)(2,1)S(1)}, u32[]{:S(2)}, u32[]{:S(2)}) collective-permute-start(bf16[2,4,32,128]{3,2,1,0:T(8,128)(2,1)S(1)} %get-tuple-element.44), channel_id=1, source_target_pairs={{0,4},{2,6},{4,0},{6,2},{8,12},{10,14},{12,8},{14,10},{1,5},{3,7},... | collective-permute-start | bytes 196616 | tf_op jit(solution)/shard_map/ppermute | solution.py:381
  23.2 1.8 %collective-permute-done.7.refs_0_ = bf16[2,4,32,128]{3,2,1,0:T(8,128)(2,1)S(1)} collective-permute-done((bf16[2,4,32,128]{3,2,1,0:T(8,128)(2,1)S(1)}, bf16[2,4,32,128]{3,2,1,0:T(8,128)(2,1)S(1)}, u32[]{:S(2)}, u32[]{:S(2)}) %collective-permute-start.7) | collective-permute-done | bytes 65568 | tf_op jit(solution)/shard_map/ppermute | solution.py:381
  25.0 0.5 %collective-permute-done.8.refs_1_ = bf16[2,4,32,128]{3,2,1,0:T(8,128)(2,1)S(1)} collective-permute-done((bf16[2,4,32,128]{3,2,1,0:T(8,128)(2,1)S(1)}, bf16[2,4,32,128]{3,2,1,0:T(8,128)(2,1)S(1)}, u32[]{:S(2)}, u32[]{:S(2)}) %collective-permute-start.8) | collective-permute-done | bytes 65568 | tf_op jit(solution)/shard_map/ppermute | solution.py:381
  25.5 0.8 %collective-permute-done.9.refs_2_ = bf16[2,4,32,128]{3,2,1,0:T(8,128)(2,1)S(1)} collective-permute-done((bf16[2,4,32,128]{3,2,1,0:T(8,128)(2,1)S(1)}, bf16[2,4,32,128]{3,2,1,0:T(8,128)(2,1)S(1)}, u32[]{:S(2)}, u32[]{:S(2)}) %collective-permute-start.9) | collective-permute-done | bytes 65568 | tf_op jit(solution)/shard_map/ppermute | solution.py:381
  26.4 1.0 %collective-permute-start.10 = (bf16[4,32,128]{2,1,0:T(8,128)(2,1)S(1)}, bf16[4,32,128]{2,1,0:T(8,128)(2,1)S(1)}, u32[]{:S(2)}, u32[]{:S(2)}) collective-permute-start(bf16[4,32,128]{2,1,0:T(8,128)(2,1)S(1)} %get-tuple-element.46), channel_id=1, source_target_pairs={{0,8},{2,10},{4,12},{6,14},{8,0},{10,2},{12,4},{14,6},{1,9},{3,11}... | collective-permute-start | bytes 98312 | tf_op jit(solution)/shard_map/ppermute | solution.py:392
  27.4 3.9 %collective-permute-done.10.got_ref = bf16[4,32,128]{2,1,0:T(8,128)(2,1)S(1)} collective-permute-done((bf16[4,32,128]{2,1,0:T(8,128)(2,1)S(1)}, bf16[4,32,128]{2,1,0:T(8,128)(2,1)S(1)}, u32[]{:S(2)}, u32[]{:S(2)}) %collective-permute-start.10) | collective-permute-done | bytes 32800 | tf_op jit(solution)/shard_map/ppermute | solution.py:392
  31.2 0.7 %total.1 = f32[32,4,128]{2,1,0:T(4,128)} custom-call(f32[4,32,128]{2,1,0:T(8,128)S(1)} %get-tuple-element.45.keep_ref, bf16[4,32,128]{2,1,0:T(8,128)(2,1)S(1)} %collective-permute-done.10.got_ref), custom_call_target="tpu_custom_call" | custom-call | tf_op jit(solution)/shard_map/total/pallas_call | solution.py:393
  (4 shorter events, 0.1 us)
Async XLA Ops:
  0.0 8.1 %copy-start.1 = (f32[16]{0:T(128)S(1)}, f32[16]{0:T(128)}, u32[]{:S(2)}) copy-start(f32[16]{0:T(128)} %param.6) | copy-start | bytes 196
  1.4 6.7 %copy-start = (s32[1,8,128]{2,1,0:T(8,128)S(1)}, s32[1,8,128]{2,1,0:T(8,128)}, u32[]{:S(2)}) copy-start(s32[1,8,128]{2,1,0:T(8,128)} %ids_ref.1) | copy-start | bytes 12292
  1.4 6.7 %collective-permute-start = (bf16[8,3,128,128]{3,2,1,0:T(8,128)(2,1)S(1)}, bf16[8,3,128,128]{3,2,1,0:T(8,128)(2,1)S(1)}, u32[]{:S(2)}, u32[]{:S(2)}) collective-permute-start(bf16[8,3,128,128]{3,2,1,0:T(8,128)(2,1)S(1)} %get-tuple-element.26.tr.own_ref), channel_id=1, source_target_pairs={{0,1},{1,0},{2,3},{3,2},{4,5},{5,4},{6,7},{7,6},{8,9},{9,8},{10,11... | collective-permute-start | bytes 2359304 | tf_op jit(solution)/shard_map/ppermute | solution.py:288
  1.9 10.8 %collective-permute-start.1 = (bf16[784,128]{1,0:T(8,128)(2,1)S(1)}, bf16[784,128]{1,0:T(8,128)(2,1)S(1)}, u32[]{:S(2)}, u32[]{:S(2)}) collective-permute-start(bf16[784,128]{1,0:T(8,128)(2,1)S(1)} %get-tuple-element.27), channel_id=1, source_target_pairs={{0,2},{1,3},{2,0},{3,1},{4,6},{5,7},{6,4},{7,5},{8,10},{9,11},{10,... | collective-permute-start | bytes 602120 | tf_op jit(solution)/shard_map/ppermute | solution.py:289
  4.5 8.2 %collective-permute-start.2 = (bf16[784,128]{1,0:T(8,128)(2,1)S(1)}, bf16[784,128]{1,0:T(8,128)(2,1)S(1)}, u32[]{:S(2)}, u32[]{:S(2)}) collective-permute-start(bf16[784,128]{1,0:T(8,128)(2,1)S(1)} %get-tuple-element.28), channel_id=1, source_target_pairs={{0,12},{1,13},{2,6},{3,7},{4,0},{5,1},{6,10},{7,11},{8,4},{9,5},{1... | collective-permute-start | bytes 602120 | tf_op jit(solution)/shard_map/ppermute | solution.py:290
  8.2 7.3 %collective-permute-start.3 = (bf16[784,128]{1,0:T(8,128)(2,1)S(1)}, bf16[784,128]{1,0:T(8,128)(2,1)S(1)}, u32[]{:S(2)}, u32[]{:S(2)}) collective-permute-start(bf16[784,128]{1,0:T(8,128)(2,1)S(1)} %get-tuple-element.29), channel_id=1, source_target_pairs={{0,3},{1,2},{2,1},{3,0},{4,7},{5,6},{6,5},{7,4},{8,11},{9,10},{10,... | collective-permute-start | bytes 602120 | tf_op jit(solution)/shard_map/ppermute | solution.py:300
  8.3 9.1 %collective-permute-start.4 = (bf16[784,128]{1,0:T(8,128)(2,1)S(1)}, bf16[784,128]{1,0:T(8,128)(2,1)S(1)}, u32[]{:S(2)}, u32[]{:S(2)}) collective-permute-start(bf16[784,128]{1,0:T(8,128)(2,1)S(1)} %get-tuple-element.30), channel_id=1, source_target_pairs={{2,7},{3,6},{4,1},{5,0},{6,11},{7,10},{8,5},{9,4},{10,15},{11,14},... | collective-permute-start | bytes 602120 | tf_op jit(solution)/shard_map/ppermute | solution.py:301
  18.1 1.4 %collective-permute-start.6 = (bf16[2,2,4,32,128]{4,3,2,1,0:T(8,128)(2,1)S(1)}, bf16[2,2,4,32,128]{4,3,2,1,0:T(8,128)(2,1)S(1)}, u32[]{:S(2)}, u32[]{:S(2)}) collective-permute-start(bf16[2,2,4,32,128]{4,3,2,1,0:T(8,128)(2,1)S(1)} %get-tuple-element.41), channel_id=1, source_target_pairs={{0,1},{1,0},{2,3},{3,2},{4,5},{5,4},{6,7},{7,6},{8,9},{9,8},{10,11... | collective-permute-start | bytes 393224 | tf_op jit(solution)/shard_map/ppermute | solution.py:363
  18.9 1.8 %collective-permute-start.5 = (bf16[2,2,4,32,128]{4,3,2,1,0:T(8,128)(2,1)S(1)}, bf16[2,2,4,32,128]{4,3,2,1,0:T(8,128)(2,1)S(1)}, u32[]{:S(2)}, u32[]{:S(2)}) collective-permute-start(bf16[2,2,4,32,128]{4,3,2,1,0:T(8,128)(2,1)S(1)} %get-tuple-element.38), channel_id=1, source_target_pairs={{0,1},{1,0},{2,3},{3,2},{4,5},{5,4},{6,7},{7,6},{8,9},{9,8},{10,11... | collective-permute-start | bytes 393224 | tf_op jit(solution)/shard_map/ppermute | solution.py:365
  19.5 5.5 %collective-permute-start.7 = (bf16[2,4,32,128]{3,2,1,0:T(8,128)(2,1)S(1)}, bf16[2,4,32,128]{3,2,1,0:T(8,128)(2,1)S(1)}, u32[]{:S(2)}, u32[]{:S(2)}) collective-permute-start(bf16[2,4,32,128]{3,2,1,0:T(8,128)(2,1)S(1)} %get-tuple-element.42), channel_id=1, source_target_pairs={{0,2},{2,0},{4,6},{6,4},{8,10},{10,8},{12,14},{14,12},{1,3},{3,1},... | collective-permute-start | bytes 196616 | tf_op jit(solution)/shard_map/ppermute | solution.py:381
  19.6 5.9 %collective-permute-start.8 = (bf16[2,4,32,128]{3,2,1,0:T(8,128)(2,1)S(1)}, bf16[2,4,32,128]{3,2,1,0:T(8,128)(2,1)S(1)}, u32[]{:S(2)}, u32[]{:S(2)}) collective-permute-start(bf16[2,4,32,128]{3,2,1,0:T(8,128)(2,1)S(1)} %get-tuple-element.43), channel_id=1, source_target_pairs={{0,6},{2,4},{4,2},{6,0},{8,14},{10,12},{12,10},{14,8},{1,7},{3,5},... | collective-permute-start | bytes 196616 | tf_op jit(solution)/shard_map/ppermute | solution.py:381
  20.7 5.6 %collective-permute-start.9 = (bf16[2,4,32,128]{3,2,1,0:T(8,128)(2,1)S(1)}, bf16[2,4,32,128]{3,2,1,0:T(8,128)(2,1)S(1)}, u32[]{:S(2)}, u32[]{:S(2)}) collective-permute-start(bf16[2,4,32,128]{3,2,1,0:T(8,128)(2,1)S(1)} %get-tuple-element.44), channel_id=1, source_target_pairs={{0,4},{2,6},{4,0},{6,2},{8,12},{10,14},{12,8},{14,10},{1,5},{3,7},... | collective-permute-start | bytes 196616 | tf_op jit(solution)/shard_map/ppermute | solution.py:381
  26.4 4.9 %collective-permute-start.10 = (bf16[4,32,128]{2,1,0:T(8,128)(2,1)S(1)}, bf16[4,32,128]{2,1,0:T(8,128)(2,1)S(1)}, u32[]{:S(2)}, u32[]{:S(2)}) collective-permute-start(bf16[4,32,128]{2,1,0:T(8,128)(2,1)S(1)} %get-tuple-element.46), channel_id=1, source_target_pairs={{0,8},{2,10},{4,12},{6,14},{8,0},{10,2},{12,4},{14,6},{1,9},{3,11}... | collective-permute-start | bytes 98312 | tf_op jit(solution)/shard_map/ppermute | solution.py:392

commit v17 on v16

--- a/solution.py
+++ b/solution.py
@@ -359,9 +359,9 @@
         def partners(*steps):
             return lambda s: [jnp.bitwise_xor(lax.rem(s, NEAR), step) for step in steps]
 
-        keep_a, send_a, w2 = crossed(2, partners(1, 3), ())
+        keep_a, send_a, w2 = crossed(2, partners(1, 2), ())
         got_a = lax.ppermute(send_a, "modes", swap)
-        keep_b, send_b = crossed(2, partners(0, 2), (w2,))
+        keep_b, send_b = crossed(2, partners(0, 3), (w2,))
         got_b = lax.ppermute(send_b, "modes", swap)
         piece = (JB, chunk, nk)
 
@@ -375,11 +375,11 @@
                 name="near",
             )(keep, got)
 
-        part_1, part_3 = summed((bf16, bf16), keep_a, got_a)
-        mine, part_2 = summed((f32, bf16), keep_b, got_b)
+        part_1, part_2 = summed((bf16, bf16), keep_a, got_a)
+        mine, part_3 = summed((f32, bf16), keep_b, got_b)
         parts = [
             lax.ppermute(part, "space", [(s, s ^ step) for s in range(n)])
-            for part, step in ((part_1, 1), (part_3, 3), (part_2, 2))
+            for part, step in ((part_1, 1), (part_2, 2), (part_3, 3))
         ]
         keep, send = pl.pallas_call(
             far_kernel,

time: 32.1 us -> 32.5 us (1.012)
  starting transfers between devices: 13.3 us -> 14 us
    ppermute x1, starting transfers between devices: 1 us -> 1.71 us  [on_device(): got = lax.ppermute(send, 'space', [(s, s ^ NEAR) for s in range(n)])]
    ppermute x1, waiting for transfers between devices: 3.88 us -> 3.5 us  [on_device(): got = lax.ppermute(send, 'space', [(s, s ^ NEAR) for s in range(n)])]
  transfers between devices with their start and end apart: 11 -> 11, of which waited for: 7 -> 7; matrix products, arithmetic and copies ran while one was open for 0% -> 0% of each run, Pallas kernels for 13% -> 12%
where the time goes in v17:
time: 32.5 us; the launch traced here: 32.3 us
  starting transfers between devices  14 us (43%)
  waiting for transfers between devices  10.8 us (33%)
  Pallas kernels  6.73 us (21%)
  between operations  0.76 us (2%)
    ppermute x3, starting transfers between devices, on_device(): lax.ppermute(part, 'space', [(s, s ^ step) for s in range(n)])  3.61 us
    ppermute x1, starting transfers between devices, on_device(): zs = lax.ppermute(zs, both, same(z_pairs))  3.6 us
    ppermute x1, waiting for transfers between devices, on_device(): got = lax.ppermute(send, 'space', [(s, s ^ NEAR) for s in range(n)])  3.5 us
    ppermute x3, waiting for transfers between devices, on_device(): lax.ppermute(part, 'space', [(s, s ^ step) for s in range(n)])  3.23 us
    ppermute x1, waiting for transfers between devices, on_device(): xc = lax.ppermute(xc, both, cross(x_pairs))  2.8 us
    ppermute x1, starting transfers between devices, on_device(): xs = lax.ppermute(xs, both, same(x_pairs))  2.56 us
    pallas_call x1, Pallas kernels, on_device(): pl.pallas_call(local_kernel, out_shape=[jax.ShapeDtypeStruct((JB * 2 * nk...  2.44 us
    ppermute x1, starting transfers between devices, on_device(): got = lax.ppermute(send, 'space', [(s, s ^ NEAR) for s in range(n)])  1.71 us
  transfers between devices with their start and end apart: 11, of which 7 were waited for; matrix products, arithmetic and copies ran while one was open for 0% of the time, Pallas kernels for 12%

profile of v17, /device:TPU:0, one launch (start us, length us, event | category | flops | bytes accessed | tf_op | source)
XLA Modules:
  0.0 32.3 jit_solution(18364151710525751911)
XLA Ops:
  0.0 0.0 copy-start.1
  0.0 1.4 %prep.1 = (bf16[8,3,128,128]{3,2,1,0:T(8,128)(2,1)S(1)}, bf16[784,128]{1,0:T(8,128)(2,1)S(1)}, bf16[784,128]{1,0:T(8,128)(2,1)S(1)}) custom-call(bf16[128,3,1,8,128]{4,3,2,1,0:T(8,128)(2,1)} %modes_hbm.1), custom_call_target="tpu_custom_call" | custom-call | flops 1500000000 | bytes 2800000 | tf_op jit(solution)/shard_map/prep/pallas_call | solution.py:271
  1.4 0.0 copy-start
  1.4 0.5 %collective-permute-start = (bf16[8,3,128,128]{3,2,1,0:T(8,128)(2,1)S(1)}, bf16[8,3,128,128]{3,2,1,0:T(8,128)(2,1)S(1)}, u32[]{:S(2)}, u32[]{:S(2)}) collective-permute-start(bf16[8,3,128,128]{3,2,1,0:T(8,128)(2,1)S(1)} %get-tuple-element.26.tr.own_ref), channel_id=1, source_target_pairs={{0,1},{1,0},{2,3},{3,2},{4,5},{5,4},{6,7},{7,6},{8,9},{9,8},{10,11... | collective-permute-start | bytes 2359304 | tf_op jit(solution)/shard_map/ppermute | solution.py:288
  1.9 2.6 %collective-permute-start.1 = (bf16[784,128]{1,0:T(8,128)(2,1)S(1)}, bf16[784,128]{1,0:T(8,128)(2,1)S(1)}, u32[]{:S(2)}, u32[]{:S(2)}) collective-permute-start(bf16[784,128]{1,0:T(8,128)(2,1)S(1)} %get-tuple-element.27), channel_id=1, source_target_pairs={{0,2},{1,3},{2,0},{3,1},{4,6},{5,7},{6,4},{7,5},{8,10},{9,11},{10,... | collective-permute-start | bytes 602120 | tf_op jit(solution)/shard_map/ppermute | solution.py:289
  4.5 3.6 %collective-permute-start.2 = (bf16[784,128]{1,0:T(8,128)(2,1)S(1)}, bf16[784,128]{1,0:T(8,128)(2,1)S(1)}, u32[]{:S(2)}, u32[]{:S(2)}) collective-permute-start(bf16[784,128]{1,0:T(8,128)(2,1)S(1)} %get-tuple-element.28), channel_id=1, source_target_pairs={{0,12},{1,13},{2,6},{3,7},{4,0},{5,1},{6,10},{7,11},{8,4},{9,5},{1... | collective-permute-start | bytes 602120 | tf_op jit(solution)/shard_map/ppermute | solution.py:290
  8.1 0.0 collective-permute-done._.other_ref
  8.1 0.0 copy-done.1
  8.1 0.0 copy-done
  8.1 0.1 weights.1
  8.2 0.1 collective-permute-start.3
  8.3 1.3 %collective-permute-start.4 = (bf16[784,128]{1,0:T(8,128)(2,1)S(1)}, bf16[784,128]{1,0:T(8,128)(2,1)S(1)}, u32[]{:S(2)}, u32[]{:S(2)}) collective-permute-start(bf16[784,128]{1,0:T(8,128)(2,1)S(1)} %get-tuple-element.30), channel_id=1, source_target_pairs={{2,7},{3,6},{4,1},{5,0},{6,11},{7,10},{8,5},{9,4},{10,15},{11,14},... | collective-permute-start | bytes 602120 | tf_op jit(solution)/shard_map/ppermute | solution.py:301
  10.3 2.4 %local.1 = (f32[1024,256]{1,0:T(8,128)S(1)}, bf16[2,256,384]{2,1,0:T(8,128)(2,1)S(1)}) custom-call(bf16[8,3,128,128]{3,2,1,0:T(8,128)(2,1)S(1)} %get-tuple-element.26.tr.own_ref, bf16[8,3,128,128]{3,2,1,0:T(8,128)(2,1)S(1)} %collective-permute-done._.other_ref, f32[8,128]{1,0:T(8,128)S(1)} %get-tuple-element.31.weight_ref, s32[1]{0:T(128)S(6)} %copy.5.jb_ref.refs_5_), custom_call_target="tpu_custom_call" | custom-call | flops 900000000 | bytes 2400000 | tf_op jit(solution)/shard_map/local/pallas_call | solution.py:305
  12.7 0.0 collective-permute-done.1.xs_ref.refs_0_
  12.7 0.0 collective-permute-done.2._.refs_1_
  12.7 2.8 %collective-permute-done.3.xc_ref.refs_2_ = bf16[784,128]{1,0:T(8,128)(2,1)S(1)} collective-permute-done((bf16[784,128]{1,0:T(8,128)(2,1)S(1)}, bf16[784,128]{1,0:T(8,128)(2,1)S(1)}, u32[]{:S(2)}, u32[]{:S(2)}) %collective-permute-start.3) | collective-permute-done | bytes 200736 | tf_op jit(solution)/shard_map/ppermute | solution.py:300
  15.5 0.8 %early.1 = (f32[1024,256]{1,0:T(8,128)S(1)}, bf16[256,768]{1,0:T(8,128)(2,1)S(1)}) custom-call(bf16[8,3,128,128]{3,2,1,0:T(8,128)(2,1)S(1)} %get-tuple-element.26.tr.own_ref, bf16[8,3,128,128]{3,2,1,0:T(8,128)(2,1)S(1)} %collective-permute-done._.other_ref, bf16[784,128]{1,0:T(8,128)(2,1)S(1)} %collective-permute-done.1.xs_ref.refs_0_, ...), custom_call_target="tpu_custom_call" | custom-call | flops 600000000 | bytes 2400000 | tf_op jit(solution)/shard_map/early/pallas_call | solution.py:322
  16.3 1.1 %collective-permute-done.4.refs_3_ = bf16[784,128]{1,0:T(8,128)(2,1)S(1)} collective-permute-done((bf16[784,128]{1,0:T(8,128)(2,1)S(1)}, bf16[784,128]{1,0:T(8,128)(2,1)S(1)}, u32[]{:S(2)}, u32[]{:S(2)}) %collective-permute-start.4) | collective-permute-done | bytes 200736 | tf_op jit(solution)/shard_map/ppermute | solution.py:301
  17.4 0.6 %cross.2 = (f32[2,2,4,32,128]{4,3,2,1,0:T(8,128)S(1)}, bf16[2,2,4,32,128]{4,3,2,1,0:T(8,128)(2,1)S(1)}, bf16[256,1536]{1,0:T(8,128)(2,1)S(1)}) custom-call(bf16[8,3,128,128]{3,2,1,0:T(8,128)(2,1)S(1)} %get-tuple-element.26.tr.own_ref, bf16[8,3,128,128]{3,2,1,0:T(8,128)(2,1)S(1)} %collective-permute-done._.other_ref, ...), custom_call_target="tpu_custom_call" | custom-call | flops 900000000 | bytes 4000000 | tf_op jit(solution)/shard_map/cross/pallas_call | solution.py:344
  18.1 0.2 collective-permute-start.6
  18.3 0.6 %cross.3 = (f32[2,2,4,32,128]{4,3,2,1,0:T(8,128)S(1)}, bf16[2,2,4,32,128]{4,3,2,1,0:T(8,128)(2,1)S(1)}) custom-call(bf16[8,3,128,128]{3,2,1,0:T(8,128)(2,1)S(1)} %get-tuple-element.26.tr.own_ref, bf16[8,3,128,128]{3,2,1,0:T(8,128)(2,1)S(1)} %collective-permute-done._.other_ref, bf16[784,128]{1,0:T(8,128)(2,1)S(1)} %collective-permute-done.1.xs_ref.refs_0_, ...), custom_call_target="tpu_custom_call" | custom-call | flops 900000000 | bytes 4000000 | tf_op jit(solution)/shard_map/cross/pallas_call | solution.py:344
  18.9 0.5 %collective-permute-start.5 = (bf16[2,2,4,32,128]{4,3,2,1,0:T(8,128)(2,1)S(1)}, bf16[2,2,4,32,128]{4,3,2,1,0:T(8,128)(2,1)S(1)}, u32[]{:S(2)}, u32[]{:S(2)}) collective-permute-start(bf16[2,2,4,32,128]{4,3,2,1,0:T(8,128)(2,1)S(1)} %get-tuple-element.38), channel_id=1, source_target_pairs={{0,1},{1,0},{2,3},{3,2},{4,5},{5,4},{6,7},{7,6},{8,9},{9,8},{10,11... | collective-permute-start | bytes 393224 | tf_op jit(solution)/shard_map/ppermute | solution.py:365
  19.4 0.1 collective-permute-done.6.got_ref
  19.5 0.1 collective-permute-start.7
  19.6 1.4 %collective-permute-start.8 = (bf16[2,4,32,128]{3,2,1,0:T(8,128)(2,1)S(1)}, bf16[2,4,32,128]{3,2,1,0:T(8,128)(2,1)S(1)}, u32[]{:S(2)}, u32[]{:S(2)}) collective-permute-start(bf16[2,4,32,128]{3,2,1,0:T(8,128)(2,1)S(1)} %get-tuple-element.43), channel_id=1, source_target_pairs={{0,4},{2,6},{4,0},{6,2},{8,12},{10,14},{12,8},{14,10},{1,5},{3,7},... | collective-permute-start | bytes 196616 | tf_op jit(solution)/shard_map/ppermute | solution.py:381
  21.0 0.0 collective-permute-done.5.got_ref
  21.0 2.2 %collective-permute-start.9 = (bf16[2,4,32,128]{3,2,1,0:T(8,128)(2,1)S(1)}, bf16[2,4,32,128]{3,2,1,0:T(8,128)(2,1)S(1)}, u32[]{:S(2)}, u32[]{:S(2)}) collective-permute-start(bf16[2,4,32,128]{3,2,1,0:T(8,128)(2,1)S(1)} %get-tuple-element.44), channel_id=1, source_target_pairs={{0,6},{2,4},{4,2},{6,0},{8,14},{10,12},{12,10},{14,8},{1,7},{3,5},... | collective-permute-start | bytes 196616 | tf_op jit(solution)/shard_map/ppermute | solution.py:381
  23.2 0.7 %collective-permute-done.7.refs_0_ = bf16[2,4,32,128]{3,2,1,0:T(8,128)(2,1)S(1)} collective-permute-done((bf16[2,4,32,128]{3,2,1,0:T(8,128)(2,1)S(1)}, bf16[2,4,32,128]{3,2,1,0:T(8,128)(2,1)S(1)}, u32[]{:S(2)}, u32[]{:S(2)}) %collective-permute-start.7) | collective-permute-done | bytes 65568 | tf_op jit(solution)/shard_map/ppermute | solution.py:381
  23.9 0.5 %collective-permute-done.8.refs_1_ = bf16[2,4,32,128]{3,2,1,0:T(8,128)(2,1)S(1)} collective-permute-done((bf16[2,4,32,128]{3,2,1,0:T(8,128)(2,1)S(1)}, bf16[2,4,32,128]{3,2,1,0:T(8,128)(2,1)S(1)}, u32[]{:S(2)}, u32[]{:S(2)}) %collective-permute-start.8) | collective-permute-done | bytes 65568 | tf_op jit(solution)/shard_map/ppermute | solution.py:381
  24.3 2.1 %collective-permute-done.9.refs_2_ = bf16[2,4,32,128]{3,2,1,0:T(8,128)(2,1)S(1)} collective-permute-done((bf16[2,4,32,128]{3,2,1,0:T(8,128)(2,1)S(1)}, bf16[2,4,32,128]{3,2,1,0:T(8,128)(2,1)S(1)}, u32[]{:S(2)}, u32[]{:S(2)}) %collective-permute-start.9) | collective-permute-done | bytes 65568 | tf_op jit(solution)/shard_map/ppermute | solution.py:381
  26.4 1.7 %collective-permute-start.10 = (bf16[4,32,128]{2,1,0:T(8,128)(2,1)S(1)}, bf16[4,32,128]{2,1,0:T(8,128)(2,1)S(1)}, u32[]{:S(2)}, u32[]{:S(2)}) collective-permute-start(bf16[4,32,128]{2,1,0:T(8,128)(2,1)S(1)} %get-tuple-element.46), channel_id=1, source_target_pairs={{0,8},{2,10},{4,12},{6,14},{8,0},{10,2},{12,4},{14,6},{1,9},{3,11}... | collective-permute-start | bytes 98312 | tf_op jit(solution)/shard_map/ppermute | solution.py:392
  28.2 3.5 %collective-permute-done.10.got_ref = bf16[4,32,128]{2,1,0:T(8,128)(2,1)S(1)} collective-permute-done((bf16[4,32,128]{2,1,0:T(8,128)(2,1)S(1)}, bf16[4,32,128]{2,1,0:T(8,128)(2,1)S(1)}, u32[]{:S(2)}, u32[]{:S(2)}) %collective-permute-start.10) | collective-permute-done | bytes 32800 | tf_op jit(solution)/shard_map/ppermute | solution.py:392
  31.7 0.7 %total.1 = f32[32,4,128]{2,1,0:T(4,128)} custom-call(f32[4,32,128]{2,1,0:T(8,128)S(1)} %get-tuple-element.45.keep_ref, bf16[4,32,128]{2,1,0:T(8,128)(2,1)S(1)} %collective-permute-done.10.got_ref), custom_call_target="tpu_custom_call" | custom-call | tf_op jit(solution)/shard_map/total/pallas_call | solution.py:393
  (4 shorter events, 0.1 us)
Async XLA Ops:
  0.0 8.1 %copy-start.1 = (f32[16]{0:T(128)S(1)}, f32[16]{0:T(128)}, u32[]{:S(2)}) copy-start(f32[16]{0:T(128)} %param.6) | copy-start | bytes 196
  1.4 6.7 %copy-start = (s32[1,8,128]{2,1,0:T(8,128)S(1)}, s32[1,8,128]{2,1,0:T(8,128)}, u32[]{:S(2)}) copy-start(s32[1,8,128]{2,1,0:T(8,128)} %ids_ref.1) | copy-start | bytes 12292
  1.4 6.7 %collective-permute-start = (bf16[8,3,128,128]{3,2,1,0:T(8,128)(2,1)S(1)}, bf16[8,3,128,128]{3,2,1,0:T(8,128)(2,1)S(1)}, u32[]{:S(2)}, u32[]{:S(2)}) collective-permute-start(bf16[8,3,128,128]{3,2,1,0:T(8,128)(2,1)S(1)} %get-tuple-element.26.tr.own_ref), channel_id=1, source_target_pairs={{0,1},{1,0},{2,3},{3,2},{4,5},{5,4},{6,7},{7,6},{8,9},{9,8},{10,11... | collective-permute-start | bytes 2359304 | tf_op jit(solution)/shard_map/ppermute | solution.py:288
  1.9 10.8 %collective-permute-start.1 = (bf16[784,128]{1,0:T(8,128)(2,1)S(1)}, bf16[784,128]{1,0:T(8,128)(2,1)S(1)}, u32[]{:S(2)}, u32[]{:S(2)}) collective-permute-start(bf16[784,128]{1,0:T(8,128)(2,1)S(1)} %get-tuple-element.27), channel_id=1, source_target_pairs={{0,2},{1,3},{2,0},{3,1},{4,6},{5,7},{6,4},{7,5},{8,10},{9,11},{10,... | collective-permute-start | bytes 602120 | tf_op jit(solution)/shard_map/ppermute | solution.py:289
  4.5 8.2 %collective-permute-start.2 = (bf16[784,128]{1,0:T(8,128)(2,1)S(1)}, bf16[784,128]{1,0:T(8,128)(2,1)S(1)}, u32[]{:S(2)}, u32[]{:S(2)}) collective-permute-start(bf16[784,128]{1,0:T(8,128)(2,1)S(1)} %get-tuple-element.28), channel_id=1, source_target_pairs={{0,12},{1,13},{2,6},{3,7},{4,0},{5,1},{6,10},{7,11},{8,4},{9,5},{1... | collective-permute-start | bytes 602120 | tf_op jit(solution)/shard_map/ppermute | solution.py:290
  8.2 7.3 %collective-permute-start.3 = (bf16[784,128]{1,0:T(8,128)(2,1)S(1)}, bf16[784,128]{1,0:T(8,128)(2,1)S(1)}, u32[]{:S(2)}, u32[]{:S(2)}) collective-permute-start(bf16[784,128]{1,0:T(8,128)(2,1)S(1)} %get-tuple-element.29), channel_id=1, source_target_pairs={{0,3},{1,2},{2,1},{3,0},{4,7},{5,6},{6,5},{7,4},{8,11},{9,10},{10,... | collective-permute-start | bytes 602120 | tf_op jit(solution)/shard_map/ppermute | solution.py:300
  8.3 9.1 %collective-permute-start.4 = (bf16[784,128]{1,0:T(8,128)(2,1)S(1)}, bf16[784,128]{1,0:T(8,128)(2,1)S(1)}, u32[]{:S(2)}, u32[]{:S(2)}) collective-permute-start(bf16[784,128]{1,0:T(8,128)(2,1)S(1)} %get-tuple-element.30), channel_id=1, source_target_pairs={{2,7},{3,6},{4,1},{5,0},{6,11},{7,10},{8,5},{9,4},{10,15},{11,14},... | collective-permute-start | bytes 602120 | tf_op jit(solution)/shard_map/ppermute | solution.py:301
  18.1 1.4 %collective-permute-start.6 = (bf16[2,2,4,32,128]{4,3,2,1,0:T(8,128)(2,1)S(1)}, bf16[2,2,4,32,128]{4,3,2,1,0:T(8,128)(2,1)S(1)}, u32[]{:S(2)}, u32[]{:S(2)}) collective-permute-start(bf16[2,2,4,32,128]{4,3,2,1,0:T(8,128)(2,1)S(1)} %get-tuple-element.41), channel_id=1, source_target_pairs={{0,1},{1,0},{2,3},{3,2},{4,5},{5,4},{6,7},{7,6},{8,9},{9,8},{10,11... | collective-permute-start | bytes 393224 | tf_op jit(solution)/shard_map/ppermute | solution.py:363
  18.9 2.1 %collective-permute-start.5 = (bf16[2,2,4,32,128]{4,3,2,1,0:T(8,128)(2,1)S(1)}, bf16[2,2,4,32,128]{4,3,2,1,0:T(8,128)(2,1)S(1)}, u32[]{:S(2)}, u32[]{:S(2)}) collective-permute-start(bf16[2,2,4,32,128]{4,3,2,1,0:T(8,128)(2,1)S(1)} %get-tuple-element.38), channel_id=1, source_target_pairs={{0,1},{1,0},{2,3},{3,2},{4,5},{5,4},{6,7},{7,6},{8,9},{9,8},{10,11... | collective-permute-start | bytes 393224 | tf_op jit(solution)/shard_map/ppermute | solution.py:365
  19.5 4.3 %collective-permute-start.7 = (bf16[2,4,32,128]{3,2,1,0:T(8,128)(2,1)S(1)}, bf16[2,4,32,128]{3,2,1,0:T(8,128)(2,1)S(1)}, u32[]{:S(2)}, u32[]{:S(2)}) collective-permute-start(bf16[2,4,32,128]{3,2,1,0:T(8,128)(2,1)S(1)} %get-tuple-element.42), channel_id=1, source_target_pairs={{0,2},{2,0},{4,6},{6,4},{8,10},{10,8},{12,14},{14,12},{1,3},{3,1},... | collective-permute-start | bytes 196616 | tf_op jit(solution)/shard_map/ppermute | solution.py:381
  19.6 4.7 %collective-permute-start.8 = (bf16[2,4,32,128]{3,2,1,0:T(8,128)(2,1)S(1)}, bf16[2,4,32,128]{3,2,1,0:T(8,128)(2,1)S(1)}, u32[]{:S(2)}, u32[]{:S(2)}) collective-permute-start(bf16[2,4,32,128]{3,2,1,0:T(8,128)(2,1)S(1)} %get-tuple-element.43), channel_id=1, source_target_pairs={{0,4},{2,6},{4,0},{6,2},{8,12},{10,14},{12,8},{14,10},{1,5},{3,7},... | collective-permute-start | bytes 196616 | tf_op jit(solution)/shard_map/ppermute | solution.py:381
  21.0 5.4 %collective-permute-start.9 = (bf16[2,4,32,128]{3,2,1,0:T(8,128)(2,1)S(1)}, bf16[2,4,32,128]{3,2,1,0:T(8,128)(2,1)S(1)}, u32[]{:S(2)}, u32[]{:S(2)}) collective-permute-start(bf16[2,4,32,128]{3,2,1,0:T(8,128)(2,1)S(1)} %get-tuple-element.44), channel_id=1, source_target_pairs={{0,6},{2,4},{4,2},{6,0},{8,14},{10,12},{12,10},{14,8},{1,7},{3,5},... | collective-permute-start | bytes 196616 | tf_op jit(solution)/shard_map/ppermute | solution.py:381
  26.4 5.2 %collective-permute-start.10 = (bf16[4,32,128]{2,1,0:T(8,128)(2,1)S(1)}, bf16[4,32,128]{2,1,0:T(8,128)(2,1)S(1)}, u32[]{:S(2)}, u32[]{:S(2)}) collective-permute-start(bf16[4,32,128]{2,1,0:T(8,128)(2,1)S(1)} %get-tuple-element.46), channel_id=1, source_target_pairs={{0,8},{2,10},{4,12},{6,14},{8,0},{10,2},{12,4},{14,6},{1,9},{3,11}... | collective-permute-start | bytes 98312 | tf_op jit(solution)/shard_map/ppermute | solution.py:392

commit v18 on v15

--- a/solution.py
+++ b/solution.py
@@ -11,9 +11,16 @@
 NW = 16
 PADROWS = 16
 LOADS = 4
+X_FIRST = 0b10011111
 NEAR = 4
 VMEM_LIMIT = 48 * 1024 * 1024
 PREP_LIMIT = 53_600 * 1024
+
+
+def x_first(s, planes):
+    if planes != 8:
+        return s >= 0
+    return lax.rem(lax.shift_right_logical(X_FIRST, s), 2) == 1
 
 
 def copy_rows(ref, tr, at):
@@ -23,9 +30,10 @@
             ref[pl.ds((row * comps + c) * nk, nk), :] = tr[at * (nx // 4) + row, c]
 
 
-def prep_kernel(modes_hbm, tr, xs_ref, zs_ref, modes_ref, sems):
+def prep_kernel(planes, modes_hbm, tr, first_ref, second_ref, modes_ref, sems):
     m = lax.axis_index("modes")
-    q = lax.rem(lax.axis_index("space"), 2)
+    s = lax.axis_index("space")
+    q = lax.rem(s, 2)
     nk, comps, _, nx, nz = modes_hbm.shape
     step = nk // LOADS
     copies = [
@@ -43,7 +51,12 @@
             value = modes_ref[block, c, 0].astype(jnp.float32)
             tr[:, c, block] = jnp.swapaxes(value, 0, 1).astype(jnp.bfloat16)
     body = nx // 4 * comps * nk
-    for ref, at in ((xs_ref, 2 * m + 1 - q), (zs_ref, 2 * m + q)):
+    to_x, to_z = 2 * m + 1 - q, 2 * m + q
+    x_now = x_first(s, planes)
+    for ref, at in (
+        (first_ref, jnp.where(x_now, to_x, to_z)),
+        (second_ref, jnp.where(x_now, to_z, to_x)),
+    ):
         copy_rows(ref, tr, at)
         ref[pl.ds(body, PADROWS), :] = jnp.zeros((PADROWS, nz), jnp.bfloat16)
 
@@ -94,9 +107,8 @@
 
 def picked(pick, own, other):
     mine, block, within = pick
-    rows = jnp.where(
-        mine, own[pl.ds(block, 16), :].astype(jnp.float32), other[pl.ds(block, 16), :].astype(jnp.float32)
-    )
+    rows = pl.ds(block, 16)
+    rows = jnp.where(mine, own(rows).astype(jnp.float32), other(rows).astype(jnp.float32))
     result = rows[0:JB]
     for start in range(JB, 16, JB):
         result = jnp.where(within == start, rows[start : start + JB], result)
@@ -125,7 +137,7 @@
     for r in range(rows):
         row = rows * m + r
         below, above = lax.rem(row + nx - 1, nx), lax.rem(row + 1, nx)
-        phi = [picked(pick, own_ref.at[row, d], other_ref.at[row, d]) for d in range(comps)]
+        phi = [picked(pick, lambda at: own_ref[row, d, at, :], lambda at: other_ref[row, d, at, :]) for d in range(comps)]
         weight = weight_ref[pl.ds(row, 1), :]
         for c in range(comps):
             for half, ref in enumerate((own_ref, other_ref)):
@@ -148,11 +160,22 @@
         w0_ref[r] = wts[quarter * q + r]
 
 
+def same_core_rows(planes, first_ref, second_ref):
+    x_came = x_first(jnp.bitwise_xor(lax.axis_index("space"), 1), planes)
+    return (
+        lambda rows: jnp.where(x_came, first_ref[rows, :], second_ref[rows, :]),
+        lambda rows: jnp.where(x_came, second_ref[rows, :], first_ref[rows, :]),
+    )
+
+
 def sign_of_plane():
     return jnp.where(lax.rem(lax.axis_index("space"), 2) == 0, 0.5, -0.5)
 
 
-def early_kernel(own_ref, other_ref, xs_ref, _, xc_ref, w0_ref, jb_ref, acc_ref, out_ref, w1_ref, adv):
+def early_kernel(
+    planes, own_ref, other_ref, first_ref, second_ref, xc_ref, w0_ref, jb_ref, acc_ref, out_ref, w1_ref, adv
+):
+    xs_rows, _ = same_core_rows(planes, first_ref, second_ref)
     m = lax.axis_index("modes")
     q = lax.rem(lax.axis_index("space"), 2)
     nx, comps, nk, nz = own_ref.shape
@@ -161,13 +184,14 @@
     weights = received_weights(xc_ref, quarter * comps * nk, quarter)
     for r in range(quarter):
         row0 = quarter * (2 * m + q) + r
-        phi0 = sign_of_plane() * picked(pick, own_ref.at[row0, 1], other_ref.at[row0, 1])
+        phi0 = sign_of_plane() * picked(
+            pick, lambda at: own_ref[row0, 1, at, :], lambda at: other_ref[row0, 1, at, :]
+        )
         phi0 = [spread(phi0[j : j + 1]) for j in range(JB)]
         for c in range(comps):
             at = pl.ds((r * comps + c) * nz, nz)
             src = pl.ds((r * comps + c) * nk, nk)
-            for half, p1 in enumerate((xs_ref, xc_ref)):
-                f1 = p1[src, :]
+            for half, f1 in enumerate((xs_rows(src), xc_ref[src, :])):
                 w1_ref[pl.ds(half * nk, nk), at] = (weights[r] * f1.astype(jnp.float32)).astype(
                     jnp.bfloat16
                 )
@@ -180,7 +204,8 @@
 
 
 def cross_kernel(classes_of, chunk, planes, has_weighted, own_ref, other_ref, *refs):
-    xs_ref, zs_ref, xc_ref, zc_ref, w1_ref, jb_ref, acc_ref, *refs = refs
+    first_ref, second_ref, xc_ref, zc_ref, w1_ref, jb_ref, acc_ref, *refs = refs
+    xs_rows, zs_rows = same_core_rows(planes, first_ref, second_ref)
     if has_weighted:
         wts, keep_ref, send_ref, adv = refs
     else:
@@ -201,15 +226,23 @@
             weight = inside * weights[r]
             for c in range(comps):
                 src = pl.ds((r * comps + c) * nk, nk)
-                for half, p2 in enumerate((zs_ref, zc_ref)):
+                for half, f2 in enumerate((zs_rows(src), zc_ref[src, :])):
                     wts[pl.ds(half * nk, nk), pl.ds(span + (r * comps + c) * nz, nz)] = (
-                        weight * p2[src, :].astype(jnp.float32)
+                        weight * f2.astype(jnp.float32)
                     ).astype(jnp.bfloat16)
     phis = []
     for r in range(quarter):
-        along = pl.ds((r * comps + 1) * nk, nk)
-        phi1 = sign_of_plane() * picked(pick, xs_ref.at[along], xc_ref.at[along])
-        phi2 = -sign_of_plane() * picked(pick, zs_ref.at[along], zc_ref.at[along])
+        along = (r * comps + 1) * nk
+
+        def moved(at):
+            return pl.ds(pl.multiple_of(along + at.start, 16), at.size)
+
+        phi1 = sign_of_plane() * picked(
+            pick, lambda at: xs_rows(moved(at)), lambda at: xc_ref[moved(at), :]
+        )
+        phi2 = -sign_of_plane() * picked(
+            pick, lambda at: zs_rows(moved(at)), lambda at: zc_ref[moved(at), :]
+        )
         phis.append([[spread(phi[j : j + 1]) for j in range(JB)] for phi in (phi1, phi2)])
     inside = inside.astype(jnp.bfloat16)
     for at, cls in enumerate(classes):
@@ -219,12 +252,15 @@
             for c in range(comps):
                 lane = (r * comps + c) * nz
                 src = (r * comps + c) * nk
-                for half, (p0, p1, p2) in enumerate(
-                    ((own_ref, xs_ref, zs_ref), (other_ref, xc_ref, zc_ref))
+                rows_at = pl.ds(pl.multiple_of(src + cls, 16), chunk)
+                for half, (p0, f1, f2) in enumerate(
+                    (
+                        (own_ref, xs_rows(rows_at), zs_rows(rows_at)),
+                        (other_ref, xc_ref[rows_at, :], zc_ref[rows_at, :]),
+                    )
                 ):
                     f0 = p0[row0, c, pl.ds(cls, chunk), :]
-                    f1 = p1[pl.ds(src + cls, chunk), :]
-                    gy = inside * p2[pl.ds(src + cls, chunk), :] - f0
+                    gy = inside * f2 - f0
                     for j in range(JB):
                         here = pl.ds((half * JB + j) * chunk, chunk)
                         adv[at, here, pl.ds(lane, nz)] = scaled(phi1[j], gy)
@@ -268,8 +304,8 @@
     params = pltpu.CompilerParams(vmem_limit_bytes=VMEM_LIMIT)
     quarter = nx // 4
     body = quarter * comps * nk
-    own, xs, zs = pl.pallas_call(
-        prep_kernel,
+    own, first, second = pl.pallas_call(
+        functools.partial(prep_kernel, n),
         out_shape=[jax.ShapeDtypeStruct((nx, comps, nk, nz), bf16)]
         + [jax.ShapeDtypeStruct((body + PADROWS, nz), bf16)] * 2,
         in_specs=[pl.BlockSpec(memory_space=pltpu.HBM)],
@@ -281,13 +317,16 @@
     )(modes)
 
     both = ("space", "modes")
-    x_pairs = [(s, s ^ 1) for s in range(n)]
-    z_pairs = [(s, (s + (2 if s % 2 else -2)) % n) for s in range(n)]
+    x_to = lambda s: s ^ 1
+    z_to = lambda s: s + 2 if s % 2 else s - 2
+    x_now = [n != 8 or X_FIRST >> s & 1 for s in range(n)]
+    firsts = [(s, x_to(s) if x_now[s] else z_to(s)) for s in range(n)]
+    seconds = [(s, z_to(s) % n if x_now[s] else x_to(s)) for s in range(n)]
     same = lambda pairs: [(2 * a + m, 2 * b + m) for a, b in pairs for m in range(2)]
     cross = lambda pairs: [(2 * a + m, 2 * b + 1 - m) for a, b in pairs for m in range(2)]
     other = lax.ppermute(own, "modes", [(0, 1), (1, 0)])
-    xs = lax.ppermute(xs, both, same(x_pairs))
-    zs = lax.ppermute(zs, both, same(z_pairs))
+    first = lax.ppermute(first, both, same(firsts))
+    second = lax.ppermute(second, both, same(seconds))
     weight, xc, zc = pl.pallas_call(
         weights_kernel,
         out_shape=[jax.ShapeDtypeStruct((nx, nz), f32)]
@@ -297,8 +336,8 @@
         compiler_params=params,
         name="weights",
     )(weight_ids, jnp.broadcast_to(weight_table[None], (8, NW)), own, other)
-    xc = lax.ppermute(xc, both, cross(x_pairs))
-    zc = lax.ppermute(zc, both, cross([(s, to) for s, to in z_pairs if abs(s - to) == 2]))
+    xc = lax.ppermute(xc, both, cross([(s, x_to(s)) for s in range(n)]))
+    zc = lax.ppermute(zc, both, cross([(s, z_to(s)) for s in range(n) if 0 <= z_to(s) < n]))
 
     depth = nx // 4 * comps * nz
     depth = quarter * comps * nz
@@ -320,18 +359,18 @@
     )(own, other, weight, j_block)
 
     acc, w1 = pl.pallas_call(
-        early_kernel,
+        functools.partial(early_kernel, n),
         out_shape=[
             jax.ShapeDtypeStruct((JB * 2 * nk, 2 * nk), f32),
             jax.ShapeDtypeStruct((2 * nk, depth), bf16),
         ],
-        in_specs=[vmem] * 3 + [pl.BlockSpec(memory_space=pl.ANY), vmem, vmem, smem, vmem],
+        in_specs=[vmem] * 6 + [smem, vmem],
         out_specs=[vmem] * 2,
         scratch_shapes=[pltpu.VMEM((quarter, JB * 2 * nk, comps * nz), bf16)],
         compiler_params=params,
         cost_estimate=pl.CostEstimate(flops=600_000_000, bytes_accessed=2_400_000, transcendentals=0),
         name="early",
-    )(own, other, xs, zs, xc, w0, j_block, acc)
+    )(own, other, first, second, xc, w0, j_block, acc)
 
     per_target = 2 * nk // n
     chunk = max(16, per_target)
@@ -352,7 +391,7 @@
                 flops=900_000_000, bytes_accessed=4_000_000, transcendentals=0
             ),
             name="cross",
-        )(own, other, xs, zs, xc, zc, w1, j_block, acc, *weighted)
+        )(own, other, first, second, xc, zc, w1, j_block, acc, *weighted)
 
     swap = [(0, 1), (1, 0)]
     if n == 2 * NEAR:

time: 31.4 us -> 31.3 us (level)
  starting transfers between devices: 13.8 us -> 13.3 us
  waiting for transfers between devices: 9.98 us -> 10.4 us
    ppermute x4, starting transfers between devices: 7.53 us -> 6.49 us  [the longest x1 2.6 us: on_device(): second = lax.ppermute(second, both, same(seconds))]
    ppermute x3, waiting for transfers between devices: 2.51 us -> 3.27 us  [on_device(): lax.ppermute(part, 'space', [(s, s ^ step) for s in range(n)])]
    ppermute x1, starting transfers between devices: 1.48 us -> 2.01 us  [on_device(): got = lax.ppermute(send, 'space', [(s, s ^ NEAR) for s in range(n)])]
    ppermute x1, waiting for transfers between devices: 3.4 us -> 2.87 us  [on_device(): got = lax.ppermute(send, 'space', [(s, s ^ NEAR) for s in range(n)])]
  transfers between devices with their start and end apart: 11 -> 11, of which waited for: 6 -> 7; matrix products, arithmetic and copies ran while one was open for 0% -> 0% of each run, Pallas kernels for 13% -> 13%
where the time goes in v18:
time: 31.3 us; the launch traced here: 31.2 us
  starting transfers between devices  13.3 us (42%)
  waiting for transfers between devices  10.4 us (33%)
  Pallas kernels  6.77 us (22%)
  between operations  0.75 us (2%)
    ppermute x3, starting transfers between devices, on_device(): lax.ppermute(part, 'space', [(s, s ^ step) for s in range(n)])  3.62 us
    ppermute x3, waiting for transfers between devices, on_device(): lax.ppermute(part, 'space', [(s, s ^ step) for s in range(n)])  3.27 us
    ppermute x1, waiting for transfers between devices, on_device(): got = lax.ppermute(send, 'space', [(s, s ^ NEAR) for s in range(n)])  2.87 us
    ppermute x1, waiting for transfers between devices, on_device(): xc = lax.ppermute(xc, both, cross([(s, x_to(s)) for s in range(n)]))  2.81 us
    ppermute x1, starting transfers between devices, on_device(): second = lax.ppermute(second, both, same(seconds))  2.6 us
    ppermute x1, starting transfers between devices, on_device(): first = lax.ppermute(first, both, same(firsts))  2.53 us
    pallas_call x1, Pallas kernels, on_device(): pl.pallas_call(local_kernel, out_shape=[jax.ShapeDtypeStruct((JB * 2 * nk...  2.43 us
    ppermute x1, starting transfers between devices, on_device(): got = lax.ppermute(send, 'space', [(s, s ^ NEAR) for s in range(n)])  2.01 us
  transfers between devices with their start and end apart: 11, of which 7 were waited for; matrix products, arithmetic and copies ran while one was open for 0% of the time, Pallas kernels for 13%

profile of v18, /device:TPU:0, one launch (start us, length us, event | category | flops | bytes accessed | tf_op | source)
XLA Modules:
  0.0 31.2 jit_solution(12230099743107418631)
XLA Ops:
  0.0 0.0 copy-start.1
  0.0 1.4 %prep.1 = (bf16[8,3,128,128]{3,2,1,0:T(8,128)(2,1)S(1)}, bf16[784,128]{1,0:T(8,128)(2,1)S(1)}, bf16[784,128]{1,0:T(8,128)(2,1)S(1)}) custom-call(bf16[128,3,1,8,128]{4,3,2,1,0:T(8,128)(2,1)} %modes_hbm.1), custom_call_target="tpu_custom_call" | custom-call | flops 1500000000 | bytes 2800000 | tf_op jit(solution)/shard_map/prep/pallas_call | solution.py:307
  1.4 0.0 copy-start
  1.4 0.5 %collective-permute-start = (bf16[8,3,128,128]{3,2,1,0:T(8,128)(2,1)S(1)}, bf16[8,3,128,128]{3,2,1,0:T(8,128)(2,1)S(1)}, u32[]{:S(2)}, u32[]{:S(2)}) collective-permute-start(bf16[8,3,128,128]{3,2,1,0:T(8,128)(2,1)S(1)} %get-tuple-element.26.tr.own_ref), channel_id=1, source_target_pairs={{0,1},{1,0},{2,3},{3,2},{4,5},{5,4},{6,7},{7,6},{8,9},{9,8},{10,11... | collective-permute-start | bytes 2359304 | tf_op jit(solution)/shard_map/ppermute | solution.py:327
  1.9 2.5 %collective-permute-start.1 = (bf16[784,128]{1,0:T(8,128)(2,1)S(1)}, bf16[784,128]{1,0:T(8,128)(2,1)S(1)}, u32[]{:S(2)}, u32[]{:S(2)}) collective-permute-start(bf16[784,128]{1,0:T(8,128)(2,1)S(1)} %get-tuple-element.27), channel_id=1, source_target_pairs={{0,2},{1,3},{2,0},{3,1},{4,6},{5,7},{6,4},{7,5},{8,10},{9,11},{10,... | collective-permute-start | bytes 602120 | tf_op jit(solution)/shard_map/ppermute | solution.py:328
  4.5 2.6 %collective-permute-start.2 = (bf16[784,128]{1,0:T(8,128)(2,1)S(1)}, bf16[784,128]{1,0:T(8,128)(2,1)S(1)}, u32[]{:S(2)}, u32[]{:S(2)}) collective-permute-start(bf16[784,128]{1,0:T(8,128)(2,1)S(1)} %get-tuple-element.28), channel_id=1, source_target_pairs={{0,12},{1,13},{2,6},{3,7},{4,0},{5,1},{6,10},{7,11},{8,4},{9,5},{1... | collective-permute-start | bytes 602120 | tf_op jit(solution)/shard_map/ppermute | solution.py:329
  7.1 0.0 collective-permute-done._.other_ref
  7.1 0.0 copy-done.1
  7.1 0.0 copy-done
  7.1 0.1 weights.1
  7.2 0.1 collective-permute-start.3
  7.3 1.3 %collective-permute-start.4 = (bf16[784,128]{1,0:T(8,128)(2,1)S(1)}, bf16[784,128]{1,0:T(8,128)(2,1)S(1)}, u32[]{:S(2)}, u32[]{:S(2)}) collective-permute-start(bf16[784,128]{1,0:T(8,128)(2,1)S(1)} %get-tuple-element.30), channel_id=1, source_target_pairs={{2,7},{3,6},{4,1},{5,0},{6,11},{7,10},{8,5},{9,4},{10,15},{11,14},... | collective-permute-start | bytes 602120 | tf_op jit(solution)/shard_map/ppermute | solution.py:340
  9.2 2.4 %local.1 = (f32[1024,256]{1,0:T(8,128)S(1)}, bf16[2,256,384]{2,1,0:T(8,128)(2,1)S(1)}) custom-call(bf16[8,3,128,128]{3,2,1,0:T(8,128)(2,1)S(1)} %get-tuple-element.26.tr.own_ref, bf16[8,3,128,128]{3,2,1,0:T(8,128)(2,1)S(1)} %collective-permute-done._.other_ref, f32[8,128]{1,0:T(8,128)S(1)} %get-tuple-element.31.weight_ref, s32[1]{0:T(128)S(6)} %copy.5.jb_ref.refs_5_), custom_call_target="tpu_custom_call" | custom-call | flops 900000000 | bytes 2400000 | tf_op jit(solution)/shard_map/local/pallas_call | solution.py:344
  11.7 0.0 collective-permute-done.1.first_ref.refs_0_
  11.7 0.0 collective-permute-done.2.second_ref.refs_1_
  11.7 2.8 %collective-permute-done.3.xc_ref.refs_2_ = bf16[784,128]{1,0:T(8,128)(2,1)S(1)} collective-permute-done((bf16[784,128]{1,0:T(8,128)(2,1)S(1)}, bf16[784,128]{1,0:T(8,128)(2,1)S(1)}, u32[]{:S(2)}, u32[]{:S(2)}) %collective-permute-start.3) | collective-permute-done | bytes 200736 | tf_op jit(solution)/shard_map/ppermute | solution.py:339
  14.5 0.8 %early.1 = (f32[1024,256]{1,0:T(8,128)S(1)}, bf16[256,768]{1,0:T(8,128)(2,1)S(1)}) custom-call(bf16[8,3,128,128]{3,2,1,0:T(8,128)(2,1)S(1)} %get-tuple-element.26.tr.own_ref, bf16[8,3,128,128]{3,2,1,0:T(8,128)(2,1)S(1)} %collective-permute-done._.other_ref, bf16[784,128]{1,0:T(8,128)(2,1)S(1)} %collective-permute-done.1.first_ref.refs_0_, ...), custom_call_target="tpu_custom_call" | custom-call | flops 600000000 | bytes 2400000 | tf_op jit(solution)/shard_map/early/pallas_call | solution.py:361
  15.3 1.3 %collective-permute-done.4.refs_3_ = bf16[784,128]{1,0:T(8,128)(2,1)S(1)} collective-permute-done((bf16[784,128]{1,0:T(8,128)(2,1)S(1)}, bf16[784,128]{1,0:T(8,128)(2,1)S(1)}, u32[]{:S(2)}, u32[]{:S(2)}) %collective-permute-start.4) | collective-permute-done | bytes 200736 | tf_op jit(solution)/shard_map/ppermute | solution.py:340
  16.5 0.7 %cross.2 = (f32[2,2,4,32,128]{4,3,2,1,0:T(8,128)S(1)}, bf16[2,2,4,32,128]{4,3,2,1,0:T(8,128)(2,1)S(1)}, bf16[256,1536]{1,0:T(8,128)(2,1)S(1)}) custom-call(bf16[8,3,128,128]{3,2,1,0:T(8,128)(2,1)S(1)} %get-tuple-element.26.tr.own_ref, bf16[8,3,128,128]{3,2,1,0:T(8,128)(2,1)S(1)} %collective-permute-done._.other_ref, ...), custom_call_target="tpu_custom_call" | custom-call | flops 900000000 | bytes 4000000 | tf_op jit(solution)/shard_map/cross/pallas_call | solution.py:383
  17.2 0.2 collective-permute-start.6
  17.4 0.6 %cross.3 = (f32[2,2,4,32,128]{4,3,2,1,0:T(8,128)S(1)}, bf16[2,2,4,32,128]{4,3,2,1,0:T(8,128)(2,1)S(1)}) custom-call(bf16[8,3,128,128]{3,2,1,0:T(8,128)(2,1)S(1)} %get-tuple-element.26.tr.own_ref, bf16[8,3,128,128]{3,2,1,0:T(8,128)(2,1)S(1)} %collective-permute-done._.other_ref, bf16[784,128]{1,0:T(8,128)(2,1)S(1)} %collective-permute-done.1.first_ref.refs_0_, ...), custom_call_target="tpu_custom_call" | custom-call | flops 900000000 | bytes 4000000 | tf_op jit(solution)/shard_map/cross/pallas_call | solution.py:383
  18.1 0.5 %collective-permute-start.5 = (bf16[2,2,4,32,128]{4,3,2,1,0:T(8,128)(2,1)S(1)}, bf16[2,2,4,32,128]{4,3,2,1,0:T(8,128)(2,1)S(1)}, u32[]{:S(2)}, u32[]{:S(2)}) collective-permute-start(bf16[2,2,4,32,128]{4,3,2,1,0:T(8,128)(2,1)S(1)} %get-tuple-element.38), channel_id=1, source_target_pairs={{0,1},{1,0},{2,3},{3,2},{4,5},{5,4},{6,7},{7,6},{8,9},{9,8},{10,11... | collective-permute-start | bytes 393224 | tf_op jit(solution)/shard_map/ppermute | solution.py:404
  18.5 0.1 collective-permute-done.6.got_ref
  18.7 1.5 %collective-permute-start.7 = (bf16[2,4,32,128]{3,2,1,0:T(8,128)(2,1)S(1)}, bf16[2,4,32,128]{3,2,1,0:T(8,128)(2,1)S(1)}, u32[]{:S(2)}, u32[]{:S(2)}) collective-permute-start(bf16[2,4,32,128]{3,2,1,0:T(8,128)(2,1)S(1)} %get-tuple-element.42), channel_id=1, source_target_pairs={{0,6},{2,4},{4,2},{6,0},{8,14},{10,12},{12,10},{14,8},{1,7},{3,5},... | collective-permute-start | bytes 196616 | tf_op jit(solution)/shard_map/ppermute | solution.py:420
  20.2 1.0 %collective-permute-start.8 = (bf16[2,4,32,128]{3,2,1,0:T(8,128)(2,1)S(1)}, bf16[2,4,32,128]{3,2,1,0:T(8,128)(2,1)S(1)}, u32[]{:S(2)}, u32[]{:S(2)}) collective-permute-start(bf16[2,4,32,128]{3,2,1,0:T(8,128)(2,1)S(1)} %get-tuple-element.43), channel_id=1, source_target_pairs={{0,2},{2,0},{4,6},{6,4},{8,10},{10,8},{12,14},{14,12},{1,3},{3,1},... | collective-permute-start | bytes 196616 | tf_op jit(solution)/shard_map/ppermute | solution.py:420
  21.2 0.0 collective-permute-done.5.got_ref
  21.3 1.1 %collective-permute-start.9 = (bf16[2,4,32,128]{3,2,1,0:T(8,128)(2,1)S(1)}, bf16[2,4,32,128]{3,2,1,0:T(8,128)(2,1)S(1)}, u32[]{:S(2)}, u32[]{:S(2)}) collective-permute-start(bf16[2,4,32,128]{3,2,1,0:T(8,128)(2,1)S(1)} %get-tuple-element.44), channel_id=1, source_target_pairs={{0,4},{2,6},{4,0},{6,2},{8,12},{10,14},{12,8},{14,10},{1,5},{3,7},... | collective-permute-start | bytes 196616 | tf_op jit(solution)/shard_map/ppermute | solution.py:420
  22.3 1.6 %collective-permute-done.7.refs_0_ = bf16[2,4,32,128]{3,2,1,0:T(8,128)(2,1)S(1)} collective-permute-done((bf16[2,4,32,128]{3,2,1,0:T(8,128)(2,1)S(1)}, bf16[2,4,32,128]{3,2,1,0:T(8,128)(2,1)S(1)}, u32[]{:S(2)}, u32[]{:S(2)}) %collective-permute-start.7) | collective-permute-done | bytes 65568 | tf_op jit(solution)/shard_map/ppermute | solution.py:420
  24.0 1.2 %collective-permute-done.8.refs_1_ = bf16[2,4,32,128]{3,2,1,0:T(8,128)(2,1)S(1)} collective-permute-done((bf16[2,4,32,128]{3,2,1,0:T(8,128)(2,1)S(1)}, bf16[2,4,32,128]{3,2,1,0:T(8,128)(2,1)S(1)}, u32[]{:S(2)}, u32[]{:S(2)}) %collective-permute-start.8) | collective-permute-done | bytes 65568 | tf_op jit(solution)/shard_map/ppermute | solution.py:420
  25.2 0.4 %collective-permute-done.9.refs_2_ = bf16[2,4,32,128]{3,2,1,0:T(8,128)(2,1)S(1)} collective-permute-done((bf16[2,4,32,128]{3,2,1,0:T(8,128)(2,1)S(1)}, bf16[2,4,32,128]{3,2,1,0:T(8,128)(2,1)S(1)}, u32[]{:S(2)}, u32[]{:S(2)}) %collective-permute-start.9) | collective-permute-done | bytes 65568 | tf_op jit(solution)/shard_map/ppermute | solution.py:420
  25.6 2.0 %collective-permute-start.10 = (bf16[4,32,128]{2,1,0:T(8,128)(2,1)S(1)}, bf16[4,32,128]{2,1,0:T(8,128)(2,1)S(1)}, u32[]{:S(2)}, u32[]{:S(2)}) collective-permute-start(bf16[4,32,128]{2,1,0:T(8,128)(2,1)S(1)} %get-tuple-element.46), channel_id=1, source_target_pairs={{0,8},{2,10},{4,12},{6,14},{8,0},{10,2},{12,4},{14,6},{1,9},{3,11}... | collective-permute-start | bytes 98312 | tf_op jit(solution)/shard_map/ppermute | solution.py:431
  27.6 2.9 %collective-permute-done.10.got_ref = bf16[4,32,128]{2,1,0:T(8,128)(2,1)S(1)} collective-permute-done((bf16[4,32,128]{2,1,0:T(8,128)(2,1)S(1)}, bf16[4,32,128]{2,1,0:T(8,128)(2,1)S(1)}, u32[]{:S(2)}, u32[]{:S(2)}) %collective-permute-start.10) | collective-permute-done | bytes 32800 | tf_op jit(solution)/shard_map/ppermute | solution.py:431
  30.5 0.7 %total.1 = f32[32,4,128]{2,1,0:T(4,128)} custom-call(f32[4,32,128]{2,1,0:T(8,128)S(1)} %get-tuple-element.45.keep_ref, bf16[4,32,128]{2,1,0:T(8,128)(2,1)S(1)} %collective-permute-done.10.got_ref), custom_call_target="tpu_custom_call" | custom-call | tf_op jit(solution)/shard_map/total/pallas_call | solution.py:432
  (4 shorter events, 0.1 us)
Async XLA Ops:
  0.0 7.1 %copy-start.1 = (f32[16]{0:T(128)S(1)}, f32[16]{0:T(128)}, u32[]{:S(2)}) copy-start(f32[16]{0:T(128)} %param.6) | copy-start | bytes 196
  1.4 5.7 %copy-start = (s32[1,8,128]{2,1,0:T(8,128)S(1)}, s32[1,8,128]{2,1,0:T(8,128)}, u32[]{:S(2)}) copy-start(s32[1,8,128]{2,1,0:T(8,128)} %ids_ref.1) | copy-start | bytes 12292
  1.4 5.7 %collective-permute-start = (bf16[8,3,128,128]{3,2,1,0:T(8,128)(2,1)S(1)}, bf16[8,3,128,128]{3,2,1,0:T(8,128)(2,1)S(1)}, u32[]{:S(2)}, u32[]{:S(2)}) collective-permute-start(bf16[8,3,128,128]{3,2,1,0:T(8,128)(2,1)S(1)} %get-tuple-element.26.tr.own_ref), channel_id=1, source_target_pairs={{0,1},{1,0},{2,3},{3,2},{4,5},{5,4},{6,7},{7,6},{8,9},{9,8},{10,11... | collective-permute-start | bytes 2359304 | tf_op jit(solution)/shard_map/ppermute | solution.py:327
  1.9 9.7 %collective-permute-start.1 = (bf16[784,128]{1,0:T(8,128)(2,1)S(1)}, bf16[784,128]{1,0:T(8,128)(2,1)S(1)}, u32[]{:S(2)}, u32[]{:S(2)}) collective-permute-start(bf16[784,128]{1,0:T(8,128)(2,1)S(1)} %get-tuple-element.27), channel_id=1, source_target_pairs={{0,2},{1,3},{2,0},{3,1},{4,6},{5,7},{6,4},{7,5},{8,10},{9,11},{10,... | collective-permute-start | bytes 602120 | tf_op jit(solution)/shard_map/ppermute | solution.py:328
  4.5 7.2 %collective-permute-start.2 = (bf16[784,128]{1,0:T(8,128)(2,1)S(1)}, bf16[784,128]{1,0:T(8,128)(2,1)S(1)}, u32[]{:S(2)}, u32[]{:S(2)}) collective-permute-start(bf16[784,128]{1,0:T(8,128)(2,1)S(1)} %get-tuple-element.28), channel_id=1, source_target_pairs={{0,12},{1,13},{2,6},{3,7},{4,0},{5,1},{6,10},{7,11},{8,4},{9,5},{1... | collective-permute-start | bytes 602120 | tf_op jit(solution)/shard_map/ppermute | solution.py:329
  7.2 7.3 %collective-permute-start.3 = (bf16[784,128]{1,0:T(8,128)(2,1)S(1)}, bf16[784,128]{1,0:T(8,128)(2,1)S(1)}, u32[]{:S(2)}, u32[]{:S(2)}) collective-permute-start(bf16[784,128]{1,0:T(8,128)(2,1)S(1)} %get-tuple-element.29), channel_id=1, source_target_pairs={{0,3},{1,2},{2,1},{3,0},{4,7},{5,6},{6,5},{7,4},{8,11},{9,10},{10,... | collective-permute-start | bytes 602120 | tf_op jit(solution)/shard_map/ppermute | solution.py:339
  7.3 9.3 %collective-permute-start.4 = (bf16[784,128]{1,0:T(8,128)(2,1)S(1)}, bf16[784,128]{1,0:T(8,128)(2,1)S(1)}, u32[]{:S(2)}, u32[]{:S(2)}) collective-permute-start(bf16[784,128]{1,0:T(8,128)(2,1)S(1)} %get-tuple-element.30), channel_id=1, source_target_pairs={{2,7},{3,6},{4,1},{5,0},{6,11},{7,10},{8,5},{9,4},{10,15},{11,14},... | collective-permute-start | bytes 602120 | tf_op jit(solution)/shard_map/ppermute | solution.py:340
  17.2 1.4 %collective-permute-start.6 = (bf16[2,2,4,32,128]{4,3,2,1,0:T(8,128)(2,1)S(1)}, bf16[2,2,4,32,128]{4,3,2,1,0:T(8,128)(2,1)S(1)}, u32[]{:S(2)}, u32[]{:S(2)}) collective-permute-start(bf16[2,2,4,32,128]{4,3,2,1,0:T(8,128)(2,1)S(1)} %get-tuple-element.41), channel_id=1, source_target_pairs={{0,1},{1,0},{2,3},{3,2},{4,5},{5,4},{6,7},{7,6},{8,9},{9,8},{10,11... | collective-permute-start | bytes 393224 | tf_op jit(solution)/shard_map/ppermute | solution.py:402
  18.1 3.2 %collective-permute-start.5 = (bf16[2,2,4,32,128]{4,3,2,1,0:T(8,128)(2,1)S(1)}, bf16[2,2,4,32,128]{4,3,2,1,0:T(8,128)(2,1)S(1)}, u32[]{:S(2)}, u32[]{:S(2)}) collective-permute-start(bf16[2,2,4,32,128]{4,3,2,1,0:T(8,128)(2,1)S(1)} %get-tuple-element.38), channel_id=1, source_target_pairs={{0,1},{1,0},{2,3},{3,2},{4,5},{5,4},{6,7},{7,6},{8,9},{9,8},{10,11... | collective-permute-start | bytes 393224 | tf_op jit(solution)/shard_map/ppermute | solution.py:404
  18.7 5.3 %collective-permute-start.7 = (bf16[2,4,32,128]{3,2,1,0:T(8,128)(2,1)S(1)}, bf16[2,4,32,128]{3,2,1,0:T(8,128)(2,1)S(1)}, u32[]{:S(2)}, u32[]{:S(2)}) collective-permute-start(bf16[2,4,32,128]{3,2,1,0:T(8,128)(2,1)S(1)} %get-tuple-element.42), channel_id=1, source_target_pairs={{0,6},{2,4},{4,2},{6,0},{8,14},{10,12},{12,10},{14,8},{1,7},{3,5},... | collective-permute-start | bytes 196616 | tf_op jit(solution)/shard_map/ppermute | solution.py:420
  20.2 5.0 %collective-permute-start.8 = (bf16[2,4,32,128]{3,2,1,0:T(8,128)(2,1)S(1)}, bf16[2,4,32,128]{3,2,1,0:T(8,128)(2,1)S(1)}, u32[]{:S(2)}, u32[]{:S(2)}) collective-permute-start(bf16[2,4,32,128]{3,2,1,0:T(8,128)(2,1)S(1)} %get-tuple-element.43), channel_id=1, source_target_pairs={{0,2},{2,0},{4,6},{6,4},{8,10},{10,8},{12,14},{14,12},{1,3},{3,1},... | collective-permute-start | bytes 196616 | tf_op jit(solution)/shard_map/ppermute | solution.py:420
  21.3 4.3 %collective-permute-start.9 = (bf16[2,4,32,128]{3,2,1,0:T(8,128)(2,1)S(1)}, bf16[2,4,32,128]{3,2,1,0:T(8,128)(2,1)S(1)}, u32[]{:S(2)}, u32[]{:S(2)}) collective-permute-start(bf16[2,4,32,128]{3,2,1,0:T(8,128)(2,1)S(1)} %get-tuple-element.44), channel_id=1, source_target_pairs={{0,4},{2,6},{4,0},{6,2},{8,12},{10,14},{12,8},{14,10},{1,5},{3,7},... | collective-permute-start | bytes 196616 | tf_op jit(solution)/shard_map/ppermute | solution.py:420
  25.6 4.9 %collective-permute-start.10 = (bf16[4,32,128]{2,1,0:T(8,128)(2,1)S(1)}, bf16[4,32,128]{2,1,0:T(8,128)(2,1)S(1)}, u32[]{:S(2)}, u32[]{:S(2)}) collective-permute-start(bf16[4,32,128]{2,1,0:T(8,128)(2,1)S(1)} %get-tuple-element.46), channel_id=1, source_target_pairs={{0,8},{2,10},{4,12},{6,14},{8,0},{10,2},{12,4},{14,6},{1,9},{3,11}... | collective-permute-start | bytes 98312 | tf_op jit(solution)/shard_map/ppermute | solution.py:431

commit v19 on v18

--- a/solution.py
+++ b/solution.py
@@ -272,26 +272,30 @@
                 first = (half * JB + j) * chunk
                 piece = total[first : first + chunk] + acc_ref[pl.ds((2 * j + half) * nk + cls, chunk), :]
                 keep_ref[at, level, j] = piece[:, :nk]
-                send_ref[at, level, j] = piece[:, nk:].astype(jnp.bfloat16)
+                row = pl.multiple_of(((2 * at + level) * JB + j) * chunk, chunk)
+                send_ref[pl.ds(row, chunk), :] = piece[:, nk:].astype(jnp.bfloat16)
 
 
 def near_kernel(keep_ref, got_ref, *out_refs):
+    got = got_ref[...].astype(jnp.float32).reshape(keep_ref.shape)
     for at, ref in enumerate(out_refs):
-        ref[...] = (keep_ref[at] + got_ref[at].astype(jnp.float32)).astype(ref.dtype)
+        ref[...] = (keep_ref[at] + got[at]).astype(ref.dtype).reshape(ref.shape)
 
 
 def far_kernel(mine_ref, *refs):
     *parts, keep_ref, send_ref = refs
     level = lax.div(lax.axis_index("space"), NEAR)
+    rows = send_ref.shape[0]
     for ref, at in ((keep_ref, level), (send_ref, 1 - level)):
         total = mine_ref[at]
         for part in parts:
-            total = total + part[at].astype(jnp.float32)
-        ref[...] = total.astype(ref.dtype)
+            piece = part[pl.ds(pl.multiple_of(at * rows, rows), rows), :]
+            total = total + piece.astype(jnp.float32).reshape(total.shape)
+        ref[...] = total.astype(ref.dtype).reshape(ref.shape)
 
 
 def total_kernel(keep_ref, got_ref, out_ref):
-    total = keep_ref[...] + got_ref[...].astype(jnp.float32)
+    total = keep_ref[...] + got_ref[...].astype(jnp.float32).reshape(keep_ref.shape)
     for j in range(JB):
         out_ref[:, j, :] = total[j]
 
@@ -377,7 +381,10 @@
 
     def crossed(count, classes_of, weighted):
         piece = (count, 2, JB, chunk, nk)
-        out_shape = [jax.ShapeDtypeStruct(piece, f32), jax.ShapeDtypeStruct(piece, bf16)]
+        out_shape = [
+            jax.ShapeDtypeStruct(piece, f32),
+            jax.ShapeDtypeStruct((count * 2 * JB * chunk, nk), bf16),
+        ]
         if not weighted:
             out_shape.append(jax.ShapeDtypeStruct((2 * nk, 2 * depth), bf16))
         return pl.pallas_call(
@@ -404,25 +411,30 @@
         got_b = lax.ppermute(send_b, "modes", swap)
         piece = (JB, chunk, nk)
 
-        def summed(kinds, keep, got):
+        def summed(out_shape, keep, got):
             return pl.pallas_call(
                 near_kernel,
-                out_shape=[jax.ShapeDtypeStruct((2, *piece), kind) for kind in kinds],
+                out_shape=out_shape,
                 in_specs=[vmem] * 2,
                 out_specs=[vmem] * 2,
                 compiler_params=params,
                 name="near",
             )(keep, got)
 
-        part_3, part_1 = summed((bf16, bf16), keep_a, got_a)
-        mine, part_2 = summed((f32, bf16), keep_b, got_b)
+        kept = jax.ShapeDtypeStruct((2, *piece), f32)
+        sent = jax.ShapeDtypeStruct((2 * JB * chunk, nk), bf16)
+        part_3, part_1 = summed([sent, sent], keep_a, got_a)
+        mine, part_2 = summed([kept, sent], keep_b, got_b)
         parts = [
             lax.ppermute(part, "space", [(s, s ^ step) for s in range(n)])
             for part, step in ((part_3, 3), (part_1, 1), (part_2, 2))
         ]
         keep, send = pl.pallas_call(
             far_kernel,
-            out_shape=[jax.ShapeDtypeStruct(piece, f32), jax.ShapeDtypeStruct(piece, bf16)],
+            out_shape=[
+                jax.ShapeDtypeStruct(piece, f32),
+                jax.ShapeDtypeStruct((JB * chunk, nk), bf16),
+            ],
             in_specs=[vmem] * NEAR,
             out_specs=[vmem] * 2,
             compiler_params=params,
@@ -440,7 +452,7 @@
 
     count = nk // chunk
     keep, send, _ = crossed(count, lambda s: list(range(count)), ())
-    share = (keep + lax.ppermute(send, "modes", swap)).astype(bf16)
+    share = (keep + lax.ppermute(send, "modes", swap).reshape(keep.shape)).astype(bf16)
     share = share.reshape(count, 2, JB, chunk // per_target, per_target, nk)
     share = share.transpose(1, 0, 3, 2, 4, 5).reshape(n, JB, per_target, nk)
     parts = lax.all_to_all(share, "space", 0, 0, tiled=True)

time: 31.3 us -> 31.3 us (level)
  no operation moved by 1% of the time
where the time goes in v19:
time: 31.3 us; the launch traced here: 31.2 us
  starting transfers between devices  13.3 us (42%)
  waiting for transfers between devices  10.4 us (33%)
  Pallas kernels  6.77 us (22%)
  between operations  0.75 us (2%)
    ppermute x3, starting transfers between devices, on_device(): lax.ppermute(part, 'space', [(s, s ^ step) for s in range(n)])  3.62 us
    ppermute x3, waiting for transfers between devices, on_device(): lax.ppermute(part, 'space', [(s, s ^ step) for s in range(n)])  3.27 us
    ppermute x1, waiting for transfers between devices, on_device(): got = lax.ppermute(send, 'space', [(s, s ^ NEAR) for s in range(n)])  2.86 us
    ppermute x1, waiting for transfers between devices, on_device(): xc = lax.ppermute(xc, both, cross([(s, x_to(s)) for s in range(n)]))  2.81 us
    ppermute x1, starting transfers between devices, on_device(): second = lax.ppermute(second, both, same(seconds))  2.6 us
    ppermute x1, starting transfers between devices, on_device(): first = lax.ppermute(first, both, same(firsts))  2.53 us
    pallas_call x1, Pallas kernels, on_device(): pl.pallas_call(local_kernel, out_shape=[jax.ShapeDtypeStruct((JB * 2 * nk...  2.43 us
    ppermute x1, starting transfers between devices, on_device(): got = lax.ppermute(send, 'space', [(s, s ^ NEAR) for s in range(n)])  2.01 us
  transfers between devices with their start and end apart: 11, of which 7 were waited for; matrix products, arithmetic and copies ran while one was open for 0% of the time, Pallas kernels for 13%

profile of v19, /device:TPU:0, one launch (start us, length us, event | category | flops | bytes accessed | tf_op | source)
XLA Modules:
  0.0 31.2 jit_solution(4766581796543243495)
XLA Ops:
  0.0 0.0 copy-start.1
  0.0 1.4 %prep.1 = (bf16[8,3,128,128]{3,2,1,0:T(8,128)(2,1)S(1)}, bf16[784,128]{1,0:T(8,128)(2,1)S(1)}, bf16[784,128]{1,0:T(8,128)(2,1)S(1)}) custom-call(bf16[128,3,1,8,128]{4,3,2,1,0:T(8,128)(2,1)} %modes_hbm.1), custom_call_target="tpu_custom_call" | custom-call | flops 1500000000 | bytes 2800000 | tf_op jit(solution)/shard_map/prep/pallas_call | solution.py:311
  1.4 0.0 copy-start
  1.4 0.5 %collective-permute-start = (bf16[8,3,128,128]{3,2,1,0:T(8,128)(2,1)S(1)}, bf16[8,3,128,128]{3,2,1,0:T(8,128)(2,1)S(1)}, u32[]{:S(2)}, u32[]{:S(2)}) collective-permute-start(bf16[8,3,128,128]{3,2,1,0:T(8,128)(2,1)S(1)} %get-tuple-element.26.tr.own_ref), channel_id=1, source_target_pairs={{0,1},{1,0},{2,3},{3,2},{4,5},{5,4},{6,7},{7,6},{8,9},{9,8},{10,11... | collective-permute-start | bytes 2359304 | tf_op jit(solution)/shard_map/ppermute | solution.py:331
  1.9 2.5 %collective-permute-start.1 = (bf16[784,128]{1,0:T(8,128)(2,1)S(1)}, bf16[784,128]{1,0:T(8,128)(2,1)S(1)}, u32[]{:S(2)}, u32[]{:S(2)}) collective-permute-start(bf16[784,128]{1,0:T(8,128)(2,1)S(1)} %get-tuple-element.27), channel_id=1, source_target_pairs={{0,2},{1,3},{2,0},{3,1},{4,6},{5,7},{6,4},{7,5},{8,10},{9,11},{10,... | collective-permute-start | bytes 602120 | tf_op jit(solution)/shard_map/ppermute | solution.py:332
  4.5 2.6 %collective-permute-start.2 = (bf16[784,128]{1,0:T(8,128)(2,1)S(1)}, bf16[784,128]{1,0:T(8,128)(2,1)S(1)}, u32[]{:S(2)}, u32[]{:S(2)}) collective-permute-start(bf16[784,128]{1,0:T(8,128)(2,1)S(1)} %get-tuple-element.28), channel_id=1, source_target_pairs={{0,12},{1,13},{2,6},{3,7},{4,0},{5,1},{6,10},{7,11},{8,4},{9,5},{1... | collective-permute-start | bytes 602120 | tf_op jit(solution)/shard_map/ppermute | solution.py:333
  7.1 0.0 collective-permute-done._.other_ref
  7.1 0.0 copy-done.1
  7.1 0.0 copy-done
  7.1 0.1 weights.1
  7.2 0.1 collective-permute-start.3
  7.3 1.3 %collective-permute-start.4 = (bf16[784,128]{1,0:T(8,128)(2,1)S(1)}, bf16[784,128]{1,0:T(8,128)(2,1)S(1)}, u32[]{:S(2)}, u32[]{:S(2)}) collective-permute-start(bf16[784,128]{1,0:T(8,128)(2,1)S(1)} %get-tuple-element.30), channel_id=1, source_target_pairs={{2,7},{3,6},{4,1},{5,0},{6,11},{7,10},{8,5},{9,4},{10,15},{11,14},... | collective-permute-start | bytes 602120 | tf_op jit(solution)/shard_map/ppermute | solution.py:344
  9.2 2.4 %local.1 = (f32[1024,256]{1,0:T(8,128)S(1)}, bf16[2,256,384]{2,1,0:T(8,128)(2,1)S(1)}) custom-call(bf16[8,3,128,128]{3,2,1,0:T(8,128)(2,1)S(1)} %get-tuple-element.26.tr.own_ref, bf16[8,3,128,128]{3,2,1,0:T(8,128)(2,1)S(1)} %collective-permute-done._.other_ref, f32[8,128]{1,0:T(8,128)S(1)} %get-tuple-element.31.weight_ref, s32[1]{0:T(128)S(6)} %copy.5.jb_ref.refs_5_), custom_call_target="tpu_custom_call" | custom-call | flops 900000000 | bytes 2400000 | tf_op jit(solution)/shard_map/local/pallas_call | solution.py:348
  11.7 0.0 collective-permute-done.1.first_ref.refs_0_
  11.7 0.0 collective-permute-done.2.second_ref.refs_1_
  11.7 2.8 %collective-permute-done.3.xc_ref.refs_2_ = bf16[784,128]{1,0:T(8,128)(2,1)S(1)} collective-permute-done((bf16[784,128]{1,0:T(8,128)(2,1)S(1)}, bf16[784,128]{1,0:T(8,128)(2,1)S(1)}, u32[]{:S(2)}, u32[]{:S(2)}) %collective-permute-start.3) | collective-permute-done | bytes 200736 | tf_op jit(solution)/shard_map/ppermute | solution.py:343
  14.5 0.8 %early.1 = (f32[1024,256]{1,0:T(8,128)S(1)}, bf16[256,768]{1,0:T(8,128)(2,1)S(1)}) custom-call(bf16[8,3,128,128]{3,2,1,0:T(8,128)(2,1)S(1)} %get-tuple-element.26.tr.own_ref, bf16[8,3,128,128]{3,2,1,0:T(8,128)(2,1)S(1)} %collective-permute-done._.other_ref, bf16[784,128]{1,0:T(8,128)(2,1)S(1)} %collective-permute-done.1.first_ref.refs_0_, ...), custom_call_target="tpu_custom_call" | custom-call | flops 600000000 | bytes 2400000 | tf_op jit(solution)/shard_map/early/pallas_call | solution.py:365
  15.3 1.3 %collective-permute-done.4.refs_3_ = bf16[784,128]{1,0:T(8,128)(2,1)S(1)} collective-permute-done((bf16[784,128]{1,0:T(8,128)(2,1)S(1)}, bf16[784,128]{1,0:T(8,128)(2,1)S(1)}, u32[]{:S(2)}, u32[]{:S(2)}) %collective-permute-start.4) | collective-permute-done | bytes 200736 | tf_op jit(solution)/shard_map/ppermute | solution.py:344
  16.5 0.7 %cross.2 = (f32[2,2,4,32,128]{4,3,2,1,0:T(8,128)S(1)}, bf16[512,128]{1,0:T(8,128)(2,1)S(1)}, bf16[256,1536]{1,0:T(8,128)(2,1)S(1)}) custom-call(bf16[8,3,128,128]{3,2,1,0:T(8,128)(2,1)S(1)} %get-tuple-element.26.tr.own_ref, bf16[8,3,128,128]{3,2,1,0:T(8,128)(2,1)S(1)} %collective-permute-done._.other_ref, ...), custom_call_target="tpu_custom_call" | custom-call | flops 900000000 | bytes 4000000 | tf_op jit(solution)/shard_map/cross/pallas_call | solution.py:390
  17.2 0.2 collective-permute-start.6
  17.4 0.6 %cross.3 = (f32[2,2,4,32,128]{4,3,2,1,0:T(8,128)S(1)}, bf16[512,128]{1,0:T(8,128)(2,1)S(1)}) custom-call(bf16[8,3,128,128]{3,2,1,0:T(8,128)(2,1)S(1)} %get-tuple-element.26.tr.own_ref, bf16[8,3,128,128]{3,2,1,0:T(8,128)(2,1)S(1)} %collective-permute-done._.other_ref, bf16[784,128]{1,0:T(8,128)(2,1)S(1)} %collective-permute-done.1.first_ref.refs_0_, ...), custom_call_target="tpu_custom_call" | custom-call | flops 900000000 | bytes 4000000 | tf_op jit(solution)/shard_map/cross/pallas_call | solution.py:390
  18.1 0.5 %collective-permute-start.5 = (bf16[512,128]{1,0:T(8,128)(2,1)S(1)}, bf16[512,128]{1,0:T(8,128)(2,1)S(1)}, u32[]{:S(2)}, u32[]{:S(2)}) collective-permute-start(bf16[512,128]{1,0:T(8,128)(2,1)S(1)} %get-tuple-element.38), channel_id=1, source_target_pairs={{0,1},{1,0},{2,3},{3,2},{4,5},{5,4},{6,7},{7,6},{8,9},{9,8},{10,11... | collective-permute-start | bytes 393224 | tf_op jit(solution)/shard_map/ppermute | solution.py:411
  18.5 0.1 collective-permute-done.6.got_ref
  18.7 1.5 %collective-permute-start.7 = (bf16[256,128]{1,0:T(8,128)(2,1)S(1)}, bf16[256,128]{1,0:T(8,128)(2,1)S(1)}, u32[]{:S(2)}, u32[]{:S(2)}) collective-permute-start(bf16[256,128]{1,0:T(8,128)(2,1)S(1)} %get-tuple-element.42), channel_id=1, source_target_pairs={{0,6},{2,4},{4,2},{6,0},{8,14},{10,12},{12,10},{14,8},{1,7},{3,5},... | collective-permute-start | bytes 196616 | tf_op jit(solution)/shard_map/ppermute | solution.py:429
  20.2 1.0 %collective-permute-start.8 = (bf16[256,128]{1,0:T(8,128)(2,1)S(1)}, bf16[256,128]{1,0:T(8,128)(2,1)S(1)}, u32[]{:S(2)}, u32[]{:S(2)}) collective-permute-start(bf16[256,128]{1,0:T(8,128)(2,1)S(1)} %get-tuple-element.43), channel_id=1, source_target_pairs={{0,2},{2,0},{4,6},{6,4},{8,10},{10,8},{12,14},{14,12},{1,3},{3,1},... | collective-permute-start | bytes 196616 | tf_op jit(solution)/shard_map/ppermute | solution.py:429
  21.2 0.0 collective-permute-done.5.got_ref
  21.3 1.1 %collective-permute-start.9 = (bf16[256,128]{1,0:T(8,128)(2,1)S(1)}, bf16[256,128]{1,0:T(8,128)(2,1)S(1)}, u32[]{:S(2)}, u32[]{:S(2)}) collective-permute-start(bf16[256,128]{1,0:T(8,128)(2,1)S(1)} %get-tuple-element.44), channel_id=1, source_target_pairs={{0,4},{2,6},{4,0},{6,2},{8,12},{10,14},{12,8},{14,10},{1,5},{3,7},... | collective-permute-start | bytes 196616 | tf_op jit(solution)/shard_map/ppermute | solution.py:429
  22.3 1.6 %collective-permute-done.7.refs_0_ = bf16[256,128]{1,0:T(8,128)(2,1)S(1)} collective-permute-done((bf16[256,128]{1,0:T(8,128)(2,1)S(1)}, bf16[256,128]{1,0:T(8,128)(2,1)S(1)}, u32[]{:S(2)}, u32[]{:S(2)}) %collective-permute-start.7) | collective-permute-done | bytes 65568 | tf_op jit(solution)/shard_map/ppermute | solution.py:429
  24.0 1.2 %collective-permute-done.8.refs_1_ = bf16[256,128]{1,0:T(8,128)(2,1)S(1)} collective-permute-done((bf16[256,128]{1,0:T(8,128)(2,1)S(1)}, bf16[256,128]{1,0:T(8,128)(2,1)S(1)}, u32[]{:S(2)}, u32[]{:S(2)}) %collective-permute-start.8) | collective-permute-done | bytes 65568 | tf_op jit(solution)/shard_map/ppermute | solution.py:429
  25.2 0.4 %collective-permute-done.9.refs_2_ = bf16[256,128]{1,0:T(8,128)(2,1)S(1)} collective-permute-done((bf16[256,128]{1,0:T(8,128)(2,1)S(1)}, bf16[256,128]{1,0:T(8,128)(2,1)S(1)}, u32[]{:S(2)}, u32[]{:S(2)}) %collective-permute-start.9) | collective-permute-done | bytes 65568 | tf_op jit(solution)/shard_map/ppermute | solution.py:429
  25.6 2.0 %collective-permute-start.10 = (bf16[128,128]{1,0:T(8,128)(2,1)S(1)}, bf16[128,128]{1,0:T(8,128)(2,1)S(1)}, u32[]{:S(2)}, u32[]{:S(2)}) collective-permute-start(bf16[128,128]{1,0:T(8,128)(2,1)S(1)} %get-tuple-element.46), channel_id=1, source_target_pairs={{0,8},{2,10},{4,12},{6,14},{8,0},{10,2},{12,4},{14,6},{1,9},{3,11}... | collective-permute-start | bytes 98312 | tf_op jit(solution)/shard_map/ppermute | solution.py:443
  27.6 2.9 %collective-permute-done.10.got_ref = bf16[128,128]{1,0:T(8,128)(2,1)S(1)} collective-permute-done((bf16[128,128]{1,0:T(8,128)(2,1)S(1)}, bf16[128,128]{1,0:T(8,128)(2,1)S(1)}, u32[]{:S(2)}, u32[]{:S(2)}) %collective-permute-start.10) | collective-permute-done | bytes 32800 | tf_op jit(solution)/shard_map/ppermute | solution.py:443
  30.5 0.7 %total.1 = f32[32,4,128]{2,1,0:T(4,128)} custom-call(f32[4,32,128]{2,1,0:T(8,128)S(1)} %get-tuple-element.45.keep_ref, bf16[128,128]{1,0:T(8,128)(2,1)S(1)} %collective-permute-done.10.got_ref), custom_call_target="tpu_custom_call" | custom-call | tf_op jit(solution)/shard_map/total/pallas_call | solution.py:444
  (4 shorter events, 0.1 us)
Async XLA Ops:
  0.0 7.1 %copy-start.1 = (f32[16]{0:T(128)S(1)}, f32[16]{0:T(128)}, u32[]{:S(2)}) copy-start(f32[16]{0:T(128)} %param.6) | copy-start | bytes 196
  1.4 5.7 %copy-start = (s32[1,8,128]{2,1,0:T(8,128)S(1)}, s32[1,8,128]{2,1,0:T(8,128)}, u32[]{:S(2)}) copy-start(s32[1,8,128]{2,1,0:T(8,128)} %ids_ref.1) | copy-start | bytes 12292
  1.4 5.7 %collective-permute-start = (bf16[8,3,128,128]{3,2,1,0:T(8,128)(2,1)S(1)}, bf16[8,3,128,128]{3,2,1,0:T(8,128)(2,1)S(1)}, u32[]{:S(2)}, u32[]{:S(2)}) collective-permute-start(bf16[8,3,128,128]{3,2,1,0:T(8,128)(2,1)S(1)} %get-tuple-element.26.tr.own_ref), channel_id=1, source_target_pairs={{0,1},{1,0},{2,3},{3,2},{4,5},{5,4},{6,7},{7,6},{8,9},{9,8},{10,11... | collective-permute-start | bytes 2359304 | tf_op jit(solution)/shard_map/ppermute | solution.py:331
  1.9 9.7 %collective-permute-start.1 = (bf16[784,128]{1,0:T(8,128)(2,1)S(1)}, bf16[784,128]{1,0:T(8,128)(2,1)S(1)}, u32[]{:S(2)}, u32[]{:S(2)}) collective-permute-start(bf16[784,128]{1,0:T(8,128)(2,1)S(1)} %get-tuple-element.27), channel_id=1, source_target_pairs={{0,2},{1,3},{2,0},{3,1},{4,6},{5,7},{6,4},{7,5},{8,10},{9,11},{10,... | collective-permute-start | bytes 602120 | tf_op jit(solution)/shard_map/ppermute | solution.py:332
  4.5 7.2 %collective-permute-start.2 = (bf16[784,128]{1,0:T(8,128)(2,1)S(1)}, bf16[784,128]{1,0:T(8,128)(2,1)S(1)}, u32[]{:S(2)}, u32[]{:S(2)}) collective-permute-start(bf16[784,128]{1,0:T(8,128)(2,1)S(1)} %get-tuple-element.28), channel_id=1, source_target_pairs={{0,12},{1,13},{2,6},{3,7},{4,0},{5,1},{6,10},{7,11},{8,4},{9,5},{1... | collective-permute-start | bytes 602120 | tf_op jit(solution)/shard_map/ppermute | solution.py:333
  7.2 7.3 %collective-permute-start.3 = (bf16[784,128]{1,0:T(8,128)(2,1)S(1)}, bf16[784,128]{1,0:T(8,128)(2,1)S(1)}, u32[]{:S(2)}, u32[]{:S(2)}) collective-permute-start(bf16[784,128]{1,0:T(8,128)(2,1)S(1)} %get-tuple-element.29), channel_id=1, source_target_pairs={{0,3},{1,2},{2,1},{3,0},{4,7},{5,6},{6,5},{7,4},{8,11},{9,10},{10,... | collective-permute-start | bytes 602120 | tf_op jit(solution)/shard_map/ppermute | solution.py:343
  7.3 9.3 %collective-permute-start.4 = (bf16[784,128]{1,0:T(8,128)(2,1)S(1)}, bf16[784,128]{1,0:T(8,128)(2,1)S(1)}, u32[]{:S(2)}, u32[]{:S(2)}) collective-permute-start(bf16[784,128]{1,0:T(8,128)(2,1)S(1)} %get-tuple-element.30), channel_id=1, source_target_pairs={{2,7},{3,6},{4,1},{5,0},{6,11},{7,10},{8,5},{9,4},{10,15},{11,14},... | collective-permute-start | bytes 602120 | tf_op jit(solution)/shard_map/ppermute | solution.py:344
  17.2 1.4 %collective-permute-start.6 = (bf16[512,128]{1,0:T(8,128)(2,1)S(1)}, bf16[512,128]{1,0:T(8,128)(2,1)S(1)}, u32[]{:S(2)}, u32[]{:S(2)}) collective-permute-start(bf16[512,128]{1,0:T(8,128)(2,1)S(1)} %get-tuple-element.41), channel_id=1, source_target_pairs={{0,1},{1,0},{2,3},{3,2},{4,5},{5,4},{6,7},{7,6},{8,9},{9,8},{10,11... | collective-permute-start | bytes 393224 | tf_op jit(solution)/shard_map/ppermute | solution.py:409
  18.1 3.2 %collective-permute-start.5 = (bf16[512,128]{1,0:T(8,128)(2,1)S(1)}, bf16[512,128]{1,0:T(8,128)(2,1)S(1)}, u32[]{:S(2)}, u32[]{:S(2)}) collective-permute-start(bf16[512,128]{1,0:T(8,128)(2,1)S(1)} %get-tuple-element.38), channel_id=1, source_target_pairs={{0,1},{1,0},{2,3},{3,2},{4,5},{5,4},{6,7},{7,6},{8,9},{9,8},{10,11... | collective-permute-start | bytes 393224 | tf_op jit(solution)/shard_map/ppermute | solution.py:411
  18.7 5.3 %collective-permute-start.7 = (bf16[256,128]{1,0:T(8,128)(2,1)S(1)}, bf16[256,128]{1,0:T(8,128)(2,1)S(1)}, u32[]{:S(2)}, u32[]{:S(2)}) collective-permute-start(bf16[256,128]{1,0:T(8,128)(2,1)S(1)} %get-tuple-element.42), channel_id=1, source_target_pairs={{0,6},{2,4},{4,2},{6,0},{8,14},{10,12},{12,10},{14,8},{1,7},{3,5},... | collective-permute-start | bytes 196616 | tf_op jit(solution)/shard_map/ppermute | solution.py:429
  20.2 5.0 %collective-permute-start.8 = (bf16[256,128]{1,0:T(8,128)(2,1)S(1)}, bf16[256,128]{1,0:T(8,128)(2,1)S(1)}, u32[]{:S(2)}, u32[]{:S(2)}) collective-permute-start(bf16[256,128]{1,0:T(8,128)(2,1)S(1)} %get-tuple-element.43), channel_id=1, source_target_pairs={{0,2},{2,0},{4,6},{6,4},{8,10},{10,8},{12,14},{14,12},{1,3},{3,1},... | collective-permute-start | bytes 196616 | tf_op jit(solution)/shard_map/ppermute | solution.py:429
  21.3 4.3 %collective-permute-start.9 = (bf16[256,128]{1,0:T(8,128)(2,1)S(1)}, bf16[256,128]{1,0:T(8,128)(2,1)S(1)}, u32[]{:S(2)}, u32[]{:S(2)}) collective-permute-start(bf16[256,128]{1,0:T(8,128)(2,1)S(1)} %get-tuple-element.44), channel_id=1, source_target_pairs={{0,4},{2,6},{4,0},{6,2},{8,12},{10,14},{12,8},{14,10},{1,5},{3,7},... | collective-permute-start | bytes 196616 | tf_op jit(solution)/shard_map/ppermute | solution.py:429
  25.6 4.9 %collective-permute-start.10 = (bf16[128,128]{1,0:T(8,128)(2,1)S(1)}, bf16[128,128]{1,0:T(8,128)(2,1)S(1)}, u32[]{:S(2)}, u32[]{:S(2)}) collective-permute-start(bf16[128,128]{1,0:T(8,128)(2,1)S(1)} %get-tuple-element.46), channel_id=1, source_target_pairs={{0,8},{2,10},{4,12},{6,14},{8,0},{10,2},{12,4},{14,6},{1,9},{3,11}... | collective-permute-start | bytes 98312 | tf_op jit(solution)/shard_map/ppermute | solution.py:443

commit v20 on v19

--- a/solution.py
+++ b/solution.py
@@ -276,20 +276,26 @@
                 send_ref[pl.ds(row, chunk), :] = piece[:, nk:].astype(jnp.bfloat16)
 
 
-def near_kernel(keep_ref, got_ref, *out_refs):
-    got = got_ref[...].astype(jnp.float32).reshape(keep_ref.shape)
-    for at, ref in enumerate(out_refs):
-        ref[...] = (keep_ref[at] + got[at]).astype(ref.dtype).reshape(ref.shape)
-
-
-def far_kernel(mine_ref, *refs):
-    *parts, keep_ref, send_ref = refs
-    level = lax.div(lax.axis_index("space"), NEAR)
+def near_kernel(keep_a_ref, got_a_ref, keep_b_ref, got_b_ref, mine_ref, send_ref):
+    low = lax.rem(lax.axis_index("space"), NEAR)
+    for keep_ref, got_ref, steps in ((keep_a_ref, got_a_ref, (3, 1)), (keep_b_ref, got_b_ref, (0, 2))):
+        got = got_ref[...].astype(jnp.float32).reshape(keep_ref.shape)
+        for at, step in enumerate(steps):
+            total = keep_ref[at] + got[at]
+            if step == 0:
+                mine_ref[...] = total
+            send_ref[jnp.bitwise_xor(low, step)] = total.astype(jnp.bfloat16).reshape(send_ref.shape[1:])
+
+
+def far_kernel(mine_ref, parts_ref, keep_ref, send_ref):
+    s = lax.axis_index("space")
+    low, level = lax.rem(s, NEAR), lax.div(s, NEAR)
     rows = send_ref.shape[0]
     for ref, at in ((keep_ref, level), (send_ref, 1 - level)):
         total = mine_ref[at]
-        for part in parts:
-            piece = part[pl.ds(pl.multiple_of(at * rows, rows), rows), :]
+        for step in range(1, NEAR):
+            from_chip = jnp.bitwise_xor(low, step)
+            piece = parts_ref[from_chip, pl.ds(pl.multiple_of(at * rows, rows), rows), :]
             total = total + piece.astype(jnp.float32).reshape(total.shape)
         ref[...] = total.astype(ref.dtype).reshape(ref.shape)
 
@@ -411,35 +417,31 @@
         got_b = lax.ppermute(send_b, "modes", swap)
         piece = (JB, chunk, nk)
 
-        def summed(out_shape, keep, got):
-            return pl.pallas_call(
-                near_kernel,
-                out_shape=out_shape,
-                in_specs=[vmem] * 2,
-                out_specs=[vmem] * 2,
-                compiler_params=params,
-                name="near",
-            )(keep, got)
-
-        kept = jax.ShapeDtypeStruct((2, *piece), f32)
-        sent = jax.ShapeDtypeStruct((2 * JB * chunk, nk), bf16)
-        part_3, part_1 = summed([sent, sent], keep_a, got_a)
-        mine, part_2 = summed([kept, sent], keep_b, got_b)
-        parts = [
-            lax.ppermute(part, "space", [(s, s ^ step) for s in range(n)])
-            for part, step in ((part_3, 3), (part_1, 1), (part_2, 2))
-        ]
+        mine, send = pl.pallas_call(
+            near_kernel,
+            out_shape=[
+                jax.ShapeDtypeStruct((2, *piece), f32),
+                jax.ShapeDtypeStruct((NEAR, 2 * JB * chunk, nk), bf16),
+            ],
+            in_specs=[vmem] * 4,
+            out_specs=[vmem] * 2,
+            compiler_params=params,
+            name="near",
+        )(keep_a, got_a, keep_b, got_b)
+        parts = lax.all_to_all(
+            send, "space", 0, 0, axis_index_groups=[list(range(NEAR)), list(range(NEAR, 2 * NEAR))], tiled=True
+        )
         keep, send = pl.pallas_call(
             far_kernel,
             out_shape=[
                 jax.ShapeDtypeStruct(piece, f32),
                 jax.ShapeDtypeStruct((JB * chunk, nk), bf16),
             ],
-            in_specs=[vmem] * NEAR,
+            in_specs=[vmem] * 2,
             out_specs=[vmem] * 2,
             compiler_params=params,
             name="far",
-        )(mine, *parts)
+        )(mine, parts)
         got = lax.ppermute(send, "space", [(s, s ^ NEAR) for s in range(n)])
         return pl.pallas_call(
             total_kernel,

time: 31.3 us -> 34.2 us (1.093)
  blocking collectives: 0 us -> 8.91 us
  starting transfers between devices: 13.3 us -> 9.86 us
  waiting for transfers between devices: 10.4 us -> 7.75 us
    all_to_all x0 -> x1, blocking collectives: none -> 8.91 us  [on_device(): lax.all_to_all(send, 'space', 0, 0, axis_index_groups=[list(range(NEAR)),...]
    ppermute x3 -> x0, starting transfers between devices: 3.62 us -> none  [on_device(): lax.ppermute(part, 'space', [(s, s ^ step) for s in range(n)])]
    ppermute x3 -> x0, waiting for transfers between devices: 3.27 us -> none  [on_device(): lax.ppermute(part, 'space', [(s, s ^ step) for s in range(n)])]
    ppermute x1, waiting for transfers between devices: 0.01 us -> 0.85 us  [on_device(): got_b = lax.ppermute(send_b, 'modes', swap)]
  transfers between devices with their start and end apart: 11 -> 8, of which waited for: 7 -> 5; matrix products, arithmetic and copies ran while one was open for 0% -> 0% of each run, Pallas kernels for 13% -> 12%
where the time goes in v20:
time: 34.2 us; the launch traced here: 34 us
  starting transfers between devices  9.86 us (29%)
  blocking collectives  8.91 us (26%)
  waiting for transfers between devices  7.75 us (23%)
  Pallas kernels  6.76 us (20%)
  between operations  0.75 us (2%)
    all_to_all x1, blocking collectives, on_device(): lax.all_to_all(send, 'space', 0, 0, axis_index_groups=[list(range(NEAR)),...  8.91 us
    ppermute x1, waiting for transfers between devices, on_device(): xc = lax.ppermute(xc, both, cross([(s, x_to(s)) for s in range(n)]))  2.81 us
    ppermute x1, waiting for transfers between devices, on_device(): got = lax.ppermute(send, 'space', [(s, s ^ NEAR) for s in range(n)])  2.68 us
    ppermute x1, starting transfers between devices, on_device(): second = lax.ppermute(second, both, same(seconds))  2.6 us
    ppermute x1, starting transfers between devices, on_device(): first = lax.ppermute(first, both, same(firsts))  2.53 us
    pallas_call x1, Pallas kernels, on_device(): pl.pallas_call(local_kernel, out_shape=[jax.ShapeDtypeStruct((JB * 2 * nk...  2.43 us
    ppermute x1, starting transfers between devices, on_device(): got = lax.ppermute(send, 'space', [(s, s ^ NEAR) for s in range(n)])  2.2 us
    pallas_call x1, Pallas kernels, on_device(): pl.pallas_call(functools.partial(prep_kernel, n), out_shape=[jax.ShapeDty...  1.38 us
  transfers between devices with their start and end apart: 8, of which 5 were waited for; matrix products, arithmetic and copies ran while one was open for 0% of the time, Pallas kernels for 12%

profile of v20, /device:TPU:0, one launch (start us, length us, event | category | flops | bytes accessed | tf_op | source)
XLA Modules:
  0.0 34.0 jit_solution(6087172121333860377)
XLA Ops:
  0.0 0.0 copy-start.1
  0.0 1.4 %prep.1 = (bf16[8,3,128,128]{3,2,1,0:T(8,128)(2,1)S(1)}, bf16[784,128]{1,0:T(8,128)(2,1)S(1)}, bf16[784,128]{1,0:T(8,128)(2,1)S(1)}) custom-call(bf16[128,3,1,8,128]{4,3,2,1,0:T(8,128)(2,1)} %modes_hbm.1), custom_call_target="tpu_custom_call" | custom-call | flops 1500000000 | bytes 2800000 | tf_op jit(solution)/shard_map/prep/pallas_call | solution.py:317
  1.4 0.0 copy-start
  1.4 0.5 %collective-permute-start = (bf16[8,3,128,128]{3,2,1,0:T(8,128)(2,1)S(1)}, bf16[8,3,128,128]{3,2,1,0:T(8,128)(2,1)S(1)}, u32[]{:S(2)}, u32[]{:S(2)}) collective-permute-start(bf16[8,3,128,128]{3,2,1,0:T(8,128)(2,1)S(1)} %get-tuple-element.24.tr.own_ref), channel_id=1, source_target_pairs={{0,1},{1,0},{2,3},{3,2},{4,5},{5,4},{6,7},{7,6},{8,9},{9,8},{10,11... | collective-permute-start | bytes 2359304 | tf_op jit(solution)/shard_map/ppermute | solution.py:337
  1.9 2.5 %collective-permute-start.1 = (bf16[784,128]{1,0:T(8,128)(2,1)S(1)}, bf16[784,128]{1,0:T(8,128)(2,1)S(1)}, u32[]{:S(2)}, u32[]{:S(2)}) collective-permute-start(bf16[784,128]{1,0:T(8,128)(2,1)S(1)} %get-tuple-element.25), channel_id=1, source_target_pairs={{0,2},{1,3},{2,0},{3,1},{4,6},{5,7},{6,4},{7,5},{8,10},{9,11},{10,... | collective-permute-start | bytes 602120 | tf_op jit(solution)/shard_map/ppermute | solution.py:338
  4.5 2.6 %collective-permute-start.2 = (bf16[784,128]{1,0:T(8,128)(2,1)S(1)}, bf16[784,128]{1,0:T(8,128)(2,1)S(1)}, u32[]{:S(2)}, u32[]{:S(2)}) collective-permute-start(bf16[784,128]{1,0:T(8,128)(2,1)S(1)} %get-tuple-element.26), channel_id=1, source_target_pairs={{0,12},{1,13},{2,6},{3,7},{4,0},{5,1},{6,10},{7,11},{8,4},{9,5},{1... | collective-permute-start | bytes 602120 | tf_op jit(solution)/shard_map/ppermute | solution.py:339
  7.1 0.0 collective-permute-done._.other_ref
  7.1 0.0 copy-done.1
  7.1 0.0 copy-done
  7.1 0.1 weights.1
  7.2 0.1 collective-permute-start.3
  7.3 1.3 %collective-permute-start.4 = (bf16[784,128]{1,0:T(8,128)(2,1)S(1)}, bf16[784,128]{1,0:T(8,128)(2,1)S(1)}, u32[]{:S(2)}, u32[]{:S(2)}) collective-permute-start(bf16[784,128]{1,0:T(8,128)(2,1)S(1)} %get-tuple-element.28), channel_id=1, source_target_pairs={{2,7},{3,6},{4,1},{5,0},{6,11},{7,10},{8,5},{9,4},{10,15},{11,14},... | collective-permute-start | bytes 602120 | tf_op jit(solution)/shard_map/ppermute | solution.py:350
  9.2 2.4 %local.1 = (f32[1024,256]{1,0:T(8,128)S(1)}, bf16[2,256,384]{2,1,0:T(8,128)(2,1)S(1)}) custom-call(bf16[8,3,128,128]{3,2,1,0:T(8,128)(2,1)S(1)} %get-tuple-element.24.tr.own_ref, bf16[8,3,128,128]{3,2,1,0:T(8,128)(2,1)S(1)} %collective-permute-done._.other_ref, f32[8,128]{1,0:T(8,128)S(1)} %get-tuple-element.29.weight_ref, s32[1]{0:T(128)S(6)} %copy.5.jb_ref.refs_5_), custom_call_target="tpu_custom_call" | custom-call | flops 900000000 | bytes 2400000 | tf_op jit(solution)/shard_map/local/pallas_call | solution.py:354
  11.7 0.0 collective-permute-done.1.first_ref.refs_0_
  11.7 0.0 collective-permute-done.2.second_ref.refs_1_
  11.7 2.8 %collective-permute-done.3.xc_ref.refs_2_ = bf16[784,128]{1,0:T(8,128)(2,1)S(1)} collective-permute-done((bf16[784,128]{1,0:T(8,128)(2,1)S(1)}, bf16[784,128]{1,0:T(8,128)(2,1)S(1)}, u32[]{:S(2)}, u32[]{:S(2)}) %collective-permute-start.3) | collective-permute-done | bytes 200736 | tf_op jit(solution)/shard_map/ppermute | solution.py:349
  14.5 0.8 %early.1 = (f32[1024,256]{1,0:T(8,128)S(1)}, bf16[256,768]{1,0:T(8,128)(2,1)S(1)}) custom-call(bf16[8,3,128,128]{3,2,1,0:T(8,128)(2,1)S(1)} %get-tuple-element.24.tr.own_ref, bf16[8,3,128,128]{3,2,1,0:T(8,128)(2,1)S(1)} %collective-permute-done._.other_ref, bf16[784,128]{1,0:T(8,128)(2,1)S(1)} %collective-permute-done.1.first_ref.refs_0_, ...), custom_call_target="tpu_custom_call" | custom-call | flops 600000000 | bytes 2400000 | tf_op jit(solution)/shard_map/early/pallas_call | solution.py:371
  15.3 1.3 %collective-permute-done.4.refs_3_ = bf16[784,128]{1,0:T(8,128)(2,1)S(1)} collective-permute-done((bf16[784,128]{1,0:T(8,128)(2,1)S(1)}, bf16[784,128]{1,0:T(8,128)(2,1)S(1)}, u32[]{:S(2)}, u32[]{:S(2)}) %collective-permute-start.4) | collective-permute-done | bytes 200736 | tf_op jit(solution)/shard_map/ppermute | solution.py:350
  16.5 0.7 %cross.2 = (f32[2,2,4,32,128]{4,3,2,1,0:T(8,128)S(1)}, bf16[512,128]{1,0:T(8,128)(2,1)S(1)}, bf16[256,1536]{1,0:T(8,128)(2,1)S(1)}) custom-call(bf16[8,3,128,128]{3,2,1,0:T(8,128)(2,1)S(1)} %get-tuple-element.24.tr.own_ref, bf16[8,3,128,128]{3,2,1,0:T(8,128)(2,1)S(1)} %collective-permute-done._.other_ref, ...), custom_call_target="tpu_custom_call" | custom-call | flops 900000000 | bytes 4000000 | tf_op jit(solution)/shard_map/cross/pallas_call | solution.py:396
  17.2 0.2 collective-permute-start.5
  17.4 0.6 %cross.3 = (f32[2,2,4,32,128]{4,3,2,1,0:T(8,128)S(1)}, bf16[512,128]{1,0:T(8,128)(2,1)S(1)}) custom-call(bf16[8,3,128,128]{3,2,1,0:T(8,128)(2,1)S(1)} %get-tuple-element.24.tr.own_ref, bf16[8,3,128,128]{3,2,1,0:T(8,128)(2,1)S(1)} %collective-permute-done._.other_ref, bf16[784,128]{1,0:T(8,128)(2,1)S(1)} %collective-permute-done.1.first_ref.refs_0_, ...), custom_call_target="tpu_custom_call" | custom-call | flops 900000000 | bytes 4000000 | tf_op jit(solution)/shard_map/cross/pallas_call | solution.py:396
  18.1 0.5 %collective-permute-start.6 = (bf16[512,128]{1,0:T(8,128)(2,1)S(1)}, bf16[512,128]{1,0:T(8,128)(2,1)S(1)}, u32[]{:S(2)}, u32[]{:S(2)}) collective-permute-start(bf16[512,128]{1,0:T(8,128)(2,1)S(1)} %get-tuple-element.38), channel_id=1, source_target_pairs={{0,1},{1,0},{2,3},{3,2},{4,5},{5,4},{6,7},{7,6},{8,9},{9,8},{10,11... | collective-permute-start | bytes 393224 | tf_op jit(solution)/shard_map/ppermute | solution.py:417
  18.5 0.1 collective-permute-done.5.got_a_ref
  18.6 0.9 %collective-permute-done.6.got_b_ref = bf16[512,128]{1,0:T(8,128)(2,1)S(1)} collective-permute-done((bf16[512,128]{1,0:T(8,128)(2,1)S(1)}, bf16[512,128]{1,0:T(8,128)(2,1)S(1)}, u32[]{:S(2)}, u32[]{:S(2)}) %collective-permute-start.6) | collective-permute-done | bytes 131104 | tf_op jit(solution)/shard_map/ppermute | solution.py:417
  19.5 8.9 %all_to_all.5.parts_ref = bf16[4,256,128]{2,1,0:T(8,128)(2,1)S(1)} all-to-all(bf16[4,256,128]{2,1,0:T(8,128)(2,1)S(1)} %get-tuple-element.40), channel_id=1, replica_groups={{0,2,4,6},{8,10,12,14},{1,3,5,7},{9,11,13,15},{16,18,20,22},{24,26,28,3..., dimensions={0} | all-to-all | bytes 524288 | tf_op jit(solution)/shard_map/all_to_all | solution.py:431
  28.5 2.2 %collective-permute-start.7 = (bf16[128,128]{1,0:T(8,128)(2,1)S(1)}, bf16[128,128]{1,0:T(8,128)(2,1)S(1)}, u32[]{:S(2)}, u32[]{:S(2)}) collective-permute-start(bf16[128,128]{1,0:T(8,128)(2,1)S(1)} %get-tuple-element.42), channel_id=1, source_target_pairs={{0,8},{2,10},{4,12},{6,14},{8,0},{10,2},{12,4},{14,6},{1,9},{3,11}... | collective-permute-start | bytes 98312 | tf_op jit(solution)/shard_map/ppermute | solution.py:445
  30.7 2.7 %collective-permute-done.7.got_ref = bf16[128,128]{1,0:T(8,128)(2,1)S(1)} collective-permute-done((bf16[128,128]{1,0:T(8,128)(2,1)S(1)}, bf16[128,128]{1,0:T(8,128)(2,1)S(1)}, u32[]{:S(2)}, u32[]{:S(2)}) %collective-permute-start.7) | collective-permute-done | bytes 32800 | tf_op jit(solution)/shard_map/ppermute | solution.py:445
  33.4 0.7 %total.1 = f32[32,4,128]{2,1,0:T(4,128)} custom-call(f32[4,32,128]{2,1,0:T(8,128)S(1)} %get-tuple-element.41.keep_ref, bf16[128,128]{1,0:T(8,128)(2,1)S(1)} %collective-permute-done.7.got_ref), custom_call_target="tpu_custom_call" | custom-call | tf_op jit(solution)/shard_map/total/pallas_call | solution.py:446
  (3 shorter events, 0.1 us)
Async XLA Ops:
  0.0 7.1 %copy-start.1 = (f32[16]{0:T(128)S(1)}, f32[16]{0:T(128)}, u32[]{:S(2)}) copy-start(f32[16]{0:T(128)} %param.6) | copy-start | bytes 196
  1.4 5.7 %copy-start = (s32[1,8,128]{2,1,0:T(8,128)S(1)}, s32[1,8,128]{2,1,0:T(8,128)}, u32[]{:S(2)}) copy-start(s32[1,8,128]{2,1,0:T(8,128)} %ids_ref.1) | copy-start | bytes 12292
  1.4 5.7 %collective-permute-start = (bf16[8,3,128,128]{3,2,1,0:T(8,128)(2,1)S(1)}, bf16[8,3,128,128]{3,2,1,0:T(8,128)(2,1)S(1)}, u32[]{:S(2)}, u32[]{:S(2)}) collective-permute-start(bf16[8,3,128,128]{3,2,1,0:T(8,128)(2,1)S(1)} %get-tuple-element.24.tr.own_ref), channel_id=1, source_target_pairs={{0,1},{1,0},{2,3},{3,2},{4,5},{5,4},{6,7},{7,6},{8,9},{9,8},{10,11... | collective-permute-start | bytes 2359304 | tf_op jit(solution)/shard_map/ppermute | solution.py:337
  1.9 9.7 %collective-permute-start.1 = (bf16[784,128]{1,0:T(8,128)(2,1)S(1)}, bf16[784,128]{1,0:T(8,128)(2,1)S(1)}, u32[]{:S(2)}, u32[]{:S(2)}) collective-permute-start(bf16[784,128]{1,0:T(8,128)(2,1)S(1)} %get-tuple-element.25), channel_id=1, source_target_pairs={{0,2},{1,3},{2,0},{3,1},{4,6},{5,7},{6,4},{7,5},{8,10},{9,11},{10,... | collective-permute-start | bytes 602120 | tf_op jit(solution)/shard_map/ppermute | solution.py:338
  4.5 7.2 %collective-permute-start.2 = (bf16[784,128]{1,0:T(8,128)(2,1)S(1)}, bf16[784,128]{1,0:T(8,128)(2,1)S(1)}, u32[]{:S(2)}, u32[]{:S(2)}) collective-permute-start(bf16[784,128]{1,0:T(8,128)(2,1)S(1)} %get-tuple-element.26), channel_id=1, source_target_pairs={{0,12},{1,13},{2,6},{3,7},{4,0},{5,1},{6,10},{7,11},{8,4},{9,5},{1... | collective-permute-start | bytes 602120 | tf_op jit(solution)/shard_map/ppermute | solution.py:339
  7.2 7.3 %collective-permute-start.3 = (bf16[784,128]{1,0:T(8,128)(2,1)S(1)}, bf16[784,128]{1,0:T(8,128)(2,1)S(1)}, u32[]{:S(2)}, u32[]{:S(2)}) collective-permute-start(bf16[784,128]{1,0:T(8,128)(2,1)S(1)} %get-tuple-element.27), channel_id=1, source_target_pairs={{0,3},{1,2},{2,1},{3,0},{4,7},{5,6},{6,5},{7,4},{8,11},{9,10},{10,... | collective-permute-start | bytes 602120 | tf_op jit(solution)/shard_map/ppermute | solution.py:349
  7.3 9.3 %collective-permute-start.4 = (bf16[784,128]{1,0:T(8,128)(2,1)S(1)}, bf16[784,128]{1,0:T(8,128)(2,1)S(1)}, u32[]{:S(2)}, u32[]{:S(2)}) collective-permute-start(bf16[784,128]{1,0:T(8,128)(2,1)S(1)} %get-tuple-element.28), channel_id=1, source_target_pairs={{2,7},{3,6},{4,1},{5,0},{6,11},{7,10},{8,5},{9,4},{10,15},{11,14},... | collective-permute-start | bytes 602120 | tf_op jit(solution)/shard_map/ppermute | solution.py:350
  17.2 1.4 %collective-permute-start.5 = (bf16[512,128]{1,0:T(8,128)(2,1)S(1)}, bf16[512,128]{1,0:T(8,128)(2,1)S(1)}, u32[]{:S(2)}, u32[]{:S(2)}) collective-permute-start(bf16[512,128]{1,0:T(8,128)(2,1)S(1)} %get-tuple-element.35), channel_id=1, source_target_pairs={{0,1},{1,0},{2,3},{3,2},{4,5},{5,4},{6,7},{7,6},{8,9},{9,8},{10,11... | collective-permute-start | bytes 393224 | tf_op jit(solution)/shard_map/ppermute | solution.py:415
  18.1 1.4 %collective-permute-start.6 = (bf16[512,128]{1,0:T(8,128)(2,1)S(1)}, bf16[512,128]{1,0:T(8,128)(2,1)S(1)}, u32[]{:S(2)}, u32[]{:S(2)}) collective-permute-start(bf16[512,128]{1,0:T(8,128)(2,1)S(1)} %get-tuple-element.38), channel_id=1, source_target_pairs={{0,1},{1,0},{2,3},{3,2},{4,5},{5,4},{6,7},{7,6},{8,9},{9,8},{10,11... | collective-permute-start | bytes 393224 | tf_op jit(solution)/shard_map/ppermute | solution.py:417
  28.5 4.9 %collective-permute-start.7 = (bf16[128,128]{1,0:T(8,128)(2,1)S(1)}, bf16[128,128]{1,0:T(8,128)(2,1)S(1)}, u32[]{:S(2)}, u32[]{:S(2)}) collective-permute-start(bf16[128,128]{1,0:T(8,128)(2,1)S(1)} %get-tuple-element.42), channel_id=1, source_target_pairs={{0,8},{2,10},{4,12},{6,14},{8,0},{10,2},{12,4},{14,6},{1,9},{3,11}... | collective-permute-start | bytes 98312 | tf_op jit(solution)/shard_map/ppermute | solution.py:445

commit v21 on v19

--- a/solution.py
+++ b/solution.py
@@ -282,6 +282,13 @@
         ref[...] = (keep_ref[at] + got[at]).astype(ref.dtype).reshape(ref.shape)
 
 
+def relay_kernel(keep_ref, got_ref, passed_ref, mine_ref, up_ref):
+    got = got_ref[...].astype(jnp.float32).reshape(keep_ref.shape)
+    mine_ref[...] = keep_ref[0] + got[0]
+    passed = passed_ref[...].astype(jnp.float32).reshape(keep_ref.shape[1:])
+    up_ref[...] = (keep_ref[1] + got[1] + passed).astype(up_ref.dtype).reshape(up_ref.shape)
+
+
 def far_kernel(mine_ref, *refs):
     *parts, keep_ref, send_ref = refs
     level = lax.div(lax.axis_index("space"), NEAR)
@@ -411,35 +418,36 @@
         got_b = lax.ppermute(send_b, "modes", swap)
         piece = (JB, chunk, nk)
 
-        def summed(out_shape, keep, got):
+        kept = jax.ShapeDtypeStruct((2, *piece), f32)
+        sent = jax.ShapeDtypeStruct((2 * JB * chunk, nk), bf16)
+
+        def summed(body_of, out_shape, *operands):
             return pl.pallas_call(
-                near_kernel,
+                body_of,
                 out_shape=out_shape,
-                in_specs=[vmem] * 2,
+                in_specs=[vmem] * len(operands),
                 out_specs=[vmem] * 2,
                 compiler_params=params,
                 name="near",
-            )(keep, got)
-
-        kept = jax.ShapeDtypeStruct((2, *piece), f32)
-        sent = jax.ShapeDtypeStruct((2 * JB * chunk, nk), bf16)
-        part_3, part_1 = summed([sent, sent], keep_a, got_a)
-        mine, part_2 = summed([kept, sent], keep_b, got_b)
-        parts = [
-            lax.ppermute(part, "space", [(s, s ^ step) for s in range(n)])
-            for part, step in ((part_3, 3), (part_1, 1), (part_2, 2))
-        ]
+            )(*operands)
+
+        along_x = [(s, s ^ 1) for s in range(n)]
+        diagonal, beside = summed(near_kernel, [sent, sent], keep_a, got_a)
+        passed = lax.ppermute(diagonal, "space", along_x)
+        beside = lax.ppermute(beside, "space", along_x)
+        mine, up = summed(relay_kernel, [kept, sent], keep_b, got_b, passed)
+        up = lax.ppermute(up, "space", [(s, s ^ 2) for s in range(n)])
         keep, send = pl.pallas_call(
             far_kernel,
             out_shape=[
                 jax.ShapeDtypeStruct(piece, f32),
                 jax.ShapeDtypeStruct((JB * chunk, nk), bf16),
             ],
-            in_specs=[vmem] * NEAR,
+            in_specs=[vmem] * 3,
             out_specs=[vmem] * 2,
             compiler_params=params,
             name="far",
-        )(mine, *parts)
+        )(mine, beside, up)
         got = lax.ppermute(send, "space", [(s, s ^ NEAR) for s in range(n)])
         return pl.pallas_call(
             total_kernel,

time: 31.3 us -> 33.7 us (1.077)
  waiting for transfers between devices: 10.4 us -> 12.8 us
    ppermute x3, waiting for transfers between devices: 3.27 us -> 5.99 us  [the longest x1 3.17 us: on_device(): up = lax.ppermute(up, 'space', [(s, s ^ 2) for s in range(n)])]
    ppermute x3, starting transfers between devices: 3.62 us -> 3.24 us  [the longest x1 2.01 us: on_device(): beside = lax.ppermute(beside, 'space', along_x)]
  transfers between devices with their start and end apart: 11 -> 11, of which waited for: 7 -> 6; matrix products, arithmetic and copies ran while one was open for 0% -> 0% of each run, Pallas kernels for 13% -> 12%
where the time goes in v21:
time: 33.7 us; the launch traced here: 33.5 us
  starting transfers between devices  13.2 us (39%)
  waiting for transfers between devices  12.8 us (38%)
  Pallas kernels  6.77 us (20%)
  between operations  0.76 us (2%)
    ppermute x1, waiting for transfers between devices, on_device(): up = lax.ppermute(up, 'space', [(s, s ^ 2) for s in range(n)])  3.17 us
    ppermute x1, waiting for transfers between devices, on_device(): passed = lax.ppermute(diagonal, 'space', along_x)  2.82 us
    ppermute x1, waiting for transfers between devices, on_device(): xc = lax.ppermute(xc, both, cross([(s, x_to(s)) for s in range(n)]))  2.81 us
    ppermute x1, waiting for transfers between devices, on_device(): got = lax.ppermute(send, 'space', [(s, s ^ NEAR) for s in range(n)])  2.6 us
    ppermute x1, starting transfers between devices, on_device(): second = lax.ppermute(second, both, same(seconds))  2.6 us
    ppermute x1, starting transfers between devices, on_device(): first = lax.ppermute(first, both, same(firsts))  2.53 us
    pallas_call x1, Pallas kernels, on_device(): pl.pallas_call(local_kernel, out_shape=[jax.ShapeDtypeStruct((JB * 2 * nk...  2.43 us
    ppermute x1, starting transfers between devices, on_device(): got = lax.ppermute(send, 'space', [(s, s ^ NEAR) for s in range(n)])  2.28 us
  transfers between devices with their start and end apart: 11, of which 6 were waited for; matrix products, arithmetic and copies ran while one was open for 0% of the time, Pallas kernels for 12%

profile of v21, /device:TPU:0, one launch (start us, length us, event | category | flops | bytes accessed | tf_op | source)
XLA Modules:
  0.0 33.5 jit_solution(5109903136468666248)
XLA Ops:
  0.0 0.0 copy-start.1
  0.0 1.4 %prep.1 = (bf16[8,3,128,128]{3,2,1,0:T(8,128)(2,1)S(1)}, bf16[784,128]{1,0:T(8,128)(2,1)S(1)}, bf16[784,128]{1,0:T(8,128)(2,1)S(1)}) custom-call(bf16[128,3,1,8,128]{4,3,2,1,0:T(8,128)(2,1)} %modes_hbm.1), custom_call_target="tpu_custom_call" | custom-call | flops 1500000000 | bytes 2800000 | tf_op jit(solution)/shard_map/prep/pallas_call | solution.py:318
  1.4 0.0 copy-start
  1.4 0.5 %collective-permute-start = (bf16[8,3,128,128]{3,2,1,0:T(8,128)(2,1)S(1)}, bf16[8,3,128,128]{3,2,1,0:T(8,128)(2,1)S(1)}, u32[]{:S(2)}, u32[]{:S(2)}) collective-permute-start(bf16[8,3,128,128]{3,2,1,0:T(8,128)(2,1)S(1)} %get-tuple-element.26.tr.own_ref), channel_id=1, source_target_pairs={{0,1},{1,0},{2,3},{3,2},{4,5},{5,4},{6,7},{7,6},{8,9},{9,8},{10,11... | collective-permute-start | bytes 2359304 | tf_op jit(solution)/shard_map/ppermute | solution.py:338
  1.9 2.5 %collective-permute-start.1 = (bf16[784,128]{1,0:T(8,128)(2,1)S(1)}, bf16[784,128]{1,0:T(8,128)(2,1)S(1)}, u32[]{:S(2)}, u32[]{:S(2)}) collective-permute-start(bf16[784,128]{1,0:T(8,128)(2,1)S(1)} %get-tuple-element.27), channel_id=1, source_target_pairs={{0,2},{1,3},{2,0},{3,1},{4,6},{5,7},{6,4},{7,5},{8,10},{9,11},{10,... | collective-permute-start | bytes 602120 | tf_op jit(solution)/shard_map/ppermute | solution.py:339
  4.5 2.6 %collective-permute-start.2 = (bf16[784,128]{1,0:T(8,128)(2,1)S(1)}, bf16[784,128]{1,0:T(8,128)(2,1)S(1)}, u32[]{:S(2)}, u32[]{:S(2)}) collective-permute-start(bf16[784,128]{1,0:T(8,128)(2,1)S(1)} %get-tuple-element.28), channel_id=1, source_target_pairs={{0,12},{1,13},{2,6},{3,7},{4,0},{5,1},{6,10},{7,11},{8,4},{9,5},{1... | collective-permute-start | bytes 602120 | tf_op jit(solution)/shard_map/ppermute | solution.py:340
  7.1 0.0 collective-permute-done._.other_ref
  7.1 0.0 copy-done.1
  7.1 0.0 copy-done
  7.1 0.1 weights.1
  7.2 0.1 collective-permute-start.3
  7.3 1.3 %collective-permute-start.4 = (bf16[784,128]{1,0:T(8,128)(2,1)S(1)}, bf16[784,128]{1,0:T(8,128)(2,1)S(1)}, u32[]{:S(2)}, u32[]{:S(2)}) collective-permute-start(bf16[784,128]{1,0:T(8,128)(2,1)S(1)} %get-tuple-element.30), channel_id=1, source_target_pairs={{2,7},{3,6},{4,1},{5,0},{6,11},{7,10},{8,5},{9,4},{10,15},{11,14},... | collective-permute-start | bytes 602120 | tf_op jit(solution)/shard_map/ppermute | solution.py:351
  9.2 2.4 %local.1 = (f32[1024,256]{1,0:T(8,128)S(1)}, bf16[2,256,384]{2,1,0:T(8,128)(2,1)S(1)}) custom-call(bf16[8,3,128,128]{3,2,1,0:T(8,128)(2,1)S(1)} %get-tuple-element.26.tr.own_ref, bf16[8,3,128,128]{3,2,1,0:T(8,128)(2,1)S(1)} %collective-permute-done._.other_ref, f32[8,128]{1,0:T(8,128)S(1)} %get-tuple-element.31.weight_ref, s32[1]{0:T(128)S(6)} %copy.5.jb_ref.refs_5_), custom_call_target="tpu_custom_call" | custom-call | flops 900000000 | bytes 2400000 | tf_op jit(solution)/shard_map/local/pallas_call | solution.py:355
  11.7 0.0 collective-permute-done.1.first_ref.refs_0_
  11.7 0.0 collective-permute-done.2.second_ref.refs_1_
  11.7 2.8 %collective-permute-done.3.xc_ref.refs_2_ = bf16[784,128]{1,0:T(8,128)(2,1)S(1)} collective-permute-done((bf16[784,128]{1,0:T(8,128)(2,1)S(1)}, bf16[784,128]{1,0:T(8,128)(2,1)S(1)}, u32[]{:S(2)}, u32[]{:S(2)}) %collective-permute-start.3) | collective-permute-done | bytes 200736 | tf_op jit(solution)/shard_map/ppermute | solution.py:350
  14.5 0.8 %early.1 = (f32[1024,256]{1,0:T(8,128)S(1)}, bf16[256,768]{1,0:T(8,128)(2,1)S(1)}) custom-call(bf16[8,3,128,128]{3,2,1,0:T(8,128)(2,1)S(1)} %get-tuple-element.26.tr.own_ref, bf16[8,3,128,128]{3,2,1,0:T(8,128)(2,1)S(1)} %collective-permute-done._.other_ref, bf16[784,128]{1,0:T(8,128)(2,1)S(1)} %collective-permute-done.1.first_ref.refs_0_, ...), custom_call_target="tpu_custom_call" | custom-call | flops 600000000 | bytes 2400000 | tf_op jit(solution)/shard_map/early/pallas_call | solution.py:372
  15.3 1.3 %collective-permute-done.4.refs_3_ = bf16[784,128]{1,0:T(8,128)(2,1)S(1)} collective-permute-done((bf16[784,128]{1,0:T(8,128)(2,1)S(1)}, bf16[784,128]{1,0:T(8,128)(2,1)S(1)}, u32[]{:S(2)}, u32[]{:S(2)}) %collective-permute-start.4) | collective-permute-done | bytes 200736 | tf_op jit(solution)/shard_map/ppermute | solution.py:351
  16.5 0.7 %cross.2 = (f32[2,2,4,32,128]{4,3,2,1,0:T(8,128)S(1)}, bf16[512,128]{1,0:T(8,128)(2,1)S(1)}, bf16[256,1536]{1,0:T(8,128)(2,1)S(1)}) custom-call(bf16[8,3,128,128]{3,2,1,0:T(8,128)(2,1)S(1)} %get-tuple-element.26.tr.own_ref, bf16[8,3,128,128]{3,2,1,0:T(8,128)(2,1)S(1)} %collective-permute-done._.other_ref, ...), custom_call_target="tpu_custom_call" | custom-call | flops 900000000 | bytes 4000000 | tf_op jit(solution)/shard_map/cross/pallas_call | solution.py:397
  17.2 0.2 collective-permute-start.6
  17.4 0.6 %cross.3 = (f32[2,2,4,32,128]{4,3,2,1,0:T(8,128)S(1)}, bf16[512,128]{1,0:T(8,128)(2,1)S(1)}) custom-call(bf16[8,3,128,128]{3,2,1,0:T(8,128)(2,1)S(1)} %get-tuple-element.26.tr.own_ref, bf16[8,3,128,128]{3,2,1,0:T(8,128)(2,1)S(1)} %collective-permute-done._.other_ref, bf16[784,128]{1,0:T(8,128)(2,1)S(1)} %collective-permute-done.1.first_ref.refs_0_, ...), custom_call_target="tpu_custom_call" | custom-call | flops 900000000 | bytes 4000000 | tf_op jit(solution)/shard_map/cross/pallas_call | solution.py:397
  18.1 0.5 %collective-permute-start.5 = (bf16[512,128]{1,0:T(8,128)(2,1)S(1)}, bf16[512,128]{1,0:T(8,128)(2,1)S(1)}, u32[]{:S(2)}, u32[]{:S(2)}) collective-permute-start(bf16[512,128]{1,0:T(8,128)(2,1)S(1)} %get-tuple-element.38), channel_id=1, source_target_pairs={{0,1},{1,0},{2,3},{3,2},{4,5},{5,4},{6,7},{7,6},{8,9},{9,8},{10,11... | collective-permute-start | bytes 393224 | tf_op jit(solution)/shard_map/ppermute | solution.py:418
  18.5 0.1 collective-permute-done.6.got_ref
  18.7 0.1 collective-permute-start.7
  18.7 2.0 %collective-permute-start.8 = (bf16[256,128]{1,0:T(8,128)(2,1)S(1)}, bf16[256,128]{1,0:T(8,128)(2,1)S(1)}, u32[]{:S(2)}, u32[]{:S(2)}) collective-permute-start(bf16[256,128]{1,0:T(8,128)(2,1)S(1)} %get-tuple-element.43), channel_id=1, source_target_pairs={{0,2},{2,0},{4,6},{6,4},{8,10},{10,8},{12,14},{14,12},{1,3},{3,1},... | collective-permute-start | bytes 196616 | tf_op jit(solution)/shard_map/ppermute | solution.py:437
  20.8 0.0 collective-permute-done.5.got_ref
  20.8 2.8 %collective-permute-done.7.passed_ref = bf16[256,128]{1,0:T(8,128)(2,1)S(1)} collective-permute-done((bf16[256,128]{1,0:T(8,128)(2,1)S(1)}, bf16[256,128]{1,0:T(8,128)(2,1)S(1)}, u32[]{:S(2)}, u32[]{:S(2)}) %collective-permute-start.7) | collective-permute-done | bytes 65568 | tf_op jit(solution)/shard_map/ppermute | solution.py:436
  23.6 1.2 %collective-permute-start.9 = (bf16[256,128]{1,0:T(8,128)(2,1)S(1)}, bf16[256,128]{1,0:T(8,128)(2,1)S(1)}, u32[]{:S(2)}, u32[]{:S(2)}) collective-permute-start(bf16[256,128]{1,0:T(8,128)(2,1)S(1)} %get-tuple-element.44), channel_id=1, source_target_pairs={{0,4},{2,6},{4,0},{6,2},{8,12},{10,14},{12,8},{14,10},{1,5},{3,7},... | collective-permute-start | bytes 196616 | tf_op jit(solution)/shard_map/ppermute | solution.py:439
  24.8 0.0 collective-permute-done.8.refs_0_
  24.8 3.2 %collective-permute-done.9.refs_1_ = bf16[256,128]{1,0:T(8,128)(2,1)S(1)} collective-permute-done((bf16[256,128]{1,0:T(8,128)(2,1)S(1)}, bf16[256,128]{1,0:T(8,128)(2,1)S(1)}, u32[]{:S(2)}, u32[]{:S(2)}) %collective-permute-start.9) | collective-permute-done | bytes 65568 | tf_op jit(solution)/shard_map/ppermute | solution.py:439
  28.0 2.3 %collective-permute-start.10 = (bf16[128,128]{1,0:T(8,128)(2,1)S(1)}, bf16[128,128]{1,0:T(8,128)(2,1)S(1)}, u32[]{:S(2)}, u32[]{:S(2)}) collective-permute-start(bf16[128,128]{1,0:T(8,128)(2,1)S(1)} %get-tuple-element.46), channel_id=1, source_target_pairs={{0,8},{2,10},{4,12},{6,14},{8,0},{10,2},{12,4},{14,6},{1,9},{3,11}... | collective-permute-start | bytes 98312 | tf_op jit(solution)/shard_map/ppermute | solution.py:451
  30.3 2.6 %collective-permute-done.10.got_ref = bf16[128,128]{1,0:T(8,128)(2,1)S(1)} collective-permute-done((bf16[128,128]{1,0:T(8,128)(2,1)S(1)}, bf16[128,128]{1,0:T(8,128)(2,1)S(1)}, u32[]{:S(2)}, u32[]{:S(2)}) %collective-permute-start.10) | collective-permute-done | bytes 32800 | tf_op jit(solution)/shard_map/ppermute | solution.py:451
  32.9 0.7 %total.1 = f32[32,4,128]{2,1,0:T(4,128)} custom-call(f32[4,32,128]{2,1,0:T(8,128)S(1)} %get-tuple-element.45.keep_ref, bf16[128,128]{1,0:T(8,128)(2,1)S(1)} %collective-permute-done.10.got_ref), custom_call_target="tpu_custom_call" | custom-call | tf_op jit(solution)/shard_map/total/pallas_call | solution.py:452
  (4 shorter events, 0.1 us)
Async XLA Ops:
  0.0 7.1 %copy-start.1 = (f32[16]{0:T(128)S(1)}, f32[16]{0:T(128)}, u32[]{:S(2)}) copy-start(f32[16]{0:T(128)} %param.6) | copy-start | bytes 196
  1.4 5.7 %copy-start = (s32[1,8,128]{2,1,0:T(8,128)S(1)}, s32[1,8,128]{2,1,0:T(8,128)}, u32[]{:S(2)}) copy-start(s32[1,8,128]{2,1,0:T(8,128)} %ids_ref.1) | copy-start | bytes 12292
  1.4 5.7 %collective-permute-start = (bf16[8,3,128,128]{3,2,1,0:T(8,128)(2,1)S(1)}, bf16[8,3,128,128]{3,2,1,0:T(8,128)(2,1)S(1)}, u32[]{:S(2)}, u32[]{:S(2)}) collective-permute-start(bf16[8,3,128,128]{3,2,1,0:T(8,128)(2,1)S(1)} %get-tuple-element.26.tr.own_ref), channel_id=1, source_target_pairs={{0,1},{1,0},{2,3},{3,2},{4,5},{5,4},{6,7},{7,6},{8,9},{9,8},{10,11... | collective-permute-start | bytes 2359304 | tf_op jit(solution)/shard_map/ppermute | solution.py:338
  1.9 9.7 %collective-permute-start.1 = (bf16[784,128]{1,0:T(8,128)(2,1)S(1)}, bf16[784,128]{1,0:T(8,128)(2,1)S(1)}, u32[]{:S(2)}, u32[]{:S(2)}) collective-permute-start(bf16[784,128]{1,0:T(8,128)(2,1)S(1)} %get-tuple-element.27), channel_id=1, source_target_pairs={{0,2},{1,3},{2,0},{3,1},{4,6},{5,7},{6,4},{7,5},{8,10},{9,11},{10,... | collective-permute-start | bytes 602120 | tf_op jit(solution)/shard_map/ppermute | solution.py:339
  4.5 7.2 %collective-permute-start.2 = (bf16[784,128]{1,0:T(8,128)(2,1)S(1)}, bf16[784,128]{1,0:T(8,128)(2,1)S(1)}, u32[]{:S(2)}, u32[]{:S(2)}) collective-permute-start(bf16[784,128]{1,0:T(8,128)(2,1)S(1)} %get-tuple-element.28), channel_id=1, source_target_pairs={{0,12},{1,13},{2,6},{3,7},{4,0},{5,1},{6,10},{7,11},{8,4},{9,5},{1... | collective-permute-start | bytes 602120 | tf_op jit(solution)/shard_map/ppermute | solution.py:340
  7.2 7.3 %collective-permute-start.3 = (bf16[784,128]{1,0:T(8,128)(2,1)S(1)}, bf16[784,128]{1,0:T(8,128)(2,1)S(1)}, u32[]{:S(2)}, u32[]{:S(2)}) collective-permute-start(bf16[784,128]{1,0:T(8,128)(2,1)S(1)} %get-tuple-element.29), channel_id=1, source_target_pairs={{0,3},{1,2},{2,1},{3,0},{4,7},{5,6},{6,5},{7,4},{8,11},{9,10},{10,... | collective-permute-start | bytes 602120 | tf_op jit(solution)/shard_map/ppermute | solution.py:350
  7.3 9.3 %collective-permute-start.4 = (bf16[784,128]{1,0:T(8,128)(2,1)S(1)}, bf16[784,128]{1,0:T(8,128)(2,1)S(1)}, u32[]{:S(2)}, u32[]{:S(2)}) collective-permute-start(bf16[784,128]{1,0:T(8,128)(2,1)S(1)} %get-tuple-element.30), channel_id=1, source_target_pairs={{2,7},{3,6},{4,1},{5,0},{6,11},{7,10},{8,5},{9,4},{10,15},{11,14},... | collective-permute-start | bytes 602120 | tf_op jit(solution)/shard_map/ppermute | solution.py:351
  17.2 1.4 %collective-permute-start.6 = (bf16[512,128]{1,0:T(8,128)(2,1)S(1)}, bf16[512,128]{1,0:T(8,128)(2,1)S(1)}, u32[]{:S(2)}, u32[]{:S(2)}) collective-permute-start(bf16[512,128]{1,0:T(8,128)(2,1)S(1)} %get-tuple-element.40), channel_id=1, source_target_pairs={{0,1},{1,0},{2,3},{3,2},{4,5},{5,4},{6,7},{7,6},{8,9},{9,8},{10,11... | collective-permute-start | bytes 393224 | tf_op jit(solution)/shard_map/ppermute | solution.py:416
  18.1 2.7 %collective-permute-start.5 = (bf16[512,128]{1,0:T(8,128)(2,1)S(1)}, bf16[512,128]{1,0:T(8,128)(2,1)S(1)}, u32[]{:S(2)}, u32[]{:S(2)}) collective-permute-start(bf16[512,128]{1,0:T(8,128)(2,1)S(1)} %get-tuple-element.38), channel_id=1, source_target_pairs={{0,1},{1,0},{2,3},{3,2},{4,5},{5,4},{6,7},{7,6},{8,9},{9,8},{10,11... | collective-permute-start | bytes 393224 | tf_op jit(solution)/shard_map/ppermute | solution.py:418
  18.7 4.9 %collective-permute-start.7 = (bf16[256,128]{1,0:T(8,128)(2,1)S(1)}, bf16[256,128]{1,0:T(8,128)(2,1)S(1)}, u32[]{:S(2)}, u32[]{:S(2)}) collective-permute-start(bf16[256,128]{1,0:T(8,128)(2,1)S(1)} %get-tuple-element.41), channel_id=1, source_target_pairs={{0,2},{2,0},{4,6},{6,4},{8,10},{10,8},{12,14},{14,12},{1,3},{3,1},... | collective-permute-start | bytes 196616 | tf_op jit(solution)/shard_map/ppermute | solution.py:436
  18.7 6.0 %collective-permute-start.8 = (bf16[256,128]{1,0:T(8,128)(2,1)S(1)}, bf16[256,128]{1,0:T(8,128)(2,1)S(1)}, u32[]{:S(2)}, u32[]{:S(2)}) collective-permute-start(bf16[256,128]{1,0:T(8,128)(2,1)S(1)} %get-tuple-element.43), channel_id=1, source_target_pairs={{0,2},{2,0},{4,6},{6,4},{8,10},{10,8},{12,14},{14,12},{1,3},{3,1},... | collective-permute-start | bytes 196616 | tf_op jit(solution)/shard_map/ppermute | solution.py:437
  23.6 4.3 %collective-permute-start.9 = (bf16[256,128]{1,0:T(8,128)(2,1)S(1)}, bf16[256,128]{1,0:T(8,128)(2,1)S(1)}, u32[]{:S(2)}, u32[]{:S(2)}) collective-permute-start(bf16[256,128]{1,0:T(8,128)(2,1)S(1)} %get-tuple-element.44), channel_id=1, source_target_pairs={{0,4},{2,6},{4,0},{6,2},{8,12},{10,14},{12,8},{14,10},{1,5},{3,7},... | collective-permute-start | bytes 196616 | tf_op jit(solution)/shard_map/ppermute | solution.py:439
  28.0 4.9 %collective-permute-start.10 = (bf16[128,128]{1,0:T(8,128)(2,1)S(1)}, bf16[128,128]{1,0:T(8,128)(2,1)S(1)}, u32[]{:S(2)}, u32[]{:S(2)}) collective-permute-start(bf16[128,128]{1,0:T(8,128)(2,1)S(1)} %get-tuple-element.46), channel_id=1, source_target_pairs={{0,8},{2,10},{4,12},{6,14},{8,0},{10,2},{12,4},{14,6},{1,9},{3,11}... | collective-permute-start | bytes 98312 | tf_op jit(solution)/shard_map/ppermute | solution.py:451

commit v22 on v19

--- a/solution.py
+++ b/solution.py
@@ -203,7 +203,7 @@
     out_ref[...] = total
 
 
-def cross_kernel(classes_of, chunk, planes, has_weighted, own_ref, other_ref, *refs):
+def cross_kernel(classes_of, chunk, planes, whole, has_weighted, own_ref, other_ref, *refs):
     first_ref, second_ref, xc_ref, zc_ref, w1_ref, jb_ref, acc_ref, *refs = refs
     xs_rows, zs_rows = same_core_rows(planes, first_ref, second_ref)
     if has_weighted:
@@ -271,9 +271,15 @@
             for j in range(JB):
                 first = (half * JB + j) * chunk
                 piece = total[first : first + chunk] + acc_ref[pl.ds((2 * j + half) * nk + cls, chunk), :]
-                keep_ref[at, level, j] = piece[:, :nk]
                 row = pl.multiple_of(((2 * at + level) * JB + j) * chunk, chunk)
-                send_ref[pl.ds(row, chunk), :] = piece[:, nk:].astype(jnp.bfloat16)
+                if whole:
+                    swapped = jnp.concatenate([piece[:, nk:], piece[:, :nk]], axis=1)
+                    piece = jnp.where(m == 0, piece, swapped)
+                    keep_ref[at, level, j] = piece
+                    send_ref[pl.ds(row, chunk), :] = piece.astype(jnp.bfloat16)
+                else:
+                    keep_ref[at, level, j] = piece[:, :nk]
+                    send_ref[pl.ds(row, chunk), :] = piece[:, nk:].astype(jnp.bfloat16)
 
 
 def near_kernel(keep_ref, got_ref, *out_refs):
@@ -294,8 +300,16 @@
         ref[...] = total.astype(ref.dtype).reshape(ref.shape)
 
 
-def total_kernel(keep_ref, got_ref, out_ref):
+def result_kernel(keep_ref, got_ref, own_ref, send_ref):
+    nk = own_ref.shape[2]
     total = keep_ref[...] + got_ref[...].astype(jnp.float32).reshape(keep_ref.shape)
+    send_ref[...] = total[:, :, :nk].reshape(send_ref.shape)
+    own_ref[...] = total[:, :, nk:]
+
+
+def total_kernel(own_ref, got_ref, out_ref):
+    first_core = lax.axis_index("modes") == 0
+    total = jnp.where(first_core, got_ref[...].reshape(own_ref.shape), own_ref[...])
     for j in range(JB):
         out_ref[:, j, :] = total[j]
 
@@ -378,17 +392,18 @@
 
     per_target = 2 * nk // n
     chunk = max(16, per_target)
+    whole = n == 2 * NEAR
 
     def crossed(count, classes_of, weighted):
-        piece = (count, 2, JB, chunk, nk)
+        lanes = 2 * nk if whole else nk
         out_shape = [
-            jax.ShapeDtypeStruct(piece, f32),
-            jax.ShapeDtypeStruct((count * 2 * JB * chunk, nk), bf16),
+            jax.ShapeDtypeStruct((count, 2, JB, chunk, lanes), f32),
+            jax.ShapeDtypeStruct((count * 2 * JB * chunk, lanes), bf16),
         ]
         if not weighted:
             out_shape.append(jax.ShapeDtypeStruct((2 * nk, 2 * depth), bf16))
         return pl.pallas_call(
-            functools.partial(cross_kernel, classes_of, chunk, n, bool(weighted)),
+            functools.partial(cross_kernel, classes_of, chunk, n, whole, bool(weighted)),
             out_shape=out_shape,
             in_specs=[vmem] * 7 + [smem] + [vmem] * (1 + len(weighted)),
             out_specs=[vmem] * len(out_shape),
@@ -401,15 +416,19 @@
         )(own, other, first, second, xc, zc, w1, j_block, acc, *weighted)
 
     swap = [(0, 1), (1, 0)]
-    if n == 2 * NEAR:
+    if whole:
         def partners(*steps):
             return lambda s: [jnp.bitwise_xor(lax.rem(s, NEAR), step) for step in steps]
+
+        def to_chip(value, step):
+            pairs = [(2 * s, 2 * s) for s in range(n)] + [(2 * s + 1, 2 * (s ^ step) + 1) for s in range(n)]
+            return lax.ppermute(value, both, pairs)
 
         keep_a, send_a, w2 = crossed(2, partners(3, 1), ())
         got_a = lax.ppermute(send_a, "modes", swap)
         keep_b, send_b = crossed(2, partners(0, 2), (w2,))
         got_b = lax.ppermute(send_b, "modes", swap)
-        piece = (JB, chunk, nk)
+        piece = (JB, chunk, 2 * nk)
 
         def summed(out_shape, keep, got):
             return pl.pallas_call(
@@ -422,25 +441,32 @@
             )(keep, got)
 
         kept = jax.ShapeDtypeStruct((2, *piece), f32)
-        sent = jax.ShapeDtypeStruct((2 * JB * chunk, nk), bf16)
+        sent = jax.ShapeDtypeStruct((2 * JB * chunk, 2 * nk), bf16)
         part_3, part_1 = summed([sent, sent], keep_a, got_a)
         mine, part_2 = summed([kept, sent], keep_b, got_b)
-        parts = [
-            lax.ppermute(part, "space", [(s, s ^ step) for s in range(n)])
-            for part, step in ((part_3, 3), (part_1, 1), (part_2, 2))
-        ]
+        parts = [to_chip(part, step) for part, step in ((part_3, 3), (part_1, 1), (part_2, 2))]
         keep, send = pl.pallas_call(
             far_kernel,
             out_shape=[
                 jax.ShapeDtypeStruct(piece, f32),
-                jax.ShapeDtypeStruct((JB * chunk, nk), bf16),
+                jax.ShapeDtypeStruct((JB * chunk, 2 * nk), bf16),
             ],
             in_specs=[vmem] * NEAR,
             out_specs=[vmem] * 2,
             compiler_params=params,
             name="far",
         )(mine, *parts)
-        got = lax.ppermute(send, "space", [(s, s ^ NEAR) for s in range(n)])
+        own_half, other_half = pl.pallas_call(
+            result_kernel,
+            out_shape=[
+                jax.ShapeDtypeStruct((JB, chunk, nk), f32),
+                jax.ShapeDtypeStruct((JB * chunk, nk), f32),
+            ],
+            in_specs=[vmem] * 2,
+            out_specs=[vmem] * 2,
+            compiler_params=params,
+            name="result",
+        )(keep, to_chip(send, NEAR))
         return pl.pallas_call(
             total_kernel,
             out_shape=jax.ShapeDtypeStruct((chunk, JB, nk), f32),
@@ -448,7 +474,7 @@
             out_specs=vmem,
             compiler_params=params,
             name="total",
-        )(keep, got)
+        )(own_half, lax.ppermute(other_half, "modes", swap))
 
     count = nk // chunk
     keep, send, _ = crossed(count, lambda s: list(range(count)), ())

time: 31.3 us -> 39.3 us (1.26)
  starting transfers between devices: 13.3 us -> 26.1 us
  waiting for transfers between devices: 10.4 us -> 5.32 us
    ppermute x4 -> x5, starting transfers between devices: 5.63 us -> 18.4 us  [the longest x1 15.7 us: on_device(): lax.ppermute(other_half, 'modes', swap)]
    ppermute x4 -> x5, waiting for transfers between devices: 6.13 us -> 0.91 us  [the longest x1 0.9 us: on_device(): lax.ppermute(other_half, 'modes', swap)]
    pallas_call x2 -> x3, Pallas kernels: 1.31 us -> 1.32 us  [the longest x2 1.31 us: crossed(): pl.pallas_call(functools.partial(cross_kernel, classes_of, chunk, n, whol...]
  transfers between devices with their start and end apart: 11 -> 12, of which waited for: 7 -> 4; matrix products, arithmetic and copies ran while one was open for 0% -> 0% of each run, Pallas kernels for 13% -> 10%
where the time goes in v22:
time: 39.3 us; the launch traced here: 39.1 us
  starting transfers between devices  26.1 us (66%)
  Pallas kernels  6.89 us (18%)
  waiting for transfers between devices  5.32 us (14%)
  between operations  0.83 us (2%)
    ppermute x1, starting transfers between devices, on_device(): lax.ppermute(other_half, 'modes', swap)  15.7 us
    ppermute x1, waiting for transfers between devices, on_device(): xc = lax.ppermute(xc, both, cross([(s, x_to(s)) for s in range(n)]))  2.81 us
    ppermute x4, starting transfers between devices, to_chip(): return lax.ppermute(value, both, pairs)  2.67 us
    ppermute x1, starting transfers between devices, on_device(): second = lax.ppermute(second, both, same(seconds))  2.6 us
    ppermute x1, starting transfers between devices, on_device(): first = lax.ppermute(first, both, same(firsts))  2.53 us
    pallas_call x1, Pallas kernels, on_device(): pl.pallas_call(local_kernel, out_shape=[jax.ShapeDtypeStruct((JB * 2 * nk...  2.43 us
    pallas_call x1, Pallas kernels, on_device(): pl.pallas_call(functools.partial(prep_kernel, n), out_shape=[jax.ShapeDty...  1.38 us
    pallas_call x2, Pallas kernels, crossed(): pl.pallas_call(functools.partial(cross_kernel, classes_of, chunk, n, whol...  1.31 us
  transfers between devices with their start and end apart: 12, of which 4 were waited for; matrix products, arithmetic and copies ran while one was open for 0% of the time, Pallas kernels for 10%

profile of v22, /device:TPU:0, one launch (start us, length us, event | category | flops | bytes accessed | tf_op | source)
XLA Modules:
  0.0 39.1 jit_solution(14268925745191263485)
XLA Ops:
  0.0 0.0 copy-start.1
  0.0 1.4 %prep.1 = (bf16[8,3,128,128]{3,2,1,0:T(8,128)(2,1)S(1)}, bf16[784,128]{1,0:T(8,128)(2,1)S(1)}, bf16[784,128]{1,0:T(8,128)(2,1)S(1)}) custom-call(bf16[128,3,1,8,128]{4,3,2,1,0:T(8,128)(2,1)} %modes_hbm.1), custom_call_target="tpu_custom_call" | custom-call | flops 1500000000 | bytes 2800000 | tf_op jit(solution)/shard_map/prep/pallas_call | solution.py:325
  1.4 0.0 copy-start
  1.4 0.5 %collective-permute-start = (bf16[8,3,128,128]{3,2,1,0:T(8,128)(2,1)S(1)}, bf16[8,3,128,128]{3,2,1,0:T(8,128)(2,1)S(1)}, u32[]{:S(2)}, u32[]{:S(2)}) collective-permute-start(bf16[8,3,128,128]{3,2,1,0:T(8,128)(2,1)S(1)} %get-tuple-element.28.tr.own_ref), channel_id=1, source_target_pairs={{0,1},{1,0},{2,3},{3,2},{4,5},{5,4},{6,7},{7,6},{8,9},{9,8},{10,11... | collective-permute-start | bytes 2359304 | tf_op jit(solution)/shard_map/ppermute | solution.py:345
  1.9 2.5 %collective-permute-start.1 = (bf16[784,128]{1,0:T(8,128)(2,1)S(1)}, bf16[784,128]{1,0:T(8,128)(2,1)S(1)}, u32[]{:S(2)}, u32[]{:S(2)}) collective-permute-start(bf16[784,128]{1,0:T(8,128)(2,1)S(1)} %get-tuple-element.29), channel_id=1, source_target_pairs={{0,2},{1,3},{2,0},{3,1},{4,6},{5,7},{6,4},{7,5},{8,10},{9,11},{10,... | collective-permute-start | bytes 602120 | tf_op jit(solution)/shard_map/ppermute | solution.py:346
  4.5 2.6 %collective-permute-start.2 = (bf16[784,128]{1,0:T(8,128)(2,1)S(1)}, bf16[784,128]{1,0:T(8,128)(2,1)S(1)}, u32[]{:S(2)}, u32[]{:S(2)}) collective-permute-start(bf16[784,128]{1,0:T(8,128)(2,1)S(1)} %get-tuple-element.30), channel_id=1, source_target_pairs={{0,12},{1,13},{2,6},{3,7},{4,0},{5,1},{6,10},{7,11},{8,4},{9,5},{1... | collective-permute-start | bytes 602120 | tf_op jit(solution)/shard_map/ppermute | solution.py:347
  7.1 0.0 collective-permute-done._.other_ref
  7.1 0.0 copy-done.1
  7.1 0.0 copy-done
  7.1 0.1 weights.1
  7.2 0.1 collective-permute-start.3
  7.3 1.3 %collective-permute-start.4 = (bf16[784,128]{1,0:T(8,128)(2,1)S(1)}, bf16[784,128]{1,0:T(8,128)(2,1)S(1)}, u32[]{:S(2)}, u32[]{:S(2)}) collective-permute-start(bf16[784,128]{1,0:T(8,128)(2,1)S(1)} %get-tuple-element.32), channel_id=1, source_target_pairs={{2,7},{3,6},{4,1},{5,0},{6,11},{7,10},{8,5},{9,4},{10,15},{11,14},... | collective-permute-start | bytes 602120 | tf_op jit(solution)/shard_map/ppermute | solution.py:358
  9.2 2.4 %local.1 = (f32[1024,256]{1,0:T(8,128)S(1)}, bf16[2,256,384]{2,1,0:T(8,128)(2,1)S(1)}) custom-call(bf16[8,3,128,128]{3,2,1,0:T(8,128)(2,1)S(1)} %get-tuple-element.28.tr.own_ref, bf16[8,3,128,128]{3,2,1,0:T(8,128)(2,1)S(1)} %collective-permute-done._.other_ref, f32[8,128]{1,0:T(8,128)S(1)} %get-tuple-element.33.weight_ref, s32[1]{0:T(128)S(6)} %copy.5.jb_ref.refs_5_), custom_call_target="tpu_custom_call" | custom-call | flops 900000000 | bytes 2400000 | tf_op jit(solution)/shard_map/local/pallas_call | solution.py:362
  11.7 0.0 collective-permute-done.1.first_ref.refs_0_
  11.7 0.0 collective-permute-done.2.second_ref.refs_1_
  11.7 2.8 %collective-permute-done.3.xc_ref.refs_2_ = bf16[784,128]{1,0:T(8,128)(2,1)S(1)} collective-permute-done((bf16[784,128]{1,0:T(8,128)(2,1)S(1)}, bf16[784,128]{1,0:T(8,128)(2,1)S(1)}, u32[]{:S(2)}, u32[]{:S(2)}) %collective-permute-start.3) | collective-permute-done | bytes 200736 | tf_op jit(solution)/shard_map/ppermute | solution.py:357
  14.5 0.8 %early.1 = (f32[1024,256]{1,0:T(8,128)S(1)}, bf16[256,768]{1,0:T(8,128)(2,1)S(1)}) custom-call(bf16[8,3,128,128]{3,2,1,0:T(8,128)(2,1)S(1)} %get-tuple-element.28.tr.own_ref, bf16[8,3,128,128]{3,2,1,0:T(8,128)(2,1)S(1)} %collective-permute-done._.other_ref, bf16[784,128]{1,0:T(8,128)(2,1)S(1)} %collective-permute-done.1.first_ref.refs_0_, ...), custom_call_target="tpu_custom_call" | custom-call | flops 600000000 | bytes 2400000 | tf_op jit(solution)/shard_map/early/pallas_call | solution.py:379
  15.3 1.3 %collective-permute-done.4.refs_3_ = bf16[784,128]{1,0:T(8,128)(2,1)S(1)} collective-permute-done((bf16[784,128]{1,0:T(8,128)(2,1)S(1)}, bf16[784,128]{1,0:T(8,128)(2,1)S(1)}, u32[]{:S(2)}, u32[]{:S(2)}) %collective-permute-start.4) | collective-permute-done | bytes 200736 | tf_op jit(solution)/shard_map/ppermute | solution.py:358
  16.5 0.7 %cross.2 = (f32[2,2,4,32,256]{4,3,2,1,0:T(8,128)S(1)}, bf16[512,256]{1,0:T(8,128)(2,1)S(1)}, bf16[256,1536]{1,0:T(8,128)(2,1)S(1)}) custom-call(bf16[8,3,128,128]{3,2,1,0:T(8,128)(2,1)S(1)} %get-tuple-element.28.tr.own_ref, bf16[8,3,128,128]{3,2,1,0:T(8,128)(2,1)S(1)} %collective-permute-done._.other_ref, ...), custom_call_target="tpu_custom_call" | custom-call | flops 900000000 | bytes 4000000 | tf_op jit(solution)/shard_map/cross/pallas_call | solution.py:405
  17.2 0.2 collective-permute-start.6
  17.4 0.6 %cross.3 = (f32[2,2,4,32,256]{4,3,2,1,0:T(8,128)S(1)}, bf16[512,256]{1,0:T(8,128)(2,1)S(1)}) custom-call(bf16[8,3,128,128]{3,2,1,0:T(8,128)(2,1)S(1)} %get-tuple-element.28.tr.own_ref, bf16[8,3,128,128]{3,2,1,0:T(8,128)(2,1)S(1)} %collective-permute-done._.other_ref, bf16[784,128]{1,0:T(8,128)(2,1)S(1)} %collective-permute-done.1.first_ref.refs_0_, ...), custom_call_target="tpu_custom_call" | custom-call | flops 900000000 | bytes 4000000 | tf_op jit(solution)/shard_map/cross/pallas_call | solution.py:405
  18.0 0.5 %collective-permute-start.5 = (bf16[512,256]{1,0:T(8,128)(2,1)S(1)}, bf16[512,256]{1,0:T(8,128)(2,1)S(1)}, u32[]{:S(2)}, u32[]{:S(2)}) collective-permute-start(bf16[512,256]{1,0:T(8,128)(2,1)S(1)} %get-tuple-element.40), channel_id=1, source_target_pairs={{0,1},{1,0},{2,3},{3,2},{4,5},{5,4},{6,7},{7,6},{8,9},{9,8},{10,11... | collective-permute-start | bytes 786440 | tf_op jit(solution)/shard_map/ppermute | solution.py:430
  18.5 0.3 collective-permute-done.6.got_ref
  18.8 0.1 near.3
  18.9 0.7 %collective-permute-start.7 = (bf16[256,256]{1,0:T(8,128)(2,1)S(1)}, bf16[256,256]{1,0:T(8,128)(2,1)S(1)}, u32[]{:S(2)}, u32[]{:S(2)}) collective-permute-start(bf16[256,256]{1,0:T(8,128)(2,1)S(1)} %get-tuple-element.44), channel_id=1, source_target_pairs={{0,0},{2,2},{4,4},{6,6},{8,8},{10,10},{12,12},{14,14},{1,7},{3,5},... | collective-permute-start | bytes 393224 | tf_op jit(solution)/shard_map/ppermute | solution.py:425
  19.6 0.7 %collective-permute-start.8 = (bf16[256,256]{1,0:T(8,128)(2,1)S(1)}, bf16[256,256]{1,0:T(8,128)(2,1)S(1)}, u32[]{:S(2)}, u32[]{:S(2)}) collective-permute-start(bf16[256,256]{1,0:T(8,128)(2,1)S(1)} %get-tuple-element.45), channel_id=1, source_target_pairs={{0,0},{2,2},{4,4},{6,6},{8,8},{10,10},{12,12},{14,14},{1,3},{3,1},... | collective-permute-start | bytes 393224 | tf_op jit(solution)/shard_map/ppermute | solution.py:425
  20.2 0.0 collective-permute-done.5.got_ref
  20.3 0.1 near.2
  20.3 0.7 %collective-permute-start.9 = (bf16[256,256]{1,0:T(8,128)(2,1)S(1)}, bf16[256,256]{1,0:T(8,128)(2,1)S(1)}, u32[]{:S(2)}, u32[]{:S(2)}) collective-permute-start(bf16[256,256]{1,0:T(8,128)(2,1)S(1)} %get-tuple-element.46), channel_id=1, source_target_pairs={{0,0},{2,2},{4,4},{6,6},{8,8},{10,10},{12,12},{14,14},{1,5},{3,7},... | collective-permute-start | bytes 393224 | tf_op jit(solution)/shard_map/ppermute | solution.py:425
  21.0 0.0 collective-permute-done.7.refs_0_
  21.0 0.0 collective-permute-done.8.refs_1_
  21.0 0.0 collective-permute-done.9.refs_2_
  21.0 0.1 far.1
  21.1 0.7 %collective-permute-start.10 = (bf16[128,256]{1,0:T(8,128)(2,1)S(1)}, bf16[128,256]{1,0:T(8,128)(2,1)S(1)}, u32[]{:S(2)}, u32[]{:S(2)}) collective-permute-start(bf16[128,256]{1,0:T(8,128)(2,1)S(1)} %get-tuple-element.48), channel_id=1, source_target_pairs={{0,0},{2,2},{4,4},{6,6},{8,8},{10,10},{12,12},{14,14},{1,9},{3,11}... | collective-permute-start | bytes 196616 | tf_op jit(solution)/shard_map/ppermute | solution.py:425
  21.8 0.0 collective-permute-done.10.got_ref
  21.8 15.7 %collective-permute-start.11 = (f32[128,128]{1,0:T(8,128)S(1)}, f32[128,128]{1,0:T(8,128)S(1)}, u32[]{:S(2)}, u32[]{:S(2)}) collective-permute-start(f32[128,128]{1,0:T(8,128)S(1)} %get-tuple-element.50), channel_id=1, source_target_pairs={{0,1},{1,0},{2,3},{3,2},{4,5},{5,4},{6,7},{7,6},{8,9},{9,8},{10,11... | collective-permute-start | bytes 196616 | tf_op jit(solution)/shard_map/ppermute | solution.py:477
  37.5 0.9 %collective-permute-done.11.got_ref = f32[128,128]{1,0:T(8,128)S(1)} collective-permute-done((f32[128,128]{1,0:T(8,128)S(1)}, f32[128,128]{1,0:T(8,128)S(1)}, u32[]{:S(2)}, u32[]{:S(2)}) %collective-permute-start.11) | collective-permute-done | bytes 65568 | tf_op jit(solution)/shard_map/ppermute | solution.py:477
  38.4 0.7 %total.1 = f32[32,4,128]{2,1,0:T(4,128)} custom-call(f32[4,32,128]{2,1,0:T(8,128)S(1)} %get-tuple-element.49.own_ref, f32[128,128]{1,0:T(8,128)S(1)} %collective-permute-done.11.got_ref), custom_call_target="tpu_custom_call" | custom-call | tf_op jit(solution)/shard_map/total/pallas_call | solution.py:470
  (2 shorter events, 0.0 us)
Async XLA Ops:
  0.0 7.1 %copy-start.1 = (f32[16]{0:T(128)S(1)}, f32[16]{0:T(128)}, u32[]{:S(2)}) copy-start(f32[16]{0:T(128)} %param.6) | copy-start | bytes 196
  1.4 5.7 %copy-start = (s32[1,8,128]{2,1,0:T(8,128)S(1)}, s32[1,8,128]{2,1,0:T(8,128)}, u32[]{:S(2)}) copy-start(s32[1,8,128]{2,1,0:T(8,128)} %ids_ref.1) | copy-start | bytes 12292
  1.4 5.7 %collective-permute-start = (bf16[8,3,128,128]{3,2,1,0:T(8,128)(2,1)S(1)}, bf16[8,3,128,128]{3,2,1,0:T(8,128)(2,1)S(1)}, u32[]{:S(2)}, u32[]{:S(2)}) collective-permute-start(bf16[8,3,128,128]{3,2,1,0:T(8,128)(2,1)S(1)} %get-tuple-element.28.tr.own_ref), channel_id=1, source_target_pairs={{0,1},{1,0},{2,3},{3,2},{4,5},{5,4},{6,7},{7,6},{8,9},{9,8},{10,11... | collective-permute-start | bytes 2359304 | tf_op jit(solution)/shard_map/ppermute | solution.py:345
  1.9 9.7 %collective-permute-start.1 = (bf16[784,128]{1,0:T(8,128)(2,1)S(1)}, bf16[784,128]{1,0:T(8,128)(2,1)S(1)}, u32[]{:S(2)}, u32[]{:S(2)}) collective-permute-start(bf16[784,128]{1,0:T(8,128)(2,1)S(1)} %get-tuple-element.29), channel_id=1, source_target_pairs={{0,2},{1,3},{2,0},{3,1},{4,6},{5,7},{6,4},{7,5},{8,10},{9,11},{10,... | collective-permute-start | bytes 602120 | tf_op jit(solution)/shard_map/ppermute | solution.py:346
  4.5 7.2 %collective-permute-start.2 = (bf16[784,128]{1,0:T(8,128)(2,1)S(1)}, bf16[784,128]{1,0:T(8,128)(2,1)S(1)}, u32[]{:S(2)}, u32[]{:S(2)}) collective-permute-start(bf16[784,128]{1,0:T(8,128)(2,1)S(1)} %get-tuple-element.30), channel_id=1, source_target_pairs={{0,12},{1,13},{2,6},{3,7},{4,0},{5,1},{6,10},{7,11},{8,4},{9,5},{1... | collective-permute-start | bytes 602120 | tf_op jit(solution)/shard_map/ppermute | solution.py:347
  7.2 7.3 %collective-permute-start.3 = (bf16[784,128]{1,0:T(8,128)(2,1)S(1)}, bf16[784,128]{1,0:T(8,128)(2,1)S(1)}, u32[]{:S(2)}, u32[]{:S(2)}) collective-permute-start(bf16[784,128]{1,0:T(8,128)(2,1)S(1)} %get-tuple-element.31), channel_id=1, source_target_pairs={{0,3},{1,2},{2,1},{3,0},{4,7},{5,6},{6,5},{7,4},{8,11},{9,10},{10,... | collective-permute-start | bytes 602120 | tf_op jit(solution)/shard_map/ppermute | solution.py:357
  7.3 9.3 %collective-permute-start.4 = (bf16[784,128]{1,0:T(8,128)(2,1)S(1)}, bf16[784,128]{1,0:T(8,128)(2,1)S(1)}, u32[]{:S(2)}, u32[]{:S(2)}) collective-permute-start(bf16[784,128]{1,0:T(8,128)(2,1)S(1)} %get-tuple-element.32), channel_id=1, source_target_pairs={{2,7},{3,6},{4,1},{5,0},{6,11},{7,10},{8,5},{9,4},{10,15},{11,14},... | collective-permute-start | bytes 602120 | tf_op jit(solution)/shard_map/ppermute | solution.py:358
  17.2 1.6 %collective-permute-start.6 = (bf16[512,256]{1,0:T(8,128)(2,1)S(1)}, bf16[512,256]{1,0:T(8,128)(2,1)S(1)}, u32[]{:S(2)}, u32[]{:S(2)}) collective-permute-start(bf16[512,256]{1,0:T(8,128)(2,1)S(1)} %get-tuple-element.43), channel_id=1, source_target_pairs={{0,1},{1,0},{2,3},{3,2},{4,5},{5,4},{6,7},{7,6},{8,9},{9,8},{10,11... | collective-permute-start | bytes 786440 | tf_op jit(solution)/shard_map/ppermute | solution.py:428
  18.0 2.2 %collective-permute-start.5 = (bf16[512,256]{1,0:T(8,128)(2,1)S(1)}, bf16[512,256]{1,0:T(8,128)(2,1)S(1)}, u32[]{:S(2)}, u32[]{:S(2)}) collective-permute-start(bf16[512,256]{1,0:T(8,128)(2,1)S(1)} %get-tuple-element.40), channel_id=1, source_target_pairs={{0,1},{1,0},{2,3},{3,2},{4,5},{5,4},{6,7},{7,6},{8,9},{9,8},{10,11... | collective-permute-start | bytes 786440 | tf_op jit(solution)/shard_map/ppermute | solution.py:430
  18.9 2.1 %collective-permute-start.7 = (bf16[256,256]{1,0:T(8,128)(2,1)S(1)}, bf16[256,256]{1,0:T(8,128)(2,1)S(1)}, u32[]{:S(2)}, u32[]{:S(2)}) collective-permute-start(bf16[256,256]{1,0:T(8,128)(2,1)S(1)} %get-tuple-element.44), channel_id=1, source_target_pairs={{0,0},{2,2},{4,4},{6,6},{8,8},{10,10},{12,12},{14,14},{1,7},{3,5},... | collective-permute-start | bytes 393224 | tf_op jit(solution)/shard_map/ppermute | solution.py:425
  19.6 1.4 %collective-permute-start.8 = (bf16[256,256]{1,0:T(8,128)(2,1)S(1)}, bf16[256,256]{1,0:T(8,128)(2,1)S(1)}, u32[]{:S(2)}, u32[]{:S(2)}) collective-permute-start(bf16[256,256]{1,0:T(8,128)(2,1)S(1)} %get-tuple-element.45), channel_id=1, source_target_pairs={{0,0},{2,2},{4,4},{6,6},{8,8},{10,10},{12,12},{14,14},{1,3},{3,1},... | collective-permute-start | bytes 393224 | tf_op jit(solution)/shard_map/ppermute | solution.py:425
  20.3 0.7 %collective-permute-start.9 = (bf16[256,256]{1,0:T(8,128)(2,1)S(1)}, bf16[256,256]{1,0:T(8,128)(2,1)S(1)}, u32[]{:S(2)}, u32[]{:S(2)}) collective-permute-start(bf16[256,256]{1,0:T(8,128)(2,1)S(1)} %get-tuple-element.46), channel_id=1, source_target_pairs={{0,0},{2,2},{4,4},{6,6},{8,8},{10,10},{12,12},{14,14},{1,5},{3,7},... | collective-permute-start | bytes 393224 | tf_op jit(solution)/shard_map/ppermute | solution.py:425
  21.1 0.7 %collective-permute-start.10 = (bf16[128,256]{1,0:T(8,128)(2,1)S(1)}, bf16[128,256]{1,0:T(8,128)(2,1)S(1)}, u32[]{:S(2)}, u32[]{:S(2)}) collective-permute-start(bf16[128,256]{1,0:T(8,128)(2,1)S(1)} %get-tuple-element.48), channel_id=1, source_target_pairs={{0,0},{2,2},{4,4},{6,6},{8,8},{10,10},{12,12},{14,14},{1,9},{3,11}... | collective-permute-start | bytes 196616 | tf_op jit(solution)/shard_map/ppermute | solution.py:425
  21.8 16.6 %collective-permute-start.11 = (f32[128,128]{1,0:T(8,128)S(1)}, f32[128,128]{1,0:T(8,128)S(1)}, u32[]{:S(2)}, u32[]{:S(2)}) collective-permute-start(f32[128,128]{1,0:T(8,128)S(1)} %get-tuple-element.50), channel_id=1, source_target_pairs={{0,1},{1,0},{2,3},{3,2},{4,5},{5,4},{6,7},{7,6},{8,9},{9,8},{10,11... | collective-permute-start | bytes 196616 | tf_op jit(solution)/shard_map/ppermute | solution.py:477

commit v23 on v19

--- a/solution.py
+++ b/solution.py
@@ -276,26 +276,53 @@
                 send_ref[pl.ds(row, chunk), :] = piece[:, nk:].astype(jnp.bfloat16)
 
 
-def near_kernel(keep_ref, got_ref, *out_refs):
-    got = got_ref[...].astype(jnp.float32).reshape(keep_ref.shape)
-    for at, ref in enumerate(out_refs):
-        ref[...] = (keep_ref[at] + got[at]).astype(ref.dtype).reshape(ref.shape)
-
-
-def far_kernel(mine_ref, *refs):
-    *parts, keep_ref, send_ref = refs
-    level = lax.div(lax.axis_index("space"), NEAR)
-    rows = send_ref.shape[0]
-    for ref, at in ((keep_ref, level), (send_ref, 1 - level)):
-        total = mine_ref[at]
-        for part in parts:
-            piece = part[pl.ds(pl.multiple_of(at * rows, rows), rows), :]
-            total = total + piece.astype(jnp.float32).reshape(total.shape)
-        ref[...] = total.astype(ref.dtype).reshape(ref.shape)
-
-
-def total_kernel(keep_ref, got_ref, out_ref):
-    total = keep_ref[...] + got_ref[...].astype(jnp.float32).reshape(keep_ref.shape)
+def level_of():
+    return lax.div(lax.axis_index("space"), NEAR)
+
+
+def chip_sum(keep_ref, got_ref, at, level):
+    rows = JB * keep_ref.shape[3]
+    row = pl.multiple_of((2 * at + level) * rows, rows)
+    got = got_ref[pl.ds(row, rows), :].astype(jnp.float32)
+    return keep_ref[at, level] + got.reshape(keep_ref.shape[2:])
+
+
+def put(ref, value):
+    ref[...] = value.astype(ref.dtype).reshape(ref.shape)
+
+
+def plus(total, refs):
+    for ref in refs:
+        total = total + ref[...].astype(jnp.float32).reshape(total.shape)
+    return total
+
+
+def away_kernel(keep_ref, got_ref, first_ref, second_ref):
+    put(first_ref, chip_sum(keep_ref, got_ref, 0, 1 - level_of()))
+    put(second_ref, chip_sum(keep_ref, got_ref, 1, 1 - level_of()))
+
+
+def mine_kernel(keep_ref, got_ref, mine_ref, up_ref):
+    for level in range(2):
+        mine_ref[level] = chip_sum(keep_ref, got_ref, 0, level)
+    put(up_ref, chip_sum(keep_ref, got_ref, 1, 1 - level_of()))
+
+
+def here_kernel(keep_ref, got_ref, _, first_ref, second_ref):
+    put(first_ref, chip_sum(keep_ref, got_ref, 0, level_of()))
+    put(second_ref, chip_sum(keep_ref, got_ref, 1, level_of()))
+
+
+def far_kernel(mine_ref, p0_ref, p1_ref, p2_ref, send_ref):
+    put(send_ref, plus(mine_ref[1 - level_of()], (p0_ref, p1_ref, p2_ref)))
+
+
+def last_kernel(keep_ref, got_ref, _, up_ref):
+    put(up_ref, chip_sum(keep_ref, got_ref, 1, level_of()))
+
+
+def total_kernel(mine_ref, p0_ref, p1_ref, p2_ref, p3_ref, out_ref):
+    total = plus(mine_ref[level_of()], (p0_ref, p1_ref, p2_ref, p3_ref))
     for j in range(JB):
         out_ref[:, j, :] = total[j]
 
@@ -411,44 +438,32 @@
         got_b = lax.ppermute(send_b, "modes", swap)
         piece = (JB, chunk, nk)
 
-        def summed(out_shape, keep, got):
+        def made(body_of, out_shape, operands, order=()):
             return pl.pallas_call(
-                near_kernel,
+                body_of,
                 out_shape=out_shape,
-                in_specs=[vmem] * 2,
-                out_specs=[vmem] * 2,
+                in_specs=[vmem] * len(operands) + [pl.BlockSpec(memory_space=pl.ANY)] * len(order),
+                out_specs=jax.tree.map(lambda _: vmem, out_shape),
                 compiler_params=params,
-                name="near",
-            )(keep, got)
+                name=body_of.__name__.removesuffix("_kernel"),
+            )(*operands, *order)
+
+        def to_chip(value, step):
+            return lax.ppermute(value, "space", [(s, s ^ step) for s in range(n)])
 
         kept = jax.ShapeDtypeStruct((2, *piece), f32)
-        sent = jax.ShapeDtypeStruct((2 * JB * chunk, nk), bf16)
-        part_3, part_1 = summed([sent, sent], keep_a, got_a)
-        mine, part_2 = summed([kept, sent], keep_b, got_b)
+        sent = jax.ShapeDtypeStruct((JB * chunk, nk), bf16)
+        away_3, away_1 = made(away_kernel, [sent, sent], (keep_a, got_a))
+        mine, away_2 = made(mine_kernel, [kept, sent], (keep_b, got_b))
+        here_3, here_1 = made(here_kernel, [sent, sent], (keep_a, got_a), (away_2,))
+        away = [to_chip(part, step) for part, step in ((away_3, 3), (away_1, 1), (away_2, 2))]
+        far = made(far_kernel, sent, (mine, *away))
+        here_2 = made(last_kernel, sent, (keep_b, got_b), (far,))
         parts = [
-            lax.ppermute(part, "space", [(s, s ^ step) for s in range(n)])
-            for part, step in ((part_3, 3), (part_1, 1), (part_2, 2))
+            to_chip(part, step)
+            for part, step in ((here_3, 3), (here_1, 1), (far, NEAR), (here_2, 2))
         ]
-        keep, send = pl.pallas_call(
-            far_kernel,
-            out_shape=[
-                jax.ShapeDtypeStruct(piece, f32),
-                jax.ShapeDtypeStruct((JB * chunk, nk), bf16),
-            ],
-            in_specs=[vmem] * NEAR,
-            out_specs=[vmem] * 2,
-            compiler_params=params,
-            name="far",
-        )(mine, *parts)
-        got = lax.ppermute(send, "space", [(s, s ^ NEAR) for s in range(n)])
-        return pl.pallas_call(
-            total_kernel,
-            out_shape=jax.ShapeDtypeStruct((chunk, JB, nk), f32),
-            in_specs=[vmem] * 2,
-            out_specs=vmem,
-            compiler_params=params,
-            name="total",
-        )(keep, got)
+        return made(total_kernel, jax.ShapeDtypeStruct((chunk, JB, nk), f32), (mine, *parts))
 
     count = nk // chunk
     keep, send, _ = crossed(count, lambda s: list(range(count)), ())

time: 31.3 us -> 32.6 us (1.042)
  starting transfers between devices: 13.3 us -> 17.2 us
  waiting for transfers between devices: 10.4 us -> 7.64 us
    ppermute x4 -> x7, starting transfers between devices: 5.63 us -> 9.57 us  [to_chip(): return lax.ppermute(value, 'space', [(s, s ^ step) for s in range(n)])]
    ppermute x4 -> x7, waiting for transfers between devices: 6.13 us -> 3.42 us  [to_chip(): return lax.ppermute(value, 'space', [(s, s ^ step) for s in range(n)])]
    pallas_call x4 -> x6, Pallas kernels: 0.75 us -> 0.79 us  [made(): pl.pallas_call(body_of, out_shape=out_shape, in_specs=[vmem] * len(operan...]
  transfers between devices with their start and end apart: 11 -> 14, of which waited for: 7 -> 6; matrix products, arithmetic and copies ran while one was open for 0% -> 0% of each run, Pallas kernels for 13% -> 13%
where the time goes in v23:
time: 32.6 us; the launch traced here: 32.4 us
  starting transfers between devices  17.2 us (53%)
  waiting for transfers between devices  7.64 us (23%)
  Pallas kernels  6.8 us (21%)
  between operations  0.77 us (2%)
    ppermute x7, starting transfers between devices, to_chip(): return lax.ppermute(value, 'space', [(s, s ^ step) for s in range(n)])  9.57 us
    ppermute x7, waiting for transfers between devices, to_chip(): return lax.ppermute(value, 'space', [(s, s ^ step) for s in range(n)])  3.42 us
    ppermute x1, waiting for transfers between devices, on_device(): xc = lax.ppermute(xc, both, cross([(s, x_to(s)) for s in range(n)]))  2.81 us
    ppermute x1, starting transfers between devices, on_device(): second = lax.ppermute(second, both, same(seconds))  2.6 us
    ppermute x1, starting transfers between devices, on_device(): first = lax.ppermute(first, both, same(firsts))  2.53 us
    pallas_call x1, Pallas kernels, on_device(): pl.pallas_call(local_kernel, out_shape=[jax.ShapeDtypeStruct((JB * 2 * nk...  2.43 us
    pallas_call x1, Pallas kernels, on_device(): pl.pallas_call(functools.partial(prep_kernel, n), out_shape=[jax.ShapeDty...  1.38 us
    pallas_call x2, Pallas kernels, crossed(): pl.pallas_call(functools.partial(cross_kernel, classes_of, chunk, n, bool...  1.31 us
  transfers between devices with their start and end apart: 14, of which 6 were waited for; matrix products, arithmetic and copies ran while one was open for 0% of the time, Pallas kernels for 13%

profile of v23, /device:TPU:0, one launch (start us, length us, event | category | flops | bytes accessed | tf_op | source)
XLA Modules:
  0.0 32.4 jit_solution(1141513663911539892)
XLA Ops:
  0.0 0.0 copy-start.1
  0.0 1.4 %prep.1 = (bf16[8,3,128,128]{3,2,1,0:T(8,128)(2,1)S(1)}, bf16[784,128]{1,0:T(8,128)(2,1)S(1)}, bf16[784,128]{1,0:T(8,128)(2,1)S(1)}) custom-call(bf16[128,3,1,8,128]{4,3,2,1,0:T(8,128)(2,1)} %modes_hbm.1), custom_call_target="tpu_custom_call" | custom-call | flops 1500000000 | bytes 2800000 | tf_op jit(solution)/shard_map/prep/pallas_call | solution.py:338
  1.4 0.0 copy-start
  1.4 0.5 %collective-permute-start = (bf16[8,3,128,128]{3,2,1,0:T(8,128)(2,1)S(1)}, bf16[8,3,128,128]{3,2,1,0:T(8,128)(2,1)S(1)}, u32[]{:S(2)}, u32[]{:S(2)}) collective-permute-start(bf16[8,3,128,128]{3,2,1,0:T(8,128)(2,1)S(1)} %get-tuple-element.26.tr.own_ref), channel_id=1, source_target_pairs={{0,1},{1,0},{2,3},{3,2},{4,5},{5,4},{6,7},{7,6},{8,9},{9,8},{10,11... | collective-permute-start | bytes 2359304 | tf_op jit(solution)/shard_map/ppermute | solution.py:358
  1.9 2.5 %collective-permute-start.1 = (bf16[784,128]{1,0:T(8,128)(2,1)S(1)}, bf16[784,128]{1,0:T(8,128)(2,1)S(1)}, u32[]{:S(2)}, u32[]{:S(2)}) collective-permute-start(bf16[784,128]{1,0:T(8,128)(2,1)S(1)} %get-tuple-element.27), channel_id=1, source_target_pairs={{0,2},{1,3},{2,0},{3,1},{4,6},{5,7},{6,4},{7,5},{8,10},{9,11},{10,... | collective-permute-start | bytes 602120 | tf_op jit(solution)/shard_map/ppermute | solution.py:359
  4.5 2.6 %collective-permute-start.2 = (bf16[784,128]{1,0:T(8,128)(2,1)S(1)}, bf16[784,128]{1,0:T(8,128)(2,1)S(1)}, u32[]{:S(2)}, u32[]{:S(2)}) collective-permute-start(bf16[784,128]{1,0:T(8,128)(2,1)S(1)} %get-tuple-element.28), channel_id=1, source_target_pairs={{0,12},{1,13},{2,6},{3,7},{4,0},{5,1},{6,10},{7,11},{8,4},{9,5},{1... | collective-permute-start | bytes 602120 | tf_op jit(solution)/shard_map/ppermute | solution.py:360
  7.1 0.0 collective-permute-done._.other_ref
  7.1 0.0 copy-done.1
  7.1 0.0 copy-done
  7.1 0.1 weights.1
  7.2 0.1 collective-permute-start.3
  7.3 1.3 %collective-permute-start.4 = (bf16[784,128]{1,0:T(8,128)(2,1)S(1)}, bf16[784,128]{1,0:T(8,128)(2,1)S(1)}, u32[]{:S(2)}, u32[]{:S(2)}) collective-permute-start(bf16[784,128]{1,0:T(8,128)(2,1)S(1)} %get-tuple-element.30), channel_id=1, source_target_pairs={{2,7},{3,6},{4,1},{5,0},{6,11},{7,10},{8,5},{9,4},{10,15},{11,14},... | collective-permute-start | bytes 602120 | tf_op jit(solution)/shard_map/ppermute | solution.py:371
  9.2 2.4 %local.1 = (f32[1024,256]{1,0:T(8,128)S(1)}, bf16[2,256,384]{2,1,0:T(8,128)(2,1)S(1)}) custom-call(bf16[8,3,128,128]{3,2,1,0:T(8,128)(2,1)S(1)} %get-tuple-element.26.tr.own_ref, bf16[8,3,128,128]{3,2,1,0:T(8,128)(2,1)S(1)} %collective-permute-done._.other_ref, f32[8,128]{1,0:T(8,128)S(1)} %get-tuple-element.31.weight_ref, s32[1]{0:T(128)S(6)} %copy.5.jb_ref.refs_5_), custom_call_target="tpu_custom_call" | custom-call | flops 900000000 | bytes 2400000 | tf_op jit(solution)/shard_map/local/pallas_call | solution.py:375
  11.7 0.0 collective-permute-done.1.first_ref.refs_0_
  11.7 0.0 collective-permute-done.2.second_ref.refs_1_
  11.7 2.8 %collective-permute-done.3.xc_ref.refs_2_ = bf16[784,128]{1,0:T(8,128)(2,1)S(1)} collective-permute-done((bf16[784,128]{1,0:T(8,128)(2,1)S(1)}, bf16[784,128]{1,0:T(8,128)(2,1)S(1)}, u32[]{:S(2)}, u32[]{:S(2)}) %collective-permute-start.3) | collective-permute-done | bytes 200736 | tf_op jit(solution)/shard_map/ppermute | solution.py:370
  14.5 0.8 %early.1 = (f32[1024,256]{1,0:T(8,128)S(1)}, bf16[256,768]{1,0:T(8,128)(2,1)S(1)}) custom-call(bf16[8,3,128,128]{3,2,1,0:T(8,128)(2,1)S(1)} %get-tuple-element.26.tr.own_ref, bf16[8,3,128,128]{3,2,1,0:T(8,128)(2,1)S(1)} %collective-permute-done._.other_ref, bf16[784,128]{1,0:T(8,128)(2,1)S(1)} %collective-permute-done.1.first_ref.refs_0_, ...), custom_call_target="tpu_custom_call" | custom-call | flops 600000000 | bytes 2400000 | tf_op jit(solution)/shard_map/early/pallas_call | solution.py:392
  15.3 1.3 %collective-permute-done.4.refs_3_ = bf16[784,128]{1,0:T(8,128)(2,1)S(1)} collective-permute-done((bf16[784,128]{1,0:T(8,128)(2,1)S(1)}, bf16[784,128]{1,0:T(8,128)(2,1)S(1)}, u32[]{:S(2)}, u32[]{:S(2)}) %collective-permute-start.4) | collective-permute-done | bytes 200736 | tf_op jit(solution)/shard_map/ppermute | solution.py:371
  16.5 0.7 %cross.2 = (f32[2,2,4,32,128]{4,3,2,1,0:T(8,128)S(1)}, bf16[512,128]{1,0:T(8,128)(2,1)S(1)}, bf16[256,1536]{1,0:T(8,128)(2,1)S(1)}) custom-call(bf16[8,3,128,128]{3,2,1,0:T(8,128)(2,1)S(1)} %get-tuple-element.26.tr.own_ref, bf16[8,3,128,128]{3,2,1,0:T(8,128)(2,1)S(1)} %collective-permute-done._.other_ref, ...), custom_call_target="tpu_custom_call" | custom-call | flops 900000000 | bytes 4000000 | tf_op jit(solution)/shard_map/cross/pallas_call | solution.py:417
  17.2 0.2 collective-permute-start.6
  17.4 0.6 %cross.3 = (f32[2,2,4,32,128]{4,3,2,1,0:T(8,128)S(1)}, bf16[512,128]{1,0:T(8,128)(2,1)S(1)}) custom-call(bf16[8,3,128,128]{3,2,1,0:T(8,128)(2,1)S(1)} %get-tuple-element.26.tr.own_ref, bf16[8,3,128,128]{3,2,1,0:T(8,128)(2,1)S(1)} %collective-permute-done._.other_ref, bf16[784,128]{1,0:T(8,128)(2,1)S(1)} %collective-permute-done.1.first_ref.refs_0_, ...), custom_call_target="tpu_custom_call" | custom-call | flops 900000000 | bytes 4000000 | tf_op jit(solution)/shard_map/cross/pallas_call | solution.py:417
  18.0 0.5 %collective-permute-start.5 = (bf16[512,128]{1,0:T(8,128)(2,1)S(1)}, bf16[512,128]{1,0:T(8,128)(2,1)S(1)}, u32[]{:S(2)}, u32[]{:S(2)}) collective-permute-start(bf16[512,128]{1,0:T(8,128)(2,1)S(1)} %get-tuple-element.38), channel_id=1, source_target_pairs={{0,1},{1,0},{2,3},{3,2},{4,5},{5,4},{6,7},{7,6},{8,9},{9,8},{10,11... | collective-permute-start | bytes 393224 | tf_op jit(solution)/shard_map/ppermute | solution.py:438
  18.5 0.1 collective-permute-done.6.got_ref
  18.7 1.5 %collective-permute-start.9 = (bf16[128,128]{1,0:T(8,128)(2,1)S(1)}, bf16[128,128]{1,0:T(8,128)(2,1)S(1)}, u32[]{:S(2)}, u32[]{:S(2)}) collective-permute-start(bf16[128,128]{1,0:T(8,128)(2,1)S(1)} %get-tuple-element.45), channel_id=1, source_target_pairs={{0,6},{2,4},{4,2},{6,0},{8,14},{10,12},{12,10},{14,8},{1,7},{3,5},... | collective-permute-start | bytes 98312 | tf_op jit(solution)/shard_map/ppermute | solution.py:452
  20.2 1.0 %collective-permute-start.10 = (bf16[128,128]{1,0:T(8,128)(2,1)S(1)}, bf16[128,128]{1,0:T(8,128)(2,1)S(1)}, u32[]{:S(2)}, u32[]{:S(2)}) collective-permute-start(bf16[128,128]{1,0:T(8,128)(2,1)S(1)} %get-tuple-element.46), channel_id=1, source_target_pairs={{0,2},{2,0},{4,6},{6,4},{8,10},{10,8},{12,14},{14,12},{1,3},{3,1},... | collective-permute-start | bytes 98312 | tf_op jit(solution)/shard_map/ppermute | solution.py:452
  21.2 0.0 collective-permute-done.5.got_ref
  21.2 1.1 %collective-permute-start.11 = (bf16[128,128]{1,0:T(8,128)(2,1)S(1)}, bf16[128,128]{1,0:T(8,128)(2,1)S(1)}, u32[]{:S(2)}, u32[]{:S(2)}) collective-permute-start(bf16[128,128]{1,0:T(8,128)(2,1)S(1)} %get-tuple-element.42._), channel_id=1, source_target_pairs={{0,4},{2,6},{4,0},{6,2},{8,12},{10,14},{12,8},{14,10},{1,5},{3,7},... | collective-permute-start | bytes 98312 | tf_op jit(solution)/shard_map/ppermute | solution.py:452
  22.3 1.5 %collective-permute-start.7 = (bf16[128,128]{1,0:T(8,128)(2,1)S(1)}, bf16[128,128]{1,0:T(8,128)(2,1)S(1)}, u32[]{:S(2)}, u32[]{:S(2)}) collective-permute-start(bf16[128,128]{1,0:T(8,128)(2,1)S(1)} %get-tuple-element.43), channel_id=1, source_target_pairs={{0,6},{2,4},{4,2},{6,0},{8,14},{10,12},{12,10},{14,8},{1,7},{3,5},... | collective-permute-start | bytes 98312 | tf_op jit(solution)/shard_map/ppermute | solution.py:452
  23.9 1.0 %collective-permute-start.8 = (bf16[128,128]{1,0:T(8,128)(2,1)S(1)}, bf16[128,128]{1,0:T(8,128)(2,1)S(1)}, u32[]{:S(2)}, u32[]{:S(2)}) collective-permute-start(bf16[128,128]{1,0:T(8,128)(2,1)S(1)} %get-tuple-element.44), channel_id=1, source_target_pairs={{0,2},{2,0},{4,6},{6,4},{8,10},{10,8},{12,14},{14,12},{1,3},{3,1},... | collective-permute-start | bytes 98312 | tf_op jit(solution)/shard_map/ppermute | solution.py:452
  24.9 0.0 collective-permute-done.9.p0_ref
  24.9 0.0 collective-permute-done.10.p1_ref
  24.9 0.3 %collective-permute-done.11.p2_ref = bf16[128,128]{1,0:T(8,128)(2,1)S(1)} collective-permute-done((bf16[128,128]{1,0:T(8,128)(2,1)S(1)}, bf16[128,128]{1,0:T(8,128)(2,1)S(1)}, u32[]{:S(2)}, u32[]{:S(2)}) %collective-permute-start.11) | collective-permute-done | bytes 32800 | tf_op jit(solution)/shard_map/ppermute | solution.py:452
  25.3 1.3 %collective-permute-start.13 = (bf16[128,128]{1,0:T(8,128)(2,1)S(1)}, bf16[128,128]{1,0:T(8,128)(2,1)S(1)}, u32[]{:S(2)}, u32[]{:S(2)}) collective-permute-start(bf16[128,128]{1,0:T(8,128)(2,1)S(1)} %last.1), channel_id=1, source_target_pairs={{0,4},{2,6},{4,0},{6,2},{8,12},{10,14},{12,8},{14,10},{1,5},{3,7},... | collective-permute-start | bytes 98312 | tf_op jit(solution)/shard_map/ppermute | solution.py:452
  26.6 2.1 %collective-permute-start.12 = (bf16[128,128]{1,0:T(8,128)(2,1)S(1)}, bf16[128,128]{1,0:T(8,128)(2,1)S(1)}, u32[]{:S(2)}, u32[]{:S(2)}) collective-permute-start(bf16[128,128]{1,0:T(8,128)(2,1)S(1)} %far.1._), channel_id=1, source_target_pairs={{0,8},{2,10},{4,12},{6,14},{8,0},{10,2},{12,4},{14,6},{1,9},{3,11}... | collective-permute-start | bytes 98312 | tf_op jit(solution)/shard_map/ppermute | solution.py:452
  28.7 0.0 collective-permute-done.7.p0_ref
  28.7 0.0 collective-permute-done.8.p1_ref
  28.7 0.6 %collective-permute-done.13.p3_ref = bf16[128,128]{1,0:T(8,128)(2,1)S(1)} collective-permute-done((bf16[128,128]{1,0:T(8,128)(2,1)S(1)}, bf16[128,128]{1,0:T(8,128)(2,1)S(1)}, u32[]{:S(2)}, u32[]{:S(2)}) %collective-permute-start.13) | collective-permute-done | bytes 32800 | tf_op jit(solution)/shard_map/ppermute | solution.py:452
  29.3 2.5 %collective-permute-done.12.p2_ref = bf16[128,128]{1,0:T(8,128)(2,1)S(1)} collective-permute-done((bf16[128,128]{1,0:T(8,128)(2,1)S(1)}, bf16[128,128]{1,0:T(8,128)(2,1)S(1)}, u32[]{:S(2)}, u32[]{:S(2)}) %collective-permute-start.12) | collective-permute-done | bytes 32800 | tf_op jit(solution)/shard_map/ppermute | solution.py:452
  31.8 0.7 %total.1 = f32[32,4,128]{2,1,0:T(4,128)} custom-call(f32[2,4,32,128]{3,2,1,0:T(8,128)S(1)} %get-tuple-element.39.mine_ref, bf16[128,128]{1,0:T(8,128)(2,1)S(1)} %collective-permute-done.7.p0_ref, bf16[128,128]{1,0:T(8,128)(2,1)S(1)} %collective-permute-done.8.p1_ref, bf16[128,128]{1,0:T(8,128)(2,1)S(1)} %collective-permute-done.12.p2_ref, ...), custom_call_target="tpu_custom_call" | custom-call | tf_op jit(solution)/shard_map/total/pallas_call | solution.py:442
  (6 shorter events, 0.1 us)
Async XLA Ops:
  0.0 7.1 %copy-start.1 = (f32[16]{0:T(128)S(1)}, f32[16]{0:T(128)}, u32[]{:S(2)}) copy-start(f32[16]{0:T(128)} %param.6) | copy-start | bytes 196
  1.4 5.7 %copy-start = (s32[1,8,128]{2,1,0:T(8,128)S(1)}, s32[1,8,128]{2,1,0:T(8,128)}, u32[]{:S(2)}) copy-start(s32[1,8,128]{2,1,0:T(8,128)} %ids_ref.1) | copy-start | bytes 12292
  1.4 5.7 %collective-permute-start = (bf16[8,3,128,128]{3,2,1,0:T(8,128)(2,1)S(1)}, bf16[8,3,128,128]{3,2,1,0:T(8,128)(2,1)S(1)}, u32[]{:S(2)}, u32[]{:S(2)}) collective-permute-start(bf16[8,3,128,128]{3,2,1,0:T(8,128)(2,1)S(1)} %get-tuple-element.26.tr.own_ref), channel_id=1, source_target_pairs={{0,1},{1,0},{2,3},{3,2},{4,5},{5,4},{6,7},{7,6},{8,9},{9,8},{10,11... | collective-permute-start | bytes 2359304 | tf_op jit(solution)/shard_map/ppermute | solution.py:358
  1.9 9.7 %collective-permute-start.1 = (bf16[784,128]{1,0:T(8,128)(2,1)S(1)}, bf16[784,128]{1,0:T(8,128)(2,1)S(1)}, u32[]{:S(2)}, u32[]{:S(2)}) collective-permute-start(bf16[784,128]{1,0:T(8,128)(2,1)S(1)} %get-tuple-element.27), channel_id=1, source_target_pairs={{0,2},{1,3},{2,0},{3,1},{4,6},{5,7},{6,4},{7,5},{8,10},{9,11},{10,... | collective-permute-start | bytes 602120 | tf_op jit(solution)/shard_map/ppermute | solution.py:359
  4.5 7.2 %collective-permute-start.2 = (bf16[784,128]{1,0:T(8,128)(2,1)S(1)}, bf16[784,128]{1,0:T(8,128)(2,1)S(1)}, u32[]{:S(2)}, u32[]{:S(2)}) collective-permute-start(bf16[784,128]{1,0:T(8,128)(2,1)S(1)} %get-tuple-element.28), channel_id=1, source_target_pairs={{0,12},{1,13},{2,6},{3,7},{4,0},{5,1},{6,10},{7,11},{8,4},{9,5},{1... | collective-permute-start | bytes 602120 | tf_op jit(solution)/shard_map/ppermute | solution.py:360
  7.2 7.3 %collective-permute-start.3 = (bf16[784,128]{1,0:T(8,128)(2,1)S(1)}, bf16[784,128]{1,0:T(8,128)(2,1)S(1)}, u32[]{:S(2)}, u32[]{:S(2)}) collective-permute-start(bf16[784,128]{1,0:T(8,128)(2,1)S(1)} %get-tuple-element.29), channel_id=1, source_target_pairs={{0,3},{1,2},{2,1},{3,0},{4,7},{5,6},{6,5},{7,4},{8,11},{9,10},{10,... | collective-permute-start | bytes 602120 | tf_op jit(solution)/shard_map/ppermute | solution.py:370
  7.3 9.3 %collective-permute-start.4 = (bf16[784,128]{1,0:T(8,128)(2,1)S(1)}, bf16[784,128]{1,0:T(8,128)(2,1)S(1)}, u32[]{:S(2)}, u32[]{:S(2)}) collective-permute-start(bf16[784,128]{1,0:T(8,128)(2,1)S(1)} %get-tuple-element.30), channel_id=1, source_target_pairs={{2,7},{3,6},{4,1},{5,0},{6,11},{7,10},{8,5},{9,4},{10,15},{11,14},... | collective-permute-start | bytes 602120 | tf_op jit(solution)/shard_map/ppermute | solution.py:371
  17.2 1.4 %collective-permute-start.6 = (bf16[512,128]{1,0:T(8,128)(2,1)S(1)}, bf16[512,128]{1,0:T(8,128)(2,1)S(1)}, u32[]{:S(2)}, u32[]{:S(2)}) collective-permute-start(bf16[512,128]{1,0:T(8,128)(2,1)S(1)} %get-tuple-element.41), channel_id=1, source_target_pairs={{0,1},{1,0},{2,3},{3,2},{4,5},{5,4},{6,7},{7,6},{8,9},{9,8},{10,11... | collective-permute-start | bytes 393224 | tf_op jit(solution)/shard_map/ppermute | solution.py:436
  18.0 3.2 %collective-permute-start.5 = (bf16[512,128]{1,0:T(8,128)(2,1)S(1)}, bf16[512,128]{1,0:T(8,128)(2,1)S(1)}, u32[]{:S(2)}, u32[]{:S(2)}) collective-permute-start(bf16[512,128]{1,0:T(8,128)(2,1)S(1)} %get-tuple-element.38), channel_id=1, source_target_pairs={{0,1},{1,0},{2,3},{3,2},{4,5},{5,4},{6,7},{7,6},{8,9},{9,8},{10,11... | collective-permute-start | bytes 393224 | tf_op jit(solution)/shard_map/ppermute | solution.py:438
  18.7 6.2 %collective-permute-start.9 = (bf16[128,128]{1,0:T(8,128)(2,1)S(1)}, bf16[128,128]{1,0:T(8,128)(2,1)S(1)}, u32[]{:S(2)}, u32[]{:S(2)}) collective-permute-start(bf16[128,128]{1,0:T(8,128)(2,1)S(1)} %get-tuple-element.45), channel_id=1, source_target_pairs={{0,6},{2,4},{4,2},{6,0},{8,14},{10,12},{12,10},{14,8},{1,7},{3,5},... | collective-permute-start | bytes 98312 | tf_op jit(solution)/shard_map/ppermute | solution.py:452
  20.2 4.7 %collective-permute-start.10 = (bf16[128,128]{1,0:T(8,128)(2,1)S(1)}, bf16[128,128]{1,0:T(8,128)(2,1)S(1)}, u32[]{:S(2)}, u32[]{:S(2)}) collective-permute-start(bf16[128,128]{1,0:T(8,128)(2,1)S(1)} %get-tuple-element.46), channel_id=1, source_target_pairs={{0,2},{2,0},{4,6},{6,4},{8,10},{10,8},{12,14},{14,12},{1,3},{3,1},... | collective-permute-start | bytes 98312 | tf_op jit(solution)/shard_map/ppermute | solution.py:452
  21.2 4.0 %collective-permute-start.11 = (bf16[128,128]{1,0:T(8,128)(2,1)S(1)}, bf16[128,128]{1,0:T(8,128)(2,1)S(1)}, u32[]{:S(2)}, u32[]{:S(2)}) collective-permute-start(bf16[128,128]{1,0:T(8,128)(2,1)S(1)} %get-tuple-element.42._), channel_id=1, source_target_pairs={{0,4},{2,6},{4,0},{6,2},{8,12},{10,14},{12,8},{14,10},{1,5},{3,7},... | collective-permute-start | bytes 98312 | tf_op jit(solution)/shard_map/ppermute | solution.py:452
  22.3 6.4 %collective-permute-start.7 = (bf16[128,128]{1,0:T(8,128)(2,1)S(1)}, bf16[128,128]{1,0:T(8,128)(2,1)S(1)}, u32[]{:S(2)}, u32[]{:S(2)}) collective-permute-start(bf16[128,128]{1,0:T(8,128)(2,1)S(1)} %get-tuple-element.43), channel_id=1, source_target_pairs={{0,6},{2,4},{4,2},{6,0},{8,14},{10,12},{12,10},{14,8},{1,7},{3,5},... | collective-permute-start | bytes 98312 | tf_op jit(solution)/shard_map/ppermute | solution.py:452
  23.9 4.8 %collective-permute-start.8 = (bf16[128,128]{1,0:T(8,128)(2,1)S(1)}, bf16[128,128]{1,0:T(8,128)(2,1)S(1)}, u32[]{:S(2)}, u32[]{:S(2)}) collective-permute-start(bf16[128,128]{1,0:T(8,128)(2,1)S(1)} %get-tuple-element.44), channel_id=1, source_target_pairs={{0,2},{2,0},{4,6},{6,4},{8,10},{10,8},{12,14},{14,12},{1,3},{3,1},... | collective-permute-start | bytes 98312 | tf_op jit(solution)/shard_map/ppermute | solution.py:452
  25.3 4.0 %collective-permute-start.13 = (bf16[128,128]{1,0:T(8,128)(2,1)S(1)}, bf16[128,128]{1,0:T(8,128)(2,1)S(1)}, u32[]{:S(2)}, u32[]{:S(2)}) collective-permute-start(bf16[128,128]{1,0:T(8,128)(2,1)S(1)} %last.1), channel_id=1, source_target_pairs={{0,4},{2,6},{4,0},{6,2},{8,12},{10,14},{12,8},{14,10},{1,5},{3,7},... | collective-permute-start | bytes 98312 | tf_op jit(solution)/shard_map/ppermute | solution.py:452
  26.6 5.2 %collective-permute-start.12 = (bf16[128,128]{1,0:T(8,128)(2,1)S(1)}, bf16[128,128]{1,0:T(8,128)(2,1)S(1)}, u32[]{:S(2)}, u32[]{:S(2)}) collective-permute-start(bf16[128,128]{1,0:T(8,128)(2,1)S(1)} %far.1._), channel_id=1, source_target_pairs={{0,8},{2,10},{4,12},{6,14},{8,0},{10,2},{12,4},{14,6},{1,9},{3,11}... | collective-permute-start | bytes 98312 | tf_op jit(solution)/shard_map/ppermute | solution.py:452

commit v24 on v19

--- a/solution.py
+++ b/solution.py
@@ -341,7 +341,7 @@
         name="weights",
     )(weight_ids, jnp.broadcast_to(weight_table[None], (8, NW)), own, other)
     xc = lax.ppermute(xc, both, cross([(s, x_to(s)) for s in range(n)]))
-    zc = lax.ppermute(zc, both, cross([(s, z_to(s)) for s in range(n) if 0 <= z_to(s) < n]))
+    zc = lax.ppermute(zc, both, cross([(s, z_to(s) % n) for s in range(n)]))
 
     depth = nx // 4 * comps * nz
     depth = quarter * comps * nz

time: 31.3 us -> 31.4 us (level)
  starting transfers between devices: 13.3 us -> 16.1 us
  waiting for transfers between devices: 10.4 us -> 7.63 us
    ppermute x1, waiting for transfers between devices: 2.81 us -> 1.16 us  [on_device(): xc = lax.ppermute(xc, both, cross([(s, x_to(s)) for s in range(n)]))]
    ppermute x1, starting transfers between devices: 1.29 us -> 2.94 us  [on_device(): zc = lax.ppermute(zc, both, cross([(s, z_to(s) % n) for s in range(n)]))]
    ppermute x1, starting transfers between devices: 2.01 us -> 3.2 us  [on_device(): got = lax.ppermute(send, 'space', [(s, s ^ NEAR) for s in range(n)])]
    ppermute x1, waiting for transfers between devices: 2.86 us -> 2.25 us  [on_device(): got = lax.ppermute(send, 'space', [(s, s ^ NEAR) for s in range(n)])]
    ppermute x1, waiting for transfers between devices: 1.27 us -> 0.66 us  [on_device(): zc = lax.ppermute(zc, both, cross([(s, z_to(s) % n) for s in range(n)]))]
where the time goes in v24:
time: 31.4 us; the launch traced here: 31.3 us
  starting transfers between devices  16.1 us (51%)
  waiting for transfers between devices  7.63 us (24%)
  Pallas kernels  6.78 us (22%)
  between operations  0.76 us (2%)
    ppermute x3, starting transfers between devices, on_device(): lax.ppermute(part, 'space', [(s, s ^ step) for s in range(n)])  3.62 us
    ppermute x3, waiting for transfers between devices, on_device(): lax.ppermute(part, 'space', [(s, s ^ step) for s in range(n)])  3.42 us
    ppermute x1, starting transfers between devices, on_device(): got = lax.ppermute(send, 'space', [(s, s ^ NEAR) for s in range(n)])  3.2 us
    ppermute x1, starting transfers between devices, on_device(): zc = lax.ppermute(zc, both, cross([(s, z_to(s) % n) for s in range(n)]))  2.94 us
    ppermute x1, starting transfers between devices, on_device(): second = lax.ppermute(second, both, same(seconds))  2.6 us
    ppermute x1, starting transfers between devices, on_device(): first = lax.ppermute(first, both, same(firsts))  2.53 us
    pallas_call x1, Pallas kernels, on_device(): pl.pallas_call(local_kernel, out_shape=[jax.ShapeDtypeStruct((JB * 2 * nk...  2.43 us
    ppermute x1, waiting for transfers between devices, on_device(): got = lax.ppermute(send, 'space', [(s, s ^ NEAR) for s in range(n)])  2.25 us
  transfers between devices with their start and end apart: 11, of which 7 were waited for; matrix products, arithmetic and copies ran while one was open for 0% of the time, Pallas kernels for 13%

profile of v24, /device:TPU:0, one launch (start us, length us, event | category | flops | bytes accessed | tf_op | source)
XLA Modules:
  0.0 31.3 jit_solution(492563995157597024)
XLA Ops:
  0.0 0.0 copy-start.1
  0.0 1.4 %prep.1 = (bf16[8,3,128,128]{3,2,1,0:T(8,128)(2,1)S(1)}, bf16[784,128]{1,0:T(8,128)(2,1)S(1)}, bf16[784,128]{1,0:T(8,128)(2,1)S(1)}) custom-call(bf16[128,3,1,8,128]{4,3,2,1,0:T(8,128)(2,1)} %modes_hbm.1), custom_call_target="tpu_custom_call" | custom-call | flops 1500000000 | bytes 2800000 | tf_op jit(solution)/shard_map/prep/pallas_call | solution.py:311
  1.4 0.0 copy-start
  1.4 0.5 %collective-permute-start = (bf16[8,3,128,128]{3,2,1,0:T(8,128)(2,1)S(1)}, bf16[8,3,128,128]{3,2,1,0:T(8,128)(2,1)S(1)}, u32[]{:S(2)}, u32[]{:S(2)}) collective-permute-start(bf16[8,3,128,128]{3,2,1,0:T(8,128)(2,1)S(1)} %get-tuple-element.26.tr.own_ref), channel_id=1, source_target_pairs={{0,1},{1,0},{2,3},{3,2},{4,5},{5,4},{6,7},{7,6},{8,9},{9,8},{10,11... | collective-permute-start | bytes 2359304 | tf_op jit(solution)/shard_map/ppermute | solution.py:331
  1.9 2.5 %collective-permute-start.1 = (bf16[784,128]{1,0:T(8,128)(2,1)S(1)}, bf16[784,128]{1,0:T(8,128)(2,1)S(1)}, u32[]{:S(2)}, u32[]{:S(2)}) collective-permute-start(bf16[784,128]{1,0:T(8,128)(2,1)S(1)} %get-tuple-element.27), channel_id=1, source_target_pairs={{0,2},{1,3},{2,0},{3,1},{4,6},{5,7},{6,4},{7,5},{8,10},{9,11},{10,... | collective-permute-start | bytes 602120 | tf_op jit(solution)/shard_map/ppermute | solution.py:332
  4.5 2.6 %collective-permute-start.2 = (bf16[784,128]{1,0:T(8,128)(2,1)S(1)}, bf16[784,128]{1,0:T(8,128)(2,1)S(1)}, u32[]{:S(2)}, u32[]{:S(2)}) collective-permute-start(bf16[784,128]{1,0:T(8,128)(2,1)S(1)} %get-tuple-element.28), channel_id=1, source_target_pairs={{0,12},{1,13},{2,6},{3,7},{4,0},{5,1},{6,10},{7,11},{8,4},{9,5},{1... | collective-permute-start | bytes 602120 | tf_op jit(solution)/shard_map/ppermute | solution.py:333
  7.1 0.0 collective-permute-done._.other_ref
  7.1 0.0 copy-done.1
  7.1 0.0 copy-done
  7.1 0.1 weights.1
  7.2 0.1 collective-permute-start.3
  7.3 2.9 %collective-permute-start.4 = (bf16[784,128]{1,0:T(8,128)(2,1)S(1)}, bf16[784,128]{1,0:T(8,128)(2,1)S(1)}, u32[]{:S(2)}, u32[]{:S(2)}) collective-permute-start(bf16[784,128]{1,0:T(8,128)(2,1)S(1)} %get-tuple-element.30), channel_id=1, source_target_pairs={{0,13},{1,12},{2,7},{3,6},{4,1},{5,0},{6,11},{7,10},{8,5},{9,4},{1... | collective-permute-start | bytes 602120 | tf_op jit(solution)/shard_map/ppermute | solution.py:344
  10.9 2.4 %local.1 = (f32[1024,256]{1,0:T(8,128)S(1)}, bf16[2,256,384]{2,1,0:T(8,128)(2,1)S(1)}) custom-call(bf16[8,3,128,128]{3,2,1,0:T(8,128)(2,1)S(1)} %get-tuple-element.26.tr.own_ref, bf16[8,3,128,128]{3,2,1,0:T(8,128)(2,1)S(1)} %collective-permute-done._.other_ref, f32[8,128]{1,0:T(8,128)S(1)} %get-tuple-element.31.weight_ref, s32[1]{0:T(128)S(6)} %copy.5.jb_ref.refs_5_), custom_call_target="tpu_custom_call" | custom-call | flops 900000000 | bytes 2400000 | tf_op jit(solution)/shard_map/local/pallas_call | solution.py:348
  13.3 0.0 collective-permute-done.1.first_ref.refs_0_
  13.3 0.0 collective-permute-done.2.second_ref.refs_1_
  13.3 1.2 %collective-permute-done.3.xc_ref.refs_2_ = bf16[784,128]{1,0:T(8,128)(2,1)S(1)} collective-permute-done((bf16[784,128]{1,0:T(8,128)(2,1)S(1)}, bf16[784,128]{1,0:T(8,128)(2,1)S(1)}, u32[]{:S(2)}, u32[]{:S(2)}) %collective-permute-start.3) | collective-permute-done | bytes 200736 | tf_op jit(solution)/shard_map/ppermute | solution.py:343
  14.5 0.8 %early.1 = (f32[1024,256]{1,0:T(8,128)S(1)}, bf16[256,768]{1,0:T(8,128)(2,1)S(1)}) custom-call(bf16[8,3,128,128]{3,2,1,0:T(8,128)(2,1)S(1)} %get-tuple-element.26.tr.own_ref, bf16[8,3,128,128]{3,2,1,0:T(8,128)(2,1)S(1)} %collective-permute-done._.other_ref, bf16[784,128]{1,0:T(8,128)(2,1)S(1)} %collective-permute-done.1.first_ref.refs_0_, ...), custom_call_target="tpu_custom_call" | custom-call | flops 600000000 | bytes 2400000 | tf_op jit(solution)/shard_map/early/pallas_call | solution.py:365
  15.3 0.7 %collective-permute-done.4.refs_3_ = bf16[784,128]{1,0:T(8,128)(2,1)S(1)} collective-permute-done((bf16[784,128]{1,0:T(8,128)(2,1)S(1)}, bf16[784,128]{1,0:T(8,128)(2,1)S(1)}, u32[]{:S(2)}, u32[]{:S(2)}) %collective-permute-start.4) | collective-permute-done | bytes 200736 | tf_op jit(solution)/shard_map/ppermute | solution.py:344
  15.9 0.7 %cross.2 = (f32[2,2,4,32,128]{4,3,2,1,0:T(8,128)S(1)}, bf16[512,128]{1,0:T(8,128)(2,1)S(1)}, bf16[256,1536]{1,0:T(8,128)(2,1)S(1)}) custom-call(bf16[8,3,128,128]{3,2,1,0:T(8,128)(2,1)S(1)} %get-tuple-element.26.tr.own_ref, bf16[8,3,128,128]{3,2,1,0:T(8,128)(2,1)S(1)} %collective-permute-done._.other_ref, ...), custom_call_target="tpu_custom_call" | custom-call | flops 900000000 | bytes 4000000 | tf_op jit(solution)/shard_map/cross/pallas_call | solution.py:390
  16.6 0.1 collective-permute-start.6
  16.7 0.6 %cross.3 = (f32[2,2,4,32,128]{4,3,2,1,0:T(8,128)S(1)}, bf16[512,128]{1,0:T(8,128)(2,1)S(1)}) custom-call(bf16[8,3,128,128]{3,2,1,0:T(8,128)(2,1)S(1)} %get-tuple-element.26.tr.own_ref, bf16[8,3,128,128]{3,2,1,0:T(8,128)(2,1)S(1)} %collective-permute-done._.other_ref, bf16[784,128]{1,0:T(8,128)(2,1)S(1)} %collective-permute-done.1.first_ref.refs_0_, ...), custom_call_target="tpu_custom_call" | custom-call | flops 900000000 | bytes 4000000 | tf_op jit(solution)/shard_map/cross/pallas_call | solution.py:390
  17.3 0.6 %collective-permute-start.5 = (bf16[512,128]{1,0:T(8,128)(2,1)S(1)}, bf16[512,128]{1,0:T(8,128)(2,1)S(1)}, u32[]{:S(2)}, u32[]{:S(2)}) collective-permute-start(bf16[512,128]{1,0:T(8,128)(2,1)S(1)} %get-tuple-element.38), channel_id=1, source_target_pairs={{0,1},{1,0},{2,3},{3,2},{4,5},{5,4},{6,7},{7,6},{8,9},{9,8},{10,11... | collective-permute-start | bytes 393224 | tf_op jit(solution)/shard_map/ppermute | solution.py:411
  17.9 0.1 collective-permute-done.6.got_ref
  18.1 1.7 %collective-permute-start.7 = (bf16[256,128]{1,0:T(8,128)(2,1)S(1)}, bf16[256,128]{1,0:T(8,128)(2,1)S(1)}, u32[]{:S(2)}, u32[]{:S(2)}) collective-permute-start(bf16[256,128]{1,0:T(8,128)(2,1)S(1)} %get-tuple-element.42), channel_id=1, source_target_pairs={{0,6},{2,4},{4,2},{6,0},{8,14},{10,12},{12,10},{14,8},{1,7},{3,5},... | collective-permute-start | bytes 196616 | tf_op jit(solution)/shard_map/ppermute | solution.py:429
  19.7 0.8 %collective-permute-start.8 = (bf16[256,128]{1,0:T(8,128)(2,1)S(1)}, bf16[256,128]{1,0:T(8,128)(2,1)S(1)}, u32[]{:S(2)}, u32[]{:S(2)}) collective-permute-start(bf16[256,128]{1,0:T(8,128)(2,1)S(1)} %get-tuple-element.43), channel_id=1, source_target_pairs={{0,2},{2,0},{4,6},{6,4},{8,10},{10,8},{12,14},{14,12},{1,3},{3,1},... | collective-permute-start | bytes 196616 | tf_op jit(solution)/shard_map/ppermute | solution.py:429
  20.5 0.0 collective-permute-done.5.got_ref
  20.6 1.1 %collective-permute-start.9 = (bf16[256,128]{1,0:T(8,128)(2,1)S(1)}, bf16[256,128]{1,0:T(8,128)(2,1)S(1)}, u32[]{:S(2)}, u32[]{:S(2)}) collective-permute-start(bf16[256,128]{1,0:T(8,128)(2,1)S(1)} %get-tuple-element.44), channel_id=1, source_target_pairs={{0,4},{2,6},{4,0},{6,2},{8,12},{10,14},{12,8},{14,10},{1,5},{3,7},... | collective-permute-start | bytes 196616 | tf_op jit(solution)/shard_map/ppermute | solution.py:429
  21.7 1.6 %collective-permute-done.7.refs_0_ = bf16[256,128]{1,0:T(8,128)(2,1)S(1)} collective-permute-done((bf16[256,128]{1,0:T(8,128)(2,1)S(1)}, bf16[256,128]{1,0:T(8,128)(2,1)S(1)}, u32[]{:S(2)}, u32[]{:S(2)}) %collective-permute-start.7) | collective-permute-done | bytes 65568 | tf_op jit(solution)/shard_map/ppermute | solution.py:429
  23.3 1.2 %collective-permute-done.8.refs_1_ = bf16[256,128]{1,0:T(8,128)(2,1)S(1)} collective-permute-done((bf16[256,128]{1,0:T(8,128)(2,1)S(1)}, bf16[256,128]{1,0:T(8,128)(2,1)S(1)}, u32[]{:S(2)}, u32[]{:S(2)}) %collective-permute-start.8) | collective-permute-done | bytes 65568 | tf_op jit(solution)/shard_map/ppermute | solution.py:429
  24.6 0.6 %collective-permute-done.9.refs_2_ = bf16[256,128]{1,0:T(8,128)(2,1)S(1)} collective-permute-done((bf16[256,128]{1,0:T(8,128)(2,1)S(1)}, bf16[256,128]{1,0:T(8,128)(2,1)S(1)}, u32[]{:S(2)}, u32[]{:S(2)}) %collective-permute-start.9) | collective-permute-done | bytes 65568 | tf_op jit(solution)/shard_map/ppermute | solution.py:429
  25.2 3.2 %collective-permute-start.10 = (bf16[128,128]{1,0:T(8,128)(2,1)S(1)}, bf16[128,128]{1,0:T(8,128)(2,1)S(1)}, u32[]{:S(2)}, u32[]{:S(2)}) collective-permute-start(bf16[128,128]{1,0:T(8,128)(2,1)S(1)} %get-tuple-element.46), channel_id=1, source_target_pairs={{0,8},{2,10},{4,12},{6,14},{8,0},{10,2},{12,4},{14,6},{1,9},{3,11}... | collective-permute-start | bytes 98312 | tf_op jit(solution)/shard_map/ppermute | solution.py:443
  28.4 2.2 %collective-permute-done.10.got_ref = bf16[128,128]{1,0:T(8,128)(2,1)S(1)} collective-permute-done((bf16[128,128]{1,0:T(8,128)(2,1)S(1)}, bf16[128,128]{1,0:T(8,128)(2,1)S(1)}, u32[]{:S(2)}, u32[]{:S(2)}) %collective-permute-start.10) | collective-permute-done | bytes 32800 | tf_op jit(solution)/shard_map/ppermute | solution.py:443
  30.6 0.7 %total.1 = f32[32,4,128]{2,1,0:T(4,128)} custom-call(f32[4,32,128]{2,1,0:T(8,128)S(1)} %get-tuple-element.45.keep_ref, bf16[128,128]{1,0:T(8,128)(2,1)S(1)} %collective-permute-done.10.got_ref), custom_call_target="tpu_custom_call" | custom-call | tf_op jit(solution)/shard_map/total/pallas_call | solution.py:444
  (4 shorter events, 0.1 us)
Async XLA Ops:
  0.0 7.1 %copy-start.1 = (f32[16]{0:T(128)S(1)}, f32[16]{0:T(128)}, u32[]{:S(2)}) copy-start(f32[16]{0:T(128)} %param.6) | copy-start | bytes 196
  1.4 5.7 %copy-start = (s32[1,8,128]{2,1,0:T(8,128)S(1)}, s32[1,8,128]{2,1,0:T(8,128)}, u32[]{:S(2)}) copy-start(s32[1,8,128]{2,1,0:T(8,128)} %ids_ref.1) | copy-start | bytes 12292
  1.4 5.7 %collective-permute-start = (bf16[8,3,128,128]{3,2,1,0:T(8,128)(2,1)S(1)}, bf16[8,3,128,128]{3,2,1,0:T(8,128)(2,1)S(1)}, u32[]{:S(2)}, u32[]{:S(2)}) collective-permute-start(bf16[8,3,128,128]{3,2,1,0:T(8,128)(2,1)S(1)} %get-tuple-element.26.tr.own_ref), channel_id=1, source_target_pairs={{0,1},{1,0},{2,3},{3,2},{4,5},{5,4},{6,7},{7,6},{8,9},{9,8},{10,11... | collective-permute-start | bytes 2359304 | tf_op jit(solution)/shard_map/ppermute | solution.py:331
  1.9 11.4 %collective-permute-start.1 = (bf16[784,128]{1,0:T(8,128)(2,1)S(1)}, bf16[784,128]{1,0:T(8,128)(2,1)S(1)}, u32[]{:S(2)}, u32[]{:S(2)}) collective-permute-start(bf16[784,128]{1,0:T(8,128)(2,1)S(1)} %get-tuple-element.27), channel_id=1, source_target_pairs={{0,2},{1,3},{2,0},{3,1},{4,6},{5,7},{6,4},{7,5},{8,10},{9,11},{10,... | collective-permute-start | bytes 602120 | tf_op jit(solution)/shard_map/ppermute | solution.py:332
  4.5 8.9 %collective-permute-start.2 = (bf16[784,128]{1,0:T(8,128)(2,1)S(1)}, bf16[784,128]{1,0:T(8,128)(2,1)S(1)}, u32[]{:S(2)}, u32[]{:S(2)}) collective-permute-start(bf16[784,128]{1,0:T(8,128)(2,1)S(1)} %get-tuple-element.28), channel_id=1, source_target_pairs={{0,12},{1,13},{2,6},{3,7},{4,0},{5,1},{6,10},{7,11},{8,4},{9,5},{1... | collective-permute-start | bytes 602120 | tf_op jit(solution)/shard_map/ppermute | solution.py:333
  7.2 7.3 %collective-permute-start.3 = (bf16[784,128]{1,0:T(8,128)(2,1)S(1)}, bf16[784,128]{1,0:T(8,128)(2,1)S(1)}, u32[]{:S(2)}, u32[]{:S(2)}) collective-permute-start(bf16[784,128]{1,0:T(8,128)(2,1)S(1)} %get-tuple-element.29), channel_id=1, source_target_pairs={{0,3},{1,2},{2,1},{3,0},{4,7},{5,6},{6,5},{7,4},{8,11},{9,10},{10,... | collective-permute-start | bytes 602120 | tf_op jit(solution)/shard_map/ppermute | solution.py:343
  7.3 8.6 %collective-permute-start.4 = (bf16[784,128]{1,0:T(8,128)(2,1)S(1)}, bf16[784,128]{1,0:T(8,128)(2,1)S(1)}, u32[]{:S(2)}, u32[]{:S(2)}) collective-permute-start(bf16[784,128]{1,0:T(8,128)(2,1)S(1)} %get-tuple-element.30), channel_id=1, source_target_pairs={{0,13},{1,12},{2,7},{3,6},{4,1},{5,0},{6,11},{7,10},{8,5},{9,4},{1... | collective-permute-start | bytes 602120 | tf_op jit(solution)/shard_map/ppermute | solution.py:344
  16.6 1.4 %collective-permute-start.6 = (bf16[512,128]{1,0:T(8,128)(2,1)S(1)}, bf16[512,128]{1,0:T(8,128)(2,1)S(1)}, u32[]{:S(2)}, u32[]{:S(2)}) collective-permute-start(bf16[512,128]{1,0:T(8,128)(2,1)S(1)} %get-tuple-element.41), channel_id=1, source_target_pairs={{0,1},{1,0},{2,3},{3,2},{4,5},{5,4},{6,7},{7,6},{8,9},{9,8},{10,11... | collective-permute-start | bytes 393224 | tf_op jit(solution)/shard_map/ppermute | solution.py:409
  17.3 3.2 %collective-permute-start.5 = (bf16[512,128]{1,0:T(8,128)(2,1)S(1)}, bf16[512,128]{1,0:T(8,128)(2,1)S(1)}, u32[]{:S(2)}, u32[]{:S(2)}) collective-permute-start(bf16[512,128]{1,0:T(8,128)(2,1)S(1)} %get-tuple-element.38), channel_id=1, source_target_pairs={{0,1},{1,0},{2,3},{3,2},{4,5},{5,4},{6,7},{7,6},{8,9},{9,8},{10,11... | collective-permute-start | bytes 393224 | tf_op jit(solution)/shard_map/ppermute | solution.py:411
  18.1 5.3 %collective-permute-start.7 = (bf16[256,128]{1,0:T(8,128)(2,1)S(1)}, bf16[256,128]{1,0:T(8,128)(2,1)S(1)}, u32[]{:S(2)}, u32[]{:S(2)}) collective-permute-start(bf16[256,128]{1,0:T(8,128)(2,1)S(1)} %get-tuple-element.42), channel_id=1, source_target_pairs={{0,6},{2,4},{4,2},{6,0},{8,14},{10,12},{12,10},{14,8},{1,7},{3,5},... | collective-permute-start | bytes 196616 | tf_op jit(solution)/shard_map/ppermute | solution.py:429
  19.7 4.8 %collective-permute-start.8 = (bf16[256,128]{1,0:T(8,128)(2,1)S(1)}, bf16[256,128]{1,0:T(8,128)(2,1)S(1)}, u32[]{:S(2)}, u32[]{:S(2)}) collective-permute-start(bf16[256,128]{1,0:T(8,128)(2,1)S(1)} %get-tuple-element.43), channel_id=1, source_target_pairs={{0,2},{2,0},{4,6},{6,4},{8,10},{10,8},{12,14},{14,12},{1,3},{3,1},... | collective-permute-start | bytes 196616 | tf_op jit(solution)/shard_map/ppermute | solution.py:429
  20.6 4.6 %collective-permute-start.9 = (bf16[256,128]{1,0:T(8,128)(2,1)S(1)}, bf16[256,128]{1,0:T(8,128)(2,1)S(1)}, u32[]{:S(2)}, u32[]{:S(2)}) collective-permute-start(bf16[256,128]{1,0:T(8,128)(2,1)S(1)} %get-tuple-element.44), channel_id=1, source_target_pairs={{0,4},{2,6},{4,0},{6,2},{8,12},{10,14},{12,8},{14,10},{1,5},{3,7},... | collective-permute-start | bytes 196616 | tf_op jit(solution)/shard_map/ppermute | solution.py:429
  25.2 5.4 %collective-permute-start.10 = (bf16[128,128]{1,0:T(8,128)(2,1)S(1)}, bf16[128,128]{1,0:T(8,128)(2,1)S(1)}, u32[]{:S(2)}, u32[]{:S(2)}) collective-permute-start(bf16[128,128]{1,0:T(8,128)(2,1)S(1)} %get-tuple-element.46), channel_id=1, source_target_pairs={{0,8},{2,10},{4,12},{6,14},{8,0},{10,2},{12,4},{14,6},{1,9},{3,11}... | collective-permute-start | bytes 98312 | tf_op jit(solution)/shard_map/ppermute | solution.py:443

commit v25 on v19

--- a/solution.py
+++ b/solution.py
@@ -58,10 +58,10 @@
         (second_ref, jnp.where(x_now, to_z, to_x)),
     ):
         copy_rows(ref, tr, at)
-        ref[pl.ds(body, PADROWS), :] = jnp.zeros((PADROWS, nz), jnp.bfloat16)
-
-
-def weights_kernel(ids_ref, table_ref, tr, _, weight_ref, xc_ref, zc_ref):
+        ref[pl.ds(body, 2 * PADROWS), :] = jnp.zeros((2 * PADROWS, nz), jnp.bfloat16)
+
+
+def weights_kernel(ids_ref, table_ref, tr, _, weight_ref, zc_ref, xc_ref):
     m = lax.axis_index("modes")
     q = lax.rem(lax.axis_index("space"), 2)
     nx, comps, nk, nz = tr.shape
@@ -71,6 +71,8 @@
     for entry in range(NW):
         weight = jnp.where(ids_ref[0] == entry, table[0:1, entry : entry + 1], weight)
     weight_ref[...] = weight
+    pad = quarter * comps * nk + 8 * quarter
+    zc_ref[pl.ds(pad, PADROWS), :] = jnp.zeros((PADROWS, nz), jnp.bfloat16)
     for ref, at in ((xc_ref, 2 * (1 - m) + 1 - q), (zc_ref, 2 * (1 - m) + q)):
         copy_rows(ref, tr, at)
         rest = jnp.concatenate(
@@ -311,7 +313,7 @@
     own, first, second = pl.pallas_call(
         functools.partial(prep_kernel, n),
         out_shape=[jax.ShapeDtypeStruct((nx, comps, nk, nz), bf16)]
-        + [jax.ShapeDtypeStruct((body + PADROWS, nz), bf16)] * 2,
+        + [jax.ShapeDtypeStruct((body + 2 * PADROWS, nz), bf16)] * 2,
         in_specs=[pl.BlockSpec(memory_space=pltpu.HBM)],
         out_specs=[vmem] * 3,
         scratch_shapes=[pltpu.VMEM(modes.shape, bf16), pltpu.SemaphoreType.DMA((LOADS,))],
@@ -331,10 +333,13 @@
     other = lax.ppermute(own, "modes", [(0, 1), (1, 0)])
     first = lax.ppermute(first, both, same(firsts))
     second = lax.ppermute(second, both, same(seconds))
-    weight, xc, zc = pl.pallas_call(
+    weight, zc, xc = pl.pallas_call(
         weights_kernel,
         out_shape=[jax.ShapeDtypeStruct((nx, nz), f32)]
-        + [jax.ShapeDtypeStruct((body + 8 * quarter, nz), bf16)] * 2,
+        + [
+            jax.ShapeDtypeStruct((body + 8 * quarter + PADROWS, nz), bf16),
+            jax.ShapeDtypeStruct((body + 8 * quarter, nz), bf16),
+        ],
         in_specs=[vmem] * 3 + [pl.BlockSpec(memory_space=pl.ANY)],
         out_specs=[vmem] * 3,
         compiler_params=params,
@@ -372,7 +377,7 @@
         out_specs=[vmem] * 2,
         scratch_shapes=[pltpu.VMEM((quarter, JB * 2 * nk, comps * nz), bf16)],
         compiler_params=params,
-        cost_estimate=pl.CostEstimate(flops=600_000_000, bytes_accessed=2_400_000, transcendentals=0),
+        cost_estimate=pl.CostEstimate(flops=1_000_000, bytes_accessed=10_000, transcendentals=0),
         name="early",
     )(own, other, first, second, xc, w0, j_block, acc)
 

time: 31.3 us -> 32 us (1.022)
  starting transfers between devices: 13.3 us -> 15.3 us
  waiting for transfers between devices: 10.4 us -> 8.97 us
    ppermute x1, starting transfers between devices: 0.07 us -> 2.58 us  [on_device(): xc = lax.ppermute(xc, both, cross([(s, x_to(s)) for s in range(n)]))]
    ppermute x1, waiting for transfers between devices: 1.27 us -> 0.01 us  [on_device(): lax.ppermute(zc, both, cross([(s, z_to(s)) for s in range(n) if 0 <= z_to...]
    ppermute x1, starting transfers between devices: 2.01 us -> 1.55 us  [on_device(): got = lax.ppermute(send, 'space', [(s, s ^ NEAR) for s in range(n)])]
    ppermute x1, waiting for transfers between devices: 2.86 us -> 3.33 us  [on_device(): got = lax.ppermute(send, 'space', [(s, s ^ NEAR) for s in range(n)])]
    ppermute x1, waiting for transfers between devices: 2.81 us -> 2.39 us  [on_device(): xc = lax.ppermute(xc, both, cross([(s, x_to(s)) for s in range(n)]))]
  transfers between devices with their start and end apart: 11 -> 11, of which waited for: 7 -> 6; matrix products, arithmetic and copies ran while one was open for 0% -> 0% of each run, Pallas kernels for 13% -> 13%
where the time goes in v25:
time: 32 us; the launch traced here: 31.9 us
  starting transfers between devices  15.3 us (48%)
  waiting for transfers between devices  8.97 us (28%)
  Pallas kernels  6.78 us (21%)
  between operations  0.76 us (2%)
    ppermute x3, starting transfers between devices, on_device(): lax.ppermute(part, 'space', [(s, s ^ step) for s in range(n)])  3.62 us
    ppermute x1, waiting for transfers between devices, on_device(): got = lax.ppermute(send, 'space', [(s, s ^ NEAR) for s in range(n)])  3.33 us
    ppermute x3, waiting for transfers between devices, on_device(): lax.ppermute(part, 'space', [(s, s ^ step) for s in range(n)])  3.12 us
    ppermute x1, starting transfers between devices, on_device(): second = lax.ppermute(second, both, same(seconds))  2.6 us
    ppermute x1, starting transfers between devices, on_device(): xc = lax.ppermute(xc, both, cross([(s, x_to(s)) for s in range(n)]))  2.58 us
    ppermute x1, starting transfers between devices, on_device(): first = lax.ppermute(first, both, same(firsts))  2.53 us
    pallas_call x1, Pallas kernels, on_device(): pl.pallas_call(local_kernel, out_shape=[jax.ShapeDtypeStruct((JB * 2 * nk...  2.42 us
    ppermute x1, waiting for transfers between devices, on_device(): xc = lax.ppermute(xc, both, cross([(s, x_to(s)) for s in range(n)]))  2.39 us
  transfers between devices with their start and end apart: 11, of which 6 were waited for; matrix products, arithmetic and copies ran while one was open for 0% of the time, Pallas kernels for 13%

profile of v25, /device:TPU:0, one launch (start us, length us, event | category | flops | bytes accessed | tf_op | source)
XLA Modules:
  0.0 31.9 jit_solution(5213368374349145673)
XLA Ops:
  0.0 0.0 copy-start.1
  0.0 1.4 %prep.1 = (bf16[8,3,128,128]{3,2,1,0:T(8,128)(2,1)S(1)}, bf16[800,128]{1,0:T(8,128)(2,1)S(1)}, bf16[800,128]{1,0:T(8,128)(2,1)S(1)}) custom-call(bf16[128,3,1,8,128]{4,3,2,1,0:T(8,128)(2,1)} %modes_hbm.1), custom_call_target="tpu_custom_call" | custom-call | flops 1500000000 | bytes 2800000 | tf_op jit(solution)/shard_map/prep/pallas_call | solution.py:313
  1.4 0.0 copy-start
  1.4 0.5 %collective-permute-start = (bf16[8,3,128,128]{3,2,1,0:T(8,128)(2,1)S(1)}, bf16[8,3,128,128]{3,2,1,0:T(8,128)(2,1)S(1)}, u32[]{:S(2)}, u32[]{:S(2)}) collective-permute-start(bf16[8,3,128,128]{3,2,1,0:T(8,128)(2,1)S(1)} %get-tuple-element.26.tr.own_ref), channel_id=1, source_target_pairs={{0,1},{1,0},{2,3},{3,2},{4,5},{5,4},{6,7},{7,6},{8,9},{9,8},{10,11... | collective-permute-start | bytes 2359304 | tf_op jit(solution)/shard_map/ppermute | solution.py:333
  1.9 2.5 %collective-permute-start.1 = (bf16[800,128]{1,0:T(8,128)(2,1)S(1)}, bf16[800,128]{1,0:T(8,128)(2,1)S(1)}, u32[]{:S(2)}, u32[]{:S(2)}) collective-permute-start(bf16[800,128]{1,0:T(8,128)(2,1)S(1)} %get-tuple-element.27), channel_id=1, source_target_pairs={{0,2},{1,3},{2,0},{3,1},{4,6},{5,7},{6,4},{7,5},{8,10},{9,11},{10,... | collective-permute-start | bytes 614408 | tf_op jit(solution)/shard_map/ppermute | solution.py:334
  4.5 2.6 %collective-permute-start.2 = (bf16[800,128]{1,0:T(8,128)(2,1)S(1)}, bf16[800,128]{1,0:T(8,128)(2,1)S(1)}, u32[]{:S(2)}, u32[]{:S(2)}) collective-permute-start(bf16[800,128]{1,0:T(8,128)(2,1)S(1)} %get-tuple-element.28), channel_id=1, source_target_pairs={{0,12},{1,13},{2,6},{3,7},{4,0},{5,1},{6,10},{7,11},{8,4},{9,5},{1... | collective-permute-start | bytes 614408 | tf_op jit(solution)/shard_map/ppermute | solution.py:335
  7.1 0.0 collective-permute-done._.other_ref
  7.1 0.0 copy-done.1
  7.1 0.0 copy-done
  7.1 0.1 weights.1
  7.2 1.3 %collective-permute-start.4 = (bf16[800,128]{1,0:T(8,128)(2,1)S(1)}, bf16[800,128]{1,0:T(8,128)(2,1)S(1)}, u32[]{:S(2)}, u32[]{:S(2)}) collective-permute-start(bf16[800,128]{1,0:T(8,128)(2,1)S(1)} %get-tuple-element.30), channel_id=1, source_target_pairs={{2,7},{3,6},{4,1},{5,0},{6,11},{7,10},{8,5},{9,4},{10,15},{11,14},... | collective-permute-start | bytes 614408 | tf_op jit(solution)/shard_map/ppermute | solution.py:349
  8.5 2.6 %collective-permute-start.3 = (bf16[784,128]{1,0:T(8,128)(2,1)S(1)}, bf16[784,128]{1,0:T(8,128)(2,1)S(1)}, u32[]{:S(2)}, u32[]{:S(2)}) collective-permute-start(bf16[784,128]{1,0:T(8,128)(2,1)S(1)} %get-tuple-element.29), channel_id=1, source_target_pairs={{0,3},{1,2},{2,1},{3,0},{4,7},{5,6},{6,5},{7,4},{8,11},{9,10},{10,... | collective-permute-start | bytes 602120 | tf_op jit(solution)/shard_map/ppermute | solution.py:348
  11.7 2.4 %local.1 = (f32[1024,256]{1,0:T(8,128)S(1)}, bf16[2,256,384]{2,1,0:T(8,128)(2,1)S(1)}) custom-call(bf16[8,3,128,128]{3,2,1,0:T(8,128)(2,1)S(1)} %get-tuple-element.26.tr.own_ref, bf16[8,3,128,128]{3,2,1,0:T(8,128)(2,1)S(1)} %collective-permute-done._.other_ref, f32[8,128]{1,0:T(8,128)S(1)} %get-tuple-element.31.weight_ref, s32[1]{0:T(128)S(6)} %copy.5.jb_ref.refs_5_), custom_call_target="tpu_custom_call" | custom-call | flops 900000000 | bytes 2400000 | tf_op jit(solution)/shard_map/local/pallas_call | solution.py:353
  14.2 0.0 collective-permute-done.1.first_ref.refs_0_
  14.2 0.0 collective-permute-done.2.second_ref.refs_1_
  14.2 2.4 %collective-permute-done.3.xc_ref.refs_2_ = bf16[784,128]{1,0:T(8,128)(2,1)S(1)} collective-permute-done((bf16[784,128]{1,0:T(8,128)(2,1)S(1)}, bf16[784,128]{1,0:T(8,128)(2,1)S(1)}, u32[]{:S(2)}, u32[]{:S(2)}) %collective-permute-start.3) | collective-permute-done | bytes 200736 | tf_op jit(solution)/shard_map/ppermute | solution.py:348
  16.6 0.8 %early.1 = (f32[1024,256]{1,0:T(8,128)S(1)}, bf16[256,768]{1,0:T(8,128)(2,1)S(1)}) custom-call(bf16[8,3,128,128]{3,2,1,0:T(8,128)(2,1)S(1)} %get-tuple-element.26.tr.own_ref, bf16[8,3,128,128]{3,2,1,0:T(8,128)(2,1)S(1)} %collective-permute-done._.other_ref, bf16[800,128]{1,0:T(8,128)(2,1)S(1)} %collective-permute-done.1.first_ref.refs_0_, ...), custom_call_target="tpu_custom_call" | custom-call | flops 1000000 | bytes 10000 | tf_op jit(solution)/shard_map/early/pallas_call | solution.py:370
  17.3 0.0 collective-permute-done.4.refs_3_
  17.4 0.7 %cross.2 = (f32[2,2,4,32,128]{4,3,2,1,0:T(8,128)S(1)}, bf16[512,128]{1,0:T(8,128)(2,1)S(1)}, bf16[256,1536]{1,0:T(8,128)(2,1)S(1)}) custom-call(bf16[8,3,128,128]{3,2,1,0:T(8,128)(2,1)S(1)} %get-tuple-element.26.tr.own_ref, bf16[8,3,128,128]{3,2,1,0:T(8,128)(2,1)S(1)} %collective-permute-done._.other_ref, ...), custom_call_target="tpu_custom_call" | custom-call | flops 900000000 | bytes 4000000 | tf_op jit(solution)/shard_map/cross/pallas_call | solution.py:395
  18.1 0.2 collective-permute-start.6
  18.2 0.6 %cross.3 = (f32[2,2,4,32,128]{4,3,2,1,0:T(8,128)S(1)}, bf16[512,128]{1,0:T(8,128)(2,1)S(1)}) custom-call(bf16[8,3,128,128]{3,2,1,0:T(8,128)(2,1)S(1)} %get-tuple-element.26.tr.own_ref, bf16[8,3,128,128]{3,2,1,0:T(8,128)(2,1)S(1)} %collective-permute-done._.other_ref, bf16[800,128]{1,0:T(8,128)(2,1)S(1)} %collective-permute-done.1.first_ref.refs_0_, ...), custom_call_target="tpu_custom_call" | custom-call | flops 900000000 | bytes 4000000 | tf_op jit(solution)/shard_map/cross/pallas_call | solution.py:395
  18.9 0.5 %collective-permute-start.5 = (bf16[512,128]{1,0:T(8,128)(2,1)S(1)}, bf16[512,128]{1,0:T(8,128)(2,1)S(1)}, u32[]{:S(2)}, u32[]{:S(2)}) collective-permute-start(bf16[512,128]{1,0:T(8,128)(2,1)S(1)} %get-tuple-element.38), channel_id=1, source_target_pairs={{0,1},{1,0},{2,3},{3,2},{4,5},{5,4},{6,7},{7,6},{8,9},{9,8},{10,11... | collective-permute-start | bytes 393224 | tf_op jit(solution)/shard_map/ppermute | solution.py:416
  19.3 0.1 collective-permute-done.6.got_ref
  19.5 1.5 %collective-permute-start.7 = (bf16[256,128]{1,0:T(8,128)(2,1)S(1)}, bf16[256,128]{1,0:T(8,128)(2,1)S(1)}, u32[]{:S(2)}, u32[]{:S(2)}) collective-permute-start(bf16[256,128]{1,0:T(8,128)(2,1)S(1)} %get-tuple-element.42), channel_id=1, source_target_pairs={{0,6},{2,4},{4,2},{6,0},{8,14},{10,12},{12,10},{14,8},{1,7},{3,5},... | collective-permute-start | bytes 196616 | tf_op jit(solution)/shard_map/ppermute | solution.py:434
  21.0 0.9 %collective-permute-start.8 = (bf16[256,128]{1,0:T(8,128)(2,1)S(1)}, bf16[256,128]{1,0:T(8,128)(2,1)S(1)}, u32[]{:S(2)}, u32[]{:S(2)}) collective-permute-start(bf16[256,128]{1,0:T(8,128)(2,1)S(1)} %get-tuple-element.43), channel_id=1, source_target_pairs={{0,2},{2,0},{4,6},{6,4},{8,10},{10,8},{12,14},{14,12},{1,3},{3,1},... | collective-permute-start | bytes 196616 | tf_op jit(solution)/shard_map/ppermute | solution.py:434
  21.9 0.0 collective-permute-done.5.got_ref
  21.9 1.2 %collective-permute-start.9 = (bf16[256,128]{1,0:T(8,128)(2,1)S(1)}, bf16[256,128]{1,0:T(8,128)(2,1)S(1)}, u32[]{:S(2)}, u32[]{:S(2)}) collective-permute-start(bf16[256,128]{1,0:T(8,128)(2,1)S(1)} %get-tuple-element.44), channel_id=1, source_target_pairs={{0,4},{2,6},{4,0},{6,2},{8,12},{10,14},{12,8},{14,10},{1,5},{3,7},... | collective-permute-start | bytes 196616 | tf_op jit(solution)/shard_map/ppermute | solution.py:434
  23.2 1.6 %collective-permute-done.7.refs_0_ = bf16[256,128]{1,0:T(8,128)(2,1)S(1)} collective-permute-done((bf16[256,128]{1,0:T(8,128)(2,1)S(1)}, bf16[256,128]{1,0:T(8,128)(2,1)S(1)}, u32[]{:S(2)}, u32[]{:S(2)}) %collective-permute-start.7) | collective-permute-done | bytes 65568 | tf_op jit(solution)/shard_map/ppermute | solution.py:434
  24.8 1.2 %collective-permute-done.8.refs_1_ = bf16[256,128]{1,0:T(8,128)(2,1)S(1)} collective-permute-done((bf16[256,128]{1,0:T(8,128)(2,1)S(1)}, bf16[256,128]{1,0:T(8,128)(2,1)S(1)}, u32[]{:S(2)}, u32[]{:S(2)}) %collective-permute-start.8) | collective-permute-done | bytes 65568 | tf_op jit(solution)/shard_map/ppermute | solution.py:434
  26.0 0.3 collective-permute-done.9.refs_2_
  26.3 1.6 %collective-permute-start.10 = (bf16[128,128]{1,0:T(8,128)(2,1)S(1)}, bf16[128,128]{1,0:T(8,128)(2,1)S(1)}, u32[]{:S(2)}, u32[]{:S(2)}) collective-permute-start(bf16[128,128]{1,0:T(8,128)(2,1)S(1)} %get-tuple-element.46), channel_id=1, source_target_pairs={{0,8},{2,10},{4,12},{6,14},{8,0},{10,2},{12,4},{14,6},{1,9},{3,11}... | collective-permute-start | bytes 98312 | tf_op jit(solution)/shard_map/ppermute | solution.py:448
  27.9 3.3 %collective-permute-done.10.got_ref = bf16[128,128]{1,0:T(8,128)(2,1)S(1)} collective-permute-done((bf16[128,128]{1,0:T(8,128)(2,1)S(1)}, bf16[128,128]{1,0:T(8,128)(2,1)S(1)}, u32[]{:S(2)}, u32[]{:S(2)}) %collective-permute-start.10) | collective-permute-done | bytes 32800 | tf_op jit(solution)/shard_map/ppermute | solution.py:448
  31.2 0.7 %total.1 = f32[32,4,128]{2,1,0:T(4,128)} custom-call(f32[4,32,128]{2,1,0:T(8,128)S(1)} %get-tuple-element.45.keep_ref, bf16[128,128]{1,0:T(8,128)(2,1)S(1)} %collective-permute-done.10.got_ref), custom_call_target="tpu_custom_call" | custom-call | tf_op jit(solution)/shard_map/total/pallas_call | solution.py:449
  (4 shorter events, 0.1 us)
Async XLA Ops:
  0.0 7.1 %copy-start.1 = (f32[16]{0:T(128)S(1)}, f32[16]{0:T(128)}, u32[]{:S(2)}) copy-start(f32[16]{0:T(128)} %param.6) | copy-start | bytes 196
  1.4 5.7 %copy-start = (s32[1,8,128]{2,1,0:T(8,128)S(1)}, s32[1,8,128]{2,1,0:T(8,128)}, u32[]{:S(2)}) copy-start(s32[1,8,128]{2,1,0:T(8,128)} %ids_ref.1) | copy-start | bytes 12292
  1.4 5.7 %collective-permute-start = (bf16[8,3,128,128]{3,2,1,0:T(8,128)(2,1)S(1)}, bf16[8,3,128,128]{3,2,1,0:T(8,128)(2,1)S(1)}, u32[]{:S(2)}, u32[]{:S(2)}) collective-permute-start(bf16[8,3,128,128]{3,2,1,0:T(8,128)(2,1)S(1)} %get-tuple-element.26.tr.own_ref), channel_id=1, source_target_pairs={{0,1},{1,0},{2,3},{3,2},{4,5},{5,4},{6,7},{7,6},{8,9},{9,8},{10,11... | collective-permute-start | bytes 2359304 | tf_op jit(solution)/shard_map/ppermute | solution.py:333
  1.9 12.2 %collective-permute-start.1 = (bf16[800,128]{1,0:T(8,128)(2,1)S(1)}, bf16[800,128]{1,0:T(8,128)(2,1)S(1)}, u32[]{:S(2)}, u32[]{:S(2)}) collective-permute-start(bf16[800,128]{1,0:T(8,128)(2,1)S(1)} %get-tuple-element.27), channel_id=1, source_target_pairs={{0,2},{1,3},{2,0},{3,1},{4,6},{5,7},{6,4},{7,5},{8,10},{9,11},{10,... | collective-permute-start | bytes 614408 | tf_op jit(solution)/shard_map/ppermute | solution.py:334
  4.5 9.7 %collective-permute-start.2 = (bf16[800,128]{1,0:T(8,128)(2,1)S(1)}, bf16[800,128]{1,0:T(8,128)(2,1)S(1)}, u32[]{:S(2)}, u32[]{:S(2)}) collective-permute-start(bf16[800,128]{1,0:T(8,128)(2,1)S(1)} %get-tuple-element.28), channel_id=1, source_target_pairs={{0,12},{1,13},{2,6},{3,7},{4,0},{5,1},{6,10},{7,11},{8,4},{9,5},{1... | collective-permute-start | bytes 614408 | tf_op jit(solution)/shard_map/ppermute | solution.py:335
  7.2 10.1 %collective-permute-start.4 = (bf16[800,128]{1,0:T(8,128)(2,1)S(1)}, bf16[800,128]{1,0:T(8,128)(2,1)S(1)}, u32[]{:S(2)}, u32[]{:S(2)}) collective-permute-start(bf16[800,128]{1,0:T(8,128)(2,1)S(1)} %get-tuple-element.30), channel_id=1, source_target_pairs={{2,7},{3,6},{4,1},{5,0},{6,11},{7,10},{8,5},{9,4},{10,15},{11,14},... | collective-permute-start | bytes 614408 | tf_op jit(solution)/shard_map/ppermute | solution.py:349
  8.5 8.1 %collective-permute-start.3 = (bf16[784,128]{1,0:T(8,128)(2,1)S(1)}, bf16[784,128]{1,0:T(8,128)(2,1)S(1)}, u32[]{:S(2)}, u32[]{:S(2)}) collective-permute-start(bf16[784,128]{1,0:T(8,128)(2,1)S(1)} %get-tuple-element.29), channel_id=1, source_target_pairs={{0,3},{1,2},{2,1},{3,0},{4,7},{5,6},{6,5},{7,4},{8,11},{9,10},{10,... | collective-permute-start | bytes 602120 | tf_op jit(solution)/shard_map/ppermute | solution.py:348
  18.1 1.4 %collective-permute-start.6 = (bf16[512,128]{1,0:T(8,128)(2,1)S(1)}, bf16[512,128]{1,0:T(8,128)(2,1)S(1)}, u32[]{:S(2)}, u32[]{:S(2)}) collective-permute-start(bf16[512,128]{1,0:T(8,128)(2,1)S(1)} %get-tuple-element.41), channel_id=1, source_target_pairs={{0,1},{1,0},{2,3},{3,2},{4,5},{5,4},{6,7},{7,6},{8,9},{9,8},{10,11... | collective-permute-start | bytes 393224 | tf_op jit(solution)/shard_map/ppermute | solution.py:414
  18.9 3.0 %collective-permute-start.5 = (bf16[512,128]{1,0:T(8,128)(2,1)S(1)}, bf16[512,128]{1,0:T(8,128)(2,1)S(1)}, u32[]{:S(2)}, u32[]{:S(2)}) collective-permute-start(bf16[512,128]{1,0:T(8,128)(2,1)S(1)} %get-tuple-element.38), channel_id=1, source_target_pairs={{0,1},{1,0},{2,3},{3,2},{4,5},{5,4},{6,7},{7,6},{8,9},{9,8},{10,11... | collective-permute-start | bytes 393224 | tf_op jit(solution)/shard_map/ppermute | solution.py:416
  19.5 5.3 %collective-permute-start.7 = (bf16[256,128]{1,0:T(8,128)(2,1)S(1)}, bf16[256,128]{1,0:T(8,128)(2,1)S(1)}, u32[]{:S(2)}, u32[]{:S(2)}) collective-permute-start(bf16[256,128]{1,0:T(8,128)(2,1)S(1)} %get-tuple-element.42), channel_id=1, source_target_pairs={{0,6},{2,4},{4,2},{6,0},{8,14},{10,12},{12,10},{14,8},{1,7},{3,5},... | collective-permute-start | bytes 196616 | tf_op jit(solution)/shard_map/ppermute | solution.py:434
  21.0 5.1 %collective-permute-start.8 = (bf16[256,128]{1,0:T(8,128)(2,1)S(1)}, bf16[256,128]{1,0:T(8,128)(2,1)S(1)}, u32[]{:S(2)}, u32[]{:S(2)}) collective-permute-start(bf16[256,128]{1,0:T(8,128)(2,1)S(1)} %get-tuple-element.43), channel_id=1, source_target_pairs={{0,2},{2,0},{4,6},{6,4},{8,10},{10,8},{12,14},{14,12},{1,3},{3,1},... | collective-permute-start | bytes 196616 | tf_op jit(solution)/shard_map/ppermute | solution.py:434
  21.9 4.3 %collective-permute-start.9 = (bf16[256,128]{1,0:T(8,128)(2,1)S(1)}, bf16[256,128]{1,0:T(8,128)(2,1)S(1)}, u32[]{:S(2)}, u32[]{:S(2)}) collective-permute-start(bf16[256,128]{1,0:T(8,128)(2,1)S(1)} %get-tuple-element.44), channel_id=1, source_target_pairs={{0,4},{2,6},{4,0},{6,2},{8,12},{10,14},{12,8},{14,10},{1,5},{3,7},... | collective-permute-start | bytes 196616 | tf_op jit(solution)/shard_map/ppermute | solution.py:434
  26.3 4.9 %collective-permute-start.10 = (bf16[128,128]{1,0:T(8,128)(2,1)S(1)}, bf16[128,128]{1,0:T(8,128)(2,1)S(1)}, u32[]{:S(2)}, u32[]{:S(2)}) collective-permute-start(bf16[128,128]{1,0:T(8,128)(2,1)S(1)} %get-tuple-element.46), channel_id=1, source_target_pairs={{0,8},{2,10},{4,12},{6,14},{8,0},{10,2},{12,4},{14,6},{1,9},{3,11}... | collective-permute-start | bytes 98312 | tf_op jit(solution)/shard_map/ppermute | solution.py:448

commit v26 on v24

--- a/solution.py
+++ b/solution.py
@@ -276,10 +276,13 @@
                 send_ref[pl.ds(row, chunk), :] = piece[:, nk:].astype(jnp.bfloat16)
 
 
-def near_kernel(keep_ref, got_ref, *out_refs):
+def near_kernel(by_level, keep_ref, got_ref, *out_refs):
     got = got_ref[...].astype(jnp.float32).reshape(keep_ref.shape)
+    totals = [keep_ref[at] + got[at] for at in range(2)]
+    lower = lax.div(lax.axis_index("space"), NEAR) == 0
     for at, ref in enumerate(out_refs):
-        ref[...] = (keep_ref[at] + got[at]).astype(ref.dtype).reshape(ref.shape)
+        total = jnp.where(lower, totals[at], totals[1 - at]) if by_level else totals[at]
+        ref[...] = total.astype(ref.dtype).reshape(ref.shape)
 
 
 def far_kernel(mine_ref, *refs):
@@ -411,9 +414,9 @@
         got_b = lax.ppermute(send_b, "modes", swap)
         piece = (JB, chunk, nk)
 
-        def summed(out_shape, keep, got):
+        def summed(by_level, out_shape, keep, got):
             return pl.pallas_call(
-                near_kernel,
+                functools.partial(near_kernel, by_level),
                 out_shape=out_shape,
                 in_specs=[vmem] * 2,
                 out_specs=[vmem] * 2,
@@ -423,11 +426,11 @@
 
         kept = jax.ShapeDtypeStruct((2, *piece), f32)
         sent = jax.ShapeDtypeStruct((2 * JB * chunk, nk), bf16)
-        part_3, part_1 = summed([sent, sent], keep_a, got_a)
-        mine, part_2 = summed([kept, sent], keep_b, got_b)
+        out_0, out_1 = summed(True, [sent, sent], keep_a, got_a)
+        mine, out_2 = summed(False, [kept, sent], keep_b, got_b)
         parts = [
-            lax.ppermute(part, "space", [(s, s ^ step) for s in range(n)])
-            for part, step in ((part_3, 3), (part_1, 1), (part_2, 2))
+            lax.ppermute(out, "space", [(s, s ^ steps[s // NEAR]) for s in range(n)])
+            for out, steps in ((out_0, (3, 1)), (out_1, (1, 3)), (out_2, (2, 2)))
         ]
         keep, send = pl.pallas_call(
             far_kernel,

time: 31.4 us -> 31.1 us (level)
  waiting for transfers between devices: 7.63 us -> 7.28 us
    ppermute x1, waiting for transfers between devices: 2.25 us -> 1.89 us  [on_device(): got = lax.ppermute(send, 'space', [(s, s ^ NEAR) for s in range(n)])]
where the time goes in v26:
time: 31.1 us; the launch traced here: 30.9 us
  starting transfers between devices  16.1 us (52%)
  waiting for transfers between devices  7.28 us (23%)
  Pallas kernels  6.79 us (22%)
  between operations  0.76 us (2%)
    ppermute x3, starting transfers between devices, on_device(): lax.ppermute(out, 'space', [(s, s ^ steps[s // NEAR]) for s in range(n)])  3.62 us
    ppermute x3, waiting for transfers between devices, on_device(): lax.ppermute(out, 'space', [(s, s ^ steps[s // NEAR]) for s in range(n)])  3.42 us
    ppermute x1, starting transfers between devices, on_device(): got = lax.ppermute(send, 'space', [(s, s ^ NEAR) for s in range(n)])  3.2 us
    ppermute x1, starting transfers between devices, on_device(): zc = lax.ppermute(zc, both, cross([(s, z_to(s) % n) for s in range(n)]))  2.94 us
    ppermute x1, starting transfers between devices, on_device(): second = lax.ppermute(second, both, same(seconds))  2.6 us
    ppermute x1, starting transfers between devices, on_device(): first = lax.ppermute(first, both, same(firsts))  2.53 us
    pallas_call x1, Pallas kernels, on_device(): pl.pallas_call(local_kernel, out_shape=[jax.ShapeDtypeStruct((JB * 2 * nk...  2.43 us
    ppermute x1, waiting for transfers between devices, on_device(): got = lax.ppermute(send, 'space', [(s, s ^ NEAR) for s in range(n)])  1.89 us
  transfers between devices with their start and end apart: 11, of which 7 were waited for; matrix products, arithmetic and copies ran while one was open for 0% of the time, Pallas kernels for 13%

profile of v26, /device:TPU:0, one launch (start us, length us, event | category | flops | bytes accessed | tf_op | source)
XLA Modules:
  0.0 30.9 jit_solution(2395928637485397159)
XLA Ops:
  0.0 0.0 copy-start.1
  0.0 1.4 %prep.1 = (bf16[8,3,128,128]{3,2,1,0:T(8,128)(2,1)S(1)}, bf16[784,128]{1,0:T(8,128)(2,1)S(1)}, bf16[784,128]{1,0:T(8,128)(2,1)S(1)}) custom-call(bf16[128,3,1,8,128]{4,3,2,1,0:T(8,128)(2,1)} %modes_hbm.1), custom_call_target="tpu_custom_call" | custom-call | flops 1500000000 | bytes 2800000 | tf_op jit(solution)/shard_map/prep/pallas_call | solution.py:314
  1.4 0.0 copy-start
  1.4 0.5 %collective-permute-start = (bf16[8,3,128,128]{3,2,1,0:T(8,128)(2,1)S(1)}, bf16[8,3,128,128]{3,2,1,0:T(8,128)(2,1)S(1)}, u32[]{:S(2)}, u32[]{:S(2)}) collective-permute-start(bf16[8,3,128,128]{3,2,1,0:T(8,128)(2,1)S(1)} %get-tuple-element.26.tr.own_ref), channel_id=1, source_target_pairs={{0,1},{1,0},{2,3},{3,2},{4,5},{5,4},{6,7},{7,6},{8,9},{9,8},{10,11... | collective-permute-start | bytes 2359304 | tf_op jit(solution)/shard_map/ppermute | solution.py:334
  1.9 2.5 %collective-permute-start.1 = (bf16[784,128]{1,0:T(8,128)(2,1)S(1)}, bf16[784,128]{1,0:T(8,128)(2,1)S(1)}, u32[]{:S(2)}, u32[]{:S(2)}) collective-permute-start(bf16[784,128]{1,0:T(8,128)(2,1)S(1)} %get-tuple-element.27), channel_id=1, source_target_pairs={{0,2},{1,3},{2,0},{3,1},{4,6},{5,7},{6,4},{7,5},{8,10},{9,11},{10,... | collective-permute-start | bytes 602120 | tf_op jit(solution)/shard_map/ppermute | solution.py:335
  4.5 2.6 %collective-permute-start.2 = (bf16[784,128]{1,0:T(8,128)(2,1)S(1)}, bf16[784,128]{1,0:T(8,128)(2,1)S(1)}, u32[]{:S(2)}, u32[]{:S(2)}) collective-permute-start(bf16[784,128]{1,0:T(8,128)(2,1)S(1)} %get-tuple-element.28), channel_id=1, source_target_pairs={{0,12},{1,13},{2,6},{3,7},{4,0},{5,1},{6,10},{7,11},{8,4},{9,5},{1... | collective-permute-start | bytes 602120 | tf_op jit(solution)/shard_map/ppermute | solution.py:336
  7.1 0.0 collective-permute-done._.other_ref
  7.1 0.0 copy-done.1
  7.1 0.0 copy-done
  7.1 0.1 weights.1
  7.2 0.1 collective-permute-start.3
  7.3 2.9 %collective-permute-start.4 = (bf16[784,128]{1,0:T(8,128)(2,1)S(1)}, bf16[784,128]{1,0:T(8,128)(2,1)S(1)}, u32[]{:S(2)}, u32[]{:S(2)}) collective-permute-start(bf16[784,128]{1,0:T(8,128)(2,1)S(1)} %get-tuple-element.30), channel_id=1, source_target_pairs={{0,13},{1,12},{2,7},{3,6},{4,1},{5,0},{6,11},{7,10},{8,5},{9,4},{1... | collective-permute-start | bytes 602120 | tf_op jit(solution)/shard_map/ppermute | solution.py:347
  10.9 2.4 %local.1 = (f32[1024,256]{1,0:T(8,128)S(1)}, bf16[2,256,384]{2,1,0:T(8,128)(2,1)S(1)}) custom-call(bf16[8,3,128,128]{3,2,1,0:T(8,128)(2,1)S(1)} %get-tuple-element.26.tr.own_ref, bf16[8,3,128,128]{3,2,1,0:T(8,128)(2,1)S(1)} %collective-permute-done._.other_ref, f32[8,128]{1,0:T(8,128)S(1)} %get-tuple-element.31.weight_ref, s32[1]{0:T(128)S(6)} %copy.5.jb_ref.refs_5_), custom_call_target="tpu_custom_call" | custom-call | flops 900000000 | bytes 2400000 | tf_op jit(solution)/shard_map/local/pallas_call | solution.py:351
  13.3 0.0 collective-permute-done.1.first_ref.refs_0_
  13.3 0.0 collective-permute-done.2.second_ref.refs_1_
  13.3 1.2 %collective-permute-done.3.xc_ref.refs_2_ = bf16[784,128]{1,0:T(8,128)(2,1)S(1)} collective-permute-done((bf16[784,128]{1,0:T(8,128)(2,1)S(1)}, bf16[784,128]{1,0:T(8,128)(2,1)S(1)}, u32[]{:S(2)}, u32[]{:S(2)}) %collective-permute-start.3) | collective-permute-done | bytes 200736 | tf_op jit(solution)/shard_map/ppermute | solution.py:346
  14.5 0.8 %early.1 = (f32[1024,256]{1,0:T(8,128)S(1)}, bf16[256,768]{1,0:T(8,128)(2,1)S(1)}) custom-call(bf16[8,3,128,128]{3,2,1,0:T(8,128)(2,1)S(1)} %get-tuple-element.26.tr.own_ref, bf16[8,3,128,128]{3,2,1,0:T(8,128)(2,1)S(1)} %collective-permute-done._.other_ref, bf16[784,128]{1,0:T(8,128)(2,1)S(1)} %collective-permute-done.1.first_ref.refs_0_, ...), custom_call_target="tpu_custom_call" | custom-call | flops 600000000 | bytes 2400000 | tf_op jit(solution)/shard_map/early/pallas_call | solution.py:368
  15.3 0.7 %collective-permute-done.4.refs_3_ = bf16[784,128]{1,0:T(8,128)(2,1)S(1)} collective-permute-done((bf16[784,128]{1,0:T(8,128)(2,1)S(1)}, bf16[784,128]{1,0:T(8,128)(2,1)S(1)}, u32[]{:S(2)}, u32[]{:S(2)}) %collective-permute-start.4) | collective-permute-done | bytes 200736 | tf_op jit(solution)/shard_map/ppermute | solution.py:347
  15.9 0.7 %cross.2 = (f32[2,2,4,32,128]{4,3,2,1,0:T(8,128)S(1)}, bf16[512,128]{1,0:T(8,128)(2,1)S(1)}, bf16[256,1536]{1,0:T(8,128)(2,1)S(1)}) custom-call(bf16[8,3,128,128]{3,2,1,0:T(8,128)(2,1)S(1)} %get-tuple-element.26.tr.own_ref, bf16[8,3,128,128]{3,2,1,0:T(8,128)(2,1)S(1)} %collective-permute-done._.other_ref, ...), custom_call_target="tpu_custom_call" | custom-call | flops 900000000 | bytes 4000000 | tf_op jit(solution)/shard_map/cross/pallas_call | solution.py:393
  16.6 0.1 collective-permute-start.6
  16.7 0.6 %cross.3 = (f32[2,2,4,32,128]{4,3,2,1,0:T(8,128)S(1)}, bf16[512,128]{1,0:T(8,128)(2,1)S(1)}) custom-call(bf16[8,3,128,128]{3,2,1,0:T(8,128)(2,1)S(1)} %get-tuple-element.26.tr.own_ref, bf16[8,3,128,128]{3,2,1,0:T(8,128)(2,1)S(1)} %collective-permute-done._.other_ref, bf16[784,128]{1,0:T(8,128)(2,1)S(1)} %collective-permute-done.1.first_ref.refs_0_, ...), custom_call_target="tpu_custom_call" | custom-call | flops 900000000 | bytes 4000000 | tf_op jit(solution)/shard_map/cross/pallas_call | solution.py:393
  17.3 0.6 %collective-permute-start.5 = (bf16[512,128]{1,0:T(8,128)(2,1)S(1)}, bf16[512,128]{1,0:T(8,128)(2,1)S(1)}, u32[]{:S(2)}, u32[]{:S(2)}) collective-permute-start(bf16[512,128]{1,0:T(8,128)(2,1)S(1)} %get-tuple-element.38), channel_id=1, source_target_pairs={{0,1},{1,0},{2,3},{3,2},{4,5},{5,4},{6,7},{7,6},{8,9},{9,8},{10,11... | collective-permute-start | bytes 393224 | tf_op jit(solution)/shard_map/ppermute | solution.py:414
  17.9 0.1 collective-permute-done.6.got_ref
  18.1 1.7 %collective-permute-start.7 = (bf16[256,128]{1,0:T(8,128)(2,1)S(1)}, bf16[256,128]{1,0:T(8,128)(2,1)S(1)}, u32[]{:S(2)}, u32[]{:S(2)}) collective-permute-start(bf16[256,128]{1,0:T(8,128)(2,1)S(1)} %get-tuple-element.42), channel_id=1, source_target_pairs={{0,6},{2,4},{4,2},{6,0},{8,10},{10,8},{12,14},{14,12},{1,7},{3,5},... | collective-permute-start | bytes 196616 | tf_op jit(solution)/shard_map/ppermute | solution.py:432
  19.7 0.8 %collective-permute-start.8 = (bf16[256,128]{1,0:T(8,128)(2,1)S(1)}, bf16[256,128]{1,0:T(8,128)(2,1)S(1)}, u32[]{:S(2)}, u32[]{:S(2)}) collective-permute-start(bf16[256,128]{1,0:T(8,128)(2,1)S(1)} %get-tuple-element.43), channel_id=1, source_target_pairs={{0,2},{2,0},{4,6},{6,4},{8,14},{10,12},{12,10},{14,8},{1,3},{3,1},... | collective-permute-start | bytes 196616 | tf_op jit(solution)/shard_map/ppermute | solution.py:432
  20.6 0.0 collective-permute-done.5.got_ref
  20.6 1.1 %collective-permute-start.9 = (bf16[256,128]{1,0:T(8,128)(2,1)S(1)}, bf16[256,128]{1,0:T(8,128)(2,1)S(1)}, u32[]{:S(2)}, u32[]{:S(2)}) collective-permute-start(bf16[256,128]{1,0:T(8,128)(2,1)S(1)} %get-tuple-element.44), channel_id=1, source_target_pairs={{0,4},{2,6},{4,0},{6,2},{8,12},{10,14},{12,8},{14,10},{1,5},{3,7},... | collective-permute-start | bytes 196616 | tf_op jit(solution)/shard_map/ppermute | solution.py:432
  21.7 1.6 %collective-permute-done.7.refs_0_ = bf16[256,128]{1,0:T(8,128)(2,1)S(1)} collective-permute-done((bf16[256,128]{1,0:T(8,128)(2,1)S(1)}, bf16[256,128]{1,0:T(8,128)(2,1)S(1)}, u32[]{:S(2)}, u32[]{:S(2)}) %collective-permute-start.7) | collective-permute-done | bytes 65568 | tf_op jit(solution)/shard_map/ppermute | solution.py:432
  23.4 1.2 %collective-permute-done.8.refs_1_ = bf16[256,128]{1,0:T(8,128)(2,1)S(1)} collective-permute-done((bf16[256,128]{1,0:T(8,128)(2,1)S(1)}, bf16[256,128]{1,0:T(8,128)(2,1)S(1)}, u32[]{:S(2)}, u32[]{:S(2)}) %collective-permute-start.8) | collective-permute-done | bytes 65568 | tf_op jit(solution)/shard_map/ppermute | solution.py:432
  24.6 0.6 %collective-permute-done.9.refs_2_ = bf16[256,128]{1,0:T(8,128)(2,1)S(1)} collective-permute-done((bf16[256,128]{1,0:T(8,128)(2,1)S(1)}, bf16[256,128]{1,0:T(8,128)(2,1)S(1)}, u32[]{:S(2)}, u32[]{:S(2)}) %collective-permute-start.9) | collective-permute-done | bytes 65568 | tf_op jit(solution)/shard_map/ppermute | solution.py:432
  25.2 3.2 %collective-permute-start.10 = (bf16[128,128]{1,0:T(8,128)(2,1)S(1)}, bf16[128,128]{1,0:T(8,128)(2,1)S(1)}, u32[]{:S(2)}, u32[]{:S(2)}) collective-permute-start(bf16[128,128]{1,0:T(8,128)(2,1)S(1)} %get-tuple-element.46), channel_id=1, source_target_pairs={{0,8},{2,10},{4,12},{6,14},{8,0},{10,2},{12,4},{14,6},{1,9},{3,11}... | collective-permute-start | bytes 98312 | tf_op jit(solution)/shard_map/ppermute | solution.py:446
  28.4 1.9 %collective-permute-done.10.got_ref = bf16[128,128]{1,0:T(8,128)(2,1)S(1)} collective-permute-done((bf16[128,128]{1,0:T(8,128)(2,1)S(1)}, bf16[128,128]{1,0:T(8,128)(2,1)S(1)}, u32[]{:S(2)}, u32[]{:S(2)}) %collective-permute-start.10) | collective-permute-done | bytes 32800 | tf_op jit(solution)/shard_map/ppermute | solution.py:446
  30.3 0.7 %total.1 = f32[32,4,128]{2,1,0:T(4,128)} custom-call(f32[4,32,128]{2,1,0:T(8,128)S(1)} %get-tuple-element.45.keep_ref, bf16[128,128]{1,0:T(8,128)(2,1)S(1)} %collective-permute-done.10.got_ref), custom_call_target="tpu_custom_call" | custom-call | tf_op jit(solution)/shard_map/total/pallas_call | solution.py:447
  (4 shorter events, 0.1 us)
Async XLA Ops:
  0.0 7.1 %copy-start.1 = (f32[16]{0:T(128)S(1)}, f32[16]{0:T(128)}, u32[]{:S(2)}) copy-start(f32[16]{0:T(128)} %param.6) | copy-start | bytes 196
  1.4 5.7 %copy-start = (s32[1,8,128]{2,1,0:T(8,128)S(1)}, s32[1,8,128]{2,1,0:T(8,128)}, u32[]{:S(2)}) copy-start(s32[1,8,128]{2,1,0:T(8,128)} %ids_ref.1) | copy-start | bytes 12292
  1.4 5.7 %collective-permute-start = (bf16[8,3,128,128]{3,2,1,0:T(8,128)(2,1)S(1)}, bf16[8,3,128,128]{3,2,1,0:T(8,128)(2,1)S(1)}, u32[]{:S(2)}, u32[]{:S(2)}) collective-permute-start(bf16[8,3,128,128]{3,2,1,0:T(8,128)(2,1)S(1)} %get-tuple-element.26.tr.own_ref), channel_id=1, source_target_pairs={{0,1},{1,0},{2,3},{3,2},{4,5},{5,4},{6,7},{7,6},{8,9},{9,8},{10,11... | collective-permute-start | bytes 2359304 | tf_op jit(solution)/shard_map/ppermute | solution.py:334
  1.9 11.4 %collective-permute-start.1 = (bf16[784,128]{1,0:T(8,128)(2,1)S(1)}, bf16[784,128]{1,0:T(8,128)(2,1)S(1)}, u32[]{:S(2)}, u32[]{:S(2)}) collective-permute-start(bf16[784,128]{1,0:T(8,128)(2,1)S(1)} %get-tuple-element.27), channel_id=1, source_target_pairs={{0,2},{1,3},{2,0},{3,1},{4,6},{5,7},{6,4},{7,5},{8,10},{9,11},{10,... | collective-permute-start | bytes 602120 | tf_op jit(solution)/shard_map/ppermute | solution.py:335
  4.5 8.9 %collective-permute-start.2 = (bf16[784,128]{1,0:T(8,128)(2,1)S(1)}, bf16[784,128]{1,0:T(8,128)(2,1)S(1)}, u32[]{:S(2)}, u32[]{:S(2)}) collective-permute-start(bf16[784,128]{1,0:T(8,128)(2,1)S(1)} %get-tuple-element.28), channel_id=1, source_target_pairs={{0,12},{1,13},{2,6},{3,7},{4,0},{5,1},{6,10},{7,11},{8,4},{9,5},{1... | collective-permute-start | bytes 602120 | tf_op jit(solution)/shard_map/ppermute | solution.py:336
  7.2 7.3 %collective-permute-start.3 = (bf16[784,128]{1,0:T(8,128)(2,1)S(1)}, bf16[784,128]{1,0:T(8,128)(2,1)S(1)}, u32[]{:S(2)}, u32[]{:S(2)}) collective-permute-start(bf16[784,128]{1,0:T(8,128)(2,1)S(1)} %get-tuple-element.29), channel_id=1, source_target_pairs={{0,3},{1,2},{2,1},{3,0},{4,7},{5,6},{6,5},{7,4},{8,11},{9,10},{10,... | collective-permute-start | bytes 602120 | tf_op jit(solution)/shard_map/ppermute | solution.py:346
  7.3 8.6 %collective-permute-start.4 = (bf16[784,128]{1,0:T(8,128)(2,1)S(1)}, bf16[784,128]{1,0:T(8,128)(2,1)S(1)}, u32[]{:S(2)}, u32[]{:S(2)}) collective-permute-start(bf16[784,128]{1,0:T(8,128)(2,1)S(1)} %get-tuple-element.30), channel_id=1, source_target_pairs={{0,13},{1,12},{2,7},{3,6},{4,1},{5,0},{6,11},{7,10},{8,5},{9,4},{1... | collective-permute-start | bytes 602120 | tf_op jit(solution)/shard_map/ppermute | solution.py:347
  16.6 1.4 %collective-permute-start.6 = (bf16[512,128]{1,0:T(8,128)(2,1)S(1)}, bf16[512,128]{1,0:T(8,128)(2,1)S(1)}, u32[]{:S(2)}, u32[]{:S(2)}) collective-permute-start(bf16[512,128]{1,0:T(8,128)(2,1)S(1)} %get-tuple-element.41), channel_id=1, source_target_pairs={{0,1},{1,0},{2,3},{3,2},{4,5},{5,4},{6,7},{7,6},{8,9},{9,8},{10,11... | collective-permute-start | bytes 393224 | tf_op jit(solution)/shard_map/ppermute | solution.py:412
  17.3 3.2 %collective-permute-start.5 = (bf16[512,128]{1,0:T(8,128)(2,1)S(1)}, bf16[512,128]{1,0:T(8,128)(2,1)S(1)}, u32[]{:S(2)}, u32[]{:S(2)}) collective-permute-start(bf16[512,128]{1,0:T(8,128)(2,1)S(1)} %get-tuple-element.38), channel_id=1, source_target_pairs={{0,1},{1,0},{2,3},{3,2},{4,5},{5,4},{6,7},{7,6},{8,9},{9,8},{10,11... | collective-permute-start | bytes 393224 | tf_op jit(solution)/shard_map/ppermute | solution.py:414
  18.1 5.3 %collective-permute-start.7 = (bf16[256,128]{1,0:T(8,128)(2,1)S(1)}, bf16[256,128]{1,0:T(8,128)(2,1)S(1)}, u32[]{:S(2)}, u32[]{:S(2)}) collective-permute-start(bf16[256,128]{1,0:T(8,128)(2,1)S(1)} %get-tuple-element.42), channel_id=1, source_target_pairs={{0,6},{2,4},{4,2},{6,0},{8,10},{10,8},{12,14},{14,12},{1,7},{3,5},... | collective-permute-start | bytes 196616 | tf_op jit(solution)/shard_map/ppermute | solution.py:432
  19.7 4.8 %collective-permute-start.8 = (bf16[256,128]{1,0:T(8,128)(2,1)S(1)}, bf16[256,128]{1,0:T(8,128)(2,1)S(1)}, u32[]{:S(2)}, u32[]{:S(2)}) collective-permute-start(bf16[256,128]{1,0:T(8,128)(2,1)S(1)} %get-tuple-element.43), channel_id=1, source_target_pairs={{0,2},{2,0},{4,6},{6,4},{8,14},{10,12},{12,10},{14,8},{1,3},{3,1},... | collective-permute-start | bytes 196616 | tf_op jit(solution)/shard_map/ppermute | solution.py:432
  20.6 4.6 %collective-permute-start.9 = (bf16[256,128]{1,0:T(8,128)(2,1)S(1)}, bf16[256,128]{1,0:T(8,128)(2,1)S(1)}, u32[]{:S(2)}, u32[]{:S(2)}) collective-permute-start(bf16[256,128]{1,0:T(8,128)(2,1)S(1)} %get-tuple-element.44), channel_id=1, source_target_pairs={{0,4},{2,6},{4,0},{6,2},{8,12},{10,14},{12,8},{14,10},{1,5},{3,7},... | collective-permute-start | bytes 196616 | tf_op jit(solution)/shard_map/ppermute | solution.py:432
  25.2 5.1 %collective-permute-start.10 = (bf16[128,128]{1,0:T(8,128)(2,1)S(1)}, bf16[128,128]{1,0:T(8,128)(2,1)S(1)}, u32[]{:S(2)}, u32[]{:S(2)}) collective-permute-start(bf16[128,128]{1,0:T(8,128)(2,1)S(1)} %get-tuple-element.46), channel_id=1, source_target_pairs={{0,8},{2,10},{4,12},{6,14},{8,0},{10,2},{12,4},{14,6},{1,9},{3,11}... | collective-permute-start | bytes 98312 | tf_op jit(solution)/shard_map/ppermute | solution.py:446

commit v27 on v24

--- a/solution.py
+++ b/solution.py
@@ -403,11 +403,13 @@
     swap = [(0, 1), (1, 0)]
     if n == 2 * NEAR:
         def partners(*steps):
-            return lambda s: [jnp.bitwise_xor(lax.rem(s, NEAR), step) for step in steps]
-
-        keep_a, send_a, w2 = crossed(2, partners(3, 1), ())
+            return lambda s: [
+                jnp.bitwise_xor(lax.rem(s, NEAR), jnp.where(s < NEAR, low, high)) for low, high in steps
+            ]
+
+        keep_a, send_a, w2 = crossed(2, partners((3, 1), (1, 2)), ())
         got_a = lax.ppermute(send_a, "modes", swap)
-        keep_b, send_b = crossed(2, partners(0, 2), (w2,))
+        keep_b, send_b = crossed(2, partners((0, 0), (2, 3)), (w2,))
         got_b = lax.ppermute(send_b, "modes", swap)
         piece = (JB, chunk, nk)
 
@@ -423,11 +425,11 @@
 
         kept = jax.ShapeDtypeStruct((2, *piece), f32)
         sent = jax.ShapeDtypeStruct((2 * JB * chunk, nk), bf16)
-        part_3, part_1 = summed([sent, sent], keep_a, got_a)
-        mine, part_2 = summed([kept, sent], keep_b, got_b)
+        out_0, out_1 = summed([sent, sent], keep_a, got_a)
+        mine, out_2 = summed([kept, sent], keep_b, got_b)
         parts = [
-            lax.ppermute(part, "space", [(s, s ^ step) for s in range(n)])
-            for part, step in ((part_3, 3), (part_1, 1), (part_2, 2))
+            lax.ppermute(out, "space", [(s, s ^ steps[s // NEAR]) for s in range(n)])
+            for out, steps in ((out_0, (3, 1)), (out_1, (1, 2)), (out_2, (2, 3)))
         ]
         keep, send = pl.pallas_call(
             far_kernel,

time: 31.4 us -> 31.1 us (level)
  waiting for transfers between devices: 7.63 us -> 7.27 us
    ppermute x1, waiting for transfers between devices: 2.25 us -> 1.89 us  [on_device(): got = lax.ppermute(send, 'space', [(s, s ^ NEAR) for s in range(n)])]
where the time goes in v27:
time: 31.1 us; the launch traced here: 30.9 us
  starting transfers between devices  16.1 us (52%)
  waiting for transfers between devices  7.27 us (23%)
  Pallas kernels  6.78 us (22%)
  between operations  0.76 us (2%)
    ppermute x3, starting transfers between devices, on_device(): lax.ppermute(out, 'space', [(s, s ^ steps[s // NEAR]) for s in range(n)])  3.62 us
    ppermute x3, waiting for transfers between devices, on_device(): lax.ppermute(out, 'space', [(s, s ^ steps[s // NEAR]) for s in range(n)])  3.42 us
    ppermute x1, starting transfers between devices, on_device(): got = lax.ppermute(send, 'space', [(s, s ^ NEAR) for s in range(n)])  3.2 us
    ppermute x1, starting transfers between devices, on_device(): zc = lax.ppermute(zc, both, cross([(s, z_to(s) % n) for s in range(n)]))  2.94 us
    ppermute x1, starting transfers between devices, on_device(): second = lax.ppermute(second, both, same(seconds))  2.6 us
    ppermute x1, starting transfers between devices, on_device(): first = lax.ppermute(first, both, same(firsts))  2.53 us
    pallas_call x1, Pallas kernels, on_device(): pl.pallas_call(local_kernel, out_shape=[jax.ShapeDtypeStruct((JB * 2 * nk...  2.43 us
    ppermute x1, waiting for transfers between devices, on_device(): got = lax.ppermute(send, 'space', [(s, s ^ NEAR) for s in range(n)])  1.89 us
  transfers between devices with their start and end apart: 11, of which 7 were waited for; matrix products, arithmetic and copies ran while one was open for 0% of the time, Pallas kernels for 13%

profile of v27, /device:TPU:0, one launch (start us, length us, event | category | flops | bytes accessed | tf_op | source)
XLA Modules:
  0.0 30.9 jit_solution(10611664281197448232)
XLA Ops:
  0.0 0.0 copy-start.1
  0.0 1.4 %prep.1 = (bf16[8,3,128,128]{3,2,1,0:T(8,128)(2,1)S(1)}, bf16[784,128]{1,0:T(8,128)(2,1)S(1)}, bf16[784,128]{1,0:T(8,128)(2,1)S(1)}) custom-call(bf16[128,3,1,8,128]{4,3,2,1,0:T(8,128)(2,1)} %modes_hbm.1), custom_call_target="tpu_custom_call" | custom-call | flops 1500000000 | bytes 2800000 | tf_op jit(solution)/shard_map/prep/pallas_call | solution.py:311
  1.4 0.0 copy-start
  1.4 0.5 %collective-permute-start = (bf16[8,3,128,128]{3,2,1,0:T(8,128)(2,1)S(1)}, bf16[8,3,128,128]{3,2,1,0:T(8,128)(2,1)S(1)}, u32[]{:S(2)}, u32[]{:S(2)}) collective-permute-start(bf16[8,3,128,128]{3,2,1,0:T(8,128)(2,1)S(1)} %get-tuple-element.26.tr.own_ref), channel_id=1, source_target_pairs={{0,1},{1,0},{2,3},{3,2},{4,5},{5,4},{6,7},{7,6},{8,9},{9,8},{10,11... | collective-permute-start | bytes 2359304 | tf_op jit(solution)/shard_map/ppermute | solution.py:331
  1.9 2.5 %collective-permute-start.1 = (bf16[784,128]{1,0:T(8,128)(2,1)S(1)}, bf16[784,128]{1,0:T(8,128)(2,1)S(1)}, u32[]{:S(2)}, u32[]{:S(2)}) collective-permute-start(bf16[784,128]{1,0:T(8,128)(2,1)S(1)} %get-tuple-element.27), channel_id=1, source_target_pairs={{0,2},{1,3},{2,0},{3,1},{4,6},{5,7},{6,4},{7,5},{8,10},{9,11},{10,... | collective-permute-start | bytes 602120 | tf_op jit(solution)/shard_map/ppermute | solution.py:332
  4.5 2.6 %collective-permute-start.2 = (bf16[784,128]{1,0:T(8,128)(2,1)S(1)}, bf16[784,128]{1,0:T(8,128)(2,1)S(1)}, u32[]{:S(2)}, u32[]{:S(2)}) collective-permute-start(bf16[784,128]{1,0:T(8,128)(2,1)S(1)} %get-tuple-element.28), channel_id=1, source_target_pairs={{0,12},{1,13},{2,6},{3,7},{4,0},{5,1},{6,10},{7,11},{8,4},{9,5},{1... | collective-permute-start | bytes 602120 | tf_op jit(solution)/shard_map/ppermute | solution.py:333
  7.1 0.0 collective-permute-done._.other_ref
  7.1 0.0 copy-done.1
  7.1 0.0 copy-done
  7.1 0.1 weights.1
  7.2 0.1 collective-permute-start.3
  7.3 2.9 %collective-permute-start.4 = (bf16[784,128]{1,0:T(8,128)(2,1)S(1)}, bf16[784,128]{1,0:T(8,128)(2,1)S(1)}, u32[]{:S(2)}, u32[]{:S(2)}) collective-permute-start(bf16[784,128]{1,0:T(8,128)(2,1)S(1)} %get-tuple-element.30), channel_id=1, source_target_pairs={{0,13},{1,12},{2,7},{3,6},{4,1},{5,0},{6,11},{7,10},{8,5},{9,4},{1... | collective-permute-start | bytes 602120 | tf_op jit(solution)/shard_map/ppermute | solution.py:344
  10.9 2.4 %local.1 = (f32[1024,256]{1,0:T(8,128)S(1)}, bf16[2,256,384]{2,1,0:T(8,128)(2,1)S(1)}) custom-call(bf16[8,3,128,128]{3,2,1,0:T(8,128)(2,1)S(1)} %get-tuple-element.26.tr.own_ref, bf16[8,3,128,128]{3,2,1,0:T(8,128)(2,1)S(1)} %collective-permute-done._.other_ref, f32[8,128]{1,0:T(8,128)S(1)} %get-tuple-element.31.weight_ref, s32[1]{0:T(128)S(6)} %copy.5.jb_ref.refs_5_), custom_call_target="tpu_custom_call" | custom-call | flops 900000000 | bytes 2400000 | tf_op jit(solution)/shard_map/local/pallas_call | solution.py:348
  13.3 0.0 collective-permute-done.1.first_ref.refs_0_
  13.3 0.0 collective-permute-done.2.second_ref.refs_1_
  13.3 1.2 %collective-permute-done.3.xc_ref.refs_2_ = bf16[784,128]{1,0:T(8,128)(2,1)S(1)} collective-permute-done((bf16[784,128]{1,0:T(8,128)(2,1)S(1)}, bf16[784,128]{1,0:T(8,128)(2,1)S(1)}, u32[]{:S(2)}, u32[]{:S(2)}) %collective-permute-start.3) | collective-permute-done | bytes 200736 | tf_op jit(solution)/shard_map/ppermute | solution.py:343
  14.5 0.8 %early.1 = (f32[1024,256]{1,0:T(8,128)S(1)}, bf16[256,768]{1,0:T(8,128)(2,1)S(1)}) custom-call(bf16[8,3,128,128]{3,2,1,0:T(8,128)(2,1)S(1)} %get-tuple-element.26.tr.own_ref, bf16[8,3,128,128]{3,2,1,0:T(8,128)(2,1)S(1)} %collective-permute-done._.other_ref, bf16[784,128]{1,0:T(8,128)(2,1)S(1)} %collective-permute-done.1.first_ref.refs_0_, ...), custom_call_target="tpu_custom_call" | custom-call | flops 600000000 | bytes 2400000 | tf_op jit(solution)/shard_map/early/pallas_call | solution.py:365
  15.3 0.7 %collective-permute-done.4.refs_3_ = bf16[784,128]{1,0:T(8,128)(2,1)S(1)} collective-permute-done((bf16[784,128]{1,0:T(8,128)(2,1)S(1)}, bf16[784,128]{1,0:T(8,128)(2,1)S(1)}, u32[]{:S(2)}, u32[]{:S(2)}) %collective-permute-start.4) | collective-permute-done | bytes 200736 | tf_op jit(solution)/shard_map/ppermute | solution.py:344
  15.9 0.7 %cross.2 = (f32[2,2,4,32,128]{4,3,2,1,0:T(8,128)S(1)}, bf16[512,128]{1,0:T(8,128)(2,1)S(1)}, bf16[256,1536]{1,0:T(8,128)(2,1)S(1)}) custom-call(bf16[8,3,128,128]{3,2,1,0:T(8,128)(2,1)S(1)} %get-tuple-element.26.tr.own_ref, bf16[8,3,128,128]{3,2,1,0:T(8,128)(2,1)S(1)} %collective-permute-done._.other_ref, ...), custom_call_target="tpu_custom_call" | custom-call | flops 900000000 | bytes 4000000 | tf_op jit(solution)/shard_map/cross/pallas_call | solution.py:390
  16.6 0.1 collective-permute-start.6
  16.7 0.6 %cross.3 = (f32[2,2,4,32,128]{4,3,2,1,0:T(8,128)S(1)}, bf16[512,128]{1,0:T(8,128)(2,1)S(1)}) custom-call(bf16[8,3,128,128]{3,2,1,0:T(8,128)(2,1)S(1)} %get-tuple-element.26.tr.own_ref, bf16[8,3,128,128]{3,2,1,0:T(8,128)(2,1)S(1)} %collective-permute-done._.other_ref, bf16[784,128]{1,0:T(8,128)(2,1)S(1)} %collective-permute-done.1.first_ref.refs_0_, ...), custom_call_target="tpu_custom_call" | custom-call | flops 900000000 | bytes 4000000 | tf_op jit(solution)/shard_map/cross/pallas_call | solution.py:390
  17.3 0.6 %collective-permute-start.5 = (bf16[512,128]{1,0:T(8,128)(2,1)S(1)}, bf16[512,128]{1,0:T(8,128)(2,1)S(1)}, u32[]{:S(2)}, u32[]{:S(2)}) collective-permute-start(bf16[512,128]{1,0:T(8,128)(2,1)S(1)} %get-tuple-element.38), channel_id=1, source_target_pairs={{0,1},{1,0},{2,3},{3,2},{4,5},{5,4},{6,7},{7,6},{8,9},{9,8},{10,11... | collective-permute-start | bytes 393224 | tf_op jit(solution)/shard_map/ppermute | solution.py:413
  17.9 0.1 collective-permute-done.6.got_ref
  18.1 1.7 %collective-permute-start.7 = (bf16[256,128]{1,0:T(8,128)(2,1)S(1)}, bf16[256,128]{1,0:T(8,128)(2,1)S(1)}, u32[]{:S(2)}, u32[]{:S(2)}) collective-permute-start(bf16[256,128]{1,0:T(8,128)(2,1)S(1)} %get-tuple-element.42), channel_id=1, source_target_pairs={{0,6},{2,4},{4,2},{6,0},{8,10},{10,8},{12,14},{14,12},{1,7},{3,5},... | collective-permute-start | bytes 196616 | tf_op jit(solution)/shard_map/ppermute | solution.py:431
  19.7 0.8 %collective-permute-start.8 = (bf16[256,128]{1,0:T(8,128)(2,1)S(1)}, bf16[256,128]{1,0:T(8,128)(2,1)S(1)}, u32[]{:S(2)}, u32[]{:S(2)}) collective-permute-start(bf16[256,128]{1,0:T(8,128)(2,1)S(1)} %get-tuple-element.43), channel_id=1, source_target_pairs={{0,2},{2,0},{4,6},{6,4},{8,12},{10,14},{12,8},{14,10},{1,3},{3,1},... | collective-permute-start | bytes 196616 | tf_op jit(solution)/shard_map/ppermute | solution.py:431
  20.5 0.0 collective-permute-done.5.got_ref
  20.6 1.1 %collective-permute-start.9 = (bf16[256,128]{1,0:T(8,128)(2,1)S(1)}, bf16[256,128]{1,0:T(8,128)(2,1)S(1)}, u32[]{:S(2)}, u32[]{:S(2)}) collective-permute-start(bf16[256,128]{1,0:T(8,128)(2,1)S(1)} %get-tuple-element.44), channel_id=1, source_target_pairs={{0,4},{2,6},{4,0},{6,2},{8,14},{10,12},{12,10},{14,8},{1,5},{3,7},... | collective-permute-start | bytes 196616 | tf_op jit(solution)/shard_map/ppermute | solution.py:431
  21.7 1.6 %collective-permute-done.7.refs_0_ = bf16[256,128]{1,0:T(8,128)(2,1)S(1)} collective-permute-done((bf16[256,128]{1,0:T(8,128)(2,1)S(1)}, bf16[256,128]{1,0:T(8,128)(2,1)S(1)}, u32[]{:S(2)}, u32[]{:S(2)}) %collective-permute-start.7) | collective-permute-done | bytes 65568 | tf_op jit(solution)/shard_map/ppermute | solution.py:431
  23.3 1.2 %collective-permute-done.8.refs_1_ = bf16[256,128]{1,0:T(8,128)(2,1)S(1)} collective-permute-done((bf16[256,128]{1,0:T(8,128)(2,1)S(1)}, bf16[256,128]{1,0:T(8,128)(2,1)S(1)}, u32[]{:S(2)}, u32[]{:S(2)}) %collective-permute-start.8) | collective-permute-done | bytes 65568 | tf_op jit(solution)/shard_map/ppermute | solution.py:431
  24.6 0.6 %collective-permute-done.9.refs_2_ = bf16[256,128]{1,0:T(8,128)(2,1)S(1)} collective-permute-done((bf16[256,128]{1,0:T(8,128)(2,1)S(1)}, bf16[256,128]{1,0:T(8,128)(2,1)S(1)}, u32[]{:S(2)}, u32[]{:S(2)}) %collective-permute-start.9) | collective-permute-done | bytes 65568 | tf_op jit(solution)/shard_map/ppermute | solution.py:431
  25.2 3.2 %collective-permute-start.10 = (bf16[128,128]{1,0:T(8,128)(2,1)S(1)}, bf16[128,128]{1,0:T(8,128)(2,1)S(1)}, u32[]{:S(2)}, u32[]{:S(2)}) collective-permute-start(bf16[128,128]{1,0:T(8,128)(2,1)S(1)} %get-tuple-element.46), channel_id=1, source_target_pairs={{0,8},{2,10},{4,12},{6,14},{8,0},{10,2},{12,4},{14,6},{1,9},{3,11}... | collective-permute-start | bytes 98312 | tf_op jit(solution)/shard_map/ppermute | solution.py:445
  28.4 1.9 %collective-permute-done.10.got_ref = bf16[128,128]{1,0:T(8,128)(2,1)S(1)} collective-permute-done((bf16[128,128]{1,0:T(8,128)(2,1)S(1)}, bf16[128,128]{1,0:T(8,128)(2,1)S(1)}, u32[]{:S(2)}, u32[]{:S(2)}) %collective-permute-start.10) | collective-permute-done | bytes 32800 | tf_op jit(solution)/shard_map/ppermute | solution.py:445
  30.3 0.7 %total.1 = f32[32,4,128]{2,1,0:T(4,128)} custom-call(f32[4,32,128]{2,1,0:T(8,128)S(1)} %get-tuple-element.45.keep_ref, bf16[128,128]{1,0:T(8,128)(2,1)S(1)} %collective-permute-done.10.got_ref), custom_call_target="tpu_custom_call" | custom-call | tf_op jit(solution)/shard_map/total/pallas_call | solution.py:446
  (4 shorter events, 0.1 us)
Async XLA Ops:
  0.0 7.1 %copy-start.1 = (f32[16]{0:T(128)S(1)}, f32[16]{0:T(128)}, u32[]{:S(2)}) copy-start(f32[16]{0:T(128)} %param.6) | copy-start | bytes 196
  1.4 5.7 %copy-start = (s32[1,8,128]{2,1,0:T(8,128)S(1)}, s32[1,8,128]{2,1,0:T(8,128)}, u32[]{:S(2)}) copy-start(s32[1,8,128]{2,1,0:T(8,128)} %ids_ref.1) | copy-start | bytes 12292
  1.4 5.7 %collective-permute-start = (bf16[8,3,128,128]{3,2,1,0:T(8,128)(2,1)S(1)}, bf16[8,3,128,128]{3,2,1,0:T(8,128)(2,1)S(1)}, u32[]{:S(2)}, u32[]{:S(2)}) collective-permute-start(bf16[8,3,128,128]{3,2,1,0:T(8,128)(2,1)S(1)} %get-tuple-element.26.tr.own_ref), channel_id=1, source_target_pairs={{0,1},{1,0},{2,3},{3,2},{4,5},{5,4},{6,7},{7,6},{8,9},{9,8},{10,11... | collective-permute-start | bytes 2359304 | tf_op jit(solution)/shard_map/ppermute | solution.py:331
  1.9 11.4 %collective-permute-start.1 = (bf16[784,128]{1,0:T(8,128)(2,1)S(1)}, bf16[784,128]{1,0:T(8,128)(2,1)S(1)}, u32[]{:S(2)}, u32[]{:S(2)}) collective-permute-start(bf16[784,128]{1,0:T(8,128)(2,1)S(1)} %get-tuple-element.27), channel_id=1, source_target_pairs={{0,2},{1,3},{2,0},{3,1},{4,6},{5,7},{6,4},{7,5},{8,10},{9,11},{10,... | collective-permute-start | bytes 602120 | tf_op jit(solution)/shard_map/ppermute | solution.py:332
  4.5 8.9 %collective-permute-start.2 = (bf16[784,128]{1,0:T(8,128)(2,1)S(1)}, bf16[784,128]{1,0:T(8,128)(2,1)S(1)}, u32[]{:S(2)}, u32[]{:S(2)}) collective-permute-start(bf16[784,128]{1,0:T(8,128)(2,1)S(1)} %get-tuple-element.28), channel_id=1, source_target_pairs={{0,12},{1,13},{2,6},{3,7},{4,0},{5,1},{6,10},{7,11},{8,4},{9,5},{1... | collective-permute-start | bytes 602120 | tf_op jit(solution)/shard_map/ppermute | solution.py:333
  7.2 7.3 %collective-permute-start.3 = (bf16[784,128]{1,0:T(8,128)(2,1)S(1)}, bf16[784,128]{1,0:T(8,128)(2,1)S(1)}, u32[]{:S(2)}, u32[]{:S(2)}) collective-permute-start(bf16[784,128]{1,0:T(8,128)(2,1)S(1)} %get-tuple-element.29), channel_id=1, source_target_pairs={{0,3},{1,2},{2,1},{3,0},{4,7},{5,6},{6,5},{7,4},{8,11},{9,10},{10,... | collective-permute-start | bytes 602120 | tf_op jit(solution)/shard_map/ppermute | solution.py:343
  7.3 8.6 %collective-permute-start.4 = (bf16[784,128]{1,0:T(8,128)(2,1)S(1)}, bf16[784,128]{1,0:T(8,128)(2,1)S(1)}, u32[]{:S(2)}, u32[]{:S(2)}) collective-permute-start(bf16[784,128]{1,0:T(8,128)(2,1)S(1)} %get-tuple-element.30), channel_id=1, source_target_pairs={{0,13},{1,12},{2,7},{3,6},{4,1},{5,0},{6,11},{7,10},{8,5},{9,4},{1... | collective-permute-start | bytes 602120 | tf_op jit(solution)/shard_map/ppermute | solution.py:344
  16.6 1.4 %collective-permute-start.6 = (bf16[512,128]{1,0:T(8,128)(2,1)S(1)}, bf16[512,128]{1,0:T(8,128)(2,1)S(1)}, u32[]{:S(2)}, u32[]{:S(2)}) collective-permute-start(bf16[512,128]{1,0:T(8,128)(2,1)S(1)} %get-tuple-element.41), channel_id=1, source_target_pairs={{0,1},{1,0},{2,3},{3,2},{4,5},{5,4},{6,7},{7,6},{8,9},{9,8},{10,11... | collective-permute-start | bytes 393224 | tf_op jit(solution)/shard_map/ppermute | solution.py:411
  17.3 3.2 %collective-permute-start.5 = (bf16[512,128]{1,0:T(8,128)(2,1)S(1)}, bf16[512,128]{1,0:T(8,128)(2,1)S(1)}, u32[]{:S(2)}, u32[]{:S(2)}) collective-permute-start(bf16[512,128]{1,0:T(8,128)(2,1)S(1)} %get-tuple-element.38), channel_id=1, source_target_pairs={{0,1},{1,0},{2,3},{3,2},{4,5},{5,4},{6,7},{7,6},{8,9},{9,8},{10,11... | collective-permute-start | bytes 393224 | tf_op jit(solution)/shard_map/ppermute | solution.py:413
  18.1 5.3 %collective-permute-start.7 = (bf16[256,128]{1,0:T(8,128)(2,1)S(1)}, bf16[256,128]{1,0:T(8,128)(2,1)S(1)}, u32[]{:S(2)}, u32[]{:S(2)}) collective-permute-start(bf16[256,128]{1,0:T(8,128)(2,1)S(1)} %get-tuple-element.42), channel_id=1, source_target_pairs={{0,6},{2,4},{4,2},{6,0},{8,10},{10,8},{12,14},{14,12},{1,7},{3,5},... | collective-permute-start | bytes 196616 | tf_op jit(solution)/shard_map/ppermute | solution.py:431
  19.7 4.8 %collective-permute-start.8 = (bf16[256,128]{1,0:T(8,128)(2,1)S(1)}, bf16[256,128]{1,0:T(8,128)(2,1)S(1)}, u32[]{:S(2)}, u32[]{:S(2)}) collective-permute-start(bf16[256,128]{1,0:T(8,128)(2,1)S(1)} %get-tuple-element.43), channel_id=1, source_target_pairs={{0,2},{2,0},{4,6},{6,4},{8,12},{10,14},{12,8},{14,10},{1,3},{3,1},... | collective-permute-start | bytes 196616 | tf_op jit(solution)/shard_map/ppermute | solution.py:431
  20.6 4.6 %collective-permute-start.9 = (bf16[256,128]{1,0:T(8,128)(2,1)S(1)}, bf16[256,128]{1,0:T(8,128)(2,1)S(1)}, u32[]{:S(2)}, u32[]{:S(2)}) collective-permute-start(bf16[256,128]{1,0:T(8,128)(2,1)S(1)} %get-tuple-element.44), channel_id=1, source_target_pairs={{0,4},{2,6},{4,0},{6,2},{8,14},{10,12},{12,10},{14,8},{1,5},{3,7},... | collective-permute-start | bytes 196616 | tf_op jit(solution)/shard_map/ppermute | solution.py:431
  25.2 5.1 %collective-permute-start.10 = (bf16[128,128]{1,0:T(8,128)(2,1)S(1)}, bf16[128,128]{1,0:T(8,128)(2,1)S(1)}, u32[]{:S(2)}, u32[]{:S(2)}) collective-permute-start(bf16[128,128]{1,0:T(8,128)(2,1)S(1)} %get-tuple-element.46), channel_id=1, source_target_pairs={{0,8},{2,10},{4,12},{6,14},{8,0},{10,2},{12,4},{14,6},{1,9},{3,11}... | collective-permute-start | bytes 98312 | tf_op jit(solution)/shard_map/ppermute | solution.py:445

commit v28 on v26

--- a/solution.py
+++ b/solution.py
@@ -10,7 +10,7 @@
 JB = 4
 NW = 16
 PADROWS = 16
-LOADS = 4
+LOADS = 8
 X_FIRST = 0b10011111
 NEAR = 4
 VMEM_LIMIT = 48 * 1024 * 1024

time: 31.1 us -> 31.1 us (level)
  no operation moved by 1% of the time
where the time goes in v28:
time: 31.1 us; the launch traced here: 30.9 us
  starting transfers between devices  16.1 us (52%)
  waiting for transfers between devices  7.28 us (23%)
  Pallas kernels  6.77 us (22%)
  between operations  0.76 us (2%)
    ppermute x3, starting transfers between devices, on_device(): lax.ppermute(out, 'space', [(s, s ^ steps[s // NEAR]) for s in range(n)])  3.62 us
    ppermute x3, waiting for transfers between devices, on_device(): lax.ppermute(out, 'space', [(s, s ^ steps[s // NEAR]) for s in range(n)])  3.42 us
    ppermute x1, starting transfers between devices, on_device(): got = lax.ppermute(send, 'space', [(s, s ^ NEAR) for s in range(n)])  3.2 us
    ppermute x1, starting transfers between devices, on_device(): zc = lax.ppermute(zc, both, cross([(s, z_to(s) % n) for s in range(n)]))  2.94 us
    ppermute x1, starting transfers between devices, on_device(): second = lax.ppermute(second, both, same(seconds))  2.6 us
    ppermute x1, starting transfers between devices, on_device(): first = lax.ppermute(first, both, same(firsts))  2.53 us
    pallas_call x1, Pallas kernels, on_device(): pl.pallas_call(local_kernel, out_shape=[jax.ShapeDtypeStruct((JB * 2 * nk...  2.43 us
    ppermute x1, waiting for transfers between devices, on_device(): got = lax.ppermute(send, 'space', [(s, s ^ NEAR) for s in range(n)])  1.89 us
  transfers between devices with their start and end apart: 11, of which 7 were waited for; matrix products, arithmetic and copies ran while one was open for 0% of the time, Pallas kernels for 13%

profile of v28, /device:TPU:0, one launch (start us, length us, event | category | flops | bytes accessed | tf_op | source)
XLA Modules:
  0.0 30.9 jit_solution(3225755113636631815)
XLA Ops:
  0.0 0.0 copy-start.1
  0.0 1.4 %prep.1 = (bf16[8,3,128,128]{3,2,1,0:T(8,128)(2,1)S(1)}, bf16[784,128]{1,0:T(8,128)(2,1)S(1)}, bf16[784,128]{1,0:T(8,128)(2,1)S(1)}) custom-call(bf16[128,3,1,8,128]{4,3,2,1,0:T(8,128)(2,1)} %modes_hbm.1), custom_call_target="tpu_custom_call" | custom-call | flops 1500000000 | bytes 2800000 | tf_op jit(solution)/shard_map/prep/pallas_call | solution.py:314
  1.4 0.0 copy-start
  1.4 0.5 %collective-permute-start = (bf16[8,3,128,128]{3,2,1,0:T(8,128)(2,1)S(1)}, bf16[8,3,128,128]{3,2,1,0:T(8,128)(2,1)S(1)}, u32[]{:S(2)}, u32[]{:S(2)}) collective-permute-start(bf16[8,3,128,128]{3,2,1,0:T(8,128)(2,1)S(1)} %get-tuple-element.26.tr.own_ref), channel_id=1, source_target_pairs={{0,1},{1,0},{2,3},{3,2},{4,5},{5,4},{6,7},{7,6},{8,9},{9,8},{10,11... | collective-permute-start | bytes 2359304 | tf_op jit(solution)/shard_map/ppermute | solution.py:334
  1.9 2.5 %collective-permute-start.1 = (bf16[784,128]{1,0:T(8,128)(2,1)S(1)}, bf16[784,128]{1,0:T(8,128)(2,1)S(1)}, u32[]{:S(2)}, u32[]{:S(2)}) collective-permute-start(bf16[784,128]{1,0:T(8,128)(2,1)S(1)} %get-tuple-element.27), channel_id=1, source_target_pairs={{0,2},{1,3},{2,0},{3,1},{4,6},{5,7},{6,4},{7,5},{8,10},{9,11},{10,... | collective-permute-start | bytes 602120 | tf_op jit(solution)/shard_map/ppermute | solution.py:335
  4.4 2.6 %collective-permute-start.2 = (bf16[784,128]{1,0:T(8,128)(2,1)S(1)}, bf16[784,128]{1,0:T(8,128)(2,1)S(1)}, u32[]{:S(2)}, u32[]{:S(2)}) collective-permute-start(bf16[784,128]{1,0:T(8,128)(2,1)S(1)} %get-tuple-element.28), channel_id=1, source_target_pairs={{0,12},{1,13},{2,6},{3,7},{4,0},{5,1},{6,10},{7,11},{8,4},{9,5},{1... | collective-permute-start | bytes 602120 | tf_op jit(solution)/shard_map/ppermute | solution.py:336
  7.0 0.0 collective-permute-done._.other_ref
  7.0 0.0 copy-done.1
  7.1 0.0 copy-done
  7.1 0.1 weights.1
  7.2 0.1 collective-permute-start.3
  7.3 2.9 %collective-permute-start.4 = (bf16[784,128]{1,0:T(8,128)(2,1)S(1)}, bf16[784,128]{1,0:T(8,128)(2,1)S(1)}, u32[]{:S(2)}, u32[]{:S(2)}) collective-permute-start(bf16[784,128]{1,0:T(8,128)(2,1)S(1)} %get-tuple-element.30), channel_id=1, source_target_pairs={{0,13},{1,12},{2,7},{3,6},{4,1},{5,0},{6,11},{7,10},{8,5},{9,4},{1... | collective-permute-start | bytes 602120 | tf_op jit(solution)/shard_map/ppermute | solution.py:347
  10.9 2.4 %local.1 = (f32[1024,256]{1,0:T(8,128)S(1)}, bf16[2,256,384]{2,1,0:T(8,128)(2,1)S(1)}) custom-call(bf16[8,3,128,128]{3,2,1,0:T(8,128)(2,1)S(1)} %get-tuple-element.26.tr.own_ref, bf16[8,3,128,128]{3,2,1,0:T(8,128)(2,1)S(1)} %collective-permute-done._.other_ref, f32[8,128]{1,0:T(8,128)S(1)} %get-tuple-element.31.weight_ref, s32[1]{0:T(128)S(6)} %copy.5.jb_ref.refs_5_), custom_call_target="tpu_custom_call" | custom-call | flops 900000000 | bytes 2400000 | tf_op jit(solution)/shard_map/local/pallas_call | solution.py:351
  13.3 0.0 collective-permute-done.1.first_ref.refs_0_
  13.3 0.0 collective-permute-done.2.second_ref.refs_1_
  13.3 1.2 %collective-permute-done.3.xc_ref.refs_2_ = bf16[784,128]{1,0:T(8,128)(2,1)S(1)} collective-permute-done((bf16[784,128]{1,0:T(8,128)(2,1)S(1)}, bf16[784,128]{1,0:T(8,128)(2,1)S(1)}, u32[]{:S(2)}, u32[]{:S(2)}) %collective-permute-start.3) | collective-permute-done | bytes 200736 | tf_op jit(solution)/shard_map/ppermute | solution.py:346
  14.5 0.8 %early.1 = (f32[1024,256]{1,0:T(8,128)S(1)}, bf16[256,768]{1,0:T(8,128)(2,1)S(1)}) custom-call(bf16[8,3,128,128]{3,2,1,0:T(8,128)(2,1)S(1)} %get-tuple-element.26.tr.own_ref, bf16[8,3,128,128]{3,2,1,0:T(8,128)(2,1)S(1)} %collective-permute-done._.other_ref, bf16[784,128]{1,0:T(8,128)(2,1)S(1)} %collective-permute-done.1.first_ref.refs_0_, ...), custom_call_target="tpu_custom_call" | custom-call | flops 600000000 | bytes 2400000 | tf_op jit(solution)/shard_map/early/pallas_call | solution.py:368
  15.3 0.7 %collective-permute-done.4.refs_3_ = bf16[784,128]{1,0:T(8,128)(2,1)S(1)} collective-permute-done((bf16[784,128]{1,0:T(8,128)(2,1)S(1)}, bf16[784,128]{1,0:T(8,128)(2,1)S(1)}, u32[]{:S(2)}, u32[]{:S(2)}) %collective-permute-start.4) | collective-permute-done | bytes 200736 | tf_op jit(solution)/shard_map/ppermute | solution.py:347
  15.9 0.7 %cross.2 = (f32[2,2,4,32,128]{4,3,2,1,0:T(8,128)S(1)}, bf16[512,128]{1,0:T(8,128)(2,1)S(1)}, bf16[256,1536]{1,0:T(8,128)(2,1)S(1)}) custom-call(bf16[8,3,128,128]{3,2,1,0:T(8,128)(2,1)S(1)} %get-tuple-element.26.tr.own_ref, bf16[8,3,128,128]{3,2,1,0:T(8,128)(2,1)S(1)} %collective-permute-done._.other_ref, ...), custom_call_target="tpu_custom_call" | custom-call | flops 900000000 | bytes 4000000 | tf_op jit(solution)/shard_map/cross/pallas_call | solution.py:393
  16.6 0.1 collective-permute-start.6
  16.7 0.6 %cross.3 = (f32[2,2,4,32,128]{4,3,2,1,0:T(8,128)S(1)}, bf16[512,128]{1,0:T(8,128)(2,1)S(1)}) custom-call(bf16[8,3,128,128]{3,2,1,0:T(8,128)(2,1)S(1)} %get-tuple-element.26.tr.own_ref, bf16[8,3,128,128]{3,2,1,0:T(8,128)(2,1)S(1)} %collective-permute-done._.other_ref, bf16[784,128]{1,0:T(8,128)(2,1)S(1)} %collective-permute-done.1.first_ref.refs_0_, ...), custom_call_target="tpu_custom_call" | custom-call | flops 900000000 | bytes 4000000 | tf_op jit(solution)/shard_map/cross/pallas_call | solution.py:393
  17.3 0.6 %collective-permute-start.5 = (bf16[512,128]{1,0:T(8,128)(2,1)S(1)}, bf16[512,128]{1,0:T(8,128)(2,1)S(1)}, u32[]{:S(2)}, u32[]{:S(2)}) collective-permute-start(bf16[512,128]{1,0:T(8,128)(2,1)S(1)} %get-tuple-element.38), channel_id=1, source_target_pairs={{0,1},{1,0},{2,3},{3,2},{4,5},{5,4},{6,7},{7,6},{8,9},{9,8},{10,11... | collective-permute-start | bytes 393224 | tf_op jit(solution)/shard_map/ppermute | solution.py:414
  17.9 0.1 collective-permute-done.6.got_ref
  18.1 1.7 %collective-permute-start.7 = (bf16[256,128]{1,0:T(8,128)(2,1)S(1)}, bf16[256,128]{1,0:T(8,128)(2,1)S(1)}, u32[]{:S(2)}, u32[]{:S(2)}) collective-permute-start(bf16[256,128]{1,0:T(8,128)(2,1)S(1)} %get-tuple-element.42), channel_id=1, source_target_pairs={{0,6},{2,4},{4,2},{6,0},{8,10},{10,8},{12,14},{14,12},{1,7},{3,5},... | collective-permute-start | bytes 196616 | tf_op jit(solution)/shard_map/ppermute | solution.py:432
  19.7 0.8 %collective-permute-start.8 = (bf16[256,128]{1,0:T(8,128)(2,1)S(1)}, bf16[256,128]{1,0:T(8,128)(2,1)S(1)}, u32[]{:S(2)}, u32[]{:S(2)}) collective-permute-start(bf16[256,128]{1,0:T(8,128)(2,1)S(1)} %get-tuple-element.43), channel_id=1, source_target_pairs={{0,2},{2,0},{4,6},{6,4},{8,14},{10,12},{12,10},{14,8},{1,3},{3,1},... | collective-permute-start | bytes 196616 | tf_op jit(solution)/shard_map/ppermute | solution.py:432
  20.5 0.0 collective-permute-done.5.got_ref
  20.6 1.1 %collective-permute-start.9 = (bf16[256,128]{1,0:T(8,128)(2,1)S(1)}, bf16[256,128]{1,0:T(8,128)(2,1)S(1)}, u32[]{:S(2)}, u32[]{:S(2)}) collective-permute-start(bf16[256,128]{1,0:T(8,128)(2,1)S(1)} %get-tuple-element.44), channel_id=1, source_target_pairs={{0,4},{2,6},{4,0},{6,2},{8,12},{10,14},{12,8},{14,10},{1,5},{3,7},... | collective-permute-start | bytes 196616 | tf_op jit(solution)/shard_map/ppermute | solution.py:432
  21.7 1.6 %collective-permute-done.7.refs_0_ = bf16[256,128]{1,0:T(8,128)(2,1)S(1)} collective-permute-done((bf16[256,128]{1,0:T(8,128)(2,1)S(1)}, bf16[256,128]{1,0:T(8,128)(2,1)S(1)}, u32[]{:S(2)}, u32[]{:S(2)}) %collective-permute-start.7) | collective-permute-done | bytes 65568 | tf_op jit(solution)/shard_map/ppermute | solution.py:432
  23.3 1.2 %collective-permute-done.8.refs_1_ = bf16[256,128]{1,0:T(8,128)(2,1)S(1)} collective-permute-done((bf16[256,128]{1,0:T(8,128)(2,1)S(1)}, bf16[256,128]{1,0:T(8,128)(2,1)S(1)}, u32[]{:S(2)}, u32[]{:S(2)}) %collective-permute-start.8) | collective-permute-done | bytes 65568 | tf_op jit(solution)/shard_map/ppermute | solution.py:432
  24.6 0.6 %collective-permute-done.9.refs_2_ = bf16[256,128]{1,0:T(8,128)(2,1)S(1)} collective-permute-done((bf16[256,128]{1,0:T(8,128)(2,1)S(1)}, bf16[256,128]{1,0:T(8,128)(2,1)S(1)}, u32[]{:S(2)}, u32[]{:S(2)}) %collective-permute-start.9) | collective-permute-done | bytes 65568 | tf_op jit(solution)/shard_map/ppermute | solution.py:432
  25.2 3.2 %collective-permute-start.10 = (bf16[128,128]{1,0:T(8,128)(2,1)S(1)}, bf16[128,128]{1,0:T(8,128)(2,1)S(1)}, u32[]{:S(2)}, u32[]{:S(2)}) collective-permute-start(bf16[128,128]{1,0:T(8,128)(2,1)S(1)} %get-tuple-element.46), channel_id=1, source_target_pairs={{0,8},{2,10},{4,12},{6,14},{8,0},{10,2},{12,4},{14,6},{1,9},{3,11}... | collective-permute-start | bytes 98312 | tf_op jit(solution)/shard_map/ppermute | solution.py:446
  28.4 1.9 %collective-permute-done.10.got_ref = bf16[128,128]{1,0:T(8,128)(2,1)S(1)} collective-permute-done((bf16[128,128]{1,0:T(8,128)(2,1)S(1)}, bf16[128,128]{1,0:T(8,128)(2,1)S(1)}, u32[]{:S(2)}, u32[]{:S(2)}) %collective-permute-start.10) | collective-permute-done | bytes 32800 | tf_op jit(solution)/shard_map/ppermute | solution.py:446
  30.3 0.7 %total.1 = f32[32,4,128]{2,1,0:T(4,128)} custom-call(f32[4,32,128]{2,1,0:T(8,128)S(1)} %get-tuple-element.45.keep_ref, bf16[128,128]{1,0:T(8,128)(2,1)S(1)} %collective-permute-done.10.got_ref), custom_call_target="tpu_custom_call" | custom-call | tf_op jit(solution)/shard_map/total/pallas_call | solution.py:447
  (4 shorter events, 0.1 us)
Async XLA Ops:
  0.0 7.0 %copy-start.1 = (f32[16]{0:T(128)S(1)}, f32[16]{0:T(128)}, u32[]{:S(2)}) copy-start(f32[16]{0:T(128)} %param.6) | copy-start | bytes 196
  1.4 5.7 %copy-start = (s32[1,8,128]{2,1,0:T(8,128)S(1)}, s32[1,8,128]{2,1,0:T(8,128)}, u32[]{:S(2)}) copy-start(s32[1,8,128]{2,1,0:T(8,128)} %ids_ref.1) | copy-start | bytes 12292
  1.4 5.7 %collective-permute-start = (bf16[8,3,128,128]{3,2,1,0:T(8,128)(2,1)S(1)}, bf16[8,3,128,128]{3,2,1,0:T(8,128)(2,1)S(1)}, u32[]{:S(2)}, u32[]{:S(2)}) collective-permute-start(bf16[8,3,128,128]{3,2,1,0:T(8,128)(2,1)S(1)} %get-tuple-element.26.tr.own_ref), channel_id=1, source_target_pairs={{0,1},{1,0},{2,3},{3,2},{4,5},{5,4},{6,7},{7,6},{8,9},{9,8},{10,11... | collective-permute-start | bytes 2359304 | tf_op jit(solution)/shard_map/ppermute | solution.py:334
  1.9 11.4 %collective-permute-start.1 = (bf16[784,128]{1,0:T(8,128)(2,1)S(1)}, bf16[784,128]{1,0:T(8,128)(2,1)S(1)}, u32[]{:S(2)}, u32[]{:S(2)}) collective-permute-start(bf16[784,128]{1,0:T(8,128)(2,1)S(1)} %get-tuple-element.27), channel_id=1, source_target_pairs={{0,2},{1,3},{2,0},{3,1},{4,6},{5,7},{6,4},{7,5},{8,10},{9,11},{10,... | collective-permute-start | bytes 602120 | tf_op jit(solution)/shard_map/ppermute | solution.py:335
  4.4 8.9 %collective-permute-start.2 = (bf16[784,128]{1,0:T(8,128)(2,1)S(1)}, bf16[784,128]{1,0:T(8,128)(2,1)S(1)}, u32[]{:S(2)}, u32[]{:S(2)}) collective-permute-start(bf16[784,128]{1,0:T(8,128)(2,1)S(1)} %get-tuple-element.28), channel_id=1, source_target_pairs={{0,12},{1,13},{2,6},{3,7},{4,0},{5,1},{6,10},{7,11},{8,4},{9,5},{1... | collective-permute-start | bytes 602120 | tf_op jit(solution)/shard_map/ppermute | solution.py:336
  7.2 7.3 %collective-permute-start.3 = (bf16[784,128]{1,0:T(8,128)(2,1)S(1)}, bf16[784,128]{1,0:T(8,128)(2,1)S(1)}, u32[]{:S(2)}, u32[]{:S(2)}) collective-permute-start(bf16[784,128]{1,0:T(8,128)(2,1)S(1)} %get-tuple-element.29), channel_id=1, source_target_pairs={{0,3},{1,2},{2,1},{3,0},{4,7},{5,6},{6,5},{7,4},{8,11},{9,10},{10,... | collective-permute-start | bytes 602120 | tf_op jit(solution)/shard_map/ppermute | solution.py:346
  7.3 8.6 %collective-permute-start.4 = (bf16[784,128]{1,0:T(8,128)(2,1)S(1)}, bf16[784,128]{1,0:T(8,128)(2,1)S(1)}, u32[]{:S(2)}, u32[]{:S(2)}) collective-permute-start(bf16[784,128]{1,0:T(8,128)(2,1)S(1)} %get-tuple-element.30), channel_id=1, source_target_pairs={{0,13},{1,12},{2,7},{3,6},{4,1},{5,0},{6,11},{7,10},{8,5},{9,4},{1... | collective-permute-start | bytes 602120 | tf_op jit(solution)/shard_map/ppermute | solution.py:347
  16.6 1.4 %collective-permute-start.6 = (bf16[512,128]{1,0:T(8,128)(2,1)S(1)}, bf16[512,128]{1,0:T(8,128)(2,1)S(1)}, u32[]{:S(2)}, u32[]{:S(2)}) collective-permute-start(bf16[512,128]{1,0:T(8,128)(2,1)S(1)} %get-tuple-element.41), channel_id=1, source_target_pairs={{0,1},{1,0},{2,3},{3,2},{4,5},{5,4},{6,7},{7,6},{8,9},{9,8},{10,11... | collective-permute-start | bytes 393224 | tf_op jit(solution)/shard_map/ppermute | solution.py:412
  17.3 3.2 %collective-permute-start.5 = (bf16[512,128]{1,0:T(8,128)(2,1)S(1)}, bf16[512,128]{1,0:T(8,128)(2,1)S(1)}, u32[]{:S(2)}, u32[]{:S(2)}) collective-permute-start(bf16[512,128]{1,0:T(8,128)(2,1)S(1)} %get-tuple-element.38), channel_id=1, source_target_pairs={{0,1},{1,0},{2,3},{3,2},{4,5},{5,4},{6,7},{7,6},{8,9},{9,8},{10,11... | collective-permute-start | bytes 393224 | tf_op jit(solution)/shard_map/ppermute | solution.py:414
  18.1 5.3 %collective-permute-start.7 = (bf16[256,128]{1,0:T(8,128)(2,1)S(1)}, bf16[256,128]{1,0:T(8,128)(2,1)S(1)}, u32[]{:S(2)}, u32[]{:S(2)}) collective-permute-start(bf16[256,128]{1,0:T(8,128)(2,1)S(1)} %get-tuple-element.42), channel_id=1, source_target_pairs={{0,6},{2,4},{4,2},{6,0},{8,10},{10,8},{12,14},{14,12},{1,7},{3,5},... | collective-permute-start | bytes 196616 | tf_op jit(solution)/shard_map/ppermute | solution.py:432
  19.7 4.8 %collective-permute-start.8 = (bf16[256,128]{1,0:T(8,128)(2,1)S(1)}, bf16[256,128]{1,0:T(8,128)(2,1)S(1)}, u32[]{:S(2)}, u32[]{:S(2)}) collective-permute-start(bf16[256,128]{1,0:T(8,128)(2,1)S(1)} %get-tuple-element.43), channel_id=1, source_target_pairs={{0,2},{2,0},{4,6},{6,4},{8,14},{10,12},{12,10},{14,8},{1,3},{3,1},... | collective-permute-start | bytes 196616 | tf_op jit(solution)/shard_map/ppermute | solution.py:432
  20.6 4.6 %collective-permute-start.9 = (bf16[256,128]{1,0:T(8,128)(2,1)S(1)}, bf16[256,128]{1,0:T(8,128)(2,1)S(1)}, u32[]{:S(2)}, u32[]{:S(2)}) collective-permute-start(bf16[256,128]{1,0:T(8,128)(2,1)S(1)} %get-tuple-element.44), channel_id=1, source_target_pairs={{0,4},{2,6},{4,0},{6,2},{8,12},{10,14},{12,8},{14,10},{1,5},{3,7},... | collective-permute-start | bytes 196616 | tf_op jit(solution)/shard_map/ppermute | solution.py:432
  25.2 5.1 %collective-permute-start.10 = (bf16[128,128]{1,0:T(8,128)(2,1)S(1)}, bf16[128,128]{1,0:T(8,128)(2,1)S(1)}, u32[]{:S(2)}, u32[]{:S(2)}) collective-permute-start(bf16[128,128]{1,0:T(8,128)(2,1)S(1)} %get-tuple-element.46), channel_id=1, source_target_pairs={{0,8},{2,10},{4,12},{6,14},{8,0},{10,2},{12,4},{14,6},{1,9},{3,11}... | collective-permute-start | bytes 98312 | tf_op jit(solution)/shard_map/ppermute | solution.py:446

commit v29 on v28

--- a/solution.py
+++ b/solution.py
@@ -10,7 +10,7 @@
 JB = 4
 NW = 16
 PADROWS = 16
-LOADS = 8
+LOADS = 2
 X_FIRST = 0b10011111
 NEAR = 4
 VMEM_LIMIT = 48 * 1024 * 1024

time: 31.1 us -> 31.1 us (level)
  no operation moved by 1% of the time
where the time goes in v29:
time: 31.1 us; the launch traced here: 31 us
  starting transfers between devices  16.1 us (52%)
  waiting for transfers between devices  7.28 us (23%)
  Pallas kernels  6.83 us (22%)
  between operations  0.76 us (2%)
    ppermute x3, starting transfers between devices, on_device(): lax.ppermute(out, 'space', [(s, s ^ steps[s // NEAR]) for s in range(n)])  3.62 us
    ppermute x3, waiting for transfers between devices, on_device(): lax.ppermute(out, 'space', [(s, s ^ steps[s // NEAR]) for s in range(n)])  3.42 us
    ppermute x1, starting transfers between devices, on_device(): got = lax.ppermute(send, 'space', [(s, s ^ NEAR) for s in range(n)])  3.2 us
    ppermute x1, starting transfers between devices, on_device(): zc = lax.ppermute(zc, both, cross([(s, z_to(s) % n) for s in range(n)]))  2.94 us
    ppermute x1, starting transfers between devices, on_device(): second = lax.ppermute(second, both, same(seconds))  2.6 us
    ppermute x1, starting transfers between devices, on_device(): first = lax.ppermute(first, both, same(firsts))  2.53 us
    pallas_call x1, Pallas kernels, on_device(): pl.pallas_call(local_kernel, out_shape=[jax.ShapeDtypeStruct((JB * 2 * nk...  2.43 us
    ppermute x1, waiting for transfers between devices, on_device(): got = lax.ppermute(send, 'space', [(s, s ^ NEAR) for s in range(n)])  1.89 us
  transfers between devices with their start and end apart: 11, of which 7 were waited for; matrix products, arithmetic and copies ran while one was open for 0% of the time, Pallas kernels for 13%

profile of v29, /device:TPU:0, one launch (start us, length us, event | category | flops | bytes accessed | tf_op | source)
XLA Modules:
  0.0 31.0 jit_solution(6868323454730516993)
XLA Ops:
  0.0 0.0 copy-start.1
  0.0 1.4 %prep.1 = (bf16[8,3,128,128]{3,2,1,0:T(8,128)(2,1)S(1)}, bf16[784,128]{1,0:T(8,128)(2,1)S(1)}, bf16[784,128]{1,0:T(8,128)(2,1)S(1)}) custom-call(bf16[128,3,1,8,128]{4,3,2,1,0:T(8,128)(2,1)} %modes_hbm.1), custom_call_target="tpu_custom_call" | custom-call | flops 1500000000 | bytes 2800000 | tf_op jit(solution)/shard_map/prep/pallas_call | solution.py:314
  1.4 0.0 copy-start
  1.4 0.5 %collective-permute-start = (bf16[8,3,128,128]{3,2,1,0:T(8,128)(2,1)S(1)}, bf16[8,3,128,128]{3,2,1,0:T(8,128)(2,1)S(1)}, u32[]{:S(2)}, u32[]{:S(2)}) collective-permute-start(bf16[8,3,128,128]{3,2,1,0:T(8,128)(2,1)S(1)} %get-tuple-element.26.tr.own_ref), channel_id=1, source_target_pairs={{0,1},{1,0},{2,3},{3,2},{4,5},{5,4},{6,7},{7,6},{8,9},{9,8},{10,11... | collective-permute-start | bytes 2359304 | tf_op jit(solution)/shard_map/ppermute | solution.py:334
  2.0 2.5 %collective-permute-start.1 = (bf16[784,128]{1,0:T(8,128)(2,1)S(1)}, bf16[784,128]{1,0:T(8,128)(2,1)S(1)}, u32[]{:S(2)}, u32[]{:S(2)}) collective-permute-start(bf16[784,128]{1,0:T(8,128)(2,1)S(1)} %get-tuple-element.27), channel_id=1, source_target_pairs={{0,2},{1,3},{2,0},{3,1},{4,6},{5,7},{6,4},{7,5},{8,10},{9,11},{10,... | collective-permute-start | bytes 602120 | tf_op jit(solution)/shard_map/ppermute | solution.py:335
  4.5 2.6 %collective-permute-start.2 = (bf16[784,128]{1,0:T(8,128)(2,1)S(1)}, bf16[784,128]{1,0:T(8,128)(2,1)S(1)}, u32[]{:S(2)}, u32[]{:S(2)}) collective-permute-start(bf16[784,128]{1,0:T(8,128)(2,1)S(1)} %get-tuple-element.28), channel_id=1, source_target_pairs={{0,12},{1,13},{2,6},{3,7},{4,0},{5,1},{6,10},{7,11},{8,4},{9,5},{1... | collective-permute-start | bytes 602120 | tf_op jit(solution)/shard_map/ppermute | solution.py:336
  7.1 0.0 collective-permute-done._.other_ref
  7.1 0.0 copy-done.1
  7.1 0.0 copy-done
  7.1 0.1 weights.1
  7.2 0.1 collective-permute-start.3
  7.3 2.9 %collective-permute-start.4 = (bf16[784,128]{1,0:T(8,128)(2,1)S(1)}, bf16[784,128]{1,0:T(8,128)(2,1)S(1)}, u32[]{:S(2)}, u32[]{:S(2)}) collective-permute-start(bf16[784,128]{1,0:T(8,128)(2,1)S(1)} %get-tuple-element.30), channel_id=1, source_target_pairs={{0,13},{1,12},{2,7},{3,6},{4,1},{5,0},{6,11},{7,10},{8,5},{9,4},{1... | collective-permute-start | bytes 602120 | tf_op jit(solution)/shard_map/ppermute | solution.py:347
  10.9 2.4 %local.1 = (f32[1024,256]{1,0:T(8,128)S(1)}, bf16[2,256,384]{2,1,0:T(8,128)(2,1)S(1)}) custom-call(bf16[8,3,128,128]{3,2,1,0:T(8,128)(2,1)S(1)} %get-tuple-element.26.tr.own_ref, bf16[8,3,128,128]{3,2,1,0:T(8,128)(2,1)S(1)} %collective-permute-done._.other_ref, f32[8,128]{1,0:T(8,128)S(1)} %get-tuple-element.31.weight_ref, s32[1]{0:T(128)S(6)} %copy.5.jb_ref.refs_5_), custom_call_target="tpu_custom_call" | custom-call | flops 900000000 | bytes 2400000 | tf_op jit(solution)/shard_map/local/pallas_call | solution.py:351
  13.3 0.0 collective-permute-done.1.first_ref.refs_0_
  13.4 0.0 collective-permute-done.2.second_ref.refs_1_
  13.4 1.2 %collective-permute-done.3.xc_ref.refs_2_ = bf16[784,128]{1,0:T(8,128)(2,1)S(1)} collective-permute-done((bf16[784,128]{1,0:T(8,128)(2,1)S(1)}, bf16[784,128]{1,0:T(8,128)(2,1)S(1)}, u32[]{:S(2)}, u32[]{:S(2)}) %collective-permute-start.3) | collective-permute-done | bytes 200736 | tf_op jit(solution)/shard_map/ppermute | solution.py:346
  14.5 0.8 %early.1 = (f32[1024,256]{1,0:T(8,128)S(1)}, bf16[256,768]{1,0:T(8,128)(2,1)S(1)}) custom-call(bf16[8,3,128,128]{3,2,1,0:T(8,128)(2,1)S(1)} %get-tuple-element.26.tr.own_ref, bf16[8,3,128,128]{3,2,1,0:T(8,128)(2,1)S(1)} %collective-permute-done._.other_ref, bf16[784,128]{1,0:T(8,128)(2,1)S(1)} %collective-permute-done.1.first_ref.refs_0_, ...), custom_call_target="tpu_custom_call" | custom-call | flops 600000000 | bytes 2400000 | tf_op jit(solution)/shard_map/early/pallas_call | solution.py:368
  15.3 0.7 %collective-permute-done.4.refs_3_ = bf16[784,128]{1,0:T(8,128)(2,1)S(1)} collective-permute-done((bf16[784,128]{1,0:T(8,128)(2,1)S(1)}, bf16[784,128]{1,0:T(8,128)(2,1)S(1)}, u32[]{:S(2)}, u32[]{:S(2)}) %collective-permute-start.4) | collective-permute-done | bytes 200736 | tf_op jit(solution)/shard_map/ppermute | solution.py:347
  16.0 0.7 %cross.2 = (f32[2,2,4,32,128]{4,3,2,1,0:T(8,128)S(1)}, bf16[512,128]{1,0:T(8,128)(2,1)S(1)}, bf16[256,1536]{1,0:T(8,128)(2,1)S(1)}) custom-call(bf16[8,3,128,128]{3,2,1,0:T(8,128)(2,1)S(1)} %get-tuple-element.26.tr.own_ref, bf16[8,3,128,128]{3,2,1,0:T(8,128)(2,1)S(1)} %collective-permute-done._.other_ref, ...), custom_call_target="tpu_custom_call" | custom-call | flops 900000000 | bytes 4000000 | tf_op jit(solution)/shard_map/cross/pallas_call | solution.py:393
  16.6 0.1 collective-permute-start.6
  16.7 0.6 %cross.3 = (f32[2,2,4,32,128]{4,3,2,1,0:T(8,128)S(1)}, bf16[512,128]{1,0:T(8,128)(2,1)S(1)}) custom-call(bf16[8,3,128,128]{3,2,1,0:T(8,128)(2,1)S(1)} %get-tuple-element.26.tr.own_ref, bf16[8,3,128,128]{3,2,1,0:T(8,128)(2,1)S(1)} %collective-permute-done._.other_ref, bf16[784,128]{1,0:T(8,128)(2,1)S(1)} %collective-permute-done.1.first_ref.refs_0_, ...), custom_call_target="tpu_custom_call" | custom-call | flops 900000000 | bytes 4000000 | tf_op jit(solution)/shard_map/cross/pallas_call | solution.py:393
  17.4 0.6 %collective-permute-start.5 = (bf16[512,128]{1,0:T(8,128)(2,1)S(1)}, bf16[512,128]{1,0:T(8,128)(2,1)S(1)}, u32[]{:S(2)}, u32[]{:S(2)}) collective-permute-start(bf16[512,128]{1,0:T(8,128)(2,1)S(1)} %get-tuple-element.38), channel_id=1, source_target_pairs={{0,1},{1,0},{2,3},{3,2},{4,5},{5,4},{6,7},{7,6},{8,9},{9,8},{10,11... | collective-permute-start | bytes 393224 | tf_op jit(solution)/shard_map/ppermute | solution.py:414
  17.9 0.1 collective-permute-done.6.got_ref
  18.1 1.7 %collective-permute-start.7 = (bf16[256,128]{1,0:T(8,128)(2,1)S(1)}, bf16[256,128]{1,0:T(8,128)(2,1)S(1)}, u32[]{:S(2)}, u32[]{:S(2)}) collective-permute-start(bf16[256,128]{1,0:T(8,128)(2,1)S(1)} %get-tuple-element.42), channel_id=1, source_target_pairs={{0,6},{2,4},{4,2},{6,0},{8,10},{10,8},{12,14},{14,12},{1,7},{3,5},... | collective-permute-start | bytes 196616 | tf_op jit(solution)/shard_map/ppermute | solution.py:432
  19.8 0.8 %collective-permute-start.8 = (bf16[256,128]{1,0:T(8,128)(2,1)S(1)}, bf16[256,128]{1,0:T(8,128)(2,1)S(1)}, u32[]{:S(2)}, u32[]{:S(2)}) collective-permute-start(bf16[256,128]{1,0:T(8,128)(2,1)S(1)} %get-tuple-element.43), channel_id=1, source_target_pairs={{0,2},{2,0},{4,6},{6,4},{8,14},{10,12},{12,10},{14,8},{1,3},{3,1},... | collective-permute-start | bytes 196616 | tf_op jit(solution)/shard_map/ppermute | solution.py:432
  20.6 0.0 collective-permute-done.5.got_ref
  20.6 1.1 %collective-permute-start.9 = (bf16[256,128]{1,0:T(8,128)(2,1)S(1)}, bf16[256,128]{1,0:T(8,128)(2,1)S(1)}, u32[]{:S(2)}, u32[]{:S(2)}) collective-permute-start(bf16[256,128]{1,0:T(8,128)(2,1)S(1)} %get-tuple-element.44), channel_id=1, source_target_pairs={{0,4},{2,6},{4,0},{6,2},{8,12},{10,14},{12,8},{14,10},{1,5},{3,7},... | collective-permute-start | bytes 196616 | tf_op jit(solution)/shard_map/ppermute | solution.py:432
  21.8 1.6 %collective-permute-done.7.refs_0_ = bf16[256,128]{1,0:T(8,128)(2,1)S(1)} collective-permute-done((bf16[256,128]{1,0:T(8,128)(2,1)S(1)}, bf16[256,128]{1,0:T(8,128)(2,1)S(1)}, u32[]{:S(2)}, u32[]{:S(2)}) %collective-permute-start.7) | collective-permute-done | bytes 65568 | tf_op jit(solution)/shard_map/ppermute | solution.py:432
  23.4 1.2 %collective-permute-done.8.refs_1_ = bf16[256,128]{1,0:T(8,128)(2,1)S(1)} collective-permute-done((bf16[256,128]{1,0:T(8,128)(2,1)S(1)}, bf16[256,128]{1,0:T(8,128)(2,1)S(1)}, u32[]{:S(2)}, u32[]{:S(2)}) %collective-permute-start.8) | collective-permute-done | bytes 65568 | tf_op jit(solution)/shard_map/ppermute | solution.py:432
  24.6 0.6 %collective-permute-done.9.refs_2_ = bf16[256,128]{1,0:T(8,128)(2,1)S(1)} collective-permute-done((bf16[256,128]{1,0:T(8,128)(2,1)S(1)}, bf16[256,128]{1,0:T(8,128)(2,1)S(1)}, u32[]{:S(2)}, u32[]{:S(2)}) %collective-permute-start.9) | collective-permute-done | bytes 65568 | tf_op jit(solution)/shard_map/ppermute | solution.py:432
  25.2 3.2 %collective-permute-start.10 = (bf16[128,128]{1,0:T(8,128)(2,1)S(1)}, bf16[128,128]{1,0:T(8,128)(2,1)S(1)}, u32[]{:S(2)}, u32[]{:S(2)}) collective-permute-start(bf16[128,128]{1,0:T(8,128)(2,1)S(1)} %get-tuple-element.46), channel_id=1, source_target_pairs={{0,8},{2,10},{4,12},{6,14},{8,0},{10,2},{12,4},{14,6},{1,9},{3,11}... | collective-permute-start | bytes 98312 | tf_op jit(solution)/shard_map/ppermute | solution.py:446
  28.4 1.9 %collective-permute-done.10.got_ref = bf16[128,128]{1,0:T(8,128)(2,1)S(1)} collective-permute-done((bf16[128,128]{1,0:T(8,128)(2,1)S(1)}, bf16[128,128]{1,0:T(8,128)(2,1)S(1)}, u32[]{:S(2)}, u32[]{:S(2)}) %collective-permute-start.10) | collective-permute-done | bytes 32800 | tf_op jit(solution)/shard_map/ppermute | solution.py:446
  30.3 0.7 %total.1 = f32[32,4,128]{2,1,0:T(4,128)} custom-call(f32[4,32,128]{2,1,0:T(8,128)S(1)} %get-tuple-element.45.keep_ref, bf16[128,128]{1,0:T(8,128)(2,1)S(1)} %collective-permute-done.10.got_ref), custom_call_target="tpu_custom_call" | custom-call | tf_op jit(solution)/shard_map/total/pallas_call | solution.py:447
  (4 shorter events, 0.1 us)
Async XLA Ops:
  0.0 7.1 %copy-start.1 = (f32[16]{0:T(128)S(1)}, f32[16]{0:T(128)}, u32[]{:S(2)}) copy-start(f32[16]{0:T(128)} %param.6) | copy-start | bytes 196
  1.4 5.7 %copy-start = (s32[1,8,128]{2,1,0:T(8,128)S(1)}, s32[1,8,128]{2,1,0:T(8,128)}, u32[]{:S(2)}) copy-start(s32[1,8,128]{2,1,0:T(8,128)} %ids_ref.1) | copy-start | bytes 12292
  1.4 5.7 %collective-permute-start = (bf16[8,3,128,128]{3,2,1,0:T(8,128)(2,1)S(1)}, bf16[8,3,128,128]{3,2,1,0:T(8,128)(2,1)S(1)}, u32[]{:S(2)}, u32[]{:S(2)}) collective-permute-start(bf16[8,3,128,128]{3,2,1,0:T(8,128)(2,1)S(1)} %get-tuple-element.26.tr.own_ref), channel_id=1, source_target_pairs={{0,1},{1,0},{2,3},{3,2},{4,5},{5,4},{6,7},{7,6},{8,9},{9,8},{10,11... | collective-permute-start | bytes 2359304 | tf_op jit(solution)/shard_map/ppermute | solution.py:334
  2.0 11.4 %collective-permute-start.1 = (bf16[784,128]{1,0:T(8,128)(2,1)S(1)}, bf16[784,128]{1,0:T(8,128)(2,1)S(1)}, u32[]{:S(2)}, u32[]{:S(2)}) collective-permute-start(bf16[784,128]{1,0:T(8,128)(2,1)S(1)} %get-tuple-element.27), channel_id=1, source_target_pairs={{0,2},{1,3},{2,0},{3,1},{4,6},{5,7},{6,4},{7,5},{8,10},{9,11},{10,... | collective-permute-start | bytes 602120 | tf_op jit(solution)/shard_map/ppermute | solution.py:335
  4.5 8.9 %collective-permute-start.2 = (bf16[784,128]{1,0:T(8,128)(2,1)S(1)}, bf16[784,128]{1,0:T(8,128)(2,1)S(1)}, u32[]{:S(2)}, u32[]{:S(2)}) collective-permute-start(bf16[784,128]{1,0:T(8,128)(2,1)S(1)} %get-tuple-element.28), channel_id=1, source_target_pairs={{0,12},{1,13},{2,6},{3,7},{4,0},{5,1},{6,10},{7,11},{8,4},{9,5},{1... | collective-permute-start | bytes 602120 | tf_op jit(solution)/shard_map/ppermute | solution.py:336
  7.2 7.3 %collective-permute-start.3 = (bf16[784,128]{1,0:T(8,128)(2,1)S(1)}, bf16[784,128]{1,0:T(8,128)(2,1)S(1)}, u32[]{:S(2)}, u32[]{:S(2)}) collective-permute-start(bf16[784,128]{1,0:T(8,128)(2,1)S(1)} %get-tuple-element.29), channel_id=1, source_target_pairs={{0,3},{1,2},{2,1},{3,0},{4,7},{5,6},{6,5},{7,4},{8,11},{9,10},{10,... | collective-permute-start | bytes 602120 | tf_op jit(solution)/shard_map/ppermute | solution.py:346
  7.3 8.6 %collective-permute-start.4 = (bf16[784,128]{1,0:T(8,128)(2,1)S(1)}, bf16[784,128]{1,0:T(8,128)(2,1)S(1)}, u32[]{:S(2)}, u32[]{:S(2)}) collective-permute-start(bf16[784,128]{1,0:T(8,128)(2,1)S(1)} %get-tuple-element.30), channel_id=1, source_target_pairs={{0,13},{1,12},{2,7},{3,6},{4,1},{5,0},{6,11},{7,10},{8,5},{9,4},{1... | collective-permute-start | bytes 602120 | tf_op jit(solution)/shard_map/ppermute | solution.py:347
  16.6 1.4 %collective-permute-start.6 = (bf16[512,128]{1,0:T(8,128)(2,1)S(1)}, bf16[512,128]{1,0:T(8,128)(2,1)S(1)}, u32[]{:S(2)}, u32[]{:S(2)}) collective-permute-start(bf16[512,128]{1,0:T(8,128)(2,1)S(1)} %get-tuple-element.41), channel_id=1, source_target_pairs={{0,1},{1,0},{2,3},{3,2},{4,5},{5,4},{6,7},{7,6},{8,9},{9,8},{10,11... | collective-permute-start | bytes 393224 | tf_op jit(solution)/shard_map/ppermute | solution.py:412
  17.4 3.2 %collective-permute-start.5 = (bf16[512,128]{1,0:T(8,128)(2,1)S(1)}, bf16[512,128]{1,0:T(8,128)(2,1)S(1)}, u32[]{:S(2)}, u32[]{:S(2)}) collective-permute-start(bf16[512,128]{1,0:T(8,128)(2,1)S(1)} %get-tuple-element.38), channel_id=1, source_target_pairs={{0,1},{1,0},{2,3},{3,2},{4,5},{5,4},{6,7},{7,6},{8,9},{9,8},{10,11... | collective-permute-start | bytes 393224 | tf_op jit(solution)/shard_map/ppermute | solution.py:414
  18.1 5.3 %collective-permute-start.7 = (bf16[256,128]{1,0:T(8,128)(2,1)S(1)}, bf16[256,128]{1,0:T(8,128)(2,1)S(1)}, u32[]{:S(2)}, u32[]{:S(2)}) collective-permute-start(bf16[256,128]{1,0:T(8,128)(2,1)S(1)} %get-tuple-element.42), channel_id=1, source_target_pairs={{0,6},{2,4},{4,2},{6,0},{8,10},{10,8},{12,14},{14,12},{1,7},{3,5},... | collective-permute-start | bytes 196616 | tf_op jit(solution)/shard_map/ppermute | solution.py:432
  19.8 4.8 %collective-permute-start.8 = (bf16[256,128]{1,0:T(8,128)(2,1)S(1)}, bf16[256,128]{1,0:T(8,128)(2,1)S(1)}, u32[]{:S(2)}, u32[]{:S(2)}) collective-permute-start(bf16[256,128]{1,0:T(8,128)(2,1)S(1)} %get-tuple-element.43), channel_id=1, source_target_pairs={{0,2},{2,0},{4,6},{6,4},{8,14},{10,12},{12,10},{14,8},{1,3},{3,1},... | collective-permute-start | bytes 196616 | tf_op jit(solution)/shard_map/ppermute | solution.py:432
  20.6 4.6 %collective-permute-start.9 = (bf16[256,128]{1,0:T(8,128)(2,1)S(1)}, bf16[256,128]{1,0:T(8,128)(2,1)S(1)}, u32[]{:S(2)}, u32[]{:S(2)}) collective-permute-start(bf16[256,128]{1,0:T(8,128)(2,1)S(1)} %get-tuple-element.44), channel_id=1, source_target_pairs={{0,4},{2,6},{4,0},{6,2},{8,12},{10,14},{12,8},{14,10},{1,5},{3,7},... | collective-permute-start | bytes 196616 | tf_op jit(solution)/shard_map/ppermute | solution.py:432
  25.2 5.1 %collective-permute-start.10 = (bf16[128,128]{1,0:T(8,128)(2,1)S(1)}, bf16[128,128]{1,0:T(8,128)(2,1)S(1)}, u32[]{:S(2)}, u32[]{:S(2)}) collective-permute-start(bf16[128,128]{1,0:T(8,128)(2,1)S(1)} %get-tuple-element.46), channel_id=1, source_target_pairs={{0,8},{2,10},{4,12},{6,14},{8,0},{10,2},{12,4},{14,6},{1,9},{3,11}... | collective-permute-start | bytes 98312 | tf_op jit(solution)/shard_map/ppermute | solution.py:446
